TPU v7x, 32 devices: a whole 2x2x4 slice. The times are simulated.
32 devices in a mesh: wide: 8 (over y, x, core), narrow: 4 (over z).
Axes of the slice: x: 2, y: 2, z: 4, core: 2. Of those that a mesh axis runs over, the one named last changes fastest.
Arguments:
- patches: bfloat16 [8192, 1536], P('wide'), may hold values from -6 to 6
- cotangent: bfloat16 [8192, 1536], P('wide'), may hold values from -6 to 6
- conditioning: bfloat16 [8, 1024], P('wide'), may hold values from -6 to 6
- captions: bfloat16 [2048, 4096], P('wide'), may hold values from -6 to 6
- item_lengths: int32 [8], replicated, may hold values from 0 to 4096, as said below
- grid_widths: int32 [8], replicated, may hold values from 16 to 64, as said below
- w_ada: bfloat16 [1024, 4, 1536], P(None, None, 'narrow'), may hold values from -0.1875 to 0.1875
- norm_gains: float32 [4, 1536], replicated, may hold values from 0.25 to 1.75
- w_qkv: bfloat16 [3, 1536, 1536], P(None, None, 'narrow'), may hold values from -0.15625 to 0.15625
- head_gains: float32 [3, 64], replicated, may hold values from 0.25 to 1.75
- cross_gate: float32 [24], P('narrow'), may hold values from -1.5 to 1.5
- w_caption: bfloat16 [2, 4096, 1536], P(None, None, 'narrow'), may hold values from -0.09375 to 0.09375
- w_out: bfloat16 [1536, 1536], P('narrow'), may hold values from -0.15625 to 0.15625
- w_gate_up: bfloat16 [2, 1536, 4096], P(None, None, 'narrow'), may hold values from -0.15625 to 0.15625
- w_down: bfloat16 [4096, 1536], P('narrow'), may hold values from -0.09375 to 0.09375
Outputs:
- output: bfloat16 [8192, 1536], P('wide')
- grad_patches: bfloat16 [8192, 1536], P('wide')
- grad_conditioning: float32 [8, 1024], P('wide')
- grad_captions: bfloat16 [2048, 4096], P('wide')
- grad_ada: float32 [1024, 4, 1536], P('wide', None, 'narrow')
- grad_norm_gains: float32 [4, 1536], P(None, 'wide')
- grad_qkv: float32 [3, 1536, 1536], P(None, 'wide', 'narrow')
- grad_head_gains: float32 [3, 64], replicated
- grad_cross_gate: float32 [24], replicated
- grad_caption_w: float32 [2, 4096, 1536], P(None, 'wide', 'narrow')
- grad_out_w: float32 [1536, 1536], P('narrow', 'wide')
- grad_gate_up: float32 [2, 1536, 4096], P(None, 'wide', 'narrow')
- grad_down: float32 [4096, 1536], P('narrow', 'wide')
Inputs may be any that keep to these rules, and one draw needn't show every extreme that they name: `item_lengths`: each length is a multiple of 1024, items fill all 8192 tokens in order with zeros after the last, and in every draw some item has exactly 4096 tokens. `grid_widths`: each is a power of two.
All inputs are finite; a program needn't handle non-finite values.
Results may differ from a plain program's by a relative error of at most 0.019.
Values may be sent and summed in bfloat16 or wider, within the bound.
No kernel may reach another device: no remote copies, remote signals or barrier semaphores. Data moves between devices by JAX's collectives and lax.ppermute only.
A program may use at most 384 MiB of HBM per device.

v0:
```python
import jax
import jax.numpy as jnp
from jax import lax
from jax.sharding import PartitionSpec as P

H = 24
HD = 64
SPAN = 4


epsilon = 1e-05
scaling = 0.125


def entering(x, axis, combine, identity, reverse):
    peers, mine = (lax.axis_size(axis), lax.axis_index(axis))
    everything = jax.tree.map(
        lambda part, kind: lax.all_gather(part.astype(kind), axis),
        x,
        jax.tree.map(lambda a: jnp.bfloat16 if a.dtype == jnp.float32 else a.dtype, x),
    )
    start = jax.tree.map(
        lambda part, zero: jnp.broadcast_to(jnp.asarray(zero, part.dtype), part.shape), x, identity
    )

    def step(k, before):
        at = peers - 1 - k if reverse else k
        reached = at > mine if reverse else at < mine
        new = combine(
            before, jax.tree.map(lambda part, own: part[at].astype(own.dtype), everything, x)
        )
        return jax.tree.map(lambda a, b: jnp.where(reached, a, b), new, before)

    return lax.fori_loop(0, peers, step, start)


def shifted(x, axis, by):
    peers = lax.axis_size(axis)
    pairs = [(i, i + by) for i in range(peers) if 0 <= i + by < peers]
    return lax.ppermute(x, axis, pairs)


def row_norm(values, gain_vec):
    return values * lax.rsqrt(jnp.mean(values * values, -1, keepdims=True) + epsilon) * gain_vec


def rotate(values, cos_tab, sin_tab):
    halfway = values.shape[-1] // 2
    former = values[..., :halfway]
    latter = values[..., halfway:]
    cos_tab = cos_tab[..., None, :]
    sin_tab = sin_tab[..., None, :]
    return jnp.concatenate(
        [former * cos_tab - latter * sin_tab, latter * cos_tab + former * sin_tab], -1
    )


def rotary(values, tables):
    halfway = values.shape[-1] // 2
    return jnp.concatenate(
        [
            rotate(values[..., :halfway], tables[0], tables[1]),
            rotate(values[..., halfway:], tables[2], tables[3]),
        ],
        -1,
    )


def rope_tables(row_pos, col_pos, quarter):
    frequency = 10000.0 ** (-jnp.arange(quarter, dtype=jnp.float32) / quarter)
    row_angle = row_pos.astype(jnp.float32)[..., None] * frequency
    col_angle = col_pos.astype(jnp.float32)[..., None] * frequency
    return (jnp.cos(row_angle), jnp.sin(row_angle), jnp.cos(col_angle), jnp.sin(col_angle))


def block_scores(query_low, key_heads):
    return (
        jnp.einsum("qhd,khd->hqk", query_low, key_heads, preferred_element_type=jnp.float32)
        * scaling
    )


def attention_input(residual, gain_vec, scale_vec):
    return row_norm(residual, gain_vec) * (1.0 + scale_vec)


def gated_residual(branch, residual, gain_vec, gate_vec):
    return residual + jnp.tanh(gate_vec) * row_norm(branch, gain_vec)


def swiglu(paired):
    return jax.nn.silu(paired[0]) * paired[1]


def take_later(earlier, later_part):
    chosen = later_part[0][0] > 0
    picked = jax.tree.map(
        lambda older_val, newer_val: jnp.where(chosen, newer_val, older_val),
        earlier[1:],
        later_part[1:],
    )
    return (jnp.maximum(earlier[0], later_part[0]),) + tuple(picked)


def add_segment(earlier, later_part):
    stopped = later_part[0][0] > 0
    summed = jax.tree.map(
        lambda older_val, newer_val: newer_val
        + jnp.where(stopped, jnp.zeros_like(older_val), older_val),
        earlier[1:],
        later_part[1:],
    )
    return (jnp.maximum(earlier[0], later_part[0]),) + tuple(summed)


def narrow_total(partial_sum):
    return lax.psum(partial_sum, "narrow")


def keep_same(carried_value, kv_pair):
    return carried_value


def local(
    patches,
    cotangent,
    conditioning,
    captions,
    item_lengths,
    grid_widths,
    w_ada,
    norm_gains,
    w_qkv,
    head_gains,
    cross_gate,
    w_caption,
    w_out,
    w_gate_up,
    w_down,
):
    tok_rows = patches.shape[0]
    model_width = patches.shape[1]
    local_width = w_qkv.shape[2]
    local_heads = local_width // HD
    ada_width = w_ada.shape[2]
    text_rows = captions.shape[0]
    my_place = lax.axis_index("wide")
    narrow_place = lax.axis_index("narrow")
    wide_count = lax.axis_size("wide")
    item_spans = item_lengths // tok_rows
    item_ends = jnp.cumsum(item_spans)
    my_item = jnp.sum((item_ends <= my_place).astype(jnp.int32))
    is_mine = jnp.arange(item_ends.shape[0], dtype=jnp.int32) == my_item
    item_end = jnp.sum(jnp.where(is_mine, item_ends, 0))
    item_first = item_end - jnp.sum(jnp.where(is_mine, item_spans, 0))
    dev_offset = my_place - item_first
    grid_width = jnp.sum(jnp.where(is_mine, grid_widths, 0))
    position = dev_offset * tok_rows + jnp.arange(tok_rows, dtype=jnp.int32)
    tables = rope_tables(position // grid_width, position % grid_width, HD // 4)
    is_first = dev_offset == 0
    first_mask = is_first.astype(jnp.float32)

    def caption_project(caption_in):
        return jnp.einsum("kd,jde->jke", caption_in, w_caption, preferred_element_type=jnp.float32)

    def caption_blank(caption_in):
        return jnp.zeros((2, text_rows, local_width), jnp.float32)

    cap_raw = lax.cond(is_first, caption_project, caption_blank, captions)
    cap_key_raw = cap_raw[0].reshape(text_rows, local_heads, HD)
    own_cap_keys = row_norm(cap_key_raw, head_gains[2]).astype(jnp.bfloat16)
    own_cap_values = cap_raw[1].reshape(text_rows, local_heads, HD).astype(jnp.bfloat16)
    start_flag = is_first.astype(jnp.int32).reshape(1)
    own_row = jnp.where(is_first, conditioning, jnp.zeros_like(conditioning))
    sent_up = (start_flag, own_cap_keys, own_cap_values, own_row)
    blank_tree = jax.tree.map(jnp.zeros_like, sent_up)
    carried = entering(sent_up, "wide", take_later, blank_tree, False)
    cap_keys = jnp.where(is_first, own_cap_keys, carried[1])
    cap_values = jnp.where(is_first, own_cap_values, carried[2])
    cond_row = jnp.where(is_first, conditioning, carried[3])
    cond_value = cond_row.astype(jnp.float32)[0]
    silu_cond = jax.nn.silu(cond_value).astype(jnp.bfloat16)
    mod_local = jnp.einsum("c,cjd->jd", silu_cond, w_ada, preferred_element_type=jnp.float32)
    modulation = lax.all_gather(mod_local, "narrow", axis=1, tiled=True)
    residual = patches.astype(jnp.float32)
    normed_in = attention_input(residual, norm_gains[0], modulation[0])
    normed_low = normed_in.astype(jnp.bfloat16)
    projected = jnp.einsum("td,jde->jte", normed_low, w_qkv, preferred_element_type=jnp.float32)
    heads_view = projected.reshape(3, tok_rows, local_heads, HD)

    def query_path(pre_norm, gain_vec):
        return rotary(row_norm(pre_norm, gain_vec), tables)

    query_low = query_path(heads_view[0], head_gains[0]).astype(jnp.bfloat16)
    key_own = query_path(heads_view[1], head_gains[1]).astype(jnp.bfloat16)
    value_own = heads_view[2].astype(jnp.bfloat16)
    stride_list = list(range(1, SPAN)) + [-stride for stride in range(1, SPAN)]
    remote = []
    live_flags = []
    for stride in stride_list:
        source = my_place - stride
        live_flags.append((source >= item_first) & (source < item_end))
        remote.append(shifted((key_own, value_own), "wide", stride))
    own_scores = block_scores(query_low, key_own)
    row_top = jnp.max(own_scores, -1)
    row_total = jnp.sum(jnp.exp(own_scores - row_top[..., None]), -1)

    def fold_stats(run_stats, kv_pair):
        scores = block_scores(query_low, kv_pair[0])
        new_top = jnp.maximum(run_stats[0], jnp.max(scores, -1))
        new_total = run_stats[1] * jnp.exp(run_stats[0] - new_top) + jnp.sum(
            jnp.exp(scores - new_top[..., None]), -1
        )
        return (new_top, new_total)

    run_stats = (row_top, row_total)
    for number in range(len(stride_list)):
        run_stats = lax.cond(live_flags[number], fold_stats, keep_same, run_stats, remote[number])
    log_total = run_stats[0] + jnp.log(run_stats[1])

    def add_values(accumulated, kv_pair):
        attn_prob = jnp.exp(block_scores(query_low, kv_pair[0]) - log_total[..., None]).astype(
            jnp.bfloat16
        )
        return accumulated + jnp.einsum(
            "hqk,khd->qhd", attn_prob, kv_pair[1], preferred_element_type=jnp.float32
        )

    self_out = add_values(jnp.zeros((tok_rows, local_heads, HD), jnp.float32), (key_own, value_own))
    for number in range(len(stride_list)):
        self_out = lax.cond(live_flags[number], add_values, keep_same, self_out, remote[number])
    cross_scores = block_scores(query_low, cap_keys)
    cross_top = jnp.max(cross_scores, -1, keepdims=True)
    cross_exp = jnp.exp(cross_scores - cross_top)
    cross_prob = cross_exp / jnp.sum(cross_exp, -1, keepdims=True)
    cross_low = cross_prob.astype(jnp.bfloat16)
    cross_out = jnp.einsum(
        "hqk,khd->qhd", cross_low, cap_values, preferred_element_type=jnp.float32
    )
    gate_tanh = jnp.tanh(cross_gate)
    mixed_heads = self_out + gate_tanh[None, :, None] * cross_out
    mixed_low = mixed_heads.astype(jnp.bfloat16).reshape(tok_rows, local_width)
    attn_part = jnp.dot(mixed_low, w_out, preferred_element_type=jnp.float32)
    attn_full = narrow_total(attn_part)
    upstream = cotangent.astype(jnp.float32)
    middle = gated_residual(attn_full, residual, norm_gains[1], modulation[1])
    ffn_in = attention_input(middle, norm_gains[2], modulation[2])
    ffn_low = ffn_in.astype(jnp.bfloat16)
    gate_up = jnp.einsum("td,jdf->jtf", ffn_low, w_gate_up, preferred_element_type=jnp.float32)
    hidden_low = swiglu(gate_up).astype(jnp.bfloat16)
    ffn_part = jnp.dot(hidden_low, w_down, preferred_element_type=jnp.float32)
    ffn_full = narrow_total(ffn_part)
    result = gated_residual(ffn_full, middle, norm_gains[3], modulation[3])
    result_low = result.astype(jnp.bfloat16)
    result_again, pull_out = jax.vjp(gated_residual, ffn_full, middle, norm_gains[3], modulation[3])
    d_ffn, d_middle, d_gain_four, d_gate_two = pull_out(upstream)
    d_ffn_low = d_ffn.astype(jnp.bfloat16)
    d_hidden = jnp.einsum("td,fd->tf", d_ffn_low, w_down, preferred_element_type=jnp.float32)
    grad_down = jnp.einsum("tf,td->fd", hidden_low, d_ffn_low, preferred_element_type=jnp.float32)
    hidden_again, pull_glu = jax.vjp(swiglu, gate_up)
    d_paired = pull_glu(d_hidden)[0].astype(jnp.bfloat16)
    d_ffn_in_part = jnp.einsum(
        "jtf,jdf->td", d_paired, w_gate_up, preferred_element_type=jnp.float32
    )
    grad_gate_up = jnp.einsum("td,jtf->jdf", ffn_low, d_paired, preferred_element_type=jnp.float32)
    d_ffn_in = narrow_total(d_ffn_in_part)
    ffn_again, pull_in_two = jax.vjp(attention_input, middle, norm_gains[2], modulation[2])
    d_middle_two, d_gain_three, d_scale_two = pull_in_two(d_ffn_in)
    mid_again, pull_mid = jax.vjp(gated_residual, attn_full, residual, norm_gains[1], modulation[1])
    d_attn, d_residual, d_gain_two, d_gate_one = pull_mid(d_middle + d_middle_two)
    d_attn_low = d_attn.astype(jnp.bfloat16)
    d_mixed = jnp.einsum("td,ed->te", d_attn_low, w_out, preferred_element_type=jnp.float32)
    grad_out = jnp.einsum("te,td->ed", mixed_low, d_attn_low, preferred_element_type=jnp.float32)
    d_self_out = d_mixed.astype(jnp.bfloat16).reshape(tok_rows, local_heads, HD)
    d_mixed_wide = d_self_out.astype(jnp.float32)
    d_gate_local = jnp.sum(d_mixed_wide * cross_out, (0, 2)) * (1.0 - gate_tanh * gate_tanh)
    d_cross_out = (gate_tanh[None, :, None] * d_mixed_wide).astype(jnp.bfloat16)
    d_cross_prob = jnp.einsum(
        "qhd,khd->hqk", d_cross_out, cap_values, preferred_element_type=jnp.float32
    )
    d_cap_values = jnp.einsum(
        "hqk,qhd->khd", cross_low, d_cross_out, preferred_element_type=jnp.float32
    )
    d_cross_low = (
        cross_prob * (d_cross_prob - jnp.sum(cross_prob * d_cross_prob, -1, keepdims=True))
    ).astype(jnp.bfloat16)
    d_query = (
        jnp.einsum("hqk,khd->qhd", d_cross_low, cap_keys, preferred_element_type=jnp.float32)
        * scaling
    )
    d_cap_keys = (
        jnp.einsum("hqk,qhd->khd", d_cross_low, query_low, preferred_element_type=jnp.float32)
        * scaling
    )
    kv_again = []
    for number, stride in enumerate(stride_list):
        kv_again.append(shifted((key_own, value_own), "wide", stride))

    def delta_terms(accumulated, kv_pair):
        attn_prob = jnp.exp(block_scores(query_low, kv_pair[0]) - log_total[..., None])
        d_prob = jnp.einsum(
            "qhd,khd->hqk", d_self_out, kv_pair[1], preferred_element_type=jnp.float32
        )
        return accumulated + jnp.sum(attn_prob * d_prob, -1)

    row_delta = delta_terms(jnp.zeros_like(log_total), (key_own, value_own))
    for number in range(len(stride_list)):
        row_delta = lax.cond(
            live_flags[number], delta_terms, keep_same, row_delta, kv_again[number]
        )

    def grad_terms(kv_pair):
        attn_prob = jnp.exp(block_scores(query_low, kv_pair[0]) - log_total[..., None])
        d_prob = jnp.einsum(
            "qhd,khd->hqk", d_self_out, kv_pair[1], preferred_element_type=jnp.float32
        )
        d_scores = (attn_prob * (d_prob - row_delta[..., None])).astype(jnp.bfloat16)
        part_q = (
            jnp.einsum("hqk,khd->qhd", d_scores, kv_pair[0], preferred_element_type=jnp.float32)
            * scaling
        )
        part_k = (
            jnp.einsum("hqk,qhd->khd", d_scores, query_low, preferred_element_type=jnp.float32)
            * scaling
        )
        part_v = jnp.einsum(
            "hqk,qhd->khd",
            attn_prob.astype(jnp.bfloat16),
            d_self_out,
            preferred_element_type=jnp.float32,
        )
        return (part_q, part_k, part_v)

    def grad_blank(kv_pair):
        blank_rows = jnp.zeros((tok_rows, local_heads, HD), jnp.float32)
        return (blank_rows, blank_rows, blank_rows)

    part_q, d_key_heads, d_value_heads = grad_terms((key_own, value_own))
    d_query = d_query + part_q
    for number, stride in enumerate(stride_list):
        part_q, part_k, part_v = lax.cond(
            live_flags[number], grad_terms, grad_blank, kv_again[number]
        )
        d_query = d_query + part_q
        returned = (
            shifted(part_k.astype(jnp.bfloat16), "wide", -stride).astype(part_k.dtype),
            shifted(part_v.astype(jnp.bfloat16), "wide", -stride).astype(part_v.dtype),
        )
        d_key_heads = d_key_heads + returned[0]
        d_value_heads = d_value_heads + returned[1]
    query_again, pull_query = jax.vjp(query_path, heads_view[0], head_gains[0])
    d_query_pre, d_gain_query = pull_query(d_query)
    key_again, pull_key = jax.vjp(query_path, heads_view[1], head_gains[1])
    d_key_pre, d_gain_key = pull_key(d_key_heads)
    d_projected = (
        jnp.stack([d_query_pre, d_key_pre, d_value_heads])
        .reshape(3, tok_rows, local_width)
        .astype(jnp.bfloat16)
    )
    d_attn_in_part = jnp.einsum(
        "jte,jde->td", d_projected, w_qkv, preferred_element_type=jnp.float32
    )
    grad_qkv = jnp.einsum(
        "td,jte->jde", normed_low, d_projected, preferred_element_type=jnp.float32
    )
    d_attn_in = narrow_total(d_attn_in_part)
    scale_rows = modulation[0]
    attn_in_again, pull_in_one = jax.vjp(attention_input, residual, norm_gains[0], scale_rows)
    d_residual_two, d_gain_one, d_scale_one = pull_in_one(d_attn_in)
    grad_rows_low = (d_residual + d_residual_two).astype(jnp.bfloat16)
    d_modulation = jnp.stack([d_scale_one, d_gate_one, d_scale_two, d_gate_two])
    gain_grads = jnp.stack([d_gain_one, d_gain_two, d_gain_three, d_gain_four])
    back_sent = (
        start_flag,
        jnp.where(is_first, 0.0, d_cap_keys),
        jnp.where(is_first, 0.0, d_cap_values),
        jnp.where(is_first, 0.0, d_modulation),
    )
    back_blank = jax.tree.map(jnp.zeros_like, back_sent)
    arrived = entering(back_sent, "wide", add_segment, back_blank, True)
    total_keys = (d_cap_keys + arrived[1]) * first_mask
    total_values = (d_cap_values + arrived[2]) * first_mask
    total_mod = (d_modulation + arrived[3]) * first_mask
    cap_again, pull_cap = jax.vjp(row_norm, cap_key_raw, head_gains[2])
    d_cap_raw, d_gain_caption = pull_cap(total_keys)
    d_cap_low = (
        jnp.stack([d_cap_raw, total_values]).reshape(2, text_rows, local_width).astype(jnp.bfloat16)
    )
    d_text_part = jnp.einsum(
        "jke,jde->kd", d_cap_low, w_caption, preferred_element_type=jnp.float32
    )
    grad_caption_w = jnp.einsum(
        "kd,jke->jde", captions, d_cap_low, preferred_element_type=jnp.float32
    )
    d_mod_local = lax.dynamic_slice_in_dim(
        total_mod.astype(jnp.bfloat16), narrow_place * ada_width, ada_width, 1
    )
    column_mask = (jnp.arange(model_width, dtype=jnp.int32) // ada_width == narrow_place).astype(
        jnp.float32
    )
    grad_ada = (
        silu_cond.astype(jnp.float32)[:, None, None] * d_mod_local.astype(jnp.float32)[None, :, :]
    )
    d_cond_part = jnp.einsum("jd,cjd->c", d_mod_local, w_ada, preferred_element_type=jnp.float32)
    text_total, cond_total = (
        lax.psum(d_text_part.astype(jnp.bfloat16), "narrow").astype(jnp.float32),
        lax.psum(d_cond_part.astype(jnp.bfloat16), "narrow").astype(jnp.float32),
    )
    silu_again, pull_silu = jax.vjp(jax.nn.silu, cond_value)
    grad_conditioning = pull_silu(cond_total)[0].reshape(1, -1)
    grad_captions = text_total.astype(jnp.bfloat16)
    weight_totals = (
        lax.psum_scatter(
            grad_ada.astype(jnp.bfloat16), "wide", scatter_dimension=0, tiled=True
        ).astype(jnp.float32),
        lax.psum_scatter(
            grad_qkv.astype(jnp.bfloat16), "wide", scatter_dimension=1, tiled=True
        ).astype(jnp.float32),
        lax.psum_scatter(
            grad_caption_w.astype(jnp.bfloat16), "wide", scatter_dimension=1, tiled=True
        ).astype(jnp.float32),
        lax.psum_scatter(
            grad_out.astype(jnp.bfloat16), "wide", scatter_dimension=1, tiled=True
        ).astype(jnp.float32),
        lax.psum_scatter(
            grad_gate_up.astype(jnp.bfloat16), "wide", scatter_dimension=1, tiled=True
        ).astype(jnp.float32),
        lax.psum_scatter(
            grad_down.astype(jnp.bfloat16), "wide", scatter_dimension=1, tiled=True
        ).astype(jnp.float32),
    )
    gate_full = lax.dynamic_update_slice(
        jnp.zeros((H,), jnp.float32), d_gate_local, (narrow_place * local_heads,)
    )
    head_sum, gate_sum, gain_sum = lax.psum(
        (
            jnp.stack([d_gain_query, d_gain_key, d_gain_caption]),
            gate_full,
            gain_grads * column_mask,
        ),
        ("wide", "narrow"),
    )
    wide_cols = model_width // wide_count
    grad_norm_gains = lax.dynamic_slice_in_dim(gain_sum, my_place * wide_cols, wide_cols, 1)
    return (
        result_low,
        grad_rows_low,
        grad_conditioning,
        grad_captions,
        weight_totals[0],
        grad_norm_gains,
        weight_totals[1],
        head_sum,
        gate_sum,
        weight_totals[2],
        weight_totals[3],
        weight_totals[4],
        weight_totals[5],
    )


def solution(mesh):
    placed = (
        P("wide", None),
        P("wide", None),
        P("wide", None),
        P("wide", None),
        P(),
        P(),
        P(None, None, "narrow"),
        P(),
        P(None, None, "narrow"),
        P(),
        P("narrow"),
        P(None, None, "narrow"),
        P("narrow", None),
        P(None, None, "narrow"),
        P("narrow", None),
    )
    return jax.shard_map(
        local,
        mesh=mesh,
        in_specs=placed,
        out_specs=(
            P("wide", None),
            P("wide", None),
            P("wide", None),
            P("wide", None),
            P("wide", None, "narrow"),
            P(None, "wide"),
            P(None, "wide", "narrow"),
            P(),
            P(),
            P(None, "wide", "narrow"),
            P("narrow", "wide"),
            P(None, "wide", "narrow"),
            P("narrow", "wide"),
        ),
        check_vma=False,
    )
```

profile of v0, /device:TPU:0, one launch (start us, length us, event | category | flops | bytes accessed | tf_op | source)
XLA Modules:
  0.0 2439.3 jit_solution(9225736796843332872)
XLA Ops:
  76.8 104.6 %while.38 = (s32[]{:T(128)}, bf16[256,6,64]{2,1,0:T(8,128)(2,1)}, bf16[256,6,64]{2,1,0:T(8,128)(2,1)}, bf16[1,1024]{1,0:T(2,128)(2,1)S(1)}, s32[]{:T(128)}, /*in...) while((s32[]{:T(128)}, bf16[256,6,64]{2,1,0:T(8,128)(2,1)}, ...), condition=%wide.region_8.9_spmd.clone, body=%wide.region_7.8_spmd.clone.sunk | while | flops 592901 | bytes 2758818 | solution.py:34
  186.1 13.5 all_gather.42
  277.0 29.1 %conditional.29 = ((f32[6,1024]{1,0:T(8,128)}, f32[6,1024]{1,0:T(8,128)})) conditional(s32[]{:T(128)} %convert_element_type.425, (f32[6,1024]{1,0:T(8,128)}, f32[6,1024]{1,0:T(8,128)}) %get-tuple-element.1557, (bf16[1024,6,64]{0,2,1:T(8,128)(2,1)}, bf16[1024,6,64]{0,2,1:T(8,128)(2,1)}, f32[6,1024]{1,0:T(8,128)}, f32[6,1024]{1,0:T(8,128)}) %tuple.228), branch_computations={%region_27.28_spmd, %region_28.31_spmd} | conditional | flops 836775936 | bytes 52519020 | solution.py:218
  281.0 13.2 multiply_reduce_fusion.3
  307.3 25.1 %conditional.30 = ((f32[6,1024]{1,0:T(8,128)}, f32[6,1024]{1,0:T(8,128)})) conditional(s32[]{:T(128)} %convert_element_type.424, (f32[6,1024]{1,0:T(8,128)}, f32[6,1024]{1,0:T(8,128)}) %get-tuple-element.1558, (bf16[1024,6,64]{0,2,1:T(8,128)(2,1)}, bf16[1024,6,64]{0,2,1:T(8,128)(2,1)}, f32[6,1024]{1,0:T(8,128)}, f32[6,1024]{1,0:T(8,128)}) %tuple.229), branch_computations={%region_31.32_spmd, %region_32.35_spmd} | conditional | flops 836775936 | bytes 52519020 | solution.py:218
  307.3 13.2 multiply_reduce_fusion.4
  332.4 33.9 %collective-permute-start.8 = (bf16[1024,6,64]{0,2,1:T(8,128)(2,1)}, bf16[1024,6,64]{0,2,1:T(8,128)(2,1)}, u32[]{:S(2)}, u32[]{:S(2)}) collective-permute-start(bf16[1024,6,64]{0,2,1:T(8,128)(2,1)} %bitcast.420), channel_id=1, source_target_pairs={{0,12},{4,16},{8,20},{12,24},{16,28},{1,13},{5,17},{9,21},{13,25},... | collective-permute-start | bytes 2359304 | tf_op jit(solution)/shard_map/ppermute | solution.py:40
  366.3 25.4 %conditional.31 = ((f32[6,1024]{1,0:T(8,128)}, f32[6,1024]{1,0:T(8,128)})) conditional(s32[]{:T(128)} %convert_element_type.423, (f32[6,1024]{1,0:T(8,128)}, f32[6,1024]{1,0:T(8,128)}) %get-tuple-element.1559, (bf16[1024,6,64]{0,2,1:T(8,128)(2,1)}, bf16[1024,6,64]{0,2,1:T(8,128)(2,1)}, f32[6,1024]{1,0:T(8,128)}, f32[6,1024]{1,0:T(8,128)}) %tuple.230), branch_computations={%region_35.36_spmd, %region_36.39_spmd} | conditional | flops 836775936 | bytes 52519020 | solution.py:218
  366.7 13.2 multiply_reduce_fusion.5
  395.3 13.8 fusion.140
  409.4 18.1 conditional.35
  457.7 222.0 %all-reduce.26.cloned.1.call-done = f32[1024,1536]{1,0:T(8,128)} async-done(((f32[1024,1536]{1,0:T(8,128)}), f32[1024,1536]{1,0:T(8,128)}) %all-reduce.26.cloned.1.call-update) | async-done | bytes 6291472 | tf_op jit(solution)/shard_map/psum | solution.py:117
  706.5 221.7 %all-reduce.28.cloned.1.call-done = f32[1024,1536]{1,0:T(8,128)} async-done(((f32[1024,1536]{1,0:T(8,128)}), f32[1024,1536]{1,0:T(8,128)}) %all-reduce.28.cloned.1.call-update) | async-done | bytes 6291472 | tf_op jit(solution)/shard_map/psum | solution.py:117
  965.0 221.7 %all-reduce.30.cloned.1.call-done = f32[1024,1536]{1,0:T(8,128)} async-done(((f32[1024,1536]{1,0:T(8,128)}), f32[1024,1536]{1,0:T(8,128)}) %all-reduce.30.cloned.1.call-update) | async-done | bytes 6291472 | tf_op jit(solution)/shard_map/psum | solution.py:117
  1213.9 20.8 multiply_reduce_fusion.12
  1245.2 34.6 %conditional.41 = (f32[6,1024]{1,0:T(8,128)}) conditional(s32[]{:T(128)} %convert_element_type.425, f32[6,1024]{1,0:T(8,128)} %get-tuple-element.1569, (bf16[1024,6,64]{0,2,1:T(8,128)(2,1)}, bf16[1024,6,64]{0,2,1:T(8,128)(2,1)}, f32[6,1024]{1,0:T(8,128)}, bf16[1024,6,64]{0,2,1:T(8,128)(2,1)}, bf16[1024,6,64]{0,2,1:T(8,128)(2,1)}, ...), branch_computations={%region_73.74_spmd, %region_74.76_spmd} | conditional | flops 1635778560 | bytes 56746020 | solution.py:308
  1253.4 13.3 fusion.219
  1266.7 11.7 multiply_reduce_fusion.9
  1279.8 26.4 %conditional.42 = (f32[6,1024]{1,0:T(8,128)}) conditional(s32[]{:T(128)} %convert_element_type.424, f32[6,1024]{1,0:T(8,128)} %get-tuple-element.1570, (bf16[1024,6,64]{0,2,1:T(8,128)(2,1)}, bf16[1024,6,64]{0,2,1:T(8,128)(2,1)}, f32[6,1024]{1,0:T(8,128)}, bf16[1024,6,64]{0,2,1:T(8,128)(2,1)}, bf16[1024,6,64]{0,2,1:T(8,128)(2,1)}, ...), branch_computations={%region_76.77_spmd, %region_77.79_spmd} | conditional | flops 1635778560 | bytes 56746020 | solution.py:308
  1279.8 13.3 fusion.220
  1306.1 26.8 %conditional.43 = (f32[6,1024]{1,0:T(8,128)}) conditional(s32[]{:T(128)} %convert_element_type.423, f32[6,1024]{1,0:T(8,128)} %get-tuple-element.1571, (bf16[1024,6,64]{0,2,1:T(8,128)(2,1)}, bf16[1024,6,64]{0,2,1:T(8,128)(2,1)}, f32[6,1024]{1,0:T(8,128)}, bf16[1024,6,64]{0,2,1:T(8,128)(2,1)}, bf16[1024,6,64]{0,2,1:T(8,128)(2,1)}, ...), branch_computations={%region_79.80_spmd, %region_80.82_spmd} | conditional | flops 1635778560 | bytes 56746020 | solution.py:308
  1306.5 13.3 fusion.221
  1332.9 21.6 multiply_convert_fusion.6
  1387.0 58.4 %conditional.47 = (f32[1024,6,64]{0,2,1:T(8,128)}, f32[1024,6,64]{0,2,1:T(8,128)}, f32[1024,6,64]{0,2,1:T(8,128)}) conditional(s32[]{:T(128)} %convert_element_type.425, () %tuple.249, (bf16[1024,6,64]{0,2,1:T(8,128)(2,1)}, bf16[1024,6,64]{0,2,1:T(8,128)(2,1)}, f32[6,1024]{1,0:T(8,128)}, bf16[1024,6,64]{0,2,1:T(8,128)(2,1)}, ...), branch_computations={%region_88.89_spmd, %region_89.90_spmd} | conditional | flops 4077649920 | bytes 126689328 | solution.py:341
  1387.0 13.2 fusion.225
  1400.2 11.8 fusion.53
  1412.1 14.8 multiply_convert_fusion.3
  1447.8 55.2 %collective-permute-start.21 = (bf16[1024,6,64]{0,2,1:T(8,128)(2,1)}, bf16[1024,6,64]{0,2,1:T(8,128)(2,1)}, u32[]{:S(2)}, u32[]{:S(2)}) collective-permute-start(bf16[1024,6,64]{0,2,1:T(8,128)(2,1)} %convert_element_type.468), channel_id=1, source_target_pairs={{0,4},{4,8},{8,12},{12,16},{16,20},{20,24},{24,28},{1,5},{5,9},{9,... | collective-permute-start | bytes 2359304 | tf_op jit(solution)/shard_map/ppermute | solution.py:40
  1503.0 58.1 %conditional.48 = (f32[1024,6,64]{0,2,1:T(8,128)}, f32[1024,6,64]{0,2,1:T(8,128)}, f32[1024,6,64]{0,2,1:T(8,128)}) conditional(s32[]{:T(128)} %convert_element_type.424, () %tuple.251, (bf16[1024,6,64]{0,2,1:T(8,128)(2,1)}, bf16[1024,6,64]{0,2,1:T(8,128)(2,1)}, f32[6,1024]{1,0:T(8,128)}, bf16[1024,6,64]{0,2,1:T(8,128)(2,1)}, ...), branch_computations={%region_90.91_spmd, %region_91.92_spmd} | conditional | flops 4077649920 | bytes 126689328 | solution.py:341
  1503.0 13.2 fusion.226
  1516.3 11.8 fusion.60
  1528.0 14.8 multiply_convert_fusion.4
  1563.6 58.4 %conditional.49 = (f32[1024,6,64]{0,2,1:T(8,128)}, f32[1024,6,64]{0,2,1:T(8,128)}, f32[1024,6,64]{0,2,1:T(8,128)}) conditional(s32[]{:T(128)} %convert_element_type.423, () %tuple.253, (bf16[1024,6,64]{0,2,1:T(8,128)(2,1)}, bf16[1024,6,64]{0,2,1:T(8,128)(2,1)}, f32[6,1024]{1,0:T(8,128)}, bf16[1024,6,64]{0,2,1:T(8,128)(2,1)}, ...), branch_computations={%region_92.93_spmd, %region_93.94_spmd} | conditional | flops 4077649920 | bytes 126689328 | solution.py:341
  1563.6 13.2 fusion.227
  1576.8 11.8 fusion.67
  1588.7 14.8 multiply_convert_fusion.5
  1643.8 15.8 collective-permute-start.23
  1701.7 13.4 fusion.123
  1758.9 13.5 convert_bitcast_fusion
  1772.4 16.6 copy.137
  1826.3 164.1 %all-reduce.32.cloned.1.call-done = f32[1024,1536]{1,0:T(8,128)} async-done(((f32[1024,1536]{1,0:T(8,128)}), f32[1024,1536]{1,0:T(8,128)}) %all-reduce.32.cloned.1.call-update) | async-done | bytes 6291472 | tf_op jit(solution)/shard_map/psum | solution.py:117
  2007.5 58.9 %while.39 = (s32[]{:T(128)}, f32[256,6,64]{2,1,0:T(8,128)}, f32[256,6,64]{2,1,0:T(8,128)}, f32[4,1536]{1,0:T(4,128)}, s32[]{:T(128)}, /*index=5*/bf16[8,256,6,64...) while((s32[]{:T(128)}, f32[256,6,64]{2,1,0:T(8,128)}, ...), condition=%wide.region_103.104_spmd.clone, body=%wide.region_102.103_spmd.clone.sunk | while | flops 1013769 | bytes 2027740 | solution.py:34
  2105.3 26.1 %reduce-scatter.13.cloned.1.call-done = bf16[192,1152]{1,0:T(8,128)(2,1)} async-done(((bf16[1536,1152]{1,0:T(8,128)(2,1)}), bf16[192,1152]{1,0:T(8,128)(2,1)}) %reduce-scatter.13.cloned.1.call-update) | async-done | bytes 442384
  2141.5 12.3 psum.67
  2162.8 39.0 %all-reduce.17 = (f32[4,1536]{1,0:T(4,128)}, f32[3,64]{1,0:T(4,128)}, f32[24]{0:T(128)}) all-reduce(f32[4,1536]{1,0:T(4,128)} %maximum_multiply_fusion, f32[3,64]{1,0:T(4,128)} %pad_maximum_fusion.8, f32[24]{0:T(128)} %multiply_dynamic-update-slice_fusion), channel_id=1, replica_groups=mesh['wide'=8,'narrow'=4] {'wide','narrow'}, use_global_device_ids=true, to_apply=%region_112.113 | all-reduce | flops 6360 | bytes 50880 | tf_op jit(solution)/shard_map/psum | solution.py:435
  2213.6 60.9 %all-reduce.36.cloned.1.call-done = (bf16[1024,4,384]{2,1,0:T(4,128)(2,1)}, bf16[2,1536,1024]{2,0,1:T(2,128)(2,1)}) async-done(((bf16[1024,4,384]{2,1,0:T(4,128)(2,1)}, bf16[2,1536,1024]{2,0,1:T(2,128)(2,1)}), (bf16[1024,4,384]{2,1,0:T(4,128)(2,1)}, bf16[2,1536,1024]{2,0,1:T(2,128)(2,1)})) %all-reduce.36.cloned.1.call-update) | async-done | bytes 9437200
  2279.8 60.4 %reduce-scatter.7.cloned.1.call-done = bf16[2,512,384]{1,2,0:T(8,128)(2,1)} async-done(((bf16[2,4096,384]{1,2,0:T(8,128)(2,1)}), bf16[2,512,384]{1,2,0:T(8,128)(2,1)}) %reduce-scatter.7.cloned.1.call-update) | async-done | bytes 786448 | tf_op jit(solution)/shard_map/reduce_scatter | solution.py:419
  2342.7 86.8 %all-reduce.34.cloned.1.call-done = bf16[256,4096]{1,0:T(8,128)(2,1)} async-done(((bf16[256,4096]{1,0:T(8,128)(2,1)}), bf16[256,4096]{1,0:T(8,128)(2,1)}) %all-reduce.34.cloned.1.call-update) | async-done | bytes 2097168 | tf_op jit(solution)/shard_map/psum | solution.py:406
  (654 shorter events, 888.1 us)
Async XLA Ops:
  7.2 193.1 %copy-start = (bf16[3,1536,384]{2,1,0:T(8,128)(2,1)S(1)}, bf16[3,1536,384]{2,1,0:T(8,128)(2,1)}, u32[]{:S(2)}) copy-start(bf16[3,1536,384]{2,1,0:T(8,128)(2,1)} %param.77) | copy-start | bytes 10616836
  7.2 60.9 %all-gather.11.cloned.1.call-start = ((), (), s32[]{:S(2)}) async-start(), calls=%async_computation.5 | async-start | bytes 1769472 | tf_op jit(solution)/shard_map/all_gather | solution.py:18
  18.3 33.5 %copy-start.127 = (bf16[1,1024]{1,0:T(2,128)(2,1)S(1)}, bf16[1,1024]{1,0:T(2,128)(2,1)}, u32[]{:S(2)}) copy-start(bf16[1,1024]{1,0:T(2,128)(2,1)} %param.71) | copy-start | bytes 6148
  20.0 56.8 %all-gather.9.cloned.1.call-start = ((), (), s32[]{:S(2)}) async-start(), calls=%async_computation.4 | async-start | bytes 1769472 | tf_op jit(solution)/shard_map/all_gather | solution.py:18
  21.9 234.0 %copy-start.90 = (f32[256,6]{0,1:T(8,128)}, f32[256,6]{0,1:T(8,128)S(1)}, u32[]{:S(2)}) copy-start(f32[256,6]{0,1:T(8,128)S(1)} %fusion.166) | copy-start | bytes 18436
  22.7 657.1 %all-reduce.26.cloned.1.call-start = ((), (), s32[]{:S(2)}) async-start(), calls=%async_computation.6 | async-start | bytes 12582912 | tf_op jit(solution)/shard_map/psum | solution.py:117
  66.9 133.4 %copy-start.114 = (f32[1024]{0:T(1024)}, f32[1024]{0:T(1024)S(1)}, u32[]{:S(2)}) copy-start(f32[1024]{0:T(1024)S(1)} %fusion.187) | copy-start | bytes 12292
  208.7 28.9 %copy-start.48 = (bf16[1024,6,16]{0,2,1:T(8,128)(2,1)}, bf16[1024,6,16]{0,2,1:T(8,128)(2,1)S(1)}, u32[]{:S(2)}) copy-start(bf16[1024,6,16]{0,2,1:T(8,128)(2,1)S(1)} %get-tuple-element.1246) | copy-start | bytes 589828
  209.8 96.3 %collective-permute-start.4 = (bf16[1024,6,64]{0,2,1:T(8,128)(2,1)}, bf16[1024,6,64]{0,2,1:T(8,128)(2,1)}, u32[]{:S(2)}, u32[]{:S(2)}) collective-permute-start(bf16[1024,6,64]{0,2,1:T(8,128)(2,1)} %pad_maximum_fusion.4), channel_id=1, source_target_pairs={{8,0},{12,4},{16,8},{20,12},{24,16},{28,20},{9,1},{13,5},{17,9},{2... | collective-permute-start | bytes 2359304 | tf_op jit(solution)/shard_map/ppermute | solution.py:40
  211.0 64.6 %collective-permute-start.3 = (bf16[1024,6,64]{0,2,1:T(8,128)(2,1)}, bf16[1024,6,64]{0,2,1:T(8,128)(2,1)}, u32[]{:S(2)}, u32[]{:S(2)}) collective-permute-start(bf16[1024,6,64]{0,2,1:T(8,128)(2,1)} %pad_maximum_fusion.4), channel_id=1, source_target_pairs={{4,0},{8,4},{12,8},{16,12},{20,16},{24,20},{28,24},{5,1},{9,5},{13... | collective-permute-start | bytes 2359304 | tf_op jit(solution)/shard_map/ppermute | solution.py:40
  212.3 62.0 %collective-permute-start.2 = (bf16[1024,6,64]{0,2,1:T(8,128)(2,1)}, bf16[1024,6,64]{0,2,1:T(8,128)(2,1)}, u32[]{:S(2)}, u32[]{:S(2)}) collective-permute-start(bf16[1024,6,64]{0,2,1:T(8,128)(2,1)} %pad_maximum_fusion.4), channel_id=1, source_target_pairs={{0,12},{4,16},{8,20},{12,24},{16,28},{1,13},{5,17},{9,21},{13,25},... | collective-permute-start | bytes 2359304 | tf_op jit(solution)/shard_map/ppermute | solution.py:40
  218.5 45.7 %collective-permute-start.1 = (bf16[1024,6,64]{0,2,1:T(8,128)(2,1)}, bf16[1024,6,64]{0,2,1:T(8,128)(2,1)}, u32[]{:S(2)}, u32[]{:S(2)}) collective-permute-start(bf16[1024,6,64]{0,2,1:T(8,128)(2,1)} %pad_maximum_fusion.4), channel_id=1, source_target_pairs={{0,8},{4,12},{8,16},{12,20},{16,24},{20,28},{1,9},{5,13},{9,17},{1... | collective-permute-start | bytes 2359304 | tf_op jit(solution)/shard_map/ppermute | solution.py:40
  223.0 42.5 %collective-permute-start = (bf16[1024,6,64]{0,2,1:T(8,128)(2,1)}, bf16[1024,6,64]{0,2,1:T(8,128)(2,1)}, u32[]{:S(2)}, u32[]{:S(2)}) collective-permute-start(bf16[1024,6,64]{0,2,1:T(8,128)(2,1)} %pad_maximum_fusion.4), channel_id=1, source_target_pairs={{0,4},{4,8},{8,12},{12,16},{16,20},{20,24},{24,28},{1,5},{5,9},{9,... | collective-permute-start | bytes 2359304 | tf_op jit(solution)/shard_map/ppermute | solution.py:40
  264.3 68.1 %collective-permute-start.5 = (bf16[1024,6,64]{0,2,1:T(8,128)(2,1)}, bf16[1024,6,64]{0,2,1:T(8,128)(2,1)}, u32[]{:S(2)}, u32[]{:S(2)}) collective-permute-start(bf16[1024,6,64]{0,2,1:T(8,128)(2,1)} %pad_maximum_fusion.4), channel_id=1, source_target_pairs={{12,0},{16,4},{20,8},{24,12},{28,16},{13,1},{17,5},{21,9},{25,13},... | collective-permute-start | bytes 2359304 | tf_op jit(solution)/shard_map/ppermute | solution.py:40
  265.6 127.6 %collective-permute-start.6 = (bf16[1024,6,64]{0,2,1:T(8,128)(2,1)}, bf16[1024,6,64]{0,2,1:T(8,128)(2,1)}, u32[]{:S(2)}, u32[]{:S(2)}) collective-permute-start(bf16[1024,6,64]{0,2,1:T(8,128)(2,1)} %bitcast.416), channel_id=1, source_target_pairs={{0,4},{4,8},{8,12},{12,16},{16,20},{20,24},{24,28},{1,5},{5,9},{9,... | collective-permute-start | bytes 2359304 | tf_op jit(solution)/shard_map/ppermute | solution.py:40
  274.3 163.5 %collective-permute-start.11 = (bf16[1024,6,64]{0,2,1:T(8,128)(2,1)}, bf16[1024,6,64]{0,2,1:T(8,128)(2,1)}, u32[]{:S(2)}, u32[]{:S(2)}) collective-permute-start(bf16[1024,6,64]{0,2,1:T(8,128)(2,1)} %bitcast.417), channel_id=1, source_target_pairs={{12,0},{16,4},{20,8},{24,12},{28,16},{13,1},{17,5},{21,9},{25,13},... | collective-permute-start | bytes 2359304 | tf_op jit(solution)/shard_map/ppermute | solution.py:40
  275.7 151.8 %collective-permute-start.10 = (bf16[1024,6,64]{0,2,1:T(8,128)(2,1)}, bf16[1024,6,64]{0,2,1:T(8,128)(2,1)}, u32[]{:S(2)}, u32[]{:S(2)}) collective-permute-start(bf16[1024,6,64]{0,2,1:T(8,128)(2,1)} %bitcast.418), channel_id=1, source_target_pairs={{8,0},{12,4},{16,8},{20,12},{24,16},{28,20},{9,1},{13,5},{17,9},{2... | collective-permute-start | bytes 2359304 | tf_op jit(solution)/shard_map/ppermute | solution.py:40
  306.0 103.3 %collective-permute-start.9 = (bf16[1024,6,64]{0,2,1:T(8,128)(2,1)}, bf16[1024,6,64]{0,2,1:T(8,128)(2,1)}, u32[]{:S(2)}, u32[]{:S(2)}) collective-permute-start(bf16[1024,6,64]{0,2,1:T(8,128)(2,1)} %bitcast.419), channel_id=1, source_target_pairs={{4,0},{8,4},{12,8},{16,12},{20,16},{24,20},{28,24},{5,1},{9,5},{13... | collective-permute-start | bytes 2359304 | tf_op jit(solution)/shard_map/ppermute | solution.py:40
  332.4 77.0 %collective-permute-start.8 = (bf16[1024,6,64]{0,2,1:T(8,128)(2,1)}, bf16[1024,6,64]{0,2,1:T(8,128)(2,1)}, u32[]{:S(2)}, u32[]{:S(2)}) collective-permute-start(bf16[1024,6,64]{0,2,1:T(8,128)(2,1)} %bitcast.420), channel_id=1, source_target_pairs={{0,12},{4,16},{8,20},{12,24},{16,28},{1,13},{5,17},{9,21},{13,25},... | collective-permute-start | bytes 2359304 | tf_op jit(solution)/shard_map/ppermute | solution.py:40
  393.1 16.2 collective-permute-start.7
  457.7 225.6 %copy-start.94 = (f32[1536]{0:T(1024)S(1)}, f32[1536]{0:T(1024)}, u32[]{:S(2)}) copy-start(f32[1536]{0:T(1024)} %get-tuple-element.1164) | copy-start | bytes 18436
  457.7 225.6 %copy-start.95 = (f32[1536]{0:T(1024)S(1)}, f32[1536]{0:T(1024)}, u32[]{:S(2)}) copy-start(f32[1536]{0:T(1024)} %get-tuple-element.1162) | copy-start | bytes 18436
  457.7 470.5 %all-reduce.28.cloned.1.call-start = ((), (), s32[]{:S(2)}) async-start(), calls=%async_computation.7 | async-start | bytes 12582912 | tf_op jit(solution)/shard_map/psum | solution.py:117
  706.3 480.4 %all-reduce.30.cloned.1.call-start = ((), (), s32[]{:S(2)}) async-start(), calls=%async_computation.8 | async-start | bytes 12582912 | tf_op jit(solution)/shard_map/psum | solution.py:117
  964.8 850.5 %all-gather.15.cloned.1.call-start = ((), (), s32[]{:S(2)}) async-start(), calls=%async_computation.15 | async-start | bytes 1769472 | tf_op jit(solution)/shard_map/all_gather | solution.py:18
  1234.7 586.1 %all-gather.13.cloned.1.call-start = ((), (), s32[]{:S(2)}) async-start(), calls=%async_computation.14 | async-start | bytes 1769472 | tf_op jit(solution)/shard_map/all_gather | solution.py:18
  1363.5 278.1 %collective-permute-start.18 = (bf16[1024,6,64]{0,2,1:T(8,128)(2,1)}, bf16[1024,6,64]{0,2,1:T(8,128)(2,1)}, u32[]{:S(2)}, u32[]{:S(2)}) collective-permute-start(bf16[1024,6,64]{0,2,1:T(8,128)(2,1)} %convert_element_type.462), channel_id=1, source_target_pairs={{4,0},{8,4},{12,8},{16,12},{20,16},{24,20},{28,24},{5,1},{9,5},{13... | collective-permute-start | bytes 2359304 | tf_op jit(solution)/shard_map/ppermute | solution.py:40
  1364.8 279.0 %collective-permute-start.12 = (bf16[1024,6,64]{0,2,1:T(8,128)(2,1)}, bf16[1024,6,64]{0,2,1:T(8,128)(2,1)}, u32[]{:S(2)}, u32[]{:S(2)}) collective-permute-start(bf16[1024,6,64]{0,2,1:T(8,128)(2,1)} %convert_element_type.450), channel_id=1, source_target_pairs={{4,0},{8,4},{12,8},{16,12},{20,16},{24,20},{28,24},{5,1},{9,5},{13... | collective-permute-start | bytes 2359304 | tf_op jit(solution)/shard_map/ppermute | solution.py:40
  1374.8 310.9 %collective-permute-start.19 = (bf16[1024,6,64]{0,2,1:T(8,128)(2,1)}, bf16[1024,6,64]{0,2,1:T(8,128)(2,1)}, u32[]{:S(2)}, u32[]{:S(2)}) collective-permute-start(bf16[1024,6,64]{0,2,1:T(8,128)(2,1)} %convert_element_type.464), channel_id=1, source_target_pairs={{8,0},{12,4},{16,8},{20,12},{24,16},{28,20},{9,1},{13,5},{17,9},{2... | collective-permute-start | bytes 2359304 | tf_op jit(solution)/shard_map/ppermute | solution.py:40
  1385.7 301.3 %collective-permute-start.20 = (bf16[1024,6,64]{0,2,1:T(8,128)(2,1)}, bf16[1024,6,64]{0,2,1:T(8,128)(2,1)}, u32[]{:S(2)}, u32[]{:S(2)}) collective-permute-start(bf16[1024,6,64]{0,2,1:T(8,128)(2,1)} %convert_element_type.466), channel_id=1, source_target_pairs={{12,0},{16,4},{20,8},{24,12},{28,16},{13,1},{17,5},{21,9},{25,13},... | collective-permute-start | bytes 2359304 | tf_op jit(solution)/shard_map/ppermute | solution.py:40
  1447.8 240.5 %collective-permute-start.21 = (bf16[1024,6,64]{0,2,1:T(8,128)(2,1)}, bf16[1024,6,64]{0,2,1:T(8,128)(2,1)}, u32[]{:S(2)}, u32[]{:S(2)}) collective-permute-start(bf16[1024,6,64]{0,2,1:T(8,128)(2,1)} %convert_element_type.468), channel_id=1, source_target_pairs={{0,4},{4,8},{8,12},{12,16},{16,20},{20,24},{24,28},{1,5},{5,9},{9,... | collective-permute-start | bytes 2359304 | tf_op jit(solution)/shard_map/ppermute | solution.py:40
  1641.6 48.9 %collective-permute-start.22 = (bf16[1024,6,64]{0,2,1:T(8,128)(2,1)}, bf16[1024,6,64]{0,2,1:T(8,128)(2,1)}, u32[]{:S(2)}, u32[]{:S(2)}) collective-permute-start(bf16[1024,6,64]{0,2,1:T(8,128)(2,1)} %convert_element_type.470), channel_id=1, source_target_pairs={{0,8},{4,12},{8,16},{12,20},{16,24},{20,28},{1,9},{5,13},{9,17},{1... | collective-permute-start | bytes 2359304 | tf_op jit(solution)/shard_map/ppermute | solution.py:40
  1643.8 52.0 %collective-permute-start.23 = (bf16[1024,6,64]{0,2,1:T(8,128)(2,1)}, bf16[1024,6,64]{0,2,1:T(8,128)(2,1)}, u32[]{:S(2)}, u32[]{:S(2)}) collective-permute-start(bf16[1024,6,64]{0,2,1:T(8,128)(2,1)} %convert_element_type.472), channel_id=1, source_target_pairs={{0,12},{4,16},{8,20},{12,24},{16,28},{1,13},{5,17},{9,21},{13,25},... | collective-permute-start | bytes 2359304 | tf_op jit(solution)/shard_map/ppermute | solution.py:40
  1675.4 315.0 %all-reduce.32.cloned.1.call-start = ((), (), s32[]{:S(2)}) async-start(), calls=%async_computation.9 | async-start | bytes 12582912 | tf_op jit(solution)/shard_map/psum | solution.py:117
  1685.7 31.7 %collective-permute-start.13 = (bf16[1024,6,64]{0,2,1:T(8,128)(2,1)}, bf16[1024,6,64]{0,2,1:T(8,128)(2,1)}, u32[]{:S(2)}, u32[]{:S(2)}) collective-permute-start(bf16[1024,6,64]{0,2,1:T(8,128)(2,1)} %convert_element_type.452), channel_id=1, source_target_pairs={{8,0},{12,4},{16,8},{20,12},{24,16},{28,20},{9,1},{13,5},{17,9},{2... | collective-permute-start | bytes 2359304 | tf_op jit(solution)/shard_map/ppermute | solution.py:40
  1687.0 38.6 %collective-permute-start.14 = (bf16[1024,6,64]{0,2,1:T(8,128)(2,1)}, bf16[1024,6,64]{0,2,1:T(8,128)(2,1)}, u32[]{:S(2)}, u32[]{:S(2)}) collective-permute-start(bf16[1024,6,64]{0,2,1:T(8,128)(2,1)} %convert_element_type.454), channel_id=1, source_target_pairs={{12,0},{16,4},{20,8},{24,12},{28,16},{13,1},{17,5},{21,9},{25,13},... | collective-permute-start | bytes 2359304 | tf_op jit(solution)/shard_map/ppermute | solution.py:40
  1688.3 37.3 %collective-permute-start.15 = (bf16[1024,6,64]{0,2,1:T(8,128)(2,1)}, bf16[1024,6,64]{0,2,1:T(8,128)(2,1)}, u32[]{:S(2)}, u32[]{:S(2)}) collective-permute-start(bf16[1024,6,64]{0,2,1:T(8,128)(2,1)} %convert_element_type.456), channel_id=1, source_target_pairs={{0,4},{4,8},{8,12},{12,16},{16,20},{20,24},{24,28},{1,5},{5,9},{9,... | collective-permute-start | bytes 2359304 | tf_op jit(solution)/shard_map/ppermute | solution.py:40
  1690.5 35.1 %collective-permute-start.16 = (bf16[1024,6,64]{0,2,1:T(8,128)(2,1)}, bf16[1024,6,64]{0,2,1:T(8,128)(2,1)}, u32[]{:S(2)}, u32[]{:S(2)}) collective-permute-start(bf16[1024,6,64]{0,2,1:T(8,128)(2,1)} %convert_element_type.458), channel_id=1, source_target_pairs={{0,8},{4,12},{8,16},{12,20},{16,24},{20,28},{1,9},{5,13},{9,17},{1... | collective-permute-start | bytes 2359304 | tf_op jit(solution)/shard_map/ppermute | solution.py:40
  1695.8 32.8 %collective-permute-start.17 = (bf16[1024,6,64]{0,2,1:T(8,128)(2,1)}, bf16[1024,6,64]{0,2,1:T(8,128)(2,1)}, u32[]{:S(2)}, u32[]{:S(2)}) collective-permute-start(bf16[1024,6,64]{0,2,1:T(8,128)(2,1)} %convert_element_type.460), channel_id=1, source_target_pairs={{0,12},{4,16},{8,20},{12,24},{16,28},{1,13},{5,17},{9,21},{13,25},... | collective-permute-start | bytes 2359304 | tf_op jit(solution)/shard_map/ppermute | solution.py:40
  1745.8 350.3 %reduce-scatter.11.cloned.1.call-start = ((), (), s32[]{:S(2)}) async-start(), calls=%async_computation.13 | async-start | bytes 3538944 | tf_op jit(solution)/shard_map/reduce_scatter | solution.py:428
  1753.5 350.2 %reduce-scatter.9.cloned.1.call-start = ((), (), s32[]{:S(2)}) async-start(), calls=%async_computation.12 | async-start | bytes 1327104 | tf_op jit(solution)/shard_map/reduce_scatter | solution.py:422
  1758.8 372.6 %reduce-scatter.13.cloned.1.call-start = ((), (), s32[]{:S(2)}) async-start(), calls=%async_computation.16 | async-start | bytes 3981312
  1814.8 459.7 %all-reduce.36.cloned.1.call-start = ((), (), s32[]{:S(2)}) async-start(), calls=%async_computation.17 | async-start | bytes 18874368
  2007.5 58.9 %copy-start.112 = (f32[1,1536]{1,0:T(1,128)S(1)}, f32[1,1536]{1,0:T(1,128)}, u32[]{:S(2)}) copy-start(f32[1,1536]{1,0:T(1,128)} %get-tuple-element.1262) | copy-start | bytes 18436
  2072.0 268.1 %reduce-scatter.7.cloned.1.call-start = ((), (), s32[]{:S(2)}) async-start(), calls=%async_computation.11 | async-start | bytes 7077888 | tf_op jit(solution)/shard_map/reduce_scatter | solution.py:419
  2092.9 336.5 %all-reduce.34.cloned.1.call-start = ((), (), s32[]{:S(2)}) async-start(), calls=%async_computation.10 | async-start | bytes 4194304 | tf_op jit(solution)/shard_map/psum | solution.py:406
  2100.0 37.9 %copy-start.125 = (f32[1536]{0:T(1024)S(1)}, f32[1536]{0:T(1024)}, u32[]{:S(2)}) copy-start(f32[1536]{0:T(1024)} %get-tuple-element.1147) | copy-start | bytes 18436
  2140.9 64.2 %copy-start.99 = (f32[1536]{0:T(1024)S(1)}, f32[1536]{0:T(1024)}, u32[]{:S(2)}) copy-start(f32[1536]{0:T(1024)} %copy-done.97) | copy-start | bytes 18436
  (124 other events, 1038.9 us)
Sparse Core Ops, SparseCore 0:
  20.2 28.4 all-gather.10
  51.1 25.7 all-gather.8
  457.8 221.9 all-reduce.25
  706.4 221.7 all-reduce.27
  964.9 221.7 all-reduce.29
  1234.8 24.7 all-gather.14
  1675.5 27.3 all-gather.12
  1745.9 244.4 all-reduce.31
  1993.8 45.1 reduce-scatter.10
  2043.0 36.7 reduce-scatter.8
  2083.3 48.0 reduce-scatter.12
  2134.9 139.5 all-reduce.35
  2278.3 61.8 reduce-scatter.6
  2342.9 86.4 all-reduce.33
where the time goes:
time: 2450 us; the launch traced here: 2440 us
  waiting for transfers between devices  1080 us (44%)
  matrix products  527 us (22%)
  other arithmetic  334 us (14%)
  local copies, waits for them, and re-layouts  189 us (8%)
  starting transfers between devices  157 us (6%)
  blocking collectives  94.5 us (4%)
  loops' own time  28.6 us (1%)
  between operations  24.5 us (1%)
    psum x4, waiting for transfers between devices, narrow_total(): return lax.psum(partial_sum, 'narrow')  830 us
    ppermute x24, starting transfers between devices, shifted(): return lax.ppermute(x, axis, pairs)  155 us
    dot_general x10, matrix products, block_scores(): jnp.einsum('qhd,khd->hqk', query_low, key_heads, preferred_element_type=j...  129 us
    unnamed x16, waiting for transfers between devices  87.2 us
    psum x1, waiting for transfers between devices, local(): lax.psum(d_text_part.astype(jnp.bfloat16), 'narrow').astype(jnp.float32)  86.8 us
    select_n x32, other arithmetic, step(): return jax.tree.map(lambda a, b: jnp.where(reached, a, b), new, before)  85.4 us
    dot_general x4, matrix products, grad_terms(): jnp.einsum('qhd,khd->hqk', d_self_out, kv_pair[1], preferred_element_type...  65 us
    unnamed x251, local copies, waits for them, and re-layouts  63.3 us
  transfers between devices with their start and end apart: 38, of which 11 were waited for; matrix products, arithmetic and copies ran while one was open for 32% of the time, Pallas kernels for 0%

commit v1 on v0

v1 whole, which is shorter than its diff:
```python
import functools

import jax
import jax.numpy as jnp
from jax import lax
from jax.experimental import pallas as pl
from jax.experimental.pallas import tpu as pltpu
from jax.sharding import PartitionSpec as P

HD = 64
SPAN = 4
EPS = 1e-05
LOG2E = 1.4426950408889634
f32 = jnp.float32
bf16 = jnp.bfloat16
VMEM = 56 * 1024 * 1024
NT = (((1,), (1,)), ((), ()))
TN = (((0,), (0,)), ((), ()))


def params(n):
    return pltpu.CompilerParams(
        dimension_semantics=("arbitrary",) * n, vmem_limit_bytes=VMEM
    )


def sds(shape, dtype):
    return jax.ShapeDtypeStruct(shape, dtype)


def mm(a, b):
    return jnp.dot(a, b, preferred_element_type=f32)


def mm_nt(a, b):
    return lax.dot_general(a, b, NT, preferred_element_type=f32)


def mm_tn(a, b):
    return lax.dot_general(a, b, TN, preferred_element_type=f32)


def split(x):
    hi = x.astype(bf16)
    return hi, (x - hi.astype(f32)).astype(bf16)


def head_sum(x, ones):
    hi, lo = split(x)
    return mm(hi, ones) + mm(lo, ones)


def head_ones(n):
    a = lax.broadcasted_iota(jnp.int32, (n, n), 0) // HD
    b = lax.broadcasted_iota(jnp.int32, (n, n), 1) // HD
    return (a == b).astype(bf16)


def halves(n):
    lane = lax.broadcasted_iota(jnp.int32, (1, n), 1)
    return (lane < HD, lane >= HD)


def keep(x, mask):
    return jnp.where(mask, x, jnp.zeros_like(x))


def inv_rms(x):
    return lax.rsqrt(jnp.mean(x * x, -1, keepdims=True) + EPS)


def row(ref, k):
    return ref[k : k + 1, :]


def whole(shape):
    zeros = (0,) * len(shape)
    return pl.BlockSpec(shape, lambda *_: zeros, pipeline_mode=pl.Buffered(1))


def rows_of(br, width, first=0):
    return pl.BlockSpec((br, width), lambda i, *_: (i, first))


def accumulate(ref, value, first):
    @pl.when(first)
    def _():
        ref[...] = value

    @pl.when(jnp.logical_not(first))
    def _():
        ref[...] += value


def col_sum(x):
    return jnp.sum(x, 0, keepdims=True)


def tile3(t, n):
    return jnp.concatenate([t] * (n // t.shape[1]), 1)


def qkv_kernel(p_ref, v_ref, w_ref, c_ref, s1_ref, s2_ref, hg_ref, a_ref, qr_ref, kr_ref, q_ref, k_ref, vv_ref):
    x = p_ref[...].astype(f32)
    a = (x * inv_rms(x) * row(v_ref, 0)).astype(bf16)
    a_ref[...] = a
    n = q_ref.shape[1]
    ones = head_ones(n)
    cos, s1, s2 = (tile3(t[...], n) for t in (c_ref, s1_ref, s2_ref))

    def turned(y, gain):
        z = y * lax.rsqrt(head_sum(y * y, ones) * (1.0 / HD) + EPS) * gain
        return z * cos + pltpu.roll(z, n - 16, 1) * s1 + pltpu.roll(z, 16, 1) * s2

    q = mm(a, w_ref[0])
    qr_ref[...] = q
    q_ref[...] = (turned(q, row(hg_ref, 0)) * (0.125 * LOG2E)).astype(bf16)
    k = mm(a, w_ref[1])
    kr_ref[...] = k
    k_ref[...] = turned(k, row(hg_ref, 1)).astype(bf16)
    vv_ref[...] = mm(a, w_ref[2]).astype(bf16)


def qkv_call(patches, vec, w, tabs, hg, br=256):
    t, d = patches.shape
    n = w.shape[2]
    return pl.pallas_call(
        qkv_kernel,
        grid=(t // br,),
        in_specs=[rows_of(br, d), whole(vec.shape), whole(w.shape)]
        + [rows_of(br, 128)] * 3
        + [whole(hg.shape)],
        out_specs=[rows_of(br, d)] + [rows_of(br, n)] * 5,
        out_shape=[sds((t, d), bf16), sds((t, n), f32), sds((t, n), f32)] + [sds((t, n), bf16)] * 3,
        compiler_params=params(1),
        name="qkv",
    )(patches, vec, w, *tabs, hg)


def dqkv_kernel(dq_ref, dk_ref, dv_ref, qr_ref, kr_ref, c_ref, s1_ref, s2_ref, hg_ref, w_ref, p_ref, g_ref, sc_ref, d_ref, da_ref, hs_ref, cs_ref):
    n = dq_ref.shape[1]
    first = pl.program_id(0) == 0
    ones = head_ones(n)
    cos, s1, s2 = (tile3(t[...], n) for t in (c_ref, s1_ref, s2_ref))

    def back(dy, x, gain):
        dz = dy * cos - pltpu.roll(dy, 16, 1) * s2 - pltpu.roll(dy, n - 16, 1) * s1
        r = lax.rsqrt(head_sum(x * x, ones) * (1.0 / HD) + EPS)
        xh = x * r
        g = dz * gain
        return r * (g - xh * (head_sum(g * xh, ones) * (1.0 / HD))), col_sum(dz * xh)

    dq, hq = back(dq_ref[...], qr_ref[...], row(hg_ref, 0))
    dk, hk = back(dk_ref[...], kr_ref[...], row(hg_ref, 1))
    dql, dkl, dvl = dq.astype(bf16), dk.astype(bf16), dv_ref[...].astype(bf16)
    d_ref[:, :n] = dql
    d_ref[:, n : 2 * n] = dkl
    d_ref[:, 2 * n :] = dvl
    da = mm_nt(dql, w_ref[0]) + mm_nt(dkl, w_ref[1]) + mm_nt(dvl, w_ref[2])
    da_ref[...] = da.astype(bf16)
    x = p_ref[...].astype(f32)
    accumulate(cs_ref, col_sum(da * (x * inv_rms(x))), first)
    accumulate(hs_ref, jnp.concatenate([hq, hk], 0), first)


def dqkv_call(dq, dk, dv, qr, kr, tabs, hg, w, patches, g, sc, br=256):
    t, n = dq.shape
    d = patches.shape[1]
    return pl.pallas_call(
        dqkv_kernel,
        grid=(t // br,),
        in_specs=[rows_of(br, n)] * 5
        + [rows_of(br, 128)] * 3
        + [whole(hg.shape), whole(w.shape), rows_of(br, d), whole(g.shape), whole(sc.shape)],
        out_specs=[rows_of(br, 3 * n), rows_of(br, d), pl.BlockSpec((2, n), lambda i: (0, 0)), pl.BlockSpec((1, d), lambda i: (0, 0))],
        out_shape=[sds((t, 3 * n), bf16), sds((t, d), bf16), sds((2, n), f32), sds((1, d), f32)],
        compiler_params=params(1),
        name="dqkv",
    )(dq, dk, dv, qr, kr, *tabs, hg, w, patches, g, sc)


def soft_sums(q, k, v, mask):
    e = jnp.exp2(mm_nt(q, keep(k, mask))).astype(bf16)
    return mm(e, jnp.where(mask, v, jnp.ones_like(v)))


def attend_kernel(sc, q_ref, k_ref, v_ref, ck_ref, cv_ref, tg_ref, mix_ref, o_ref, li_ref, acc):
    j = pl.program_id(2)
    masks = halves(128)
    keys = 512

    @pl.when(j == 0)
    def _():
        acc[...] = jnp.zeros_like(acc)

    @pl.when(j < sc[0])
    def _():
        q = q_ref[...]
        for h in range(2):
            total = acc[h]
            for c in range(k_ref.shape[0] // keys):
                at = slice(c * keys, (c + 1) * keys)
                total = total + soft_sums(q, k_ref[at, :], v_ref[at, :], masks[h])
            acc[h] = total

    @pl.when(j == SPAN - 1)
    def _():
        q = q_ref[...]

        def finish(a0, a1):
            inverse = 1.0 / jnp.where(masks[0], pltpu.roll(a0, HD, 1), pltpu.roll(a1, HD, 1))
            return jnp.where(masks[0], a0, a1) * inverse, inverse

        o, li = finish(acc[0], acc[1])
        c0, c1 = (soft_sums(q, ck_ref[...], cv_ref[...], m) for m in masks)
        mix_ref[...] = (o + tg_ref[...] * finish(c0, c1)[0]).astype(bf16)
        o_ref[...] = o.astype(bf16)
        li_ref[...] = li


def attend_call(sc, q, k, v, cap, tg, block, bq=512):
    t, n = q.shape
    pairs = n // 128
    text = 256
    mine = lambda p, i, j, s: (i, p)
    return pl.pallas_call(
        attend_kernel,
        grid_spec=pltpu.PrefetchScalarGridSpec(
            num_scalar_prefetch=1,
            grid=(pairs, t // bq, SPAN),
            in_specs=[
                pl.BlockSpec((bq, 128), mine),
                pl.BlockSpec((block, 128), lambda p, i, j, s: (s[2 + j], p)),
                pl.BlockSpec((block, 128), lambda p, i, j, s: (s[2 + j], p)),
                pl.BlockSpec((text, 128), lambda p, i, j, s: (s[1], p)),
                pl.BlockSpec((text, 128), lambda p, i, j, s: (s[1], pairs + p)),
                pl.BlockSpec((1, 128), lambda p, i, j, s: (0, p)),
            ],
            out_specs=[pl.BlockSpec((bq, 128), mine)] * 3,
            scratch_shapes=[pltpu.VMEM((2, bq, 128), f32)],
        ),
        out_shape=[sds((t, n), bf16), sds((t, n), bf16), sds((t, n), f32)],
        compiler_params=params(3),
        name="attend",
    )(sc, q, k, v, cap, cap, tg)


def caption_back_kernel(sc, q_ref, d_ref, ck_ref, cv_ref, tg_ref, dq_ref, dk_ref, dv_ref, gs_ref):
    first = pl.program_id(1) == 0
    masks = halves(128)
    q, d = q_ref[...], d_ref[...]
    dq = jnp.zeros(q.shape, f32)
    dk = jnp.zeros(ck_ref.shape, f32)
    dv = jnp.zeros(ck_ref.shape, f32)
    sums = []
    for h in range(2):
        ck, cv = keep(ck_ref[...], masks[h]), keep(cv_ref[...], masks[h])
        gate = tg_ref[:, h * HD : h * HD + 1]
        e = jnp.exp2(mm_nt(q, ck))
        prob = e * (1.0 / jnp.sum(e, -1, keepdims=True))
        dp = mm_nt(d, cv)
        m = jnp.sum(prob * dp, -1, keepdims=True)
        dc = (prob * (dp - m) * gate).astype(bf16)
        dq = dq + mm(dc, ck)
        dk = dk + mm_tn(dc, keep(q, masks[h]))
        dv = dv + mm_tn(prob.astype(bf16), keep(d, masks[h]))
        sums.append(jnp.sum(m, 0, keepdims=True))
    dq_ref[...] = dq * 0.125
    accumulate(dk_ref, dk * (1.0 / LOG2E), first)
    accumulate(dv_ref, dv * tg_ref[...], first)
    accumulate(gs_ref, jnp.where(masks[0], sums[0], sums[1]), first)


def caption_back_call(sc, q, d, cap, tg, bq=512):
    t, n = q.shape
    pairs = n // 128
    text = 256
    mine = lambda p, i, s: (i, p)
    held = lambda p, i, s: (0, p)
    return pl.pallas_call(
        caption_back_kernel,
        grid_spec=pltpu.PrefetchScalarGridSpec(
            num_scalar_prefetch=1,
            grid=(pairs, t // bq),
            in_specs=[
                pl.BlockSpec((bq, 128), mine),
                pl.BlockSpec((bq, 128), mine),
                pl.BlockSpec((text, 128), lambda p, i, s: (s[1], p)),
                pl.BlockSpec((text, 128), lambda p, i, s: (s[1], pairs + p)),
                pl.BlockSpec((1, 128), held),
            ],
            out_specs=[
                pl.BlockSpec((bq, 128), mine),
                pl.BlockSpec((text, 128), held),
                pl.BlockSpec((text, 128), held),
                pl.BlockSpec((1, 128), held),
            ],
        ),
        out_shape=[sds((t, n), f32), sds((text, n), f32), sds((text, n), f32), sds((1, n), f32)],
        compiler_params=params(2),
        name="caption_back",
    )(sc, q, d, cap, cap, tg)


def dq_kernel(sc, q_ref, d_ref, dl_ref, k_ref, v_ref, c_ref, dq_ref, acc):
    j = pl.program_id(2)
    masks = halves(128)
    keys = 512

    @pl.when(j == 0)
    def _():
        acc[...] = jnp.zeros_like(acc)

    @pl.when(j < sc[0])
    def _():
        q, d = q_ref[...], d_ref[...]
        total = acc[...]
        for c in range(k_ref.shape[0] // keys):
            at = slice(c * keys, (c + 1) * keys)
            for h in range(2):
                k = keep(k_ref[at, :], masks[h])
                e = jnp.exp2(mm_nt(q, k))
                dp = mm_nt(d, keep(v_ref[at, :], masks[h]))
                ds = (e * (dp - dl_ref[:, h * HD : h * HD + 1])).astype(bf16)
                total = total + mm(ds, k)
        acc[...] = total

    @pl.when(j == SPAN - 1)
    def _():
        dq_ref[...] = acc[...] * 0.125 + c_ref[...]


def dq_call(sc, q, d, dl, k, v, cap_dq, block, bq=512):
    t, n = q.shape
    pairs = n // 128
    mine = lambda p, i, j, s: (i, p)
    other = lambda p, i, j, s: (s[2 + j], p)
    return pl.pallas_call(
        dq_kernel,
        grid_spec=pltpu.PrefetchScalarGridSpec(
            num_scalar_prefetch=1,
            grid=(pairs, t // bq, SPAN),
            in_specs=[pl.BlockSpec((bq, 128), mine)] * 3
            + [pl.BlockSpec((block, 128), other)] * 2
            + [pl.BlockSpec((bq, 128), mine)],
            out_specs=pl.BlockSpec((bq, 128), mine),
            scratch_shapes=[pltpu.VMEM((bq, 128), f32)],
        ),
        out_shape=sds((t, n), f32),
        compiler_params=params(3),
        name="dq",
    )(sc, q, d, dl, k, v, cap_dq)


def dkv_kernel(sc, k_ref, v_ref, q_ref, d_ref, dl_ref, dk_ref, dv_ref, acc):
    pair = pl.program_id(0)
    j = pl.program_id(2)
    masks = halves(128)
    queries = 512

    @pl.when(j == 0)
    def _():
        acc[...] = jnp.zeros_like(acc)

    @pl.when(j < sc[0])
    def _():
        k, v = k_ref[...], v_ref[...]
        dk, dv = acc[0], acc[1]
        for h in range(2):
            km, vm = keep(k, masks[h]), keep(v, masks[h])
            delta = dl_ref[0, pl.ds(2 * pair + h, 1), :]
            for c in range(q_ref.shape[0] // queries):
                at = slice(c * queries, (c + 1) * queries)
                q, d = q_ref[at, :], d_ref[at, :]
                e = jnp.exp2(mm_nt(km, q))
                ds = (e * (mm_nt(vm, d) - delta[:, at])).astype(bf16)
                dv = dv + mm(e.astype(bf16), keep(d, masks[h]))
                dk = dk + mm(ds, keep(q, masks[h]))
        acc[0] = dk
        acc[1] = dv

    @pl.when(j == SPAN - 1)
    def _():
        dk_ref[...] = acc[0] * (1.0 / LOG2E)
        dv_ref[...] = acc[1]


def dkv_call(sc, k, v, q, d, dl, block, bk=512):
    t, n = k.shape
    pairs = n // 128
    mine = lambda p, i, j, s: (i, p)
    other = lambda p, i, j, s: (s[2 + j], p)
    return pl.pallas_call(
        dkv_kernel,
        grid_spec=pltpu.PrefetchScalarGridSpec(
            num_scalar_prefetch=1,
            grid=(pairs, t // bk, SPAN),
            in_specs=[pl.BlockSpec((bk, 128), mine)] * 2
            + [pl.BlockSpec((block, 128), other)] * 2
            + [pl.BlockSpec((1, dl.shape[1], block), lambda p, i, j, s: (s[2 + j], 0, 0))],
            out_specs=[pl.BlockSpec((bk, 128), mine)] * 2,
            scratch_shapes=[pltpu.VMEM((2, bk, 128), f32)],
        ),
        out_shape=[sds((t, n), f32)] * 2,
        compiler_params=params(3),
        name="dkv",
    )(sc, k, v, q, d, dl)


def ffn_kernel(p_ref, at_ref, v_ref, wg_ref, wd_ref, mid_ref, a_ref, gu_ref, h_ref, f_ref):
    at = at_ref[...].astype(f32)
    mid = p_ref[...].astype(f32) + row(v_ref, 1) * (at * inv_rms(at))
    mid_ref[...] = mid
    a = (mid * inv_rms(mid) * row(v_ref, 2)).astype(bf16)
    a_ref[...] = a
    g = mm(a, wg_ref[0])
    u = mm(a, wg_ref[1])
    n = g.shape[1]
    gu_ref[:, :n] = g.astype(bf16)
    gu_ref[:, n:] = u.astype(bf16)
    h = (g * jax.nn.sigmoid(g) * u).astype(bf16)
    h_ref[...] = h
    f_ref[...] = mm(h, wd_ref[...]).astype(bf16)


def ffn_call(patches, at, vec, wg, wd, br=256):
    t, d = patches.shape
    n = wd.shape[0]
    return pl.pallas_call(
        ffn_kernel,
        grid=(t // br,),
        in_specs=[rows_of(br, d), rows_of(br, d), whole(vec.shape), whole(wg.shape), whole(wd.shape)],
        out_specs=[rows_of(br, d), rows_of(br, d), rows_of(br, 2 * n), rows_of(br, n), rows_of(br, d)],
        out_shape=[sds((t, d), f32), sds((t, d), bf16), sds((t, 2 * n), bf16), sds((t, n), bf16), sds((t, d), bf16)],
        compiler_params=params(1),
        name="ffn",
    )(patches, at, vec, wg, wd)


def ffn_back_kernel(f_ref, mid_ref, c_ref, gu_ref, v_ref, wg_ref, wd_ref, y_ref, df_ref, dgu_ref, da_ref, cs_ref):
    f = f_ref[...].astype(f32)
    cot = c_ref[...].astype(f32)
    r = inv_rms(f)
    fh = f * r
    y_ref[...] = (mid_ref[...] + row(v_ref, 3) * fh).astype(bf16)
    z = cot * row(v_ref, 3)
    df = (r * (z - fh * jnp.mean(z * fh, -1, keepdims=True))).astype(bf16)
    df_ref[...] = df
    accumulate(cs_ref, col_sum(cot * fh), pl.program_id(0) == 0)
    dh = mm_nt(df, wd_ref[...])
    n = dh.shape[1]
    g = gu_ref[:, :n].astype(f32)
    u = gu_ref[:, n:].astype(f32)
    s = jax.nn.sigmoid(g)
    gs = g * s
    dg = (dh * u * (s + gs * (1.0 - s))).astype(bf16)
    du = (dh * gs).astype(bf16)
    dgu_ref[:, :n] = dg
    dgu_ref[:, n:] = du
    da_ref[...] = (mm_nt(dg, wg_ref[0]) + mm_nt(du, wg_ref[1])).astype(bf16)


def ffn_back_call(f, mid, cot, gu, vec, wg, wd, br=256):
    t, d = f.shape
    n = wd.shape[0]
    return pl.pallas_call(
        ffn_back_kernel,
        grid=(t // br,),
        in_specs=[rows_of(br, d), rows_of(br, d), rows_of(br, d), rows_of(br, 2 * n), whole(vec.shape), whole(wg.shape), whole(wd.shape)],
        out_specs=[rows_of(br, d), rows_of(br, d), rows_of(br, 2 * n), rows_of(br, d), pl.BlockSpec((1, d), lambda i: (0, 0))],
        out_shape=[sds((t, d), bf16), sds((t, d), bf16), sds((t, 2 * n), bf16), sds((t, d), bf16), sds((1, d), f32)],
        compiler_params=params(1),
        name="ffn_back",
    )(f, mid, cot, gu, vec, wg, wd)


def out_back_kernel(da_ref, mid_ref, at_ref, c_ref, v_ref, w_ref, o_ref, li_ref, dm_ref, dat_ref, dx_ref, ds_ref, dc_ref, dr_ref, c3_ref, c2_ref):
    first = pl.program_id(0) == 0
    da = da_ref[...].astype(f32)
    mid = mid_ref[...]
    r = inv_rms(mid)
    mh = mid * r
    z = da * row(v_ref, 2)
    dm = c_ref[...].astype(f32) + r * (z - mh * jnp.mean(z * mh, -1, keepdims=True))
    dm_ref[...] = dm
    accumulate(c3_ref, col_sum(da * mh), first)
    at = at_ref[...].astype(f32)
    ra = inv_rms(at)
    ah = at * ra
    accumulate(c2_ref, col_sum(dm * ah), first)
    z = dm * row(v_ref, 1)
    dat = (ra * (z - ah * jnp.mean(z * ah, -1, keepdims=True))).astype(bf16)
    dat_ref[...] = dat
    dx = mm_nt(dat, w_ref[...]).astype(bf16)
    dx_ref[...] = dx
    n = dx.shape[1]
    ds = dx.astype(f32) * li_ref[...]
    ds_ref[...] = ds.astype(bf16)
    prod = ds * o_ref[...].astype(f32)
    dc_ref[...] = head_sum(prod, head_ones(n))
    hi, lo = split(prod)
    a = lax.broadcasted_iota(jnp.int32, (8, n), 0)
    b = lax.broadcasted_iota(jnp.int32, (8, n), 1) // HD
    sel = (a == b).astype(bf16)
    dr_ref[...] = mm_nt(sel, hi) + mm_nt(sel, lo)


def out_back_call(da, mid, at, cot, vec, w, o, li, br=256):
    t, d = da.shape
    n = w.shape[0]
    one = pl.BlockSpec((1, d), lambda i: (0, 0))
    return pl.pallas_call(
        out_back_kernel,
        grid=(t // br,),
        in_specs=[rows_of(br, d)] * 4 + [whole(vec.shape), whole(w.shape), rows_of(br, n), rows_of(br, n)],
        out_specs=[rows_of(br, d), rows_of(br, d), rows_of(br, n), rows_of(br, n), rows_of(br, n), pl.BlockSpec((8, br), lambda i: (0, i)), one, one],
        out_shape=[sds((t, d), f32), sds((t, d), bf16), sds((t, n), bf16), sds((t, n), bf16), sds((t, n), f32), sds((8, t), f32), sds((1, d), f32), sds((1, d), f32)],
        compiler_params=params(1),
        name="out_back",
    )(da, mid, at, cot, vec, w, o, li)


def last_kernel(da_ref, p_ref, dm_ref, v_ref, o_ref):
    x = p_ref[...].astype(f32)
    r = inv_rms(x)
    xh = x * r
    z = da_ref[...].astype(f32) * row(v_ref, 0)
    o_ref[...] = (dm_ref[...] + r * (z - xh * jnp.mean(z * xh, -1, keepdims=True))).astype(bf16)


def last_call(da, patches, dm, vec, br=256):
    t, d = da.shape
    return pl.pallas_call(
        last_kernel,
        grid=(t // br,),
        in_specs=[rows_of(br, d)] * 3 + [whole(vec.shape)],
        out_specs=rows_of(br, d),
        out_shape=sds((t, d), bf16),
        compiler_params=params(1),
        name="last",
    )(da, patches, dm, vec)


def caption_grad_kernel(dk_ref, dv_ref, kr_ref, hg_ref, d_ref, hs_ref):
    n = dk_ref.shape[1]
    ones = head_ones(n)
    x = kr_ref[...]
    r = lax.rsqrt(head_sum(x * x, ones) * (1.0 / HD) + EPS)
    xh = x * r
    dy = dk_ref[...]
    g = dy * row(hg_ref, 2)
    d_ref[:, :n] = (r * (g - xh * (head_sum(g * xh, ones) * (1.0 / HD)))).astype(bf16)
    d_ref[:, n:] = dv_ref[...].astype(bf16)
    hs_ref[...] = col_sum(dy * xh)


def caption_norm_kernel(kr_ref, v_ref, hg_ref, o_ref):
    n = kr_ref.shape[1]
    x = kr_ref[...]
    r = lax.rsqrt(head_sum(x * x, head_ones(n)) * (1.0 / HD) + EPS)
    o_ref[:, :n] = (x * r * row(hg_ref, 2)).astype(bf16)
    o_ref[:, n:] = v_ref[...].astype(bf16)


def xor_gather(x):
    half = x.shape[0] // 2
    swap = lambda a, m: lax.ppermute(a, "wide", [(i, i ^ m) for i in range(8)])
    a, b = x[:half], x[half:]
    ra, rb = swap(a, 2), swap(b, 4)
    a4, a6 = swap(a, 4), swap(ra, 4)
    b2, b6 = swap(b, 2), swap(rb, 2)
    parts = [x, None, jnp.concatenate([ra, b2]), None, jnp.concatenate([a4, rb]), None, jnp.concatenate([a6, b6]), None]
    for m in (0, 2, 4, 6):
        parts[m + 1] = swap(parts[m], 1)
    return jnp.concatenate(parts)


def gather_wide(x, place):
    if lax.axis_size("wide") == 8:
        return xor_gather(x)
    return lax.all_gather(x, "wide", axis=0, tiled=True)


def narrow_sum(x):
    return lax.psum(x, "narrow")


def scatter_rows(x):
    return lax.psum_scatter(x.astype(bf16), "wide", scatter_dimension=0, tiled=True)


def rope_tables(position, width):
    lane = jnp.arange(128, dtype=jnp.int32)
    within = lane % HD
    quarter = HD // 4
    frequency = 10000.0 ** (-(within % quarter).astype(f32) / quarter)
    by_row = within < HD // 2
    where = jnp.where(by_row[None, :], (position // width)[:, None], (position % width)[:, None])
    angle = where.astype(f32) * frequency[None, :]
    cos, sin = jnp.cos(angle), jnp.sin(angle)
    former = (within % (HD // 2) < quarter)[None, :]
    return cos, jnp.where(former, -sin, 0.0), jnp.where(former, 0.0, sin)


def local(
    patches,
    cotangent,
    conditioning,
    captions,
    item_lengths,
    grid_widths,
    w_ada,
    norm_gains,
    w_qkv,
    head_gains,
    cross_gate,
    w_caption,
    w_out,
    w_gate_up,
    w_down,
):
    t, d = patches.shape
    n = w_qkv.shape[2]
    heads = n // HD
    ada = w_ada.shape[2]
    ff = w_down.shape[0]
    text = captions.shape[0]
    cd = conditioning.shape[1]
    count = lax.axis_size("wide")
    deep = lax.axis_size("narrow")
    me = lax.axis_index("wide")
    mz = lax.axis_index("narrow")

    slots = item_lengths.shape[0]
    spans = item_lengths // t
    order = jnp.arange(slots, dtype=jnp.int32)
    ends = jnp.sum(jnp.where(order[None, :] <= order[:, None], spans[None, :], 0), 1)
    blocks = jnp.arange(count, dtype=jnp.int32)
    item = jnp.sum((ends[None, :] <= blocks[:, None]).astype(jnp.int32), 1)
    is_item = item[:, None] == order[None, :]
    pick = lambda values: jnp.sum(jnp.where(is_item, values[None, :], 0), 1)
    firsts = pick(ends - spans)
    mine = blocks == me
    of_me = lambda values: jnp.sum(jnp.where(mine, values, 0))
    first = of_me(firsts)
    length = of_me(pick(spans))
    width = of_me(pick(grid_widths))
    position = (me - first) * t + jnp.arange(t, dtype=jnp.int32)
    tabs = rope_tables(position, width)
    steps = first + jnp.minimum(jnp.arange(SPAN, dtype=jnp.int32), length - 1)
    if count == 8:
        steps = steps ^ me
    sc = jnp.concatenate([jnp.stack([length, first]), steps]).astype(jnp.int32)

    cond = conditioning.astype(f32)[0]
    silu_low = jax.nn.silu(cond).astype(bf16)
    mod = jnp.sum(silu_low.astype(f32)[:, None, None] * w_ada.astype(f32), 0)
    share = cd // deep
    sent = jnp.concatenate([mod.reshape(-1), lax.dynamic_slice_in_dim(cond, mz * share, share)])
    got = lax.all_gather(lax.all_gather(sent, "narrow"), "wide")
    mods = got[:, :, : 4 * ada].reshape(count, deep, 4, ada).transpose(0, 2, 1, 3).reshape(count, 4, d)
    conds = got[:, :, 4 * ada :].reshape(count, cd)
    my_mod = lax.dynamic_index_in_dim(mods, first, 0, False)
    of_block = jnp.sum(jnp.where((firsts[:, None] == blocks[None, :])[:, :, None, None], mods[None], 0.0), 1)
    scales = 1.0 + of_block
    gates = jnp.tanh(of_block)
    factor = jnp.stack([1.0 + my_mod[0], jnp.tanh(my_mod[1]), 1.0 + my_mod[2], jnp.tanh(my_mod[3])])
    vec = norm_gains * factor
    hg = jnp.tile(head_gains, (1, heads))
    tg_heads = jnp.tanh(cross_gate)
    tg = jnp.repeat(tg_heads, HD)[None, :]

    cap_raw = jnp.einsum("kd,jde->jke", captions, w_caption, preferred_element_type=f32)
    cap_own = pl.pallas_call(
        caption_norm_kernel,
        out_shape=sds((text, 2 * n), bf16),
        compiler_params=params(0),
        name="caption_norm",
    )(cap_raw[0], cap_raw[1], hg)
    cap = lax.all_gather(cap_own, "wide", axis=0, tiled=True)

    a1, q_raw, k_raw, q, k, v = qkv_call(patches, vec, w_qkv, tabs, hg)
    k_all = gather_wide(k, me)
    v_all = gather_wide(v, me)
    q_all = gather_wide(q, me)
    mixed, o_self, linv = attend_call(sc, q, k_all, v_all, cap, tg, t)
    attn = narrow_sum(mm(mixed, w_out).astype(bf16))

    mid, a3, gu, hidden, ffn_part = ffn_call(patches, attn, vec, w_gate_up, w_down)
    ffn = narrow_sum(ffn_part)
    output, d_ffn, d_gu, da3_part, c4 = ffn_back_call(ffn, mid, cotangent, gu, vec, w_gate_up, w_down)
    da3 = narrow_sum(da3_part)
    g_down = scatter_rows(mm_tn(d_ffn, hidden))
    g_gu = scatter_rows(mm_tn(a3, d_gu))

    d_mid, d_attn, d_mixed, d_scaled, delta, delta_row, c3, c2 = out_back_call(
        da3, mid, attn, cotangent, vec, w_out, o_self, linv
    )
    d_all = gather_wide(d_scaled, me)
    if count == 8:
        delta_all = lax.all_gather(delta_row, "wide")
        delta_all = jnp.stack([lax.dynamic_index_in_dim(delta_all, me ^ m, 0, False) for m in range(8)])
    else:
        delta_all = lax.all_gather(delta_row, "wide")
    dq_cap, dck, dcv, gate_sum = caption_back_call(sc, q, d_mixed, cap, tg)
    cap_sent = jnp.concatenate([dck, dcv], 1).astype(bf16)
    cap_got = lax.all_gather(cap_sent, "wide")
    cap_total = jnp.sum(jnp.where((firsts == me)[:, None, None], cap_got.astype(f32), 0.0), 0)
    dq = dq_call(sc, q, d_scaled, delta, k_all, v_all, dq_cap, t)
    dk, dv = dkv_call(sc, k, v, q_all, d_all, delta_all, t)
    d_qkv, da1_part, hs_qk, c1 = dqkv_call(dq, dk, dv, q_raw, k_raw, tabs, hg, w_qkv, patches, vec, vec)
    da1 = narrow_sum(da1_part)
    grad_patches = last_call(da1, patches, d_mid, vec)
    g_out = scatter_rows(mm_tn(d_attn, mixed))
    g_qkv = scatter_rows(mm_tn(a1, d_qkv))

    d_cap, hs_c = pl.pallas_call(
        caption_grad_kernel,
        out_shape=[sds((text, 2 * n), bf16), sds((1, n), f32)],
        compiler_params=params(0),
        name="caption_grad",
    )(cap_total[:, :n], cap_total[:, n:], cap_raw[0], hg)
    g_cap = scatter_rows(mm_tn(captions, d_cap))
    d_text = mm_nt(d_cap[:, :n], w_caption[0]) + mm_nt(d_cap[:, n:], w_caption[1])
    grad_captions = narrow_sum(d_text.astype(bf16))

    head_part = jnp.concatenate([hs_qk, hs_c]).reshape(3, heads, HD).sum(1)
    gate_part = gate_sum[0, ::HD] * (1.0 - tg_heads * tg_heads)
    sent = jnp.concatenate([c1[0], head_part.reshape(-1), gate_part])
    got = lax.all_gather(sent, "narrow")
    summed = jnp.sum(got[:, : d + 3 * HD], 0)
    sent = jnp.concatenate([summed, got[:, d + 3 * HD :].reshape(-1), c2[0], c3[0], c4[0]])
    got = lax.all_gather(sent, "wide")
    one, rest = got[:, :d], got[:, d:]
    grad_head_gains = jnp.sum(rest[:, : 3 * HD], 0).reshape(3, HD)
    grad_cross_gate = jnp.sum(rest[:, 3 * HD : 3 * HD + deep * heads], 0)
    two, three, four = (rest[:, 3 * HD + deep * heads + k * d :][:, :d] for k in range(3))
    cols = jnp.stack([one, two, three, four], 1)
    gain_factor = jnp.stack([scales[:, 0], gates[:, 1], scales[:, 2], gates[:, 3]], 1)
    gain_grads = jnp.sum(gain_factor * cols, 0)
    wide_cols = d // count
    grad_norm_gains = lax.dynamic_slice_in_dim(gain_grads, me * wide_cols, wide_cols, 1)
    ones = jnp.ones_like(one)
    slope = jnp.stack([ones, 1.0 - gates[:, 1] ** 2, ones, 1.0 - gates[:, 3] ** 2], 1)
    d_mod = lax.dynamic_slice_in_dim(slope * norm_gains[None] * cols, mz * ada, ada, 2)
    at_slot = (firsts[None, :] == blocks[:, None]).astype(f32)
    d_slots = jnp.sum(at_slot[:, :, None, None] * d_mod[None], 1).astype(bf16).astype(f32)
    cond_rows = cd // count
    silu_mine = lax.dynamic_slice_in_dim(jax.nn.silu(conds).astype(bf16).astype(f32), me * cond_rows, cond_rows, 1)
    grad_ada = jnp.sum(silu_mine[:, :, None, None] * d_slots[:, None], 0)
    d_mine = lax.dynamic_index_in_dim(d_slots, me, 0, False)
    cond_part = jnp.sum(d_mine[None] * w_ada.astype(f32), (1, 2))
    cond_total = jnp.sum(lax.all_gather(cond_part, "narrow"), 0)
    pull_silu = jax.vjp(jax.nn.silu, cond)[1]
    grad_conditioning = pull_silu(cond_total)[0].reshape(1, -1)

    rows = d // count
    return (
        output,
        grad_patches,
        grad_conditioning,
        grad_captions,
        grad_ada,
        grad_norm_gains,
        g_qkv.astype(f32).reshape(rows, 3, n).transpose(1, 0, 2),
        grad_head_gains,
        grad_cross_gate,
        g_cap.astype(f32).reshape(-1, 2, n).transpose(1, 0, 2),
        g_out.astype(f32).T,
        g_gu.astype(f32).reshape(rows, 2, ff).transpose(1, 0, 2),
        g_down.astype(f32).T,
    )


def solution(mesh):
    placed = (
        P("wide", None),
        P("wide", None),
        P("wide", None),
        P("wide", None),
        P(),
        P(),
        P(None, None, "narrow"),
        P(),
        P(None, None, "narrow"),
        P(),
        P("narrow"),
        P(None, None, "narrow"),
        P("narrow", None),
        P(None, None, "narrow"),
        P("narrow", None),
    )
    return jax.shard_map(
        local,
        mesh=mesh,
        in_specs=placed,
        out_specs=(
            P("wide", None),
            P("wide", None),
            P("wide", None),
            P("wide", None),
            P("wide", None, "narrow"),
            P(None, "wide"),
            P(None, "wide", "narrow"),
            P(),
            P(),
            P(None, "wide", "narrow"),
            P("narrow", "wide"),
            P(None, "wide", "narrow"),
            P("narrow", "wide"),
        ),
        check_vma=False,
    )
```

time: 2450 us -> 1370 us (0.56)
  matrix products: 527 us -> 54.1 us
  other arithmetic: 334 us -> 47.3 us
  waiting for transfers between devices: 1080 us -> 825 us
  Pallas kernels: 0 us -> 174 us
  starting transfers between devices: 157 us -> 57.6 us
  local copies, waits for them, and re-layouts: 189 us -> 94.5 us
  loops' own time: 28.6 us -> 0 us
    dot_general x55 -> x9, matrix products: 520 us -> 54.1 us  [the longest x5 37.2 us: mm_tn(): return lax.dot_general(a, b, TN, preferred_element_type=f32)]
    psum x5 -> x4, waiting for transfers between devices: 916 us -> 574 us  [narrow_sum(): return lax.psum(x, 'narrow')]
    pallas_call x0 -> x12, Pallas kernels: none -> 174 us  [the longest x1 24.4 us: dkv_call(): pl.pallas_call(dkv_kernel, grid_spec=pltpu.PrefetchScalarGridSpec(num_sca...]
    ppermute x24 -> x40, starting transfers between devices: 155 us -> 56.1 us  [xor_gather(): swap = lambda a, m: lax.ppermute(a, 'wide', [(i, i ^ m) for i in range(8)])]
    convert_element_type x32 -> x5, other arithmetic: 91.7 us -> 0.11 us  [the longest x1 0.07 us: local(): at_slot = (firsts[None, :] == blocks[:, None]).astype(f32)]
    reduce_scatter x3 -> x5, waiting for transfers between devices: 60.4 us -> 147 us  [scatter_rows(): lax.psum_scatter(x.astype(bf16), 'wide', scatter_dimension=0, tiled=True)]
    select_n x33 -> x3, other arithmetic: 87.2 us -> 3.97 us  [the longest x1 3.19 us: rope_tables(): return (cos, jnp.where(former, -sin, 0.0), jnp.where(former, 0.0, sin))]
    reduce_sum x22 -> x18, other arithmetic: 97.3 us -> 16.4 us  [the longest x1 4.96 us: local(): cond_part = jnp.sum(d_mine[None] * w_ada.astype(f32), (1, 2))]
  transfers between devices with their start and end apart: 38 -> 52, of which waited for: 11 -> 20; matrix products, arithmetic and copies ran while one was open for 32% -> 13% of each run, Pallas kernels for 0% -> 6%
where the time goes in v1:
time: 1370 us; the launch traced here: 1360 us
  waiting for transfers between devices  825 us (60%)
  Pallas kernels  174 us (13%)
  local copies, waits for them, and re-layouts  94.5 us (7%)
  blocking collectives  85.2 us (6%)
  starting transfers between devices  57.6 us (4%)
  matrix products  54.1 us (4%)
  other arithmetic  47.3 us (3%)
  between operations  21.7 us (2%)
    psum x4, waiting for transfers between devices, narrow_sum(): return lax.psum(x, 'narrow')  574 us
    reduce_scatter x5, waiting for transfers between devices, scatter_rows(): lax.psum_scatter(x.astype(bf16), 'wide', scatter_dimension=0, tiled=True)  147 us
    unnamed x122, local copies, waits for them, and re-layouts  69.4 us
    ppermute x40, starting transfers between devices, xor_gather(): swap = lambda a, m: lax.ppermute(a, 'wide', [(i, i ^ m) for i in range(8)])  56.1 us
    ppermute x40, waiting for transfers between devices, xor_gather(): swap = lambda a, m: lax.ppermute(a, 'wide', [(i, i ^ m) for i in range(8)])  54.3 us
    unnamed x13, waiting for transfers between devices  49.3 us
    dot_general x5, matrix products, mm_tn(): return lax.dot_general(a, b, TN, preferred_element_type=f32)  37.2 us
    all_gather x1, blocking collectives, local(): delta_all = lax.all_gather(delta_row, 'wide')  27.5 us
  transfers between devices with their start and end apart: 52, of which 20 were waited for; matrix products, arithmetic and copies ran while one was open for 13% of the time, Pallas kernels for 6%

profile of v1, /device:TPU:0, one launch (start us, length us, event | category | flops | bytes accessed | tf_op | source)
XLA Modules:
  0.0 1359.3 jit_solution(15494935503972894797)
XLA Ops:
  8.8 4.6 fusion.11
  21.2 4.4 fusion
  25.6 14.8 %all-gather.6 = f32[4,1,1792]{2,1,0:T(1,128)S(1)} all-gather(f32[1,1,1792]{2,1,0:T(1,128)S(1)} %reshape.312), channel_id=2, replica_groups=mesh['wide'=8,'narrow'=4] {'narrow'}, dimensions={0}, use_global_device_ids=true | all-gather | bytes 35840 | tf_op jit(solution)/shard_map/all_gather | solution.py:660
  40.5 10.8 all-gather.7
  54.3 3.2 fusion.16
  58.2 12.7 qkv.1
  87.2 6.5 collective-permute-done.2
  99.1 3.1 collective-permute-done.11
  105.9 4.1 collective-permute-done.12
  112.8 6.1 collective-permute-done.15
  135.3 2.5 collective-permute-done.18
  151.7 19.1 %attend.1 = (bf16[1024,384]{1,0:T(8,128)(2,1)}, bf16[1024,384]{1,0:T(8,128)(2,1)}, f32[1024,384]{1,0:T(8,128)}) custom-call(s32[6]{0:T(128)} %pad_add_fusion.sc, bf16[1024,384]{1,0:T(8,128)(2,1)} %get-tuple-element.52.q_ref, bf16[8192,384]{1,0:T(8,128)(2,1)} %constant_dynamic-update-slice_fusion.k_ref, ...), custom_call_target="tpu_custom_call" | custom-call | tf_op jit(solution)/shard_map/attend/pallas_call | solution.py:226
  170.8 4.6 convolution_convert_fusion.3
  175.6 144.0 %all-reduce.9.cloned.1.call-done.at_ref = bf16[1024,1536]{1,0:T(8,128)(2,1)} async-done(((bf16[1024,1536]{1,0:T(8,128)(2,1)}), bf16[1024,1536]{1,0:T(8,128)(2,1)}) %all-reduce.9.cloned.1.call-update) | async-done | bytes 3145744 | tf_op jit(solution)/shard_map/psum | solution.py:585
  319.6 18.1 %ffn.1 = (f32[1024,1536]{1,0:T(8,128)}, bf16[1024,1536]{1,0:T(8,128)(2,1)}, bf16[1024,2048]{1,0:T(8,128)(2,1)}, bf16[1024,1024]{1,0:T(8,128)(2,1)}, bf16[1024,1536]{1,0:T(8,128)(2,1)}) custom-call(bf16[1024,1536]{1,0:T(8,128)(2,1)} %p_ref.7, bf16[1024,1536]{1,0:T(8,128)(2,1)} %all-reduce.9.cloned.1.call-done.at_ref, ...), custom_call_target="tpu_custom_call" | custom-call | tf_op jit(solution)/shard_map/ffn/pallas_call | solution.py:429
  337.8 120.2 %all-reduce.11.cloned.1.call-done.f_ref = bf16[1024,1536]{1,0:T(8,128)(2,1)} async-done(((bf16[1024,1536]{1,0:T(8,128)(2,1)}), bf16[1024,1536]{1,0:T(8,128)(2,1)}) %all-reduce.11.cloned.1.call-update) | async-done | bytes 3145744 | tf_op jit(solution)/shard_map/psum | solution.py:585
  458.0 22.2 %ffn_back.1 = (bf16[1024,1536]{1,0:T(8,128)(2,1)}, bf16[1024,1536]{1,0:T(8,128)(2,1)}, bf16[1024,2048]{1,0:T(8,128)(2,1)}, bf16[1024,1536]{1,0:T(8,128)(2,1)}, f32[1,1536]{1,0:T(1,128)}) custom-call(bf16[1024,1536]{1,0:T(8,128)(2,1)} %all-reduce.11.cloned.1.call-done.f_ref, f32[1024,1536]{1,0:T(8,128)} %get-tuple-element.57.mid_ref, ...), custom_call_target="tpu_custom_call" | custom-call | tf_op jit(solution)/shard_map/ffn_back/pallas_call | solution.py:466
  480.4 120.2 %all-reduce.13.cloned.1.call-done.da_ref = bf16[1024,1536]{1,0:T(8,128)(2,1)} async-done(((bf16[1024,1536]{1,0:T(8,128)(2,1)}), bf16[1024,1536]{1,0:T(8,128)(2,1)}) %all-reduce.13.cloned.1.call-update) | async-done | bytes 3145744 | tf_op jit(solution)/shard_map/psum | solution.py:585
  600.6 14.7 %out_back.1 = (f32[1024,1536]{1,0:T(8,128)}, bf16[1024,1536]{1,0:T(8,128)(2,1)}, bf16[1024,384]{1,0:T(8,128)(2,1)}, bf16[1024,384]{1,0:T(8,128)(2,1)}, f32[1024,...) custom-call(bf16[1024,1536]{1,0:T(8,128)(2,1)} %all-reduce.13.cloned.1.call-done.da_ref, ...), custom_call_target="tpu_custom_call" | custom-call | tf_op jit(solution)/shard_map/out_back/pallas_call | solution.py:512
  615.3 10.6 caption_back.1
  629.1 7.8 convolution_convert_fusion.4
  641.8 9.4 collective-permute-done.21
  651.3 13.4 collective-permute-done.22
  674.0 4.6 collective-permute-done.27
  703.5 27.5 %all-gather.2 = f32[64,1024]{1,0:T(8,128)S(1)} all-gather(f32[8,1024]{1,0:T(8,128)} %get-tuple-element.67), channel_id=4, replica_groups=mesh['wide'=8,'narrow'=4] {'wide'}, dimensions={0}, use_global_device_ids=true | all-gather | bytes 294912 | tf_op jit(solution)/shard_map/all_gather | solution.py:701
  733.4 4.9 convolution_convert_fusion.5
  745.6 22.8 %dq.1.dq_ref = f32[1024,384]{1,0:T(8,128)} custom-call(s32[6]{0:T(128)} %pad_add_fusion.sc, bf16[1024,384]{1,0:T(8,128)(2,1)} %get-tuple-element.52.q_ref, bf16[1024,384]{1,0:T(8,128)(2,1)} %get-tuple-element.63.d_ref, f32[1024,384]{1,0:T(8,128)} %get-tuple-element.64.dl_ref, bf16[8192,384]{1,0:T(8,128)(2,1)} %constant_dynamic-update-slice_fusion.k_ref, ...), custom_call_target="tpu_custom_call" | custom-call | tf_op jit(solution)/shard_map/dq/pallas_call | solution.py:338
  771.0 29.4 %collective-permute-start.36 = (bf16[1024,384]{1,0:T(8,128)(2,1)S(1)}, bf16[1024,384]{1,0:T(8,128)(2,1)S(1)}, u32[]{:S(2)}, u32[]{:S(2)}) collective-permute-start(bf16[1024,384]{1,0:T(8,128)(2,1)S(1)} %pad_maximum_fusion.10), channel_id=1, source_target_pairs={{0,4},{4,0},{8,12},{12,8},{16,20},{20,16},{24,28},{28,24},{1,5},{5... | collective-permute-start | bytes 2359304 | tf_op jit(solution)/shard_map/ppermute | solution.py:567
  816.7 24.4 %dkv.1 = (f32[1024,384]{1,0:T(8,128)}, f32[1024,384]{1,0:T(8,128)}) custom-call(s32[6]{0:T(128)} %pad_add_fusion.sc, bf16[1024,384]{1,0:T(8,128)(2,1)} %get-tuple-element.53.k_ref, bf16[1024,384]{1,0:T(8,128)(2,1)} %get-tuple-element.54.v_ref, bf16[8192,384]{1,0:T(8,128)(2,1)} %constant_dynamic-update-slice_fusion.22.q_ref, ...), custom_call_target="tpu_custom_call" | custom-call | tf_op jit(solution)/shard_map/dkv/pallas_call | solution.py:393
  841.1 16.1 %dqkv.1 = (bf16[1024,1152]{1,0:T(8,128)(2,1)}, bf16[1024,1536]{1,0:T(8,128)(2,1)}, f32[2,384]{1,0:T(2,128)}, f32[1,1536]{1,0:T(1,128)}) custom-call(f32[1024,384]{1,0:T(8,128)} %dq.1.dq_ref, f32[1024,384]{1,0:T(8,128)} %get-tuple-element.68.dk_ref, f32[1024,384]{1,0:T(8,128)} %get-tuple-element.69.dv_ref, f32[1024,384]{1,0:T(8,128)} %get-tuple-element.70.qr_ref, ...), custom_call_target="tpu_custom_call" | custom-call | tf_op jit(solution)/shard_map/dqkv/pallas_call | solution.py:169
  858.0 2.7 select_reduce_fusion
  861.6 2.7 caption_grad.1
  865.5 19.0 %all-reduce = f32[6936]{0:T(1024)S(1)} all-reduce(f32[6936]{0:T(1024)S(1)} %dynamic-update-slice), channel_id=5, replica_groups=mesh['wide'=8,'narrow'=4] {'narrow'}, use_global_device_ids=true, to_apply=%add | all-reduce | flops 6936 | bytes 55488
  886.2 11.3 convolution_convert_fusion.1
  897.7 8.8 convolution_convert_fusion
  906.6 3.2 fusion.5
  909.8 4.6 fusion.3
  914.4 4.4 fusion.2
  923.4 49.1 %all-reduce.15.cloned.1.call-done = f32[50880]{0:T(1024)} async-done(((f32[50880]{0:T(1024)}), f32[50880]{0:T(1024)}) %all-reduce.15.cloned.1.call-update) | async-done | bytes 203536
  974.0 5.0 fusion.1
  978.9 13.2 all-gather.5
  996.6 42.2 %reduce-scatter.12.cloned.1.call-done = bf16[192,2048]{1,0:T(8,128)(2,1)} async-done(((bf16[1536,2048]{1,0:T(8,128)(2,1)}), bf16[192,2048]{1,0:T(8,128)(2,1)}) %reduce-scatter.12.cloned.1.call-update) | async-done | bytes 786448 | tf_op jit(solution)/shard_map/reduce_scatter | solution.py:589
  1041.4 48.9 %reduce-scatter.6.cloned.1.call-done = bf16[192,1152]{1,0:T(8,128)(2,1)} async-done(((bf16[1536,1152]{1,0:T(8,128)(2,1)}), bf16[192,1152]{1,0:T(8,128)(2,1)}) %reduce-scatter.6.cloned.1.call-update) | async-done | bytes 442384 | tf_op jit(solution)/shard_map/reduce_scatter | solution.py:589
  1092.7 189.9 %all-reduce.17.cloned.1.call-done = (bf16[1024,1536]{1,0:T(8,128)(2,1)}, bf16[256,4096]{1,0:T(8,128)(2,1)}) async-done(((bf16[1024,1536]{1,0:T(8,128)(2,1)}, bf16[256,4096]{1,0:T(8,128)(2,1)}), (bf16[1024,1536]{1,0:T(8,128)(2,1)}, bf16[256,4096]{1,0:T(8,128)(2,1)})) %all-reduce.17.cloned.1.call-update) | async-done | bytes 5242896 | tf_op jit(solution)/shard_map/psum | solution.py:585
  1282.6 7.9 last.1
  1290.5 56.1 %reduce-scatter.8.cloned.1.call-done = bf16[512,768]{0,1:T(8,128)(2,1)} async-done(((bf16[4096,768]{0,1:T(8,128)(2,1)}), bf16[512,768]{0,1:T(8,128)(2,1)}) %reduce-scatter.8.cloned.1.call-update) | async-done | bytes 786448 | tf_op jit(solution)/shard_map/reduce_scatter | solution.py:589
  1346.6 2.5 copy.88
  1349.1 3.1 copy.157
  (321 shorter events, 156.3 us)
Async XLA Ops:
  7.2 144.6 %all-gather.11.cloned.1.call-start = ((), (), s32[]{:S(2)}) async-start(), calls=%async_computation.5 | async-start | bytes 3538944 | tf_op jit(solution)/shard_map/all_gather | solution.py:680
  16.7 303.0 %all-reduce.9.cloned.1.call-start = ((), (), s32[]{:S(2)}) async-start(), calls=%async_computation.6 | async-start | bytes 6291456 | tf_op jit(solution)/shard_map/psum | solution.py:585
  73.1 12.2 collective-permute-start.1
  74.3 21.3 %collective-permute-start.4 = (bf16[512,384]{1,0:T(8,128)(2,1)}, bf16[512,384]{1,0:T(8,128)(2,1)S(1)}, u32[]{:S(2)}, u32[]{:S(2)}) collective-permute-start(bf16[512,384]{1,0:T(8,128)(2,1)} %get-tuple-element.172), channel_id=1, source_target_pairs={{0,16},{4,20},{8,24},{12,28},{16,0},{20,4},{24,8},{28,12},{1,17},{... | collective-permute-start | bytes 1179656 | tf_op jit(solution)/shard_map/ppermute | solution.py:567
  75.1 18.7 %collective-permute-start.2 = (bf16[512,384]{1,0:T(8,128)(2,1)}, bf16[512,384]{1,0:T(8,128)(2,1)}, u32[]{:S(2)}, u32[]{:S(2)}) collective-permute-start(bf16[512,384]{1,0:T(8,128)(2,1)} %get-tuple-element.171), channel_id=1, source_target_pairs={{0,8},{4,12},{8,0},{12,4},{16,24},{20,28},{24,16},{28,20},{1,9},{5... | collective-permute-start | bytes 1179656 | tf_op jit(solution)/shard_map/ppermute | solution.py:567
  76.6 21.7 %collective-permute-start.5 = (bf16[512,384]{1,0:T(8,128)(2,1)}, bf16[512,384]{1,0:T(8,128)(2,1)}, u32[]{:S(2)}, u32[]{:S(2)}) collective-permute-start(bf16[512,384]{1,0:T(8,128)(2,1)} %get-tuple-element.171), channel_id=1, source_target_pairs={{0,16},{4,20},{8,24},{12,28},{16,0},{20,4},{24,8},{28,12},{1,17},{... | collective-permute-start | bytes 1179656 | tf_op jit(solution)/shard_map/ppermute | solution.py:567
  79.2 23.0 %collective-permute-start.11 = (bf16[512,384]{1,0:T(8,128)(2,1)}, bf16[512,384]{1,0:T(8,128)(2,1)}, u32[]{:S(2)}, u32[]{:S(2)}) collective-permute-start(bf16[512,384]{1,0:T(8,128)(2,1)} %get-tuple-element.170), channel_id=1, source_target_pairs={{0,8},{4,12},{8,0},{12,4},{16,24},{20,28},{24,16},{28,20},{1,9},{5... | collective-permute-start | bytes 1179656 | tf_op jit(solution)/shard_map/ppermute | solution.py:567
  85.2 34.5 %collective-permute-start = (bf16[1024,384]{1,0:T(8,128)(2,1)S(1)}, bf16[1024,384]{1,0:T(8,128)(2,1)}, u32[]{:S(2)}, u32[]{:S(2)}) collective-permute-start(bf16[1024,384]{1,0:T(8,128)(2,1)S(1)} %copy-done.3), channel_id=1, source_target_pairs={{0,4},{4,0},{8,12},{12,8},{16,20},{20,16},{24,28},{28,24},{1,5},{5... | collective-permute-start | bytes 2359304 | tf_op jit(solution)/shard_map/ppermute | solution.py:567
  93.7 16.2 %collective-permute-start.12 = (bf16[512,384]{1,0:T(8,128)(2,1)}, bf16[512,384]{1,0:T(8,128)(2,1)}, u32[]{:S(2)}, u32[]{:S(2)}) collective-permute-start(bf16[512,384]{1,0:T(8,128)(2,1)} %get-tuple-element.169), channel_id=1, source_target_pairs={{0,8},{4,12},{8,0},{12,4},{16,24},{20,28},{24,16},{28,20},{1,9},{5... | collective-permute-start | bytes 1179656 | tf_op jit(solution)/shard_map/ppermute | solution.py:567
  95.6 28.6 %collective-permute-start.10 = (bf16[1024,384]{1,0:T(8,128)(2,1)}, bf16[1024,384]{1,0:T(8,128)(2,1)}, u32[]{:S(2)}, u32[]{:S(2)}) collective-permute-start(bf16[1024,384]{1,0:T(8,128)(2,1)} %get-tuple-element.54.v_ref), channel_id=1, source_target_pairs={{0,4},{4,0},{8,12},{12,8},{16,20},{20,16},{24,28},{28,24},{1,5},{5... | collective-permute-start | bytes 2359304 | tf_op jit(solution)/shard_map/ppermute | solution.py:567
  98.3 12.9 collective-permute-start.14
  102.2 16.7 %collective-permute-start.15 = (bf16[512,384]{1,0:T(8,128)(2,1)}, bf16[512,384]{1,0:T(8,128)(2,1)S(1)}, u32[]{:S(2)}, u32[]{:S(2)}) collective-permute-start(bf16[512,384]{1,0:T(8,128)(2,1)} %get-tuple-element.169), channel_id=1, source_target_pairs={{0,16},{4,20},{8,24},{12,28},{16,0},{20,4},{24,8},{28,12},{1,17},{... | collective-permute-start | bytes 1179656 | tf_op jit(solution)/shard_map/ppermute | solution.py:567
  110.0 27.9 %collective-permute-start.3 = (bf16[1024,384]{1,0:T(8,128)(2,1)S(1)}, bf16[1024,384]{1,0:T(8,128)(2,1)S(1)}, u32[]{:S(2)}, u32[]{:S(2)}) collective-permute-start(bf16[1024,384]{1,0:T(8,128)(2,1)S(1)} %pad_maximum_fusion), channel_id=1, source_target_pairs={{0,4},{4,0},{8,12},{12,8},{16,20},{20,16},{24,28},{28,24},{1,5},{5... | collective-permute-start | bytes 2359304 | tf_op jit(solution)/shard_map/ppermute | solution.py:567
  111.2 17.4 %collective-permute-start.7 = (bf16[512,384]{1,0:T(8,128)(2,1)}, bf16[512,384]{1,0:T(8,128)(2,1)S(1)}, u32[]{:S(2)}, u32[]{:S(2)}) collective-permute-start(bf16[512,384]{1,0:T(8,128)(2,1)} %copy-done.7), channel_id=1, source_target_pairs={{0,16},{4,20},{8,24},{12,28},{16,0},{20,4},{24,8},{28,12},{1,17},{... | collective-permute-start | bytes 1179656 | tf_op jit(solution)/shard_map/ppermute | solution.py:567
  118.8 12.3 collective-permute-start.8
  119.8 15.5 %collective-permute-start.17 = (bf16[512,384]{1,0:T(8,128)(2,1)}, bf16[512,384]{1,0:T(8,128)(2,1)S(1)}, u32[]{:S(2)}, u32[]{:S(2)}) collective-permute-start(bf16[512,384]{1,0:T(8,128)(2,1)} %collective-permute-done.11), channel_id=1, source_target_pairs={{0,16},{4,20},{8,24},{12,28},{16,0},{20,4},{24,8},{28,12},{1,17},{... | collective-permute-start | bytes 1179656 | tf_op jit(solution)/shard_map/ppermute | solution.py:567
  124.2 13.6 collective-permute-start.18
  128.6 13.4 collective-permute-start.6
  137.8 11.9 collective-permute-start.9
  137.9 12.9 collective-permute-start.19
  175.4 282.6 %all-reduce.11.cloned.1.call-start = ((), (), s32[]{:S(2)}) async-start(), calls=%async_computation.7 | async-start | bytes 6291456 | tf_op jit(solution)/shard_map/psum | solution.py:585
  337.8 262.8 %all-reduce.13.cloned.1.call-start = ((), (), s32[]{:S(2)}) async-start(), calls=%async_computation.8 | async-start | bytes 6291456 | tf_op jit(solution)/shard_map/psum | solution.py:585
  480.3 377.7 %all-gather.13.cloned.1.call-start = ((), (), s32[]{:S(2)}) async-start(), calls=%async_computation.9 | async-start | bytes 3538944 | tf_op jit(solution)/shard_map/all_gather | solution.py:707
  628.8 290.9 %reduce-scatter.14.cloned.1.call-start = ((), (), s32[]{:S(2)}) async-start(), calls=%async_computation.14 | async-start | bytes 3538944 | tf_op jit(solution)/shard_map/reduce_scatter | solution.py:589
  636.9 284.8 %reduce-scatter.10.cloned.1.call-start = ((), (), s32[]{:S(2)}) async-start(), calls=%async_computation.12 | async-start | bytes 1327104 | tf_op jit(solution)/shard_map/reduce_scatter | solution.py:589
  637.8 13.5 collective-permute-start.21
  639.2 25.5 %collective-permute-start.22 = (bf16[512,384]{1,0:T(8,128)(2,1)S(1)}, bf16[512,384]{1,0:T(8,128)(2,1)S(1)}, u32[]{:S(2)}, u32[]{:S(2)}) collective-permute-start(bf16[512,384]{1,0:T(8,128)(2,1)S(1)} %get-tuple-element.165), channel_id=1, source_target_pairs={{0,8},{4,12},{8,0},{12,4},{16,24},{20,28},{24,16},{28,20},{1,9},{5... | collective-permute-start | bytes 1179656 | tf_op jit(solution)/shard_map/ppermute | solution.py:567
  639.8 28.5 %collective-permute-start.25 = (bf16[512,384]{1,0:T(8,128)(2,1)S(1)}, bf16[512,384]{1,0:T(8,128)(2,1)S(1)}, u32[]{:S(2)}, u32[]{:S(2)}) collective-permute-start(bf16[512,384]{1,0:T(8,128)(2,1)S(1)} %get-tuple-element.165), channel_id=1, source_target_pairs={{0,16},{4,20},{8,24},{12,28},{16,0},{20,4},{24,8},{28,12},{1,17},{... | collective-permute-start | bytes 1179656 | tf_op jit(solution)/shard_map/ppermute | solution.py:567
  641.3 39.7 %collective-permute-start.20 = (bf16[1024,384]{1,0:T(8,128)(2,1)S(1)}, bf16[1024,384]{1,0:T(8,128)(2,1)}, u32[]{:S(2)}, u32[]{:S(2)}) collective-permute-start(bf16[1024,384]{1,0:T(8,128)(2,1)S(1)} %copy-done.1), channel_id=1, source_target_pairs={{0,4},{4,0},{8,12},{12,8},{16,20},{20,16},{24,28},{28,24},{1,5},{5... | collective-permute-start | bytes 2359304 | tf_op jit(solution)/shard_map/ppermute | solution.py:567
  641.3 31.6 %collective-permute-start.24 = (bf16[512,384]{1,0:T(8,128)(2,1)}, bf16[512,384]{1,0:T(8,128)(2,1)}, u32[]{:S(2)}, u32[]{:S(2)}) collective-permute-start(bf16[512,384]{1,0:T(8,128)(2,1)} %get-tuple-element.166), channel_id=1, source_target_pairs={{0,16},{4,20},{8,24},{12,28},{16,0},{20,4},{24,8},{28,12},{1,17},{... | collective-permute-start | bytes 1179656 | tf_op jit(solution)/shard_map/ppermute | solution.py:567
  666.8 19.0 %collective-permute-start.23 = (bf16[1024,384]{1,0:T(8,128)(2,1)}, bf16[1024,384]{1,0:T(8,128)(2,1)}, u32[]{:S(2)}, u32[]{:S(2)}) collective-permute-start(bf16[1024,384]{1,0:T(8,128)(2,1)} %pad_maximum_fusion.6), channel_id=1, source_target_pairs={{0,4},{4,0},{8,12},{12,8},{16,20},{20,16},{24,28},{28,24},{1,5},{5... | collective-permute-start | bytes 2359304 | tf_op jit(solution)/shard_map/ppermute | solution.py:567
  673.9 16.5 %collective-permute-start.26 = (bf16[1024,384]{1,0:T(8,128)(2,1)S(1)}, bf16[1024,384]{1,0:T(8,128)(2,1)S(1)}, u32[]{:S(2)}, u32[]{:S(2)}) collective-permute-start(bf16[1024,384]{1,0:T(8,128)(2,1)S(1)} %pad_maximum_fusion.7), channel_id=1, source_target_pairs={{0,4},{4,0},{8,12},{12,8},{16,20},{20,16},{24,28},{28,24},{1,5},{5... | collective-permute-start | bytes 2359304 | tf_op jit(solution)/shard_map/ppermute | solution.py:567
  680.9 14.2 %collective-permute-start.29 = (bf16[1024,384]{1,0:T(8,128)(2,1)S(1)}, bf16[1024,384]{1,0:T(8,128)(2,1)S(1)}, u32[]{:S(2)}, u32[]{:S(2)}) collective-permute-start(bf16[1024,384]{1,0:T(8,128)(2,1)S(1)} %pad_maximum_fusion.8), channel_id=1, source_target_pairs={{0,4},{4,0},{8,12},{12,8},{16,20},{20,16},{24,28},{28,24},{1,5},{5... | collective-permute-start | bytes 2359304 | tf_op jit(solution)/shard_map/ppermute | solution.py:567
  696.1 105.6 %collective-permute-start.30 = (bf16[1024,384]{1,0:T(8,128)(2,1)}, bf16[1024,384]{1,0:T(8,128)(2,1)}, u32[]{:S(2)}, u32[]{:S(2)}) collective-permute-start(bf16[1024,384]{1,0:T(8,128)(2,1)} %get-tuple-element.63.d_ref), channel_id=1, source_target_pairs={{0,4},{4,0},{8,12},{12,8},{16,20},{20,16},{24,28},{28,24},{1,5},{5... | collective-permute-start | bytes 2359304 | tf_op jit(solution)/shard_map/ppermute | solution.py:567
  698.6 42.1 %collective-permute-start.31 = (bf16[512,384]{1,0:T(8,128)(2,1)}, bf16[512,384]{1,0:T(8,128)(2,1)}, u32[]{:S(2)}, u32[]{:S(2)}) collective-permute-start(bf16[512,384]{1,0:T(8,128)(2,1)} %get-tuple-element.164), channel_id=1, source_target_pairs={{0,8},{4,12},{8,0},{12,4},{16,24},{20,28},{24,16},{28,20},{1,9},{5... | collective-permute-start | bytes 1179656 | tf_op jit(solution)/shard_map/ppermute | solution.py:567
  699.3 70.7 %collective-permute-start.34 = (bf16[512,384]{1,0:T(8,128)(2,1)}, bf16[512,384]{1,0:T(8,128)(2,1)S(1)}, u32[]{:S(2)}, u32[]{:S(2)}) collective-permute-start(bf16[512,384]{1,0:T(8,128)(2,1)} %get-tuple-element.164), channel_id=1, source_target_pairs={{0,16},{4,20},{8,24},{12,28},{16,0},{20,4},{24,8},{28,12},{1,17},{... | collective-permute-start | bytes 1179656 | tf_op jit(solution)/shard_map/ppermute | solution.py:567
  700.0 42.8 %collective-permute-start.32 = (bf16[512,384]{1,0:T(8,128)(2,1)}, bf16[512,384]{1,0:T(8,128)(2,1)S(1)}, u32[]{:S(2)}, u32[]{:S(2)}) collective-permute-start(bf16[512,384]{1,0:T(8,128)(2,1)} %get-tuple-element.163), channel_id=1, source_target_pairs={{0,8},{4,12},{8,0},{12,4},{16,24},{20,28},{24,16},{28,20},{1,9},{5... | collective-permute-start | bytes 1179656 | tf_op jit(solution)/shard_map/ppermute | solution.py:567
  701.3 40.0 %collective-permute-start.35 = (bf16[512,384]{1,0:T(8,128)(2,1)}, bf16[512,384]{1,0:T(8,128)(2,1)}, u32[]{:S(2)}, u32[]{:S(2)}) collective-permute-start(bf16[512,384]{1,0:T(8,128)(2,1)} %get-tuple-element.163), channel_id=1, source_target_pairs={{0,16},{4,20},{8,24},{12,28},{16,0},{20,4},{24,8},{28,12},{1,17},{... | collective-permute-start | bytes 1179656 | tf_op jit(solution)/shard_map/ppermute | solution.py:567
  740.8 59.6 %collective-permute-start.37 = (bf16[512,384]{1,0:T(8,128)(2,1)}, bf16[512,384]{1,0:T(8,128)(2,1)}, u32[]{:S(2)}, u32[]{:S(2)}) collective-permute-start(bf16[512,384]{1,0:T(8,128)(2,1)} %collective-permute-done.31), channel_id=1, source_target_pairs={{0,16},{4,20},{8,24},{12,28},{16,0},{20,4},{24,8},{28,12},{1,17},{... | collective-permute-start | bytes 1179656 | tf_op jit(solution)/shard_map/ppermute | solution.py:567
  741.3 59.0 %collective-permute-start.38 = (bf16[512,384]{1,0:T(8,128)(2,1)}, bf16[512,384]{1,0:T(8,128)(2,1)}, u32[]{:S(2)}, u32[]{:S(2)}) collective-permute-start(bf16[512,384]{1,0:T(8,128)(2,1)} %collective-permute-done.35), channel_id=1, source_target_pairs={{0,8},{4,12},{8,0},{12,4},{16,24},{20,28},{24,16},{28,20},{1,9},{5... | collective-permute-start | bytes 1179656 | tf_op jit(solution)/shard_map/ppermute | solution.py:567
  744.9 61.5 %collective-permute-start.33 = (bf16[1024,384]{1,0:T(8,128)(2,1)}, bf16[1024,384]{1,0:T(8,128)(2,1)}, u32[]{:S(2)}, u32[]{:S(2)}) collective-permute-start(bf16[1024,384]{1,0:T(8,128)(2,1)} %pad_maximum_fusion.9), channel_id=1, source_target_pairs={{0,4},{4,0},{8,12},{12,8},{16,20},{20,16},{24,28},{28,24},{1,5},{5... | collective-permute-start | bytes 2359304 | tf_op jit(solution)/shard_map/ppermute | solution.py:567
  768.4 204.0 %all-reduce.15.cloned.1.call-start = ((), (), s32[]{:S(2)}) async-start(), calls=%async_computation.15 | async-start | bytes 409600
  771.0 40.2 %collective-permute-start.36 = (bf16[1024,384]{1,0:T(8,128)(2,1)S(1)}, bf16[1024,384]{1,0:T(8,128)(2,1)S(1)}, u32[]{:S(2)}, u32[]{:S(2)}) collective-permute-start(bf16[1024,384]{1,0:T(8,128)(2,1)S(1)} %pad_maximum_fusion.10), channel_id=1, source_target_pairs={{0,4},{4,0},{8,12},{12,8},{16,20},{20,16},{24,28},{28,24},{1,5},{5... | collective-permute-start | bytes 2359304 | tf_op jit(solution)/shard_map/ppermute | solution.py:567
  801.6 14.2 %collective-permute-start.39 = (bf16[1024,384]{1,0:T(8,128)(2,1)S(1)}, bf16[1024,384]{1,0:T(8,128)(2,1)S(1)}, u32[]{:S(2)}, u32[]{:S(2)}) collective-permute-start(bf16[1024,384]{1,0:T(8,128)(2,1)S(1)} %pad_maximum_fusion.11), channel_id=1, source_target_pairs={{0,4},{4,0},{8,12},{12,8},{16,20},{20,16},{24,28},{28,24},{1,5},{5... | collective-permute-start | bytes 2359304 | tf_op jit(solution)/shard_map/ppermute | solution.py:567
  886.1 152.7 %reduce-scatter.12.cloned.1.call-start = ((), (), s32[]{:S(2)}) async-start(), calls=%async_computation.13 | async-start | bytes 7077888 | tf_op jit(solution)/shard_map/reduce_scatter | solution.py:589
  897.5 192.8 %reduce-scatter.6.cloned.1.call-start = ((), (), s32[]{:S(2)}) async-start(), calls=%async_computation.10 | async-start | bytes 3981312 | tf_op jit(solution)/shard_map/reduce_scatter | solution.py:589
  906.5 376.0 %all-reduce.17.cloned.1.call-start = ((), (), s32[]{:S(2)}) async-start(), calls=%async_computation.16 | async-start | bytes 10485760 | tf_op jit(solution)/shard_map/psum | solution.py:585
  914.4 432.2 %reduce-scatter.8.cloned.1.call-start = ((), (), s32[]{:S(2)}) async-start(), calls=%async_computation.11 | async-start | bytes 7077888 | tf_op jit(solution)/shard_map/reduce_scatter | solution.py:589
  (35 other events, 1276.2 us)
Sparse Core Ops, SparseCore 0:
  16.8 35.8 all-gather.10
  175.5 144.0 all-reduce.8
  337.9 120.0 all-reduce.10
  480.4 120.0 all-reduce.12
  628.9 40.5 all-gather.12
  672.8 55.6 reduce-scatter.13
  768.5 64.8 reduce-scatter.9
  886.2 86.1 all-reduce.14
  976.2 62.5 reduce-scatter.11
  1042.1 48.0 reduce-scatter.5
  1093.3 189.2 all-reduce.16
  1285.8 60.7 reduce-scatter.7

commit v2 on v1

v2 whole, which is shorter than its diff:
```python
import functools

import jax
import jax.numpy as jnp
from jax import lax
from jax.experimental import pallas as pl
from jax.experimental.pallas import tpu as pltpu
from jax.sharding import PartitionSpec as P

HD = 64
SPAN = 4
EPS = 1e-05
LOG2E = 1.4426950408889634
f32 = jnp.float32
bf16 = jnp.bfloat16
VMEM = 56 * 1024 * 1024
BR = 256
NT = (((1,), (1,)), ((), ()))
TN = (((0,), (0,)), ((), ()))


def params(n):
    return pltpu.CompilerParams(
        dimension_semantics=("arbitrary",) * n, vmem_limit_bytes=VMEM
    )


def sds(shape, dtype):
    return jax.ShapeDtypeStruct(shape, dtype)


def mm(a, b):
    return jnp.dot(a, b, preferred_element_type=f32)


def mm_nt(a, b):
    return lax.dot_general(a, b, NT, preferred_element_type=f32)


def mm_tn(a, b):
    return lax.dot_general(a, b, TN, preferred_element_type=f32)


def split(x):
    hi = x.astype(bf16)
    return hi, (x - hi.astype(f32)).astype(bf16)


def head_sum(x, ones):
    hi, lo = split(x)
    return mm(hi, ones) + mm(lo, ones)


def head_ones(n):
    a = lax.broadcasted_iota(jnp.int32, (n, n), 0) // HD
    b = lax.broadcasted_iota(jnp.int32, (n, n), 1) // HD
    return (a == b).astype(bf16)


def halves(n):
    lane = lax.broadcasted_iota(jnp.int32, (1, n), 1)
    return (lane < HD, lane >= HD)


def keep(x, mask):
    return jnp.where(mask, x, jnp.zeros_like(x))


def inv_rms(x):
    return lax.rsqrt(jnp.mean(x * x, -1, keepdims=True) + EPS)


def row(ref, k):
    return ref[k : k + 1, :]


def whole(shape):
    zeros = (0,) * len(shape)
    return pl.BlockSpec(shape, lambda *_: zeros, pipeline_mode=pl.Buffered(1))


def rows_of(br, width, first=0):
    return pl.BlockSpec((br, width), lambda i, *_: (i, first))


def accumulate(ref, value, first):
    @pl.when(first)
    def _():
        ref[...] = value

    @pl.when(jnp.logical_not(first))
    def _():
        ref[...] += value


def col_sum(x):
    return jnp.sum(x, 0, keepdims=True)


def tile3(t, n):
    return jnp.concatenate([t] * (n // t.shape[1]), 1)


def qkv_kernel(p_ref, v_ref, w_ref, c_ref, s1_ref, s2_ref, hg_ref, a_ref, qr_ref, kr_ref, q_ref, k_ref, vv_ref):
    x = p_ref[...].astype(f32)
    a = (x * inv_rms(x) * row(v_ref, 0)).astype(bf16)
    a_ref[...] = a
    n = q_ref.shape[1]
    ones = head_ones(n)
    cos, s1, s2 = (tile3(t[...], n) for t in (c_ref, s1_ref, s2_ref))

    def turned(y, gain):
        z = y * lax.rsqrt(head_sum(y * y, ones) * (1.0 / HD) + EPS) * gain
        return z * cos + pltpu.roll(z, n - 16, 1) * s1 + pltpu.roll(z, 16, 1) * s2

    q = mm(a, w_ref[0])
    qr_ref[...] = q
    q_ref[...] = (turned(q, row(hg_ref, 0)) * (0.125 * LOG2E)).astype(bf16)
    k = mm(a, w_ref[1])
    kr_ref[...] = k
    k_ref[...] = turned(k, row(hg_ref, 1)).astype(bf16)
    vv_ref[...] = mm(a, w_ref[2]).astype(bf16)


def qkv_call(patches, vec, w, tabs, hg, br=256):
    t, d = patches.shape
    n = w.shape[2]
    return pl.pallas_call(
        qkv_kernel,
        grid=(t // br,),
        in_specs=[rows_of(br, d), whole(vec.shape), whole(w.shape)]
        + [rows_of(br, 128)] * 3
        + [whole(hg.shape)],
        out_specs=[rows_of(br, d)] + [rows_of(br, n)] * 5,
        out_shape=[sds((t, d), bf16), sds((t, n), f32), sds((t, n), f32)] + [sds((t, n), bf16)] * 3,
        compiler_params=params(1),
        name="qkv",
    )(patches, vec, w, *tabs, hg)


def soft_sums(q, k, v, mask):
    e = jnp.exp2(mm_nt(q, keep(k, mask))).astype(bf16)
    return mm(e, jnp.where(mask, v, jnp.ones_like(v)))


def attend_kernel(sc, q_ref, k_ref, v_ref, ck_ref, cv_ref, tg_ref, mix_ref, o_ref, li_ref, acc):
    j = pl.program_id(1)
    masks = halves(128)
    keys = 512

    @pl.when(j == 0)
    def _():
        acc[...] = jnp.zeros_like(acc)

    @pl.when(j < sc[0])
    def _():
        q = q_ref[...]
        for h in range(2):
            total = acc[h]
            for c in range(k_ref.shape[0] // keys):
                at = slice(c * keys, (c + 1) * keys)
                total = total + soft_sums(q, k_ref[at, :], v_ref[at, :], masks[h])
            acc[h] = total

    @pl.when(j == SPAN - 1)
    def _():
        q = q_ref[...]

        def finish(a0, a1):
            inverse = 1.0 / jnp.where(masks[0], pltpu.roll(a0, HD, 1), pltpu.roll(a1, HD, 1))
            return jnp.where(masks[0], a0, a1) * inverse, inverse

        o, li = finish(acc[0], acc[1])
        c0, c1 = (soft_sums(q, ck_ref[...], cv_ref[...], m) for m in masks)
        mix_ref[...] = (o + tg_ref[...] * finish(c0, c1)[0]).astype(bf16)
        o_ref[...] = o.astype(bf16)
        li_ref[...] = li


def attend_call(sc, q, k, v, cap, tg, c, block):
    n = q.shape[1]
    pairs = n // 128
    text = cap.shape[0] * block // k.shape[0]
    mine = lambda p, j, s: (0, p)
    return pl.pallas_call(
        attend_kernel,
        grid_spec=pltpu.PrefetchScalarGridSpec(
            num_scalar_prefetch=1,
            grid=(pairs, SPAN),
            in_specs=[
                pl.BlockSpec((BR, 128), lambda p, j, s: (c, p)),
                pl.BlockSpec((block, 128), lambda p, j, s: (s[2 + j], p)),
                pl.BlockSpec((block, 128), lambda p, j, s: (s[2 + j], p)),
                pl.BlockSpec((text, 128), lambda p, j, s: (s[1], p)),
                pl.BlockSpec((text, 128), lambda p, j, s: (s[1], pairs + p)),
                pl.BlockSpec((1, 128), mine),
            ],
            out_specs=[pl.BlockSpec((BR, 128), mine)] * 3,
            scratch_shapes=[pltpu.VMEM((2, BR, 128), f32)],
        ),
        out_shape=[sds((BR, n), bf16), sds((BR, n), bf16), sds((BR, n), f32)],
        compiler_params=params(2),
        name="attend",
    )(sc, q, k, v, cap, cap, tg)


def caption_back_kernel(sc, q_ref, d_ref, ck_ref, cv_ref, tg_ref, dq_ref, dk_ref, dv_ref, gs_ref):
    masks = halves(128)
    q, d = q_ref[...], d_ref[...]
    dq = jnp.zeros(q.shape, f32)
    dk = jnp.zeros(ck_ref.shape, f32)
    dv = jnp.zeros(ck_ref.shape, f32)
    sums = []
    for h in range(2):
        ck, cv = keep(ck_ref[...], masks[h]), keep(cv_ref[...], masks[h])
        gate = tg_ref[:, h * HD : h * HD + 1]
        e = jnp.exp2(mm_nt(q, ck))
        prob = e * (1.0 / jnp.sum(e, -1, keepdims=True))
        dp = mm_nt(d, cv)
        m = jnp.sum(prob * dp, -1, keepdims=True)
        dc = (prob * (dp - m) * gate).astype(bf16)
        dq = dq + mm(dc, ck)
        dk = dk + mm_tn(dc, keep(q, masks[h]))
        dv = dv + mm_tn(prob.astype(bf16), keep(d, masks[h]))
        sums.append(jnp.sum(m, 0, keepdims=True))
    dq_ref[...] = dq * 0.125
    dk_ref[...] = dk * (1.0 / LOG2E)
    dv_ref[...] = dv * tg_ref[...]
    gs_ref[...] = jnp.where(masks[0], sums[0], sums[1])


def caption_back_call(sc, q, d, cap, tg, c, text):
    n = q.shape[1]
    pairs = n // 128
    mine = lambda p, s: (0, p)
    return pl.pallas_call(
        caption_back_kernel,
        grid_spec=pltpu.PrefetchScalarGridSpec(
            num_scalar_prefetch=1,
            grid=(pairs,),
            in_specs=[
                pl.BlockSpec((BR, 128), lambda p, s: (c, p)),
                pl.BlockSpec((BR, 128), mine),
                pl.BlockSpec((text, 128), lambda p, s: (s[1], p)),
                pl.BlockSpec((text, 128), lambda p, s: (s[1], pairs + p)),
                pl.BlockSpec((1, 128), mine),
            ],
            out_specs=[
                pl.BlockSpec((BR, 128), mine),
                pl.BlockSpec((text, 128), mine),
                pl.BlockSpec((text, 128), mine),
                pl.BlockSpec((1, 128), mine),
            ],
        ),
        out_shape=[sds((BR, n), f32), sds((text, n), f32), sds((text, n), f32), sds((1, n), f32)],
        compiler_params=params(1),
        name="caption_back",
    )(sc, q, d, cap, cap, tg)


def minus_delta(rows, head):
    lane = lax.broadcasted_iota(jnp.int32, (rows, 128), 1)
    return jnp.where((lane >= 3 * head) & (lane < 3 * head + 3), -1.0, 0.0).astype(bf16)


def dq_kernel(sc, q_ref, d_ref, x_ref, k_ref, v_ref, c_ref, dq_ref, acc):
    pair = pl.program_id(0)
    j = pl.program_id(1)
    masks = halves(128)
    keys = 512

    @pl.when(j == 0)
    def _():
        acc[...] = jnp.zeros_like(acc)

    @pl.when(j < sc[0])
    def _():
        q = q_ref[...]
        dx = jnp.concatenate([d_ref[...], x_ref[...]], 1)
        total = acc[...]
        for h in range(2):
            off = minus_delta(keys, 2 * pair + h)
            for c in range(k_ref.shape[0] // keys):
                at = slice(c * keys, (c + 1) * keys)
                k = keep(k_ref[at, :], masks[h])
                e = jnp.exp2(mm_nt(q, k))
                dp = mm_nt(dx, jnp.concatenate([keep(v_ref[at, :], masks[h]), off], 1))
                total = total + mm((e * dp).astype(bf16), k)
        acc[...] = total

    @pl.when(j == SPAN - 1)
    def _():
        dq_ref[...] = acc[...] * 0.125 + c_ref[...]


def dq_call(sc, q, d, k, v, cap_dq, c, block):
    n = q.shape[1]
    pairs = n // 128
    mine = lambda p, j, s: (0, p)
    other = lambda p, j, s: (s[2 + j], p)
    return pl.pallas_call(
        dq_kernel,
        grid_spec=pltpu.PrefetchScalarGridSpec(
            num_scalar_prefetch=1,
            grid=(pairs, SPAN),
            in_specs=[
                pl.BlockSpec((BR, 128), lambda p, j, s: (c, p)),
                pl.BlockSpec((BR, 128), mine),
                pl.BlockSpec((BR, 128), lambda p, j, s: (0, pairs)),
                pl.BlockSpec((block, 128), other),
                pl.BlockSpec((block, 128), other),
                pl.BlockSpec((BR, 128), mine),
            ],
            out_specs=pl.BlockSpec((BR, 128), mine),
            scratch_shapes=[pltpu.VMEM((BR, 128), f32)],
        ),
        out_shape=sds((BR, n), f32),
        compiler_params=params(2),
        name="dq",
    )(sc, q, d, d, k, v, cap_dq)


def dkv_kernel(start, sc, k_ref, v_ref, q_ref, d_ref, x_ref, *rest):
    dk_ref, dv_ref = rest[-2:]
    pair = pl.program_id(0)
    j = pl.program_id(1)
    masks = halves(128)
    keys = 512

    @pl.when(j == 0)
    def _():
        if start:
            dk_ref[...] = jnp.zeros_like(dk_ref)
            dv_ref[...] = jnp.zeros_like(dv_ref)
        else:
            dk_ref[...] = rest[0][...]
            dv_ref[...] = rest[1][...]

    @pl.when(j < sc[0])
    def _():
        q, d = q_ref[...], d_ref[...]
        dx = jnp.concatenate([d, x_ref[...]], 1)
        qs = [keep(q, m) for m in masks]
        ds = [keep(d, m) for m in masks]
        for c in range(k_ref.shape[0] // keys):
            at = slice(c * keys, (c + 1) * keys)
            dk, dv = dk_ref[at, :], dv_ref[at, :]
            for h in range(2):
                off = minus_delta(keys, 2 * pair + h)
                e = jnp.exp2(mm_nt(k_ref[at, :], qs[h]))
                dp = mm_nt(jnp.concatenate([keep(v_ref[at, :], masks[h]), off], 1), dx)
                dv = dv + mm(e.astype(bf16), ds[h])
                dk = dk + mm((e * dp).astype(bf16), qs[h])
            dk_ref[at, :] = dk
            dv_ref[at, :] = dv


def dkv_call(sc, k, v, q_all, d_all, before, c):
    t, n = k.shape
    pairs = n // 128
    chunks = t // BR
    mine = pl.BlockSpec((t, 128), lambda p, j, s: (0, p))
    return pl.pallas_call(
        functools.partial(dkv_kernel, not before),
        grid_spec=pltpu.PrefetchScalarGridSpec(
            num_scalar_prefetch=1,
            grid=(pairs, SPAN),
            in_specs=[
                mine,
                mine,
                pl.BlockSpec((BR, 128), lambda p, j, s: (s[2 + SPAN + j] * chunks + c, p)),
                pl.BlockSpec((BR, 128), lambda p, j, s: (s[2 + j], p)),
                pl.BlockSpec((BR, 128), lambda p, j, s: (s[2 + j], pairs)),
            ]
            + [mine] * len(before),
            out_specs=[mine, mine],
        ),
        out_shape=[sds((t, n), f32)] * 2,
        input_output_aliases={6: 0, 7: 1} if before else {},
        compiler_params=params(2),
        name="dkv",
    )(sc, k, v, q_all, d_all, d_all, *before)


def chunk_call(kernel, name, c, ins, specs, chunk_outs, sum_outs, whole_outs, before):
    one = lambda r, w: pl.BlockSpec((r, w), lambda i: (0, 0))
    loose = chunk_outs + sum_outs
    into = [pl.BlockSpec((BR, w), lambda i: (c, 0)) for _, w, _ in whole_outs]
    held = list(before)
    body = kernel
    if held:

        def body(*refs):
            kernel(*refs[: len(ins)], *refs[len(ins) + len(held) :])

    return pl.pallas_call(
        body,
        grid=(1,),
        in_specs=specs + [pl.BlockSpec(memory_space=pl.ANY)] * len(held),
        out_specs=[one(r, w) for r, w, _ in loose] + into,
        out_shape=[sds((r, w), k) for r, w, k in loose + whole_outs],
        input_output_aliases={len(ins) + k: len(loose) + k for k in range(len(held))},
        compiler_params=params(1),
        name=name,
    )(*ins, *held)


def part(c, width):
    return pl.BlockSpec((BR, width), lambda i: (c, 0))


def alone(width):
    return pl.BlockSpec((BR, width), lambda i: (0, 0))


def ffn_kernel(p_ref, at_ref, v_ref, wg_ref, wd_ref, mid_ref, gu_ref, f_ref, a_ref, h_ref):
    at = at_ref[...].astype(f32)
    mid = p_ref[...].astype(f32) + row(v_ref, 1) * (at * inv_rms(at))
    mid_ref[...] = mid
    a = (mid * inv_rms(mid) * row(v_ref, 2)).astype(bf16)
    a_ref[...] = a
    g = mm(a, wg_ref[0])
    u = mm(a, wg_ref[1])
    n = g.shape[1]
    gu_ref[:, :n] = g.astype(bf16)
    gu_ref[:, n:] = u.astype(bf16)
    h = (g * jax.nn.sigmoid(g) * u).astype(bf16)
    h_ref[...] = h
    f_ref[...] = mm(h, wd_ref[...]).astype(bf16)


def ffn_call(c, patches, at, vec, wg, wd, before):
    t, d = patches.shape
    n = wd.shape[0]
    return chunk_call(
        ffn_kernel,
        "ffn",
        c,
        (patches, at, vec, wg, wd),
        [part(c, d), alone(d), whole(vec.shape), whole(wg.shape), whole(wd.shape)],
        [(BR, d, f32), (BR, 2 * n, bf16), (BR, d, bf16)],
        [],
        [(t, d, bf16), (t, n, bf16)],
        before,
    )


def ffn_back_kernel(f_ref, mid_ref, c_ref, gu_ref, v_ref, wg_ref, wd_ref, da_ref, cs_ref, y_ref, df_ref, dgu_ref):
    f = f_ref[...].astype(f32)
    cot = c_ref[...].astype(f32)
    r = inv_rms(f)
    fh = f * r
    y_ref[...] = (mid_ref[...] + row(v_ref, 3) * fh).astype(bf16)
    z = cot * row(v_ref, 3)
    df = (r * (z - fh * jnp.mean(z * fh, -1, keepdims=True))).astype(bf16)
    df_ref[...] = df
    cs_ref[...] = col_sum(cot * fh)
    dh = mm_nt(df, wd_ref[...])
    n = dh.shape[1]
    g = gu_ref[:, :n].astype(f32)
    u = gu_ref[:, n:].astype(f32)
    s = jax.nn.sigmoid(g)
    gs = g * s
    dg = (dh * u * (s + gs * (1.0 - s))).astype(bf16)
    du = (dh * gs).astype(bf16)
    dgu_ref[:, :n] = dg
    dgu_ref[:, n:] = du
    da_ref[...] = (mm_nt(dg, wg_ref[0]) + mm_nt(du, wg_ref[1])).astype(bf16)


def ffn_back_call(c, f, mid, cot, gu, vec, wg, wd, before):
    t, d = cot.shape
    n = wd.shape[0]
    return chunk_call(
        ffn_back_kernel,
        "ffn_back",
        c,
        (f, mid, cot, gu, vec, wg, wd),
        [alone(d), alone(d), part(c, d), alone(2 * n), whole(vec.shape), whole(wg.shape), whole(wd.shape)],
        [(BR, d, bf16)],
        [(1, d, f32)],
        [(t, d, bf16), (t, d, bf16), (t, 2 * n, bf16)],
        before,
    )


def out_back_kernel(da_ref, mid_ref, at_ref, c_ref, v_ref, w_ref, o_ref, li_ref, dm_ref, dx_ref, ds_ref, c3_ref, c2_ref, dat_ref):
    da = da_ref[...].astype(f32)
    mid = mid_ref[...]
    r = inv_rms(mid)
    mh = mid * r
    z = da * row(v_ref, 2)
    dm = c_ref[...].astype(f32) + r * (z - mh * jnp.mean(z * mh, -1, keepdims=True))
    dm_ref[...] = dm
    c3_ref[...] = col_sum(da * mh)
    at = at_ref[...].astype(f32)
    ra = inv_rms(at)
    ah = at * ra
    c2_ref[...] = col_sum(dm * ah)
    z = dm * row(v_ref, 1)
    dat = (ra * (z - ah * jnp.mean(z * ah, -1, keepdims=True))).astype(bf16)
    dat_ref[...] = dat
    dx = mm_nt(dat, w_ref[...]).astype(bf16)
    dx_ref[...] = dx
    n = dx.shape[1]
    ds = dx.astype(f32) * li_ref[...]
    ds_ref[:, :n] = ds.astype(bf16)
    hi, lo = split(ds * o_ref[...].astype(f32))
    head = lax.broadcasted_iota(jnp.int32, (n, 128), 0) // HD
    lane = lax.broadcasted_iota(jnp.int32, (n, 128), 1)
    to_lanes = (lane // 3 == head).astype(bf16)
    delta = mm(hi, to_lanes) + mm(lo, to_lanes)
    one = delta.astype(bf16).astype(f32)
    two = (delta - one).astype(bf16).astype(f32)
    which = lax.broadcasted_iota(jnp.int32, (1, 128), 1) % 3
    ds_ref[:, n:] = jnp.where(which == 0, one, jnp.where(which == 1, two, delta - one - two)).astype(bf16)


def out_back_call(c, da, mid, at, cot, vec, w, o, li, before):
    t, d = cot.shape
    n = w.shape[0]
    return chunk_call(
        out_back_kernel,
        "out_back",
        c,
        (da, mid, at, cot, vec, w, o, li),
        [alone(d), alone(d), alone(d), part(c, d), whole(vec.shape), whole(w.shape), alone(n), alone(n)],
        [(BR, d, f32), (BR, n, bf16), (BR, n + 128, bf16)],
        [(1, d, f32), (1, d, f32)],
        [(t, d, bf16)],
        before,
    )


def dqkv_kernel(dq_ref, dk_ref, dv_ref, qr_ref, kr_ref, c_ref, s1_ref, s2_ref, hg_ref, w_ref, p_ref, da_ref, hs_ref, cs_ref, d_ref):
    n = dq_ref.shape[1]
    ones = head_ones(n)
    cos, s1, s2 = (tile3(t[...], n) for t in (c_ref, s1_ref, s2_ref))

    def back(dy, x, gain):
        dz = dy * cos - pltpu.roll(dy, 16, 1) * s2 - pltpu.roll(dy, n - 16, 1) * s1
        r = lax.rsqrt(head_sum(x * x, ones) * (1.0 / HD) + EPS)
        xh = x * r
        g = dz * gain
        return r * (g - xh * (head_sum(g * xh, ones) * (1.0 / HD))), col_sum(dz * xh)

    dq, hq = back(dq_ref[...], qr_ref[...], row(hg_ref, 0))
    dk, hk = back(dk_ref[...] * (1.0 / LOG2E), kr_ref[...], row(hg_ref, 1))
    dql, dkl, dvl = dq.astype(bf16), dk.astype(bf16), dv_ref[...].astype(bf16)
    d_ref[:, :n] = dql
    d_ref[:, n : 2 * n] = dkl
    d_ref[:, 2 * n :] = dvl
    da = mm_nt(dql, w_ref[0]) + mm_nt(dkl, w_ref[1]) + mm_nt(dvl, w_ref[2])
    da_ref[...] = da.astype(bf16)
    x = p_ref[...].astype(f32)
    cs_ref[...] = col_sum(da * (x * inv_rms(x)))
    hs_ref[0:1, :] = hq
    hs_ref[1:2, :] = hk


def dqkv_call(c, dq, dk, dv, qr, kr, tabs, hg, w, patches, before):
    t, d = patches.shape
    n = dq.shape[1]
    return chunk_call(
        dqkv_kernel,
        "dqkv",
        c,
        (dq, dk, dv, qr, kr, *tabs, hg, w, patches),
        [alone(n)] + [part(c, n)] * 4 + [part(c, 128)] * 3 + [whole(hg.shape), whole(w.shape), part(c, d)],
        [(BR, d, bf16)],
        [(2, n, f32), (1, d, f32)],
        [(t, 3 * n, bf16)],
        before,
    )


def last_kernel(da_ref, p_ref, dm_ref, v_ref, o_ref):
    x = p_ref[...].astype(f32)
    r = inv_rms(x)
    xh = x * r
    z = da_ref[...].astype(f32) * row(v_ref, 0)
    o_ref[...] = (dm_ref[...] + r * (z - xh * jnp.mean(z * xh, -1, keepdims=True))).astype(bf16)


def last_call(c, da, patches, dm, vec, before):
    t, d = patches.shape
    return chunk_call(
        last_kernel,
        "last",
        c,
        (da, patches, dm, vec),
        [alone(d), part(c, d), alone(d), whole(vec.shape)],
        [],
        [],
        [(t, d, bf16)],
        before,
    )


def caption_grad_kernel(dk_ref, dv_ref, kr_ref, hg_ref, d_ref, hs_ref):
    n = dk_ref.shape[1]
    ones = head_ones(n)
    x = kr_ref[...]
    r = lax.rsqrt(head_sum(x * x, ones) * (1.0 / HD) + EPS)
    xh = x * r
    dy = dk_ref[...]
    g = dy * row(hg_ref, 2)
    d_ref[:, :n] = (r * (g - xh * (head_sum(g * xh, ones) * (1.0 / HD)))).astype(bf16)
    d_ref[:, n:] = dv_ref[...].astype(bf16)
    hs_ref[...] = col_sum(dy * xh)


def caption_norm_kernel(kr_ref, v_ref, hg_ref, o_ref):
    n = kr_ref.shape[1]
    x = kr_ref[...]
    r = lax.rsqrt(head_sum(x * x, head_ones(n)) * (1.0 / HD) + EPS)
    o_ref[:, :n] = (x * r * row(hg_ref, 2)).astype(bf16)
    o_ref[:, n:] = v_ref[...].astype(bf16)


def xor_gather(x):
    half = x.shape[0] // 2
    swap = lambda a, m: lax.ppermute(a, "wide", [(i, i ^ m) for i in range(8)])
    a, b = x[:half], x[half:]
    ra, rb = swap(a, 2), swap(b, 4)
    a4, b2 = swap(jnp.concatenate([a, ra]), 4), swap(jnp.concatenate([b, rb]), 2)
    parts = [x, None, jnp.concatenate([ra, b2[:half]]), None, jnp.concatenate([a4[:half], rb]), None, jnp.concatenate([a4[half:], b2[half:]]), None]
    for m in (0, 2, 4, 6):
        parts[m + 1] = swap(parts[m], 1)
    return jnp.concatenate(parts)


def gather_wide(x):
    if lax.axis_size("wide") == 8:
        return xor_gather(x)
    return lax.all_gather(x, "wide", axis=0, tiled=True)


def gather_small(x, axis):
    size = x.shape[0]
    wide = -(-size // 1024) * 1024
    padded = jnp.pad(x, (0, wide - size)).reshape(1, 8, wide // 8)
    return lax.all_gather(padded, axis, axis=0, tiled=True).reshape(-1, wide)[:, :size]


class Line:
    def __init__(self, place):
        self.end = (place == 0) | (place == 3)
        self.second = self.third = None

    def step(self, x):
        send = functools.partial(lax.ppermute, axis_name="narrow")
        inwards, out = [(0, 1), (3, 2)], [(1, 0), (2, 3)]
        second, third = self.second, self.third
        got_in = got_out = None
        if x is not None and third is not None and x.shape == third.shape:
            got_in = got_out = send(jnp.where(self.end, x, third), perm=inwards + out)
        else:
            if x is not None:
                got_in = send(x, perm=inwards)
            if third is not None:
                got_out = send(third, perm=out)
        total = None if third is None else jnp.where(self.end, got_out, third)
        self.third = None if second is None else second + send(second, perm=[(1, 2), (2, 1)])
        self.second = None if x is None else x + got_in
        return total


class Sums:
    def __init__(self, size, place):
        self.line = Line(place) if size == 4 else None
        self.names, self.done = [], {}

    def add(self, name, x):
        if self.line is None:
            self.done[name] = lax.psum(x, "narrow")
            return
        self._step(name, x)

    def _step(self, name, x):
        total = self.line.step(x)
        self.names.append(name)
        if total is not None:
            self.done[self.names[-3]] = total

    def get(self, name):
        while name not in self.done:
            self._step(None, None)
        return self.done[name]


def scatter_rows(x):
    return lax.psum_scatter(x.astype(bf16), "wide", scatter_dimension=0, tiled=True)


def rope_tables(position, width):
    lane = jnp.arange(128, dtype=jnp.int32)
    within = lane % HD
    quarter = HD // 4
    frequency = 10000.0 ** (-(within % quarter).astype(f32) / quarter)
    by_row = within < HD // 2
    where = jnp.where(by_row[None, :], (position // width)[:, None], (position % width)[:, None])
    angle = where.astype(f32) * frequency[None, :]
    cos, sin = jnp.cos(angle), jnp.sin(angle)
    former = (within % (HD // 2) < quarter)[None, :]
    return cos, jnp.where(former, -sin, 0.0), jnp.where(former, 0.0, sin)


def local(
    patches,
    cotangent,
    conditioning,
    captions,
    item_lengths,
    grid_widths,
    w_ada,
    norm_gains,
    w_qkv,
    head_gains,
    cross_gate,
    w_caption,
    w_out,
    w_gate_up,
    w_down,
):
    t, d = patches.shape
    n = w_qkv.shape[2]
    heads = n // HD
    ada = w_ada.shape[2]
    ff = w_down.shape[0]
    text = captions.shape[0]
    cd = conditioning.shape[1]
    count = lax.axis_size("wide")
    deep = lax.axis_size("narrow")
    me = lax.axis_index("wide")
    mz = lax.axis_index("narrow")

    slots = item_lengths.shape[0]
    spans = item_lengths // t
    order = jnp.arange(slots, dtype=jnp.int32)
    ends = jnp.sum(jnp.where(order[None, :] <= order[:, None], spans[None, :], 0), 1)
    blocks = jnp.arange(count, dtype=jnp.int32)
    item = jnp.sum((ends[None, :] <= blocks[:, None]).astype(jnp.int32), 1)
    is_item = item[:, None] == order[None, :]
    pick = lambda values: jnp.sum(jnp.where(is_item, values[None, :], 0), 1)
    firsts = pick(ends - spans)
    mine = blocks == me
    of_me = lambda values: jnp.sum(jnp.where(mine, values, 0))
    first = of_me(firsts)
    length = of_me(pick(spans))
    width = of_me(pick(grid_widths))
    position = (me - first) * t + jnp.arange(t, dtype=jnp.int32)
    tabs = rope_tables(position, width)
    steps = first + jnp.minimum(jnp.arange(SPAN, dtype=jnp.int32), length - 1)
    places = steps ^ me if count == 8 else steps
    sc = jnp.concatenate([jnp.stack([length, first]), places, steps]).astype(jnp.int32)

    cond = conditioning.astype(f32)[0]
    silu_low = jax.nn.silu(cond).astype(bf16)
    mod = jnp.sum(silu_low.astype(f32)[:, None, None] * w_ada.astype(f32), 0)
    share = cd // deep
    sent = jnp.concatenate([mod.reshape(-1), lax.dynamic_slice_in_dim(cond, mz * share, share)])
    got = gather_small(sent, "narrow").reshape(-1)
    got = gather_small(got, "wide").reshape(count, deep, -1)
    mods = got[:, :, : 4 * ada].reshape(count, deep, 4, ada).transpose(0, 2, 1, 3).reshape(count, 4, d)
    conds = got[:, :, 4 * ada :].reshape(count, cd)
    my_mod = lax.dynamic_index_in_dim(mods, first, 0, False)
    of_block = jnp.sum(jnp.where((firsts[:, None] == blocks[None, :])[:, :, None, None], mods[None], 0.0), 1)
    scales = 1.0 + of_block
    gates = jnp.tanh(of_block)
    factor = jnp.stack([1.0 + my_mod[0], jnp.tanh(my_mod[1]), 1.0 + my_mod[2], jnp.tanh(my_mod[3])])
    vec = norm_gains * factor
    hg = jnp.tile(head_gains, (1, heads))
    tg_heads = jnp.tanh(cross_gate)
    tg = jnp.repeat(tg_heads, HD)[None, :]

    cap_raw = jnp.einsum("kd,jde->jke", captions, w_caption, preferred_element_type=f32)
    cap_own = pl.pallas_call(
        caption_norm_kernel,
        out_shape=sds((text, 2 * n), bf16),
        compiler_params=params(0),
        name="caption_norm",
    )(cap_raw[0], cap_raw[1], hg)
    cap = lax.all_gather(cap_own, "wide", axis=0, tiled=True)

    chunks = range(t // BR)
    sums = Sums(deep, mz)
    a1, q_raw, k_raw, q, k, v = qkv_call(patches, vec, w_qkv, tabs, hg)
    k_all = gather_wide(k)
    v_all = gather_wide(v)
    q_all = lax.all_gather(q, "wide", axis=0, tiled=True)
    heads_out = [None for _ in chunks]
    for c in chunks:
        heads_out[c] = attend_call(sc, q, k_all, v_all, cap, tg, c, t)
        sums.add(("attn", c), mm(heads_out[c][0], w_out).astype(bf16))

    mids, gus = {}, {}
    whole_out = ()
    for c in chunks:
        mids[c], gus[c], ffn_part, *whole_out = ffn_call(c, patches, sums.get(("attn", c)), vec, w_gate_up, w_down, whole_out)
        sums.add(("ffn", c), ffn_part)
    a3, hidden = whole_out
    whole_out = ()
    c4 = 0.0
    for c in chunks:
        da3_part, part_sum, *whole_out = ffn_back_call(
            c, sums.get(("ffn", c)), mids[c], cotangent, gus[c], vec, w_gate_up, w_down, whole_out
        )
        sums.add(("da3", c), da3_part)
        c4 = c4 + part_sum
    output, d_ffn, d_gu = whole_out
    g_down = scatter_rows(mm_tn(d_ffn, hidden))
    g_gu = scatter_rows(mm_tn(a3, d_gu))

    d_mids, dqs = {}, {}
    whole_out, dkv = (), ()
    c2 = c3 = dck = dcv = gate_sum = 0.0
    for c in chunks:
        mixed, o_self, linv = heads_out[c]
        d_mids[c], d_mixed, d_scaled, p3, p2, *whole_out = out_back_call(
            c, sums.get(("da3", c)), mids[c], sums.get(("attn", c)), cotangent, vec, w_out, o_self, linv, whole_out
        )
        c2, c3 = c2 + p2, c3 + p3
        d_all = gather_wide(d_scaled)
        dq_cap, pk, pv, pg = caption_back_call(sc, q, d_mixed, cap, tg, c, text)
        dck, dcv, gate_sum = dck + pk, dcv + pv, gate_sum + pg
        dqs[c] = dq_call(sc, q, d_scaled, k_all, v_all, dq_cap, c, t)
        dkv = dkv_call(sc, k, v, q_all, d_all, dkv, c)
    (d_attn,) = whole_out
    mixed = jnp.concatenate([heads_out[c][0] for c in chunks])
    g_out = scatter_rows(mm_tn(d_attn, mixed))
    whole_out = ()
    c1 = hs_qk = 0.0
    for c in chunks:
        da1_part, p_hs, p1, *whole_out = dqkv_call(c, dqs[c], *dkv, q_raw, k_raw, tabs, hg, w_qkv, patches, whole_out)
        sums.add(("da1", c), da1_part)
        hs_qk, c1 = hs_qk + p_hs, c1 + p1
    (d_qkv,) = whole_out
    g_qkv = scatter_rows(mm_tn(a1, d_qkv))

    cap_got = gather_wide(jnp.concatenate([dck, dcv], 1).astype(bf16)).reshape(count, text, 2 * n)
    from_block = blocks ^ me if count == 8 else blocks
    in_slot = jnp.sum(jnp.where(from_block[:, None] == blocks[None, :], (firsts == me)[None, :], False), 1) > 0
    cap_total = jnp.sum(jnp.where(in_slot[:, None, None], cap_got.astype(f32), 0.0), 0)
    d_cap, hs_c = pl.pallas_call(
        caption_grad_kernel,
        out_shape=[sds((text, 2 * n), bf16), sds((1, n), f32)],
        compiler_params=params(0),
        name="caption_grad",
    )(cap_total[:, :n], cap_total[:, n:], cap_raw[0], hg)
    g_cap = scatter_rows(mm_tn(captions, d_cap))
    d_text = (mm_nt(d_cap[:, :n], w_caption[0]) + mm_nt(d_cap[:, n:], w_caption[1])).astype(bf16)
    pieces = 4
    cut = d_text.shape[1] // pieces
    for k in range(pieces):
        sums.add(("text", k), d_text[:, k * cut : (k + 1) * cut])
    whole_out = ()
    for c in chunks:
        whole_out = last_call(c, sums.get(("da1", c)), patches, d_mids[c], vec, whole_out)
    (grad_patches,) = whole_out
    grad_captions = jnp.concatenate([sums.get(("text", k)) for k in range(pieces)], 1)

    head_part = jnp.concatenate([hs_qk, hs_c]).reshape(3, heads, HD).sum(1)
    gate_part = gate_sum[0, ::HD] * (1.0 - tg_heads * tg_heads)
    sent = jnp.concatenate([c1[0], head_part.reshape(-1), gate_part])
    got = gather_small(sent, "narrow")
    summed = jnp.sum(got[:, : d + 3 * HD], 0)
    sent = jnp.concatenate([summed, got[:, d + 3 * HD :].reshape(-1), c2[0], c3[0], c4[0]])
    got = gather_small(sent, "wide")
    one, rest = got[:, :d], got[:, d:]
    grad_head_gains = jnp.sum(rest[:, : 3 * HD], 0).reshape(3, HD)
    grad_cross_gate = jnp.sum(rest[:, 3 * HD : 3 * HD + deep * heads], 0)
    two, three, four = (rest[:, 3 * HD + deep * heads + k * d :][:, :d] for k in range(3))
    cols = jnp.stack([one, two, three, four], 1)
    gain_factor = jnp.stack([scales[:, 0], gates[:, 1], scales[:, 2], gates[:, 3]], 1)
    gain_grads = jnp.sum(gain_factor * cols, 0)
    wide_cols = d // count
    grad_norm_gains = lax.dynamic_slice_in_dim(gain_grads, me * wide_cols, wide_cols, 1)
    ones = jnp.ones_like(one)
    slope = jnp.stack([ones, 1.0 - gates[:, 1] ** 2, ones, 1.0 - gates[:, 3] ** 2], 1)
    d_mod = lax.dynamic_slice_in_dim(slope * norm_gains[None] * cols, mz * ada, ada, 2)
    at_slot = (firsts[None, :] == blocks[:, None]).astype(f32)
    d_slots = jnp.sum(at_slot[:, :, None, None] * d_mod[None], 1).astype(bf16).astype(f32)
    cond_rows = cd // count
    silu_mine = lax.dynamic_slice_in_dim(jax.nn.silu(conds).astype(bf16).astype(f32), me * cond_rows, cond_rows, 1)
    grad_ada = jnp.sum(silu_mine[:, :, None, None] * d_slots[:, None], 0)
    d_mine = lax.dynamic_index_in_dim(d_slots, me, 0, False)
    cond_part = jnp.sum(d_mine[None] * w_ada.astype(f32), (1, 2))
    cond_total = jnp.sum(gather_small(cond_part, "narrow"), 0)
    pull_silu = jax.vjp(jax.nn.silu, cond)[1]
    grad_conditioning = pull_silu(cond_total)[0].reshape(1, -1)

    rows = d // count
    return (
        output,
        grad_patches,
        grad_conditioning,
        grad_captions,
        grad_ada,
        grad_norm_gains,
        g_qkv.astype(f32).reshape(rows, 3, n).transpose(1, 0, 2),
        grad_head_gains,
        grad_cross_gate,
        g_cap.astype(f32).reshape(-1, 2, n).transpose(1, 0, 2),
        g_out.astype(f32).T,
        g_gu.astype(f32).reshape(rows, 2, ff).transpose(1, 0, 2),
        g_down.astype(f32).T,
    )


def solution(mesh):
    placed = (
        P("wide", None),
        P("wide", None),
        P("wide", None),
        P("wide", None),
        P(),
        P(),
        P(None, None, "narrow"),
        P(),
        P(None, None, "narrow"),
        P(),
        P("narrow"),
        P(None, None, "narrow"),
        P("narrow", None),
        P(None, None, "narrow"),
        P("narrow", None),
    )
    return jax.shard_map(
        local,
        mesh=mesh,
        in_specs=placed,
        out_specs=(
            P("wide", None),
            P("wide", None),
            P("wide", None),
            P("wide", None),
            P("wide", None, "narrow"),
            P(None, "wide"),
            P(None, "wide", "narrow"),
            P(),
            P(),
            P(None, "wide", "narrow"),
            P("narrow", "wide"),
            P(None, "wide", "narrow"),
            P("narrow", "wide"),
        ),
        check_vma=False,
    )
```

time: 1370 us -> 1160 us (0.85)
  waiting for transfers between devices: 825 us -> 231 us
  Pallas kernels: 174 us -> 401 us
  starting transfers between devices: 57.6 us -> 176 us
  other arithmetic: 47.3 us -> 101 us
  blocking collectives: 85.2 us -> 66.9 us
    psum x4 -> x0, waiting for transfers between devices: 574 us -> none  [narrow_sum(): return lax.psum(x, 'narrow')]
    reduce_scatter x5, waiting for transfers between devices: 147 us -> 0.01 us  [scatter_rows(): lax.psum_scatter(x.astype(bf16), 'wide', scatter_dimension=0, tiled=True)]
    ppermute x0 -> x46, starting transfers between devices: none -> 146 us  [the longest x14 80.3 us: step(): got_in = got_out = send(jnp.where(self.end, x, third), perm=inwards + out)]
    ppermute x0 -> x46, waiting for transfers between devices: none -> 131 us  [the longest x14 102 us: step(): got_in = got_out = send(jnp.where(self.end, x, third), perm=inwards + out)]
    pallas_call x6 -> x24, Pallas kernels: 104 us -> 214 us  [the longest x20 136 us: chunk_call(): pl.pallas_call(body, grid=(1,), in_specs=specs + [pl.BlockSpec(memory_spa...]
    pallas_call x1 -> x4, Pallas kernels: 22.8 us -> 76.4 us  [dq_call(): pl.pallas_call(dq_kernel, grid_spec=pltpu.PrefetchScalarGridSpec(num_scal...]
    pallas_call x1 -> x4, Pallas kernels: 19.1 us -> 72.3 us  [attend_call(): pl.pallas_call(attend_kernel, grid_spec=pltpu.PrefetchScalarGridSpec(num_...]
    unnamed x13 -> x7, waiting for transfers between devices: 49.3 us -> 0.11 us
  transfers between devices with their start and end apart: 52 -> 109, of which waited for: 20 -> 34; matrix products, arithmetic and copies ran while one was open for 13% -> 20% of each run, Pallas kernels for 6% -> 32%
where the time goes in v2:
time: 1160 us; the launch traced here: 1150 us
  Pallas kernels  401 us (35%)
  waiting for transfers between devices  231 us (20%)
  starting transfers between devices  176 us (15%)
  other arithmetic  101 us (9%)
  local copies, waits for them, and re-layouts  100 us (9%)
  blocking collectives  66.9 us (6%)
  matrix products  51.2 us (4%)
  between operations  21.7 us (2%)
    pallas_call x20, Pallas kernels, chunk_call(): pl.pallas_call(body, grid=(1,), in_specs=specs + [pl.BlockSpec(memory_spa...  136 us
    ppermute x14, waiting for transfers between devices, step(): got_in = got_out = send(jnp.where(self.end, x, third), perm=inwards + out)  102 us
    ppermute x56, waiting for transfers between devices, xor_gather(): swap = lambda a, m: lax.ppermute(a, 'wide', [(i, i ^ m) for i in range(8)])  100 us
    ppermute x14, starting transfers between devices, step(): got_in = got_out = send(jnp.where(self.end, x, third), perm=inwards + out)  80.3 us
    pallas_call x4, Pallas kernels, dkv_call(): pl.pallas_call(functools.partial(dkv_kernel, not before), grid_spec=pltpu...  78.8 us
    pallas_call x4, Pallas kernels, dq_call(): pl.pallas_call(dq_kernel, grid_spec=pltpu.PrefetchScalarGridSpec(num_scal...  76.4 us
    pallas_call x4, Pallas kernels, attend_call(): pl.pallas_call(attend_kernel, grid_spec=pltpu.PrefetchScalarGridSpec(num_...  72.3 us
    all_gather x5, blocking collectives, gather_small(): lax.all_gather(padded, axis, axis=0, tiled=True).reshape(-1, wide)[:, :size]  66.9 us
  transfers between devices with their start and end apart: 109, of which 34 were waited for; matrix products, arithmetic and copies ran while one was open for 20% of the time, Pallas kernels for 32%

profile of v2, /device:TPU:0, one launch (start us, length us, event | category | flops | bytes accessed | tf_op | source)
XLA Modules:
  0.0 1149.8 jit_solution(18440840757493892643)
XLA Ops:
  20.1 14.8 %all_gather.21 = f32[4,8,256]{2,1,0:T(8,128)S(1)} all-gather(f32[1,8,256]{2,1,0:T(8,128)S(1)} %reshape.295), channel_id=1, replica_groups=mesh['wide'=8,'narrow'=4] {'narrow'}, dimensions={0}, use_global_device_ids=true | all-gather | bytes 40960 | tf_op jit(solution)/shard_map/all_gather | solution.py:643
  35.0 9.3 all_gather.22
  51.3 12.7 %qkv.1 = (bf16[1024,1536]{1,0:T(8,128)(2,1)}, f32[1024,384]{1,0:T(8,128)}, f32[1024,384]{1,0:T(8,128)}, bf16[1024,384]{1,0:T(8,128)(2,1)}, bf16[1024,384]{1,0:T(8,128)(2,1)}, /*index=5*/bf16[1024,384]{1,0:T(8,128)(2,1)}) custom-call(bf16[1024,1536]{1,0:T(8,128)(2,1)} %refs_1_.5, f32[4,1536]{1,0:T(4,128)} %maximum_multiply_fusion.1.v_ref.refs_2_.refs_4_.refs_3_, ...), custom_call_target="tpu_custom_call" | custom-call | tf_op jit(solution)/shard_map/qkv/pallas_call | solution.py:128
  99.9 9.3 collective-permute-done.11
  123.8 15.4 %collective-permute-done.3 = bf16[1024,384]{1,0:T(8,128)(2,1)S(1)} collective-permute-done((bf16[1024,384]{1,0:T(8,128)(2,1)S(1)}, bf16[1024,384]{1,0:T(8,128)(2,1)S(1)}, u32[]{:S(2)}, u32[]{:S(2)}) %collective-permute-start.3) | collective-permute-done | bytes 786464 | tf_op jit(solution)/shard_map/ppermute | solution.py:623
  152.3 12.6 %collective-permute-done.5 = bf16[1024,384]{1,0:T(8,128)(2,1)S(1)} collective-permute-done((bf16[1024,384]{1,0:T(8,128)(2,1)}, bf16[1024,384]{1,0:T(8,128)(2,1)S(1)}, u32[]{:S(2)}, u32[]{:S(2)}) %collective-permute-start.5) | collective-permute-done | bytes 786464 | tf_op jit(solution)/shard_map/ppermute | solution.py:623
  179.4 18.2 %attend.7 = (bf16[256,384]{1,0:T(8,128)(2,1)}, bf16[256,384]{1,0:T(8,128)(2,1)}, f32[256,384]{1,0:T(8,128)}) custom-call(s32[10]{0:T(128)} %pad_add_fusion.sc, bf16[1024,384]{1,0:T(8,128)(2,1)} %get-tuple-element.137.q_ref, bf16[8192,384]{1,0:T(8,128)(2,1)} %constant_dynamic-update-slice_fusion.k_ref, ...), custom_call_target="tpu_custom_call" | custom-call | tf_op jit(solution)/shard_map/attend/pallas_call | solution.py:185
  202.6 18.0 %attend.5 = (bf16[256,384]{1,0:T(8,128)(2,1)}, bf16[256,384]{1,0:T(8,128)(2,1)}, f32[256,384]{1,0:T(8,128)}) custom-call(s32[10]{0:T(128)} %pad_add_fusion.sc, bf16[1024,384]{1,0:T(8,128)(2,1)} %get-tuple-element.137.q_ref, bf16[8192,384]{1,0:T(8,128)(2,1)} %constant_dynamic-update-slice_fusion.k_ref, ...), custom_call_target="tpu_custom_call" | custom-call | tf_op jit(solution)/shard_map/attend/pallas_call | solution.py:185
  227.9 18.0 %attend.6 = (bf16[256,384]{1,0:T(8,128)(2,1)}, bf16[256,384]{1,0:T(8,128)(2,1)}, f32[256,384]{1,0:T(8,128)}) custom-call(s32[10]{0:T(128)} %pad_add_fusion.sc, bf16[1024,384]{1,0:T(8,128)(2,1)} %get-tuple-element.137.q_ref, bf16[8192,384]{1,0:T(8,128)(2,1)} %constant_dynamic-update-slice_fusion.k_ref, ...), custom_call_target="tpu_custom_call" | custom-call | tf_op jit(solution)/shard_map/attend/pallas_call | solution.py:185
  245.9 18.1 %attend.4 = (bf16[256,384]{1,0:T(8,128)(2,1)}, bf16[256,384]{1,0:T(8,128)(2,1)}, f32[256,384]{1,0:T(8,128)}) custom-call(s32[10]{0:T(128)} %pad_add_fusion.sc, bf16[1024,384]{1,0:T(8,128)(2,1)} %get-tuple-element.137.q_ref, bf16[8192,384]{1,0:T(8,128)(2,1)} %constant_dynamic-update-slice_fusion.k_ref, ...), custom_call_target="tpu_custom_call" | custom-call | tf_op jit(solution)/shard_map/attend/pallas_call | solution.py:185
  271.5 15.2 %collective-permute-start.18 = (bf16[256,1536]{1,0:T(8,128)(2,1)S(1)}, bf16[256,1536]{1,0:T(8,128)(2,1)S(1)}, u32[]{:S(2)}, u32[]{:S(2)}) collective-permute-start(bf16[256,1536]{1,0:T(8,128)(2,1)S(1)} %get-tuple-element.342), channel_id=1, source_target_pairs={{0,1},{3,2},{1,0},{2,3},{4,5},{7,6},{5,4},{6,7},{8,9},{11,10},{9,8... | collective-permute-start | bytes 2359304 | tf_op jit(solution)/shard_map/ppermute | solution.py:657
  291.0 13.8 %collective-permute-done.18 = bf16[256,1536]{1,0:T(8,128)(2,1)S(1)} collective-permute-done((bf16[256,1536]{1,0:T(8,128)(2,1)S(1)}, bf16[256,1536]{1,0:T(8,128)(2,1)S(1)}, u32[]{:S(2)}, u32[]{:S(2)}) %collective-permute-start.18) | collective-permute-done | bytes 786464 | tf_op jit(solution)/shard_map/ppermute | solution.py:657
  306.6 8.5 ffn.4
  318.5 8.5 ffn.5
  328.4 8.5 collective-permute-done.25
  338.7 13.0 %collective-permute-done.23 = bf16[256,1536]{1,0:T(8,128)(2,1)S(1)} collective-permute-done((bf16[256,1536]{1,0:T(8,128)(2,1)S(1)}, bf16[256,1536]{1,0:T(8,128)(2,1)S(1)}, u32[]{:S(2)}, u32[]{:S(2)}) %collective-permute-start.23) | collective-permute-done | bytes 786464 | tf_op jit(solution)/shard_map/ppermute | solution.py:657
  353.7 8.5 ffn.6
  367.0 8.5 ffn.7
  377.0 8.5 collective-permute-done.29
  387.3 11.7 %collective-permute-done.27 = bf16[256,1536]{1,0:T(8,128)(2,1)S(1)} collective-permute-done((bf16[256,1536]{1,0:T(8,128)(2,1)S(1)}, bf16[256,1536]{1,0:T(8,128)(2,1)S(1)}, u32[]{:S(2)}, u32[]{:S(2)}) %collective-permute-start.27) | collective-permute-done | bytes 786464 | tf_op jit(solution)/shard_map/ppermute | solution.py:657
  401.1 9.6 ffn_back.4
  414.1 9.5 ffn_back.5
  434.4 10.7 collective-permute-done.31
  448.4 9.6 ffn_back.6
  458.0 9.7 ffn_back.7
  481.5 10.1 collective-permute-done.39
  519.4 19.2 %dq.7.dq_ref = f32[256,384]{1,0:T(8,128)} custom-call(s32[10]{0:T(128)} %pad_add_fusion.sc, bf16[1024,384]{1,0:T(8,128)(2,1)} %get-tuple-element.137.q_ref, bf16[256,512]{1,0:T(8,128)(2,1)} %get-tuple-element.192.d_ref.x_ref, bf16[256,512]{1,0:T(8,128)(2,1)} %get-tuple-element.192.d_ref.x_ref, bf16[8192,384]{1,0:T(8,128)(2,1)} %constant_dynamic-update-slice_fusion.k_ref, ...), custom_call_target="tpu_custom_call" | custom-call | tf_op jit(solution)/shard_map/dq/pallas_call | solution.py:301
  543.5 19.1 %dq.6.refs_0_ = f32[256,384]{1,0:T(8,128)} custom-call(s32[10]{0:T(128)} %pad_add_fusion.sc, bf16[1024,384]{1,0:T(8,128)(2,1)} %get-tuple-element.137.q_ref, bf16[256,512]{1,0:T(8,128)(2,1)} %get-tuple-element.191.d_ref.x_ref, bf16[256,512]{1,0:T(8,128)(2,1)} %get-tuple-element.191.d_ref.x_ref, bf16[8192,384]{1,0:T(8,128)(2,1)} %constant_dynamic-update-slice_fusion.k_ref, ...), custom_call_target="tpu_custom_call" | custom-call | tf_op jit(solution)/shard_map/dq/pallas_call | solution.py:301
  606.3 19.3 %dkv.4 = (f32[1024,384]{1,0:T(8,128)}, f32[1024,384]{1,0:T(8,128)}) custom-call(s32[10]{0:T(128)} %pad_add_fusion.sc, bf16[1024,384]{1,0:T(8,128)(2,1)} %get-tuple-element.138.k_ref, bf16[1024,384]{1,0:T(8,128)(2,1)} %get-tuple-element.139.v_ref, bf16[8192,384]{1,0:T(8,128)(2,1)} %all-gather.5.cloned.1.call-done.q_ref, ...), custom_call_target="tpu_custom_call" | custom-call | tf_op jit(solution)/shard_map/dkv/pallas_call | solution.py:363
  625.6 19.8 %dkv.5 = (f32[1024,384]{1,0:T(8,128)}, f32[1024,384]{1,0:T(8,128)}) custom-call(s32[10]{0:T(128)} %pad_add_fusion.sc, bf16[1024,384]{1,0:T(8,128)(2,1)} %get-tuple-element.138.k_ref, bf16[1024,384]{1,0:T(8,128)(2,1)} %get-tuple-element.139.v_ref, bf16[8192,384]{1,0:T(8,128)(2,1)} %all-gather.5.cloned.1.call-done.q_ref, ...), custom_call_target="tpu_custom_call", output_to_operand_aliasing={{0}: (6, {}), {1}: (7, {})} | custom-call | tf_op jit(solution)/shard_map/dkv/pallas_call | solution.py:363
  676.0 19.1 %dq.5.refs_0_ = f32[256,384]{1,0:T(8,128)} custom-call(s32[10]{0:T(128)} %pad_add_fusion.sc, bf16[1024,384]{1,0:T(8,128)(2,1)} %get-tuple-element.137.q_ref, bf16[256,512]{1,0:T(8,128)(2,1)} %get-tuple-element.190.d_ref.x_ref, bf16[256,512]{1,0:T(8,128)(2,1)} %get-tuple-element.190.d_ref.x_ref, bf16[8192,384]{1,0:T(8,128)(2,1)} %constant_dynamic-update-slice_fusion.k_ref, ...), custom_call_target="tpu_custom_call" | custom-call | tf_op jit(solution)/shard_map/dq/pallas_call | solution.py:301
  700.4 19.1 %dq.4.refs_0_ = f32[256,384]{1,0:T(8,128)} custom-call(s32[10]{0:T(128)} %pad_add_fusion.sc, bf16[1024,384]{1,0:T(8,128)(2,1)} %get-tuple-element.137.q_ref, bf16[256,512]{1,0:T(8,128)(2,1)} %get-tuple-element.187.d_ref.x_ref, bf16[256,512]{1,0:T(8,128)(2,1)} %get-tuple-element.187.d_ref.x_ref, bf16[8192,384]{1,0:T(8,128)(2,1)} %constant_dynamic-update-slice_fusion.k_ref, ...), custom_call_target="tpu_custom_call" | custom-call | tf_op jit(solution)/shard_map/dq/pallas_call | solution.py:301
  754.1 19.8 %dkv.6 = (f32[1024,384]{1,0:T(8,128)}, f32[1024,384]{1,0:T(8,128)}) custom-call(s32[10]{0:T(128)} %pad_add_fusion.sc, bf16[1024,384]{1,0:T(8,128)(2,1)} %get-tuple-element.138.k_ref, bf16[1024,384]{1,0:T(8,128)(2,1)} %get-tuple-element.139.v_ref, bf16[8192,384]{1,0:T(8,128)(2,1)} %all-gather.5.cloned.1.call-done.q_ref, ...), custom_call_target="tpu_custom_call", output_to_operand_aliasing={{0}: (6, {}), {1}: (7, {})} | custom-call | tf_op jit(solution)/shard_map/dkv/pallas_call | solution.py:363
  775.3 19.9 %dkv.7 = (f32[1024,384]{1,0:T(8,128)}, f32[1024,384]{1,0:T(8,128)}) custom-call(s32[10]{0:T(128)} %pad_add_fusion.sc, bf16[1024,384]{1,0:T(8,128)(2,1)} %get-tuple-element.138.k_ref, bf16[1024,384]{1,0:T(8,128)(2,1)} %get-tuple-element.139.v_ref, bf16[8192,384]{1,0:T(8,128)(2,1)} %all-gather.5.cloned.1.call-done.q_ref, ...), custom_call_target="tpu_custom_call", output_to_operand_aliasing={{0}: (6, {}), {1}: (7, {})} | custom-call | tf_op jit(solution)/shard_map/dkv/pallas_call | solution.py:363
  829.2 11.4 convolution_convert_fusion.1
  856.6 12.7 %collective-permute-done.87 = bf16[256,768]{1,0:T(8,128)(2,1)S(1)} collective-permute-done((bf16[256,768]{1,0:T(8,128)(2,1)S(1)}, bf16[256,768]{1,0:T(8,128)(2,1)S(1)}, u32[]{:S(2)}, u32[]{:S(2)}) %collective-permute-start.87) | collective-permute-done | bytes 393248 | tf_op jit(solution)/shard_map/ppermute | solution.py:623
  871.4 17.3 %collective-permute-start.79 = (bf16[256,1536]{1,0:T(8,128)(2,1)}, bf16[256,1536]{1,0:T(8,128)(2,1)}, u32[]{:S(2)}, u32[]{:S(2)}) collective-permute-start(bf16[256,1536]{1,0:T(8,128)(2,1)} %get-tuple-element.216), channel_id=1, source_target_pairs={{0,1},{3,2},{4,5},{7,6},{8,9},{11,10},{12,13},{15,14},{16,17},{19,... | collective-permute-start | bytes 2359304 | tf_op jit(solution)/shard_map/ppermute | solution.py:660
  921.0 9.7 collective-permute-start.92
  930.9 19.1 %all_gather.25 = f32[4,8,256]{2,1,0:T(8,128)S(1)} all-gather(f32[1,8,256]{2,1,0:T(8,128)S(1)} %reshape.302), channel_id=1, replica_groups=mesh['wide'=8,'narrow'=4] {'narrow'}, dimensions={0}, use_global_device_ids=true | all-gather | bytes 40960 | tf_op jit(solution)/shard_map/all_gather | solution.py:643
  950.3 10.6 all_gather.26
  966.5 13.1 %all_gather.27 = f32[4,8,128]{2,1,0:T(8,128)S(1)} all-gather(f32[1,8,128]{2,1,0:T(8,128)S(1)} %bitcast.111), channel_id=1, replica_groups=mesh['wide'=8,'narrow'=4] {'narrow'}, dimensions={0}, use_global_device_ids=true | all-gather | bytes 20480 | tf_op jit(solution)/shard_map/all_gather | solution.py:643
  988.1 28.2 %collective-permute-start.94 = (bf16[256,1024]{1,0:T(8,128)(2,1)S(1)}, bf16[256,1024]{1,0:T(8,128)(2,1)S(1)}, u32[]{:S(2)}, u32[]{:S(2)}) collective-permute-start(bf16[256,1024]{1,0:T(8,128)(2,1)S(1)} %get-tuple-element.316), channel_id=1, source_target_pairs={{0,1},{3,2},{1,0},{2,3},{4,5},{7,6},{5,4},{6,7},{8,9},{11,10},{9,8... | collective-permute-start | bytes 1572872 | tf_op jit(solution)/shard_map/ppermute | solution.py:657
  1018.8 10.9 collective-permute-start.76
  1029.7 10.3 collective-permute-done.95
  1043.0 13.8 %collective-permute-done.81 = bf16[256,1536]{1,0:T(8,128)(2,1)S(1)} collective-permute-done((bf16[256,1536]{1,0:T(8,128)(2,1)S(1)}, bf16[256,1536]{1,0:T(8,128)(2,1)S(1)}, u32[]{:S(2)}, u32[]{:S(2)}) %collective-permute-start.81) | collective-permute-done | bytes 786464 | tf_op jit(solution)/shard_map/ppermute | solution.py:657
  1060.5 10.9 collective-permute-start.97
  1105.1 8.7 collective-permute-done.83
  1119.4 8.6 collective-permute-done.78
  (660 shorter events, 477.4 us)
Async XLA Ops:
  7.2 172.2 %all-gather.3.cloned.1.call-start = ((), (), s32[]{:S(2)}) async-start(), calls=%async_computation.5 | async-start | bytes 3538944 | tf_op jit(solution)/shard_map/all_gather | solution.py:784
  64.1 31.2 %collective-permute-start.8 = (bf16[1024,384]{1,0:T(8,128)(2,1)}, bf16[1024,384]{1,0:T(8,128)(2,1)}, u32[]{:S(2)}, u32[]{:S(2)}) collective-permute-start(bf16[1024,384]{1,0:T(8,128)(2,1)} %get-tuple-element.139.v_ref), channel_id=1, source_target_pairs={{0,4},{4,0},{8,12},{12,8},{16,20},{20,16},{24,28},{28,24},{1,5},{5... | collective-permute-start | bytes 2359304 | tf_op jit(solution)/shard_map/ppermute | solution.py:623
  66.5 31.6 %collective-permute-start.9 = (bf16[512,384]{1,0:T(8,128)(2,1)}, bf16[512,384]{1,0:T(8,128)(2,1)}, u32[]{:S(2)}, u32[]{:S(2)}) collective-permute-start(bf16[512,384]{1,0:T(8,128)(2,1)} %get-tuple-element.384), channel_id=1, source_target_pairs={{0,8},{4,12},{8,0},{12,4},{16,24},{20,28},{24,16},{28,20},{1,9},{5... | collective-permute-start | bytes 1179656 | tf_op jit(solution)/shard_map/ppermute | solution.py:623
  68.6 45.5 %collective-permute-start = (bf16[1024,384]{1,0:T(8,128)(2,1)}, bf16[1024,384]{1,0:T(8,128)(2,1)}, u32[]{:S(2)}, u32[]{:S(2)}) collective-permute-start(bf16[1024,384]{1,0:T(8,128)(2,1)} %get-tuple-element.138.k_ref), channel_id=1, source_target_pairs={{0,4},{4,0},{8,12},{12,8},{16,20},{20,16},{24,28},{28,24},{1,5},{5... | collective-permute-start | bytes 2359304 | tf_op jit(solution)/shard_map/ppermute | solution.py:623
  76.4 530.0 %all-gather.5.cloned.1.call-start = ((), (), s32[]{:S(2)}) async-start(), calls=%async_computation.6 | async-start | bytes 7077888 | tf_op jit(solution)/shard_map/all_gather | solution.py:791
  81.4 27.8 %collective-permute-start.11 = (bf16[1024,384]{1,0:T(8,128)(2,1)}, bf16[1024,384]{1,0:T(8,128)(2,1)}, u32[]{:S(2)}, u32[]{:S(2)}) collective-permute-start(bf16[1024,384]{1,0:T(8,128)(2,1)} %pad_maximum_fusion.4), channel_id=1, source_target_pairs={{0,8},{4,12},{8,0},{12,4},{16,24},{20,28},{24,16},{28,20},{1,9},{5... | collective-permute-start | bytes 2359304 | tf_op jit(solution)/shard_map/ppermute | solution.py:623
  92.7 30.3 %collective-permute-start.1 = (bf16[512,384]{1,0:T(8,128)(2,1)S(1)}, bf16[512,384]{1,0:T(8,128)(2,1)S(1)}, u32[]{:S(2)}, u32[]{:S(2)}) collective-permute-start(bf16[512,384]{1,0:T(8,128)(2,1)S(1)} %copy-done.27), channel_id=1, source_target_pairs={{0,8},{4,12},{8,0},{12,4},{16,24},{20,28},{24,16},{28,20},{1,9},{5... | collective-permute-start | bytes 1179656 | tf_op jit(solution)/shard_map/ppermute | solution.py:623
  95.3 43.9 %collective-permute-start.3 = (bf16[1024,384]{1,0:T(8,128)(2,1)S(1)}, bf16[1024,384]{1,0:T(8,128)(2,1)S(1)}, u32[]{:S(2)}, u32[]{:S(2)}) collective-permute-start(bf16[1024,384]{1,0:T(8,128)(2,1)S(1)} %pad_maximum_fusion.2), channel_id=1, source_target_pairs={{0,8},{4,12},{8,0},{12,4},{16,24},{20,28},{24,16},{28,20},{1,9},{5... | collective-permute-start | bytes 2359304 | tf_op jit(solution)/shard_map/ppermute | solution.py:623
  114.0 31.3 %collective-permute-start.12 = (bf16[1024,384]{1,0:T(8,128)(2,1)}, bf16[1024,384]{1,0:T(8,128)(2,1)}, u32[]{:S(2)}, u32[]{:S(2)}) collective-permute-start(bf16[1024,384]{1,0:T(8,128)(2,1)} %get-tuple-element.407), channel_id=1, source_target_pairs={{0,4},{4,0},{8,12},{12,8},{16,20},{20,16},{24,28},{28,24},{1,5},{5... | collective-permute-start | bytes 2359304 | tf_op jit(solution)/shard_map/ppermute | solution.py:623
  116.2 31.3 %collective-permute-start.13 = (bf16[1024,384]{1,0:T(8,128)(2,1)}, bf16[1024,384]{1,0:T(8,128)(2,1)}, u32[]{:S(2)}, u32[]{:S(2)}) collective-permute-start(bf16[1024,384]{1,0:T(8,128)(2,1)} %get-tuple-element.406), channel_id=1, source_target_pairs={{0,16},{4,20},{8,24},{12,28},{16,0},{20,4},{24,8},{28,12},{1,17},{... | collective-permute-start | bytes 2359304 | tf_op jit(solution)/shard_map/ppermute | solution.py:623
  199.1 26.0 %collective-permute-start.19 = (bf16[256,1536]{1,0:T(8,128)(2,1)S(1)}, bf16[256,1536]{1,0:T(8,128)(2,1)S(1)}, u32[]{:S(2)}, u32[]{:S(2)}) collective-permute-start(bf16[256,1536]{1,0:T(8,128)(2,1)S(1)} %convolution_convert_fusion.5), channel_id=1, source_target_pairs={{0,1},{3,2},{4,5},{7,6},{8,9},{11,10},{12,13},{15,14},{16,17},{19,... | collective-permute-start | bytes 2359304 | tf_op jit(solution)/shard_map/ppermute | solution.py:660
  223.0 41.5 %collective-permute-start.16 = (bf16[256,1536]{1,0:T(8,128)(2,1)}, bf16[256,1536]{1,0:T(8,128)(2,1)}, u32[]{:S(2)}, u32[]{:S(2)}) collective-permute-start(bf16[256,1536]{1,0:T(8,128)(2,1)} %convolution_convert_fusion.7), channel_id=1, source_target_pairs={{0,1},{3,2},{4,5},{7,6},{8,9},{11,10},{12,13},{15,14},{16,17},{19,... | collective-permute-start | bytes 2359304 | tf_op jit(solution)/shard_map/ppermute | solution.py:660
  226.2 40.9 %collective-permute-start.20 = (bf16[256,1536]{1,0:T(8,128)(2,1)}, bf16[256,1536]{1,0:T(8,128)(2,1)}, u32[]{:S(2)}, u32[]{:S(2)}) collective-permute-start(bf16[256,1536]{1,0:T(8,128)(2,1)} %add.373), channel_id=1, source_target_pairs={{1,2},{2,1},{5,6},{6,5},{9,10},{10,9},{13,14},{14,13},{17,18},{18,... | collective-permute-start | bytes 2359304 | tf_op jit(solution)/shard_map/ppermute | solution.py:664
  227.8 860.2 %reduce-scatter.14.cloned.1.call-start = ((), (), s32[]{:S(2)}) async-start(), calls=%async_computation.11 | async-start | bytes 3538944 | tf_op jit(solution)/shard_map/reduce_scatter | solution.py:693
  271.5 33.3 %collective-permute-start.18 = (bf16[256,1536]{1,0:T(8,128)(2,1)S(1)}, bf16[256,1536]{1,0:T(8,128)(2,1)S(1)}, u32[]{:S(2)}, u32[]{:S(2)}) collective-permute-start(bf16[256,1536]{1,0:T(8,128)(2,1)S(1)} %get-tuple-element.342), channel_id=1, source_target_pairs={{0,1},{3,2},{1,0},{2,3},{4,5},{7,6},{5,4},{6,7},{8,9},{11,10},{9,8... | collective-permute-start | bytes 2359304 | tf_op jit(solution)/shard_map/ppermute | solution.py:657
  433.7 34.1 %collective-permute-start.38 = (bf16[256,1536]{1,0:T(8,128)(2,1)S(1)}, bf16[256,1536]{1,0:T(8,128)(2,1)S(1)}, u32[]{:S(2)}, u32[]{:S(2)}) collective-permute-start(bf16[256,1536]{1,0:T(8,128)(2,1)S(1)} %get-tuple-element.359), channel_id=1, source_target_pairs={{1,2},{2,1},{5,6},{6,5},{9,10},{10,9},{13,14},{14,13},{17,18},{18,... | collective-permute-start | bytes 2359304 | tf_op jit(solution)/shard_map/ppermute | solution.py:664
  446.5 31.5 %collective-permute-start.34 = (bf16[256,1536]{1,0:T(8,128)(2,1)}, bf16[256,1536]{1,0:T(8,128)(2,1)}, u32[]{:S(2)}, u32[]{:S(2)}) collective-permute-start(bf16[256,1536]{1,0:T(8,128)(2,1)} %get-tuple-element.361), channel_id=1, source_target_pairs={{1,2},{2,1},{5,6},{6,5},{9,10},{10,9},{13,14},{14,13},{17,18},{18,... | collective-permute-start | bytes 2359304 | tf_op jit(solution)/shard_map/ppermute | solution.py:664
  477.7 612.3 %reduce-scatter.10.cloned.1.call-start = ((), (), s32[]{:S(2)}) async-start(), calls=%async_computation.9 | async-start | bytes 1327104 | tf_op jit(solution)/shard_map/reduce_scatter | solution.py:693
  499.4 64.1 %collective-permute-start.66 = (bf16[256,512]{1,0:T(8,128)(2,1)}, bf16[256,512]{1,0:T(8,128)(2,1)S(1)}, u32[]{:S(2)}, u32[]{:S(2)}) collective-permute-start(bf16[256,512]{1,0:T(8,128)(2,1)} %get-tuple-element.192.d_ref.x_ref), channel_id=1, source_target_pairs={{0,4},{4,0},{8,12},{12,8},{16,20},{20,16},{24,28},{28,24},{1,5},{5... | collective-permute-start | bytes 786440 | tf_op jit(solution)/shard_map/ppermute | solution.py:623
  500.4 62.1 %collective-permute-start.68 = (bf16[128,512]{1,0:T(8,128)(2,1)S(1)}, bf16[128,512]{1,0:T(8,128)(2,1)S(1)}, u32[]{:S(2)}, u32[]{:S(2)}) collective-permute-start(bf16[128,512]{1,0:T(8,128)(2,1)S(1)} %get-tuple-element.416), channel_id=1, source_target_pairs={{0,16},{4,20},{8,24},{12,28},{16,0},{20,4},{24,8},{28,12},{1,17},{... | collective-permute-start | bytes 393224 | tf_op jit(solution)/shard_map/ppermute | solution.py:623
  510.4 52.9 %collective-permute-start.60 = (bf16[128,512]{1,0:T(8,128)(2,1)S(1)}, bf16[128,512]{1,0:T(8,128)(2,1)S(1)}, u32[]{:S(2)}, u32[]{:S(2)}) collective-permute-start(bf16[128,512]{1,0:T(8,128)(2,1)S(1)} %get-tuple-element.424), channel_id=1, source_target_pairs={{0,16},{4,20},{8,24},{12,28},{16,0},{20,4},{24,8},{28,12},{1,17},{... | collective-permute-start | bytes 393224 | tf_op jit(solution)/shard_map/ppermute | solution.py:623
  513.7 56.8 %collective-permute-start.58 = (bf16[256,512]{1,0:T(8,128)(2,1)}, bf16[256,512]{1,0:T(8,128)(2,1)S(1)}, u32[]{:S(2)}, u32[]{:S(2)}) collective-permute-start(bf16[256,512]{1,0:T(8,128)(2,1)} %get-tuple-element.191.d_ref.x_ref), channel_id=1, source_target_pairs={{0,4},{4,0},{8,12},{12,8},{16,20},{20,16},{24,28},{28,24},{1,5},{5... | collective-permute-start | bytes 786440 | tf_op jit(solution)/shard_map/ppermute | solution.py:623
  513.7 82.5 %collective-permute-start.40 = (bf16[256,1536]{1,0:T(8,128)(2,1)S(1)}, bf16[256,1536]{1,0:T(8,128)(2,1)S(1)}, u32[]{:S(2)}, u32[]{:S(2)}) collective-permute-start(bf16[256,1536]{1,0:T(8,128)(2,1)S(1)} %get-tuple-element.356), channel_id=1, source_target_pairs={{1,2},{2,1},{5,6},{6,5},{9,10},{10,9},{13,14},{14,13},{17,18},{18,... | collective-permute-start | bytes 2359304 | tf_op jit(solution)/shard_map/ppermute | solution.py:664
  562.6 35.2 %collective-permute-start.36 = (bf16[256,1536]{1,0:T(8,128)(2,1)S(1)}, bf16[256,1536]{1,0:T(8,128)(2,1)S(1)}, u32[]{:S(2)}, u32[]{:S(2)}) collective-permute-start(bf16[256,1536]{1,0:T(8,128)(2,1)S(1)} %get-tuple-element.358), channel_id=1, source_target_pairs={{1,2},{2,1},{5,6},{6,5},{9,10},{10,9},{13,14},{14,13},{17,18},{18,... | collective-permute-start | bytes 2359304 | tf_op jit(solution)/shard_map/ppermute | solution.py:664
  597.8 47.6 %collective-permute-start.41 = (bf16[256,1536]{1,0:T(8,128)(2,1)}, bf16[256,1536]{1,0:T(8,128)(2,1)}, u32[]{:S(2)}, u32[]{:S(2)}) collective-permute-start(bf16[256,1536]{1,0:T(8,128)(2,1)} %add.394), channel_id=1, source_target_pairs={{1,0},{2,3},{5,4},{6,7},{9,8},{10,11},{13,12},{14,15},{17,16},{18,... | collective-permute-start | bytes 2359304 | tf_op jit(solution)/shard_map/ppermute | solution.py:662
  599.3 55.0 %collective-permute-start.37 = (bf16[256,1536]{1,0:T(8,128)(2,1)S(1)}, bf16[256,1536]{1,0:T(8,128)(2,1)}, u32[]{:S(2)}, u32[]{:S(2)}) collective-permute-start(bf16[256,1536]{1,0:T(8,128)(2,1)S(1)} %add.390), channel_id=1, source_target_pairs={{1,0},{2,3},{5,4},{6,7},{9,8},{10,11},{13,12},{14,15},{17,16},{18,... | collective-permute-start | bytes 2359304 | tf_op jit(solution)/shard_map/ppermute | solution.py:662
  653.2 68.6 %collective-permute-start.50 = (bf16[256,512]{1,0:T(8,128)(2,1)}, bf16[256,512]{1,0:T(8,128)(2,1)}, u32[]{:S(2)}, u32[]{:S(2)}) collective-permute-start(bf16[256,512]{1,0:T(8,128)(2,1)} %get-tuple-element.190.d_ref.x_ref), channel_id=1, source_target_pairs={{0,4},{4,0},{8,12},{12,8},{16,20},{20,16},{24,28},{28,24},{1,5},{5... | collective-permute-start | bytes 786440 | tf_op jit(solution)/shard_map/ppermute | solution.py:623
  654.2 65.3 %collective-permute-start.52 = (bf16[128,512]{1,0:T(8,128)(2,1)S(1)}, bf16[128,512]{1,0:T(8,128)(2,1)S(1)}, u32[]{:S(2)}, u32[]{:S(2)}) collective-permute-start(bf16[128,512]{1,0:T(8,128)(2,1)S(1)} %get-tuple-element.432), channel_id=1, source_target_pairs={{0,16},{4,20},{8,24},{12,28},{16,0},{20,4},{24,8},{28,12},{1,17},{... | collective-permute-start | bytes 393224 | tf_op jit(solution)/shard_map/ppermute | solution.py:623
  662.3 63.7 %collective-permute-start.42 = (bf16[256,512]{1,0:T(8,128)(2,1)}, bf16[256,512]{1,0:T(8,128)(2,1)}, u32[]{:S(2)}, u32[]{:S(2)}) collective-permute-start(bf16[256,512]{1,0:T(8,128)(2,1)} %get-tuple-element.187.d_ref.x_ref), channel_id=1, source_target_pairs={{0,4},{4,0},{8,12},{12,8},{16,20},{20,16},{24,28},{28,24},{1,5},{5... | collective-permute-start | bytes 786440 | tf_op jit(solution)/shard_map/ppermute | solution.py:623
  668.3 53.2 %collective-permute-start.44 = (bf16[128,512]{1,0:T(8,128)(2,1)S(1)}, bf16[128,512]{1,0:T(8,128)(2,1)S(1)}, u32[]{:S(2)}, u32[]{:S(2)}) collective-permute-start(bf16[128,512]{1,0:T(8,128)(2,1)S(1)} %get-tuple-element.440), channel_id=1, source_target_pairs={{0,16},{4,20},{8,24},{12,28},{16,0},{20,4},{24,8},{28,12},{1,17},{... | collective-permute-start | bytes 393224 | tf_op jit(solution)/shard_map/ppermute | solution.py:623
  670.8 54.5 %collective-permute-start.51 = (bf16[128,512]{1,0:T(8,128)(2,1)S(1)}, bf16[128,512]{1,0:T(8,128)(2,1)S(1)}, u32[]{:S(2)}, u32[]{:S(2)}) collective-permute-start(bf16[128,512]{1,0:T(8,128)(2,1)S(1)} %get-tuple-element.433), channel_id=1, source_target_pairs={{0,8},{4,12},{8,0},{12,4},{16,24},{20,28},{24,16},{28,20},{1,9},{5... | collective-permute-start | bytes 393224 | tf_op jit(solution)/shard_map/ppermute | solution.py:623
  719.5 415.7 %reduce-scatter.6.cloned.1.call-start = ((), (), s32[]{:S(2)}) async-start(), calls=%async_computation.7 | async-start | bytes 3981312 | tf_op jit(solution)/shard_map/reduce_scatter | solution.py:693
  748.0 26.6 %collective-permute-start.49 = (bf16[256,512]{1,0:T(8,128)(2,1)S(1)}, bf16[256,512]{1,0:T(8,128)(2,1)S(1)}, u32[]{:S(2)}, u32[]{:S(2)}) collective-permute-start(bf16[256,512]{1,0:T(8,128)(2,1)S(1)} %pad_maximum_fusion.27), channel_id=1, source_target_pairs={{0,4},{4,0},{8,12},{12,8},{16,20},{20,16},{24,28},{28,24},{1,5},{5... | collective-permute-start | bytes 786440 | tf_op jit(solution)/shard_map/ppermute | solution.py:623
  829.2 308.5 %reduce-scatter.12.cloned.1.call-start = ((), (), s32[]{:S(2)}) async-start(), calls=%async_computation.10 | async-start | bytes 7077888 | tf_op jit(solution)/shard_map/reduce_scatter | solution.py:693
  840.6 299.6 %reduce-scatter.8.cloned.1.call-start = ((), (), s32[]{:S(2)}) async-start(), calls=%async_computation.8 | async-start | bytes 7077888 | tf_op jit(solution)/shard_map/reduce_scatter | solution.py:693
  871.4 108.3 %collective-permute-start.79 = (bf16[256,1536]{1,0:T(8,128)(2,1)}, bf16[256,1536]{1,0:T(8,128)(2,1)}, u32[]{:S(2)}, u32[]{:S(2)}) collective-permute-start(bf16[256,1536]{1,0:T(8,128)(2,1)} %get-tuple-element.216), channel_id=1, source_target_pairs={{0,1},{3,2},{4,5},{7,6},{8,9},{11,10},{12,13},{15,14},{16,17},{19,... | collective-permute-start | bytes 2359304 | tf_op jit(solution)/shard_map/ppermute | solution.py:660
  888.7 97.0 %collective-permute-start.74 = (bf16[256,1536]{1,0:T(8,128)(2,1)}, bf16[256,1536]{1,0:T(8,128)(2,1)}, u32[]{:S(2)}, u32[]{:S(2)}) collective-permute-start(bf16[256,1536]{1,0:T(8,128)(2,1)} %get-tuple-element.213), channel_id=1, source_target_pairs={{0,1},{3,2},{4,5},{7,6},{8,9},{11,10},{12,13},{15,14},{16,17},{19,... | collective-permute-start | bytes 2359304 | tf_op jit(solution)/shard_map/ppermute | solution.py:660
  921.0 61.0 %collective-permute-start.92 = (bf16[256,1024]{1,0:T(8,128)(2,1)}, bf16[256,1024]{1,0:T(8,128)(2,1)}, u32[]{:S(2)}, u32[]{:S(2)}) collective-permute-start(bf16[256,1024]{1,0:T(8,128)(2,1)} %slice.366), channel_id=1, source_target_pairs={{0,1},{3,2},{4,5},{7,6},{8,9},{11,10},{12,13},{15,14},{16,17},{19,... | collective-permute-start | bytes 1572872 | tf_op jit(solution)/shard_map/ppermute | solution.py:660
  981.3 37.1 %collective-permute-start.80 = (bf16[256,1536]{1,0:T(8,128)(2,1)S(1)}, bf16[256,1536]{1,0:T(8,128)(2,1)S(1)}, u32[]{:S(2)}, u32[]{:S(2)}) collective-permute-start(bf16[256,1536]{1,0:T(8,128)(2,1)S(1)} %add.399), channel_id=1, source_target_pairs={{1,2},{2,1},{5,6},{6,5},{9,10},{10,9},{13,14},{14,13},{17,18},{18,... | collective-permute-start | bytes 2359304 | tf_op jit(solution)/shard_map/ppermute | solution.py:664
  987.0 31.7 %collective-permute-start.75 = (bf16[256,1536]{1,0:T(8,128)(2,1)S(1)}, bf16[256,1536]{1,0:T(8,128)(2,1)S(1)}, u32[]{:S(2)}, u32[]{:S(2)}) collective-permute-start(bf16[256,1536]{1,0:T(8,128)(2,1)S(1)} %add.395), channel_id=1, source_target_pairs={{1,2},{2,1},{5,6},{6,5},{9,10},{10,9},{13,14},{14,13},{17,18},{18,... | collective-permute-start | bytes 2359304 | tf_op jit(solution)/shard_map/ppermute | solution.py:664
  988.1 41.6 %collective-permute-start.94 = (bf16[256,1024]{1,0:T(8,128)(2,1)S(1)}, bf16[256,1024]{1,0:T(8,128)(2,1)S(1)}, u32[]{:S(2)}, u32[]{:S(2)}) collective-permute-start(bf16[256,1024]{1,0:T(8,128)(2,1)S(1)} %get-tuple-element.316), channel_id=1, source_target_pairs={{0,1},{3,2},{1,0},{2,3},{4,5},{7,6},{5,4},{6,7},{8,9},{11,10},{9,8... | collective-permute-start | bytes 1572872 | tf_op jit(solution)/shard_map/ppermute | solution.py:657
  1018.6 38.2 %collective-permute-start.81 = (bf16[256,1536]{1,0:T(8,128)(2,1)S(1)}, bf16[256,1536]{1,0:T(8,128)(2,1)S(1)}, u32[]{:S(2)}, u32[]{:S(2)}) collective-permute-start(bf16[256,1536]{1,0:T(8,128)(2,1)S(1)} %get-tuple-element.320), channel_id=1, source_target_pairs={{0,1},{3,2},{1,0},{2,3},{4,5},{7,6},{5,4},{6,7},{8,9},{11,10},{9,8... | collective-permute-start | bytes 2359304 | tf_op jit(solution)/shard_map/ppermute | solution.py:657
  1018.8 52.6 %collective-permute-start.76 = (bf16[256,1536]{1,0:T(8,128)(2,1)S(1)}, bf16[256,1536]{1,0:T(8,128)(2,1)S(1)}, u32[]{:S(2)}, u32[]{:S(2)}) collective-permute-start(bf16[256,1536]{1,0:T(8,128)(2,1)S(1)} %get-tuple-element.322), channel_id=1, source_target_pairs={{0,1},{3,2},{1,0},{2,3},{4,5},{7,6},{5,4},{6,7},{8,9},{11,10},{9,8... | collective-permute-start | bytes 2359304 | tf_op jit(solution)/shard_map/ppermute | solution.py:657
  1040.9 36.1 %collective-permute-start.98 = (bf16[256,1024]{1,0:T(8,128)(2,1)S(1)}, bf16[256,1024]{1,0:T(8,128)(2,1)}, u32[]{:S(2)}, u32[]{:S(2)}) collective-permute-start(bf16[256,1024]{1,0:T(8,128)(2,1)S(1)} %get-tuple-element.346), channel_id=1, source_target_pairs={{1,2},{2,1},{5,6},{6,5},{9,10},{10,9},{13,14},{14,13},{17,18},{18,... | collective-permute-start | bytes 1572872 | tf_op jit(solution)/shard_map/ppermute | solution.py:664
  1072.7 25.8 %collective-permute-start.77 = (bf16[256,1536]{1,0:T(8,128)(2,1)}, bf16[256,1536]{1,0:T(8,128)(2,1)}, u32[]{:S(2)}, u32[]{:S(2)}) collective-permute-start(bf16[256,1536]{1,0:T(8,128)(2,1)} %get-tuple-element.354), channel_id=1, source_target_pairs={{1,2},{2,1},{5,6},{6,5},{9,10},{10,9},{13,14},{14,13},{17,18},{18,... | collective-permute-start | bytes 2359304 | tf_op jit(solution)/shard_map/ppermute | solution.py:664
  1081.8 32.1 %collective-permute-start.83 = (bf16[256,1536]{1,0:T(8,128)(2,1)S(1)}, bf16[256,1536]{1,0:T(8,128)(2,1)}, u32[]{:S(2)}, u32[]{:S(2)}) collective-permute-start(bf16[256,1536]{1,0:T(8,128)(2,1)S(1)} %add.402), channel_id=1, source_target_pairs={{1,0},{2,3},{5,4},{6,7},{9,8},{10,11},{13,12},{14,15},{17,16},{18,... | collective-permute-start | bytes 2359304 | tf_op jit(solution)/shard_map/ppermute | solution.py:662
  1100.1 27.9 %collective-permute-start.78 = (bf16[256,1536]{1,0:T(8,128)(2,1)S(1)}, bf16[256,1536]{1,0:T(8,128)(2,1)S(1)}, u32[]{:S(2)}, u32[]{:S(2)}) collective-permute-start(bf16[256,1536]{1,0:T(8,128)(2,1)S(1)} %add.398), channel_id=1, source_target_pairs={{1,0},{2,3},{5,4},{6,7},{9,8},{10,11},{13,12},{14,15},{17,16},{18,... | collective-permute-start | bytes 2359304 | tf_op jit(solution)/shard_map/ppermute | solution.py:662
  1103.8 29.9 %collective-permute-start.101 = (bf16[256,1024]{1,0:T(8,128)(2,1)S(1)}, bf16[256,1024]{1,0:T(8,128)(2,1)S(1)}, u32[]{:S(2)}, u32[]{:S(2)}) collective-permute-start(bf16[256,1024]{1,0:T(8,128)(2,1)S(1)} %add.438), channel_id=1, source_target_pairs={{1,0},{2,3},{5,4},{6,7},{9,8},{10,11},{13,12},{14,15},{17,16},{18,... | collective-permute-start | bytes 1572872 | tf_op jit(solution)/shard_map/ppermute | solution.py:662
  (146 other events, 2162.6 us)
Sparse Core Ops, SparseCore 0:
  76.5 45.1 all-gather.2
  227.9 42.7 all-gather.4
  477.8 45.9 reduce-scatter.13
  719.6 43.3 reduce-scatter.9
  829.3 63.6 reduce-scatter.5
  896.2 66.4 reduce-scatter.11
  966.5 61.7 reduce-scatter.7

commit v3 on v2

--- a/solution.py
+++ b/solution.py
@@ -143,6 +143,14 @@
     return mm(e, jnp.where(mask, v, jnp.ones_like(v)))
 
 
+def loose(n):
+    return [pl.BlockSpec(memory_space=pl.ANY)] * n
+
+
+def item_block(j, s):
+    return jnp.minimum(j, s[0] - 1)
+
+
 def attend_kernel(sc, q_ref, k_ref, v_ref, ck_ref, cv_ref, tg_ref, mix_ref, o_ref, li_ref, acc):
     j = pl.program_id(1)
     masks = halves(128)
@@ -177,36 +185,39 @@
         li_ref[...] = li
 
 
-def attend_call(sc, q, k, v, cap, tg, c, block):
+def attend_call(sc, q, k, v, ck, cv, tg, h):
     n = q.shape[1]
     pairs = n // 128
-    text = cap.shape[0] * block // k.shape[0]
+    block = k.shape[0] // SPAN
+    bq = 2 * BR
+    text = ck.shape[0]
     mine = lambda p, j, s: (0, p)
+    other = lambda p, j, s: (item_block(j, s), p)
     return pl.pallas_call(
         attend_kernel,
         grid_spec=pltpu.PrefetchScalarGridSpec(
             num_scalar_prefetch=1,
             grid=(pairs, SPAN),
             in_specs=[
-                pl.BlockSpec((BR, 128), lambda p, j, s: (c, p)),
-                pl.BlockSpec((block, 128), lambda p, j, s: (s[2 + j], p)),
-                pl.BlockSpec((block, 128), lambda p, j, s: (s[2 + j], p)),
-                pl.BlockSpec((text, 128), lambda p, j, s: (s[1], p)),
-                pl.BlockSpec((text, 128), lambda p, j, s: (s[1], pairs + p)),
+                pl.BlockSpec((bq, 128), lambda p, j, s: (h, p)),
+                pl.BlockSpec((block, 128), other),
+                pl.BlockSpec((block, 128), other),
+                pl.BlockSpec((text, 128), mine),
+                pl.BlockSpec((text, 128), mine),
                 pl.BlockSpec((1, 128), mine),
             ],
-            out_specs=[pl.BlockSpec((BR, 128), mine)] * 3,
-            scratch_shapes=[pltpu.VMEM((2, BR, 128), f32)],
+            out_specs=[pl.BlockSpec((bq, 128), mine)] * 3,
+            scratch_shapes=[pltpu.VMEM((2, bq, 128), f32)],
         ),
-        out_shape=[sds((BR, n), bf16), sds((BR, n), bf16), sds((BR, n), f32)],
+        out_shape=[sds((bq, n), bf16), sds((bq, n), bf16), sds((bq, n), f32)],
         compiler_params=params(2),
         name="attend",
-    )(sc, q, k, v, cap, cap, tg)
-
-
-def caption_back_kernel(sc, q_ref, d_ref, ck_ref, cv_ref, tg_ref, dq_ref, dk_ref, dv_ref, gs_ref):
+    )(sc, q, k, v, ck, cv, tg)
+
+
+def caption_back_kernel(q_ref, da_ref, db_ref, ck_ref, cv_ref, tg_ref, dq_ref, dk_ref, dv_ref, gs_ref):
     masks = halves(128)
-    q, d = q_ref[...], d_ref[...]
+    q, d = q_ref[...], jnp.concatenate([da_ref[...], db_ref[...]], 0)
     dq = jnp.zeros(q.shape, f32)
     dk = jnp.zeros(ck_ref.shape, f32)
     dv = jnp.zeros(ck_ref.shape, f32)
@@ -229,33 +240,33 @@
     gs_ref[...] = jnp.where(masks[0], sums[0], sums[1])
 
 
-def caption_back_call(sc, q, d, cap, tg, c, text):
+def caption_back_call(q, da, db, ck, cv, tg, h):
     n = q.shape[1]
     pairs = n // 128
-    mine = lambda p, s: (0, p)
+    bq = 2 * BR
+    text = ck.shape[0]
+    mine = lambda p: (0, p)
     return pl.pallas_call(
         caption_back_kernel,
-        grid_spec=pltpu.PrefetchScalarGridSpec(
-            num_scalar_prefetch=1,
-            grid=(pairs,),
-            in_specs=[
-                pl.BlockSpec((BR, 128), lambda p, s: (c, p)),
-                pl.BlockSpec((BR, 128), mine),
-                pl.BlockSpec((text, 128), lambda p, s: (s[1], p)),
-                pl.BlockSpec((text, 128), lambda p, s: (s[1], pairs + p)),
-                pl.BlockSpec((1, 128), mine),
-            ],
-            out_specs=[
-                pl.BlockSpec((BR, 128), mine),
-                pl.BlockSpec((text, 128), mine),
-                pl.BlockSpec((text, 128), mine),
-                pl.BlockSpec((1, 128), mine),
-            ],
-        ),
-        out_shape=[sds((BR, n), f32), sds((text, n), f32), sds((text, n), f32), sds((1, n), f32)],
+        grid=(pairs,),
+        in_specs=[
+            pl.BlockSpec((bq, 128), lambda p: (h, p)),
+            pl.BlockSpec((BR, 128), mine),
+            pl.BlockSpec((BR, 128), mine),
+            pl.BlockSpec((text, 128), mine),
+            pl.BlockSpec((text, 128), mine),
+            pl.BlockSpec((1, 128), mine),
+        ],
+        out_specs=[
+            pl.BlockSpec((bq, 128), mine),
+            pl.BlockSpec((text, 128), mine),
+            pl.BlockSpec((text, 128), mine),
+            pl.BlockSpec((1, 128), mine),
+        ],
+        out_shape=[sds((bq, n), f32), sds((text, n), f32), sds((text, n), f32), sds((1, n), f32)],
         compiler_params=params(1),
         name="caption_back",
-    )(sc, q, d, cap, cap, tg)
+    )(q, da, db, ck, cv, tg)
 
 
 def minus_delta(rows, head):
@@ -263,7 +274,8 @@
     return jnp.where((lane >= 3 * head) & (lane < 3 * head + 3), -1.0, 0.0).astype(bf16)
 
 
-def dq_kernel(sc, q_ref, d_ref, x_ref, k_ref, v_ref, c_ref, dq_ref, acc):
+def dq_kernel(sc, q_ref, da_ref, xa_ref, db_ref, xb_ref, k_ref, v_ref, c_ref, *rest):
+    dq_ref, acc = rest[-2:]
     pair = pl.program_id(0)
     j = pl.program_id(1)
     masks = halves(128)
@@ -276,7 +288,9 @@
     @pl.when(j < sc[0])
     def _():
         q = q_ref[...]
-        dx = jnp.concatenate([d_ref[...], x_ref[...]], 1)
+        dx = jnp.concatenate(
+            [jnp.concatenate([da_ref[...], xa_ref[...]], 1), jnp.concatenate([db_ref[...], xb_ref[...]], 1)], 0
+        )
         total = acc[...]
         for h in range(2):
             off = minus_delta(keys, 2 * pair + h)
@@ -293,34 +307,40 @@
         dq_ref[...] = acc[...] * 0.125 + c_ref[...]
 
 
-def dq_call(sc, q, d, k, v, cap_dq, c, block):
+def dq_call(sc, q, da, db, k, v, cap_dq, h, after):
     n = q.shape[1]
     pairs = n // 128
+    block = k.shape[0] // SPAN
+    bq = 2 * BR
     mine = lambda p, j, s: (0, p)
-    other = lambda p, j, s: (s[2 + j], p)
+    extra = lambda p, j, s: (0, pairs)
+    other = lambda p, j, s: (item_block(j, s), p)
     return pl.pallas_call(
         dq_kernel,
         grid_spec=pltpu.PrefetchScalarGridSpec(
             num_scalar_prefetch=1,
             grid=(pairs, SPAN),
             in_specs=[
-                pl.BlockSpec((BR, 128), lambda p, j, s: (c, p)),
+                pl.BlockSpec((bq, 128), lambda p, j, s: (h, p)),
                 pl.BlockSpec((BR, 128), mine),
-                pl.BlockSpec((BR, 128), lambda p, j, s: (0, pairs)),
+                pl.BlockSpec((BR, 128), extra),
+                pl.BlockSpec((BR, 128), mine),
+                pl.BlockSpec((BR, 128), extra),
                 pl.BlockSpec((block, 128), other),
                 pl.BlockSpec((block, 128), other),
-                pl.BlockSpec((BR, 128), mine),
-            ],
-            out_specs=pl.BlockSpec((BR, 128), mine),
-            scratch_shapes=[pltpu.VMEM((BR, 128), f32)],
+                pl.BlockSpec((bq, 128), mine),
+            ]
+            + loose(len(after)),
+            out_specs=pl.BlockSpec((bq, 128), mine),
+            scratch_shapes=[pltpu.VMEM((bq, 128), f32)],
         ),
-        out_shape=sds((BR, n), f32),
+        out_shape=sds((bq, n), f32),
         compiler_params=params(2),
         name="dq",
-    )(sc, q, d, d, k, v, cap_dq)
-
-
-def dkv_kernel(start, sc, k_ref, v_ref, q_ref, d_ref, x_ref, *rest):
+    )(sc, q, da, da, db, db, k, v, cap_dq, *after)
+
+
+def dkv_kernel(start, sc, k_ref, v_ref, q_ref, da_ref, xa_ref, db_ref, xb_ref, *rest):
     dk_ref, dv_ref = rest[-2:]
     pair = pl.program_id(0)
     j = pl.program_id(1)
@@ -338,8 +358,9 @@
 
     @pl.when(j < sc[0])
     def _():
-        q, d = q_ref[...], d_ref[...]
-        dx = jnp.concatenate([d, x_ref[...]], 1)
+        q = q_ref[...]
+        d = jnp.concatenate([da_ref[...], db_ref[...]], 0)
+        dx = jnp.concatenate([d, jnp.concatenate([xa_ref[...], xb_ref[...]], 0)], 1)
         qs = [keep(q, m) for m in masks]
         ds = [keep(d, m) for m in masks]
         for c in range(k_ref.shape[0] // keys):
@@ -355,11 +376,15 @@
             dv_ref[at, :] = dv
 
 
-def dkv_call(sc, k, v, q_all, d_all, before, c):
+def dkv_call(sc, k, v, q_all, da, db, h, rows, at, before, after):
     t, n = k.shape
     pairs = n // 128
-    chunks = t // BR
-    mine = pl.BlockSpec((t, 128), lambda p, j, s: (0, p))
+    bq = 2 * BR
+    per = t // bq
+    mine = pl.BlockSpec((rows, 128), lambda p, j, s: (at, p))
+    out = pl.BlockSpec((rows, 128), lambda p, j, s: (0, p))
+    other = pl.BlockSpec((BR, 128), lambda p, j, s: (item_block(j, s), p))
+    extra = pl.BlockSpec((BR, 128), lambda p, j, s: (item_block(j, s), pairs))
     return pl.pallas_call(
         functools.partial(dkv_kernel, not before),
         grid_spec=pltpu.PrefetchScalarGridSpec(
@@ -368,18 +393,20 @@
             in_specs=[
                 mine,
                 mine,
-                pl.BlockSpec((BR, 128), lambda p, j, s: (s[2 + SPAN + j] * chunks + c, p)),
-                pl.BlockSpec((BR, 128), lambda p, j, s: (s[2 + j], p)),
-                pl.BlockSpec((BR, 128), lambda p, j, s: (s[2 + j], pairs)),
+                pl.BlockSpec((bq, 128), lambda p, j, s: (s[1 + SPAN + j] * per + h, p)),
+                other,
+                extra,
+                other,
+                extra,
             ]
-            + [mine] * len(before),
-            out_specs=[mine, mine],
+            + [mine] * len(before)
+            + loose(len(after)),
+            out_specs=[out, out],
         ),
-        out_shape=[sds((t, n), f32)] * 2,
-        input_output_aliases={6: 0, 7: 1} if before else {},
+        out_shape=[sds((rows, n), f32)] * 2,
         compiler_params=params(2),
         name="dkv",
-    )(sc, k, v, q_all, d_all, d_all, *before)
+    )(sc, k, v, q_all, da, da, db, db, *before, *after)
 
 
 def chunk_call(kernel, name, c, ins, specs, chunk_outs, sum_outs, whole_outs, before):
@@ -411,6 +438,28 @@
 
 def alone(width):
     return pl.BlockSpec((BR, width), lambda i: (0, 0))
+
+
+def pair_grad_kernel(a_ref, b_ref, c_ref, d_ref, o_ref):
+    n = b_ref.shape[1]
+    o_ref[:, :n] = mm_tn(a_ref[...], b_ref[...]).astype(bf16)
+    o_ref[:, n:] = mm_tn(c_ref[...], d_ref[...]).astype(bf16)
+
+
+def pair_grad_call(a, b, c, d):
+    t, m = a.shape
+    n, k = b.shape[1], d.shape[1]
+    blk = 256
+    cols = pl.BlockSpec((t, blk), lambda i: (0, i))
+    return pl.pallas_call(
+        pair_grad_kernel,
+        grid=(m // blk,),
+        in_specs=[cols, whole(b.shape), cols, whole(d.shape)],
+        out_specs=pl.BlockSpec((blk, n + k), lambda i: (i, 0)),
+        out_shape=sds((m, n + k), bf16),
+        compiler_params=params(1),
+        name="pair_grad",
+    )(a, b, c, d)
 
 
 def ffn_kernel(p_ref, at_ref, v_ref, wg_ref, wd_ref, mid_ref, gu_ref, f_ref, a_ref, h_ref):
@@ -524,7 +573,7 @@
         "out_back",
         c,
         (da, mid, at, cot, vec, w, o, li),
-        [alone(d), alone(d), alone(d), part(c, d), whole(vec.shape), whole(w.shape), alone(n), alone(n)],
+        [alone(d), alone(d), alone(d), part(c, d), whole(vec.shape), whole(w.shape), part(c % 2, n), part(c % 2, n)],
         [(BR, d, f32), (BR, n, bf16), (BR, n + 128, bf16)],
         [(1, d, f32), (1, d, f32)],
         [(t, d, bf16)],
@@ -566,7 +615,7 @@
         "dqkv",
         c,
         (dq, dk, dv, qr, kr, *tabs, hg, w, patches),
-        [alone(n)] + [part(c, n)] * 4 + [part(c, 128)] * 3 + [whole(hg.shape), whole(w.shape), part(c, d)],
+        [part(c % 2, n)] * 3 + [part(c, n)] * 2 + [part(c, 128)] * 3 + [whole(hg.shape), whole(w.shape), part(c, d)],
         [(BR, d, bf16)],
         [(2, n, f32), (1, d, f32)],
         [(t, 3 * n, bf16)],
@@ -610,60 +659,136 @@
     hs_ref[...] = col_sum(dy * xh)
 
 
-def caption_norm_kernel(kr_ref, v_ref, hg_ref, o_ref):
-    n = kr_ref.shape[1]
+def caption_norm_kernel(kr_ref, v_ref, hg_ref, k_ref, o_ref):
     x = kr_ref[...]
-    r = lax.rsqrt(head_sum(x * x, head_ones(n)) * (1.0 / HD) + EPS)
-    o_ref[:, :n] = (x * r * row(hg_ref, 2)).astype(bf16)
-    o_ref[:, n:] = v_ref[...].astype(bf16)
-
-
-def xor_gather(x):
-    half = x.shape[0] // 2
-    swap = lambda a, m: lax.ppermute(a, "wide", [(i, i ^ m) for i in range(8)])
-    a, b = x[:half], x[half:]
-    ra, rb = swap(a, 2), swap(b, 4)
-    a4, b2 = swap(jnp.concatenate([a, ra]), 4), swap(jnp.concatenate([b, rb]), 2)
-    parts = [x, None, jnp.concatenate([ra, b2[:half]]), None, jnp.concatenate([a4[:half], rb]), None, jnp.concatenate([a4[half:], b2[half:]]), None]
-    for m in (0, 2, 4, 6):
-        parts[m + 1] = swap(parts[m], 1)
-    return jnp.concatenate(parts)
-
-
-def gather_wide(x):
-    if lax.axis_size("wide") == 8:
-        return xor_gather(x)
-    return lax.all_gather(x, "wide", axis=0, tiled=True)
+    r = lax.rsqrt(head_sum(x * x, head_ones(x.shape[1])) * (1.0 / HD) + EPS)
+    k_ref[...] = (x * r * row(hg_ref, 2)).astype(bf16)
+    o_ref[...] = v_ref[...].astype(bf16)
+
+
+def swap(x, axis, size, m):
+    return lax.ppermute(x, axis, [(i, i ^ m) for i in range(size)])
+
+
+def pick_kernel(count, n_pieces, sc, *refs):
+    a, b = refs[:n_pieces], refs[n_pieces : 2 * n_pieces]
+    outs, sem = refs[2 * n_pieces : 2 * n_pieces + 2], refs[-1]
+    rows = a[0].shape[0]
+    for k, (pieces, out) in enumerate(zip((a, b), outs)):
+        for j in range(count):
+            for m in range(n_pieces):
+
+                @pl.when(sc[1 + j] == m)
+                def _():
+                    pltpu.make_async_copy(pieces[m], out.at[pl.ds(j * rows, rows)], sem.at[k, j]).start()
+
+    for k, (pieces, out) in enumerate(zip((a, b), outs)):
+        for j in range(count):
+            pltpu.make_async_copy(pieces[0], out.at[pl.ds(j * rows, rows)], sem.at[k, j]).wait()
+
+
+def gather_item(a, b, sc, count):
+    size = lax.axis_size("wide")
+    if size != 8:
+        full = [lax.all_gather(x, "wide") for x in (a, b)]
+        return [
+            jnp.concatenate([lax.dynamic_index_in_dim(x, sc[1 + SPAN + j], 0, False) for j in range(count)]) for x in full
+        ]
+    go = lambda x, m: swap(x, "wide", 8, m)
+    a2, b4 = go(a, 2), go(b, 4)
+    a4, b2 = go(a, 4), go(b, 2)
+    a6, b6 = go(a2, 4), go(b4, 2)
+    pieces = []
+    for four in ((a, a2, a4, a6), (b, b2, b4, b6)):
+        for x in four:
+            pieces += [x, go(x, 1)]
+    out = [sds((count * x.shape[0], x.shape[1]), x.dtype) for x in (a, b)]
+    return pl.pallas_call(
+        functools.partial(pick_kernel, count, 8),
+        grid_spec=pltpu.PrefetchScalarGridSpec(
+            num_scalar_prefetch=1,
+            grid=(1,),
+            in_specs=loose(16),
+            out_specs=loose(2),
+            scratch_shapes=[pltpu.SemaphoreType.DMA((2, count))],
+        ),
+        out_shape=out,
+        compiler_params=params(1),
+        name="pick",
+    )(sc, *pieces)
 
 
 def gather_small(x, axis):
-    size = x.shape[0]
-    wide = -(-size // 1024) * 1024
-    padded = jnp.pad(x, (0, wide - size)).reshape(1, 8, wide // 8)
-    return lax.all_gather(padded, axis, axis=0, tiled=True).reshape(-1, wide)[:, :size]
+    n = x.shape[0]
+    wide = -(-n // 1024) * 1024
+    x = jnp.pad(x, (0, wide - n)).reshape(wide // 128, 128)
+    size = lax.axis_size(axis)
+    if size > 8:
+        return lax.all_gather(x, axis).reshape(size, wide)[:, :n]
+    got = jnp.stack([x] + [swap(x, axis, size, m) for m in range(1, size)])
+    order = jnp.arange(size, dtype=jnp.int32)
+    mine = (order[:, None] ^ lax.axis_index(axis)) == order[None, :]
+    out = jnp.sum(jnp.where(mine[:, :, None, None], got[None], 0.0), 1)
+    return out.reshape(size, wide)[:, :n]
+
+
+def hop_kernel(have, sc, *refs):
+    ins = dict(zip(have["in"], refs))
+    outs = dict(zip(have["out"], refs[len(have["in"]) :]))
+    end = sc[0] == 1
+    if "total" in outs:
+        outs["total"][...] = jnp.where(end, ins["r1"][...], ins["send"][...])
+    third = None
+    if "second" in ins:
+        third = ins["second"][...] + ins["r2"][...]
+    if "second" in outs:
+        outs["second"][...] = ins["x"][...] + ins["r1"][...]
+    if "send" in outs:
+        new = ins["new"][...] if "new" in ins else third
+        outs["send"][...] = new if third is None else jnp.where(end, new, third)
 
 
 class Line:
     def __init__(self, place):
-        self.end = (place == 0) | (place == 3)
-        self.second = self.third = None
-
-    def step(self, x):
-        send = functools.partial(lax.ppermute, axis_name="narrow")
-        inwards, out = [(0, 1), (3, 2)], [(1, 0), (2, 3)]
-        second, third = self.second, self.third
-        got_in = got_out = None
-        if x is not None and third is not None and x.shape == third.shape:
-            got_in = got_out = send(jnp.where(self.end, x, third), perm=inwards + out)
-        else:
-            if x is not None:
-                got_in = send(x, perm=inwards)
-            if third is not None:
-                got_out = send(third, perm=out)
-        total = None if third is None else jnp.where(self.end, got_out, third)
-        self.third = None if second is None else second + send(second, perm=[(1, 2), (2, 1)])
-        self.second = None if x is None else x + got_in
-        return total
+        self.end = ((place == 0) | (place == 3)).astype(jnp.int32).reshape(1)
+        self.x = self.second = self.send = None
+        self.third = False
+
+    def step(self, new):
+        if self.send is None:
+            self.x = self.send = new
+            return None
+        go = lambda x, perm: lax.ppermute(x, "narrow", perm)
+        ins = {"r1": go(self.send, [(0, 1), (3, 2), (1, 0), (2, 3)])}
+        outs = []
+        if self.third:
+            ins["send"] = self.send
+            outs.append("total")
+        if self.second is not None:
+            ins["r2"] = go(self.second, [(1, 2), (2, 1)])
+            ins["second"] = self.second
+        if self.x is not None:
+            ins["x"] = self.x
+            outs.append("second")
+        if new is not None:
+            ins["new"] = new
+        if new is not None or self.second is not None:
+            outs.append("send")
+        like = ins["r1"]
+        block = pl.BlockSpec((BR // 2, like.shape[1]), lambda i, s: (i, 0))
+        got = pl.pallas_call(
+            functools.partial(hop_kernel, {"in": list(ins), "out": outs}),
+            grid_spec=pltpu.PrefetchScalarGridSpec(
+                num_scalar_prefetch=1, grid=(2,), in_specs=[block] * len(ins), out_specs=[block] * len(outs)
+            ),
+            out_shape=[sds(like.shape, like.dtype)] * len(outs),
+            compiler_params=params(1),
+            name="hop",
+        )(self.end, *ins.values())
+        got = dict(zip(outs, got))
+        self.third = self.second is not None
+        self.x, self.second, self.send = new, got.get("second"), got.get("send")
+        return got.get("total")
 
 
 class Sums:
@@ -675,13 +800,15 @@
         if self.line is None:
             self.done[name] = lax.psum(x, "narrow")
             return
+        if self.line.send is None:
+            self.names = [None]
         self._step(name, x)
 
     def _step(self, name, x):
         total = self.line.step(x)
         self.names.append(name)
         if total is not None:
-            self.done[self.names[-3]] = total
+            self.done[self.names[-4]] = total
 
     def get(self, name):
         while name not in self.done:
@@ -753,7 +880,7 @@
     tabs = rope_tables(position, width)
     steps = first + jnp.minimum(jnp.arange(SPAN, dtype=jnp.int32), length - 1)
     places = steps ^ me if count == 8 else steps
-    sc = jnp.concatenate([jnp.stack([length, first]), places, steps]).astype(jnp.int32)
+    sc = jnp.concatenate([length.reshape(1), places, steps]).astype(jnp.int32)
 
     cond = conditioning.astype(f32)[0]
     silu_low = jax.nn.silu(cond).astype(bf16)
@@ -777,22 +904,23 @@
     cap_raw = jnp.einsum("kd,jde->jke", captions, w_caption, preferred_element_type=f32)
     cap_own = pl.pallas_call(
         caption_norm_kernel,
-        out_shape=sds((text, 2 * n), bf16),
+        out_shape=[sds((text, n), bf16)] * 2,
         compiler_params=params(0),
         name="caption_norm",
     )(cap_raw[0], cap_raw[1], hg)
-    cap = lax.all_gather(cap_own, "wide", axis=0, tiled=True)
+    ck, cv = gather_item(*cap_own, sc, 1)
 
     chunks = range(t // BR)
+    pairs_of = range(t // (2 * BR))
     sums = Sums(deep, mz)
     a1, q_raw, k_raw, q, k, v = qkv_call(patches, vec, w_qkv, tabs, hg)
-    k_all = gather_wide(k)
-    v_all = gather_wide(v)
+    k_all, v_all = gather_item(k, v, sc, SPAN)
     q_all = lax.all_gather(q, "wide", axis=0, tiled=True)
-    heads_out = [None for _ in chunks]
-    for c in chunks:
-        heads_out[c] = attend_call(sc, q, k_all, v_all, cap, tg, c, t)
-        sums.add(("attn", c), mm(heads_out[c][0], w_out).astype(bf16))
+    heads_out = {}
+    for h in pairs_of:
+        heads_out[h] = attend_call(sc, q, k_all, v_all, ck, cv, tg, h)
+        for c in (0, 1):
+            sums.add(("attn", 2 * h + c), mm(heads_out[h][0][c * BR : (c + 1) * BR], w_out).astype(bf16))
 
     mids, gus = {}, {}
     whole_out = ()
@@ -809,56 +937,63 @@
         sums.add(("da3", c), da3_part)
         c4 = c4 + part_sum
     output, d_ffn, d_gu = whole_out
-    g_down = scatter_rows(mm_tn(d_ffn, hidden))
-    g_gu = scatter_rows(mm_tn(a3, d_gu))
-
-    d_mids, dqs = {}, {}
-    whole_out, dkv = (), ()
+    mlp_part = pair_grad_call(a3, d_gu, d_ffn, hidden)
+    g_mlp = scatter_rows(mlp_part)
+
+    d_mids, dqs, d_item, d_mixed, d_scaled = {}, {}, {}, {}, {}
+    whole_out = ()
     c2 = c3 = dck = dcv = gate_sum = 0.0
-    for c in chunks:
-        mixed, o_self, linv = heads_out[c]
-        d_mids[c], d_mixed, d_scaled, p3, p2, *whole_out = out_back_call(
-            c, sums.get(("da3", c)), mids[c], sums.get(("attn", c)), cotangent, vec, w_out, o_self, linv, whole_out
-        )
-        c2, c3 = c2 + p2, c3 + p3
-        d_all = gather_wide(d_scaled)
-        dq_cap, pk, pv, pg = caption_back_call(sc, q, d_mixed, cap, tg, c, text)
+    for h in pairs_of:
+        mixed, o_self, linv = heads_out[h]
+        for c in (2 * h, 2 * h + 1):
+            d_mids[c], d_mixed[c], d_scaled[c], p3, p2, *whole_out = out_back_call(
+                c, sums.get(("da3", c)), mids[c], sums.get(("attn", c)), cotangent, vec, w_out, o_self, linv, whole_out
+            )
+            c2, c3 = c2 + p2, c3 + p3
+        two = (d_scaled[2 * h], d_scaled[2 * h + 1])
+        d_item[h] = gather_item(*two, sc, SPAN)
+        dq_cap, pk, pv, pg = caption_back_call(q, d_mixed[2 * h], d_mixed[2 * h + 1], ck, cv, tg, h)
         dck, dcv, gate_sum = dck + pk, dcv + pv, gate_sum + pg
-        dqs[c] = dq_call(sc, q, d_scaled, k_all, v_all, dq_cap, c, t)
-        dkv = dkv_call(sc, k, v, q_all, d_all, dkv, c)
+        dqs[h] = dq_call(sc, q, *two, k_all, v_all, dq_cap, h, (mlp_part,) if h == 0 else ())
     (d_attn,) = whole_out
-    mixed = jnp.concatenate([heads_out[c][0] for c in chunks])
-    g_out = scatter_rows(mm_tn(d_attn, mixed))
-    whole_out = ()
-    c1 = hs_qk = 0.0
-    for c in chunks:
-        da1_part, p_hs, p1, *whole_out = dqkv_call(c, dqs[c], *dkv, q_raw, k_raw, tabs, hg, w_qkv, patches, whole_out)
-        sums.add(("da1", c), da1_part)
-        hs_qk, c1 = hs_qk + p_hs, c1 + p1
-    (d_qkv,) = whole_out
-    g_qkv = scatter_rows(mm_tn(a1, d_qkv))
-
-    cap_got = gather_wide(jnp.concatenate([dck, dcv], 1).astype(bf16)).reshape(count, text, 2 * n)
-    from_block = blocks ^ me if count == 8 else blocks
-    in_slot = jnp.sum(jnp.where(from_block[:, None] == blocks[None, :], (firsts == me)[None, :], False), 1) > 0
-    cap_total = jnp.sum(jnp.where(in_slot[:, None, None], cap_got.astype(f32), 0.0), 0)
+
+    kept = (jnp.arange(SPAN) < length) & (first == me)
+    in_slot = lambda x: jnp.sum(jnp.where(kept[:, None, None], x.reshape(SPAN, text, n).astype(f32), 0.0), 0)
+    got_k, got_v = gather_item(dck.astype(bf16), dcv.astype(bf16), sc, SPAN)
     d_cap, hs_c = pl.pallas_call(
         caption_grad_kernel,
         out_shape=[sds((text, 2 * n), bf16), sds((1, n), f32)],
         compiler_params=params(0),
         name="caption_grad",
-    )(cap_total[:, :n], cap_total[:, n:], cap_raw[0], hg)
-    g_cap = scatter_rows(mm_tn(captions, d_cap))
+    )(in_slot(got_k), in_slot(got_v), cap_raw[0], hg)
+    cap_part = mm_tn(captions, d_cap).astype(bf16)
+    g_cap = scatter_rows(cap_part)
     d_text = (mm_nt(d_cap[:, :n], w_caption[0]) + mm_nt(d_cap[:, n:], w_caption[1])).astype(bf16)
-    pieces = 4
-    cut = d_text.shape[1] // pieces
-    for k in range(pieces):
-        sums.add(("text", k), d_text[:, k * cut : (k + 1) * cut])
+    pieces = -(-d_text.shape[1] // d)
+    padded = jnp.pad(d_text, ((0, 0), (0, pieces * d - d_text.shape[1])))
+    for k_ in range(pieces):
+        sums.add(("text", k_), padded[:, k_ * d : (k_ + 1) * d])
+
+    last_half = len(pairs_of) - 1
+    before = ()
+    for h in pairs_of[:-1]:
+        before = dkv_call(sc, k, v, q_all, *d_item[h], h, t, 0, before, ())
+    whole_out = ()
+    c1 = hs_qk = 0.0
+    for h in pairs_of:
+        dkv = dkv_call(sc, k, v, q_all, *d_item[last_half], last_half, 2 * BR, h, before, (d_text,))
+        for c in (2 * h, 2 * h + 1):
+            da1_part, p_hs, p1, *whole_out = dqkv_call(c, dqs[h], *dkv, q_raw, k_raw, tabs, hg, w_qkv, patches, whole_out)
+            sums.add(("da1", c), da1_part)
+            hs_qk, c1 = hs_qk + p_hs, c1 + p1
+    (d_qkv,) = whole_out
+    mixed = jnp.concatenate([heads_out[h][0] for h in pairs_of])
+    g_attn = scatter_rows(pair_grad_call(a1, d_qkv, d_attn, mixed))
     whole_out = ()
     for c in chunks:
         whole_out = last_call(c, sums.get(("da1", c)), patches, d_mids[c], vec, whole_out)
     (grad_patches,) = whole_out
-    grad_captions = jnp.concatenate([sums.get(("text", k)) for k in range(pieces)], 1)
+    grad_captions = jnp.concatenate([sums.get(("text", k_)) for k_ in range(pieces)], 1)[:, : d_text.shape[1]]
 
     head_part = jnp.concatenate([hs_qk, hs_c]).reshape(3, heads, HD).sum(1)
     gate_part = gate_sum[0, ::HD] * (1.0 - tg_heads * tg_heads)
@@ -898,13 +1033,13 @@
         grad_captions,
         grad_ada,
         grad_norm_gains,
-        g_qkv.astype(f32).reshape(rows, 3, n).transpose(1, 0, 2),
+        g_attn[:, : 3 * n].astype(f32).reshape(rows, 3, n).transpose(1, 0, 2),
         grad_head_gains,
         grad_cross_gate,
         g_cap.astype(f32).reshape(-1, 2, n).transpose(1, 0, 2),
-        g_out.astype(f32).T,
-        g_gu.astype(f32).reshape(rows, 2, ff).transpose(1, 0, 2),
-        g_down.astype(f32).T,
+        g_attn[:, 3 * n :].astype(f32).T,
+        g_mlp[:, : 2 * ff].astype(f32).reshape(rows, 2, ff).transpose(1, 0, 2),
+        g_mlp[:, 2 * ff :].astype(f32).T,
     )
 
 

time: 1160 us -> 1410 us (1.22)
  Pallas kernels: 401 us -> 803 us
  blocking collectives: 66.9 us -> 0 us
  other arithmetic: 101 us -> 36 us
  waiting for transfers between devices: 231 us -> 296 us
  local copies, waits for them, and re-layouts: 100 us -> 44.3 us
  matrix products: 51.2 us -> 25.6 us
    pallas_call x5 -> x33, Pallas kernels: 22.4 us -> 502 us  [the longest x5 386 us: gather_item(): pl.pallas_call(functools.partial(pick_kernel, count, 8), grid_spec=pltpu....]
    all_gather x5 -> x0, blocking collectives: 66.9 us -> none  [gather_small(): lax.all_gather(padded, axis, axis=0, tiled=True).reshape(-1, wide)[:, :size]]
    ppermute x102 -> x135, waiting for transfers between devices: 231 us -> 295 us  [the longest x42 175 us: step(): go = lambda x, perm: lax.ppermute(x, 'narrow', perm)]
    pallas_call x4 -> x2, Pallas kernels: 72.3 us -> 38.1 us  [attend_call(): pl.pallas_call(attend_kernel, grid_spec=pltpu.PrefetchScalarGridSpec(num_...]
    unnamed x232 -> x293, local copies, waits for them, and re-layouts: 63.3 us -> 30.8 us
    dot_general x5 -> x1, matrix products: 34.7 us -> 4.5 us  [mm_tn(): return lax.dot_general(a, b, TN, preferred_element_type=f32)]
    select_n x25 -> x0, other arithmetic: 29.8 us -> none  [the longest x11 15.9 us: step(): total = None if third is None else jnp.where(self.end, got_out, third)]
    pallas_call x4 -> x2, Pallas kernels: 76.4 us -> 47.1 us  [dq_call(): pl.pallas_call(dq_kernel, grid_spec=pltpu.PrefetchScalarGridSpec(num_scal...]
  transfers between devices with their start and end apart: 109 -> 139, of which waited for: 34 -> 46; matrix products, arithmetic and copies ran while one was open for 20% -> 5% of each run, Pallas kernels for 32% -> 32%
where the time goes in v3:
time: 1410 us
  Pallas kernels  803 us (57%)
  waiting for transfers between devices  296 us (21%)
  starting transfers between devices  187 us (13%)
  local copies, waits for them, and re-layouts  44.3 us (3%)
  other arithmetic  36 us (3%)
  matrix products  25.6 us (2%)
  between operations  21.7 us (2%)
    pallas_call x5, Pallas kernels, gather_item(): pl.pallas_call(functools.partial(pick_kernel, count, 8), grid_spec=pltpu....  386 us
    ppermute x42, waiting for transfers between devices, step(): go = lambda x, perm: lax.ppermute(x, 'narrow', perm)  175 us
    pallas_call x20, Pallas kernels, chunk_call(): pl.pallas_call(body, grid=(1,), in_specs=specs + [pl.BlockSpec(memory_spa...  136 us
    ppermute x93, waiting for transfers between devices, swap(): return lax.ppermute(x, axis, [(i, i ^ m) for i in range(size)])  121 us
    ppermute x93, starting transfers between devices, swap(): return lax.ppermute(x, axis, [(i, i ^ m) for i in range(size)])  110 us
    ppermute x42, starting transfers between devices, step(): go = lambda x, perm: lax.ppermute(x, 'narrow', perm)  76.4 us
    pallas_call x23, Pallas kernels, step(): pl.pallas_call(functools.partial(hop_kernel, {'in': list(ins), 'out': out...  75.8 us
    pallas_call x3, Pallas kernels, dkv_call(): pl.pallas_call(functools.partial(dkv_kernel, not before), grid_spec=pltpu...  65 us
  transfers between devices with their start and end apart: 139, of which 46 were waited for; matrix products, arithmetic and copies ran while one was open for 5% of the time, Pallas kernels for 32%

profile of v3, /device:TPU:0, one launch (start us, length us, event | category | flops | bytes accessed | tf_op | source)
XLA Modules:
  0.0 1413.7 jit_solution(11801421055011491510)
XLA Ops:
  72.5 12.7 qkv.1
  94.1 11.8 collective-permute-done.11.refs_2_
  108.0 16.1 %collective-permute-done.13.refs_4_ = bf16[1024,384]{1,0:T(8,128)(2,1)} collective-permute-done((bf16[1024,384]{1,0:T(8,128)(2,1)}, bf16[1024,384]{1,0:T(8,128)(2,1)}, u32[]{:S(2)}, u32[]{:S(2)}) %collective-permute-start.13) | collective-permute-done | bytes 786464 | tf_op jit(solution)/shard_map/ppermute | solution.py:670
  125.6 14.3 %collective-permute-done.15.refs_6_ = bf16[1024,384]{1,0:T(8,128)(2,1)} collective-permute-done((bf16[1024,384]{1,0:T(8,128)(2,1)S(1)}, bf16[1024,384]{1,0:T(8,128)(2,1)}, u32[]{:S(2)}, u32[]{:S(2)}) %collective-permute-start.15) | collective-permute-done | bytes 786464 | tf_op jit(solution)/shard_map/ppermute | solution.py:670
  147.3 13.7 pick.6
  161.0 192.4 %pick.5 = (bf16[4096,384]{1,0:T(8,128)(2,1)}, bf16[4096,384]{1,0:T(8,128)(2,1)}) custom-call(s32[9]{0:T(128)} %pad_add_fusion.sc, bf16[1024,384]{1,0:T(8,128)(2,1)} %get-tuple-element.191.refs_0_.k_ref, bf16[1024,384]{1,0:T(8,128)(2,1)} %copy-done.15, bf16[1024,384]{1,0:T(8,128)(2,1)} %copy-done.14, bf16[1024,384]{1,0:T(8,128)(2,1)} %copy-done.18, ...), custom_call_target="tpu_custom_call" | custom-call | tf_op jit(solution)/shard_map/pick/pallas_call | solution.py:706
  353.5 19.3 %attend.2 = (bf16[512,384]{1,0:T(8,128)(2,1)}, bf16[512,384]{1,0:T(8,128)(2,1)}, f32[512,384]{1,0:T(8,128)}) custom-call(s32[9]{0:T(128)} %pad_add_fusion.sc, bf16[1024,384]{1,0:T(8,128)(2,1)} %get-tuple-element.190.q_ref, bf16[4096,384]{1,0:T(8,128)(2,1)} %get-tuple-element.193.k_ref, bf16[4096,384]{1,0:T(8,128)(2,1)} %get-tuple-element.194.v_ref, ...), custom_call_target="tpu_custom_call" | custom-call | tf_op jit(solution)/shard_map/attend/pallas_call | solution.py:196
  378.3 16.7 %collective-permute-done.38.refs_0_ = bf16[256,1536]{1,0:T(8,128)(2,1)} collective-permute-done((bf16[256,1536]{1,0:T(8,128)(2,1)}, bf16[256,1536]{1,0:T(8,128)(2,1)}, u32[]{:S(2)}, u32[]{:S(2)}) %collective-permute-start.38) | collective-permute-done | bytes 786464 | tf_op jit(solution)/shard_map/ppermute | solution.py:761
  399.8 18.8 %attend.3 = (bf16[512,384]{1,0:T(8,128)(2,1)}, bf16[512,384]{1,0:T(8,128)(2,1)}, f32[512,384]{1,0:T(8,128)}) custom-call(s32[9]{0:T(128)} %pad_add_fusion.sc, bf16[1024,384]{1,0:T(8,128)(2,1)} %get-tuple-element.190.q_ref, bf16[4096,384]{1,0:T(8,128)(2,1)} %get-tuple-element.193.k_ref, bf16[4096,384]{1,0:T(8,128)(2,1)} %get-tuple-element.194.v_ref, ...), custom_call_target="tpu_custom_call" | custom-call | tf_op jit(solution)/shard_map/attend/pallas_call | solution.py:196
  430.7 14.4 %collective-permute-done.41.refs_0_ = bf16[256,1536]{1,0:T(8,128)(2,1)S(1)} collective-permute-done((bf16[256,1536]{1,0:T(8,128)(2,1)}, bf16[256,1536]{1,0:T(8,128)(2,1)S(1)}, u32[]{:S(2)}, u32[]{:S(2)}) %collective-permute-start.41) | collective-permute-done | bytes 786464 | tf_op jit(solution)/shard_map/ppermute | solution.py:761
  453.7 8.5 ffn.4
  462.2 6.5 collective-permute-done.43.refs_0_
  477.6 8.5 ffn.5
  500.3 8.5 ffn.6
  522.2 8.5 ffn.7
  543.3 9.6 ffn_back.4
  563.1 9.6 ffn_back.5
  582.3 9.6 ffn_back.6
  600.8 9.6 ffn_back.7
  619.3 10.2 collective-permute-done.59.refs_0_
  639.1 11.3 collective-permute-done.61.refs_0_
  663.1 34.0 %collective-permute-start.98 = (bf16[256,512]{1,0:T(8,128)(2,1)}, bf16[256,512]{1,0:T(8,128)(2,1)S(1)}, u32[]{:S(2)}, u32[]{:S(2)}) collective-permute-start(bf16[256,512]{1,0:T(8,128)(2,1)} %get-tuple-element.291.da_ref.xa_ref.refs_0_), channel_id=1, source_target_pairs={{0,8},{4,12},{8,0},{12,4},{16,24},{20,28},{24,16},{28,20},{1,9},{5... | collective-permute-start | bytes 786440 | tf_op jit(solution)/shard_map/ppermute | solution.py:670
  701.7 5.8 out_back.5
  725.0 5.8 out_back.6
  733.0 5.8 out_back.7
  738.9 5.8 caption_back.3
  772.4 15.4 %pair_grad.2.rest_0_ = bf16[1536,3072]{1,0:T(8,128)(2,1)} custom-call(bf16[1024,1536]{1,0:T(8,128)(2,1)} %get-tuple-element.294.a_ref, bf16[1024,2048]{1,0:T(8,128)(2,1)} %get-tuple-element.295.b_ref, bf16[1024,1536]{1,0:T(8,128)(2,1)} %get-tuple-element.296.c_ref, bf16[1024,1024]{1,0:T(8,128)(2,1)} %get-tuple-element.297.d_ref), custom_call_target="tpu_custom_call" | custom-call | tf_op jit(solution)/shard_map/pair_grad/pallas_call | solution.py:454
  787.9 23.4 %dq.2.dq_ref.refs_0_ = f32[512,384]{1,0:T(8,128)} custom-call(s32[9]{0:T(128)} %pad_add_fusion.sc, bf16[1024,384]{1,0:T(8,128)(2,1)} %get-tuple-element.190.q_ref, bf16[256,512]{1,0:T(8,128)(2,1)} %get-tuple-element.291.da_ref.xa_ref.refs_0_, bf16[256,512]{1,0:T(8,128)(2,1)} %get-tuple-element.291.da_ref.xa_ref.refs_0_, ...), custom_call_target="tpu_custom_call" | custom-call | tf_op jit(solution)/shard_map/dq/pallas_call | solution.py:318
  811.3 65.4 %pick.9 = (bf16[1024,512]{1,0:T(8,128)(2,1)}, bf16[1024,512]{1,0:T(8,128)(2,1)}) custom-call(s32[9]{0:T(128)} %pad_add_fusion.sc, bf16[256,512]{1,0:T(8,128)(2,1)} %get-tuple-element.291.da_ref.xa_ref.refs_0_, bf16[256,512]{1,0:T(8,128)(2,1)} %copy-done.65, bf16[256,512]{1,0:T(8,128)(2,1)} %copy-done.61, bf16[256,512]{1,0:T(8,128)(2,1)} %copy-done.70, ...), custom_call_target="tpu_custom_call" | custom-call | tf_op jit(solution)/shard_map/pick/pallas_call | solution.py:706
  876.7 28.2 %dkv.3 = (f32[1024,384]{1,0:T(8,128)}, f32[1024,384]{1,0:T(8,128)}) custom-call(s32[9]{0:T(128)} %pad_add_fusion.sc, bf16[1024,384]{1,0:T(8,128)(2,1)} %get-tuple-element.191.refs_0_.k_ref, bf16[1024,384]{1,0:T(8,128)(2,1)} %get-tuple-element.192.refs_8_.v_ref, bf16[8192,384]{1,0:T(8,128)(2,1)} %all-gather.2.cloned.1.call-done.q_ref, ...), custom_call_target="tpu_custom_call" | custom-call | tf_op jit(solution)/shard_map/dkv/pallas_call | solution.py:388
  904.9 23.7 %dq.3.refs_0_ = f32[512,384]{1,0:T(8,128)} custom-call(s32[9]{0:T(128)} %pad_add_fusion.sc, bf16[1024,384]{1,0:T(8,128)(2,1)} %get-tuple-element.190.q_ref, bf16[256,512]{1,0:T(8,128)(2,1)} %get-tuple-element.298.refs_0_.da_ref.xa_ref, bf16[256,512]{1,0:T(8,128)(2,1)} %get-tuple-element.298.refs_0_.da_ref.xa_ref, ...), custom_call_target="tpu_custom_call" | custom-call | tf_op jit(solution)/shard_map/dq/pallas_call | solution.py:318
  928.6 13.3 collective-permute-start.88
  942.4 49.5 %pick.7 = (bf16[1024,384]{1,0:T(8,128)(2,1)}, bf16[1024,384]{1,0:T(8,128)(2,1)}) custom-call(s32[9]{0:T(128)} %pad_add_fusion.sc, bf16[256,384]{1,0:T(8,128)(2,1)} %copy-done.56, bf16[256,384]{1,0:T(8,128)(2,1)} %copy-done.96, bf16[256,384]{1,0:T(8,128)(2,1)} %collective-permute-done.65.refs_2_, bf16[256,384]{1,0:T(8,128)(2,1)} %collective-permute-done.66.refs_3_, ...), custom_call_target="tpu_custom_call" | custom-call | tf_op jit(solution)/shard_map/pick/pallas_call | solution.py:706
  1018.2 65.4 %pick.8 = (bf16[1024,512]{1,0:T(8,128)(2,1)}, bf16[1024,512]{1,0:T(8,128)(2,1)}) custom-call(s32[9]{0:T(128)} %pad_add_fusion.sc, bf16[256,512]{1,0:T(8,128)(2,1)} %get-tuple-element.298.refs_0_.da_ref.xa_ref, bf16[256,512]{1,0:T(8,128)(2,1)} %collective-permute-done.83.refs_1_, bf16[256,512]{1,0:T(8,128)(2,1)} %copy-done.59, bf16[256,512]{1,0:T(8,128)(2,1)} %copy-done.78, ...), custom_call_target="tpu_custom_call" | custom-call | tf_op jit(solution)/shard_map/pick/pallas_call | solution.py:706
  1083.5 18.2 %dkv.4 = (f32[512,384]{1,0:T(8,128)}, f32[512,384]{1,0:T(8,128)}) custom-call(s32[9]{0:T(128)} %pad_add_fusion.sc, bf16[1024,384]{1,0:T(8,128)(2,1)} %get-tuple-element.191.refs_0_.k_ref, bf16[1024,384]{1,0:T(8,128)(2,1)} %get-tuple-element.192.refs_8_.v_ref, bf16[8192,384]{1,0:T(8,128)(2,1)} %all-gather.2.cloned.1.call-done.q_ref, ...), custom_call_target="tpu_custom_call" | custom-call | tf_op jit(solution)/shard_map/dkv/pallas_call | solution.py:388
  1101.7 6.5 dqkv.4
  1108.3 6.6 dqkv.5
  1114.9 18.6 %dkv.5 = (f32[512,384]{1,0:T(8,128)}, f32[512,384]{1,0:T(8,128)}) custom-call(s32[9]{0:T(128)} %pad_add_fusion.sc, bf16[1024,384]{1,0:T(8,128)(2,1)} %get-tuple-element.191.refs_0_.k_ref, bf16[1024,384]{1,0:T(8,128)(2,1)} %get-tuple-element.192.refs_8_.v_ref, bf16[8192,384]{1,0:T(8,128)(2,1)} %all-gather.2.cloned.1.call-done.q_ref, ...), custom_call_target="tpu_custom_call" | custom-call | tf_op jit(solution)/shard_map/dkv/pallas_call | solution.py:388
  1133.5 6.6 dqkv.6
  1140.0 6.5 dqkv.7
  1146.6 11.0 pair_grad.3
  1167.1 19.1 %collective-permute-done.78.refs_0_ = bf16[256,1536]{1,0:T(8,128)(2,1)S(1)} collective-permute-done((bf16[256,1536]{1,0:T(8,128)(2,1)S(1)}, bf16[256,1536]{1,0:T(8,128)(2,1)S(1)}, u32[]{:S(2)}, u32[]{:S(2)}) %collective-permute-start.78) | collective-permute-done | bytes 786464 | tf_op jit(solution)/shard_map/ppermute | solution.py:761
  1192.8 16.2 %collective-permute-done.79.refs_0_ = bf16[256,1536]{1,0:T(8,128)(2,1)S(1)} collective-permute-done((bf16[256,1536]{1,0:T(8,128)(2,1)}, bf16[256,1536]{1,0:T(8,128)(2,1)S(1)}, u32[]{:S(2)}, u32[]{:S(2)}) %collective-permute-start.79) | collective-permute-done | bytes 786464 | tf_op jit(solution)/shard_map/ppermute | solution.py:761
  1218.0 14.3 %collective-permute-done.81.refs_0_ = bf16[256,1536]{1,0:T(8,128)(2,1)S(1)} collective-permute-done((bf16[256,1536]{1,0:T(8,128)(2,1)}, bf16[256,1536]{1,0:T(8,128)(2,1)S(1)}, u32[]{:S(2)}, u32[]{:S(2)}) %collective-permute-start.81) | collective-permute-done | bytes 786464 | tf_op jit(solution)/shard_map/ppermute | solution.py:761
  1245.8 9.8 collective-permute-done.122
  1274.3 15.6 %collective-permute-done.113.refs_0_ = bf16[256,1536]{1,0:T(8,128)(2,1)S(1)} collective-permute-done((bf16[256,1536]{1,0:T(8,128)(2,1)}, bf16[256,1536]{1,0:T(8,128)(2,1)S(1)}, u32[]{:S(2)}, u32[]{:S(2)}) %collective-permute-start.113) | collective-permute-done | bytes 786464 | tf_op jit(solution)/shard_map/ppermute | solution.py:761
  1300.4 16.2 %collective-permute-done.115.refs_0_ = bf16[256,1536]{1,0:T(8,128)(2,1)S(1)} collective-permute-done((bf16[256,1536]{1,0:T(8,128)(2,1)}, bf16[256,1536]{1,0:T(8,128)(2,1)S(1)}, u32[]{:S(2)}, u32[]{:S(2)}) %collective-permute-start.115) | collective-permute-done | bytes 786464 | tf_op jit(solution)/shard_map/ppermute | solution.py:761
  1326.0 15.5 %collective-permute-done.117.refs_0_ = bf16[256,1536]{1,0:T(8,128)(2,1)S(1)} collective-permute-done((bf16[256,1536]{1,0:T(8,128)(2,1)}, bf16[256,1536]{1,0:T(8,128)(2,1)S(1)}, u32[]{:S(2)}, u32[]{:S(2)}) %collective-permute-start.117) | collective-permute-done | bytes 786464 | tf_op jit(solution)/shard_map/ppermute | solution.py:761
  (700 shorter events, 439.1 us)
Async XLA Ops:
  7.2 869.5 %all-gather.2.cloned.1.call-start = ((), (), s32[]{:S(2)}) async-start(), calls=%async_computation.3 | async-start | bytes 7077888 | tf_op jit(solution)/shard_map/all_gather | solution.py:918
  12.5 28.0 %collective-permute-start = (f32[16,128]{1,0:T(8,128)S(1)}, f32[16,128]{1,0:T(8,128)S(1)}, u32[]{:S(2)}, u32[]{:S(2)}) collective-permute-start(f32[16,128]{1,0:T(8,128)S(1)} %get-tuple-element.440), channel_id=1, source_target_pairs={{0,1},{1,0},{2,3},{3,2},{4,5},{5,4},{6,7},{7,6},{8,9},{9,8},{10,11... | collective-permute-start | bytes 24584 | tf_op jit(solution)/shard_map/ppermute | solution.py:670
  15.6 25.5 %collective-permute-start.1 = (f32[16,128]{1,0:T(8,128)S(1)}, f32[16,128]{1,0:T(8,128)S(1)}, u32[]{:S(2)}, u32[]{:S(2)}) collective-permute-start(f32[16,128]{1,0:T(8,128)S(1)} %get-tuple-element.440), channel_id=1, source_target_pairs={{0,2},{1,3},{2,0},{3,1},{4,6},{5,7},{6,4},{7,5},{8,10},{9,11},{10,... | collective-permute-start | bytes 24584 | tf_op jit(solution)/shard_map/ppermute | solution.py:670
  18.2 23.2 %collective-permute-start.2 = (f32[16,128]{1,0:T(8,128)S(1)}, f32[16,128]{1,0:T(8,128)S(1)}, u32[]{:S(2)}, u32[]{:S(2)}) collective-permute-start(f32[16,128]{1,0:T(8,128)S(1)} %get-tuple-element.440), channel_id=1, source_target_pairs={{0,3},{1,2},{2,1},{3,0},{4,7},{5,6},{6,5},{7,4},{8,11},{9,10},{10,... | collective-permute-start | bytes 24584 | tf_op jit(solution)/shard_map/ppermute | solution.py:670
  26.7 41.8 %collective-permute-start.25 = (bf16[256,384]{1,0:T(8,128)(2,1)}, bf16[256,384]{1,0:T(8,128)(2,1)S(1)}, u32[]{:S(2)}, u32[]{:S(2)}) collective-permute-start(bf16[256,384]{1,0:T(8,128)(2,1)} %get-tuple-element.195.refs_0_), channel_id=1, source_target_pairs={{0,8},{4,12},{8,0},{12,4},{16,24},{20,28},{24,16},{28,20},{1,9},{5... | collective-permute-start | bytes 589832 | tf_op jit(solution)/shard_map/ppermute | solution.py:670
  28.5 41.9 %collective-permute-start.27 = (bf16[256,384]{1,0:T(8,128)(2,1)}, bf16[256,384]{1,0:T(8,128)(2,1)}, u32[]{:S(2)}, u32[]{:S(2)}) collective-permute-start(bf16[256,384]{1,0:T(8,128)(2,1)} %get-tuple-element.195.refs_0_), channel_id=1, source_target_pairs={{0,16},{4,20},{8,24},{12,28},{16,0},{20,4},{24,8},{28,12},{1,17},{... | collective-permute-start | bytes 589832 | tf_op jit(solution)/shard_map/ppermute | solution.py:670
  40.5 28.6 %collective-permute-start.34 = (bf16[256,384]{1,0:T(8,128)(2,1)}, bf16[256,384]{1,0:T(8,128)(2,1)}, u32[]{:S(2)}, u32[]{:S(2)}) collective-permute-start(bf16[256,384]{1,0:T(8,128)(2,1)} %get-tuple-element.196.refs_8_), channel_id=1, source_target_pairs={{0,16},{4,20},{8,24},{12,28},{16,0},{20,4},{24,8},{28,12},{1,17},{... | collective-permute-start | bytes 589832 | tf_op jit(solution)/shard_map/ppermute | solution.py:670
  41.1 29.3 %collective-permute-start.32 = (bf16[256,384]{1,0:T(8,128)(2,1)}, bf16[256,384]{1,0:T(8,128)(2,1)}, u32[]{:S(2)}, u32[]{:S(2)}) collective-permute-start(bf16[256,384]{1,0:T(8,128)(2,1)} %get-tuple-element.196.refs_8_), channel_id=1, source_target_pairs={{0,8},{4,12},{8,0},{12,4},{16,24},{20,28},{24,16},{28,20},{1,9},{5... | collective-permute-start | bytes 589832 | tf_op jit(solution)/shard_map/ppermute | solution.py:670
  85.3 20.7 %collective-permute-start.11 = (bf16[1024,384]{1,0:T(8,128)(2,1)}, bf16[1024,384]{1,0:T(8,128)(2,1)S(1)}, u32[]{:S(2)}, u32[]{:S(2)}) collective-permute-start(bf16[1024,384]{1,0:T(8,128)(2,1)} %get-tuple-element.191.refs_0_.k_ref), channel_id=1, source_target_pairs={{0,8},{4,12},{8,0},{12,4},{16,24},{20,28},{24,16},{28,20},{1,9},{5... | collective-permute-start | bytes 2359304 | tf_op jit(solution)/shard_map/ppermute | solution.py:670
  86.5 20.7 %collective-permute-start.20 = (bf16[1024,384]{1,0:T(8,128)(2,1)}, bf16[1024,384]{1,0:T(8,128)(2,1)}, u32[]{:S(2)}, u32[]{:S(2)}) collective-permute-start(bf16[1024,384]{1,0:T(8,128)(2,1)} %get-tuple-element.192.refs_8_.v_ref), channel_id=1, source_target_pairs={{0,16},{4,20},{8,24},{12,28},{16,0},{20,4},{24,8},{28,12},{1,17},{... | collective-permute-start | bytes 2359304 | tf_op jit(solution)/shard_map/ppermute | solution.py:670
  87.3 36.8 %collective-permute-start.13 = (bf16[1024,384]{1,0:T(8,128)(2,1)}, bf16[1024,384]{1,0:T(8,128)(2,1)}, u32[]{:S(2)}, u32[]{:S(2)}) collective-permute-start(bf16[1024,384]{1,0:T(8,128)(2,1)} %get-tuple-element.191.refs_0_.k_ref), channel_id=1, source_target_pairs={{0,16},{4,20},{8,24},{12,28},{16,0},{20,4},{24,8},{28,12},{1,17},{... | collective-permute-start | bytes 2359304 | tf_op jit(solution)/shard_map/ppermute | solution.py:670
  88.5 36.4 %collective-permute-start.18 = (bf16[1024,384]{1,0:T(8,128)(2,1)}, bf16[1024,384]{1,0:T(8,128)(2,1)}, u32[]{:S(2)}, u32[]{:S(2)}) collective-permute-start(bf16[1024,384]{1,0:T(8,128)(2,1)} %get-tuple-element.192.refs_8_.v_ref), channel_id=1, source_target_pairs={{0,8},{4,12},{8,0},{12,4},{16,24},{20,28},{24,16},{28,20},{1,9},{5... | collective-permute-start | bytes 2359304 | tf_op jit(solution)/shard_map/ppermute | solution.py:670
  94.0 31.0 %collective-permute-start.10 = (bf16[1024,384]{1,0:T(8,128)(2,1)}, bf16[1024,384]{1,0:T(8,128)(2,1)S(1)}, u32[]{:S(2)}, u32[]{:S(2)}) collective-permute-start(bf16[1024,384]{1,0:T(8,128)(2,1)} %get-tuple-element.191.refs_0_.k_ref), channel_id=1, source_target_pairs={{0,4},{4,0},{8,12},{12,8},{16,20},{20,16},{24,28},{28,24},{1,5},{5... | collective-permute-start | bytes 2359304 | tf_op jit(solution)/shard_map/ppermute | solution.py:670
  107.3 32.6 %collective-permute-start.15 = (bf16[1024,384]{1,0:T(8,128)(2,1)S(1)}, bf16[1024,384]{1,0:T(8,128)(2,1)}, u32[]{:S(2)}, u32[]{:S(2)}) collective-permute-start(bf16[1024,384]{1,0:T(8,128)(2,1)S(1)} %collective-permute-done.11.refs_2_), channel_id=1, source_target_pairs={{0,16},{4,20},{8,24},{12,28},{16,0},{20,4},{24,8},{28,12},{1,17},{... | collective-permute-start | bytes 2359304 | tf_op jit(solution)/shard_map/ppermute | solution.py:670
  125.0 36.0 %collective-permute-start.21 = (bf16[1024,384]{1,0:T(8,128)(2,1)}, bf16[1024,384]{1,0:T(8,128)(2,1)}, u32[]{:S(2)}, u32[]{:S(2)}) collective-permute-start(bf16[1024,384]{1,0:T(8,128)(2,1)} %collective-permute-done.20.refs_12_), channel_id=1, source_target_pairs={{0,4},{4,0},{8,12},{12,8},{16,20},{20,16},{24,28},{28,24},{1,5},{5... | collective-permute-start | bytes 2359304 | tf_op jit(solution)/shard_map/ppermute | solution.py:670
  125.5 35.5 %collective-permute-start.14 = (bf16[1024,384]{1,0:T(8,128)(2,1)}, bf16[1024,384]{1,0:T(8,128)(2,1)}, u32[]{:S(2)}, u32[]{:S(2)}) collective-permute-start(bf16[1024,384]{1,0:T(8,128)(2,1)} %collective-permute-done.13.refs_4_), channel_id=1, source_target_pairs={{0,4},{4,0},{8,12},{12,8},{16,20},{20,16},{24,28},{28,24},{1,5},{5... | collective-permute-start | bytes 2359304 | tf_op jit(solution)/shard_map/ppermute | solution.py:670
  139.9 21.1 %collective-permute-start.19 = (bf16[1024,384]{1,0:T(8,128)(2,1)}, bf16[1024,384]{1,0:T(8,128)(2,1)}, u32[]{:S(2)}, u32[]{:S(2)}) collective-permute-start(bf16[1024,384]{1,0:T(8,128)(2,1)} %collective-permute-done.18.refs_10_), channel_id=1, source_target_pairs={{0,4},{4,0},{8,12},{12,8},{16,20},{20,16},{24,28},{28,24},{1,5},{5... | collective-permute-start | bytes 2359304 | tf_op jit(solution)/shard_map/ppermute | solution.py:670
  397.5 23.5 %collective-permute-start.39 = (bf16[256,1536]{1,0:T(8,128)(2,1)}, bf16[256,1536]{1,0:T(8,128)(2,1)}, u32[]{:S(2)}, u32[]{:S(2)}) collective-permute-start(bf16[256,1536]{1,0:T(8,128)(2,1)} %get-tuple-element.200), channel_id=1, source_target_pairs={{0,1},{3,2},{1,0},{2,3},{4,5},{7,6},{5,4},{6,7},{8,9},{11,10},{9,8... | collective-permute-start | bytes 2359304 | tf_op jit(solution)/shard_map/ppermute | solution.py:761
  398.2 22.8 %collective-permute-start.40 = (bf16[256,1536]{1,0:T(8,128)(2,1)}, bf16[256,1536]{1,0:T(8,128)(2,1)}, u32[]{:S(2)}, u32[]{:S(2)}) collective-permute-start(bf16[256,1536]{1,0:T(8,128)(2,1)} %get-tuple-element.201.refs_2_), channel_id=1, source_target_pairs={{1,2},{2,1},{5,6},{6,5},{9,10},{10,9},{13,14},{14,13},{17,18},{18,... | collective-permute-start | bytes 2359304 | tf_op jit(solution)/shard_map/ppermute | solution.py:761
  399.8 994.0 %reduce-scatter.4.cloned.1.call-start = ((), (), s32[]{:S(2)}) async-start(), calls=%async_computation.4 | async-start | bytes 5308416 | tf_op jit(solution)/shard_map/reduce_scatter | solution.py:820
  424.1 20.9 %collective-permute-start.41 = (bf16[256,1536]{1,0:T(8,128)(2,1)}, bf16[256,1536]{1,0:T(8,128)(2,1)S(1)}, u32[]{:S(2)}, u32[]{:S(2)}) collective-permute-start(bf16[256,1536]{1,0:T(8,128)(2,1)} %get-tuple-element.203.refs_1_), channel_id=1, source_target_pairs={{0,1},{3,2},{1,0},{2,3},{4,5},{7,6},{5,4},{6,7},{8,9},{11,10},{9,8... | collective-permute-start | bytes 2359304 | tf_op jit(solution)/shard_map/ppermute | solution.py:761
  655.0 63.9 %collective-permute-start.63 = (bf16[256,1536]{1,0:T(8,128)(2,1)}, bf16[256,1536]{1,0:T(8,128)(2,1)S(1)}, u32[]{:S(2)}, u32[]{:S(2)}) collective-permute-start(bf16[256,1536]{1,0:T(8,128)(2,1)} %get-tuple-element.278.refs_1_), channel_id=1, source_target_pairs={{0,1},{3,2},{1,0},{2,3},{4,5},{7,6},{5,4},{6,7},{8,9},{11,10},{9,8... | collective-permute-start | bytes 2359304 | tf_op jit(solution)/shard_map/ppermute | solution.py:761
  663.1 38.6 %collective-permute-start.98 = (bf16[256,512]{1,0:T(8,128)(2,1)}, bf16[256,512]{1,0:T(8,128)(2,1)S(1)}, u32[]{:S(2)}, u32[]{:S(2)}) collective-permute-start(bf16[256,512]{1,0:T(8,128)(2,1)} %get-tuple-element.291.da_ref.xa_ref.refs_0_), channel_id=1, source_target_pairs={{0,8},{4,12},{8,0},{12,4},{16,24},{20,28},{24,16},{28,20},{1,9},{5... | collective-permute-start | bytes 786440 | tf_op jit(solution)/shard_map/ppermute | solution.py:670
  711.5 33.2 %collective-permute-start.99 = (bf16[256,512]{1,0:T(8,128)(2,1)S(1)}, bf16[256,512]{1,0:T(8,128)(2,1)S(1)}, u32[]{:S(2)}, u32[]{:S(2)}) collective-permute-start(bf16[256,512]{1,0:T(8,128)(2,1)S(1)} %collective-permute-done.98.refs_2_), channel_id=1, source_target_pairs={{0,4},{4,0},{8,12},{12,8},{16,20},{20,16},{24,28},{28,24},{1,5},{5... | collective-permute-start | bytes 786440 | tf_op jit(solution)/shard_map/ppermute | solution.py:670
  714.5 30.5 %collective-permute-start.109 = (bf16[256,512]{1,0:T(8,128)(2,1)S(1)}, bf16[256,512]{1,0:T(8,128)(2,1)S(1)}, u32[]{:S(2)}, u32[]{:S(2)}) collective-permute-start(bf16[256,512]{1,0:T(8,128)(2,1)S(1)} %collective-permute-done.107.refs_12_), channel_id=1, source_target_pairs={{0,8},{4,12},{8,0},{12,4},{16,24},{20,28},{24,16},{28,20},{1,9},{5... | collective-permute-start | bytes 786440 | tf_op jit(solution)/shard_map/ppermute | solution.py:670
  716.1 29.2 %collective-permute-start.103 = (bf16[256,512]{1,0:T(8,128)(2,1)S(1)}, bf16[256,512]{1,0:T(8,128)(2,1)S(1)}, u32[]{:S(2)}, u32[]{:S(2)}) collective-permute-start(bf16[256,512]{1,0:T(8,128)(2,1)S(1)} %collective-permute-done.102.refs_6_), channel_id=1, source_target_pairs={{0,4},{4,0},{8,12},{12,8},{16,20},{20,16},{24,28},{28,24},{1,5},{5... | collective-permute-start | bytes 786440 | tf_op jit(solution)/shard_map/ppermute | solution.py:670
  718.9 29.5 %collective-permute-start.104 = (bf16[256,512]{1,0:T(8,128)(2,1)}, bf16[256,512]{1,0:T(8,128)(2,1)S(1)}, u32[]{:S(2)}, u32[]{:S(2)}) collective-permute-start(bf16[256,512]{1,0:T(8,128)(2,1)} %get-tuple-element.292.db_ref.xb_ref.refs_8_), channel_id=1, source_target_pairs={{0,4},{4,0},{8,12},{12,8},{16,20},{20,16},{24,28},{28,24},{1,5},{5... | collective-permute-start | bytes 786440 | tf_op jit(solution)/shard_map/ppermute | solution.py:670
  718.9 29.6 %collective-permute-start.106 = (bf16[256,512]{1,0:T(8,128)(2,1)S(1)}, bf16[256,512]{1,0:T(8,128)(2,1)S(1)}, u32[]{:S(2)}, u32[]{:S(2)}) collective-permute-start(bf16[256,512]{1,0:T(8,128)(2,1)S(1)} %collective-permute-done.105.refs_10_), channel_id=1, source_target_pairs={{0,4},{4,0},{8,12},{12,8},{16,20},{20,16},{24,28},{28,24},{1,5},{5... | collective-permute-start | bytes 786440 | tf_op jit(solution)/shard_map/ppermute | solution.py:670
  769.6 159.0 %collective-permute-start.68 = (bf16[256,384]{1,0:T(8,128)(2,1)}, bf16[256,384]{1,0:T(8,128)(2,1)}, u32[]{:S(2)}, u32[]{:S(2)}) collective-permute-start(bf16[256,384]{1,0:T(8,128)(2,1)} %copy-done.95), channel_id=1, source_target_pairs={{0,4},{4,0},{8,12},{12,8},{16,20},{20,16},{24,28},{28,24},{1,5},{5... | collective-permute-start | bytes 589832 | tf_op jit(solution)/shard_map/ppermute | solution.py:670
  769.6 172.3 %collective-permute-start.77 = (bf16[256,384]{1,0:T(8,128)(2,1)}, bf16[256,384]{1,0:T(8,128)(2,1)}, u32[]{:S(2)}, u32[]{:S(2)}) collective-permute-start(bf16[256,384]{1,0:T(8,128)(2,1)} %collective-permute-done.76.refs_14_), channel_id=1, source_target_pairs={{0,4},{4,0},{8,12},{12,8},{16,20},{20,16},{24,28},{28,24},{1,5},{5... | collective-permute-start | bytes 589832 | tf_op jit(solution)/shard_map/ppermute | solution.py:670
  770.1 171.8 %collective-permute-start.70 = (bf16[256,384]{1,0:T(8,128)(2,1)}, bf16[256,384]{1,0:T(8,128)(2,1)}, u32[]{:S(2)}, u32[]{:S(2)}) collective-permute-start(bf16[256,384]{1,0:T(8,128)(2,1)} %collective-permute-done.69.refs_6_), channel_id=1, source_target_pairs={{0,4},{4,0},{8,12},{12,8},{16,20},{20,16},{24,28},{28,24},{1,5},{5... | collective-permute-start | bytes 589832 | tf_op jit(solution)/shard_map/ppermute | solution.py:670
  770.9 226.5 %collective-permute-start.83 = (bf16[256,512]{1,0:T(8,128)(2,1)S(1)}, bf16[256,512]{1,0:T(8,128)(2,1)}, u32[]{:S(2)}, u32[]{:S(2)}) collective-permute-start(bf16[256,512]{1,0:T(8,128)(2,1)S(1)} %copy-done.4), channel_id=1, source_target_pairs={{0,4},{4,0},{8,12},{12,8},{16,20},{20,16},{24,28},{28,24},{1,5},{5... | collective-permute-start | bytes 786440 | tf_op jit(solution)/shard_map/ppermute | solution.py:670
  771.4 227.7 %collective-permute-start.93 = (bf16[256,512]{1,0:T(8,128)(2,1)S(1)}, bf16[256,512]{1,0:T(8,128)(2,1)}, u32[]{:S(2)}, u32[]{:S(2)}) collective-permute-start(bf16[256,512]{1,0:T(8,128)(2,1)S(1)} %copy-done.5), channel_id=1, source_target_pairs={{0,16},{4,20},{8,24},{12,28},{16,0},{20,4},{24,8},{28,12},{1,17},{... | collective-permute-start | bytes 786440 | tf_op jit(solution)/shard_map/ppermute | solution.py:670
  928.6 74.2 %collective-permute-start.88 = (bf16[256,512]{1,0:T(8,128)(2,1)S(1)}, bf16[256,512]{1,0:T(8,128)(2,1)S(1)}, u32[]{:S(2)}, u32[]{:S(2)}) collective-permute-start(bf16[256,512]{1,0:T(8,128)(2,1)S(1)} %copy-done.60), channel_id=1, source_target_pairs={{0,16},{4,20},{8,24},{12,28},{16,0},{20,4},{24,8},{28,12},{1,17},{... | collective-permute-start | bytes 786440 | tf_op jit(solution)/shard_map/ppermute | solution.py:670
  941.9 61.0 %collective-permute-start.85 = (bf16[256,512]{1,0:T(8,128)(2,1)S(1)}, bf16[256,512]{1,0:T(8,128)(2,1)S(1)}, u32[]{:S(2)}, u32[]{:S(2)}) collective-permute-start(bf16[256,512]{1,0:T(8,128)(2,1)S(1)} %copy-done.60), channel_id=1, source_target_pairs={{0,4},{4,0},{8,12},{12,8},{16,20},{20,16},{24,28},{28,24},{1,5},{5... | collective-permute-start | bytes 786440 | tf_op jit(solution)/shard_map/ppermute | solution.py:670
  941.9 61.5 %collective-permute-start.87 = (bf16[256,512]{1,0:T(8,128)(2,1)S(1)}, bf16[256,512]{1,0:T(8,128)(2,1)}, u32[]{:S(2)}, u32[]{:S(2)}) collective-permute-start(bf16[256,512]{1,0:T(8,128)(2,1)S(1)} %copy-done.64), channel_id=1, source_target_pairs={{0,4},{4,0},{8,12},{12,8},{16,20},{20,16},{24,28},{28,24},{1,5},{5... | collective-permute-start | bytes 786440 | tf_op jit(solution)/shard_map/ppermute | solution.py:670
  1157.6 242.3 %reduce-scatter.6.cloned.1.call-start = ((), (), s32[]{:S(2)}) async-start(), calls=%async_computation.5 | async-start | bytes 7077888 | tf_op jit(solution)/shard_map/reduce_scatter | solution.py:820
  1162.2 240.3 %reduce-scatter.8.cloned.1.call-start = ((), (), s32[]{:S(2)}) async-start(), calls=%async_computation.6 | async-start | bytes 10616832 | tf_op jit(solution)/shard_map/reduce_scatter | solution.py:820
  1236.8 28.2 %collective-permute-start.111 = (bf16[256,1536]{1,0:T(8,128)(2,1)}, bf16[256,1536]{1,0:T(8,128)(2,1)S(1)}, u32[]{:S(2)}, u32[]{:S(2)}) collective-permute-start(bf16[256,1536]{1,0:T(8,128)(2,1)} %get-tuple-element.311.refs_1_), channel_id=1, source_target_pairs={{0,1},{3,2},{1,0},{2,3},{4,5},{7,6},{5,4},{6,7},{8,9},{11,10},{9,8... | collective-permute-start | bytes 2359304 | tf_op jit(solution)/shard_map/ppermute | solution.py:761
  1239.6 26.1 %collective-permute-start.112 = (bf16[256,1536]{1,0:T(8,128)(2,1)}, bf16[256,1536]{1,0:T(8,128)(2,1)}, u32[]{:S(2)}, u32[]{:S(2)}) collective-permute-start(bf16[256,1536]{1,0:T(8,128)(2,1)} %get-tuple-element.312.refs_3_), channel_id=1, source_target_pairs={{1,2},{2,1},{5,6},{6,5},{9,10},{10,9},{13,14},{14,13},{17,18},{18,... | collective-permute-start | bytes 2359304 | tf_op jit(solution)/shard_map/ppermute | solution.py:761
  1269.8 20.1 %collective-permute-start.113 = (bf16[256,1536]{1,0:T(8,128)(2,1)}, bf16[256,1536]{1,0:T(8,128)(2,1)S(1)}, u32[]{:S(2)}, u32[]{:S(2)}) collective-permute-start(bf16[256,1536]{1,0:T(8,128)(2,1)} %get-tuple-element.315.refs_1_), channel_id=1, source_target_pairs={{0,1},{3,2},{1,0},{2,3},{4,5},{7,6},{5,4},{6,7},{8,9},{11,10},{9,8... | collective-permute-start | bytes 2359304 | tf_op jit(solution)/shard_map/ppermute | solution.py:761
  1270.0 20.0 %collective-permute-start.114 = (bf16[256,1536]{1,0:T(8,128)(2,1)}, bf16[256,1536]{1,0:T(8,128)(2,1)S(1)}, u32[]{:S(2)}, u32[]{:S(2)}) collective-permute-start(bf16[256,1536]{1,0:T(8,128)(2,1)} %get-tuple-element.316.refs_3_), channel_id=1, source_target_pairs={{1,2},{2,1},{5,6},{6,5},{9,10},{10,9},{13,14},{14,13},{17,18},{18,... | collective-permute-start | bytes 2359304 | tf_op jit(solution)/shard_map/ppermute | solution.py:761
  1270.7 29.4 %collective-permute-start.129 = (f32[56,128]{1,0:T(8,128)S(1)}, f32[56,128]{1,0:T(8,128)S(1)}, u32[]{:S(2)}, u32[]{:S(2)}) collective-permute-start(f32[56,128]{1,0:T(8,128)S(1)} %pad_bitcast_fusion), channel_id=1, source_target_pairs={{0,20},{4,16},{8,28},{12,24},{16,4},{20,0},{24,12},{28,8},{1,21},{... | collective-permute-start | bytes 86024 | tf_op jit(solution)/shard_map/ppermute | solution.py:670
  1271.2 28.9 %collective-permute-start.130 = (f32[56,128]{1,0:T(8,128)S(1)}, f32[56,128]{1,0:T(8,128)S(1)}, u32[]{:S(2)}, u32[]{:S(2)}) collective-permute-start(f32[56,128]{1,0:T(8,128)S(1)} %pad_bitcast_fusion), channel_id=1, source_target_pairs={{0,24},{4,28},{8,16},{12,20},{16,8},{20,12},{24,0},{28,4},{1,25},{... | collective-permute-start | bytes 86024 | tf_op jit(solution)/shard_map/ppermute | solution.py:670
  1273.8 26.3 %collective-permute-start.131 = (f32[56,128]{1,0:T(8,128)S(1)}, f32[56,128]{1,0:T(8,128)S(1)}, u32[]{:S(2)}, u32[]{:S(2)}) collective-permute-start(f32[56,128]{1,0:T(8,128)S(1)} %pad_bitcast_fusion), channel_id=1, source_target_pairs={{0,28},{4,24},{8,20},{12,16},{16,12},{20,8},{24,4},{28,0},{1,29},{... | collective-permute-start | bytes 86024 | tf_op jit(solution)/shard_map/ppermute | solution.py:670
  1296.0 20.6 %collective-permute-start.115 = (bf16[256,1536]{1,0:T(8,128)(2,1)}, bf16[256,1536]{1,0:T(8,128)(2,1)S(1)}, u32[]{:S(2)}, u32[]{:S(2)}) collective-permute-start(bf16[256,1536]{1,0:T(8,128)(2,1)} %get-tuple-element.322.refs_1_), channel_id=1, source_target_pairs={{0,1},{3,2},{1,0},{2,3},{4,5},{7,6},{5,4},{6,7},{8,9},{11,10},{9,8... | collective-permute-start | bytes 2359304 | tf_op jit(solution)/shard_map/ppermute | solution.py:761
  1321.2 20.3 %collective-permute-start.117 = (bf16[256,1536]{1,0:T(8,128)(2,1)}, bf16[256,1536]{1,0:T(8,128)(2,1)S(1)}, u32[]{:S(2)}, u32[]{:S(2)}) collective-permute-start(bf16[256,1536]{1,0:T(8,128)(2,1)} %get-tuple-element.326.refs_1_), channel_id=1, source_target_pairs={{0,1},{3,2},{1,0},{2,3},{4,5},{7,6},{5,4},{6,7},{8,9},{11,10},{9,8... | collective-permute-start | bytes 2359304 | tf_op jit(solution)/shard_map/ppermute | solution.py:761
  1347.4 21.2 %collective-permute-start.119 = (bf16[256,1536]{1,0:T(8,128)(2,1)}, bf16[256,1536]{1,0:T(8,128)(2,1)}, u32[]{:S(2)}, u32[]{:S(2)}) collective-permute-start(bf16[256,1536]{1,0:T(8,128)(2,1)} %get-tuple-element.328.refs_1_), channel_id=1, source_target_pairs={{0,1},{3,2},{1,0},{2,3},{4,5},{7,6},{5,4},{6,7},{8,9},{11,10},{9,8... | collective-permute-start | bytes 2359304 | tf_op jit(solution)/shard_map/ppermute | solution.py:761
  (227 other events, 3263.5 us)
Sparse Core Ops, SparseCore 0:
  399.9 49.1 all-gather.1
  1157.7 55.8 reduce-scatter.3
  1217.3 63.5 reduce-scatter.5
  1284.2 76.4 reduce-scatter.7

commit v4 on v3

--- a/solution.py
+++ b/solution.py
@@ -29,6 +29,41 @@
     return jax.ShapeDtypeStruct(shape, dtype)
 
 
+class Order:
+    def __init__(self):
+        self.token = ()
+
+    def run(self, name, kernel, grid, ins, in_specs, out_specs, out_shape, scratch=(), scalar=None, held=(), first_held=0, after=()):
+        pre = 0 if scalar is None else 1
+        given = pre + len(ins)
+        extra = [*self.token, *after, *held]
+
+        def body(*refs):
+            kernel(*refs[:given], *refs[given + len(extra) :])
+
+        at = given + len(extra) - len(held)
+        out = pl.pallas_call(
+            body,
+            grid_spec=pltpu.PrefetchScalarGridSpec(
+                num_scalar_prefetch=pre,
+                grid=grid,
+                in_specs=list(in_specs) + loose(len(extra)),
+                out_specs=out_specs,
+                scratch_shapes=list(scratch),
+            ),
+            out_shape=out_shape,
+            input_output_aliases={at + k: first_held + k for k in range(len(held))},
+            compiler_params=params(len(grid)),
+            name=name,
+        )(*(() if scalar is None else (scalar,)), *ins, *extra)
+        self.token = (out[0],)
+        return out
+
+
+def loose(n):
+    return [pl.BlockSpec(memory_space=pl.ANY)] * n
+
+
 def mm(a, b):
     return jnp.dot(a, b, preferred_element_type=f32)
 
@@ -122,29 +157,23 @@
     vv_ref[...] = mm(a, w_ref[2]).astype(bf16)
 
 
-def qkv_call(patches, vec, w, tabs, hg, br=256):
+def qkv_call(order, patches, vec, w, tabs, hg, br=256):
     t, d = patches.shape
     n = w.shape[2]
-    return pl.pallas_call(
+    return order.run(
+        "qkv",
         qkv_kernel,
-        grid=(t // br,),
-        in_specs=[rows_of(br, d), whole(vec.shape), whole(w.shape)]
-        + [rows_of(br, 128)] * 3
-        + [whole(hg.shape)],
-        out_specs=[rows_of(br, d)] + [rows_of(br, n)] * 5,
-        out_shape=[sds((t, d), bf16), sds((t, n), f32), sds((t, n), f32)] + [sds((t, n), bf16)] * 3,
-        compiler_params=params(1),
-        name="qkv",
-    )(patches, vec, w, *tabs, hg)
+        (t // br,),
+        (patches, vec, w, *tabs, hg),
+        [rows_of(br, d), whole(vec.shape), whole(w.shape)] + [rows_of(br, 128)] * 3 + [whole(hg.shape)],
+        [rows_of(br, d)] + [rows_of(br, n)] * 5,
+        [sds((t, d), bf16), sds((t, n), f32), sds((t, n), f32)] + [sds((t, n), bf16)] * 3,
+    )
 
 
 def soft_sums(q, k, v, mask):
     e = jnp.exp2(mm_nt(q, keep(k, mask))).astype(bf16)
     return mm(e, jnp.where(mask, v, jnp.ones_like(v)))
-
-
-def loose(n):
-    return [pl.BlockSpec(memory_space=pl.ANY)] * n
 
 
 def item_block(j, s):
@@ -185,7 +214,7 @@
         li_ref[...] = li
 
 
-def attend_call(sc, q, k, v, ck, cv, tg, h):
+def attend_call(order, sc, q, k, v, ck, cv, tg, h):
     n = q.shape[1]
     pairs = n // 128
     block = k.shape[0] // SPAN
@@ -193,26 +222,24 @@
     text = ck.shape[0]
     mine = lambda p, j, s: (0, p)
     other = lambda p, j, s: (item_block(j, s), p)
-    return pl.pallas_call(
+    return order.run(
+        "attend",
         attend_kernel,
-        grid_spec=pltpu.PrefetchScalarGridSpec(
-            num_scalar_prefetch=1,
-            grid=(pairs, SPAN),
-            in_specs=[
-                pl.BlockSpec((bq, 128), lambda p, j, s: (h, p)),
-                pl.BlockSpec((block, 128), other),
-                pl.BlockSpec((block, 128), other),
-                pl.BlockSpec((text, 128), mine),
-                pl.BlockSpec((text, 128), mine),
-                pl.BlockSpec((1, 128), mine),
-            ],
-            out_specs=[pl.BlockSpec((bq, 128), mine)] * 3,
-            scratch_shapes=[pltpu.VMEM((2, bq, 128), f32)],
-        ),
-        out_shape=[sds((bq, n), bf16), sds((bq, n), bf16), sds((bq, n), f32)],
-        compiler_params=params(2),
-        name="attend",
-    )(sc, q, k, v, ck, cv, tg)
+        (pairs, SPAN),
+        (q, k, v, ck, cv, tg),
+        [
+            pl.BlockSpec((bq, 128), lambda p, j, s: (h, p)),
+            pl.BlockSpec((block, 128), other),
+            pl.BlockSpec((block, 128), other),
+            pl.BlockSpec((text, 128), mine),
+            pl.BlockSpec((text, 128), mine),
+            pl.BlockSpec((1, 128), mine),
+        ],
+        [pl.BlockSpec((bq, 128), mine)] * 3,
+        [sds((bq, n), bf16), sds((bq, n), bf16), sds((bq, n), f32)],
+        [pltpu.VMEM((2, bq, 128), f32)],
+        sc,
+    )
 
 
 def caption_back_kernel(q_ref, da_ref, db_ref, ck_ref, cv_ref, tg_ref, dq_ref, dk_ref, dv_ref, gs_ref):
@@ -240,16 +267,18 @@
     gs_ref[...] = jnp.where(masks[0], sums[0], sums[1])
 
 
-def caption_back_call(q, da, db, ck, cv, tg, h):
+def caption_back_call(order, q, da, db, ck, cv, tg, h):
     n = q.shape[1]
     pairs = n // 128
     bq = 2 * BR
     text = ck.shape[0]
     mine = lambda p: (0, p)
-    return pl.pallas_call(
+    return order.run(
+        "caption_back",
         caption_back_kernel,
-        grid=(pairs,),
-        in_specs=[
+        (pairs,),
+        (q, da, db, ck, cv, tg),
+        [
             pl.BlockSpec((bq, 128), lambda p: (h, p)),
             pl.BlockSpec((BR, 128), mine),
             pl.BlockSpec((BR, 128), mine),
@@ -257,16 +286,14 @@
             pl.BlockSpec((text, 128), mine),
             pl.BlockSpec((1, 128), mine),
         ],
-        out_specs=[
+        [
             pl.BlockSpec((bq, 128), mine),
             pl.BlockSpec((text, 128), mine),
             pl.BlockSpec((text, 128), mine),
             pl.BlockSpec((1, 128), mine),
         ],
-        out_shape=[sds((bq, n), f32), sds((text, n), f32), sds((text, n), f32), sds((1, n), f32)],
-        compiler_params=params(1),
-        name="caption_back",
-    )(q, da, db, ck, cv, tg)
+        [sds((bq, n), f32), sds((text, n), f32), sds((text, n), f32), sds((1, n), f32)],
+    )
 
 
 def minus_delta(rows, head):
@@ -274,8 +301,7 @@
     return jnp.where((lane >= 3 * head) & (lane < 3 * head + 3), -1.0, 0.0).astype(bf16)
 
 
-def dq_kernel(sc, q_ref, da_ref, xa_ref, db_ref, xb_ref, k_ref, v_ref, c_ref, *rest):
-    dq_ref, acc = rest[-2:]
+def dq_kernel(sc, q_ref, da_ref, xa_ref, db_ref, xb_ref, k_ref, v_ref, c_ref, dq_ref, acc):
     pair = pl.program_id(0)
     j = pl.program_id(1)
     masks = halves(128)
@@ -307,7 +333,7 @@
         dq_ref[...] = acc[...] * 0.125 + c_ref[...]
 
 
-def dq_call(sc, q, da, db, k, v, cap_dq, h, after):
+def dq_call(order, sc, q, da, db, k, v, cap_dq, h):
     n = q.shape[1]
     pairs = n // 128
     block = k.shape[0] // SPAN
@@ -315,121 +341,95 @@
     mine = lambda p, j, s: (0, p)
     extra = lambda p, j, s: (0, pairs)
     other = lambda p, j, s: (item_block(j, s), p)
-    return pl.pallas_call(
+    return order.run(
+        "dq",
         dq_kernel,
-        grid_spec=pltpu.PrefetchScalarGridSpec(
-            num_scalar_prefetch=1,
-            grid=(pairs, SPAN),
-            in_specs=[
-                pl.BlockSpec((bq, 128), lambda p, j, s: (h, p)),
-                pl.BlockSpec((BR, 128), mine),
-                pl.BlockSpec((BR, 128), extra),
-                pl.BlockSpec((BR, 128), mine),
-                pl.BlockSpec((BR, 128), extra),
-                pl.BlockSpec((block, 128), other),
-                pl.BlockSpec((block, 128), other),
-                pl.BlockSpec((bq, 128), mine),
-            ]
-            + loose(len(after)),
-            out_specs=pl.BlockSpec((bq, 128), mine),
-            scratch_shapes=[pltpu.VMEM((bq, 128), f32)],
-        ),
-        out_shape=sds((bq, n), f32),
-        compiler_params=params(2),
-        name="dq",
-    )(sc, q, da, da, db, db, k, v, cap_dq, *after)
-
-
-def dkv_kernel(start, sc, k_ref, v_ref, q_ref, da_ref, xa_ref, db_ref, xb_ref, *rest):
-    dk_ref, dv_ref = rest[-2:]
-    pair = pl.program_id(0)
-    j = pl.program_id(1)
+        (pairs, SPAN),
+        (q, da, da, db, db, k, v, cap_dq),
+        [
+            pl.BlockSpec((bq, 128), lambda p, j, s: (h, p)),
+            pl.BlockSpec((BR, 128), mine),
+            pl.BlockSpec((BR, 128), extra),
+            pl.BlockSpec((BR, 128), mine),
+            pl.BlockSpec((BR, 128), extra),
+            pl.BlockSpec((block, 128), other),
+            pl.BlockSpec((block, 128), other),
+            pl.BlockSpec((bq, 128), mine),
+        ],
+        [pl.BlockSpec((bq, 128), mine)],
+        [sds((bq, n), f32)],
+        [pltpu.VMEM((bq, 128), f32)],
+        sc,
+    )[0]
+
+
+def dkv_kernel(parts, pair, sc, k_ref, v_ref, q_ref, *rest):
+    d_refs, x_refs = rest[0 : 2 * parts : 2], rest[1 : 2 * parts : 2]
+    dk_ref, dv_ref = rest[2 * parts :]
+    j = pl.program_id(0)
     masks = halves(128)
     keys = 512
+    queries = 2 * BR
 
     @pl.when(j == 0)
     def _():
-        if start:
-            dk_ref[...] = jnp.zeros_like(dk_ref)
-            dv_ref[...] = jnp.zeros_like(dv_ref)
-        else:
-            dk_ref[...] = rest[0][...]
-            dv_ref[...] = rest[1][...]
+        dk_ref[...] = jnp.zeros_like(dk_ref)
+        dv_ref[...] = jnp.zeros_like(dv_ref)
 
     @pl.when(j < sc[0])
     def _():
-        q = q_ref[...]
-        d = jnp.concatenate([da_ref[...], db_ref[...]], 0)
-        dx = jnp.concatenate([d, jnp.concatenate([xa_ref[...], xb_ref[...]], 0)], 1)
-        qs = [keep(q, m) for m in masks]
-        ds = [keep(d, m) for m in masks]
         for c in range(k_ref.shape[0] // keys):
             at = slice(c * keys, (c + 1) * keys)
             dk, dv = dk_ref[at, :], dv_ref[at, :]
             for h in range(2):
                 off = minus_delta(keys, 2 * pair + h)
-                e = jnp.exp2(mm_nt(k_ref[at, :], qs[h]))
-                dp = mm_nt(jnp.concatenate([keep(v_ref[at, :], masks[h]), off], 1), dx)
-                dv = dv + mm(e.astype(bf16), ds[h])
-                dk = dk + mm((e * dp).astype(bf16), qs[h])
+                vx = jnp.concatenate([keep(v_ref[at, :], masks[h]), off], 1)
+                for r in range(parts // 2):
+                    q = keep(q_ref[r * queries : (r + 1) * queries, :], masks[h])
+                    d = jnp.concatenate([d_refs[2 * r][...], d_refs[2 * r + 1][...]], 0)
+                    x = jnp.concatenate([x_refs[2 * r][...], x_refs[2 * r + 1][...]], 0)
+                    e = jnp.exp2(mm_nt(k_ref[at, :], q))
+                    dp = mm_nt(vx, jnp.concatenate([d, x], 1))
+                    dv = dv + mm(e.astype(bf16), keep(d, masks[h]))
+                    dk = dk + mm((e * dp).astype(bf16), q)
             dk_ref[at, :] = dk
             dv_ref[at, :] = dv
 
 
-def dkv_call(sc, k, v, q_all, da, db, h, rows, at, before, after):
+def dkv_call(order, sc, k, v, q_all, ds, pair):
     t, n = k.shape
     pairs = n // 128
-    bq = 2 * BR
-    per = t // bq
-    mine = pl.BlockSpec((rows, 128), lambda p, j, s: (at, p))
-    out = pl.BlockSpec((rows, 128), lambda p, j, s: (0, p))
-    other = pl.BlockSpec((BR, 128), lambda p, j, s: (item_block(j, s), p))
-    extra = pl.BlockSpec((BR, 128), lambda p, j, s: (item_block(j, s), pairs))
-    return pl.pallas_call(
-        functools.partial(dkv_kernel, not before),
-        grid_spec=pltpu.PrefetchScalarGridSpec(
-            num_scalar_prefetch=1,
-            grid=(pairs, SPAN),
-            in_specs=[
-                mine,
-                mine,
-                pl.BlockSpec((bq, 128), lambda p, j, s: (s[1 + SPAN + j] * per + h, p)),
-                other,
-                extra,
-                other,
-                extra,
-            ]
-            + [mine] * len(before)
-            + loose(len(after)),
-            out_specs=[out, out],
-        ),
-        out_shape=[sds((rows, n), f32)] * 2,
-        compiler_params=params(2),
-        name="dkv",
-    )(sc, k, v, q_all, da, da, db, db, *before, *after)
-
-
-def chunk_call(kernel, name, c, ins, specs, chunk_outs, sum_outs, whole_outs, before):
+    mine = pl.BlockSpec((t, 128), lambda j, s: (0, pair))
+    out = pl.BlockSpec((t, 128), lambda j, s: (0, 0))
+    other = pl.BlockSpec((BR, 128), lambda j, s: (item_block(j, s), pair))
+    extra = pl.BlockSpec((BR, 128), lambda j, s: (item_block(j, s), pairs))
+    return order.run(
+        "dkv",
+        functools.partial(dkv_kernel, len(ds), pair),
+        (SPAN,),
+        (k, v, q_all, *(x for d in ds for x in (d, d))),
+        [mine, mine, pl.BlockSpec((t, 128), lambda j, s: (s[1 + SPAN + j], pair))] + [other, extra] * len(ds),
+        [out, out],
+        [sds((t, 128), f32)] * 2,
+        scalar=sc,
+    )
+
+
+def chunk_call(order, kernel, name, c, ins, specs, chunk_outs, sum_outs, whole_outs, before):
     one = lambda r, w: pl.BlockSpec((r, w), lambda i: (0, 0))
-    loose = chunk_outs + sum_outs
+    own = chunk_outs + sum_outs
     into = [pl.BlockSpec((BR, w), lambda i: (c, 0)) for _, w, _ in whole_outs]
-    held = list(before)
-    body = kernel
-    if held:
-
-        def body(*refs):
-            kernel(*refs[: len(ins)], *refs[len(ins) + len(held) :])
-
-    return pl.pallas_call(
-        body,
-        grid=(1,),
-        in_specs=specs + [pl.BlockSpec(memory_space=pl.ANY)] * len(held),
-        out_specs=[one(r, w) for r, w, _ in loose] + into,
-        out_shape=[sds((r, w), k) for r, w, k in loose + whole_outs],
-        input_output_aliases={len(ins) + k: len(loose) + k for k in range(len(held))},
-        compiler_params=params(1),
-        name=name,
-    )(*ins, *held)
+    return order.run(
+        name,
+        kernel,
+        (1,),
+        ins,
+        specs,
+        [one(r, w) for r, w, _ in own] + into,
+        [sds((r, w), k) for r, w, k in own + whole_outs],
+        held=tuple(before),
+        first_held=len(own),
+    )
 
 
 def part(c, width):
@@ -446,20 +446,22 @@
     o_ref[:, n:] = mm_tn(c_ref[...], d_ref[...]).astype(bf16)
 
 
-def pair_grad_call(a, b, c, d):
+def pair_grad_call(order, a, b, c, d, part=0, parts=1, before=()):
     t, m = a.shape
     n, k = b.shape[1], d.shape[1]
     blk = 256
-    cols = pl.BlockSpec((t, blk), lambda i: (0, i))
-    return pl.pallas_call(
+    steps = m // blk // parts
+    cols = pl.BlockSpec((t, blk), lambda i: (0, part * steps + i))
+    return order.run(
+        "pair_grad",
         pair_grad_kernel,
-        grid=(m // blk,),
-        in_specs=[cols, whole(b.shape), cols, whole(d.shape)],
-        out_specs=pl.BlockSpec((blk, n + k), lambda i: (i, 0)),
-        out_shape=sds((m, n + k), bf16),
-        compiler_params=params(1),
-        name="pair_grad",
-    )(a, b, c, d)
+        (steps,),
+        (a, b, c, d),
+        [cols, whole(b.shape), cols, whole(d.shape)],
+        [pl.BlockSpec((blk, n + k), lambda i: (part * steps + i, 0))],
+        [sds((m, n + k), bf16)],
+        held=before,
+    )
 
 
 def ffn_kernel(p_ref, at_ref, v_ref, wg_ref, wd_ref, mid_ref, gu_ref, f_ref, a_ref, h_ref):
@@ -478,10 +480,11 @@
     f_ref[...] = mm(h, wd_ref[...]).astype(bf16)
 
 
-def ffn_call(c, patches, at, vec, wg, wd, before):
+def ffn_call(order, c, patches, at, vec, wg, wd, before):
     t, d = patches.shape
     n = wd.shape[0]
     return chunk_call(
+        order,
         ffn_kernel,
         "ffn",
         c,
@@ -517,10 +520,11 @@
     da_ref[...] = (mm_nt(dg, wg_ref[0]) + mm_nt(du, wg_ref[1])).astype(bf16)
 
 
-def ffn_back_call(c, f, mid, cot, gu, vec, wg, wd, before):
+def ffn_back_call(order, c, f, mid, cot, gu, vec, wg, wd, before):
     t, d = cot.shape
     n = wd.shape[0]
     return chunk_call(
+        order,
         ffn_back_kernel,
         "ffn_back",
         c,
@@ -565,10 +569,11 @@
     ds_ref[:, n:] = jnp.where(which == 0, one, jnp.where(which == 1, two, delta - one - two)).astype(bf16)
 
 
-def out_back_call(c, da, mid, at, cot, vec, w, o, li, before):
+def out_back_call(order, c, da, mid, at, cot, vec, w, o, li, before):
     t, d = cot.shape
     n = w.shape[0]
     return chunk_call(
+        order,
         out_back_kernel,
         "out_back",
         c,
@@ -581,7 +586,10 @@
     )
 
 
-def dqkv_kernel(dq_ref, dk_ref, dv_ref, qr_ref, kr_ref, c_ref, s1_ref, s2_ref, hg_ref, w_ref, p_ref, da_ref, hs_ref, cs_ref, d_ref):
+def dqkv_kernel(pairs, dq_ref, *refs):
+    dk_refs, dv_refs = refs[0 : 2 * pairs : 2], refs[1 : 2 * pairs : 2]
+    (qr_ref, kr_ref, c_ref, s1_ref, s2_ref, hg_ref, w_ref, p_ref, da_ref, hs_ref, cs_ref, d_ref) = refs[2 * pairs :]
+    side = lambda parts: jnp.concatenate([x[...] for x in parts], 1)
     n = dq_ref.shape[1]
     ones = head_ones(n)
     cos, s1, s2 = (tile3(t[...], n) for t in (c_ref, s1_ref, s2_ref))
@@ -594,8 +602,8 @@
         return r * (g - xh * (head_sum(g * xh, ones) * (1.0 / HD))), col_sum(dz * xh)
 
     dq, hq = back(dq_ref[...], qr_ref[...], row(hg_ref, 0))
-    dk, hk = back(dk_ref[...] * (1.0 / LOG2E), kr_ref[...], row(hg_ref, 1))
-    dql, dkl, dvl = dq.astype(bf16), dk.astype(bf16), dv_ref[...].astype(bf16)
+    dk, hk = back(side(dk_refs) * (1.0 / LOG2E), kr_ref[...], row(hg_ref, 1))
+    dql, dkl, dvl = dq.astype(bf16), dk.astype(bf16), side(dv_refs).astype(bf16)
     d_ref[:, :n] = dql
     d_ref[:, n : 2 * n] = dkl
     d_ref[:, 2 * n :] = dvl
@@ -607,15 +615,16 @@
     hs_ref[1:2, :] = hk
 
 
-def dqkv_call(c, dq, dk, dv, qr, kr, tabs, hg, w, patches, before):
+def dqkv_call(order, c, dq, dkv, qr, kr, tabs, hg, w, patches, before):
     t, d = patches.shape
     n = dq.shape[1]
     return chunk_call(
-        dqkv_kernel,
+        order,
+        functools.partial(dqkv_kernel, len(dkv)),
         "dqkv",
         c,
-        (dq, dk, dv, qr, kr, *tabs, hg, w, patches),
-        [part(c % 2, n)] * 3 + [part(c, n)] * 2 + [part(c, 128)] * 3 + [whole(hg.shape), whole(w.shape), part(c, d)],
+        (dq, *(x for two in dkv for x in two), qr, kr, *tabs, hg, w, patches),
+        [part(c % 2, n)] + [part(c, 128)] * (2 * len(dkv)) + [part(c, n)] * 2 + [part(c, 128)] * 3 + [whole(hg.shape), whole(w.shape), part(c, d)],
         [(BR, d, bf16)],
         [(2, n, f32), (1, d, f32)],
         [(t, 3 * n, bf16)],
@@ -631,9 +640,10 @@
     o_ref[...] = (dm_ref[...] + r * (z - xh * jnp.mean(z * xh, -1, keepdims=True))).astype(bf16)
 
 
-def last_call(c, da, patches, dm, vec, before):
+def last_call(order, c, da, patches, dm, vec, before):
     t, d = patches.shape
     return chunk_call(
+        order,
         last_kernel,
         "last",
         c,
@@ -687,13 +697,10 @@
             pltpu.make_async_copy(pieces[0], out.at[pl.ds(j * rows, rows)], sem.at[k, j]).wait()
 
 
-def gather_item(a, b, sc, count):
+def gather_item(a, b):
     size = lax.axis_size("wide")
     if size != 8:
-        full = [lax.all_gather(x, "wide") for x in (a, b)]
-        return [
-            jnp.concatenate([lax.dynamic_index_in_dim(x, sc[1 + SPAN + j], 0, False) for j in range(count)]) for x in full
-        ]
+        return [lax.all_gather(x, "wide") for x in (a, b)]
     go = lambda x, m: swap(x, "wide", 8, m)
     a2, b4 = go(a, 2), go(b, 4)
     a4, b2 = go(a, 4), go(b, 2)
@@ -702,20 +709,25 @@
     for four in ((a, a2, a4, a6), (b, b2, b4, b6)):
         for x in four:
             pieces += [x, go(x, 1)]
-    out = [sds((count * x.shape[0], x.shape[1]), x.dtype) for x in (a, b)]
-    return pl.pallas_call(
+    return pieces
+
+
+def pick(order, sc, pieces, count):
+    if len(pieces) == 2:
+        one = lambda x, j: lax.dynamic_index_in_dim(x, sc[1 + SPAN + j], 0, False)
+        return [jnp.concatenate([one(x, j) for j in range(count)]) for x in pieces]
+    rows, width = pieces[0].shape
+    return order.run(
+        "pick",
         functools.partial(pick_kernel, count, 8),
-        grid_spec=pltpu.PrefetchScalarGridSpec(
-            num_scalar_prefetch=1,
-            grid=(1,),
-            in_specs=loose(16),
-            out_specs=loose(2),
-            scratch_shapes=[pltpu.SemaphoreType.DMA((2, count))],
-        ),
-        out_shape=out,
-        compiler_params=params(1),
-        name="pick",
-    )(sc, *pieces)
+        (1,),
+        pieces,
+        loose(16),
+        [pl.BlockSpec((count * rows, width), lambda i, s: (0, 0))] * 2,
+        [sds((count * rows, width), pieces[0].dtype)] * 2,
+        [pltpu.SemaphoreType.DMA((2, count))],
+        sc,
+    )
 
 
 def gather_small(x, axis):
@@ -730,6 +742,13 @@
     mine = (order[:, None] ^ lax.axis_index(axis)) == order[None, :]
     out = jnp.sum(jnp.where(mine[:, :, None, None], got[None], 0.0), 1)
     return out.reshape(size, wide)[:, :n]
+
+
+def gather_now(x, axis):
+    n = x.shape[0]
+    wide = -(-n // 1024) * 1024
+    padded = jnp.pad(x, (0, wide - n)).reshape(1, 8, wide // 8)
+    return lax.all_gather(padded, axis, axis=0, tiled=True).reshape(-1, wide)[:, :n]
 
 
 def hop_kernel(have, sc, *refs):
@@ -749,12 +768,13 @@
 
 
 class Line:
-    def __init__(self, place):
+    def __init__(self, order, place):
+        self.order = order
         self.end = ((place == 0) | (place == 3)).astype(jnp.int32).reshape(1)
         self.x = self.second = self.send = None
         self.third = False
 
-    def step(self, new):
+    def step(self, new, after=()):
         if self.send is None:
             self.x = self.send = new
             return None
@@ -776,15 +796,17 @@
             outs.append("send")
         like = ins["r1"]
         block = pl.BlockSpec((BR // 2, like.shape[1]), lambda i, s: (i, 0))
-        got = pl.pallas_call(
+        got = self.order.run(
+            "hop",
             functools.partial(hop_kernel, {"in": list(ins), "out": outs}),
-            grid_spec=pltpu.PrefetchScalarGridSpec(
-                num_scalar_prefetch=1, grid=(2,), in_specs=[block] * len(ins), out_specs=[block] * len(outs)
-            ),
-            out_shape=[sds(like.shape, like.dtype)] * len(outs),
-            compiler_params=params(1),
-            name="hop",
-        )(self.end, *ins.values())
+            (2,),
+            list(ins.values()),
+            [block] * len(ins),
+            [block] * len(outs),
+            [sds(like.shape, like.dtype)] * len(outs),
+            scalar=self.end,
+            after=after,
+        )
         got = dict(zip(outs, got))
         self.third = self.second is not None
         self.x, self.second, self.send = new, got.get("second"), got.get("send")
@@ -792,27 +814,28 @@
 
 
 class Sums:
-    def __init__(self, size, place):
-        self.line = Line(place) if size == 4 else None
+    def __init__(self, order, size, place):
+        self.line = Line(order, place) if size == 4 else None
         self.names, self.done = [], {}
 
-    def add(self, name, x):
+    def add(self, name, x, after=()):
         if self.line is None:
             self.done[name] = lax.psum(x, "narrow")
             return
         if self.line.send is None:
             self.names = [None]
-        self._step(name, x)
-
-    def _step(self, name, x):
-        total = self.line.step(x)
+        self._step(name, x, after)
+
+    def _step(self, name, x, after):
+        total = self.line.step(x, after)
         self.names.append(name)
         if total is not None:
             self.done[self.names[-4]] = total
 
-    def get(self, name):
+    def get(self, name, after=()):
         while name not in self.done:
-            self._step(None, None)
+            self._step(None, None, after)
+            after = ()
         return self.done[name]
 
 
@@ -869,13 +892,13 @@
     blocks = jnp.arange(count, dtype=jnp.int32)
     item = jnp.sum((ends[None, :] <= blocks[:, None]).astype(jnp.int32), 1)
     is_item = item[:, None] == order[None, :]
-    pick = lambda values: jnp.sum(jnp.where(is_item, values[None, :], 0), 1)
-    firsts = pick(ends - spans)
+    choose = lambda values: jnp.sum(jnp.where(is_item, values[None, :], 0), 1)
+    firsts = choose(ends - spans)
     mine = blocks == me
     of_me = lambda values: jnp.sum(jnp.where(mine, values, 0))
     first = of_me(firsts)
-    length = of_me(pick(spans))
-    width = of_me(pick(grid_widths))
+    length = of_me(choose(spans))
+    width = of_me(choose(grid_widths))
     position = (me - first) * t + jnp.arange(t, dtype=jnp.int32)
     tabs = rope_tables(position, width)
     steps = first + jnp.minimum(jnp.arange(SPAN, dtype=jnp.int32), length - 1)
@@ -887,8 +910,7 @@
     mod = jnp.sum(silu_low.astype(f32)[:, None, None] * w_ada.astype(f32), 0)
     share = cd // deep
     sent = jnp.concatenate([mod.reshape(-1), lax.dynamic_slice_in_dim(cond, mz * share, share)])
-    got = gather_small(sent, "narrow").reshape(-1)
-    got = gather_small(got, "wide").reshape(count, deep, -1)
+    got = gather_now(gather_now(sent, "narrow").reshape(-1), "wide").reshape(count, deep, -1)
     mods = got[:, :, : 4 * ada].reshape(count, deep, 4, ada).transpose(0, 2, 1, 3).reshape(count, 4, d)
     conds = got[:, :, 4 * ada :].reshape(count, cd)
     my_mod = lax.dynamic_index_in_dim(mods, first, 0, False)
@@ -901,99 +923,121 @@
     tg_heads = jnp.tanh(cross_gate)
     tg = jnp.repeat(tg_heads, HD)[None, :]
 
+    order = Order()
     cap_raw = jnp.einsum("kd,jde->jke", captions, w_caption, preferred_element_type=f32)
-    cap_own = pl.pallas_call(
+    whole_cap = pl.BlockSpec((text, n), lambda i: (0, 0))
+    cap_own = order.run(
+        "caption_norm",
         caption_norm_kernel,
-        out_shape=[sds((text, n), bf16)] * 2,
-        compiler_params=params(0),
-        name="caption_norm",
-    )(cap_raw[0], cap_raw[1], hg)
-    ck, cv = gather_item(*cap_own, sc, 1)
+        (1,),
+        (cap_raw[0], cap_raw[1], hg),
+        [whole_cap, whole_cap, whole(hg.shape)],
+        [whole_cap, whole_cap],
+        [sds((text, n), bf16)] * 2,
+    )
+    cap_pieces = gather_item(*cap_own)
 
     chunks = range(t // BR)
     pairs_of = range(t // (2 * BR))
-    sums = Sums(deep, mz)
-    a1, q_raw, k_raw, q, k, v = qkv_call(patches, vec, w_qkv, tabs, hg)
-    k_all, v_all = gather_item(k, v, sc, SPAN)
+    sums = Sums(order, deep, mz)
+    a1, q_raw, k_raw, q, k, v = qkv_call(order, patches, vec, w_qkv, tabs, hg)
+    kv_pieces = gather_item(k, v)
     q_all = lax.all_gather(q, "wide", axis=0, tiled=True)
+    ck, cv = pick(order, sc, cap_pieces, 1)
+    k_all, v_all = pick(order, sc, kv_pieces, SPAN)
     heads_out = {}
     for h in pairs_of:
-        heads_out[h] = attend_call(sc, q, k_all, v_all, ck, cv, tg, h)
-        for c in (0, 1):
-            sums.add(("attn", 2 * h + c), mm(heads_out[h][0][c * BR : (c + 1) * BR], w_out).astype(bf16))
+        heads_out[h] = attend_call(order, sc, q, k_all, v_all, ck, cv, tg, h)
+        if h == 0:
+            sums.add(("attn", 0), mm(heads_out[0][0][:BR], w_out).astype(bf16))
+    for c in chunks[1:]:
+        at = (c % 2) * BR
+        sums.add(("attn", c), mm(heads_out[c // 2][0][at : at + BR], w_out).astype(bf16))
 
     mids, gus = {}, {}
     whole_out = ()
     for c in chunks:
-        mids[c], gus[c], ffn_part, *whole_out = ffn_call(c, patches, sums.get(("attn", c)), vec, w_gate_up, w_down, whole_out)
+        mids[c], gus[c], ffn_part, *whole_out = ffn_call(
+            order, c, patches, sums.get(("attn", c)), vec, w_gate_up, w_down, whole_out
+        )
         sums.add(("ffn", c), ffn_part)
     a3, hidden = whole_out
     whole_out = ()
     c4 = 0.0
     for c in chunks:
         da3_part, part_sum, *whole_out = ffn_back_call(
-            c, sums.get(("ffn", c)), mids[c], cotangent, gus[c], vec, w_gate_up, w_down, whole_out
+            order, c, sums.get(("ffn", c)), mids[c], cotangent, gus[c], vec, w_gate_up, w_down, whole_out
         )
         sums.add(("da3", c), da3_part)
         c4 = c4 + part_sum
     output, d_ffn, d_gu = whole_out
-    mlp_part = pair_grad_call(a3, d_gu, d_ffn, hidden)
-    g_mlp = scatter_rows(mlp_part)
-
-    d_mids, dqs, d_item, d_mixed, d_scaled = {}, {}, {}, {}, {}
+
+    d_mids, dqs, dq_caps, d_pieces, d_mixed, d_scaled = {}, {}, {}, {}, {}, {}
     whole_out = ()
+    mlp_part = ()
     c2 = c3 = dck = dcv = gate_sum = 0.0
     for h in pairs_of:
         mixed, o_self, linv = heads_out[h]
         for c in (2 * h, 2 * h + 1):
             d_mids[c], d_mixed[c], d_scaled[c], p3, p2, *whole_out = out_back_call(
-                c, sums.get(("da3", c)), mids[c], sums.get(("attn", c)), cotangent, vec, w_out, o_self, linv, whole_out
+                order, c, sums.get(("da3", c)), mids[c], sums.get(("attn", c)), cotangent, vec, w_out, o_self, linv, whole_out
             )
             c2, c3 = c2 + p2, c3 + p3
-        two = (d_scaled[2 * h], d_scaled[2 * h + 1])
-        d_item[h] = gather_item(*two, sc, SPAN)
-        dq_cap, pk, pv, pg = caption_back_call(q, d_mixed[2 * h], d_mixed[2 * h + 1], ck, cv, tg, h)
+            if c % 2 == 0:
+                mlp_part = pair_grad_call(order, a3, d_gu, d_ffn, hidden, h, len(pairs_of), mlp_part)
+        d_pieces[h] = gather_item(d_scaled[2 * h], d_scaled[2 * h + 1])
+        dq_caps[h], pk, pv, pg = caption_back_call(order, q, d_mixed[2 * h], d_mixed[2 * h + 1], ck, cv, tg, h)
         dck, dcv, gate_sum = dck + pk, dcv + pv, gate_sum + pg
-        dqs[h] = dq_call(sc, q, *two, k_all, v_all, dq_cap, h, (mlp_part,) if h == 0 else ())
     (d_attn,) = whole_out
+    g_mlp = scatter_rows(mlp_part[0])
+    back_pieces = gather_item(dck.astype(bf16), dcv.astype(bf16))
+    for h in pairs_of:
+        dqs[h] = dq_call(order, sc, q, d_scaled[2 * h], d_scaled[2 * h + 1], k_all, v_all, dq_caps[h], h)
 
     kept = (jnp.arange(SPAN) < length) & (first == me)
     in_slot = lambda x: jnp.sum(jnp.where(kept[:, None, None], x.reshape(SPAN, text, n).astype(f32), 0.0), 0)
-    got_k, got_v = gather_item(dck.astype(bf16), dcv.astype(bf16), sc, SPAN)
-    d_cap, hs_c = pl.pallas_call(
+    got_k, got_v = pick(order, sc, back_pieces, SPAN)
+    d_cap, hs_c = order.run(
+        "caption_grad",
         caption_grad_kernel,
-        out_shape=[sds((text, 2 * n), bf16), sds((1, n), f32)],
-        compiler_params=params(0),
-        name="caption_grad",
-    )(in_slot(got_k), in_slot(got_v), cap_raw[0], hg)
+        (1,),
+        (in_slot(got_k), in_slot(got_v), cap_raw[0], hg),
+        [whole_cap, whole_cap, whole_cap, whole(hg.shape)],
+        [pl.BlockSpec((text, 2 * n), lambda i: (0, 0)), pl.BlockSpec((1, n), lambda i: (0, 0))],
+        [sds((text, 2 * n), bf16), sds((1, n), f32)],
+    )
+    d_text = (mm_nt(d_cap[:, :n], w_caption[0]) + mm_nt(d_cap[:, n:], w_caption[1])).astype(bf16)
     cap_part = mm_tn(captions, d_cap).astype(bf16)
     g_cap = scatter_rows(cap_part)
-    d_text = (mm_nt(d_cap[:, :n], w_caption[0]) + mm_nt(d_cap[:, n:], w_caption[1])).astype(bf16)
     pieces = -(-d_text.shape[1] // d)
     padded = jnp.pad(d_text, ((0, 0), (0, pieces * d - d_text.shape[1])))
-    for k_ in range(pieces):
-        sums.add(("text", k_), padded[:, k_ * d : (k_ + 1) * d])
-
-    last_half = len(pairs_of) - 1
-    before = ()
-    for h in pairs_of[:-1]:
-        before = dkv_call(sc, k, v, q_all, *d_item[h], h, t, 0, before, ())
+    text_parts = [padded[:, p * d : (p + 1) * d] for p in range(pieces)]
+
+    ds = [x for h in pairs_of for x in pick(order, sc, d_pieces[h], SPAN)]
+    sums.add(("text", 0), text_parts[0])
+    dkv = []
+    for p in range(n // 128):
+        dkv.append(dkv_call(order, sc, k, v, q_all, ds, p))
+        if p + 1 < pieces:
+            sums.add(("text", p + 1), text_parts[p + 1], (cap_part,) if p == 0 else ())
+    for p in range(n // 128 + 1, pieces):
+        sums.add(("text", p), text_parts[p])
     whole_out = ()
     c1 = hs_qk = 0.0
-    for h in pairs_of:
-        dkv = dkv_call(sc, k, v, q_all, *d_item[last_half], last_half, 2 * BR, h, before, (d_text,))
-        for c in (2 * h, 2 * h + 1):
-            da1_part, p_hs, p1, *whole_out = dqkv_call(c, dqs[h], *dkv, q_raw, k_raw, tabs, hg, w_qkv, patches, whole_out)
-            sums.add(("da1", c), da1_part)
-            hs_qk, c1 = hs_qk + p_hs, c1 + p1
-    (d_qkv,) = whole_out
     mixed = jnp.concatenate([heads_out[h][0] for h in pairs_of])
-    g_attn = scatter_rows(pair_grad_call(a1, d_qkv, d_attn, mixed))
+    for c in chunks:
+        da1_part, p_hs, p1, *whole_out = dqkv_call(order, c, dqs[c // 2], dkv, q_raw, k_raw, tabs, hg, w_qkv, patches, whole_out)
+        if c == chunks[-1]:
+            (d_qkv,) = whole_out
+            attn_part = pair_grad_call(order, a1, d_qkv, d_attn, mixed)[0]
+        sums.add(("da1", c), da1_part, (g_mlp,) if c == 0 else ())
+        hs_qk, c1 = hs_qk + p_hs, c1 + p1
+    g_attn = scatter_rows(attn_part)
     whole_out = ()
     for c in chunks:
-        whole_out = last_call(c, sums.get(("da1", c)), patches, d_mids[c], vec, whole_out)
+        whole_out = last_call(order, c, sums.get(("da1", c), (g_cap,)), patches, d_mids[c], vec, whole_out)
     (grad_patches,) = whole_out
-    grad_captions = jnp.concatenate([sums.get(("text", k_)) for k_ in range(pieces)], 1)[:, : d_text.shape[1]]
+    grad_captions = jnp.concatenate([sums.get(("text", p)) for p in range(pieces)], 1)[:, : d_text.shape[1]]
 
     head_part = jnp.concatenate([hs_qk, hs_c]).reshape(3, heads, HD).sum(1)
     gate_part = gate_sum[0, ::HD] * (1.0 - tg_heads * tg_heads)

time: 1410 us -> 988 us (0.70); the launches traced: 1410 us -> 973 us
  Pallas kernels: 803 us -> 452 us
  waiting for transfers between devices: 296 us -> 233 us
  starting transfers between devices: 187 us -> 135 us
  blocking collectives: 0 us -> 23.1 us
    pallas_call x62 -> x63, Pallas kernels: 803 us -> 452 us  [run(): pl.pallas_call(body, grid_spec=pltpu.PrefetchScalarGridSpec(num_scalar_pr...]
    ppermute x42, waiting for transfers between devices: 175 us -> 104 us  [step(): go = lambda x, perm: lax.ppermute(x, 'narrow', perm)]
    ppermute x93 -> x83, starting transfers between devices: 110 us -> 56.8 us  [swap(): return lax.ppermute(x, axis, [(i, i ^ m) for i in range(size)])]
    all_gather x0 -> x2, blocking collectives: none -> 23.1 us  [gather_now(): lax.all_gather(padded, axis, axis=0, tiled=True).reshape(-1, wide)[:, :n]]
    ppermute x93 -> x83, waiting for transfers between devices: 121 us -> 129 us  [swap(): return lax.ppermute(x, axis, [(i, i ^ m) for i in range(size)])]
    unnamed x293 -> x300, local copies, waits for them, and re-layouts: 30.8 us -> 32 us
  transfers between devices with their start and end apart: 139 -> 129, of which waited for: 46 -> 44; matrix products, arithmetic and copies ran while one was open for 5% -> 7% of each run, Pallas kernels for 32% -> 46%
where the time goes in v4:
time: 988 us; the launch traced here: 973 us
  Pallas kernels  452 us (46%)
  waiting for transfers between devices  233 us (24%)
  starting transfers between devices  135 us (14%)
  local copies, waits for them, and re-layouts  44.2 us (4%)
  other arithmetic  39.6 us (4%)
  matrix products  23.3 us (2%)
  blocking collectives  23.1 us (2%)
  between operations  22.2 us (2%)
    pallas_call x63, Pallas kernels, run(): pl.pallas_call(body, grid_spec=pltpu.PrefetchScalarGridSpec(num_scalar_pr...  452 us
    ppermute x83, waiting for transfers between devices, swap(): return lax.ppermute(x, axis, [(i, i ^ m) for i in range(size)])  129 us
    ppermute x42, waiting for transfers between devices, step(): go = lambda x, perm: lax.ppermute(x, 'narrow', perm)  104 us
    ppermute x42, starting transfers between devices, step(): go = lambda x, perm: lax.ppermute(x, 'narrow', perm)  77.5 us
    ppermute x83, starting transfers between devices, swap(): return lax.ppermute(x, axis, [(i, i ^ m) for i in range(size)])  56.8 us
    unnamed x300, local copies, waits for them, and re-layouts  32 us
    all_gather x2, blocking collectives, gather_now(): lax.all_gather(padded, axis, axis=0, tiled=True).reshape(-1, wide)[:, :n]  23.1 us
  transfers between devices with their start and end apart: 129, of which 44 were waited for; matrix products, arithmetic and copies ran while one was open for 7% of the time, Pallas kernels for 46%

profile of v4, /device:TPU:0, one launch (start us, length us, event | category | flops | bytes accessed | tf_op | source)
XLA Modules:
  0.0 972.6 jit_solution(5137536018314591252)
XLA Ops:
  31.2 13.8 %all_gather.9 = f32[4,8,256]{2,1,0:T(8,128)S(1)} all-gather(f32[1,8,256]{2,1,0:T(8,128)S(1)} %reshape.357), channel_id=1, replica_groups=mesh['wide'=8,'narrow'=4] {'narrow'}, dimensions={0}, use_global_device_ids=true | all-gather | bytes 40960 | tf_op jit(solution)/shard_map/all_gather | solution.py:751
  45.1 9.3 all_gather.10
  63.8 12.7 %qkv.1 = (bf16[1024,1536]{1,0:T(8,128)(2,1)}, f32[1024,384]{1,0:T(8,128)}, f32[1024,384]{1,0:T(8,128)}, bf16[1024,384]{1,0:T(8,128)(2,1)}, bf16[1024,384]{1,0:T(8,128)(2,1)}, /*index=5*/bf16[1024,384]{1,0:T(8,128)(2,1)}) custom-call(bf16[1024,1536]{1,0:T(8,128)(2,1)} %refs_1_.7, f32[4,1536]{1,0:T(4,128)} %maximum_multiply_fusion.1.refs_1_.refs_2_.refs_4_.refs_3_, ...), custom_call_target="tpu_custom_call" | custom-call | tf_op jit(solution)/shard_map/qkv/pallas_call | solution.py:45
  85.4 11.8 %collective-permute-done.10.refs_13_ = bf16[1024,384]{1,0:T(8,128)(2,1)S(1)} collective-permute-done((bf16[1024,384]{1,0:T(8,128)(2,1)}, bf16[1024,384]{1,0:T(8,128)(2,1)S(1)}, u32[]{:S(2)}, u32[]{:S(2)}) %collective-permute-start.10) | collective-permute-done | bytes 786464 | tf_op jit(solution)/shard_map/ppermute | solution.py:680
  99.5 14.0 %collective-permute-done.3.refs_5_ = bf16[1024,384]{1,0:T(8,128)(2,1)} collective-permute-done((bf16[1024,384]{1,0:T(8,128)(2,1)}, bf16[1024,384]{1,0:T(8,128)(2,1)}, u32[]{:S(2)}, u32[]{:S(2)}) %collective-permute-start.3) | collective-permute-done | bytes 786464 | tf_op jit(solution)/shard_map/ppermute | solution.py:680
  116.4 15.2 %collective-permute-done.12.refs_15_ = bf16[1024,384]{1,0:T(8,128)(2,1)} collective-permute-done((bf16[1024,384]{1,0:T(8,128)(2,1)S(1)}, bf16[1024,384]{1,0:T(8,128)(2,1)}, u32[]{:S(2)}, u32[]{:S(2)}) %collective-permute-start.12) | collective-permute-done | bytes 786464 | tf_op jit(solution)/shard_map/ppermute | solution.py:680
  140.2 6.6 pick.6
  146.8 22.1 %attend.2 = (bf16[512,384]{1,0:T(8,128)(2,1)}, bf16[512,384]{1,0:T(8,128)(2,1)}, f32[512,384]{1,0:T(8,128)}) custom-call(s32[9]{0:T(128)} %pad_add_fusion.refs_0_, bf16[1024,384]{1,0:T(8,128)(2,1)} %get-tuple-element.191.refs_1_.refs_0_, bf16[4096,384]{1,0:T(8,128)(2,1)} %get-tuple-element.197.refs_2_.refs_7_.refs_6_, ...), custom_call_target="tpu_custom_call" | custom-call | tf_op jit(solution)/shard_map/attend/pallas_call | solution.py:45
  173.0 22.2 %attend.3 = (bf16[512,384]{1,0:T(8,128)(2,1)}, bf16[512,384]{1,0:T(8,128)(2,1)}, f32[512,384]{1,0:T(8,128)}) custom-call(s32[9]{0:T(128)} %pad_add_fusion.refs_0_, bf16[1024,384]{1,0:T(8,128)(2,1)} %get-tuple-element.191.refs_1_.refs_0_, bf16[4096,384]{1,0:T(8,128)(2,1)} %get-tuple-element.197.refs_2_.refs_7_.refs_6_, ...), custom_call_target="tpu_custom_call" | custom-call | tf_op jit(solution)/shard_map/attend/pallas_call | solution.py:45
  201.7 17.2 %collective-permute-done.29.refs_1_ = bf16[256,1536]{1,0:T(8,128)(2,1)S(1)} collective-permute-done((bf16[256,1536]{1,0:T(8,128)(2,1)}, bf16[256,1536]{1,0:T(8,128)(2,1)S(1)}, u32[]{:S(2)}, u32[]{:S(2)}) %collective-permute-start.29) | collective-permute-done | bytes 786464 | tf_op jit(solution)/shard_map/ppermute | solution.py:781
  228.7 14.6 %collective-permute-done.31.refs_1_ = bf16[256,1536]{1,0:T(8,128)(2,1)S(1)} collective-permute-done((bf16[256,1536]{1,0:T(8,128)(2,1)}, bf16[256,1536]{1,0:T(8,128)(2,1)S(1)}, u32[]{:S(2)}, u32[]{:S(2)}) %collective-permute-start.31) | collective-permute-done | bytes 786464 | tf_op jit(solution)/shard_map/ppermute | solution.py:781
  252.1 8.5 ffn.4
  260.5 6.7 collective-permute-done.33.refs_1_
  276.5 8.5 ffn.5
  299.4 8.5 ffn.6
  321.9 8.5 ffn.7
  343.5 9.6 ffn_back.4
  363.9 9.6 ffn_back.5
  383.5 9.6 ffn_back.6
  402.7 9.6 ffn_back.7
  420.7 5.7 out_back.4
  426.5 10.0 %pair_grad.3.refs_6_.refs_5_ = bf16[1536,3072]{1,0:T(8,128)(2,1)} custom-call(bf16[1024,1536]{1,0:T(8,128)(2,1)} %get-tuple-element.268.refs_0_, bf16[1024,2048]{1,0:T(8,128)(2,1)} %get-tuple-element.269.refs_1_, bf16[1024,1536]{1,0:T(8,128)(2,1)} %get-tuple-element.270.refs_2_, bf16[1024,1024]{1,0:T(8,128)(2,1)} %get-tuple-element.271.refs_3_, ...), custom_call_target="tpu_custom_call" | custom-call | tf_op jit(solution)/shard_map/pair_grad/pallas_call | solution.py:45
  445.1 5.8 out_back.5
  460.4 5.8 out_back.6
  466.2 10.0 %pair_grad.4.refs_3_ = bf16[1536,3072]{1,0:T(8,128)(2,1)} custom-call(bf16[1024,1536]{1,0:T(8,128)(2,1)} %get-tuple-element.268.refs_0_, bf16[1024,2048]{1,0:T(8,128)(2,1)} %get-tuple-element.269.refs_1_, bf16[1024,1536]{1,0:T(8,128)(2,1)} %get-tuple-element.270.refs_2_, ...), custom_call_target="tpu_custom_call", output_to_operand_aliasing={{}: (5, {})} | custom-call | tf_op jit(solution)/shard_map/pair_grad/pallas_call | solution.py:45
  479.3 10.0 %collective-permute-done.53.refs_1_ = bf16[256,1536]{1,0:T(8,128)(2,1)S(1)} collective-permute-done((bf16[256,1536]{1,0:T(8,128)(2,1)S(1)}, bf16[256,1536]{1,0:T(8,128)(2,1)S(1)}, u32[]{:S(2)}, u32[]{:S(2)}) %collective-permute-start.53) | collective-permute-done | bytes 786464 | tf_op jit(solution)/shard_map/ppermute | solution.py:781
  492.6 5.9 out_back.7
  498.6 5.6 caption_back.3
  510.5 5.9 collective-permute-done.64.refs_13_
  518.6 6.4 collective-permute-done.55.refs_3_
  536.5 26.9 %dq.2.refs_9_.refs_0_ = f32[512,384]{1,0:T(8,128)} custom-call(s32[9]{0:T(128)} %pad_add_fusion.refs_0_, bf16[1024,384]{1,0:T(8,128)(2,1)} %get-tuple-element.191.refs_1_.refs_0_, bf16[256,512]{1,0:T(8,128)(2,1)} %get-tuple-element.297.refs_2_.refs_3_.refs_1_, bf16[256,512]{1,0:T(8,128)(2,1)} %get-tuple-element.297.refs_2_.refs_3_.refs_1_, ...), custom_call_target="tpu_custom_call" | custom-call | tf_op jit(solution)/shard_map/dq/pallas_call | solution.py:45
  563.5 26.8 %dq.3.refs_17_.refs_0_ = f32[512,384]{1,0:T(8,128)} custom-call(s32[9]{0:T(128)} %pad_add_fusion.refs_0_, bf16[1024,384]{1,0:T(8,128)(2,1)} %get-tuple-element.191.refs_1_.refs_0_, bf16[256,512]{1,0:T(8,128)(2,1)} %get-tuple-element.294.refs_2_.refs_3_.refs_1_, bf16[256,512]{1,0:T(8,128)(2,1)} %get-tuple-element.294.refs_2_.refs_3_.refs_1_, ...), custom_call_target="tpu_custom_call" | custom-call | tf_op jit(solution)/shard_map/dq/pallas_call | solution.py:45
  607.2 7.0 collective-permute-done.70.refs_3_
  616.8 6.7 collective-permute-done.74.refs_7_
  635.4 10.8 %collective-permute-done.81.refs_15_ = bf16[256,512]{1,0:T(8,128)(2,1)S(1)} collective-permute-done((bf16[256,512]{1,0:T(8,128)(2,1)S(1)}, bf16[256,512]{1,0:T(8,128)(2,1)S(1)}, u32[]{:S(2)}, u32[]{:S(2)}) %collective-permute-start.81) | collective-permute-done | bytes 262176 | tf_op jit(solution)/shard_map/ppermute | solution.py:680
  652.4 7.9 collective-permute-done.84.refs_3_
  672.4 8.4 collective-permute-done.93.refs_13_
  696.1 21.7 %dkv.3 = (f32[1024,128]{1,0:T(8,128)}, f32[1024,128]{1,0:T(8,128)}) custom-call(s32[9]{0:T(128)} %pad_add_fusion.refs_0_, bf16[1024,384]{1,0:T(8,128)(2,1)} %get-tuple-element.192.refs_1_, bf16[1024,384]{1,0:T(8,128)(2,1)} %get-tuple-element.193.refs_9_.refs_2_, bf16[8192,384]{1,0:T(8,128)(2,1)} %all-gather.2.cloned.1.call-done.refs_3_, ...), custom_call_target="tpu_custom_call" | custom-call | tf_op jit(solution)/shard_map/dkv/pallas_call | solution.py:45
  722.8 21.7 %dkv.4 = (f32[1024,128]{1,0:T(8,128)}, f32[1024,128]{1,0:T(8,128)}) custom-call(s32[9]{0:T(128)} %pad_add_fusion.refs_0_, bf16[1024,384]{1,0:T(8,128)(2,1)} %get-tuple-element.192.refs_1_, bf16[1024,384]{1,0:T(8,128)(2,1)} %get-tuple-element.193.refs_9_.refs_2_, bf16[8192,384]{1,0:T(8,128)(2,1)} %all-gather.2.cloned.1.call-done.refs_3_, ...), custom_call_target="tpu_custom_call" | custom-call | tf_op jit(solution)/shard_map/dkv/pallas_call | solution.py:45
  758.1 21.7 %dkv.5 = (f32[1024,128]{1,0:T(8,128)}, f32[1024,128]{1,0:T(8,128)}) custom-call(s32[9]{0:T(128)} %pad_add_fusion.refs_0_, bf16[1024,384]{1,0:T(8,128)(2,1)} %get-tuple-element.192.refs_1_, bf16[1024,384]{1,0:T(8,128)(2,1)} %get-tuple-element.193.refs_9_.refs_2_, bf16[8192,384]{1,0:T(8,128)(2,1)} %all-gather.2.cloned.1.call-done.refs_3_, ...), custom_call_target="tpu_custom_call" | custom-call | tf_op jit(solution)/shard_map/dkv/pallas_call | solution.py:45
  779.8 6.6 dqkv.4
  792.3 6.6 dqkv.5
  798.9 11.2 %collective-permute-done.101.refs_1_ = bf16[256,1536]{1,0:T(8,128)(2,1)S(1)} collective-permute-done((bf16[256,1536]{1,0:T(8,128)(2,1)}, bf16[256,1536]{1,0:T(8,128)(2,1)S(1)}, u32[]{:S(2)}, u32[]{:S(2)}) %collective-permute-start.101) | collective-permute-done | bytes 786464 | tf_op jit(solution)/shard_map/ppermute | solution.py:781
  821.4 6.6 dqkv.6
  828.0 6.7 collective-permute-done.103.refs_1_
  839.2 6.6 dqkv.7
  845.9 11.0 %pair_grad.5.refs_7_ = bf16[1536,1536]{1,0:T(8,128)(2,1)} custom-call(bf16[1024,1536]{1,0:T(8,128)(2,1)} %get-tuple-element.195.refs_17_.refs_0_, bf16[1024,1152]{1,0:T(8,128)(2,1)} %get-tuple-element.334.refs_1_, bf16[1024,1536]{1,0:T(8,128)(2,1)} %get-tuple-element.335.refs_2_, bf16[1024,384]{1,0:T(8,128)(2,1)} %pad_maximum_fusion.2.refs_3_, ...), custom_call_target="tpu_custom_call" | custom-call | tf_op jit(solution)/shard_map/pair_grad/pallas_call | solution.py:45
  902.6 9.4 collective-permute-done.107.refs_1_
  (687 shorter events, 416.1 us)
Async XLA Ops:
  7.2 688.9 %all-gather.2.cloned.1.call-start = ((), (), s32[]{:S(2)}) async-start(), calls=%async_computation.3 | async-start | bytes 7077888 | tf_op jit(solution)/shard_map/all_gather | solution.py:945
  16.6 41.0 %collective-permute-start.15 = (bf16[256,384]{1,0:T(8,128)(2,1)}, bf16[256,384]{1,0:T(8,128)(2,1)S(1)}, u32[]{:S(2)}, u32[]{:S(2)}) collective-permute-start(bf16[256,384]{1,0:T(8,128)(2,1)} %get-tuple-element.190.refs_7_.refs_1_), channel_id=1, source_target_pairs={{0,8},{4,12},{8,0},{12,4},{16,24},{20,28},{24,16},{28,20},{1,9},{5... | collective-permute-start | bytes 589832 | tf_op jit(solution)/shard_map/ppermute | solution.py:680
  19.5 40.0 %collective-permute-start.17 = (bf16[256,384]{1,0:T(8,128)(2,1)}, bf16[256,384]{1,0:T(8,128)(2,1)S(1)}, u32[]{:S(2)}, u32[]{:S(2)}) collective-permute-start(bf16[256,384]{1,0:T(8,128)(2,1)} %get-tuple-element.190.refs_7_.refs_1_), channel_id=1, source_target_pairs={{0,16},{4,20},{8,24},{12,28},{16,0},{20,4},{24,8},{28,12},{1,17},{... | collective-permute-start | bytes 589832 | tf_op jit(solution)/shard_map/ppermute | solution.py:680
  21.0 37.0 %collective-permute-start.24 = (bf16[256,384]{1,0:T(8,128)(2,1)}, bf16[256,384]{1,0:T(8,128)(2,1)}, u32[]{:S(2)}, u32[]{:S(2)}) collective-permute-start(bf16[256,384]{1,0:T(8,128)(2,1)} %get-tuple-element.194.refs_9_), channel_id=1, source_target_pairs={{0,16},{4,20},{8,24},{12,28},{16,0},{20,4},{24,8},{28,12},{1,17},{... | collective-permute-start | bytes 589832 | tf_op jit(solution)/shard_map/ppermute | solution.py:680
  21.5 38.0 %collective-permute-start.22 = (bf16[256,384]{1,0:T(8,128)(2,1)}, bf16[256,384]{1,0:T(8,128)(2,1)}, u32[]{:S(2)}, u32[]{:S(2)}) collective-permute-start(bf16[256,384]{1,0:T(8,128)(2,1)} %get-tuple-element.194.refs_9_), channel_id=1, source_target_pairs={{0,8},{4,12},{8,0},{12,4},{16,24},{20,28},{24,16},{28,20},{1,9},{5... | collective-permute-start | bytes 589832 | tf_op jit(solution)/shard_map/ppermute | solution.py:680
  21.6 38.5 %collective-permute-start.14 = (bf16[256,384]{1,0:T(8,128)(2,1)}, bf16[256,384]{1,0:T(8,128)(2,1)}, u32[]{:S(2)}, u32[]{:S(2)}) collective-permute-start(bf16[256,384]{1,0:T(8,128)(2,1)} %get-tuple-element.190.refs_7_.refs_1_), channel_id=1, source_target_pairs={{0,4},{4,0},{8,12},{12,8},{16,20},{20,16},{24,28},{28,24},{1,5},{5... | collective-permute-start | bytes 589832 | tf_op jit(solution)/shard_map/ppermute | solution.py:680
  58.0 18.6 %collective-permute-start.19 = (bf16[256,384]{1,0:T(8,128)(2,1)S(1)}, bf16[256,384]{1,0:T(8,128)(2,1)S(1)}, u32[]{:S(2)}, u32[]{:S(2)}) collective-permute-start(bf16[256,384]{1,0:T(8,128)(2,1)S(1)} %collective-permute-done.15.refs_3_), channel_id=1, source_target_pairs={{0,16},{4,20},{8,24},{12,28},{16,0},{20,4},{24,8},{28,12},{1,17},{... | collective-permute-start | bytes 589832 | tf_op jit(solution)/shard_map/ppermute | solution.py:680
  59.5 19.2 %collective-permute-start.16 = (bf16[256,384]{1,0:T(8,128)(2,1)S(1)}, bf16[256,384]{1,0:T(8,128)(2,1)S(1)}, u32[]{:S(2)}, u32[]{:S(2)}) collective-permute-start(bf16[256,384]{1,0:T(8,128)(2,1)S(1)} %collective-permute-done.15.refs_3_), channel_id=1, source_target_pairs={{0,4},{4,0},{8,12},{12,8},{16,20},{20,16},{24,28},{28,24},{1,5},{5... | collective-permute-start | bytes 589832 | tf_op jit(solution)/shard_map/ppermute | solution.py:680
  59.5 18.7 %collective-permute-start.26 = (bf16[256,384]{1,0:T(8,128)(2,1)}, bf16[256,384]{1,0:T(8,128)(2,1)S(1)}, u32[]{:S(2)}, u32[]{:S(2)}) collective-permute-start(bf16[256,384]{1,0:T(8,128)(2,1)} %collective-permute-done.24.refs_13_), channel_id=1, source_target_pairs={{0,8},{4,12},{8,0},{12,4},{16,24},{20,28},{24,16},{28,20},{1,9},{5... | collective-permute-start | bytes 589832 | tf_op jit(solution)/shard_map/ppermute | solution.py:680
  60.1 20.1 %collective-permute-start.18 = (bf16[256,384]{1,0:T(8,128)(2,1)S(1)}, bf16[256,384]{1,0:T(8,128)(2,1)S(1)}, u32[]{:S(2)}, u32[]{:S(2)}) collective-permute-start(bf16[256,384]{1,0:T(8,128)(2,1)S(1)} %collective-permute-done.17.refs_5_), channel_id=1, source_target_pairs={{0,4},{4,0},{8,12},{12,8},{16,20},{20,16},{24,28},{28,24},{1,5},{5... | collective-permute-start | bytes 589832 | tf_op jit(solution)/shard_map/ppermute | solution.py:680
  76.6 20.7 %collective-permute-start.10 = (bf16[1024,384]{1,0:T(8,128)(2,1)}, bf16[1024,384]{1,0:T(8,128)(2,1)S(1)}, u32[]{:S(2)}, u32[]{:S(2)}) collective-permute-start(bf16[1024,384]{1,0:T(8,128)(2,1)} %get-tuple-element.193.refs_9_.refs_2_), channel_id=1, source_target_pairs={{0,16},{4,20},{8,24},{12,28},{16,0},{20,4},{24,8},{28,12},{1,17},{... | collective-permute-start | bytes 2359304 | tf_op jit(solution)/shard_map/ppermute | solution.py:680
  78.2 20.7 %collective-permute-start.1 = (bf16[1024,384]{1,0:T(8,128)(2,1)}, bf16[1024,384]{1,0:T(8,128)(2,1)}, u32[]{:S(2)}, u32[]{:S(2)}) collective-permute-start(bf16[1024,384]{1,0:T(8,128)(2,1)} %get-tuple-element.192.refs_1_), channel_id=1, source_target_pairs={{0,8},{4,12},{8,0},{12,4},{16,24},{20,28},{24,16},{28,20},{1,9},{5... | collective-permute-start | bytes 2359304 | tf_op jit(solution)/shard_map/ppermute | solution.py:680
  78.7 34.7 %collective-permute-start.3 = (bf16[1024,384]{1,0:T(8,128)(2,1)}, bf16[1024,384]{1,0:T(8,128)(2,1)}, u32[]{:S(2)}, u32[]{:S(2)}) collective-permute-start(bf16[1024,384]{1,0:T(8,128)(2,1)} %get-tuple-element.192.refs_1_), channel_id=1, source_target_pairs={{0,16},{4,20},{8,24},{12,28},{16,0},{20,4},{24,8},{28,12},{1,17},{... | collective-permute-start | bytes 2359304 | tf_op jit(solution)/shard_map/ppermute | solution.py:680
  80.2 35.6 %collective-permute-start.8 = (bf16[1024,384]{1,0:T(8,128)(2,1)}, bf16[1024,384]{1,0:T(8,128)(2,1)}, u32[]{:S(2)}, u32[]{:S(2)}) collective-permute-start(bf16[1024,384]{1,0:T(8,128)(2,1)} %get-tuple-element.193.refs_9_.refs_2_), channel_id=1, source_target_pairs={{0,8},{4,12},{8,0},{12,4},{16,24},{20,28},{24,16},{28,20},{1,9},{5... | collective-permute-start | bytes 2359304 | tf_op jit(solution)/shard_map/ppermute | solution.py:680
  85.3 30.5 %collective-permute-start = (bf16[1024,384]{1,0:T(8,128)(2,1)}, bf16[1024,384]{1,0:T(8,128)(2,1)S(1)}, u32[]{:S(2)}, u32[]{:S(2)}) collective-permute-start(bf16[1024,384]{1,0:T(8,128)(2,1)} %get-tuple-element.192.refs_1_), channel_id=1, source_target_pairs={{0,4},{4,0},{8,12},{12,8},{16,20},{20,16},{24,28},{28,24},{1,5},{5... | collective-permute-start | bytes 2359304 | tf_op jit(solution)/shard_map/ppermute | solution.py:680
  97.3 19.0 %collective-permute-start.7 = (bf16[1024,384]{1,0:T(8,128)(2,1)}, bf16[1024,384]{1,0:T(8,128)(2,1)S(1)}, u32[]{:S(2)}, u32[]{:S(2)}) collective-permute-start(bf16[1024,384]{1,0:T(8,128)(2,1)} %get-tuple-element.193.refs_9_.refs_2_), channel_id=1, source_target_pairs={{0,4},{4,0},{8,12},{12,8},{16,20},{20,16},{24,28},{28,24},{1,5},{5... | collective-permute-start | bytes 2359304 | tf_op jit(solution)/shard_map/ppermute | solution.py:680
  98.9 32.6 %collective-permute-start.12 = (bf16[1024,384]{1,0:T(8,128)(2,1)S(1)}, bf16[1024,384]{1,0:T(8,128)(2,1)}, u32[]{:S(2)}, u32[]{:S(2)}) collective-permute-start(bf16[1024,384]{1,0:T(8,128)(2,1)S(1)} %collective-permute-done.10.refs_13_), channel_id=1, source_target_pairs={{0,8},{4,12},{8,0},{12,4},{16,24},{20,28},{24,16},{28,20},{1,9},{5... | collective-permute-start | bytes 2359304 | tf_op jit(solution)/shard_map/ppermute | solution.py:680
  113.5 19.1 %collective-permute-start.5 = (bf16[1024,384]{1,0:T(8,128)(2,1)}, bf16[1024,384]{1,0:T(8,128)(2,1)}, u32[]{:S(2)}, u32[]{:S(2)}) collective-permute-start(bf16[1024,384]{1,0:T(8,128)(2,1)} %collective-permute-done.1.refs_3_), channel_id=1, source_target_pairs={{0,16},{4,20},{8,24},{12,28},{16,0},{20,4},{24,8},{28,12},{1,17},{... | collective-permute-start | bytes 2359304 | tf_op jit(solution)/shard_map/ppermute | solution.py:680
  115.8 24.3 %collective-permute-start.2 = (bf16[1024,384]{1,0:T(8,128)(2,1)}, bf16[1024,384]{1,0:T(8,128)(2,1)}, u32[]{:S(2)}, u32[]{:S(2)}) collective-permute-start(bf16[1024,384]{1,0:T(8,128)(2,1)} %collective-permute-done.1.refs_3_), channel_id=1, source_target_pairs={{0,4},{4,0},{8,12},{12,8},{16,20},{20,16},{24,28},{28,24},{1,5},{5... | collective-permute-start | bytes 2359304 | tf_op jit(solution)/shard_map/ppermute | solution.py:680
  116.3 23.8 %collective-permute-start.4 = (bf16[1024,384]{1,0:T(8,128)(2,1)}, bf16[1024,384]{1,0:T(8,128)(2,1)}, u32[]{:S(2)}, u32[]{:S(2)}) collective-permute-start(bf16[1024,384]{1,0:T(8,128)(2,1)} %collective-permute-done.3.refs_5_), channel_id=1, source_target_pairs={{0,4},{4,0},{8,12},{12,8},{16,20},{20,16},{24,28},{28,24},{1,5},{5... | collective-permute-start | bytes 2359304 | tf_op jit(solution)/shard_map/ppermute | solution.py:680
  133.5 653.0 %reduce-scatter.4.cloned.1.call-start = ((), (), s32[]{:S(2)}) async-start(), calls=%async_computation.4 | async-start | bytes 10616832 | tf_op jit(solution)/shard_map/reduce_scatter | solution.py:843
  171.4 25.3 %collective-permute-start.28 = (bf16[256,1536]{1,0:T(8,128)(2,1)}, bf16[256,1536]{1,0:T(8,128)(2,1)}, u32[]{:S(2)}, u32[]{:S(2)}) collective-permute-start(bf16[256,1536]{1,0:T(8,128)(2,1)} %convolution_convert_fusion.4.refs_2_), channel_id=1, source_target_pairs={{0,1},{3,2},{1,0},{2,3},{4,5},{7,6},{5,4},{6,7},{8,9},{11,10},{9,8... | collective-permute-start | bytes 2359304 | tf_op jit(solution)/shard_map/ppermute | solution.py:781
  199.2 19.7 %collective-permute-start.29 = (bf16[256,1536]{1,0:T(8,128)(2,1)}, bf16[256,1536]{1,0:T(8,128)(2,1)S(1)}, u32[]{:S(2)}, u32[]{:S(2)}) collective-permute-start(bf16[256,1536]{1,0:T(8,128)(2,1)} %get-tuple-element.202), channel_id=1, source_target_pairs={{0,1},{3,2},{1,0},{2,3},{4,5},{7,6},{5,4},{6,7},{8,9},{11,10},{9,8... | collective-permute-start | bytes 2359304 | tf_op jit(solution)/shard_map/ppermute | solution.py:781
  199.5 19.4 %collective-permute-start.30 = (bf16[256,1536]{1,0:T(8,128)(2,1)}, bf16[256,1536]{1,0:T(8,128)(2,1)S(1)}, u32[]{:S(2)}, u32[]{:S(2)}) collective-permute-start(bf16[256,1536]{1,0:T(8,128)(2,1)} %get-tuple-element.203.refs_3_.refs_6_), channel_id=1, source_target_pairs={{1,2},{2,1},{5,6},{6,5},{9,10},{10,9},{13,14},{14,13},{17,18},{18,... | collective-permute-start | bytes 2359304 | tf_op jit(solution)/shard_map/ppermute | solution.py:781
  223.8 19.6 %collective-permute-start.31 = (bf16[256,1536]{1,0:T(8,128)(2,1)}, bf16[256,1536]{1,0:T(8,128)(2,1)S(1)}, u32[]{:S(2)}, u32[]{:S(2)}) collective-permute-start(bf16[256,1536]{1,0:T(8,128)(2,1)} %get-tuple-element.204.refs_2_), channel_id=1, source_target_pairs={{0,1},{3,2},{1,0},{2,3},{4,5},{7,6},{5,4},{6,7},{8,9},{11,10},{9,8... | collective-permute-start | bytes 2359304 | tf_op jit(solution)/shard_map/ppermute | solution.py:781
  248.6 18.6 %collective-permute-start.33 = (bf16[256,1536]{1,0:T(8,128)(2,1)}, bf16[256,1536]{1,0:T(8,128)(2,1)S(1)}, u32[]{:S(2)}, u32[]{:S(2)}) collective-permute-start(bf16[256,1536]{1,0:T(8,128)(2,1)} %get-tuple-element.206.refs_2_), channel_id=1, source_target_pairs={{0,1},{3,2},{1,0},{2,3},{4,5},{7,6},{5,4},{6,7},{8,9},{11,10},{9,8... | collective-permute-start | bytes 2359304 | tf_op jit(solution)/shard_map/ppermute | solution.py:781
  271.9 18.6 %collective-permute-start.35 = (bf16[256,1536]{1,0:T(8,128)(2,1)}, bf16[256,1536]{1,0:T(8,128)(2,1)S(1)}, u32[]{:S(2)}, u32[]{:S(2)}) collective-permute-start(bf16[256,1536]{1,0:T(8,128)(2,1)} %get-tuple-element.211.refs_2_), channel_id=1, source_target_pairs={{0,1},{3,2},{1,0},{2,3},{4,5},{7,6},{5,4},{6,7},{8,9},{11,10},{9,8... | collective-permute-start | bytes 2359304 | tf_op jit(solution)/shard_map/ppermute | solution.py:781
  416.9 19.6 %collective-permute-start.49 = (bf16[256,1536]{1,0:T(8,128)(2,1)}, bf16[256,1536]{1,0:T(8,128)(2,1)S(1)}, u32[]{:S(2)}, u32[]{:S(2)}) collective-permute-start(bf16[256,1536]{1,0:T(8,128)(2,1)} %get-tuple-element.266.refs_2_), channel_id=1, source_target_pairs={{0,1},{3,2},{1,0},{2,3},{4,5},{7,6},{5,4},{6,7},{8,9},{11,10},{9,8... | collective-permute-start | bytes 2359304 | tf_op jit(solution)/shard_map/ppermute | solution.py:781
  476.2 382.2 %reduce-scatter.6.cloned.1.call-start = ((), (), s32[]{:S(2)}) async-start(), calls=%async_computation.5 | async-start | bytes 7077888 | tf_op jit(solution)/shard_map/reduce_scatter | solution.py:843
  527.0 63.3 %collective-permute-start.65 = (bf16[256,384]{1,0:T(8,128)(2,1)S(1)}, bf16[256,384]{1,0:T(8,128)(2,1)}, u32[]{:S(2)}, u32[]{:S(2)}) collective-permute-start(bf16[256,384]{1,0:T(8,128)(2,1)S(1)} %collective-permute-done.64.refs_13_), channel_id=1, source_target_pairs={{0,4},{4,0},{8,12},{12,8},{16,20},{20,16},{24,28},{28,24},{1,5},{5... | collective-permute-start | bytes 589832 | tf_op jit(solution)/shard_map/ppermute | solution.py:680
  527.0 63.3 %collective-permute-start.56 = (bf16[256,384]{1,0:T(8,128)(2,1)S(1)}, bf16[256,384]{1,0:T(8,128)(2,1)}, u32[]{:S(2)}, u32[]{:S(2)}) collective-permute-start(bf16[256,384]{1,0:T(8,128)(2,1)S(1)} %collective-permute-done.55.refs_3_), channel_id=1, source_target_pairs={{0,4},{4,0},{8,12},{12,8},{16,20},{20,16},{24,28},{28,24},{1,5},{5... | collective-permute-start | bytes 589832 | tf_op jit(solution)/shard_map/ppermute | solution.py:680
  532.2 58.1 %collective-permute-start.58 = (bf16[256,384]{1,0:T(8,128)(2,1)S(1)}, bf16[256,384]{1,0:T(8,128)(2,1)}, u32[]{:S(2)}, u32[]{:S(2)}) collective-permute-start(bf16[256,384]{1,0:T(8,128)(2,1)S(1)} %collective-permute-done.57.refs_5_), channel_id=1, source_target_pairs={{0,4},{4,0},{8,12},{12,8},{16,20},{20,16},{24,28},{28,24},{1,5},{5... | collective-permute-start | bytes 589832 | tf_op jit(solution)/shard_map/ppermute | solution.py:680
  532.2 58.1 %collective-permute-start.67 = (bf16[256,384]{1,0:T(8,128)(2,1)}, bf16[256,384]{1,0:T(8,128)(2,1)}, u32[]{:S(2)}, u32[]{:S(2)}) collective-permute-start(bf16[256,384]{1,0:T(8,128)(2,1)} %collective-permute-done.66.refs_15_), channel_id=1, source_target_pairs={{0,4},{4,0},{8,12},{12,8},{16,20},{20,16},{24,28},{28,24},{1,5},{5... | collective-permute-start | bytes 589832 | tf_op jit(solution)/shard_map/ppermute | solution.py:680
  535.2 55.1 %collective-permute-start.60 = (bf16[256,384]{1,0:T(8,128)(2,1)}, bf16[256,384]{1,0:T(8,128)(2,1)}, u32[]{:S(2)}, u32[]{:S(2)}) collective-permute-start(bf16[256,384]{1,0:T(8,128)(2,1)} %collective-permute-done.59.refs_7_), channel_id=1, source_target_pairs={{0,4},{4,0},{8,12},{12,8},{16,20},{20,16},{24,28},{28,24},{1,5},{5... | collective-permute-start | bytes 589832 | tf_op jit(solution)/shard_map/ppermute | solution.py:680
  604.7 354.8 %reduce-scatter.8.cloned.1.call-start = ((), (), s32[]{:S(2)}) async-start(), calls=%async_computation.6 | async-start | bytes 5308416 | tf_op jit(solution)/shard_map/reduce_scatter | solution.py:843
  623.5 22.7 %collective-permute-start.75 = (bf16[256,512]{1,0:T(8,128)(2,1)S(1)}, bf16[256,512]{1,0:T(8,128)(2,1)S(1)}, u32[]{:S(2)}, u32[]{:S(2)}) collective-permute-start(bf16[256,512]{1,0:T(8,128)(2,1)S(1)} %collective-permute-done.74.refs_7_), channel_id=1, source_target_pairs={{0,4},{4,0},{8,12},{12,8},{16,20},{20,16},{24,28},{28,24},{1,5},{5... | collective-permute-start | bytes 786440 | tf_op jit(solution)/shard_map/ppermute | solution.py:680
  632.6 19.4 %collective-permute-start.76 = (bf16[256,512]{1,0:T(8,128)(2,1)S(1)}, bf16[256,512]{1,0:T(8,128)(2,1)S(1)}, u32[]{:S(2)}, u32[]{:S(2)}) collective-permute-start(bf16[256,512]{1,0:T(8,128)(2,1)S(1)} %copy-done.11), channel_id=1, source_target_pairs={{0,4},{4,0},{8,12},{12,8},{16,20},{20,16},{24,28},{28,24},{1,5},{5... | collective-permute-start | bytes 786440 | tf_op jit(solution)/shard_map/ppermute | solution.py:680
  632.8 27.6 %collective-permute-start.80 = (bf16[256,512]{1,0:T(8,128)(2,1)S(1)}, bf16[256,512]{1,0:T(8,128)(2,1)S(1)}, u32[]{:S(2)}, u32[]{:S(2)}) collective-permute-start(bf16[256,512]{1,0:T(8,128)(2,1)S(1)} %collective-permute-done.79.refs_13_), channel_id=1, source_target_pairs={{0,4},{4,0},{8,12},{12,8},{16,20},{20,16},{24,28},{28,24},{1,5},{5... | collective-permute-start | bytes 786440 | tf_op jit(solution)/shard_map/ppermute | solution.py:680
  660.4 20.4 %collective-permute-start.93 = (bf16[256,512]{1,0:T(8,128)(2,1)S(1)}, bf16[256,512]{1,0:T(8,128)(2,1)S(1)}, u32[]{:S(2)}, u32[]{:S(2)}) collective-permute-start(bf16[256,512]{1,0:T(8,128)(2,1)S(1)} %copy-done.12), channel_id=1, source_target_pairs={{0,16},{4,20},{8,24},{12,28},{16,0},{20,4},{24,8},{28,12},{1,17},{... | collective-permute-start | bytes 786440 | tf_op jit(solution)/shard_map/ppermute | solution.py:680
  663.8 54.0 %collective-permute-start.68 = (bf16[256,1536]{1,0:T(8,128)(2,1)S(1)}, bf16[256,1536]{1,0:T(8,128)(2,1)}, u32[]{:S(2)}, u32[]{:S(2)}) collective-permute-start(bf16[256,1536]{1,0:T(8,128)(2,1)S(1)} %get-tuple-element.428.refs_2_), channel_id=1, source_target_pairs={{0,1},{3,2},{1,0},{2,3},{4,5},{7,6},{5,4},{6,7},{8,9},{11,10},{9,8... | collective-permute-start | bytes 2359304 | tf_op jit(solution)/shard_map/ppermute | solution.py:781
  720.4 24.1 %collective-permute-start.97 = (bf16[256,1536]{1,0:T(8,128)(2,1)}, bf16[256,1536]{1,0:T(8,128)(2,1)S(1)}, u32[]{:S(2)}, u32[]{:S(2)}) collective-permute-start(bf16[256,1536]{1,0:T(8,128)(2,1)} %get-tuple-element.307), channel_id=1, source_target_pairs={{0,1},{3,2},{1,0},{2,3},{4,5},{7,6},{5,4},{6,7},{8,9},{11,10},{9,8... | collective-permute-start | bytes 2359304 | tf_op jit(solution)/shard_map/ppermute | solution.py:781
  722.1 22.5 %collective-permute-start.98 = (bf16[256,1536]{1,0:T(8,128)(2,1)}, bf16[256,1536]{1,0:T(8,128)(2,1)S(1)}, u32[]{:S(2)}, u32[]{:S(2)}) collective-permute-start(bf16[256,1536]{1,0:T(8,128)(2,1)} %get-tuple-element.308.refs_12_.refs_3_), channel_id=1, source_target_pairs={{1,2},{2,1},{5,6},{6,5},{9,10},{10,9},{13,14},{14,13},{17,18},{18,... | collective-permute-start | bytes 2359304 | tf_op jit(solution)/shard_map/ppermute | solution.py:781
  748.7 37.7 %collective-permute-start.100 = (bf16[256,1536]{1,0:T(8,128)(2,1)}, bf16[256,1536]{1,0:T(8,128)(2,1)S(1)}, u32[]{:S(2)}, u32[]{:S(2)}) collective-permute-start(bf16[256,1536]{1,0:T(8,128)(2,1)} %get-tuple-element.311.refs_12_.refs_4_), channel_id=1, source_target_pairs={{1,2},{2,1},{5,6},{6,5},{9,10},{10,9},{13,14},{14,13},{17,18},{18,... | collective-permute-start | bytes 2359304 | tf_op jit(solution)/shard_map/ppermute | solution.py:781
  749.6 36.8 %collective-permute-start.99 = (bf16[256,1536]{1,0:T(8,128)(2,1)}, bf16[256,1536]{1,0:T(8,128)(2,1)}, u32[]{:S(2)}, u32[]{:S(2)}) collective-permute-start(bf16[256,1536]{1,0:T(8,128)(2,1)} %get-tuple-element.310.refs_2_), channel_id=1, source_target_pairs={{0,1},{3,2},{1,0},{2,3},{4,5},{7,6},{5,4},{6,7},{8,9},{11,10},{9,8... | collective-permute-start | bytes 2359304 | tf_op jit(solution)/shard_map/ppermute | solution.py:781
  790.8 19.3 %collective-permute-start.101 = (bf16[256,1536]{1,0:T(8,128)(2,1)}, bf16[256,1536]{1,0:T(8,128)(2,1)S(1)}, u32[]{:S(2)}, u32[]{:S(2)}) collective-permute-start(bf16[256,1536]{1,0:T(8,128)(2,1)} %get-tuple-element.319.refs_2_), channel_id=1, source_target_pairs={{0,1},{3,2},{1,0},{2,3},{4,5},{7,6},{5,4},{6,7},{8,9},{11,10},{9,8... | collective-permute-start | bytes 2359304 | tf_op jit(solution)/shard_map/ppermute | solution.py:781
  790.8 19.3 %collective-permute-start.102 = (bf16[256,1536]{1,0:T(8,128)(2,1)}, bf16[256,1536]{1,0:T(8,128)(2,1)S(1)}, u32[]{:S(2)}, u32[]{:S(2)}) collective-permute-start(bf16[256,1536]{1,0:T(8,128)(2,1)} %get-tuple-element.320.refs_4_), channel_id=1, source_target_pairs={{1,2},{2,1},{5,6},{6,5},{9,10},{10,9},{13,14},{14,13},{17,18},{18,... | collective-permute-start | bytes 2359304 | tf_op jit(solution)/shard_map/ppermute | solution.py:781
  814.9 19.8 %collective-permute-start.103 = (bf16[256,1536]{1,0:T(8,128)(2,1)}, bf16[256,1536]{1,0:T(8,128)(2,1)S(1)}, u32[]{:S(2)}, u32[]{:S(2)}) collective-permute-start(bf16[256,1536]{1,0:T(8,128)(2,1)} %get-tuple-element.324.refs_2_), channel_id=1, source_target_pairs={{0,1},{3,2},{1,0},{2,3},{4,5},{7,6},{5,4},{6,7},{8,9},{11,10},{9,8... | collective-permute-start | bytes 2359304 | tf_op jit(solution)/shard_map/ppermute | solution.py:781
  924.2 20.4 %collective-permute-start.122 = (f32[8,128]{1,0:T(8,128)S(1)}, f32[8,128]{1,0:T(8,128)S(1)}, u32[]{:S(2)}, u32[]{:S(2)}) collective-permute-start(f32[8,128]{1,0:T(8,128)S(1)} %bitcast.141), channel_id=1, source_target_pairs={{0,1},{1,0},{2,3},{3,2},{4,5},{5,4},{6,7},{7,6},{8,9},{9,8},{10,11... | collective-permute-start | bytes 12296 | tf_op jit(solution)/shard_map/ppermute | solution.py:680
  (224 other events, 2764.7 us)
Sparse Core Ops, SparseCore 0:
  133.6 45.7 all-gather.1
  476.3 86.3 reduce-scatter.3
  604.8 79.0 reduce-scatter.5
  857.1 55.6 reduce-scatter.7

commit v5 on v4

--- a/solution.py
+++ b/solution.py
@@ -136,38 +136,59 @@
     return jnp.concatenate([t] * (n // t.shape[1]), 1)
 
 
-def qkv_kernel(p_ref, v_ref, w_ref, c_ref, s1_ref, s2_ref, hg_ref, a_ref, qr_ref, kr_ref, q_ref, k_ref, vv_ref):
+def key_kernel(p_ref, v_ref, w_ref, c_ref, s1_ref, s2_ref, hg_ref, a_ref, kr_ref, k_ref):
     x = p_ref[...].astype(f32)
     a = (x * inv_rms(x) * row(v_ref, 0)).astype(bf16)
     a_ref[...] = a
-    n = q_ref.shape[1]
-    ones = head_ones(n)
-    cos, s1, s2 = (tile3(t[...], n) for t in (c_ref, s1_ref, s2_ref))
-
-    def turned(y, gain):
-        z = y * lax.rsqrt(head_sum(y * y, ones) * (1.0 / HD) + EPS) * gain
-        return z * cos + pltpu.roll(z, n - 16, 1) * s1 + pltpu.roll(z, 16, 1) * s2
-
-    q = mm(a, w_ref[0])
+    k = mm(a, w_ref[0])
+    kr_ref[...] = k
+    k_ref[...] = turned(k, row(hg_ref, 1), (c_ref, s1_ref, s2_ref)).astype(bf16)
+
+
+def turned(y, gain, tabs):
+    n = y.shape[1]
+    cos, s1, s2 = (tile3(t[...], n) for t in tabs)
+    z = y * lax.rsqrt(head_sum(y * y, head_ones(n)) * (1.0 / HD) + EPS) * gain
+    return z * cos + pltpu.roll(z, n - 16, 1) * s1 + pltpu.roll(z, 16, 1) * s2
+
+
+def query_kernel(a_ref, wq_ref, wv_ref, c_ref, s1_ref, s2_ref, hg_ref, qr_ref, q_ref, v_ref):
+    a = a_ref[...]
+    v_ref[...] = mm(a, wv_ref[0]).astype(bf16)
+    q = mm(a, wq_ref[0])
     qr_ref[...] = q
-    q_ref[...] = (turned(q, row(hg_ref, 0)) * (0.125 * LOG2E)).astype(bf16)
-    k = mm(a, w_ref[1])
-    kr_ref[...] = k
-    k_ref[...] = turned(k, row(hg_ref, 1)).astype(bf16)
-    vv_ref[...] = mm(a, w_ref[2]).astype(bf16)
-
-
-def qkv_call(order, patches, vec, w, tabs, hg, br=256):
+    q_ref[...] = (turned(q, row(hg_ref, 0), (c_ref, s1_ref, s2_ref)) * (0.125 * LOG2E)).astype(bf16)
+
+
+def one_weight(w, k):
+    return pl.BlockSpec((1, *w.shape[1:]), lambda *_: (k, 0, 0), pipeline_mode=pl.Buffered(1))
+
+
+def key_call(order, patches, vec, w, tabs, hg, br=256):
     t, d = patches.shape
     n = w.shape[2]
     return order.run(
-        "qkv",
-        qkv_kernel,
+        "key",
+        key_kernel,
         (t // br,),
         (patches, vec, w, *tabs, hg),
-        [rows_of(br, d), whole(vec.shape), whole(w.shape)] + [rows_of(br, 128)] * 3 + [whole(hg.shape)],
-        [rows_of(br, d)] + [rows_of(br, n)] * 5,
-        [sds((t, d), bf16), sds((t, n), f32), sds((t, n), f32)] + [sds((t, n), bf16)] * 3,
+        [rows_of(br, d), whole(vec.shape), one_weight(w, 1)] + [rows_of(br, 128)] * 3 + [whole(hg.shape)],
+        [rows_of(br, d)] + [rows_of(br, n)] * 2,
+        [sds((t, d), bf16), sds((t, n), f32), sds((t, n), bf16)],
+    )
+
+
+def query_call(order, a, w, tabs, hg, br=256):
+    t, d = a.shape
+    n = w.shape[2]
+    return order.run(
+        "query",
+        query_kernel,
+        (t // br,),
+        (a, w, w, *tabs, hg),
+        [rows_of(br, d), one_weight(w, 0), one_weight(w, 2)] + [rows_of(br, 128)] * 3 + [whole(hg.shape)],
+        [rows_of(br, n)] * 3,
+        [sds((t, n), f32), sds((t, n), bf16), sds((t, n), bf16)],
     )
 
 
@@ -214,25 +235,24 @@
         li_ref[...] = li
 
 
-def attend_call(order, sc, q, k, v, ck, cv, tg, h):
+def attend_call(order, sc, q, k, v, cap, tg, at, bq):
     n = q.shape[1]
     pairs = n // 128
     block = k.shape[0] // SPAN
-    bq = 2 * BR
-    text = ck.shape[0]
+    text = cap.shape[0]
     mine = lambda p, j, s: (0, p)
     other = lambda p, j, s: (item_block(j, s), p)
     return order.run(
         "attend",
         attend_kernel,
         (pairs, SPAN),
-        (q, k, v, ck, cv, tg),
+        (q, k, v, cap, cap, tg),
         [
-            pl.BlockSpec((bq, 128), lambda p, j, s: (h, p)),
+            pl.BlockSpec((bq, 128), lambda p, j, s: (at, p)),
             pl.BlockSpec((block, 128), other),
             pl.BlockSpec((block, 128), other),
             pl.BlockSpec((text, 128), mine),
-            pl.BlockSpec((text, 128), mine),
+            pl.BlockSpec((text, 128), lambda p, j, s: (0, pairs + p)),
             pl.BlockSpec((1, 128), mine),
         ],
         [pl.BlockSpec((bq, 128), mine)] * 3,
@@ -267,23 +287,23 @@
     gs_ref[...] = jnp.where(masks[0], sums[0], sums[1])
 
 
-def caption_back_call(order, q, da, db, ck, cv, tg, h):
+def caption_back_call(order, q, da, db, cap, tg, h):
     n = q.shape[1]
     pairs = n // 128
     bq = 2 * BR
-    text = ck.shape[0]
+    text = cap.shape[0]
     mine = lambda p: (0, p)
     return order.run(
         "caption_back",
         caption_back_kernel,
         (pairs,),
-        (q, da, db, ck, cv, tg),
+        (q, da, db, cap, cap, tg),
         [
             pl.BlockSpec((bq, 128), lambda p: (h, p)),
             pl.BlockSpec((BR, 128), mine),
             pl.BlockSpec((BR, 128), mine),
             pl.BlockSpec((text, 128), mine),
-            pl.BlockSpec((text, 128), mine),
+            pl.BlockSpec((text, 128), lambda p: (0, pairs + p)),
             pl.BlockSpec((1, 128), mine),
         ],
         [
@@ -333,7 +353,7 @@
         dq_ref[...] = acc[...] * 0.125 + c_ref[...]
 
 
-def dq_call(order, sc, q, da, db, k, v, cap_dq, h):
+def dq_call(order, sc, q, da, db, k, v, cap_dq, h, after=()):
     n = q.shape[1]
     pairs = n // 128
     block = k.shape[0] // SPAN
@@ -360,6 +380,7 @@
         [sds((bq, n), f32)],
         [pltpu.VMEM((bq, 128), f32)],
         sc,
+        after=after,
     )[0]
 
 
@@ -446,7 +467,7 @@
     o_ref[:, n:] = mm_tn(c_ref[...], d_ref[...]).astype(bf16)
 
 
-def pair_grad_call(order, a, b, c, d, part=0, parts=1, before=()):
+def pair_grad_call(order, a, b, c, d, part=0, parts=1, before=(), after=()):
     t, m = a.shape
     n, k = b.shape[1], d.shape[1]
     blk = 256
@@ -461,6 +482,7 @@
         [pl.BlockSpec((blk, n + k), lambda i: (part * steps + i, 0))],
         [sds((m, n + k), bf16)],
         held=before,
+        after=after,
     )
 
 
@@ -569,7 +591,7 @@
     ds_ref[:, n:] = jnp.where(which == 0, one, jnp.where(which == 1, two, delta - one - two)).astype(bf16)
 
 
-def out_back_call(order, c, da, mid, at, cot, vec, w, o, li, before):
+def out_back_call(order, c, da, mid, at, cot, vec, w, o, li, place, before):
     t, d = cot.shape
     n = w.shape[0]
     return chunk_call(
@@ -578,7 +600,7 @@
         "out_back",
         c,
         (da, mid, at, cot, vec, w, o, li),
-        [alone(d), alone(d), alone(d), part(c, d), whole(vec.shape), whole(w.shape), part(c % 2, n), part(c % 2, n)],
+        [alone(d), alone(d), alone(d), part(c, d), whole(vec.shape), whole(w.shape), part(place, n), part(place, n)],
         [(BR, d, f32), (BR, n, bf16), (BR, n + 128, bf16)],
         [(1, d, f32), (1, d, f32)],
         [(t, d, bf16)],
@@ -669,11 +691,12 @@
     hs_ref[...] = col_sum(dy * xh)
 
 
-def caption_norm_kernel(kr_ref, v_ref, hg_ref, k_ref, o_ref):
+def caption_norm_kernel(kr_ref, v_ref, hg_ref, o_ref):
+    n = kr_ref.shape[1]
     x = kr_ref[...]
-    r = lax.rsqrt(head_sum(x * x, head_ones(x.shape[1])) * (1.0 / HD) + EPS)
-    k_ref[...] = (x * r * row(hg_ref, 2)).astype(bf16)
-    o_ref[...] = v_ref[...].astype(bf16)
+    r = lax.rsqrt(head_sum(x * x, head_ones(n)) * (1.0 / HD) + EPS)
+    o_ref[:, :n] = (x * r * row(hg_ref, 2)).astype(bf16)
+    o_ref[:, n:] = v_ref[...].astype(bf16)
 
 
 def swap(x, axis, size, m):
@@ -697,19 +720,32 @@
             pltpu.make_async_copy(pieces[0], out.at[pl.ds(j * rows, rows)], sem.at[k, j]).wait()
 
 
-def gather_item(a, b):
+class Gather:
+    def __init__(self, a, b):
+        self.all = None
+        if lax.axis_size("wide") != 8:
+            self.first = self.second = ()
+            self.all = [lax.all_gather(x, "wide") for x in (a, b)]
+            return
+        send = lambda x, pairs: lax.ppermute(x, "wide", pairs)
+        over_x = [(i, i ^ 2) for i in range(8)]
+        over_y = [(1, 5), (4, 0), (3, 7), (6, 2)]
+        a2, a4, b4, b2 = send(a, over_x), send(a, over_y), send(b, over_y), send(b, over_x)
+        a6 = send(a2, [(0, 4), (1, 5), (6, 2), (7, 3)])
+        b6x, b6y = send(b2, [(0, 4), (7, 3)]), send(b4, [(7, 5), (0, 2)])
+        self.first = (a2, a4, b4, b2)
+        self.second = (a6, b6x, b6y)
+        self.kept = ((a, a2, a4, a6), (b, b2, b4, b6x + b6y))
+
+    def pieces(self):
+        if self.all is not None:
+            return self.all
+        return [y for four in self.kept for x in four for y in (x, swap(x, "wide", 8, 1))]
+
+
+def shift(x, by):
     size = lax.axis_size("wide")
-    if size != 8:
-        return [lax.all_gather(x, "wide") for x in (a, b)]
-    go = lambda x, m: swap(x, "wide", 8, m)
-    a2, b4 = go(a, 2), go(b, 4)
-    a4, b2 = go(a, 4), go(b, 2)
-    a6, b6 = go(a2, 4), go(b4, 2)
-    pieces = []
-    for four in ((a, a2, a4, a6), (b, b2, b4, b6)):
-        for x in four:
-            pieces += [x, go(x, 1)]
-    return pieces
+    return lax.ppermute(x, "wide", [(i, i + by) for i in range(size) if 0 <= i + by < size])
 
 
 def pick(order, sc, pieces, count):
@@ -795,11 +831,11 @@
         if new is not None or self.second is not None:
             outs.append("send")
         like = ins["r1"]
-        block = pl.BlockSpec((BR // 2, like.shape[1]), lambda i, s: (i, 0))
+        block = pl.BlockSpec((BR // 4, like.shape[1]), lambda i, s: (i, 0))
         got = self.order.run(
             "hop",
             functools.partial(hop_kernel, {"in": list(ins), "out": outs}),
-            (2,),
+            (4,),
             list(ins.values()),
             [block] * len(ins),
             [block] * len(outs),
@@ -924,35 +960,41 @@
     tg = jnp.repeat(tg_heads, HD)[None, :]
 
     order = Order()
+    chunks = range(t // BR)
+    pairs_of = range(t // (2 * BR))
+    sums = Sums(order, deep, mz)
+    a1, k_raw, k = key_call(order, patches, vec, w_qkv, tabs, hg)
+    q_raw, q, v = query_call(order, a1, w_qkv, tabs, hg)
+    kv = Gather(k, v)
+
     cap_raw = jnp.einsum("kd,jde->jke", captions, w_caption, preferred_element_type=f32)
     whole_cap = pl.BlockSpec((text, n), lambda i: (0, 0))
-    cap_own = order.run(
+    both_cap = pl.BlockSpec((text, 2 * n), lambda i: (0, 0))
+    (cap,) = order.run(
         "caption_norm",
         caption_norm_kernel,
         (1,),
         (cap_raw[0], cap_raw[1], hg),
         [whole_cap, whole_cap, whole(hg.shape)],
-        [whole_cap, whole_cap],
-        [sds((text, n), bf16)] * 2,
-    )
-    cap_pieces = gather_item(*cap_own)
-
-    chunks = range(t // BR)
-    pairs_of = range(t // (2 * BR))
-    sums = Sums(order, deep, mz)
-    a1, q_raw, k_raw, q, k, v = qkv_call(order, patches, vec, w_qkv, tabs, hg)
-    kv_pieces = gather_item(k, v)
+        [both_cap],
+        [sds((text, 2 * n), bf16)],
+    )
+    offset = me - first
+    cap = jnp.where(offset == 1, shift(cap, 1), cap)
+    cap = jnp.where(offset >= 2, shift(cap, 2), cap)
+
     q_all = lax.all_gather(q, "wide", axis=0, tiled=True)
-    ck, cv = pick(order, sc, cap_pieces, 1)
-    k_all, v_all = pick(order, sc, kv_pieces, SPAN)
+    k_all, v_all = pick(order, sc, kv.pieces(), SPAN)
     heads_out = {}
-    for h in pairs_of:
-        heads_out[h] = attend_call(order, sc, q, k_all, v_all, ck, cv, tg, h)
-        if h == 0:
-            sums.add(("attn", 0), mm(heads_out[0][0][:BR], w_out).astype(bf16))
-    for c in chunks[1:]:
-        at = (c % 2) * BR
-        sums.add(("attn", c), mm(heads_out[c // 2][0][at : at + BR], w_out).astype(bf16))
+    for c in chunks[: len(chunks) // 2]:
+        heads_out[c] = (*attend_call(order, sc, q, k_all, v_all, cap, tg, c, BR), 0)
+        sums.add(("attn", c), mm(heads_out[c][0], w_out).astype(bf16))
+    half = (len(chunks) + 1) // 2
+    later = attend_call(order, sc, q, k_all, v_all, cap, tg, 1, half * BR)
+    for c in chunks[half:]:
+        heads_out[c] = (*later, c - half)
+        at = (c - half) * BR
+        sums.add(("attn", c), mm(later[0][at : at + BR], w_out).astype(bf16))
 
     mids, gus = {}, {}
     whole_out = ()
@@ -972,39 +1014,49 @@
         c4 = c4 + part_sum
     output, d_ffn, d_gu = whole_out
 
-    d_mids, dqs, dq_caps, d_pieces, d_mixed, d_scaled = {}, {}, {}, {}, {}, {}
+    d_mids, dqs, dq_caps, d_got, d_mixed, d_scaled = {}, {}, {}, {}, {}, {}
     whole_out = ()
     mlp_part = ()
+    behind = ()
     c2 = c3 = dck = dcv = gate_sum = 0.0
     for h in pairs_of:
-        mixed, o_self, linv = heads_out[h]
         for c in (2 * h, 2 * h + 1):
+            _, o_self, linv, place = heads_out[c]
+            if c == 2 * h + 1 and h > 0:
+                behind = d_got[h - 1].second
+            da3 = sums.get(("da3", c), behind)
             d_mids[c], d_mixed[c], d_scaled[c], p3, p2, *whole_out = out_back_call(
-                order, c, sums.get(("da3", c)), mids[c], sums.get(("attn", c)), cotangent, vec, w_out, o_self, linv, whole_out
+                order, c, da3, mids[c], sums.get(("attn", c)), cotangent, vec, w_out, o_self, linv, place, whole_out
             )
             c2, c3 = c2 + p2, c3 + p3
-            if c % 2 == 0:
-                mlp_part = pair_grad_call(order, a3, d_gu, d_ffn, hidden, h, len(pairs_of), mlp_part)
-        d_pieces[h] = gather_item(d_scaled[2 * h], d_scaled[2 * h + 1])
-        dq_caps[h], pk, pv, pg = caption_back_call(order, q, d_mixed[2 * h], d_mixed[2 * h + 1], ck, cv, tg, h)
+            behind = ()
+            if c == 2 * h:
+                early = d_got[h - 1].first if h > 0 else ()
+                mlp_part = pair_grad_call(order, a3, d_gu, d_ffn, hidden, h, len(pairs_of), mlp_part, early)
+        d_got[h] = Gather(d_scaled[2 * h], d_scaled[2 * h + 1])
+        dq_caps[h], pk, pv, pg = caption_back_call(order, q, d_mixed[2 * h], d_mixed[2 * h + 1], cap, tg, h)
         dck, dcv, gate_sum = dck + pk, dcv + pv, gate_sum + pg
     (d_attn,) = whole_out
     g_mlp = scatter_rows(mlp_part[0])
-    back_pieces = gather_item(dck.astype(bf16), dcv.astype(bf16))
+    cap_sum = jnp.concatenate([dck, dcv], 1)
+    got_two = shift(cap_sum.astype(bf16), -2)
+    cap_sum = cap_sum + jnp.where(offset + 2 < length, got_two.astype(f32), 0.0)
+    got_one = shift(cap_sum.astype(bf16), -1)
+    cap_sum = jnp.where(offset == 0, cap_sum + jnp.where(offset + 1 < length, got_one.astype(f32), 0.0), 0.0)
+    last_half = pairs_of[-1]
     for h in pairs_of:
-        dqs[h] = dq_call(order, sc, q, d_scaled[2 * h], d_scaled[2 * h + 1], k_all, v_all, dq_caps[h], h)
-
-    kept = (jnp.arange(SPAN) < length) & (first == me)
-    in_slot = lambda x: jnp.sum(jnp.where(kept[:, None, None], x.reshape(SPAN, text, n).astype(f32), 0.0), 0)
-    got_k, got_v = pick(order, sc, back_pieces, SPAN)
+        after = () if h == 0 else (*d_got[last_half].first, got_two)
+        dqs[h] = dq_call(order, sc, q, d_scaled[2 * h], d_scaled[2 * h + 1], k_all, v_all, dq_caps[h], h, after)
+
     d_cap, hs_c = order.run(
         "caption_grad",
         caption_grad_kernel,
         (1,),
-        (in_slot(got_k), in_slot(got_v), cap_raw[0], hg),
+        (cap_sum[:, :n], cap_sum[:, n:], cap_raw[0], hg),
         [whole_cap, whole_cap, whole_cap, whole(hg.shape)],
-        [pl.BlockSpec((text, 2 * n), lambda i: (0, 0)), pl.BlockSpec((1, n), lambda i: (0, 0))],
+        [both_cap, pl.BlockSpec((1, n), lambda i: (0, 0))],
         [sds((text, 2 * n), bf16), sds((1, n), f32)],
+        after=d_got[last_half].second,
     )
     d_text = (mm_nt(d_cap[:, :n], w_caption[0]) + mm_nt(d_cap[:, n:], w_caption[1])).astype(bf16)
     cap_part = mm_tn(captions, d_cap).astype(bf16)
@@ -1013,7 +1065,7 @@
     padded = jnp.pad(d_text, ((0, 0), (0, pieces * d - d_text.shape[1])))
     text_parts = [padded[:, p * d : (p + 1) * d] for p in range(pieces)]
 
-    ds = [x for h in pairs_of for x in pick(order, sc, d_pieces[h], SPAN)]
+    ds = [x for h in pairs_of for x in pick(order, sc, d_got[h].pieces(), SPAN)]
     sums.add(("text", 0), text_parts[0])
     dkv = []
     for p in range(n // 128):
@@ -1024,7 +1076,7 @@
         sums.add(("text", p), text_parts[p])
     whole_out = ()
     c1 = hs_qk = 0.0
-    mixed = jnp.concatenate([heads_out[h][0] for h in pairs_of])
+    mixed = jnp.concatenate([heads_out[c][0] for c in chunks[:half]] + [later[0]])
     for c in chunks:
         da1_part, p_hs, p1, *whole_out = dqkv_call(order, c, dqs[c // 2], dkv, q_raw, k_raw, tabs, hg, w_qkv, patches, whole_out)
         if c == chunks[-1]:

time: 988 us -> 1000 us (1.012)
  waiting for transfers between devices: 233 us -> 164 us
  Pallas kernels: 452 us -> 486 us
  starting transfers between devices: 135 us -> 160 us
  other arithmetic: 39.6 us -> 51.1 us
    ppermute x83 -> x37, waiting for transfers between devices: 129 us -> 8.19 us  [swap(): return lax.ppermute(x, axis, [(i, i ^ m) for i in range(size)])]
    ppermute x0 -> x25, waiting for transfers between devices: none -> 75.4 us  [the longest x4 40.7 us: shift(): lax.ppermute(x, 'wide', [(i, i + by) for i in range(size) if 0 <= i + by...]
    ppermute x0 -> x25, starting transfers between devices: none -> 63.9 us  [the longest x21 52.7 us: __init__(): send = lambda x, pairs: lax.ppermute(x, 'wide', pairs)]
    ppermute x83 -> x37, starting transfers between devices: 56.8 us -> 20.4 us  [swap(): return lax.ppermute(x, axis, [(i, i ^ m) for i in range(size)])]
    pallas_call x63, Pallas kernels: 452 us -> 486 us  [run(): pl.pallas_call(body, grid_spec=pltpu.PrefetchScalarGridSpec(num_scalar_pr...]
    ppermute x42, waiting for transfers between devices: 104 us -> 80.5 us  [step(): go = lambda x, perm: lax.ppermute(x, 'narrow', perm)]
    unnamed x300 -> x258, local copies, waits for them, and re-layouts: 32 us -> 36.1 us
  transfers between devices with their start and end apart: 129 -> 108, of which waited for: 44 -> 30; matrix products, arithmetic and copies ran while one was open for 7% -> 7% of each run, Pallas kernels for 46% -> 48%
where the time goes in v5:
time: 1000 us; the launch traced here: 983 us
  Pallas kernels  486 us (49%)
  waiting for transfers between devices  164 us (16%)
  starting transfers between devices  160 us (16%)
  other arithmetic  51.1 us (5%)
  local copies, waits for them, and re-layouts  49 us (5%)
  matrix products  26.3 us (3%)
  blocking collectives  24.1 us (2%)
  between operations  22.4 us (2%)
    pallas_call x63, Pallas kernels, run(): pl.pallas_call(body, grid_spec=pltpu.PrefetchScalarGridSpec(num_scalar_pr...  486 us
    ppermute x42, waiting for transfers between devices, step(): go = lambda x, perm: lax.ppermute(x, 'narrow', perm)  80.5 us
    ppermute x42, starting transfers between devices, step(): go = lambda x, perm: lax.ppermute(x, 'narrow', perm)  75 us
    ppermute x21, starting transfers between devices, __init__(): send = lambda x, pairs: lax.ppermute(x, 'wide', pairs)  52.7 us
    ppermute x4, waiting for transfers between devices, shift(): lax.ppermute(x, 'wide', [(i, i + by) for i in range(size) if 0 <= i + by...  40.7 us
    unnamed x258, local copies, waits for them, and re-layouts  36.1 us
    ppermute x21, waiting for transfers between devices, __init__(): send = lambda x, pairs: lax.ppermute(x, 'wide', pairs)  34.7 us
    all_gather x2, blocking collectives, gather_now(): lax.all_gather(padded, axis, axis=0, tiled=True).reshape(-1, wide)[:, :n]  24.1 us
  transfers between devices with their start and end apart: 108, of which 30 were waited for; matrix products, arithmetic and copies ran while one was open for 7% of the time, Pallas kernels for 48%

profile of v5, /device:TPU:0, one launch (start us, length us, event | category | flops | bytes accessed | tf_op | source)
XLA Modules:
  0.0 983.1 jit_solution(10057454228783467279)
XLA Ops:
  20.1 14.8 %all_gather.9 = f32[4,8,256]{2,1,0:T(8,128)S(1)} all-gather(f32[1,8,256]{2,1,0:T(8,128)S(1)} %reshape.346), channel_id=1, replica_groups=mesh['wide'=8,'narrow'=4] {'narrow'}, dimensions={0}, use_global_device_ids=true | all-gather | bytes 40960 | tf_op jit(solution)/shard_map/all_gather | solution.py:787
  35.0 9.3 all_gather.10
  51.3 7.8 key.1
  59.2 8.7 query.1
  100.4 24.4 %collective-permute-done.16 = bf16[256,768]{1,0:T(8,128)(2,1)S(1)} collective-permute-done((bf16[256,768]{1,0:T(8,128)(2,1)S(1)}, bf16[256,768]{1,0:T(8,128)(2,1)S(1)}, u32[]{:S(2)}, u32[]{:S(2)}) %collective-permute-start.16) | collective-permute-done | bytes 393248 | tf_op jit(solution)/shard_map/ppermute | solution.py:748
  126.7 6.3 collective-permute-start.5
  141.1 8.3 collective-permute-done.5.refs_7_
  155.4 6.1 pick.3
  161.6 18.1 %attend.3 = (bf16[256,384]{1,0:T(8,128)(2,1)}, bf16[256,384]{1,0:T(8,128)(2,1)}, f32[256,384]{1,0:T(8,128)}) custom-call(s32[9]{0:T(128)} %pad_add_fusion.refs_0_, bf16[1024,384]{1,0:T(8,128)(2,1)} %get-tuple-element.188.refs_1_.refs_0_, bf16[4096,384]{1,0:T(8,128)(2,1)} %get-tuple-element.192.refs_2_.refs_7_.refs_6_, ...), custom_call_target="tpu_custom_call" | custom-call | tf_op jit(solution)/shard_map/attend/pallas_call | solution.py:45
  183.6 17.7 %attend.4 = (bf16[256,384]{1,0:T(8,128)(2,1)}, bf16[256,384]{1,0:T(8,128)(2,1)}, f32[256,384]{1,0:T(8,128)}) custom-call(s32[9]{0:T(128)} %pad_add_fusion.refs_0_, bf16[1024,384]{1,0:T(8,128)(2,1)} %get-tuple-element.188.refs_1_.refs_0_, bf16[4096,384]{1,0:T(8,128)(2,1)} %get-tuple-element.192.refs_2_.refs_7_.refs_6_, ...), custom_call_target="tpu_custom_call" | custom-call | tf_op jit(solution)/shard_map/attend/pallas_call | solution.py:45
  208.7 22.2 %attend.5 = (bf16[512,384]{1,0:T(8,128)(2,1)}, bf16[512,384]{1,0:T(8,128)(2,1)}, f32[512,384]{1,0:T(8,128)}) custom-call(s32[9]{0:T(128)} %pad_add_fusion.refs_0_, bf16[1024,384]{1,0:T(8,128)(2,1)} %get-tuple-element.188.refs_1_.refs_0_, bf16[4096,384]{1,0:T(8,128)(2,1)} %get-tuple-element.192.refs_2_.refs_7_.refs_6_, ...), custom_call_target="tpu_custom_call" | custom-call | tf_op jit(solution)/shard_map/attend/pallas_call | solution.py:45
  245.3 15.5 %collective-permute-done.20.refs_1_ = bf16[256,1536]{1,0:T(8,128)(2,1)S(1)} collective-permute-done((bf16[256,1536]{1,0:T(8,128)(2,1)}, bf16[256,1536]{1,0:T(8,128)(2,1)S(1)}, u32[]{:S(2)}, u32[]{:S(2)}) %collective-permute-start.20) | collective-permute-done | bytes 786464 | tf_op jit(solution)/shard_map/ppermute | solution.py:817
  270.5 8.5 ffn.4
  279.0 7.6 collective-permute-done.22.refs_1_
  296.8 8.5 ffn.5
  305.2 6.3 collective-permute-done.24.refs_1_
  321.2 8.5 ffn.6
  329.6 5.8 collective-permute-done.26.refs_1_
  345.2 8.5 ffn.7
  368.4 9.6 ffn_back.4
  390.3 9.6 ffn_back.5
  411.5 9.5 ffn_back.6
  432.0 9.6 ffn_back.7
  451.2 5.7 out_back.4
  457.0 9.9 %pair_grad.3.refs_6_.refs_9_ = bf16[1536,3072]{1,0:T(8,128)(2,1)} custom-call(bf16[1024,1536]{1,0:T(8,128)(2,1)} %get-tuple-element.263.refs_0_, bf16[1024,2048]{1,0:T(8,128)(2,1)} %get-tuple-element.264.refs_1_, bf16[1024,1536]{1,0:T(8,128)(2,1)} %get-tuple-element.265.refs_2_, bf16[1024,1024]{1,0:T(8,128)(2,1)} %get-tuple-element.266.refs_3_, ...), custom_call_target="tpu_custom_call" | custom-call | tf_op jit(solution)/shard_map/pair_grad/pallas_call | solution.py:45
  475.2 10.1 %collective-permute-start.43 = (bf16[256,512]{1,0:T(8,128)(2,1)S(1)}, bf16[256,512]{1,0:T(8,128)(2,1)S(1)}, u32[]{:S(2)}, u32[]{:S(2)}) collective-permute-start(bf16[256,512]{1,0:T(8,128)(2,1)S(1)} %copy-done.14), channel_id=1, source_target_pairs={{0,8},{4,12},{8,0},{12,4},{16,24},{20,28},{24,16},{28,20},{1,9},{5... | collective-permute-start | bytes 786440 | tf_op jit(solution)/shard_map/ppermute | solution.py:730
  486.6 5.8 out_back.5
  495.2 5.5 caption_back.2
  505.6 5.8 out_back.6
  512.3 9.9 %pair_grad.4.refs_3_ = bf16[1536,3072]{1,0:T(8,128)(2,1)} custom-call(bf16[1024,1536]{1,0:T(8,128)(2,1)} %get-tuple-element.263.refs_0_, bf16[1024,2048]{1,0:T(8,128)(2,1)} %get-tuple-element.264.refs_1_, bf16[1024,1536]{1,0:T(8,128)(2,1)} %get-tuple-element.265.refs_2_, ...), custom_call_target="tpu_custom_call", output_to_operand_aliasing={{}: (9, {})} | custom-call | tf_op jit(solution)/shard_map/pair_grad/pallas_call | solution.py:45
  541.2 5.9 out_back.7
  547.0 5.6 caption_back.3
  557.6 16.3 %collective-permute-done.50.refs_14_ = bf16[256,768]{1,0:T(8,128)(2,1)S(1)} collective-permute-done((bf16[256,768]{1,0:T(8,128)(2,1)}, bf16[256,768]{1,0:T(8,128)(2,1)S(1)}, u32[]{:S(2)}, u32[]{:S(2)}) %collective-permute-start.50) | collective-permute-done | bytes 393248 | tf_op jit(solution)/shard_map/ppermute | solution.py:748
  583.0 14.2 %collective-permute-done.52.refs_10_.refs_3_ = bf16[256,512]{1,0:T(8,128)(2,1)} collective-permute-done((bf16[256,512]{1,0:T(8,128)(2,1)S(1)}, bf16[256,512]{1,0:T(8,128)(2,1)}, u32[]{:S(2)}, u32[]{:S(2)}) %collective-permute-start.52) | collective-permute-done | bytes 262176 | tf_op jit(solution)/shard_map/ppermute | solution.py:730
  601.7 26.8 %dq.2.refs_9_.refs_0_ = f32[512,384]{1,0:T(8,128)} custom-call(s32[9]{0:T(128)} %pad_add_fusion.refs_0_, bf16[1024,384]{1,0:T(8,128)(2,1)} %get-tuple-element.188.refs_1_.refs_0_, bf16[256,512]{1,0:T(8,128)(2,1)} %get-tuple-element.285.refs_2_.refs_3_.refs_1_, bf16[256,512]{1,0:T(8,128)(2,1)} %get-tuple-element.285.refs_2_.refs_3_.refs_1_, ...), custom_call_target="tpu_custom_call" | custom-call | tf_op jit(solution)/shard_map/dq/pallas_call | solution.py:45
  631.5 26.8 %dq.3.refs_4_.refs_0_ = f32[512,384]{1,0:T(8,128)} custom-call(s32[9]{0:T(128)} %pad_add_fusion.refs_0_, bf16[1024,384]{1,0:T(8,128)(2,1)} %get-tuple-element.188.refs_1_.refs_0_, bf16[256,512]{1,0:T(8,128)(2,1)} %get-tuple-element.293.refs_2_.refs_3_.refs_1_, bf16[256,512]{1,0:T(8,128)(2,1)} %get-tuple-element.293.refs_2_.refs_3_.refs_1_, ...), custom_call_target="tpu_custom_call" | custom-call | tf_op jit(solution)/shard_map/dq/pallas_call | solution.py:45
  664.1 5.5 fusion.2.refs_5_
  694.8 21.7 %dkv.3 = (f32[1024,128]{1,0:T(8,128)}, f32[1024,128]{1,0:T(8,128)}) custom-call(s32[9]{0:T(128)} %pad_add_fusion.refs_0_, bf16[1024,384]{1,0:T(8,128)(2,1)} %get-tuple-element.189.refs_1_, bf16[1024,384]{1,0:T(8,128)(2,1)} %get-tuple-element.190.refs_9_.refs_2_, bf16[8192,384]{1,0:T(8,128)(2,1)} %all-gather.2.cloned.1.call-done.refs_3_, ...), custom_call_target="tpu_custom_call" | custom-call | tf_op jit(solution)/shard_map/dkv/pallas_call | solution.py:45
  723.4 21.7 %dkv.4 = (f32[1024,128]{1,0:T(8,128)}, f32[1024,128]{1,0:T(8,128)}) custom-call(s32[9]{0:T(128)} %pad_add_fusion.refs_0_, bf16[1024,384]{1,0:T(8,128)(2,1)} %get-tuple-element.189.refs_1_, bf16[1024,384]{1,0:T(8,128)(2,1)} %get-tuple-element.190.refs_9_.refs_2_, bf16[8192,384]{1,0:T(8,128)(2,1)} %all-gather.2.cloned.1.call-done.refs_3_, ...), custom_call_target="tpu_custom_call" | custom-call | tf_op jit(solution)/shard_map/dkv/pallas_call | solution.py:45
  757.1 21.7 %dkv.5 = (f32[1024,128]{1,0:T(8,128)}, f32[1024,128]{1,0:T(8,128)}) custom-call(s32[9]{0:T(128)} %pad_add_fusion.refs_0_, bf16[1024,384]{1,0:T(8,128)(2,1)} %get-tuple-element.189.refs_1_, bf16[1024,384]{1,0:T(8,128)(2,1)} %get-tuple-element.190.refs_9_.refs_2_, bf16[8192,384]{1,0:T(8,128)(2,1)} %all-gather.2.cloned.1.call-done.refs_3_, ...), custom_call_target="tpu_custom_call" | custom-call | tf_op jit(solution)/shard_map/dkv/pallas_call | solution.py:45
  778.8 6.6 dqkv.4
  793.9 6.6 dqkv.5
  800.6 9.4 collective-permute-done.80.refs_1_
  822.0 6.6 dqkv.6
  828.6 6.6 collective-permute-done.82.refs_1_
  840.7 6.6 dqkv.7
  847.3 11.0 %pair_grad.5.refs_7_ = bf16[1536,1536]{1,0:T(8,128)(2,1)} custom-call(bf16[1024,1536]{1,0:T(8,128)(2,1)} %get-tuple-element.187.refs_0_.refs_7_, bf16[1024,1152]{1,0:T(8,128)(2,1)} %get-tuple-element.328.refs_1_, bf16[1024,1536]{1,0:T(8,128)(2,1)} %get-tuple-element.329.refs_2_, bf16[1024,384]{1,0:T(8,128)(2,1)} %pad_maximum_fusion.3.refs_3_, ...), custom_call_target="tpu_custom_call" | custom-call | tf_op jit(solution)/shard_map/pair_grad/pallas_call | solution.py:45
  908.6 10.0 %collective-permute-done.86.refs_1_ = bf16[256,1536]{1,0:T(8,128)(2,1)S(1)} collective-permute-done((bf16[256,1536]{1,0:T(8,128)(2,1)}, bf16[256,1536]{1,0:T(8,128)(2,1)S(1)}, u32[]{:S(2)}, u32[]{:S(2)}) %collective-permute-start.86) | collective-permute-done | bytes 786464 | tf_op jit(solution)/shard_map/ppermute | solution.py:817
  (610 shorter events, 427.0 us)
Async XLA Ops:
  7.2 687.6 %all-gather.2.cloned.1.call-start = ((), (), s32[]{:S(2)}) async-start(), calls=%async_computation.3 | async-start | bytes 7077888 | tf_op jit(solution)/shard_map/all_gather | solution.py:986
  67.9 20.7 %collective-permute-start.8 = (bf16[1024,384]{1,0:T(8,128)(2,1)}, bf16[1024,384]{1,0:T(8,128)(2,1)}, u32[]{:S(2)}, u32[]{:S(2)}) collective-permute-start(bf16[1024,384]{1,0:T(8,128)(2,1)} %get-tuple-element.190.refs_9_.refs_2_), channel_id=1, source_target_pairs={{0,8},{4,12},{8,0},{12,4},{16,24},{20,28},{24,16},{28,20},{1,9},{5... | collective-permute-start | bytes 2359304 | tf_op jit(solution)/shard_map/ppermute | solution.py:730
  69.4 23.5 %collective-permute-start.10 = (bf16[1024,384]{1,0:T(8,128)(2,1)}, bf16[1024,384]{1,0:T(8,128)(2,1)}, u32[]{:S(2)}, u32[]{:S(2)}) collective-permute-start(bf16[1024,384]{1,0:T(8,128)(2,1)} %get-tuple-element.190.refs_9_.refs_2_), channel_id=1, source_target_pairs={{4,20},{16,0},{12,28},{24,8},{5,21},{17,1},{13,29},{25,9},{6,22},{... | collective-permute-start | bytes 2359304 | tf_op jit(solution)/shard_map/ppermute | solution.py:730
  83.0 43.2 %collective-permute-start.1 = (bf16[1024,384]{1,0:T(8,128)(2,1)S(1)}, bf16[1024,384]{1,0:T(8,128)(2,1)}, u32[]{:S(2)}, u32[]{:S(2)}) collective-permute-start(bf16[1024,384]{1,0:T(8,128)(2,1)S(1)} %copy-done.2), channel_id=1, source_target_pairs={{0,8},{4,12},{8,0},{12,4},{16,24},{20,28},{24,16},{28,20},{1,9},{5... | collective-permute-start | bytes 2359304 | tf_op jit(solution)/shard_map/ppermute | solution.py:730
  88.6 37.6 %collective-permute-start.12 = (bf16[1024,384]{1,0:T(8,128)(2,1)}, bf16[1024,384]{1,0:T(8,128)(2,1)}, u32[]{:S(2)}, u32[]{:S(2)}) collective-permute-start(bf16[1024,384]{1,0:T(8,128)(2,1)} %collective-permute-done.8.refs_11_), channel_id=1, source_target_pairs={{0,16},{28,12},{1,17},{29,13},{2,18},{30,14},{3,19},{31,15}} | collective-permute-start | bytes 2359304 | tf_op jit(solution)/shard_map/ppermute | solution.py:730
  92.8 33.9 %collective-permute-start.13 = (bf16[1024,384]{1,0:T(8,128)(2,1)}, bf16[1024,384]{1,0:T(8,128)(2,1)}, u32[]{:S(2)}, u32[]{:S(2)}) collective-permute-start(bf16[1024,384]{1,0:T(8,128)(2,1)} %collective-permute-done.10.refs_13_), channel_id=1, source_target_pairs={{28,20},{0,8},{29,21},{1,9},{30,22},{2,10},{31,23},{3,11}} | collective-permute-start | bytes 2359304 | tf_op jit(solution)/shard_map/ppermute | solution.py:730
  96.1 28.7 %collective-permute-start.16 = (bf16[256,768]{1,0:T(8,128)(2,1)S(1)}, bf16[256,768]{1,0:T(8,128)(2,1)S(1)}, u32[]{:S(2)}, u32[]{:S(2)}) collective-permute-start(bf16[256,768]{1,0:T(8,128)(2,1)S(1)} %broadcast_select_fusion), channel_id=1, source_target_pairs={{0,8},{4,12},{8,16},{12,20},{16,24},{20,28},{1,9},{5,13},{9,17},{1... | collective-permute-start | bytes 1179656 | tf_op jit(solution)/shard_map/ppermute | solution.py:748
  100.3 35.1 %collective-permute-start.7 = (bf16[1024,384]{1,0:T(8,128)(2,1)}, bf16[1024,384]{1,0:T(8,128)(2,1)S(1)}, u32[]{:S(2)}, u32[]{:S(2)}) collective-permute-start(bf16[1024,384]{1,0:T(8,128)(2,1)} %get-tuple-element.190.refs_9_.refs_2_), channel_id=1, source_target_pairs={{0,4},{4,0},{8,12},{12,8},{16,20},{20,16},{24,28},{28,24},{1,5},{5... | collective-permute-start | bytes 2359304 | tf_op jit(solution)/shard_map/ppermute | solution.py:703
  126.7 22.7 %collective-permute-start.5 = (bf16[1024,384]{1,0:T(8,128)(2,1)}, bf16[1024,384]{1,0:T(8,128)(2,1)}, u32[]{:S(2)}, u32[]{:S(2)}) collective-permute-start(bf16[1024,384]{1,0:T(8,128)(2,1)} %collective-permute-done.1.refs_3_), channel_id=1, source_target_pairs={{0,16},{4,20},{24,8},{28,12},{1,17},{5,21},{25,9},{29,13},{2,18},{... | collective-permute-start | bytes 2359304 | tf_op jit(solution)/shard_map/ppermute | solution.py:730
  135.5 19.1 %collective-permute-start.9 = (bf16[1024,384]{1,0:T(8,128)(2,1)}, bf16[1024,384]{1,0:T(8,128)(2,1)}, u32[]{:S(2)}, u32[]{:S(2)}) collective-permute-start(bf16[1024,384]{1,0:T(8,128)(2,1)} %collective-permute-done.8.refs_11_), channel_id=1, source_target_pairs={{0,4},{4,0},{8,12},{12,8},{16,20},{20,16},{24,28},{28,24},{1,5},{5... | collective-permute-start | bytes 2359304 | tf_op jit(solution)/shard_map/ppermute | solution.py:703
  149.5 636.0 %reduce-scatter.4.cloned.1.call-start = ((), (), s32[]{:S(2)}) async-start(), calls=%async_computation.4 | async-start | bytes 10616832 | tf_op jit(solution)/shard_map/reduce_scatter | solution.py:879
  182.1 21.6 %collective-permute-start.17 = (bf16[256,1536]{1,0:T(8,128)(2,1)}, bf16[256,1536]{1,0:T(8,128)(2,1)}, u32[]{:S(2)}, u32[]{:S(2)}) collective-permute-start(bf16[256,1536]{1,0:T(8,128)(2,1)} %convolution_convert_fusion.4.refs_2_), channel_id=1, source_target_pairs={{0,1},{3,2},{1,0},{2,3},{4,5},{7,6},{5,4},{6,7},{8,9},{11,10},{9,8... | collective-permute-start | bytes 2359304 | tf_op jit(solution)/shard_map/ppermute | solution.py:817
  207.5 26.0 %collective-permute-start.18 = (bf16[256,1536]{1,0:T(8,128)(2,1)}, bf16[256,1536]{1,0:T(8,128)(2,1)S(1)}, u32[]{:S(2)}, u32[]{:S(2)}) collective-permute-start(bf16[256,1536]{1,0:T(8,128)(2,1)} %get-tuple-element.196), channel_id=1, source_target_pairs={{0,1},{3,2},{1,0},{2,3},{4,5},{7,6},{5,4},{6,7},{8,9},{11,10},{9,8... | collective-permute-start | bytes 2359304 | tf_op jit(solution)/shard_map/ppermute | solution.py:817
  208.0 25.4 %collective-permute-start.19 = (bf16[256,1536]{1,0:T(8,128)(2,1)}, bf16[256,1536]{1,0:T(8,128)(2,1)S(1)}, u32[]{:S(2)}, u32[]{:S(2)}) collective-permute-start(bf16[256,1536]{1,0:T(8,128)(2,1)} %get-tuple-element.197.refs_7_.refs_3_), channel_id=1, source_target_pairs={{1,2},{2,1},{5,6},{6,5},{9,10},{10,9},{13,14},{14,13},{17,18},{18,... | collective-permute-start | bytes 2359304 | tf_op jit(solution)/shard_map/ppermute | solution.py:817
  239.3 21.5 %collective-permute-start.20 = (bf16[256,1536]{1,0:T(8,128)(2,1)}, bf16[256,1536]{1,0:T(8,128)(2,1)S(1)}, u32[]{:S(2)}, u32[]{:S(2)}) collective-permute-start(bf16[256,1536]{1,0:T(8,128)(2,1)} %get-tuple-element.199.refs_2_), channel_id=1, source_target_pairs={{0,1},{3,2},{1,0},{2,3},{4,5},{7,6},{5,4},{6,7},{8,9},{11,10},{9,8... | collective-permute-start | bytes 2359304 | tf_op jit(solution)/shard_map/ppermute | solution.py:817
  243.2 17.7 %collective-permute-start.21 = (bf16[256,1536]{1,0:T(8,128)(2,1)}, bf16[256,1536]{1,0:T(8,128)(2,1)S(1)}, u32[]{:S(2)}, u32[]{:S(2)}) collective-permute-start(bf16[256,1536]{1,0:T(8,128)(2,1)} %get-tuple-element.200.refs_4_.refs_7_), channel_id=1, source_target_pairs={{1,2},{2,1},{5,6},{6,5},{9,10},{10,9},{13,14},{14,13},{17,18},{18,... | collective-permute-start | bytes 2359304 | tf_op jit(solution)/shard_map/ppermute | solution.py:817
  267.0 19.6 %collective-permute-start.22 = (bf16[256,1536]{1,0:T(8,128)(2,1)}, bf16[256,1536]{1,0:T(8,128)(2,1)S(1)}, u32[]{:S(2)}, u32[]{:S(2)}) collective-permute-start(bf16[256,1536]{1,0:T(8,128)(2,1)} %get-tuple-element.201.refs_2_), channel_id=1, source_target_pairs={{0,1},{3,2},{1,0},{2,3},{4,5},{7,6},{5,4},{6,7},{8,9},{11,10},{9,8... | collective-permute-start | bytes 2359304 | tf_op jit(solution)/shard_map/ppermute | solution.py:817
  292.3 19.3 %collective-permute-start.24 = (bf16[256,1536]{1,0:T(8,128)(2,1)}, bf16[256,1536]{1,0:T(8,128)(2,1)S(1)}, u32[]{:S(2)}, u32[]{:S(2)}) collective-permute-start(bf16[256,1536]{1,0:T(8,128)(2,1)} %get-tuple-element.206.refs_2_), channel_id=1, source_target_pairs={{0,1},{3,2},{1,0},{2,3},{4,5},{7,6},{5,4},{6,7},{8,9},{11,10},{9,8... | collective-permute-start | bytes 2359304 | tf_op jit(solution)/shard_map/ppermute | solution.py:817
  317.1 18.4 %collective-permute-start.26 = (bf16[256,1536]{1,0:T(8,128)(2,1)}, bf16[256,1536]{1,0:T(8,128)(2,1)S(1)}, u32[]{:S(2)}, u32[]{:S(2)}) collective-permute-start(bf16[256,1536]{1,0:T(8,128)(2,1)} %get-tuple-element.213.refs_2_), channel_id=1, source_target_pairs={{0,1},{3,2},{1,0},{2,3},{4,5},{7,6},{5,4},{6,7},{8,9},{11,10},{9,8... | collective-permute-start | bytes 2359304 | tf_op jit(solution)/shard_map/ppermute | solution.py:817
  447.2 19.7 %collective-permute-start.38 = (bf16[256,1536]{1,0:T(8,128)(2,1)}, bf16[256,1536]{1,0:T(8,128)(2,1)S(1)}, u32[]{:S(2)}, u32[]{:S(2)}) collective-permute-start(bf16[256,1536]{1,0:T(8,128)(2,1)} %get-tuple-element.261.refs_2_), channel_id=1, source_target_pairs={{0,1},{3,2},{1,0},{2,3},{4,5},{7,6},{5,4},{6,7},{8,9},{11,10},{9,8... | collective-permute-start | bytes 2359304 | tf_op jit(solution)/shard_map/ppermute | solution.py:817
  473.0 21.1 %collective-permute-start.40 = (bf16[256,1536]{1,0:T(8,128)(2,1)}, bf16[256,1536]{1,0:T(8,128)(2,1)S(1)}, u32[]{:S(2)}, u32[]{:S(2)}) collective-permute-start(bf16[256,1536]{1,0:T(8,128)(2,1)} %get-tuple-element.275.refs_2_), channel_id=1, source_target_pairs={{0,1},{3,2},{1,0},{2,3},{4,5},{7,6},{5,4},{6,7},{8,9},{11,10},{9,8... | collective-permute-start | bytes 2359304 | tf_op jit(solution)/shard_map/ppermute | solution.py:817
  474.5 26.2 %collective-permute-start.41 = (bf16[256,1536]{1,0:T(8,128)(2,1)}, bf16[256,1536]{1,0:T(8,128)(2,1)S(1)}, u32[]{:S(2)}, u32[]{:S(2)}) collective-permute-start(bf16[256,1536]{1,0:T(8,128)(2,1)} %get-tuple-element.276.refs_4_), channel_id=1, source_target_pairs={{1,2},{2,1},{5,6},{6,5},{9,10},{10,9},{13,14},{14,13},{17,18},{18,... | collective-permute-start | bytes 2359304 | tf_op jit(solution)/shard_map/ppermute | solution.py:817
  475.2 36.1 %collective-permute-start.43 = (bf16[256,512]{1,0:T(8,128)(2,1)S(1)}, bf16[256,512]{1,0:T(8,128)(2,1)S(1)}, u32[]{:S(2)}, u32[]{:S(2)}) collective-permute-start(bf16[256,512]{1,0:T(8,128)(2,1)S(1)} %copy-done.14), channel_id=1, source_target_pairs={{0,8},{4,12},{8,0},{12,4},{16,24},{20,28},{24,16},{28,20},{1,9},{5... | collective-permute-start | bytes 786440 | tf_op jit(solution)/shard_map/ppermute | solution.py:730
  485.3 26.1 %collective-permute-start.44 = (bf16[256,512]{1,0:T(8,128)(2,1)S(1)}, bf16[256,512]{1,0:T(8,128)(2,1)S(1)}, u32[]{:S(2)}, u32[]{:S(2)}) collective-permute-start(bf16[256,512]{1,0:T(8,128)(2,1)S(1)} %copy-done.14), channel_id=1, source_target_pairs={{4,20},{16,0},{12,28},{24,8},{5,21},{17,1},{13,29},{25,9},{6,22},{... | collective-permute-start | bytes 786440 | tf_op jit(solution)/shard_map/ppermute | solution.py:730
  492.4 19.0 %collective-permute-start.45 = (bf16[256,512]{1,0:T(8,128)(2,1)}, bf16[256,512]{1,0:T(8,128)(2,1)S(1)}, u32[]{:S(2)}, u32[]{:S(2)}) collective-permute-start(bf16[256,512]{1,0:T(8,128)(2,1)} %get-tuple-element.286.refs_4_.refs_5_.refs_9_), channel_id=1, source_target_pairs={{4,20},{16,0},{12,28},{24,8},{5,21},{17,1},{13,29},{25,9},{6,22},{... | collective-permute-start | bytes 786440 | tf_op jit(solution)/shard_map/ppermute | solution.py:730
  522.3 341.5 %reduce-scatter.6.cloned.1.call-start = ((), (), s32[]{:S(2)}) async-start(), calls=%async_computation.5 | async-start | bytes 7077888 | tf_op jit(solution)/shard_map/reduce_scatter | solution.py:879
  555.6 18.3 %collective-permute-start.50 = (bf16[256,768]{1,0:T(8,128)(2,1)}, bf16[256,768]{1,0:T(8,128)(2,1)S(1)}, u32[]{:S(2)}, u32[]{:S(2)}) collective-permute-start(bf16[256,768]{1,0:T(8,128)(2,1)} %fusion.14), channel_id=1, source_target_pairs={{8,0},{12,4},{16,8},{20,12},{24,16},{28,20},{9,1},{13,5},{17,9},{2... | collective-permute-start | bytes 1179656 | tf_op jit(solution)/shard_map/ppermute | solution.py:748
  574.8 83.5 %collective-permute-start.51 = (bf16[256,768]{1,0:T(8,128)(2,1)}, bf16[256,768]{1,0:T(8,128)(2,1)}, u32[]{:S(2)}, u32[]{:S(2)}) collective-permute-start(bf16[256,768]{1,0:T(8,128)(2,1)} %fusion.18), channel_id=1, source_target_pairs={{4,0},{8,4},{12,8},{16,12},{20,16},{24,20},{28,24},{5,1},{9,5},{13... | collective-permute-start | bytes 1179656 | tf_op jit(solution)/shard_map/ppermute | solution.py:748
  576.1 21.1 %collective-permute-start.52 = (bf16[256,512]{1,0:T(8,128)(2,1)S(1)}, bf16[256,512]{1,0:T(8,128)(2,1)}, u32[]{:S(2)}, u32[]{:S(2)}) collective-permute-start(bf16[256,512]{1,0:T(8,128)(2,1)S(1)} %copy-done.11), channel_id=1, source_target_pairs={{0,8},{4,12},{8,0},{12,4},{16,24},{20,28},{24,16},{28,20},{1,9},{5... | collective-permute-start | bytes 786440 | tf_op jit(solution)/shard_map/ppermute | solution.py:730
  579.7 48.8 %collective-permute-start.55 = (bf16[256,512]{1,0:T(8,128)(2,1)}, bf16[256,512]{1,0:T(8,128)(2,1)}, u32[]{:S(2)}, u32[]{:S(2)}) collective-permute-start(bf16[256,512]{1,0:T(8,128)(2,1)} %get-tuple-element.294.refs_4_.refs_5_.refs_9_), channel_id=1, source_target_pairs={{0,8},{4,12},{8,0},{12,4},{16,24},{20,28},{24,16},{28,20},{1,9},{5... | collective-permute-start | bytes 786440 | tf_op jit(solution)/shard_map/ppermute | solution.py:730
  579.8 50.2 %collective-permute-start.54 = (bf16[256,512]{1,0:T(8,128)(2,1)}, bf16[256,512]{1,0:T(8,128)(2,1)}, u32[]{:S(2)}, u32[]{:S(2)}) collective-permute-start(bf16[256,512]{1,0:T(8,128)(2,1)} %get-tuple-element.294.refs_4_.refs_5_.refs_9_), channel_id=1, source_target_pairs={{4,20},{16,0},{12,28},{24,8},{5,21},{17,1},{13,29},{25,9},{6,22},{... | collective-permute-start | bytes 786440 | tf_op jit(solution)/shard_map/ppermute | solution.py:730
  581.1 50.4 %collective-permute-start.53 = (bf16[256,512]{1,0:T(8,128)(2,1)S(1)}, bf16[256,512]{1,0:T(8,128)(2,1)}, u32[]{:S(2)}, u32[]{:S(2)}) collective-permute-start(bf16[256,512]{1,0:T(8,128)(2,1)S(1)} %copy-done.11), channel_id=1, source_target_pairs={{4,20},{16,0},{12,28},{24,8},{5,21},{17,1},{13,29},{25,9},{6,22},{... | collective-permute-start | bytes 786440 | tf_op jit(solution)/shard_map/ppermute | solution.py:730
  597.2 63.3 %collective-permute-start.56 = (bf16[256,512]{1,0:T(8,128)(2,1)}, bf16[256,512]{1,0:T(8,128)(2,1)S(1)}, u32[]{:S(2)}, u32[]{:S(2)}) collective-permute-start(bf16[256,512]{1,0:T(8,128)(2,1)} %collective-permute-done.52.refs_10_.refs_3_), channel_id=1, source_target_pairs={{0,16},{4,20},{24,8},{28,12},{1,17},{5,21},{25,9},{29,13},{2,18},{... | collective-permute-start | bytes 786440 | tf_op jit(solution)/shard_map/ppermute | solution.py:730
  628.6 31.9 %collective-permute-start.57 = (bf16[256,512]{1,0:T(8,128)(2,1)}, bf16[256,512]{1,0:T(8,128)(2,1)S(1)}, u32[]{:S(2)}, u32[]{:S(2)}) collective-permute-start(bf16[256,512]{1,0:T(8,128)(2,1)} %collective-permute-done.55.refs_13_.refs_11_), channel_id=1, source_target_pairs={{0,16},{28,12},{1,17},{29,13},{2,18},{30,14},{3,19},{31,15}} | collective-permute-start | bytes 786440 | tf_op jit(solution)/shard_map/ppermute | solution.py:730
  630.0 30.5 %collective-permute-start.58 = (bf16[256,512]{1,0:T(8,128)(2,1)}, bf16[256,512]{1,0:T(8,128)(2,1)S(1)}, u32[]{:S(2)}, u32[]{:S(2)}) collective-permute-start(bf16[256,512]{1,0:T(8,128)(2,1)} %collective-permute-done.54.refs_12_.refs_13_), channel_id=1, source_target_pairs={{28,20},{0,8},{29,21},{1,9},{30,22},{2,10},{31,23},{3,11}} | collective-permute-start | bytes 786440 | tf_op jit(solution)/shard_map/ppermute | solution.py:730
  669.6 300.7 %reduce-scatter.8.cloned.1.call-start = ((), (), s32[]{:S(2)}) async-start(), calls=%async_computation.6 | async-start | bytes 5308416 | tf_op jit(solution)/shard_map/reduce_scatter | solution.py:879
  683.0 33.6 %collective-permute-start.59 = (bf16[256,1536]{1,0:T(8,128)(2,1)S(1)}, bf16[256,1536]{1,0:T(8,128)(2,1)}, u32[]{:S(2)}, u32[]{:S(2)}) collective-permute-start(bf16[256,1536]{1,0:T(8,128)(2,1)S(1)} %get-tuple-element.420.refs_2_), channel_id=1, source_target_pairs={{0,1},{3,2},{1,0},{2,3},{4,5},{7,6},{5,4},{6,7},{8,9},{11,10},{9,8... | collective-permute-start | bytes 2359304 | tf_op jit(solution)/shard_map/ppermute | solution.py:817
  720.3 24.8 %collective-permute-start.76 = (bf16[256,1536]{1,0:T(8,128)(2,1)}, bf16[256,1536]{1,0:T(8,128)(2,1)S(1)}, u32[]{:S(2)}, u32[]{:S(2)}) collective-permute-start(bf16[256,1536]{1,0:T(8,128)(2,1)} %get-tuple-element.302), channel_id=1, source_target_pairs={{0,1},{3,2},{1,0},{2,3},{4,5},{7,6},{5,4},{6,7},{8,9},{11,10},{9,8... | collective-permute-start | bytes 2359304 | tf_op jit(solution)/shard_map/ppermute | solution.py:817
  722.3 22.9 %collective-permute-start.77 = (bf16[256,1536]{1,0:T(8,128)(2,1)}, bf16[256,1536]{1,0:T(8,128)(2,1)S(1)}, u32[]{:S(2)}, u32[]{:S(2)}) collective-permute-start(bf16[256,1536]{1,0:T(8,128)(2,1)} %get-tuple-element.303.refs_12_.refs_3_), channel_id=1, source_target_pairs={{1,2},{2,1},{5,6},{6,5},{9,10},{10,9},{13,14},{14,13},{17,18},{18,... | collective-permute-start | bytes 2359304 | tf_op jit(solution)/shard_map/ppermute | solution.py:817
  750.4 35.1 %collective-permute-start.78 = (bf16[256,1536]{1,0:T(8,128)(2,1)}, bf16[256,1536]{1,0:T(8,128)(2,1)S(1)}, u32[]{:S(2)}, u32[]{:S(2)}) collective-permute-start(bf16[256,1536]{1,0:T(8,128)(2,1)} %get-tuple-element.305.refs_2_), channel_id=1, source_target_pairs={{0,1},{3,2},{1,0},{2,3},{4,5},{7,6},{5,4},{6,7},{8,9},{11,10},{9,8... | collective-permute-start | bytes 2359304 | tf_op jit(solution)/shard_map/ppermute | solution.py:817
  752.3 33.2 %collective-permute-start.79 = (bf16[256,1536]{1,0:T(8,128)(2,1)}, bf16[256,1536]{1,0:T(8,128)(2,1)}, u32[]{:S(2)}, u32[]{:S(2)}) collective-permute-start(bf16[256,1536]{1,0:T(8,128)(2,1)} %get-tuple-element.306.refs_12_.refs_4_), channel_id=1, source_target_pairs={{1,2},{2,1},{5,6},{6,5},{9,10},{10,9},{13,14},{14,13},{17,18},{18,... | collective-permute-start | bytes 2359304 | tf_op jit(solution)/shard_map/ppermute | solution.py:817
  790.7 19.3 %collective-permute-start.80 = (bf16[256,1536]{1,0:T(8,128)(2,1)}, bf16[256,1536]{1,0:T(8,128)(2,1)S(1)}, u32[]{:S(2)}, u32[]{:S(2)}) collective-permute-start(bf16[256,1536]{1,0:T(8,128)(2,1)} %get-tuple-element.313.refs_2_), channel_id=1, source_target_pairs={{0,1},{3,2},{1,0},{2,3},{4,5},{7,6},{5,4},{6,7},{8,9},{11,10},{9,8... | collective-permute-start | bytes 2359304 | tf_op jit(solution)/shard_map/ppermute | solution.py:817
  792.4 17.5 %collective-permute-start.81 = (bf16[256,1536]{1,0:T(8,128)(2,1)}, bf16[256,1536]{1,0:T(8,128)(2,1)S(1)}, u32[]{:S(2)}, u32[]{:S(2)}) collective-permute-start(bf16[256,1536]{1,0:T(8,128)(2,1)} %get-tuple-element.314.refs_4_), channel_id=1, source_target_pairs={{1,2},{2,1},{5,6},{6,5},{9,10},{10,9},{13,14},{14,13},{17,18},{18,... | collective-permute-start | bytes 2359304 | tf_op jit(solution)/shard_map/ppermute | solution.py:817
  815.5 19.7 %collective-permute-start.82 = (bf16[256,1536]{1,0:T(8,128)(2,1)}, bf16[256,1536]{1,0:T(8,128)(2,1)S(1)}, u32[]{:S(2)}, u32[]{:S(2)}) collective-permute-start(bf16[256,1536]{1,0:T(8,128)(2,1)} %get-tuple-element.318.refs_2_), channel_id=1, source_target_pairs={{0,1},{3,2},{1,0},{2,3},{4,5},{7,6},{5,4},{6,7},{8,9},{11,10},{9,8... | collective-permute-start | bytes 2359304 | tf_op jit(solution)/shard_map/ppermute | solution.py:817
  900.7 17.9 %collective-permute-start.86 = (bf16[256,1536]{1,0:T(8,128)(2,1)}, bf16[256,1536]{1,0:T(8,128)(2,1)S(1)}, u32[]{:S(2)}, u32[]{:S(2)}) collective-permute-start(bf16[256,1536]{1,0:T(8,128)(2,1)} %get-tuple-element.330.refs_2_), channel_id=1, source_target_pairs={{0,1},{3,2},{1,0},{2,3},{4,5},{7,6},{5,4},{6,7},{8,9},{11,10},{9,8... | collective-permute-start | bytes 2359304 | tf_op jit(solution)/shard_map/ppermute | solution.py:817
  931.7 22.0 %collective-permute-start.101 = (f32[8,128]{1,0:T(8,128)S(1)}, f32[8,128]{1,0:T(8,128)S(1)}, u32[]{:S(2)}, u32[]{:S(2)}) collective-permute-start(f32[8,128]{1,0:T(8,128)S(1)} %bitcast.137), channel_id=1, source_target_pairs={{0,1},{1,0},{2,3},{3,2},{4,5},{5,4},{6,7},{7,6},{8,9},{9,8},{10,11... | collective-permute-start | bytes 12296 | tf_op jit(solution)/shard_map/ppermute | solution.py:703
  933.6 20.1 %collective-permute-start.102 = (f32[8,128]{1,0:T(8,128)S(1)}, f32[8,128]{1,0:T(8,128)S(1)}, u32[]{:S(2)}, u32[]{:S(2)}) collective-permute-start(f32[8,128]{1,0:T(8,128)S(1)} %bitcast.138), channel_id=1, source_target_pairs={{0,2},{1,3},{2,0},{3,1},{4,6},{5,7},{6,4},{7,5},{8,10},{9,11},{10,... | collective-permute-start | bytes 12296 | tf_op jit(solution)/shard_map/ppermute | solution.py:703
  934.5 19.2 %collective-permute-start.103 = (f32[8,128]{1,0:T(8,128)S(1)}, f32[8,128]{1,0:T(8,128)S(1)}, u32[]{:S(2)}, u32[]{:S(2)}) collective-permute-start(f32[8,128]{1,0:T(8,128)S(1)} %bitcast.139), channel_id=1, source_target_pairs={{0,3},{1,2},{2,1},{3,0},{4,7},{5,6},{6,5},{7,4},{8,11},{9,10},{10,... | collective-permute-start | bytes 12296 | tf_op jit(solution)/shard_map/ppermute | solution.py:703
  (182 other events, 1452.5 us)
Sparse Core Ops, SparseCore 0:
  149.6 52.9 all-gather.1
  522.4 90.4 reduce-scatter.3
  669.7 57.6 reduce-scatter.5
  858.5 56.1 reduce-scatter.7

commit v6 on v5

--- a/solution.py
+++ b/solution.py
@@ -27,6 +27,12 @@
 
 def sds(shape, dtype):
     return jax.ShapeDtypeStruct(shape, dtype)
+
+
+COST = {
+    "key": 8, "query": 9, "caption_norm": 2, "pick": 5, "attend": 18, "hop": 3, "ffn": 9, "ffn_back": 10, "out_back": 6,
+    "pair_grad": 10, "caption_back": 6, "dq": 27, "dkv": 24, "dqkv": 7, "caption_grad": 3, "last": 3, "note": 1, "pin": 1,
+}
 
 
 class Order:
@@ -54,6 +60,9 @@
             out_shape=out_shape,
             input_output_aliases={at + k: first_held + k for k in range(len(held))},
             compiler_params=params(len(grid)),
+            cost_estimate=pl.CostEstimate(
+                flops=COST[name] * 250_000_000, bytes_accessed=COST[name] * 750_000, transcendentals=0
+            ),
             name=name,
         )(*(() if scalar is None else (scalar,)), *ins, *extra)
         self.token = (out[0],)
@@ -136,13 +145,14 @@
     return jnp.concatenate([t] * (n // t.shape[1]), 1)
 
 
-def key_kernel(p_ref, v_ref, w_ref, c_ref, s1_ref, s2_ref, hg_ref, a_ref, kr_ref, k_ref):
+def key_kernel(p_ref, v_ref, w_ref, wv_ref, c_ref, s1_ref, s2_ref, hg_ref, a_ref, kr_ref, k_ref, vv_ref):
     x = p_ref[...].astype(f32)
     a = (x * inv_rms(x) * row(v_ref, 0)).astype(bf16)
     a_ref[...] = a
     k = mm(a, w_ref[0])
     kr_ref[...] = k
     k_ref[...] = turned(k, row(hg_ref, 1), (c_ref, s1_ref, s2_ref)).astype(bf16)
+    vv_ref[...] = mm(a, wv_ref[0]).astype(bf16)
 
 
 def turned(y, gain, tabs):
@@ -152,10 +162,8 @@
     return z * cos + pltpu.roll(z, n - 16, 1) * s1 + pltpu.roll(z, 16, 1) * s2
 
 
-def query_kernel(a_ref, wq_ref, wv_ref, c_ref, s1_ref, s2_ref, hg_ref, qr_ref, q_ref, v_ref):
-    a = a_ref[...]
-    v_ref[...] = mm(a, wv_ref[0]).astype(bf16)
-    q = mm(a, wq_ref[0])
+def query_kernel(a_ref, wq_ref, c_ref, s1_ref, s2_ref, hg_ref, qr_ref, q_ref):
+    q = mm(a_ref[...], wq_ref[0])
     qr_ref[...] = q
     q_ref[...] = (turned(q, row(hg_ref, 0), (c_ref, s1_ref, s2_ref)) * (0.125 * LOG2E)).astype(bf16)
 
@@ -164,31 +172,33 @@
     return pl.BlockSpec((1, *w.shape[1:]), lambda *_: (k, 0, 0), pipeline_mode=pl.Buffered(1))
 
 
-def key_call(order, patches, vec, w, tabs, hg, br=256):
+def key_call(order, patches, vec, w, tabs, hg, after, br=256):
     t, d = patches.shape
     n = w.shape[2]
     return order.run(
         "key",
         key_kernel,
         (t // br,),
-        (patches, vec, w, *tabs, hg),
-        [rows_of(br, d), whole(vec.shape), one_weight(w, 1)] + [rows_of(br, 128)] * 3 + [whole(hg.shape)],
-        [rows_of(br, d)] + [rows_of(br, n)] * 2,
-        [sds((t, d), bf16), sds((t, n), f32), sds((t, n), bf16)],
-    )
-
-
-def query_call(order, a, w, tabs, hg, br=256):
+        (patches, vec, w, w, *tabs, hg),
+        [rows_of(br, d), whole(vec.shape), one_weight(w, 1), one_weight(w, 2)] + [rows_of(br, 128)] * 3 + [whole(hg.shape)],
+        [rows_of(br, d)] + [rows_of(br, n)] * 3,
+        [sds((t, d), bf16), sds((t, n), f32), sds((t, n), bf16), sds((t, n), bf16)],
+        after=after,
+    )
+
+
+def query_call(order, a, w, tabs, hg, after, br=256):
     t, d = a.shape
     n = w.shape[2]
     return order.run(
         "query",
         query_kernel,
         (t // br,),
-        (a, w, w, *tabs, hg),
-        [rows_of(br, d), one_weight(w, 0), one_weight(w, 2)] + [rows_of(br, 128)] * 3 + [whole(hg.shape)],
-        [rows_of(br, n)] * 3,
-        [sds((t, n), f32), sds((t, n), bf16), sds((t, n), bf16)],
+        (a, w, *tabs, hg),
+        [rows_of(br, d), one_weight(w, 0)] + [rows_of(br, 128)] * 3 + [whole(hg.shape)],
+        [rows_of(br, n)] * 2,
+        [sds((t, n), f32), sds((t, n), bf16)],
+        after=after,
     )
 
 
@@ -321,7 +331,7 @@
     return jnp.where((lane >= 3 * head) & (lane < 3 * head + 3), -1.0, 0.0).astype(bf16)
 
 
-def dq_kernel(sc, q_ref, da_ref, xa_ref, db_ref, xb_ref, k_ref, v_ref, c_ref, dq_ref, acc):
+def dq_kernel(sc, q_ref, d_ref, x_ref, k_ref, v_ref, c_ref, dq_ref, acc):
     pair = pl.program_id(0)
     j = pl.program_id(1)
     masks = halves(128)
@@ -334,9 +344,7 @@
     @pl.when(j < sc[0])
     def _():
         q = q_ref[...]
-        dx = jnp.concatenate(
-            [jnp.concatenate([da_ref[...], xa_ref[...]], 1), jnp.concatenate([db_ref[...], xb_ref[...]], 1)], 0
-        )
+        dx = jnp.concatenate([d_ref[...], x_ref[...]], 1)
         total = acc[...]
         for h in range(2):
             off = minus_delta(keys, 2 * pair + h)
@@ -353,7 +361,7 @@
         dq_ref[...] = acc[...] * 0.125 + c_ref[...]
 
 
-def dq_call(order, sc, q, da, db, k, v, cap_dq, h, after=()):
+def dq_call(order, sc, q, d, k, v, cap_dq, h, after=()):
     n = q.shape[1]
     pairs = n // 128
     block = k.shape[0] // SPAN
@@ -365,13 +373,11 @@
         "dq",
         dq_kernel,
         (pairs, SPAN),
-        (q, da, da, db, db, k, v, cap_dq),
+        (q, d, d, k, v, cap_dq),
         [
             pl.BlockSpec((bq, 128), lambda p, j, s: (h, p)),
-            pl.BlockSpec((BR, 128), mine),
-            pl.BlockSpec((BR, 128), extra),
-            pl.BlockSpec((BR, 128), mine),
-            pl.BlockSpec((BR, 128), extra),
+            pl.BlockSpec((bq, 128), mine),
+            pl.BlockSpec((bq, 128), extra),
             pl.BlockSpec((block, 128), other),
             pl.BlockSpec((block, 128), other),
             pl.BlockSpec((bq, 128), mine),
@@ -384,12 +390,12 @@
     )[0]
 
 
-def dkv_kernel(parts, pair, sc, k_ref, v_ref, q_ref, *rest):
+def dkv_kernel(parts, base, sc, k_ref, v_ref, q_ref, *rest):
     d_refs, x_refs = rest[0 : 2 * parts : 2], rest[1 : 2 * parts : 2]
     dk_ref, dv_ref = rest[2 * parts :]
-    j = pl.program_id(0)
+    pair = base + pl.program_id(0)
+    j = pl.program_id(1)
     masks = halves(128)
-    keys = 512
     queries = 2 * BR
 
     @pl.when(j == 0)
@@ -399,39 +405,36 @@
 
     @pl.when(j < sc[0])
     def _():
-        for c in range(k_ref.shape[0] // keys):
-            at = slice(c * keys, (c + 1) * keys)
-            dk, dv = dk_ref[at, :], dv_ref[at, :]
-            for h in range(2):
-                off = minus_delta(keys, 2 * pair + h)
-                vx = jnp.concatenate([keep(v_ref[at, :], masks[h]), off], 1)
-                for r in range(parts // 2):
-                    q = keep(q_ref[r * queries : (r + 1) * queries, :], masks[h])
-                    d = jnp.concatenate([d_refs[2 * r][...], d_refs[2 * r + 1][...]], 0)
-                    x = jnp.concatenate([x_refs[2 * r][...], x_refs[2 * r + 1][...]], 0)
-                    e = jnp.exp2(mm_nt(k_ref[at, :], q))
-                    dp = mm_nt(vx, jnp.concatenate([d, x], 1))
-                    dv = dv + mm(e.astype(bf16), keep(d, masks[h]))
-                    dk = dk + mm((e * dp).astype(bf16), q)
-            dk_ref[at, :] = dk
-            dv_ref[at, :] = dv
-
-
-def dkv_call(order, sc, k, v, q_all, ds, pair):
+        dk, dv = dk_ref[...], dv_ref[...]
+        for h in range(2):
+            vx = jnp.concatenate([keep(v_ref[...], masks[h]), minus_delta(v_ref.shape[0], 2 * pair + h)], 1)
+            for r in range(parts):
+                q = keep(q_ref[r * queries : (r + 1) * queries, :], masks[h])
+                d, x = d_refs[r][...], x_refs[r][...]
+                e = jnp.exp2(mm_nt(k_ref[...], q))
+                dp = mm_nt(vx, jnp.concatenate([d, x], 1))
+                dv = dv + mm(e.astype(bf16), keep(d, masks[h]))
+                dk = dk + mm((e * dp).astype(bf16), q)
+        dk_ref[...] = dk
+        dv_ref[...] = dv
+
+
+def dkv_call(order, sc, k, v, q_all, ds, half, base, n_pairs):
     t, n = k.shape
     pairs = n // 128
-    mine = pl.BlockSpec((t, 128), lambda j, s: (0, pair))
-    out = pl.BlockSpec((t, 128), lambda j, s: (0, 0))
-    other = pl.BlockSpec((BR, 128), lambda j, s: (item_block(j, s), pair))
-    extra = pl.BlockSpec((BR, 128), lambda j, s: (item_block(j, s), pairs))
+    rows = 2 * BR
+    mine = pl.BlockSpec((rows, 128), lambda p, j, s: (half, base + p))
+    out = pl.BlockSpec((rows, 128), lambda p, j, s: (0, p))
+    other = pl.BlockSpec((rows, 128), lambda p, j, s: (item_block(j, s), base + p))
+    extra = pl.BlockSpec((rows, 128), lambda p, j, s: (item_block(j, s), pairs))
     return order.run(
         "dkv",
-        functools.partial(dkv_kernel, len(ds), pair),
-        (SPAN,),
+        functools.partial(dkv_kernel, len(ds), base),
+        (n_pairs, SPAN),
         (k, v, q_all, *(x for d in ds for x in (d, d))),
-        [mine, mine, pl.BlockSpec((t, 128), lambda j, s: (s[1 + SPAN + j], pair))] + [other, extra] * len(ds),
+        [mine, mine, pl.BlockSpec((t, 128), lambda p, j, s: (s[1 + SPAN + j], base + p))] + [other, extra] * len(ds),
         [out, out],
-        [sds((t, 128), f32)] * 2,
+        [sds((rows, n_pairs * 128), f32)] * 2,
         scalar=sc,
     )
 
@@ -439,7 +442,7 @@
 def chunk_call(order, kernel, name, c, ins, specs, chunk_outs, sum_outs, whole_outs, before):
     one = lambda r, w: pl.BlockSpec((r, w), lambda i: (0, 0))
     own = chunk_outs + sum_outs
-    into = [pl.BlockSpec((BR, w), lambda i: (c, 0)) for _, w, _ in whole_outs]
+    into = [pl.BlockSpec((BR, w), lambda i, at=c % (r // BR): (at, 0)) for r, w, _ in whole_outs]
     return order.run(
         name,
         kernel,
@@ -559,7 +562,7 @@
     )
 
 
-def out_back_kernel(da_ref, mid_ref, at_ref, c_ref, v_ref, w_ref, o_ref, li_ref, dm_ref, dx_ref, ds_ref, c3_ref, c2_ref, dat_ref):
+def out_back_kernel(da_ref, mid_ref, at_ref, c_ref, v_ref, w_ref, o_ref, li_ref, dm_ref, dx_ref, c3_ref, c2_ref, dat_ref, ds_ref):
     da = da_ref[...].astype(f32)
     mid = mid_ref[...]
     r = inv_rms(mid)
@@ -601,9 +604,9 @@
         c,
         (da, mid, at, cot, vec, w, o, li),
         [alone(d), alone(d), alone(d), part(c, d), whole(vec.shape), whole(w.shape), part(place, n), part(place, n)],
-        [(BR, d, f32), (BR, n, bf16), (BR, n + 128, bf16)],
+        [(BR, d, f32), (BR, n, bf16)],
         [(1, d, f32), (1, d, f32)],
-        [(t, d, bf16)],
+        [(t, d, bf16), (2 * BR, n + 128, bf16)],
         before,
     )
 
@@ -646,7 +649,7 @@
         "dqkv",
         c,
         (dq, *(x for two in dkv for x in two), qr, kr, *tabs, hg, w, patches),
-        [part(c % 2, n)] + [part(c, 128)] * (2 * len(dkv)) + [part(c, n)] * 2 + [part(c, 128)] * 3 + [whole(hg.shape), whole(w.shape), part(c, d)],
+        [part(c % 2, n)] + [part(c % 2, x.shape[1]) for two in dkv for x in two] + [part(c, n)] * 2 + [part(c, 128)] * 3 + [whole(hg.shape), whole(w.shape), part(c, d)],
         [(BR, d, bf16)],
         [(2, n, f32), (1, d, f32)],
         [(t, 3 * n, bf16)],
@@ -703,11 +706,11 @@
     return lax.ppermute(x, axis, [(i, i ^ m) for i in range(size)])
 
 
-def pick_kernel(count, n_pieces, sc, *refs):
-    a, b = refs[:n_pieces], refs[n_pieces : 2 * n_pieces]
-    outs, sem = refs[2 * n_pieces : 2 * n_pieces + 2], refs[-1]
-    rows = a[0].shape[0]
-    for k, (pieces, out) in enumerate(zip((a, b), outs)):
+def pick_kernel(count, n_arrays, n_pieces, sc, *refs):
+    outs, sem = refs[n_arrays * n_pieces :][:n_arrays], refs[-1]
+    for k, out in enumerate(outs):
+        pieces = refs[k * n_pieces : (k + 1) * n_pieces]
+        rows = pieces[0].shape[0]
         for j in range(count):
             for m in range(n_pieces):
 
@@ -715,9 +718,11 @@
                 def _():
                     pltpu.make_async_copy(pieces[m], out.at[pl.ds(j * rows, rows)], sem.at[k, j]).start()
 
-    for k, (pieces, out) in enumerate(zip((a, b), outs)):
+    for k, out in enumerate(outs):
+        first = refs[k * n_pieces]
+        rows = first.shape[0]
         for j in range(count):
-            pltpu.make_async_copy(pieces[0], out.at[pl.ds(j * rows, rows)], sem.at[k, j]).wait()
+            pltpu.make_async_copy(first, out.at[pl.ds(j * rows, rows)], sem.at[k, j]).wait()
 
 
 class Gather:
@@ -740,7 +745,24 @@
     def pieces(self):
         if self.all is not None:
             return self.all
-        return [y for four in self.kept for x in four for y in (x, swap(x, "wide", 8, 1))]
+        return [[y for x in four for y in (x, swap(x, "wide", 8, 1))] for four in self.kept]
+
+
+class GatherOne:
+    def __init__(self, a):
+        self.all = None
+        if lax.axis_size("wide") != 8:
+            self.first = self.second = ()
+            self.all = [lax.all_gather(a, "wide")]
+            return
+        send = lambda x, pairs: lax.ppermute(x, "wide", pairs)
+        a2 = send(a, [(i, i ^ 2) for i in range(8)])
+        a4 = send(a, [(1, 5), (4, 0), (3, 7), (6, 2)])
+        a6 = send(a2, [(0, 4), (1, 5), (6, 2), (7, 3)])
+        self.first, self.second = (a2, a4), (a6,)
+        self.kept = ((a, a2, a4, a6),)
+
+    pieces = Gather.pieces
 
 
 def shift(x, by):
@@ -749,21 +771,41 @@
 
 
 def pick(order, sc, pieces, count):
-    if len(pieces) == 2:
+    if not isinstance(pieces[0], list):
         one = lambda x, j: lax.dynamic_index_in_dim(x, sc[1 + SPAN + j], 0, False)
         return [jnp.concatenate([one(x, j) for j in range(count)]) for x in pieces]
-    rows, width = pieces[0].shape
+    outs = [(count * p[0].shape[0], p[0].shape[1]) for p in pieces]
     return order.run(
         "pick",
-        functools.partial(pick_kernel, count, 8),
+        functools.partial(pick_kernel, count, len(pieces), 8),
         (1,),
-        pieces,
-        loose(16),
-        [pl.BlockSpec((count * rows, width), lambda i, s: (0, 0))] * 2,
-        [sds((count * rows, width), pieces[0].dtype)] * 2,
-        [pltpu.SemaphoreType.DMA((2, count))],
+        [x for p in pieces for x in p],
+        loose(8 * len(pieces)),
+        [pl.BlockSpec(shape, lambda i, s: (0, 0)) for shape in outs],
+        [sds(shape, bf16) for shape in outs],
+        [pltpu.SemaphoreType.DMA((len(pieces), count))],
         sc,
     )
+
+
+def pin_kernel(o_ref):
+    pass
+
+
+def pin(order, x):
+    return order.run("pin", pin_kernel, (1,), (), [], loose(1), [sds(x.shape, x.dtype)], held=(x,))[0]
+
+
+def note_kernel(x_ref, o_ref):
+    o_ref[...] = x_ref[...]
+
+
+def note(order, x):
+    n = x.shape[0]
+    size = -(-n // 1024) * 8
+    x = jnp.pad(x, (0, size * 128 - n)).reshape(size, 128)
+    spec = pl.BlockSpec(x.shape, lambda i: (0, 0))
+    return order.run("note", note_kernel, (1,), (x,), [spec], [spec], [sds(x.shape, f32)])[0].reshape(-1)[:n]
 
 
 def gather_small(x, axis):
@@ -831,11 +873,11 @@
         if new is not None or self.second is not None:
             outs.append("send")
         like = ins["r1"]
-        block = pl.BlockSpec((BR // 4, like.shape[1]), lambda i, s: (i, 0))
+        block = pl.BlockSpec((BR // 2, like.shape[1]), lambda i, s: (i, 0))
         got = self.order.run(
             "hop",
             functools.partial(hop_kernel, {"in": list(ins), "out": outs}),
-            (4,),
+            (2,),
             list(ins.values()),
             [block] * len(ins),
             [block] * len(outs),
@@ -963,10 +1005,6 @@
     chunks = range(t // BR)
     pairs_of = range(t // (2 * BR))
     sums = Sums(order, deep, mz)
-    a1, k_raw, k = key_call(order, patches, vec, w_qkv, tabs, hg)
-    q_raw, q, v = query_call(order, a1, w_qkv, tabs, hg)
-    kv = Gather(k, v)
-
     cap_raw = jnp.einsum("kd,jde->jke", captions, w_caption, preferred_element_type=f32)
     whole_cap = pl.BlockSpec((text, n), lambda i: (0, 0))
     both_cap = pl.BlockSpec((text, 2 * n), lambda i: (0, 0))
@@ -980,8 +1018,14 @@
         [sds((text, 2 * n), bf16)],
     )
     offset = me - first
-    cap = jnp.where(offset == 1, shift(cap, 1), cap)
-    cap = jnp.where(offset >= 2, shift(cap, 2), cap)
+    own_cap = cap
+    got_caps = tuple(shift(own_cap, by) for by in range(1, SPAN))
+    for by in range(1, SPAN):
+        cap = jnp.where(offset == by, got_caps[by - 1], cap)
+
+    a1, k_raw, k, v = key_call(order, patches, vec, w_qkv, tabs, hg, got_caps)
+    kv = Gather(k, v)
+    q_raw, q = query_call(order, a1, w_qkv, tabs, hg, kv.first)
 
     q_all = lax.all_gather(q, "wide", axis=0, tiled=True)
     k_all, v_all = pick(order, sc, kv.pieces(), SPAN)
@@ -1025,28 +1069,33 @@
             if c == 2 * h + 1 and h > 0:
                 behind = d_got[h - 1].second
             da3 = sums.get(("da3", c), behind)
-            d_mids[c], d_mixed[c], d_scaled[c], p3, p2, *whole_out = out_back_call(
+            if c == chunks[-1]:
+                g_mlp = scatter_rows(pin(order, mlp_part[0]))
+            d_mids[c], d_mixed[c], p3, p2, *outs = out_back_call(
                 order, c, da3, mids[c], sums.get(("attn", c)), cotangent, vec, w_out, o_self, linv, place, whole_out
             )
+            whole_out, d_scaled[h] = (outs if c % 2 == 0 else outs[:1]), outs[1]
             c2, c3 = c2 + p2, c3 + p3
             behind = ()
             if c == 2 * h:
                 early = d_got[h - 1].first if h > 0 else ()
                 mlp_part = pair_grad_call(order, a3, d_gu, d_ffn, hidden, h, len(pairs_of), mlp_part, early)
-        d_got[h] = Gather(d_scaled[2 * h], d_scaled[2 * h + 1])
+        d_got[h] = GatherOne(d_scaled[h])
         dq_caps[h], pk, pv, pg = caption_back_call(order, q, d_mixed[2 * h], d_mixed[2 * h + 1], cap, tg, h)
         dck, dcv, gate_sum = dck + pk, dcv + pv, gate_sum + pg
-    (d_attn,) = whole_out
-    g_mlp = scatter_rows(mlp_part[0])
+    d_attn = whole_out[0]
     cap_sum = jnp.concatenate([dck, dcv], 1)
-    got_two = shift(cap_sum.astype(bf16), -2)
-    cap_sum = cap_sum + jnp.where(offset + 2 < length, got_two.astype(f32), 0.0)
-    got_one = shift(cap_sum.astype(bf16), -1)
-    cap_sum = jnp.where(offset == 0, cap_sum + jnp.where(offset + 1 < length, got_one.astype(f32), 0.0), 0.0)
+    cap_low = cap_sum.astype(bf16)
+    for by in range(1, SPAN):
+        cap_sum = cap_sum + jnp.where(by < length, shift(cap_low, -by).astype(f32), 0.0)
+    cap_sum = jnp.where(offset == 0, cap_sum, 0.0)
     last_half = pairs_of[-1]
-    for h in pairs_of:
-        after = () if h == 0 else (*d_got[last_half].first, got_two)
-        dqs[h] = dq_call(order, sc, q, d_scaled[2 * h], d_scaled[2 * h + 1], k_all, v_all, dq_caps[h], h, after)
+
+    def make_dq(h, after):
+        return dq_call(order, sc, q, d_scaled[h], k_all, v_all, dq_caps[h], h, after)
+
+    for h in pairs_of[:-1]:
+        dqs[h] = make_dq(h, ())
 
     d_cap, hs_c = order.run(
         "caption_grad",
@@ -1056,48 +1105,62 @@
         [whole_cap, whole_cap, whole_cap, whole(hg.shape)],
         [both_cap, pl.BlockSpec((1, n), lambda i: (0, 0))],
         [sds((text, 2 * n), bf16), sds((1, n), f32)],
-        after=d_got[last_half].second,
+        after=d_got[last_half].first,
     )
     d_text = (mm_nt(d_cap[:, :n], w_caption[0]) + mm_nt(d_cap[:, n:], w_caption[1])).astype(bf16)
     cap_part = mm_tn(captions, d_cap).astype(bf16)
-    g_cap = scatter_rows(cap_part)
     pieces = -(-d_text.shape[1] // d)
     padded = jnp.pad(d_text, ((0, 0), (0, pieces * d - d_text.shape[1])))
     text_parts = [padded[:, p * d : (p + 1) * d] for p in range(pieces)]
 
+    sums.add(("text", 0), text_parts[0])
+    dqs[last_half] = make_dq(last_half, (*d_got[last_half].second, *text_parts))
+    sums.add(("text", 1), text_parts[1], (cap_part,))
     ds = [x for h in pairs_of for x in pick(order, sc, d_got[h].pieces(), SPAN)]
-    sums.add(("text", 0), text_parts[0])
-    dkv = []
-    for p in range(n // 128):
-        dkv.append(dkv_call(order, sc, k, v, q_all, ds, p))
-        if p + 1 < pieces:
-            sums.add(("text", p + 1), text_parts[p + 1], (cap_part,) if p == 0 else ())
-    for p in range(n // 128 + 1, pieces):
-        sums.add(("text", p), text_parts[p])
     whole_out = ()
     c1 = hs_qk = 0.0
     mixed = jnp.concatenate([heads_out[c][0] for c in chunks[:half]] + [later[0]])
-    for c in chunks:
+    pairs = n // 128
+
+    def project(c, dkv, after=()):
+        nonlocal whole_out, c1, hs_qk
         da1_part, p_hs, p1, *whole_out = dqkv_call(order, c, dqs[c // 2], dkv, q_raw, k_raw, tabs, hg, w_qkv, patches, whole_out)
+        hs_qk, c1 = hs_qk + p_hs, c1 + p1
+        return da1_part
+
+    dkv = [dkv_call(order, sc, k, v, q_all, ds, 0, 0, pairs)]
+    for p in range(2, pieces):
+        sums.add(("text", p), text_parts[p])
+    g_cap = scatter_rows(pin(order, cap_part))
+    sums.add(("da1", 0), project(0, dkv), (g_mlp,))
+    da1_part = project(1, dkv)
+    dkv = [dkv_call(order, sc, k, v, q_all, ds, 1, 0, 1)]
+    sums.add(("da1", 1), da1_part)
+    dkv.append(dkv_call(order, sc, k, v, q_all, ds, 1, 1, pairs - 1))
+    for c in chunks[2:]:
+        da1_part = project(c, dkv)
         if c == chunks[-1]:
             (d_qkv,) = whole_out
             attn_part = pair_grad_call(order, a1, d_qkv, d_attn, mixed)[0]
-        sums.add(("da1", c), da1_part, (g_mlp,) if c == 0 else ())
-        hs_qk, c1 = hs_qk + p_hs, c1 + p1
-    g_attn = scatter_rows(attn_part)
-    whole_out = ()
-    for c in chunks:
-        whole_out = last_call(order, c, sums.get(("da1", c), (g_cap,)), patches, d_mids[c], vec, whole_out)
+        sums.add(("da1", c), da1_part)
+    g_attn = scatter_rows(pin(order, attn_part))
+
+    head_part = jnp.concatenate([hs_qk, hs_c]).reshape(3, heads, HD).sum(1)
+    gate_part = gate_sum[0, ::HD] * (1.0 - tg_heads * tg_heads)
+    got_narrow = gather_small(note(order, jnp.concatenate([c1[0], head_part.reshape(-1), gate_part])), "narrow")
+    whole_out = last_call(order, 0, sums.get(("da1", 0)), patches, d_mids[0], vec, ())
+    da1 = sums.get(("da1", 1), (g_cap, got_narrow))
+    summed = jnp.sum(got_narrow[:, : d + 3 * HD], 0)
+    sent = note(order, jnp.concatenate([summed, got_narrow[:, d + 3 * HD :].reshape(-1), c2[0], c3[0], c4[0]]))
+    got_wide = gather_small(sent, "wide")
+    whole_out = last_call(order, 1, da1, patches, d_mids[1], vec, whole_out)
+    da1 = sums.get(("da1", 2), (got_wide,))
+    for c in chunks[2:]:
+        whole_out = last_call(order, c, da1 if c == 2 else sums.get(("da1", c)), patches, d_mids[c], vec, whole_out)
     (grad_patches,) = whole_out
     grad_captions = jnp.concatenate([sums.get(("text", p)) for p in range(pieces)], 1)[:, : d_text.shape[1]]
 
-    head_part = jnp.concatenate([hs_qk, hs_c]).reshape(3, heads, HD).sum(1)
-    gate_part = gate_sum[0, ::HD] * (1.0 - tg_heads * tg_heads)
-    sent = jnp.concatenate([c1[0], head_part.reshape(-1), gate_part])
-    got = gather_small(sent, "narrow")
-    summed = jnp.sum(got[:, : d + 3 * HD], 0)
-    sent = jnp.concatenate([summed, got[:, d + 3 * HD :].reshape(-1), c2[0], c3[0], c4[0]])
-    got = gather_small(sent, "wide")
+    got = got_wide
     one, rest = got[:, :d], got[:, d:]
     grad_head_gains = jnp.sum(rest[:, : 3 * HD], 0).reshape(3, HD)
     grad_cross_gate = jnp.sum(rest[:, 3 * HD : 3 * HD + deep * heads], 0)

time: 1000 us -> 945 us (0.945)
  waiting for transfers between devices: 164 us -> 141 us
  Pallas kernels: 486 us -> 468 us
  starting transfers between devices: 160 us -> 150 us
    ppermute x4 -> x6, waiting for transfers between devices: 40.7 us -> 2.69 us  [shift(): lax.ppermute(x, 'wide', [(i, i + by) for i in range(size) if 0 <= i + by...]
    ppermute x21 -> x13, starting transfers between devices: 52.7 us -> 28.7 us  [__init__(): send = lambda x, pairs: lax.ppermute(x, 'wide', pairs)]
    ppermute x21 -> x13, waiting for transfers between devices: 34.7 us -> 57.6 us  [__init__(): send = lambda x, pairs: lax.ppermute(x, 'wide', pairs)]
    pallas_call x63 -> x68, Pallas kernels: 486 us -> 468 us  [run(): pl.pallas_call(body, grid_spec=pltpu.PrefetchScalarGridSpec(num_scalar_pr...]
    ppermute x42, waiting for transfers between devices: 80.5 us -> 69 us  [step(): go = lambda x, perm: lax.ppermute(x, 'narrow', perm)]
    ppermute x37 -> x29, starting transfers between devices: 20.4 us -> 26.7 us  [swap(): return lax.ppermute(x, axis, [(i, i ^ m) for i in range(size)])]
    unnamed x258 -> x213, local copies, waits for them, and re-layouts: 36.1 us -> 30 us
  transfers between devices with their start and end apart: 108 -> 94, of which waited for: 30 -> 24; matrix products, arithmetic and copies ran while one was open for 7% -> 9% of each run, Pallas kernels for 48% -> 45%
where the time goes in v6:
time: 945 us; the launch traced here: 929 us
  Pallas kernels  468 us (50%)
  starting transfers between devices  150 us (16%)
  waiting for transfers between devices  141 us (15%)
  local copies, waits for them, and re-layouts  51.1 us (5%)
  other arithmetic  48.9 us (5%)
  matrix products  24.3 us (3%)
  between operations  23 us (2%)
  blocking collectives  22.7 us (2%)
    pallas_call x68, Pallas kernels, run(): pl.pallas_call(body, grid_spec=pltpu.PrefetchScalarGridSpec(num_scalar_pr...  468 us
    ppermute x42, starting transfers between devices, step(): go = lambda x, perm: lax.ppermute(x, 'narrow', perm)  79.3 us
    ppermute x42, waiting for transfers between devices, step(): go = lambda x, perm: lax.ppermute(x, 'narrow', perm)  69 us
    ppermute x13, waiting for transfers between devices, __init__(): send = lambda x, pairs: lax.ppermute(x, 'wide', pairs)  57.6 us
    unnamed x213, local copies, waits for them, and re-layouts  30 us
    ppermute x13, starting transfers between devices, __init__(): send = lambda x, pairs: lax.ppermute(x, 'wide', pairs)  28.7 us
    ppermute x29, starting transfers between devices, swap(): return lax.ppermute(x, axis, [(i, i ^ m) for i in range(size)])  26.7 us
    all_gather x2, blocking collectives, gather_now(): lax.all_gather(padded, axis, axis=0, tiled=True).reshape(-1, wide)[:, :n]  22.7 us
  transfers between devices with their start and end apart: 94, of which 24 were waited for; matrix products, arithmetic and copies ran while one was open for 9% of the time, Pallas kernels for 45%

profile of v6, /device:TPU:0, one launch (start us, length us, event | category | flops | bytes accessed | tf_op | source)
XLA Modules:
  0.0 928.6 jit_solution(6398268142848624769)
XLA Ops:
  37.3 13.4 %all_gather.9 = f32[4,8,256]{2,1,0:T(8,128)S(1)} all-gather(f32[1,8,256]{2,1,0:T(8,128)S(1)} %reshape.354), channel_id=1, replica_groups=mesh['wide'=8,'narrow'=4] {'narrow'}, dimensions={0}, use_global_device_ids=true | all-gather | bytes 40960 | tf_op jit(solution)/shard_map/all_gather | solution.py:829
  50.7 9.3 %all_gather.10 = f32[8,8,896]{2,1,0:T(8,128)} all-gather(f32[1,8,896]{2,1,0:T(8,128)S(1)} %reshape.356), channel_id=1, replica_groups=mesh['wide'=8,'narrow'=4] {'wide'}, dimensions={0}, use_global_device_ids=true | all-gather | bytes 258048 | tf_op jit(solution)/shard_map/all_gather | solution.py:829
  73.2 9.0 key.1
  85.6 17.2 %collective-permute-done.6.refs_10_.refs_11_ = bf16[1024,384]{1,0:T(8,128)(2,1)S(1)} collective-permute-done((bf16[1024,384]{1,0:T(8,128)(2,1)}, bf16[1024,384]{1,0:T(8,128)(2,1)S(1)}, u32[]{:S(2)}, u32[]{:S(2)}) %collective-permute-start.6) | collective-permute-done | bytes 786464 | tf_op jit(solution)/shard_map/ppermute | solution.py:735
  109.0 10.2 %collective-permute-done.3.refs_7_.refs_3_ = bf16[1024,384]{1,0:T(8,128)(2,1)} collective-permute-done((bf16[1024,384]{1,0:T(8,128)(2,1)}, bf16[1024,384]{1,0:T(8,128)(2,1)}, u32[]{:S(2)}, u32[]{:S(2)}) %collective-permute-start.3) | collective-permute-done | bytes 786464 | tf_op jit(solution)/shard_map/ppermute | solution.py:735
  134.4 6.7 collective-permute-done.10.refs_7_
  145.7 7.0 query.1
  152.7 6.2 pick.3
  159.0 18.1 %attend.3 = (bf16[256,384]{1,0:T(8,128)(2,1)}, bf16[256,384]{1,0:T(8,128)(2,1)}, f32[256,384]{1,0:T(8,128)}) custom-call(s32[9]{0:T(128)} %pad_add_fusion.refs_0_, bf16[1024,384]{1,0:T(8,128)(2,1)} %get-tuple-element.186.refs_1_.refs_0_, bf16[4096,384]{1,0:T(8,128)(2,1)} %get-tuple-element.188.refs_2_.refs_7_.refs_4_, ...), custom_call_target="tpu_custom_call" | custom-call | flops 4499999744 | bytes 13500000 | tf_op jit(solution)/shard_map/attend/pallas_call | solution.py:51
  181.1 17.8 %attend.4 = (bf16[256,384]{1,0:T(8,128)(2,1)}, bf16[256,384]{1,0:T(8,128)(2,1)}, f32[256,384]{1,0:T(8,128)}) custom-call(s32[9]{0:T(128)} %pad_add_fusion.refs_0_, bf16[1024,384]{1,0:T(8,128)(2,1)} %get-tuple-element.186.refs_1_.refs_0_, bf16[4096,384]{1,0:T(8,128)(2,1)} %get-tuple-element.188.refs_2_.refs_7_.refs_4_, ...), custom_call_target="tpu_custom_call" | custom-call | flops 4499999744 | bytes 13500000 | tf_op jit(solution)/shard_map/attend/pallas_call | solution.py:51
  205.9 22.1 %attend.5 = (bf16[512,384]{1,0:T(8,128)(2,1)}, bf16[512,384]{1,0:T(8,128)(2,1)}, f32[512,384]{1,0:T(8,128)}) custom-call(s32[9]{0:T(128)} %pad_add_fusion.refs_0_, bf16[1024,384]{1,0:T(8,128)(2,1)} %get-tuple-element.186.refs_1_.refs_0_, bf16[4096,384]{1,0:T(8,128)(2,1)} %get-tuple-element.188.refs_2_.refs_7_.refs_4_, ...), custom_call_target="tpu_custom_call" | custom-call | flops 4499999744 | bytes 13500000 | tf_op jit(solution)/shard_map/attend/pallas_call | solution.py:51
  239.4 15.8 %collective-permute-done.21.refs_1_ = bf16[256,1536]{1,0:T(8,128)(2,1)S(1)} collective-permute-done((bf16[256,1536]{1,0:T(8,128)(2,1)}, bf16[256,1536]{1,0:T(8,128)(2,1)S(1)}, u32[]{:S(2)}, u32[]{:S(2)}) %collective-permute-start.21) | collective-permute-done | bytes 786464 | tf_op jit(solution)/shard_map/ppermute | solution.py:859
  264.2 8.5 ffn.4
  272.6 7.8 collective-permute-done.23.refs_1_
  289.2 8.5 ffn.5
  297.7 7.1 collective-permute-done.25.refs_1_
  313.5 8.5 ffn.6
  322.0 6.2 collective-permute-done.27.refs_1_
  336.9 8.5 ffn.7
  359.7 9.6 %ffn_back.4 = (bf16[256,1536]{1,0:T(8,128)(2,1)}, f32[1,1536]{1,0:T(1,128)}, bf16[1024,1536]{1,0:T(8,128)(2,1)}, bf16[1024,1536]{1,0:T(8,128)(2,1)}, bf16[1024,2048]{1,0:T(8,128)(2,1)}) custom-call(bf16[256,1536]{1,0:T(8,128)(2,1)} %get-tuple-element.225.refs_0_.refs_7_, f32[256,1536]{1,0:T(8,128)} %get-tuple-element.201.refs_7_.refs_1_, ...), custom_call_target="tpu_custom_call" | custom-call | flops 2500000000 | bytes 7500000 | tf_op jit(solution)/shard_map/ffn_back/pallas_call | solution.py:51
  380.8 9.6 %ffn_back.5 = (bf16[256,1536]{1,0:T(8,128)(2,1)}, f32[1,1536]{1,0:T(1,128)}, bf16[1024,1536]{1,0:T(8,128)(2,1)}, bf16[1024,1536]{1,0:T(8,128)(2,1)}, bf16[1024,2048]{1,0:T(8,128)(2,1)}) custom-call(bf16[256,1536]{1,0:T(8,128)(2,1)} %get-tuple-element.230.refs_0_.refs_7_, ...), custom_call_target="tpu_custom_call", output_to_operand_aliasing={{2}: (8, {}), {3}: (9, {}), {4}: (10, {})} | custom-call | flops 2500000000 | bytes 7500000 | tf_op jit(solution)/shard_map/ffn_back/pallas_call | solution.py:51
  401.5 9.6 %ffn_back.6 = (bf16[256,1536]{1,0:T(8,128)(2,1)}, f32[1,1536]{1,0:T(1,128)}, bf16[1024,1536]{1,0:T(8,128)(2,1)}, bf16[1024,1536]{1,0:T(8,128)(2,1)}, bf16[1024,2048]{1,0:T(8,128)(2,1)}) custom-call(bf16[256,1536]{1,0:T(8,128)(2,1)} %get-tuple-element.238.refs_0_.refs_7_, ...), custom_call_target="tpu_custom_call", output_to_operand_aliasing={{2}: (8, {}), {3}: (9, {}), {4}: (10, {})} | custom-call | flops 2500000000 | bytes 7500000 | tf_op jit(solution)/shard_map/ffn_back/pallas_call | solution.py:51
  421.4 9.5 %ffn_back.7 = (bf16[256,1536]{1,0:T(8,128)(2,1)}, f32[1,1536]{1,0:T(1,128)}, bf16[1024,1536]{1,0:T(8,128)(2,1)}, bf16[1024,1536]{1,0:T(8,128)(2,1)}, bf16[1024,2048]{1,0:T(8,128)(2,1)}) custom-call(bf16[256,1536]{1,0:T(8,128)(2,1)} %get-tuple-element.244.refs_0_.refs_7_, ...), custom_call_target="tpu_custom_call", output_to_operand_aliasing={{2}: (8, {}), {3}: (9, {}), {4}: (10, {})} | custom-call | flops 2500000000 | bytes 7500000 | tf_op jit(solution)/shard_map/ffn_back/pallas_call | solution.py:51
  440.0 5.6 out_back.4
  445.6 9.9 %pair_grad.3.refs_6_.refs_7_ = bf16[1536,3072]{1,0:T(8,128)(2,1)} custom-call(bf16[1024,1536]{1,0:T(8,128)(2,1)} %get-tuple-element.259.refs_0_, bf16[1024,2048]{1,0:T(8,128)(2,1)} %get-tuple-element.260.refs_1_, bf16[1024,1536]{1,0:T(8,128)(2,1)} %get-tuple-element.261.refs_2_, bf16[1024,1024]{1,0:T(8,128)(2,1)} %get-tuple-element.262.refs_3_, ...), custom_call_target="tpu_custom_call" | custom-call | flops 2500000000 | bytes 7500000 | tf_op jit(solution)/shard_map/pair_grad/pallas_call | solution.py:51
  463.9 5.6 out_back.5
  469.6 5.5 caption_back.2
  482.4 6.0 collective-permute-start.46
  488.4 5.6 out_back.6
  494.9 9.9 %pair_grad.4.refs_3_.refs_1_ = bf16[1536,3072]{1,0:T(8,128)(2,1)} custom-call(bf16[1024,1536]{1,0:T(8,128)(2,1)} %get-tuple-element.259.refs_0_, bf16[1024,2048]{1,0:T(8,128)(2,1)} %get-tuple-element.260.refs_1_, bf16[1024,1536]{1,0:T(8,128)(2,1)} %get-tuple-element.261.refs_2_, ...), custom_call_target="tpu_custom_call", output_to_operand_aliasing={{}: (7, {})} | custom-call | flops 2500000000 | bytes 7500000 | tf_op jit(solution)/shard_map/pair_grad/pallas_call | solution.py:51
  510.6 6.5 out_back.7
  517.1 5.7 caption_back.3
  533.4 26.7 %dq.2.refs_4_.refs_0_ = f32[512,384]{1,0:T(8,128)} custom-call(s32[9]{0:T(128)} %pad_add_fusion.refs_0_, bf16[1024,384]{1,0:T(8,128)(2,1)} %get-tuple-element.186.refs_1_.refs_0_, bf16[512,512]{1,0:T(8,128)(2,1)} %get-tuple-element.282.refs_2_.refs_3_.refs_1_, bf16[512,512]{1,0:T(8,128)(2,1)} %get-tuple-element.282.refs_2_.refs_3_.refs_1_, ...), custom_call_target="tpu_custom_call" | custom-call | flops 6750000128 | bytes 20250000 | tf_op jit(solution)/shard_map/dq/pallas_call | solution.py:51
  563.9 11.2 %collective-permute-done.50.refs_5_.refs_3_ = bf16[512,512]{1,0:T(8,128)(2,1)S(1)} collective-permute-done((bf16[512,512]{1,0:T(8,128)(2,1)S(1)}, bf16[512,512]{1,0:T(8,128)(2,1)S(1)}, u32[]{:S(2)}, u32[]{:S(2)}) %collective-permute-start.50) | collective-permute-done | bytes 524320 | tf_op jit(solution)/shard_map/ppermute | solution.py:758
  586.9 8.2 collective-permute-start.56
  602.9 7.6 collective-permute-done.53.refs_8_.refs_7_
  611.2 26.7 %dq.3.refs_4_.refs_0_ = f32[512,384]{1,0:T(8,128)} custom-call(s32[9]{0:T(128)} %pad_add_fusion.refs_0_, bf16[1024,384]{1,0:T(8,128)(2,1)} %get-tuple-element.186.refs_1_.refs_0_, bf16[512,512]{1,0:T(8,128)(2,1)} %get-tuple-element.291.refs_2_.refs_3_.refs_1_, bf16[512,512]{1,0:T(8,128)(2,1)} %get-tuple-element.291.refs_2_.refs_3_.refs_1_, ...), custom_call_target="tpu_custom_call" | custom-call | flops 6750000128 | bytes 20250000 | tf_op jit(solution)/shard_map/dq/pallas_call | solution.py:51
  652.8 32.5 %dkv.3 = (f32[512,384]{1,0:T(8,128)}, f32[512,384]{1,0:T(8,128)}) custom-call(s32[9]{0:T(128)} %pad_add_fusion.refs_0_, bf16[1024,384]{1,0:T(8,128)(2,1)} %get-tuple-element.184.refs_1_, bf16[1024,384]{1,0:T(8,128)(2,1)} %get-tuple-element.185.refs_9_.refs_2_, bf16[8192,384]{1,0:T(8,128)(2,1)} %all-gather.2.cloned.1.call-done.refs_3_, ...), custom_call_target="tpu_custom_call" | custom-call | flops 6000000000 | bytes 18000000 | tf_op jit(solution)/shard_map/dkv/pallas_call | solution.py:51
  706.8 6.6 dqkv.4
  722.8 6.7 dqkv.5
  729.5 12.5 %dkv.4 = (f32[512,128]{1,0:T(8,128)}, f32[512,128]{1,0:T(8,128)}) custom-call(s32[9]{0:T(128)} %pad_add_fusion.refs_0_, bf16[1024,384]{1,0:T(8,128)(2,1)} %get-tuple-element.184.refs_1_, bf16[1024,384]{1,0:T(8,128)(2,1)} %get-tuple-element.185.refs_9_.refs_2_, bf16[8192,384]{1,0:T(8,128)(2,1)} %all-gather.2.cloned.1.call-done.refs_3_, ...), custom_call_target="tpu_custom_call" | custom-call | flops 6000000000 | bytes 18000000 | tf_op jit(solution)/shard_map/dkv/pallas_call | solution.py:51
  755.8 22.6 %dkv.5 = (f32[512,256]{1,0:T(8,128)}, f32[512,256]{1,0:T(8,128)}) custom-call(s32[9]{0:T(128)} %pad_add_fusion.refs_0_, bf16[1024,384]{1,0:T(8,128)(2,1)} %get-tuple-element.184.refs_1_, bf16[1024,384]{1,0:T(8,128)(2,1)} %get-tuple-element.185.refs_9_.refs_2_, bf16[8192,384]{1,0:T(8,128)(2,1)} %all-gather.2.cloned.1.call-done.refs_3_, ...), custom_call_target="tpu_custom_call" | custom-call | flops 6000000000 | bytes 18000000 | tf_op jit(solution)/shard_map/dkv/pallas_call | solution.py:51
  778.4 6.5 dqkv.6
  792.1 6.6 dqkv.7
  798.7 10.9 %pair_grad.5.refs_7_.refs_1_ = bf16[1536,1536]{1,0:T(8,128)(2,1)} custom-call(bf16[1024,1536]{1,0:T(8,128)(2,1)} %get-tuple-element.183.refs_0_.refs_6_, bf16[1024,1152]{1,0:T(8,128)(2,1)} %get-tuple-element.320.refs_1_, bf16[1024,1536]{1,0:T(8,128)(2,1)} %get-tuple-element.321.refs_2_, bf16[1024,384]{1,0:T(8,128)(2,1)} %pad_maximum_fusion.3.refs_3_, ...), custom_call_target="tpu_custom_call" | custom-call | flops 2500000000 | bytes 7500000 | tf_op jit(solution)/shard_map/pair_grad/pallas_call | solution.py:51
  838.6 5.5 collective-permute-done.74
  878.5 6.9 collective-permute-done.77.refs_1_
  899.5 9.6 %collective-permute-done.86.refs_1_ = bf16[256,1536]{1,0:T(8,128)(2,1)S(1)} collective-permute-done((bf16[256,1536]{1,0:T(8,128)(2,1)}, bf16[256,1536]{1,0:T(8,128)(2,1)S(1)}, u32[]{:S(2)}, u32[]{:S(2)}) %collective-permute-start.86) | collective-permute-done | bytes 786464 | tf_op jit(solution)/shard_map/ppermute | solution.py:859
  (543 shorter events, 391.8 us)
Async XLA Ops:
  7.2 645.6 %all-gather.2.cloned.1.call-start = ((), (), s32[]{:S(2)}) async-start(), calls=%async_computation.3 | async-start | bytes 7077888 | tf_op jit(solution)/shard_map/all_gather | solution.py:1030
  16.6 55.5 %collective-permute-start = (bf16[256,768]{1,0:T(8,128)(2,1)}, bf16[256,768]{1,0:T(8,128)(2,1)S(1)}, u32[]{:S(2)}, u32[]{:S(2)}) collective-permute-start(bf16[256,768]{1,0:T(8,128)(2,1)} %caption_norm.1.refs_8_), channel_id=1, source_target_pairs={{0,4},{4,8},{8,12},{12,16},{16,20},{20,24},{24,28},{1,5},{5,9},{9,... | collective-permute-start | bytes 1179656 | tf_op jit(solution)/shard_map/ppermute | solution.py:770
  18.9 53.2 %collective-permute-start.1 = (bf16[256,768]{1,0:T(8,128)(2,1)}, bf16[256,768]{1,0:T(8,128)(2,1)S(1)}, u32[]{:S(2)}, u32[]{:S(2)}) collective-permute-start(bf16[256,768]{1,0:T(8,128)(2,1)} %caption_norm.1.refs_8_), channel_id=1, source_target_pairs={{0,8},{4,12},{8,16},{12,20},{16,24},{20,28},{1,9},{5,13},{9,17},{1... | collective-permute-start | bytes 1179656 | tf_op jit(solution)/shard_map/ppermute | solution.py:770
  23.4 48.8 %collective-permute-start.2 = (bf16[256,768]{1,0:T(8,128)(2,1)}, bf16[256,768]{1,0:T(8,128)(2,1)S(1)}, u32[]{:S(2)}, u32[]{:S(2)}) collective-permute-start(bf16[256,768]{1,0:T(8,128)(2,1)} %caption_norm.1.refs_8_), channel_id=1, source_target_pairs={{0,12},{4,16},{8,20},{12,24},{16,28},{1,13},{5,17},{9,21},{13,25},... | collective-permute-start | bytes 1179656 | tf_op jit(solution)/shard_map/ppermute | solution.py:770
  82.2 20.6 %collective-permute-start.6 = (bf16[1024,384]{1,0:T(8,128)(2,1)}, bf16[1024,384]{1,0:T(8,128)(2,1)S(1)}, u32[]{:S(2)}, u32[]{:S(2)}) collective-permute-start(bf16[1024,384]{1,0:T(8,128)(2,1)} %get-tuple-element.185.refs_9_.refs_2_), channel_id=1, source_target_pairs={{0,8},{4,12},{8,0},{12,4},{16,24},{20,28},{24,16},{28,20},{1,9},{5... | collective-permute-start | bytes 2359304 | tf_op jit(solution)/shard_map/ppermute | solution.py:735
  83.7 22.5 %collective-permute-start.5 = (bf16[1024,384]{1,0:T(8,128)(2,1)}, bf16[1024,384]{1,0:T(8,128)(2,1)S(1)}, u32[]{:S(2)}, u32[]{:S(2)}) collective-permute-start(bf16[1024,384]{1,0:T(8,128)(2,1)} %get-tuple-element.185.refs_9_.refs_2_), channel_id=1, source_target_pairs={{4,20},{16,0},{12,28},{24,8},{5,21},{17,1},{13,29},{25,9},{6,22},{... | collective-permute-start | bytes 2359304 | tf_op jit(solution)/shard_map/ppermute | solution.py:735
  85.0 34.2 %collective-permute-start.3 = (bf16[1024,384]{1,0:T(8,128)(2,1)}, bf16[1024,384]{1,0:T(8,128)(2,1)}, u32[]{:S(2)}, u32[]{:S(2)}) collective-permute-start(bf16[1024,384]{1,0:T(8,128)(2,1)} %get-tuple-element.184.refs_1_), channel_id=1, source_target_pairs={{0,8},{4,12},{8,0},{12,4},{16,24},{20,28},{24,16},{28,20},{1,9},{5... | collective-permute-start | bytes 2359304 | tf_op jit(solution)/shard_map/ppermute | solution.py:735
  102.8 21.0 %collective-permute-start.15 = (bf16[1024,384]{1,0:T(8,128)(2,1)S(1)}, bf16[1024,384]{1,0:T(8,128)(2,1)S(1)}, u32[]{:S(2)}, u32[]{:S(2)}) collective-permute-start(bf16[1024,384]{1,0:T(8,128)(2,1)S(1)} %collective-permute-done.6.refs_10_.refs_11_), channel_id=1, source_target_pairs={{0,16},{28,12},{1,17},{29,13},{2,18},{30,14},{3,19},{31,15}} | collective-permute-start | bytes 2359304 | tf_op jit(solution)/shard_map/ppermute | solution.py:735
  106.3 23.0 %collective-permute-start.16 = (bf16[1024,384]{1,0:T(8,128)(2,1)S(1)}, bf16[1024,384]{1,0:T(8,128)(2,1)S(1)}, u32[]{:S(2)}, u32[]{:S(2)}) collective-permute-start(bf16[1024,384]{1,0:T(8,128)(2,1)S(1)} %collective-permute-done.5.refs_9_.refs_13_), channel_id=1, source_target_pairs={{28,20},{0,8},{29,21},{1,9},{30,22},{2,10},{31,23},{3,11}} | collective-permute-start | bytes 2359304 | tf_op jit(solution)/shard_map/ppermute | solution.py:735
  107.6 25.7 %collective-permute-start.4 = (bf16[1024,384]{1,0:T(8,128)(2,1)}, bf16[1024,384]{1,0:T(8,128)(2,1)}, u32[]{:S(2)}, u32[]{:S(2)}) collective-permute-start(bf16[1024,384]{1,0:T(8,128)(2,1)} %get-tuple-element.184.refs_1_), channel_id=1, source_target_pairs={{4,20},{16,0},{12,28},{24,8},{5,21},{17,1},{13,29},{25,9},{6,22},{... | collective-permute-start | bytes 2359304 | tf_op jit(solution)/shard_map/ppermute | solution.py:735
  108.9 24.9 %collective-permute-start.12 = (bf16[1024,384]{1,0:T(8,128)(2,1)}, bf16[1024,384]{1,0:T(8,128)(2,1)}, u32[]{:S(2)}, u32[]{:S(2)}) collective-permute-start(bf16[1024,384]{1,0:T(8,128)(2,1)} %get-tuple-element.185.refs_9_.refs_2_), channel_id=1, source_target_pairs={{0,4},{4,0},{8,12},{12,8},{16,20},{20,16},{24,28},{28,24},{1,5},{5... | collective-permute-start | bytes 2359304 | tf_op jit(solution)/shard_map/ppermute | solution.py:706
  179.5 21.7 %collective-permute-start.18 = (bf16[256,1536]{1,0:T(8,128)(2,1)}, bf16[256,1536]{1,0:T(8,128)(2,1)}, u32[]{:S(2)}, u32[]{:S(2)}) collective-permute-start(bf16[256,1536]{1,0:T(8,128)(2,1)} %convolution_convert_fusion.4.refs_2_), channel_id=1, source_target_pairs={{0,1},{3,2},{1,0},{2,3},{4,5},{7,6},{5,4},{6,7},{8,9},{11,10},{9,8... | collective-permute-start | bytes 2359304 | tf_op jit(solution)/shard_map/ppermute | solution.py:859
  203.7 26.7 %collective-permute-start.19 = (bf16[256,1536]{1,0:T(8,128)(2,1)}, bf16[256,1536]{1,0:T(8,128)(2,1)}, u32[]{:S(2)}, u32[]{:S(2)}) collective-permute-start(bf16[256,1536]{1,0:T(8,128)(2,1)} %get-tuple-element.192), channel_id=1, source_target_pairs={{0,1},{3,2},{1,0},{2,3},{4,5},{7,6},{5,4},{6,7},{8,9},{11,10},{9,8... | collective-permute-start | bytes 2359304 | tf_op jit(solution)/shard_map/ppermute | solution.py:859
  204.3 26.1 %collective-permute-start.20 = (bf16[256,1536]{1,0:T(8,128)(2,1)}, bf16[256,1536]{1,0:T(8,128)(2,1)}, u32[]{:S(2)}, u32[]{:S(2)}) collective-permute-start(bf16[256,1536]{1,0:T(8,128)(2,1)} %get-tuple-element.193.refs_7_.refs_3_), channel_id=1, source_target_pairs={{1,2},{2,1},{5,6},{6,5},{9,10},{10,9},{13,14},{14,13},{17,18},{18,... | collective-permute-start | bytes 2359304 | tf_op jit(solution)/shard_map/ppermute | solution.py:859
  205.8 510.9 %reduce-scatter.4.cloned.1.call-start = ((), (), s32[]{:S(2)}) async-start(), calls=%async_computation.4 | async-start | bytes 10616832 | tf_op jit(solution)/shard_map/reduce_scatter | solution.py:921
  233.9 21.3 %collective-permute-start.21 = (bf16[256,1536]{1,0:T(8,128)(2,1)}, bf16[256,1536]{1,0:T(8,128)(2,1)S(1)}, u32[]{:S(2)}, u32[]{:S(2)}) collective-permute-start(bf16[256,1536]{1,0:T(8,128)(2,1)} %get-tuple-element.195.refs_2_), channel_id=1, source_target_pairs={{0,1},{3,2},{1,0},{2,3},{4,5},{7,6},{5,4},{6,7},{8,9},{11,10},{9,8... | collective-permute-start | bytes 2359304 | tf_op jit(solution)/shard_map/ppermute | solution.py:859
  260.5 20.0 %collective-permute-start.23 = (bf16[256,1536]{1,0:T(8,128)(2,1)}, bf16[256,1536]{1,0:T(8,128)(2,1)S(1)}, u32[]{:S(2)}, u32[]{:S(2)}) collective-permute-start(bf16[256,1536]{1,0:T(8,128)(2,1)} %get-tuple-element.197.refs_2_), channel_id=1, source_target_pairs={{0,1},{3,2},{1,0},{2,3},{4,5},{7,6},{5,4},{6,7},{8,9},{11,10},{9,8... | collective-permute-start | bytes 2359304 | tf_op jit(solution)/shard_map/ppermute | solution.py:859
  479.1 25.6 %collective-permute-start.43 = (bf16[256,1536]{1,0:T(8,128)(2,1)}, bf16[256,1536]{1,0:T(8,128)(2,1)S(1)}, u32[]{:S(2)}, u32[]{:S(2)}) collective-permute-start(bf16[256,1536]{1,0:T(8,128)(2,1)} %get-tuple-element.280.refs_2_), channel_id=1, source_target_pairs={{0,1},{3,2},{1,0},{2,3},{4,5},{7,6},{5,4},{6,7},{8,9},{11,10},{9,8... | collective-permute-start | bytes 2359304 | tf_op jit(solution)/shard_map/ppermute | solution.py:859
  482.4 22.3 %collective-permute-start.46 = (bf16[512,512]{1,0:T(8,128)(2,1)S(1)}, bf16[512,512]{1,0:T(8,128)(2,1)S(1)}, u32[]{:S(2)}, u32[]{:S(2)}) collective-permute-start(bf16[512,512]{1,0:T(8,128)(2,1)S(1)} %collective-permute-done.44.refs_5_.refs_3_), channel_id=1, source_target_pairs={{0,16},{4,20},{24,8},{28,12},{1,17},{5,21},{25,9},{29,13},{2,18},{... | collective-permute-start | bytes 1572872 | tf_op jit(solution)/shard_map/ppermute | solution.py:758
  508.6 244.7 %reduce-scatter.6.cloned.1.call-start = ((), (), s32[]{:S(2)}) async-start(), calls=%async_computation.5 | async-start | bytes 7077888 | tf_op jit(solution)/shard_map/reduce_scatter | solution.py:921
  525.0 35.0 %collective-permute-start.47 = (bf16[256,768]{1,0:T(8,128)(2,1)S(1)}, bf16[256,768]{1,0:T(8,128)(2,1)S(1)}, u32[]{:S(2)}, u32[]{:S(2)}) collective-permute-start(bf16[256,768]{1,0:T(8,128)(2,1)S(1)} %fusion.14), channel_id=1, source_target_pairs={{4,0},{8,4},{12,8},{16,12},{20,16},{24,20},{28,24},{5,1},{9,5},{13... | collective-permute-start | bytes 1179656 | tf_op jit(solution)/shard_map/ppermute | solution.py:770
  526.4 33.7 %collective-permute-start.48 = (bf16[256,768]{1,0:T(8,128)(2,1)S(1)}, bf16[256,768]{1,0:T(8,128)(2,1)S(1)}, u32[]{:S(2)}, u32[]{:S(2)}) collective-permute-start(bf16[256,768]{1,0:T(8,128)(2,1)S(1)} %fusion.14), channel_id=1, source_target_pairs={{8,0},{12,4},{16,8},{20,12},{24,16},{28,20},{9,1},{13,5},{17,9},{2... | collective-permute-start | bytes 1179656 | tf_op jit(solution)/shard_map/ppermute | solution.py:770
  527.6 35.1 %collective-permute-start.49 = (bf16[256,768]{1,0:T(8,128)(2,1)S(1)}, bf16[256,768]{1,0:T(8,128)(2,1)S(1)}, u32[]{:S(2)}, u32[]{:S(2)}) collective-permute-start(bf16[256,768]{1,0:T(8,128)(2,1)S(1)} %fusion.14), channel_id=1, source_target_pairs={{12,0},{16,4},{20,8},{24,12},{28,16},{13,1},{17,5},{21,9},{25,13},... | collective-permute-start | bytes 1179656 | tf_op jit(solution)/shard_map/ppermute | solution.py:770
  529.0 46.2 %collective-permute-start.50 = (bf16[512,512]{1,0:T(8,128)(2,1)S(1)}, bf16[512,512]{1,0:T(8,128)(2,1)S(1)}, u32[]{:S(2)}, u32[]{:S(2)}) collective-permute-start(bf16[512,512]{1,0:T(8,128)(2,1)S(1)} %copy-done.20), channel_id=1, source_target_pairs={{0,8},{4,12},{8,0},{12,4},{16,24},{20,28},{24,16},{28,20},{1,9},{5... | collective-permute-start | bytes 1572872 | tf_op jit(solution)/shard_map/ppermute | solution.py:758
  531.7 43.5 %collective-permute-start.51 = (bf16[512,512]{1,0:T(8,128)(2,1)S(1)}, bf16[512,512]{1,0:T(8,128)(2,1)S(1)}, u32[]{:S(2)}, u32[]{:S(2)}) collective-permute-start(bf16[512,512]{1,0:T(8,128)(2,1)S(1)} %copy-done.20), channel_id=1, source_target_pairs={{4,20},{16,0},{12,28},{24,8},{5,21},{17,1},{13,29},{25,9},{6,22},{... | collective-permute-start | bytes 1572872 | tf_op jit(solution)/shard_map/ppermute | solution.py:758
  586.9 23.6 %collective-permute-start.52 = (bf16[256,1536]{1,0:T(8,128)(2,1)S(1)}, bf16[256,1536]{1,0:T(8,128)(2,1)S(1)}, u32[]{:S(2)}, u32[]{:S(2)}) collective-permute-start(bf16[256,1536]{1,0:T(8,128)(2,1)S(1)} %get-tuple-element.399.refs_9_.refs_2_), channel_id=1, source_target_pairs={{0,1},{3,2},{1,0},{2,3},{4,5},{7,6},{5,4},{6,7},{8,9},{11,10},{9,8... | collective-permute-start | bytes 2359304 | tf_op jit(solution)/shard_map/ppermute | solution.py:859
  602.2 38.3 %collective-permute-start.59 = (bf16[512,512]{1,0:T(8,128)(2,1)S(1)}, bf16[512,512]{1,0:T(8,128)(2,1)S(1)}, u32[]{:S(2)}, u32[]{:S(2)}) collective-permute-start(bf16[512,512]{1,0:T(8,128)(2,1)S(1)} %copy-done.15), channel_id=1, source_target_pairs={{0,4},{4,0},{8,12},{12,8},{16,20},{20,16},{24,28},{28,24},{1,5},{5... | collective-permute-start | bytes 1572872 | tf_op jit(solution)/shard_map/ppermute | solution.py:706
  602.4 39.9 %collective-permute-start.60 = (bf16[512,512]{1,0:T(8,128)(2,1)S(1)}, bf16[512,512]{1,0:T(8,128)(2,1)S(1)}, u32[]{:S(2)}, u32[]{:S(2)}) collective-permute-start(bf16[512,512]{1,0:T(8,128)(2,1)S(1)} %copy-done.20), channel_id=1, source_target_pairs={{0,4},{4,0},{8,12},{12,8},{16,20},{20,16},{24,28},{28,24},{1,5},{5... | collective-permute-start | bytes 1572872 | tf_op jit(solution)/shard_map/ppermute | solution.py:706
  602.8 44.8 %collective-permute-start.61 = (bf16[512,512]{1,0:T(8,128)(2,1)S(1)}, bf16[512,512]{1,0:T(8,128)(2,1)S(1)}, u32[]{:S(2)}, u32[]{:S(2)}) collective-permute-start(bf16[512,512]{1,0:T(8,128)(2,1)S(1)} %copy-done.17), channel_id=1, source_target_pairs={{0,4},{4,0},{8,12},{12,8},{16,20},{20,16},{24,28},{28,24},{1,5},{5... | collective-permute-start | bytes 1572872 | tf_op jit(solution)/shard_map/ppermute | solution.py:706
  610.6 37.1 %collective-permute-start.62 = (bf16[512,512]{1,0:T(8,128)(2,1)S(1)}, bf16[512,512]{1,0:T(8,128)(2,1)}, u32[]{:S(2)}, u32[]{:S(2)}) collective-permute-start(bf16[512,512]{1,0:T(8,128)(2,1)S(1)} %copy-done.19), channel_id=1, source_target_pairs={{0,4},{4,0},{8,12},{12,8},{16,20},{20,16},{24,28},{28,24},{1,5},{5... | collective-permute-start | bytes 1572872 | tf_op jit(solution)/shard_map/ppermute | solution.py:706
  610.6 37.1 %collective-permute-start.63 = (bf16[512,512]{1,0:T(8,128)(2,1)}, bf16[512,512]{1,0:T(8,128)(2,1)S(1)}, u32[]{:S(2)}, u32[]{:S(2)}) collective-permute-start(bf16[512,512]{1,0:T(8,128)(2,1)} %collective-permute-done.53.refs_8_.refs_7_), channel_id=1, source_target_pairs={{0,4},{4,0},{8,12},{12,8},{16,20},{20,16},{24,28},{28,24},{1,5},{5... | collective-permute-start | bytes 1572872 | tf_op jit(solution)/shard_map/ppermute | solution.py:706
  640.5 44.9 %collective-permute-start.54 = (bf16[256,1536]{1,0:T(8,128)(2,1)}, bf16[256,1536]{1,0:T(8,128)(2,1)S(1)}, u32[]{:S(2)}, u32[]{:S(2)}) collective-permute-start(bf16[256,1536]{1,0:T(8,128)(2,1)} %get-tuple-element.293), channel_id=1, source_target_pairs={{0,1},{3,2},{1,0},{2,3},{4,5},{7,6},{5,4},{6,7},{8,9},{11,10},{9,8... | collective-permute-start | bytes 2359304 | tf_op jit(solution)/shard_map/ppermute | solution.py:859
  642.3 43.1 %collective-permute-start.55 = (bf16[256,1536]{1,0:T(8,128)(2,1)}, bf16[256,1536]{1,0:T(8,128)(2,1)}, u32[]{:S(2)}, u32[]{:S(2)}) collective-permute-start(bf16[256,1536]{1,0:T(8,128)(2,1)} %get-tuple-element.294.refs_9_.refs_3_), channel_id=1, source_target_pairs={{1,2},{2,1},{5,6},{6,5},{9,10},{10,9},{13,14},{14,13},{17,18},{18,... | collective-permute-start | bytes 2359304 | tf_op jit(solution)/shard_map/ppermute | solution.py:859
  689.4 226.2 %reduce-scatter.8.cloned.1.call-start = ((), (), s32[]{:S(2)}) async-start(), calls=%async_computation.6 | async-start | bytes 5308416 | tf_op jit(solution)/shard_map/reduce_scatter | solution.py:921
  694.0 22.8 %collective-permute-start.65 = (bf16[256,1536]{1,0:T(8,128)(2,1)S(1)}, bf16[256,1536]{1,0:T(8,128)(2,1)}, u32[]{:S(2)}, u32[]{:S(2)}) collective-permute-start(bf16[256,1536]{1,0:T(8,128)(2,1)S(1)} %copy-done.8), channel_id=1, source_target_pairs={{1,2},{2,1},{5,6},{6,5},{9,10},{10,9},{13,14},{14,13},{17,18},{18,... | collective-permute-start | bytes 2359304 | tf_op jit(solution)/shard_map/ppermute | solution.py:859
  695.6 21.2 %collective-permute-start.64 = (bf16[256,1536]{1,0:T(8,128)(2,1)}, bf16[256,1536]{1,0:T(8,128)(2,1)}, u32[]{:S(2)}, u32[]{:S(2)}) collective-permute-start(bf16[256,1536]{1,0:T(8,128)(2,1)} %get-tuple-element.296.refs_2_), channel_id=1, source_target_pairs={{0,1},{3,2},{1,0},{2,3},{4,5},{7,6},{5,4},{6,7},{8,9},{11,10},{9,8... | collective-permute-start | bytes 2359304 | tf_op jit(solution)/shard_map/ppermute | solution.py:859
  720.3 21.8 %collective-permute-start.66 = (bf16[256,1536]{1,0:T(8,128)(2,1)}, bf16[256,1536]{1,0:T(8,128)(2,1)S(1)}, u32[]{:S(2)}, u32[]{:S(2)}) collective-permute-start(bf16[256,1536]{1,0:T(8,128)(2,1)} %get-tuple-element.301.refs_2_), channel_id=1, source_target_pairs={{0,1},{3,2},{1,0},{2,3},{4,5},{7,6},{5,4},{6,7},{8,9},{11,10},{9,8... | collective-permute-start | bytes 2359304 | tf_op jit(solution)/shard_map/ppermute | solution.py:859
  722.0 20.0 %collective-permute-start.67 = (bf16[256,1536]{1,0:T(8,128)(2,1)}, bf16[256,1536]{1,0:T(8,128)(2,1)S(1)}, u32[]{:S(2)}, u32[]{:S(2)}) collective-permute-start(bf16[256,1536]{1,0:T(8,128)(2,1)} %get-tuple-element.302.refs_4_), channel_id=1, source_target_pairs={{1,2},{2,1},{5,6},{6,5},{9,10},{10,9},{13,14},{14,13},{17,18},{18,... | collective-permute-start | bytes 2359304 | tf_op jit(solution)/shard_map/ppermute | solution.py:859
  746.6 38.3 %collective-permute-start.68 = (bf16[256,1536]{1,0:T(8,128)(2,1)}, bf16[256,1536]{1,0:T(8,128)(2,1)}, u32[]{:S(2)}, u32[]{:S(2)}) collective-permute-start(bf16[256,1536]{1,0:T(8,128)(2,1)} %get-tuple-element.307.refs_2_), channel_id=1, source_target_pairs={{0,1},{3,2},{1,0},{2,3},{4,5},{7,6},{5,4},{6,7},{8,9},{11,10},{9,8... | collective-permute-start | bytes 2359304 | tf_op jit(solution)/shard_map/ppermute | solution.py:859
  749.9 35.1 %collective-permute-start.69 = (bf16[256,1536]{1,0:T(8,128)(2,1)}, bf16[256,1536]{1,0:T(8,128)(2,1)}, u32[]{:S(2)}, u32[]{:S(2)}) collective-permute-start(bf16[256,1536]{1,0:T(8,128)(2,1)} %get-tuple-element.308.refs_4_), channel_id=1, source_target_pairs={{1,2},{2,1},{5,6},{6,5},{9,10},{10,9},{13,14},{14,13},{17,18},{18,... | collective-permute-start | bytes 2359304 | tf_op jit(solution)/shard_map/ppermute | solution.py:859
  788.5 21.1 %collective-permute-start.70 = (bf16[256,1536]{1,0:T(8,128)(2,1)}, bf16[256,1536]{1,0:T(8,128)(2,1)S(1)}, u32[]{:S(2)}, u32[]{:S(2)}) collective-permute-start(bf16[256,1536]{1,0:T(8,128)(2,1)} %get-tuple-element.315.refs_2_), channel_id=1, source_target_pairs={{0,1},{3,2},{1,0},{2,3},{4,5},{7,6},{5,4},{6,7},{8,9},{11,10},{9,8... | collective-permute-start | bytes 2359304 | tf_op jit(solution)/shard_map/ppermute | solution.py:859
  822.1 26.8 %collective-permute-start.72 = (bf16[256,1536]{1,0:T(8,128)(2,1)}, bf16[256,1536]{1,0:T(8,128)(2,1)}, u32[]{:S(2)}, u32[]{:S(2)}) collective-permute-start(bf16[256,1536]{1,0:T(8,128)(2,1)} %get-tuple-element.322.refs_2_), channel_id=1, source_target_pairs={{0,1},{3,2},{1,0},{2,3},{4,5},{7,6},{5,4},{6,7},{8,9},{11,10},{9,8... | collective-permute-start | bytes 2359304 | tf_op jit(solution)/shard_map/ppermute | solution.py:859
  826.3 22.6 %collective-permute-start.73 = (bf16[256,1536]{1,0:T(8,128)(2,1)S(1)}, bf16[256,1536]{1,0:T(8,128)(2,1)}, u32[]{:S(2)}, u32[]{:S(2)}) collective-permute-start(bf16[256,1536]{1,0:T(8,128)(2,1)S(1)} %copy-done.32), channel_id=1, source_target_pairs={{1,2},{2,1},{5,6},{6,5},{9,10},{10,9},{13,14},{14,13},{17,18},{18,... | collective-permute-start | bytes 2359304 | tf_op jit(solution)/shard_map/ppermute | solution.py:859
  865.4 20.0 %collective-permute-start.77 = (bf16[256,1536]{1,0:T(8,128)(2,1)S(1)}, bf16[256,1536]{1,0:T(8,128)(2,1)S(1)}, u32[]{:S(2)}, u32[]{:S(2)}) collective-permute-start(bf16[256,1536]{1,0:T(8,128)(2,1)S(1)} %copy-done.31), channel_id=1, source_target_pairs={{0,1},{3,2},{1,0},{2,3},{4,5},{7,6},{5,4},{6,7},{8,9},{11,10},{9,8... | collective-permute-start | bytes 2359304 | tf_op jit(solution)/shard_map/ppermute | solution.py:859
  872.7 22.6 %collective-permute-start.87 = (f32[8,128]{1,0:T(8,128)S(1)}, f32[8,128]{1,0:T(8,128)S(1)}, u32[]{:S(2)}, u32[]{:S(2)}) collective-permute-start(f32[8,128]{1,0:T(8,128)S(1)} %bitcast.139), channel_id=1, source_target_pairs={{0,1},{1,0},{2,3},{3,2},{4,5},{5,4},{6,7},{7,6},{8,9},{9,8},{10,11... | collective-permute-start | bytes 12296 | tf_op jit(solution)/shard_map/ppermute | solution.py:706
  873.4 21.9 %collective-permute-start.88 = (f32[8,128]{1,0:T(8,128)S(1)}, f32[8,128]{1,0:T(8,128)S(1)}, u32[]{:S(2)}, u32[]{:S(2)}) collective-permute-start(f32[8,128]{1,0:T(8,128)S(1)} %bitcast.140), channel_id=1, source_target_pairs={{0,2},{1,3},{2,0},{3,1},{4,6},{5,7},{6,4},{7,5},{8,10},{9,11},{10,... | collective-permute-start | bytes 12296 | tf_op jit(solution)/shard_map/ppermute | solution.py:706
  874.9 20.4 %collective-permute-start.89 = (f32[8,128]{1,0:T(8,128)S(1)}, f32[8,128]{1,0:T(8,128)S(1)}, u32[]{:S(2)}, u32[]{:S(2)}) collective-permute-start(f32[8,128]{1,0:T(8,128)S(1)} %bitcast.141), channel_id=1, source_target_pairs={{0,3},{1,2},{2,1},{3,0},{4,7},{5,6},{6,5},{7,4},{8,11},{9,10},{10,... | collective-permute-start | bytes 12296 | tf_op jit(solution)/shard_map/ppermute | solution.py:706
  889.0 20.1 %collective-permute-start.86 = (bf16[256,1536]{1,0:T(8,128)(2,1)}, bf16[256,1536]{1,0:T(8,128)(2,1)S(1)}, u32[]{:S(2)}, u32[]{:S(2)}) collective-permute-start(bf16[256,1536]{1,0:T(8,128)(2,1)} %get-tuple-element.351.refs_2_), channel_id=1, source_target_pairs={{0,1},{3,2},{1,0},{2,3},{4,5},{7,6},{5,4},{6,7},{8,9},{11,10},{9,8... | collective-permute-start | bytes 2359304 | tf_op jit(solution)/shard_map/ppermute | solution.py:859
  (146 other events, 1467.7 us)
Sparse Core Ops, SparseCore 0:
  206.0 46.7 all-gather.1
  508.7 94.4 reduce-scatter.3
  689.5 63.7 reduce-scatter.5
  815.1 55.9 reduce-scatter.7

commit v7 on v6

--- a/solution.py
+++ b/solution.py
@@ -245,11 +245,10 @@
         li_ref[...] = li
 
 
-def attend_call(order, sc, q, k, v, cap, tg, at, bq):
+def attend_call(order, sc, q, k, v, cap, text, tg, at, bq):
     n = q.shape[1]
     pairs = n // 128
     block = k.shape[0] // SPAN
-    text = cap.shape[0]
     mine = lambda p, j, s: (0, p)
     other = lambda p, j, s: (item_block(j, s), p)
     return order.run(
@@ -261,8 +260,8 @@
             pl.BlockSpec((bq, 128), lambda p, j, s: (at, p)),
             pl.BlockSpec((block, 128), other),
             pl.BlockSpec((block, 128), other),
-            pl.BlockSpec((text, 128), mine),
-            pl.BlockSpec((text, 128), lambda p, j, s: (0, pairs + p)),
+            pl.BlockSpec((text, 128), lambda p, j, s: (s[1 + SPAN], p)),
+            pl.BlockSpec((text, 128), lambda p, j, s: (s[1 + SPAN], pairs + p)),
             pl.BlockSpec((1, 128), mine),
         ],
         [pl.BlockSpec((bq, 128), mine)] * 3,
@@ -272,7 +271,7 @@
     )
 
 
-def caption_back_kernel(q_ref, da_ref, db_ref, ck_ref, cv_ref, tg_ref, dq_ref, dk_ref, dv_ref, gs_ref):
+def caption_back_kernel(sc, q_ref, da_ref, db_ref, ck_ref, cv_ref, tg_ref, dq_ref, dk_ref, dv_ref, gs_ref):
     masks = halves(128)
     q, d = q_ref[...], jnp.concatenate([da_ref[...], db_ref[...]], 0)
     dq = jnp.zeros(q.shape, f32)
@@ -297,23 +296,22 @@
     gs_ref[...] = jnp.where(masks[0], sums[0], sums[1])
 
 
-def caption_back_call(order, q, da, db, cap, tg, h):
+def caption_back_call(order, sc, q, da, db, cap, text, tg, h):
     n = q.shape[1]
     pairs = n // 128
     bq = 2 * BR
-    text = cap.shape[0]
-    mine = lambda p: (0, p)
+    mine = lambda p, s: (0, p)
     return order.run(
         "caption_back",
         caption_back_kernel,
         (pairs,),
         (q, da, db, cap, cap, tg),
         [
-            pl.BlockSpec((bq, 128), lambda p: (h, p)),
+            pl.BlockSpec((bq, 128), lambda p, s: (h, p)),
             pl.BlockSpec((BR, 128), mine),
             pl.BlockSpec((BR, 128), mine),
-            pl.BlockSpec((text, 128), mine),
-            pl.BlockSpec((text, 128), lambda p: (0, pairs + p)),
+            pl.BlockSpec((text, 128), lambda p, s: (s[1 + SPAN], p)),
+            pl.BlockSpec((text, 128), lambda p, s: (s[1 + SPAN], pairs + p)),
             pl.BlockSpec((1, 128), mine),
         ],
         [
@@ -323,6 +321,7 @@
             pl.BlockSpec((1, 128), mine),
         ],
         [sds((bq, n), f32), sds((text, n), f32), sds((text, n), f32), sds((1, n), f32)],
+        scalar=sc,
     )
 
 
@@ -792,8 +791,8 @@
     pass
 
 
-def pin(order, x):
-    return order.run("pin", pin_kernel, (1,), (), [], loose(1), [sds(x.shape, x.dtype)], held=(x,))[0]
+def pin(order, x, after=()):
+    return order.run("pin", pin_kernel, (1,), (), [], loose(1), [sds(x.shape, x.dtype)], held=(x,), after=after)[0]
 
 
 def note_kernel(x_ref, o_ref):
@@ -1005,6 +1004,9 @@
     chunks = range(t // BR)
     pairs_of = range(t // (2 * BR))
     sums = Sums(order, deep, mz)
+    a1, k_raw, k, v = key_call(order, patches, vec, w_qkv, tabs, hg, ())
+    kv = Gather(k, v)
+
     cap_raw = jnp.einsum("kd,jde->jke", captions, w_caption, preferred_element_type=f32)
     whole_cap = pl.BlockSpec((text, n), lambda i: (0, 0))
     both_cap = pl.BlockSpec((text, 2 * n), lambda i: (0, 0))
@@ -1018,23 +1020,17 @@
         [sds((text, 2 * n), bf16)],
     )
     offset = me - first
-    own_cap = cap
-    got_caps = tuple(shift(own_cap, by) for by in range(1, SPAN))
-    for by in range(1, SPAN):
-        cap = jnp.where(offset == by, got_caps[by - 1], cap)
-
-    a1, k_raw, k, v = key_call(order, patches, vec, w_qkv, tabs, hg, got_caps)
-    kv = Gather(k, v)
-    q_raw, q = query_call(order, a1, w_qkv, tabs, hg, kv.first)
+    q_raw, q = query_call(order, a1, w_qkv, tabs, hg, ())
+    cap = lax.all_gather(pin(order, cap, kv.first), "wide", axis=0, tiled=True)
 
     q_all = lax.all_gather(q, "wide", axis=0, tiled=True)
     k_all, v_all = pick(order, sc, kv.pieces(), SPAN)
     heads_out = {}
     for c in chunks[: len(chunks) // 2]:
-        heads_out[c] = (*attend_call(order, sc, q, k_all, v_all, cap, tg, c, BR), 0)
+        heads_out[c] = (*attend_call(order, sc, q, k_all, v_all, cap, text, tg, c, BR), 0)
         sums.add(("attn", c), mm(heads_out[c][0], w_out).astype(bf16))
     half = (len(chunks) + 1) // 2
-    later = attend_call(order, sc, q, k_all, v_all, cap, tg, 1, half * BR)
+    later = attend_call(order, sc, q, k_all, v_all, cap, text, tg, 1, half * BR)
     for c in chunks[half:]:
         heads_out[c] = (*later, c - half)
         at = (c - half) * BR
@@ -1069,8 +1065,6 @@
             if c == 2 * h + 1 and h > 0:
                 behind = d_got[h - 1].second
             da3 = sums.get(("da3", c), behind)
-            if c == chunks[-1]:
-                g_mlp = scatter_rows(pin(order, mlp_part[0]))
             d_mids[c], d_mixed[c], p3, p2, *outs = out_back_call(
                 order, c, da3, mids[c], sums.get(("attn", c)), cotangent, vec, w_out, o_self, linv, place, whole_out
             )
@@ -1081,7 +1075,7 @@
                 early = d_got[h - 1].first if h > 0 else ()
                 mlp_part = pair_grad_call(order, a3, d_gu, d_ffn, hidden, h, len(pairs_of), mlp_part, early)
         d_got[h] = GatherOne(d_scaled[h])
-        dq_caps[h], pk, pv, pg = caption_back_call(order, q, d_mixed[2 * h], d_mixed[2 * h + 1], cap, tg, h)
+        dq_caps[h], pk, pv, pg = caption_back_call(order, sc, q, d_mixed[2 * h], d_mixed[2 * h + 1], cap, text, tg, h)
         dck, dcv, gate_sum = dck + pk, dcv + pv, gate_sum + pg
     d_attn = whole_out[0]
     cap_sum = jnp.concatenate([dck, dcv], 1)
@@ -1105,7 +1099,6 @@
         [whole_cap, whole_cap, whole_cap, whole(hg.shape)],
         [both_cap, pl.BlockSpec((1, n), lambda i: (0, 0))],
         [sds((text, 2 * n), bf16), sds((1, n), f32)],
-        after=d_got[last_half].first,
     )
     d_text = (mm_nt(d_cap[:, :n], w_caption[0]) + mm_nt(d_cap[:, n:], w_caption[1])).astype(bf16)
     cap_part = mm_tn(captions, d_cap).astype(bf16)
@@ -1114,9 +1107,10 @@
     text_parts = [padded[:, p * d : (p + 1) * d] for p in range(pieces)]
 
     sums.add(("text", 0), text_parts[0])
-    dqs[last_half] = make_dq(last_half, (*d_got[last_half].second, *text_parts))
-    sums.add(("text", 1), text_parts[1], (cap_part,))
+    dqs[last_half] = make_dq(last_half, (*d_got[last_half].first, *text_parts))
+    sums.add(("text", 1), text_parts[1], (cap_part, *d_got[last_half].second))
     ds = [x for h in pairs_of for x in pick(order, sc, d_got[h].pieces(), SPAN)]
+    g_mlp = scatter_rows(pin(order, mlp_part[0]))
     whole_out = ()
     c1 = hs_qk = 0.0
     mixed = jnp.concatenate([heads_out[c][0] for c in chunks[:half]] + [later[0]])
@@ -1132,7 +1126,7 @@
     for p in range(2, pieces):
         sums.add(("text", p), text_parts[p])
     g_cap = scatter_rows(pin(order, cap_part))
-    sums.add(("da1", 0), project(0, dkv), (g_mlp,))
+    sums.add(("da1", 0), project(0, dkv))
     da1_part = project(1, dkv)
     dkv = [dkv_call(order, sc, k, v, q_all, ds, 1, 0, 1)]
     sums.add(("da1", 1), da1_part)
@@ -1142,21 +1136,21 @@
         if c == chunks[-1]:
             (d_qkv,) = whole_out
             attn_part = pair_grad_call(order, a1, d_qkv, d_attn, mixed)[0]
-        sums.add(("da1", c), da1_part)
+        sums.add(("da1", c), da1_part, (g_mlp,) if c == chunks[-1] else ())
     g_attn = scatter_rows(pin(order, attn_part))
 
     head_part = jnp.concatenate([hs_qk, hs_c]).reshape(3, heads, HD).sum(1)
     gate_part = gate_sum[0, ::HD] * (1.0 - tg_heads * tg_heads)
-    got_narrow = gather_small(note(order, jnp.concatenate([c1[0], head_part.reshape(-1), gate_part])), "narrow")
+    got_narrow = gather_now(note(order, jnp.concatenate([c1[0], head_part.reshape(-1), gate_part])), "narrow")
     whole_out = last_call(order, 0, sums.get(("da1", 0)), patches, d_mids[0], vec, ())
     da1 = sums.get(("da1", 1), (g_cap, got_narrow))
     summed = jnp.sum(got_narrow[:, : d + 3 * HD], 0)
     sent = note(order, jnp.concatenate([summed, got_narrow[:, d + 3 * HD :].reshape(-1), c2[0], c3[0], c4[0]]))
-    got_wide = gather_small(sent, "wide")
+    got_wide = gather_now(sent, "wide")
     whole_out = last_call(order, 1, da1, patches, d_mids[1], vec, whole_out)
     da1 = sums.get(("da1", 2), (got_wide,))
     for c in chunks[2:]:
-        whole_out = last_call(order, c, da1 if c == 2 else sums.get(("da1", c)), patches, d_mids[c], vec, whole_out)
+        whole_out = last_call(order, c, da1 if c == 2 else sums.get(("da1", c), (g_attn,)), patches, d_mids[c], vec, whole_out)
     (grad_patches,) = whole_out
     grad_captions = jnp.concatenate([sums.get(("text", p)) for p in range(pieces)], 1)[:, : d_text.shape[1]]
 
@@ -1180,7 +1174,7 @@
     grad_ada = jnp.sum(silu_mine[:, :, None, None] * d_slots[:, None], 0)
     d_mine = lax.dynamic_index_in_dim(d_slots, me, 0, False)
     cond_part = jnp.sum(d_mine[None] * w_ada.astype(f32), (1, 2))
-    cond_total = jnp.sum(gather_small(cond_part, "narrow"), 0)
+    cond_total = jnp.sum(gather_now(cond_part, "narrow"), 0)
     pull_silu = jax.vjp(jax.nn.silu, cond)[1]
     grad_conditioning = pull_silu(cond_total)[0].reshape(1, -1)
 

time: 945 us -> 936 us (level); the launches traced: 929 us -> 933 us
  Pallas kernels: 468 us -> 375 us
  blocking collectives: 22.7 us -> 103 us
  waiting for transfers between devices: 141 us -> 165 us
  other arithmetic: 48.9 us -> 35.4 us
    pallas_call x68 -> x69, Pallas kernels: 468 us -> 375 us  [run(): pl.pallas_call(body, grid_spec=pltpu.PrefetchScalarGridSpec(num_scalar_pr...]
    all_gather x2 -> x5, blocking collectives: 22.7 us -> 103 us  [gather_now(): lax.all_gather(padded, axis, axis=0, tiled=True).reshape(-1, wide)[:, :n]]
    reduce_scatter x3, waiting for transfers between devices: 1.61 us -> 35.2 us  [scatter_rows(): lax.psum_scatter(x.astype(bf16), 'wide', scatter_dimension=0, tiled=True)]
    ppermute x13, starting transfers between devices: 28.7 us -> 52.6 us  [__init__(): send = lambda x, pairs: lax.ppermute(x, 'wide', pairs)]
    ppermute x6 -> x3, starting transfers between devices: 15 us -> 4.28 us  [shift(): lax.ppermute(x, 'wide', [(i, i + by) for i in range(size) if 0 <= i + by...]
    ppermute x29 -> x16, waiting for transfers between devices: 10.3 us -> 0.04 us  [swap(): return lax.ppermute(x, axis, [(i, i ^ m) for i in range(size)])]
    ppermute x29 -> x16, starting transfers between devices: 26.7 us -> 17.6 us  [swap(): return lax.ppermute(x, axis, [(i, i ^ m) for i in range(size)])]
    unnamed x213 -> x237, local copies, waits for them, and re-layouts: 30 us -> 35.5 us
  transfers between devices with their start and end apart: 94 -> 79, of which waited for: 24 -> 21; matrix products, arithmetic and copies ran while one was open for 9% -> 6% of each run, Pallas kernels for 45% -> 36%
where the time goes in v7:
time: 936 us; the launch traced here: 933 us
  Pallas kernels  375 us (40%)
  waiting for transfers between devices  165 us (18%)
  starting transfers between devices  156 us (17%)
  blocking collectives  103 us (11%)
  local copies, waits for them, and re-layouts  49.6 us (5%)
  other arithmetic  35.4 us (4%)
  matrix products  24.2 us (3%)
  between operations  23.1 us (2%)
    pallas_call x69, Pallas kernels, run(): pl.pallas_call(body, grid_spec=pltpu.PrefetchScalarGridSpec(num_scalar_pr...  375 us
    all_gather x5, blocking collectives, gather_now(): lax.all_gather(padded, axis, axis=0, tiled=True).reshape(-1, wide)[:, :n]  103 us
    ppermute x42, starting transfers between devices, step(): go = lambda x, perm: lax.ppermute(x, 'narrow', perm)  81.7 us
    ppermute x42, waiting for transfers between devices, step(): go = lambda x, perm: lax.ppermute(x, 'narrow', perm)  70.3 us
    ppermute x13, waiting for transfers between devices, __init__(): send = lambda x, pairs: lax.ppermute(x, 'wide', pairs)  55.5 us
    ppermute x13, starting transfers between devices, __init__(): send = lambda x, pairs: lax.ppermute(x, 'wide', pairs)  52.6 us
    unnamed x237, local copies, waits for them, and re-layouts  35.5 us
    reduce_scatter x3, waiting for transfers between devices, scatter_rows(): lax.psum_scatter(x.astype(bf16), 'wide', scatter_dimension=0, tiled=True)  35.2 us
  transfers between devices with their start and end apart: 79, of which 21 were waited for; matrix products, arithmetic and copies ran while one was open for 6% of the time, Pallas kernels for 36%

profile of v7, /device:TPU:0, one launch (start us, length us, event | category | flops | bytes accessed | tf_op | source)
XLA Modules:
  0.0 932.7 jit_solution(15238488655891532400)
XLA Ops:
  20.1 14.8 %all_gather.21 = f32[4,8,256]{2,1,0:T(8,128)S(1)} all-gather(f32[1,8,256]{2,1,0:T(8,128)S(1)} %reshape.327), channel_id=1, replica_groups=mesh['wide'=8,'narrow'=4] {'narrow'}, dimensions={0}, use_global_device_ids=true | all-gather | bytes 40960 | tf_op jit(solution)/shard_map/all_gather | solution.py:828
  34.9 9.3 all_gather.22
  51.3 9.0 key.1
  72.8 7.0 query.1
  84.4 12.8 %collective-permute-done.8.refs_4_.refs_11_ = bf16[1024,384]{1,0:T(8,128)(2,1)S(1)} collective-permute-done((bf16[1024,384]{1,0:T(8,128)(2,1)}, bf16[1024,384]{1,0:T(8,128)(2,1)S(1)}, u32[]{:S(2)}, u32[]{:S(2)}) %collective-permute-start.8) | collective-permute-done | bytes 786464 | tf_op jit(solution)/shard_map/ppermute | solution.py:734
  105.9 15.4 %collective-permute-done.12 = bf16[1024,384]{1,0:T(8,128)(2,1)S(1)} collective-permute-done((bf16[1024,384]{1,0:T(8,128)(2,1)}, bf16[1024,384]{1,0:T(8,128)(2,1)S(1)}, u32[]{:S(2)}, u32[]{:S(2)}) %collective-permute-start.12) | collective-permute-done | bytes 786464 | tf_op jit(solution)/shard_map/ppermute | solution.py:734
  124.3 16.6 %collective-permute-done.5.refs_7_ = bf16[1024,384]{1,0:T(8,128)(2,1)} collective-permute-done((bf16[1024,384]{1,0:T(8,128)(2,1)}, bf16[1024,384]{1,0:T(8,128)(2,1)}, u32[]{:S(2)}, u32[]{:S(2)}) %collective-permute-start.5) | collective-permute-done | bytes 786464 | tf_op jit(solution)/shard_map/ppermute | solution.py:734
  146.2 6.8 pick.3
  153.1 9.5 %attend.3 = (bf16[256,384]{1,0:T(8,128)(2,1)}, bf16[256,384]{1,0:T(8,128)(2,1)}, f32[256,384]{1,0:T(8,128)}) custom-call(s32[9]{0:T(128)} %pad_add_fusion.refs_0_, bf16[1024,384]{1,0:T(8,128)(2,1)} %get-tuple-element.184.refs_1_, bf16[4096,384]{1,0:T(8,128)(2,1)} %get-tuple-element.188.refs_2_.refs_7_.refs_4_, ...), custom_call_target="tpu_custom_call" | custom-call | flops 4499999744 | bytes 13500000 | tf_op jit(solution)/shard_map/attend/pallas_call | solution.py:51
  166.5 9.4 %attend.4 = (bf16[256,384]{1,0:T(8,128)(2,1)}, bf16[256,384]{1,0:T(8,128)(2,1)}, f32[256,384]{1,0:T(8,128)}) custom-call(s32[9]{0:T(128)} %pad_add_fusion.refs_0_, bf16[1024,384]{1,0:T(8,128)(2,1)} %get-tuple-element.184.refs_1_, bf16[4096,384]{1,0:T(8,128)(2,1)} %get-tuple-element.188.refs_2_.refs_7_.refs_4_, ...), custom_call_target="tpu_custom_call" | custom-call | flops 4499999744 | bytes 13500000 | tf_op jit(solution)/shard_map/attend/pallas_call | solution.py:51
  183.3 10.8 %attend.5 = (bf16[512,384]{1,0:T(8,128)(2,1)}, bf16[512,384]{1,0:T(8,128)(2,1)}, f32[512,384]{1,0:T(8,128)}) custom-call(s32[9]{0:T(128)} %pad_add_fusion.refs_0_, bf16[1024,384]{1,0:T(8,128)(2,1)} %get-tuple-element.184.refs_1_, bf16[4096,384]{1,0:T(8,128)(2,1)} %get-tuple-element.188.refs_2_.refs_7_.refs_4_, ...), custom_call_target="tpu_custom_call" | custom-call | flops 4499999744 | bytes 13500000 | tf_op jit(solution)/shard_map/attend/pallas_call | solution.py:51
  207.6 9.2 collective-permute-done.18.refs_1_
  225.6 8.5 ffn.4
  247.2 8.5 ffn.5
  269.5 8.5 ffn.6
  293.9 8.5 ffn.7
  302.3 5.8 collective-permute-done.26.refs_1_
  317.3 9.5 %ffn_back.4 = (bf16[256,1536]{1,0:T(8,128)(2,1)}, f32[1,1536]{1,0:T(1,128)}, bf16[1024,1536]{1,0:T(8,128)(2,1)}, bf16[1024,1536]{1,0:T(8,128)(2,1)}, bf16[1024,2048]{1,0:T(8,128)(2,1)}) custom-call(bf16[256,1536]{1,0:T(8,128)(2,1)} %get-tuple-element.225.refs_0_.refs_7_, f32[256,1536]{1,0:T(8,128)} %get-tuple-element.201.refs_7_.refs_1_, ...), custom_call_target="tpu_custom_call" | custom-call | flops 2500000000 | bytes 7500000 | tf_op jit(solution)/shard_map/ffn_back/pallas_call | solution.py:51
  326.9 5.8 collective-permute-done.28.refs_1_
  342.6 9.6 %ffn_back.5 = (bf16[256,1536]{1,0:T(8,128)(2,1)}, f32[1,1536]{1,0:T(1,128)}, bf16[1024,1536]{1,0:T(8,128)(2,1)}, bf16[1024,1536]{1,0:T(8,128)(2,1)}, bf16[1024,2048]{1,0:T(8,128)(2,1)}) custom-call(bf16[256,1536]{1,0:T(8,128)(2,1)} %get-tuple-element.230.refs_0_.refs_7_, ...), custom_call_target="tpu_custom_call", output_to_operand_aliasing={{2}: (8, {}), {3}: (9, {}), {4}: (10, {})} | custom-call | flops 2500000000 | bytes 7500000 | tf_op jit(solution)/shard_map/ffn_back/pallas_call | solution.py:51
  352.2 8.2 collective-permute-done.30.refs_1_
  369.7 9.7 %ffn_back.6 = (bf16[256,1536]{1,0:T(8,128)(2,1)}, f32[1,1536]{1,0:T(1,128)}, bf16[1024,1536]{1,0:T(8,128)(2,1)}, bf16[1024,1536]{1,0:T(8,128)(2,1)}, bf16[1024,2048]{1,0:T(8,128)(2,1)}) custom-call(bf16[256,1536]{1,0:T(8,128)(2,1)} %get-tuple-element.238.refs_0_.refs_7_, ...), custom_call_target="tpu_custom_call", output_to_operand_aliasing={{2}: (8, {}), {3}: (9, {}), {4}: (10, {})} | custom-call | flops 2500000000 | bytes 7500000 | tf_op jit(solution)/shard_map/ffn_back/pallas_call | solution.py:51
  379.4 7.6 collective-permute-done.32.refs_1_
  395.9 9.6 %ffn_back.7 = (bf16[256,1536]{1,0:T(8,128)(2,1)}, f32[1,1536]{1,0:T(1,128)}, bf16[1024,1536]{1,0:T(8,128)(2,1)}, bf16[1024,1536]{1,0:T(8,128)(2,1)}, bf16[1024,2048]{1,0:T(8,128)(2,1)}) custom-call(bf16[256,1536]{1,0:T(8,128)(2,1)} %get-tuple-element.244.refs_0_.refs_7_, ...), custom_call_target="tpu_custom_call", output_to_operand_aliasing={{2}: (8, {}), {3}: (9, {}), {4}: (10, {})} | custom-call | flops 2500000000 | bytes 7500000 | tf_op jit(solution)/shard_map/ffn_back/pallas_call | solution.py:51
  405.5 6.7 collective-permute-done.34.refs_1_
  426.6 9.9 %pair_grad.3.refs_6_.refs_7_ = bf16[1536,3072]{1,0:T(8,128)(2,1)} custom-call(bf16[1024,1536]{1,0:T(8,128)(2,1)} %get-tuple-element.259.refs_0_, bf16[1024,2048]{1,0:T(8,128)(2,1)} %get-tuple-element.260.refs_1_, bf16[1024,1536]{1,0:T(8,128)(2,1)} %get-tuple-element.261.refs_2_, bf16[1024,1024]{1,0:T(8,128)(2,1)} %get-tuple-element.262.refs_3_, ...), custom_call_target="tpu_custom_call" | custom-call | flops 2500000000 | bytes 7500000 | tf_op jit(solution)/shard_map/pair_grad/pallas_call | solution.py:51
  450.5 10.9 %collective-permute-start.41 = (bf16[512,512]{1,0:T(8,128)(2,1)}, bf16[512,512]{1,0:T(8,128)(2,1)S(1)}, u32[]{:S(2)}, u32[]{:S(2)}) collective-permute-start(bf16[512,512]{1,0:T(8,128)(2,1)} %get-tuple-element.282.refs_2_.refs_3_.refs_1_), channel_id=1, source_target_pairs={{0,8},{4,12},{8,0},{12,4},{16,24},{20,28},{24,16},{28,20},{1,9},{5... | collective-permute-start | bytes 1572872 | tf_op jit(solution)/shard_map/ppermute | solution.py:757
  461.5 6.3 caption_back.2
  475.7 18.5 %collective-permute-start.43 = (bf16[512,512]{1,0:T(8,128)(2,1)S(1)}, bf16[512,512]{1,0:T(8,128)(2,1)}, u32[]{:S(2)}, u32[]{:S(2)}) collective-permute-start(bf16[512,512]{1,0:T(8,128)(2,1)S(1)} %collective-permute-done.41.refs_5_.refs_3_), channel_id=1, source_target_pairs={{0,16},{4,20},{24,8},{28,12},{1,17},{5,21},{25,9},{29,13},{2,18},{... | collective-permute-start | bytes 1572872 | tf_op jit(solution)/shard_map/ppermute | solution.py:757
  502.6 9.9 %pair_grad.4.refs_3_.refs_1_ = bf16[1536,3072]{1,0:T(8,128)(2,1)} custom-call(bf16[1024,1536]{1,0:T(8,128)(2,1)} %get-tuple-element.259.refs_0_, bf16[1024,2048]{1,0:T(8,128)(2,1)} %get-tuple-element.260.refs_1_, bf16[1024,1536]{1,0:T(8,128)(2,1)} %get-tuple-element.261.refs_2_, ...), custom_call_target="tpu_custom_call", output_to_operand_aliasing={{}: (7, {})} | custom-call | flops 2500000000 | bytes 7500000 | tf_op jit(solution)/shard_map/pair_grad/pallas_call | solution.py:51
  514.7 5.8 out_back.7
  520.5 6.4 caption_back.3
  536.8 11.9 %dq.2.refs_4_.refs_0_ = f32[512,384]{1,0:T(8,128)} custom-call(s32[9]{0:T(128)} %pad_add_fusion.refs_0_, bf16[1024,384]{1,0:T(8,128)(2,1)} %get-tuple-element.184.refs_1_, bf16[512,512]{1,0:T(8,128)(2,1)} %get-tuple-element.282.refs_2_.refs_3_.refs_1_, bf16[512,512]{1,0:T(8,128)(2,1)} %get-tuple-element.282.refs_2_.refs_3_.refs_1_, ...), custom_call_target="tpu_custom_call" | custom-call | flops 6750000128 | bytes 20250000 | tf_op jit(solution)/shard_map/dq/pallas_call | solution.py:51
  565.0 11.0 %collective-permute-start.54 = (bf16[512,512]{1,0:T(8,128)(2,1)S(1)}, bf16[512,512]{1,0:T(8,128)(2,1)S(1)}, u32[]{:S(2)}, u32[]{:S(2)}) collective-permute-start(bf16[512,512]{1,0:T(8,128)(2,1)S(1)} %copy-done.19), channel_id=1, source_target_pairs={{0,4},{4,0},{8,12},{12,8},{16,20},{20,16},{24,28},{28,24},{1,5},{5... | collective-permute-start | bytes 1572872 | tf_op jit(solution)/shard_map/ppermute | solution.py:705
  588.9 6.1 collective-permute-done.50.refs_6_.refs_7_
  597.8 11.9 %dq.3.refs_4_.refs_0_ = f32[512,384]{1,0:T(8,128)} custom-call(s32[9]{0:T(128)} %pad_add_fusion.refs_0_, bf16[1024,384]{1,0:T(8,128)(2,1)} %get-tuple-element.184.refs_1_, bf16[512,512]{1,0:T(8,128)(2,1)} %get-tuple-element.292.refs_2_.refs_3_.refs_1_, bf16[512,512]{1,0:T(8,128)(2,1)} %get-tuple-element.292.refs_2_.refs_3_.refs_1_, ...), custom_call_target="tpu_custom_call" | custom-call | flops 6750000128 | bytes 20250000 | tf_op jit(solution)/shard_map/dq/pallas_call | solution.py:51
  625.6 13.8 %dkv.3 = (f32[512,384]{1,0:T(8,128)}, f32[512,384]{1,0:T(8,128)}) custom-call(s32[9]{0:T(128)} %pad_add_fusion.refs_0_, bf16[1024,384]{1,0:T(8,128)(2,1)} %get-tuple-element.185.refs_1_, bf16[1024,384]{1,0:T(8,128)(2,1)} %get-tuple-element.186.refs_9_.refs_2_, bf16[8192,384]{1,0:T(8,128)(2,1)} %all-gather.5.cloned.1.call-done.refs_3_, ...), custom_call_target="tpu_custom_call" | custom-call | flops 6000000000 | bytes 18000000 | tf_op jit(solution)/shard_map/dkv/pallas_call | solution.py:51
  649.4 7.8 dqkv.4
  668.8 6.9 dqkv.5
  689.0 9.8 %dkv.5 = (f32[512,256]{1,0:T(8,128)}, f32[512,256]{1,0:T(8,128)}) custom-call(s32[9]{0:T(128)} %pad_add_fusion.refs_0_, bf16[1024,384]{1,0:T(8,128)(2,1)} %get-tuple-element.185.refs_1_, bf16[1024,384]{1,0:T(8,128)(2,1)} %get-tuple-element.186.refs_9_.refs_2_, bf16[8192,384]{1,0:T(8,128)(2,1)} %all-gather.5.cloned.1.call-done.refs_3_, ...), custom_call_target="tpu_custom_call" | custom-call | flops 6000000000 | bytes 18000000 | tf_op jit(solution)/shard_map/dkv/pallas_call | solution.py:51
  698.8 6.6 dqkv.6
  715.7 6.6 dqkv.7
  722.3 11.4 %pair_grad.5.refs_7_.refs_1_ = bf16[1536,1536]{1,0:T(8,128)(2,1)} custom-call(bf16[1024,1536]{1,0:T(8,128)(2,1)} %get-tuple-element.183.refs_3_.refs_0_, bf16[1024,1152]{1,0:T(8,128)(2,1)} %get-tuple-element.320.refs_1_, bf16[1024,1536]{1,0:T(8,128)(2,1)} %get-tuple-element.321.refs_2_, bf16[1024,384]{1,0:T(8,128)(2,1)} %pad_maximum_fusion.3.refs_3_, ...), custom_call_target="tpu_custom_call" | custom-call | flops 2500000000 | bytes 7500000 | tf_op jit(solution)/shard_map/pair_grad/pallas_call | solution.py:51
  743.4 35.1 %reduce-scatter.6.cloned.1.call-done.refs_7_ = bf16[512,768]{1,0:T(8,128)(2,1)} async-done(((bf16[4096,768]{1,0:T(8,128)(2,1)}), bf16[512,768]{1,0:T(8,128)(2,1)}) %reduce-scatter.6.cloned.1.call-update) | async-done | bytes 786448 | tf_op jit(solution)/shard_map/reduce_scatter | solution.py:920
  786.4 17.7 %all_gather.25 = f32[4,8,256]{2,1,0:T(8,128)S(1)} all-gather(f32[1,8,256]{2,1,0:T(8,128)S(1)} %pad.30), channel_id=1, replica_groups=mesh['wide'=8,'narrow'=4] {'narrow'}, dimensions={0}, use_global_device_ids=true | all-gather | bytes 40960 | tf_op jit(solution)/shard_map/all_gather | solution.py:828
  817.0 38.0 %all_gather.26 = f32[8,8,896]{2,1,0:T(8,128)S(1)} all-gather(f32[1,8,896]{2,1,0:T(8,128)S(1)} %pad.33), channel_id=1, replica_groups=mesh['wide'=8,'narrow'=4] {'wide'}, dimensions={0}, use_global_device_ids=true | all-gather | bytes 258048 | tf_op jit(solution)/shard_map/all_gather | solution.py:828
  863.8 11.4 %collective-permute-done.71.refs_1_ = bf16[256,1536]{1,0:T(8,128)(2,1)S(1)} collective-permute-done((bf16[256,1536]{1,0:T(8,128)(2,1)}, bf16[256,1536]{1,0:T(8,128)(2,1)S(1)}, u32[]{:S(2)}, u32[]{:S(2)}) %collective-permute-start.71) | collective-permute-done | bytes 786464 | tf_op jit(solution)/shard_map/ppermute | solution.py:858
  884.5 23.5 %all_gather.27 = f32[4,8,128]{2,1,0:T(8,128)S(1)} all-gather(f32[1,8,128]{2,1,0:T(8,128)S(1)} %bitcast.110), channel_id=1, replica_groups=mesh['wide'=8,'narrow'=4] {'narrow'}, dimensions={0}, use_global_device_ids=true | all-gather | bytes 20480 | tf_op jit(solution)/shard_map/all_gather | solution.py:828
  (533 shorter events, 375.4 us)
Async XLA Ops:
  7.2 145.8 %all-gather.3.cloned.1.call-start = ((), (), s32[]{:S(2)}) async-start(), calls=%async_computation.3 | async-start | bytes 3538944 | tf_op jit(solution)/shard_map/all_gather | solution.py:1024
  60.3 20.6 %collective-permute-start.1 = (bf16[1024,384]{1,0:T(8,128)(2,1)}, bf16[1024,384]{1,0:T(8,128)(2,1)S(1)}, u32[]{:S(2)}, u32[]{:S(2)}) collective-permute-start(bf16[1024,384]{1,0:T(8,128)(2,1)} %get-tuple-element.185.refs_1_), channel_id=1, source_target_pairs={{0,8},{4,12},{8,0},{12,4},{16,24},{20,28},{24,16},{28,20},{1,9},{5... | collective-permute-start | bytes 2359304 | tf_op jit(solution)/shard_map/ppermute | solution.py:734
  61.8 22.5 %collective-permute-start.3 = (bf16[1024,384]{1,0:T(8,128)(2,1)}, bf16[1024,384]{1,0:T(8,128)(2,1)S(1)}, u32[]{:S(2)}, u32[]{:S(2)}) collective-permute-start(bf16[1024,384]{1,0:T(8,128)(2,1)} %get-tuple-element.185.refs_1_), channel_id=1, source_target_pairs={{4,20},{16,0},{12,28},{24,8},{5,21},{17,1},{13,29},{25,9},{6,22},{... | collective-permute-start | bytes 2359304 | tf_op jit(solution)/shard_map/ppermute | solution.py:734
  63.1 21.2 %collective-permute-start.10 = (bf16[1024,384]{1,0:T(8,128)(2,1)}, bf16[1024,384]{1,0:T(8,128)(2,1)S(1)}, u32[]{:S(2)}, u32[]{:S(2)}) collective-permute-start(bf16[1024,384]{1,0:T(8,128)(2,1)} %get-tuple-element.186.refs_9_.refs_2_), channel_id=1, source_target_pairs={{4,20},{16,0},{12,28},{24,8},{5,21},{17,1},{13,29},{25,9},{6,22},{... | collective-permute-start | bytes 2359304 | tf_op jit(solution)/shard_map/ppermute | solution.py:734
  64.4 32.8 %collective-permute-start.8 = (bf16[1024,384]{1,0:T(8,128)(2,1)}, bf16[1024,384]{1,0:T(8,128)(2,1)S(1)}, u32[]{:S(2)}, u32[]{:S(2)}) collective-permute-start(bf16[1024,384]{1,0:T(8,128)(2,1)} %get-tuple-element.186.refs_9_.refs_2_), channel_id=1, source_target_pairs={{0,8},{4,12},{8,0},{12,4},{16,24},{20,28},{24,16},{28,20},{1,9},{5... | collective-permute-start | bytes 2359304 | tf_op jit(solution)/shard_map/ppermute | solution.py:734
  98.1 527.5 %all-gather.5.cloned.1.call-start = ((), (), s32[]{:S(2)}) async-start(), calls=%async_computation.4 | async-start | bytes 7077888 | tf_op jit(solution)/shard_map/all_gather | solution.py:1026
  98.1 23.1 %collective-permute-start.12 = (bf16[1024,384]{1,0:T(8,128)(2,1)}, bf16[1024,384]{1,0:T(8,128)(2,1)S(1)}, u32[]{:S(2)}, u32[]{:S(2)}) collective-permute-start(bf16[1024,384]{1,0:T(8,128)(2,1)} %copy-done.14), channel_id=1, source_target_pairs={{0,16},{28,12},{1,17},{29,13},{2,18},{30,14},{3,19},{31,15}} | collective-permute-start | bytes 2359304 | tf_op jit(solution)/shard_map/ppermute | solution.py:734
  101.6 19.7 %collective-permute-start.13 = (bf16[1024,384]{1,0:T(8,128)(2,1)}, bf16[1024,384]{1,0:T(8,128)(2,1)S(1)}, u32[]{:S(2)}, u32[]{:S(2)}) collective-permute-start(bf16[1024,384]{1,0:T(8,128)(2,1)} %copy-done.13), channel_id=1, source_target_pairs={{28,20},{0,8},{29,21},{1,9},{30,22},{2,10},{31,23},{3,11}} | collective-permute-start | bytes 2359304 | tf_op jit(solution)/shard_map/ppermute | solution.py:734
  103.0 19.9 %collective-permute-start = (bf16[1024,384]{1,0:T(8,128)(2,1)S(1)}, bf16[1024,384]{1,0:T(8,128)(2,1)S(1)}, u32[]{:S(2)}, u32[]{:S(2)}) collective-permute-start(bf16[1024,384]{1,0:T(8,128)(2,1)S(1)} %copy-done.7), channel_id=1, source_target_pairs={{0,4},{4,0},{8,12},{12,8},{16,20},{20,16},{24,28},{28,24},{1,5},{5... | collective-permute-start | bytes 2359304 | tf_op jit(solution)/shard_map/ppermute | solution.py:705
  103.0 20.7 %collective-permute-start.7 = (bf16[1024,384]{1,0:T(8,128)(2,1)}, bf16[1024,384]{1,0:T(8,128)(2,1)}, u32[]{:S(2)}, u32[]{:S(2)}) collective-permute-start(bf16[1024,384]{1,0:T(8,128)(2,1)} %get-tuple-element.186.refs_9_.refs_2_), channel_id=1, source_target_pairs={{0,4},{4,0},{8,12},{12,8},{16,20},{20,16},{24,28},{28,24},{1,5},{5... | collective-permute-start | bytes 2359304 | tf_op jit(solution)/shard_map/ppermute | solution.py:705
  103.5 37.3 %collective-permute-start.5 = (bf16[1024,384]{1,0:T(8,128)(2,1)}, bf16[1024,384]{1,0:T(8,128)(2,1)}, u32[]{:S(2)}, u32[]{:S(2)}) collective-permute-start(bf16[1024,384]{1,0:T(8,128)(2,1)} %copy-done.11), channel_id=1, source_target_pairs={{0,16},{4,20},{24,8},{28,12},{1,17},{5,21},{25,9},{29,13},{2,18},{... | collective-permute-start | bytes 2359304 | tf_op jit(solution)/shard_map/ppermute | solution.py:734
  121.3 19.6 %collective-permute-start.11 = (bf16[1024,384]{1,0:T(8,128)(2,1)}, bf16[1024,384]{1,0:T(8,128)(2,1)}, u32[]{:S(2)}, u32[]{:S(2)}) collective-permute-start(bf16[1024,384]{1,0:T(8,128)(2,1)} %copy-done.13), channel_id=1, source_target_pairs={{0,4},{4,0},{8,12},{12,8},{16,20},{20,16},{24,28},{28,24},{1,5},{5... | collective-permute-start | bytes 2359304 | tf_op jit(solution)/shard_map/ppermute | solution.py:705
  121.3 24.1 %collective-permute-start.2 = (bf16[1024,384]{1,0:T(8,128)(2,1)}, bf16[1024,384]{1,0:T(8,128)(2,1)}, u32[]{:S(2)}, u32[]{:S(2)}) collective-permute-start(bf16[1024,384]{1,0:T(8,128)(2,1)} %copy-done.11), channel_id=1, source_target_pairs={{0,4},{4,0},{8,12},{12,8},{16,20},{20,16},{24,28},{28,24},{1,5},{5... | collective-permute-start | bytes 2359304 | tf_op jit(solution)/shard_map/ppermute | solution.py:705
  123.8 21.6 %collective-permute-start.4 = (bf16[1024,384]{1,0:T(8,128)(2,1)}, bf16[1024,384]{1,0:T(8,128)(2,1)S(1)}, u32[]{:S(2)}, u32[]{:S(2)}) collective-permute-start(bf16[1024,384]{1,0:T(8,128)(2,1)} %copy-done.12), channel_id=1, source_target_pairs={{0,4},{4,0},{8,12},{12,8},{16,20},{20,16},{24,28},{28,24},{1,5},{5... | collective-permute-start | bytes 2359304 | tf_op jit(solution)/shard_map/ppermute | solution.py:705
  123.8 21.6 %collective-permute-start.9 = (bf16[1024,384]{1,0:T(8,128)(2,1)}, bf16[1024,384]{1,0:T(8,128)(2,1)}, u32[]{:S(2)}, u32[]{:S(2)}) collective-permute-start(bf16[1024,384]{1,0:T(8,128)(2,1)} %copy-done.14), channel_id=1, source_target_pairs={{0,4},{4,0},{8,12},{12,8},{16,20},{20,16},{24,28},{28,24},{1,5},{5... | collective-permute-start | bytes 2359304 | tf_op jit(solution)/shard_map/ppermute | solution.py:705
  288.3 19.9 %collective-permute-start.26 = (bf16[256,1536]{1,0:T(8,128)(2,1)}, bf16[256,1536]{1,0:T(8,128)(2,1)S(1)}, u32[]{:S(2)}, u32[]{:S(2)}) collective-permute-start(bf16[256,1536]{1,0:T(8,128)(2,1)} %get-tuple-element.216.refs_2_), channel_id=1, source_target_pairs={{0,1},{3,2},{1,0},{2,3},{4,5},{7,6},{5,4},{6,7},{8,9},{11,10},{9,8... | collective-permute-start | bytes 2359304 | tf_op jit(solution)/shard_map/ppermute | solution.py:858
  293.8 439.9 %reduce-scatter.4.cloned.1.call-start = ((), (), s32[]{:S(2)}) async-start(), calls=%async_computation.5 | async-start | bytes 10616832 | tf_op jit(solution)/shard_map/reduce_scatter | solution.py:920
  312.5 20.1 %collective-permute-start.28 = (bf16[256,1536]{1,0:T(8,128)(2,1)}, bf16[256,1536]{1,0:T(8,128)(2,1)S(1)}, u32[]{:S(2)}, u32[]{:S(2)}) collective-permute-start(bf16[256,1536]{1,0:T(8,128)(2,1)} %get-tuple-element.223.refs_2_), channel_id=1, source_target_pairs={{0,1},{3,2},{1,0},{2,3},{4,5},{7,6},{5,4},{6,7},{8,9},{11,10},{9,8... | collective-permute-start | bytes 2359304 | tf_op jit(solution)/shard_map/ppermute | solution.py:858
  337.5 22.9 %collective-permute-start.30 = (bf16[256,1536]{1,0:T(8,128)(2,1)}, bf16[256,1536]{1,0:T(8,128)(2,1)S(1)}, u32[]{:S(2)}, u32[]{:S(2)}) collective-permute-start(bf16[256,1536]{1,0:T(8,128)(2,1)} %get-tuple-element.228.refs_2_), channel_id=1, source_target_pairs={{0,1},{3,2},{1,0},{2,3},{4,5},{7,6},{5,4},{6,7},{8,9},{11,10},{9,8... | collective-permute-start | bytes 2359304 | tf_op jit(solution)/shard_map/ppermute | solution.py:858
  365.2 21.8 %collective-permute-start.32 = (bf16[256,1536]{1,0:T(8,128)(2,1)}, bf16[256,1536]{1,0:T(8,128)(2,1)S(1)}, u32[]{:S(2)}, u32[]{:S(2)}) collective-permute-start(bf16[256,1536]{1,0:T(8,128)(2,1)} %get-tuple-element.236.refs_2_), channel_id=1, source_target_pairs={{0,1},{3,2},{1,0},{2,3},{4,5},{7,6},{5,4},{6,7},{8,9},{11,10},{9,8... | collective-permute-start | bytes 2359304 | tf_op jit(solution)/shard_map/ppermute | solution.py:858
  391.6 20.6 %collective-permute-start.34 = (bf16[256,1536]{1,0:T(8,128)(2,1)}, bf16[256,1536]{1,0:T(8,128)(2,1)S(1)}, u32[]{:S(2)}, u32[]{:S(2)}) collective-permute-start(bf16[256,1536]{1,0:T(8,128)(2,1)} %get-tuple-element.250.refs_2_), channel_id=1, source_target_pairs={{0,1},{3,2},{1,0},{2,3},{4,5},{7,6},{5,4},{6,7},{8,9},{11,10},{9,8... | collective-permute-start | bytes 2359304 | tf_op jit(solution)/shard_map/ppermute | solution.py:858
  416.8 19.6 %collective-permute-start.36 = (bf16[256,1536]{1,0:T(8,128)(2,1)}, bf16[256,1536]{1,0:T(8,128)(2,1)S(1)}, u32[]{:S(2)}, u32[]{:S(2)}) collective-permute-start(bf16[256,1536]{1,0:T(8,128)(2,1)} %get-tuple-element.257.refs_2_), channel_id=1, source_target_pairs={{0,1},{3,2},{1,0},{2,3},{4,5},{7,6},{5,4},{6,7},{8,9},{11,10},{9,8... | collective-permute-start | bytes 2359304 | tf_op jit(solution)/shard_map/ppermute | solution.py:858
  441.4 26.3 %collective-permute-start.38 = (bf16[256,1536]{1,0:T(8,128)(2,1)}, bf16[256,1536]{1,0:T(8,128)(2,1)S(1)}, u32[]{:S(2)}, u32[]{:S(2)}) collective-permute-start(bf16[256,1536]{1,0:T(8,128)(2,1)} %get-tuple-element.272.refs_2_), channel_id=1, source_target_pairs={{0,1},{3,2},{1,0},{2,3},{4,5},{7,6},{5,4},{6,7},{8,9},{11,10},{9,8... | collective-permute-start | bytes 2359304 | tf_op jit(solution)/shard_map/ppermute | solution.py:858
  444.2 23.6 %collective-permute-start.39 = (bf16[256,1536]{1,0:T(8,128)(2,1)}, bf16[256,1536]{1,0:T(8,128)(2,1)S(1)}, u32[]{:S(2)}, u32[]{:S(2)}) collective-permute-start(bf16[256,1536]{1,0:T(8,128)(2,1)} %get-tuple-element.273.refs_4_), channel_id=1, source_target_pairs={{1,2},{2,1},{5,6},{6,5},{9,10},{10,9},{13,14},{14,13},{17,18},{18,... | collective-permute-start | bytes 2359304 | tf_op jit(solution)/shard_map/ppermute | solution.py:858
  450.5 25.1 %collective-permute-start.41 = (bf16[512,512]{1,0:T(8,128)(2,1)}, bf16[512,512]{1,0:T(8,128)(2,1)S(1)}, u32[]{:S(2)}, u32[]{:S(2)}) collective-permute-start(bf16[512,512]{1,0:T(8,128)(2,1)} %get-tuple-element.282.refs_2_.refs_3_.refs_1_), channel_id=1, source_target_pairs={{0,8},{4,12},{8,0},{12,4},{16,24},{20,28},{24,16},{28,20},{1,9},{5... | collective-permute-start | bytes 1572872 | tf_op jit(solution)/shard_map/ppermute | solution.py:757
  471.7 40.8 %collective-permute-start.40 = (bf16[256,1536]{1,0:T(8,128)(2,1)}, bf16[256,1536]{1,0:T(8,128)(2,1)}, u32[]{:S(2)}, u32[]{:S(2)}) collective-permute-start(bf16[256,1536]{1,0:T(8,128)(2,1)} %get-tuple-element.280.refs_2_), channel_id=1, source_target_pairs={{0,1},{3,2},{1,0},{2,3},{4,5},{7,6},{5,4},{6,7},{8,9},{11,10},{9,8... | collective-permute-start | bytes 2359304 | tf_op jit(solution)/shard_map/ppermute | solution.py:858
  474.4 27.5 %collective-permute-start.42 = (bf16[512,512]{1,0:T(8,128)(2,1)}, bf16[512,512]{1,0:T(8,128)(2,1)S(1)}, u32[]{:S(2)}, u32[]{:S(2)}) collective-permute-start(bf16[512,512]{1,0:T(8,128)(2,1)} %get-tuple-element.282.refs_2_.refs_3_.refs_1_), channel_id=1, source_target_pairs={{4,20},{16,0},{12,28},{24,8},{5,21},{17,1},{13,29},{25,9},{6,22},{... | collective-permute-start | bytes 1572872 | tf_op jit(solution)/shard_map/ppermute | solution.py:757
  475.7 36.8 %collective-permute-start.43 = (bf16[512,512]{1,0:T(8,128)(2,1)S(1)}, bf16[512,512]{1,0:T(8,128)(2,1)}, u32[]{:S(2)}, u32[]{:S(2)}) collective-permute-start(bf16[512,512]{1,0:T(8,128)(2,1)S(1)} %collective-permute-done.41.refs_5_.refs_3_), channel_id=1, source_target_pairs={{0,16},{4,20},{24,8},{28,12},{1,17},{5,21},{25,9},{29,13},{2,18},{... | collective-permute-start | bytes 1572872 | tf_op jit(solution)/shard_map/ppermute | solution.py:757
  496.1 80.0 %collective-permute-start.53 = (bf16[512,512]{1,0:T(8,128)(2,1)}, bf16[512,512]{1,0:T(8,128)(2,1)S(1)}, u32[]{:S(2)}, u32[]{:S(2)}) collective-permute-start(bf16[512,512]{1,0:T(8,128)(2,1)} %get-tuple-element.282.refs_2_.refs_3_.refs_1_), channel_id=1, source_target_pairs={{0,4},{4,0},{8,12},{12,8},{16,20},{20,16},{24,28},{28,24},{1,5},{5... | collective-permute-start | bytes 1572872 | tf_op jit(solution)/shard_map/ppermute | solution.py:705
  529.0 19.7 %collective-permute-start.44 = (bf16[256,768]{1,0:T(8,128)(2,1)S(1)}, bf16[256,768]{1,0:T(8,128)(2,1)S(1)}, u32[]{:S(2)}, u32[]{:S(2)}) collective-permute-start(bf16[256,768]{1,0:T(8,128)(2,1)S(1)} %fusion.14), channel_id=1, source_target_pairs={{4,0},{8,4},{12,8},{16,12},{20,16},{24,20},{28,24},{5,1},{9,5},{13... | collective-permute-start | bytes 1179656 | tf_op jit(solution)/shard_map/ppermute | solution.py:769
  530.3 19.7 %collective-permute-start.45 = (bf16[256,768]{1,0:T(8,128)(2,1)S(1)}, bf16[256,768]{1,0:T(8,128)(2,1)S(1)}, u32[]{:S(2)}, u32[]{:S(2)}) collective-permute-start(bf16[256,768]{1,0:T(8,128)(2,1)S(1)} %fusion.14), channel_id=1, source_target_pairs={{8,0},{12,4},{16,8},{20,12},{24,16},{28,20},{9,1},{13,5},{17,9},{2... | collective-permute-start | bytes 1179656 | tf_op jit(solution)/shard_map/ppermute | solution.py:769
  531.6 21.2 %collective-permute-start.46 = (bf16[256,768]{1,0:T(8,128)(2,1)S(1)}, bf16[256,768]{1,0:T(8,128)(2,1)S(1)}, u32[]{:S(2)}, u32[]{:S(2)}) collective-permute-start(bf16[256,768]{1,0:T(8,128)(2,1)S(1)} %fusion.14), channel_id=1, source_target_pairs={{12,0},{16,4},{20,8},{24,12},{28,16},{13,1},{17,5},{21,9},{25,13},... | collective-permute-start | bytes 1179656 | tf_op jit(solution)/shard_map/ppermute | solution.py:769
  533.4 44.0 %collective-permute-start.48 = (bf16[512,512]{1,0:T(8,128)(2,1)S(1)}, bf16[512,512]{1,0:T(8,128)(2,1)S(1)}, u32[]{:S(2)}, u32[]{:S(2)}) collective-permute-start(bf16[512,512]{1,0:T(8,128)(2,1)S(1)} %copy-done.23), channel_id=1, source_target_pairs={{0,8},{4,12},{8,0},{12,4},{16,24},{20,28},{24,16},{28,20},{1,9},{5... | collective-permute-start | bytes 1572872 | tf_op jit(solution)/shard_map/ppermute | solution.py:757
  564.7 32.9 %collective-permute-start.47 = (bf16[256,1536]{1,0:T(8,128)(2,1)S(1)}, bf16[256,1536]{1,0:T(8,128)(2,1)S(1)}, u32[]{:S(2)}, u32[]{:S(2)}) collective-permute-start(bf16[256,1536]{1,0:T(8,128)(2,1)S(1)} %get-tuple-element.399.refs_10_.refs_2_), channel_id=1, source_target_pairs={{0,1},{3,2},{1,0},{2,3},{4,5},{7,6},{5,4},{6,7},{8,9},{11,10},{9,8... | collective-permute-start | bytes 2359304 | tf_op jit(solution)/shard_map/ppermute | solution.py:858
  565.0 22.2 %collective-permute-start.54 = (bf16[512,512]{1,0:T(8,128)(2,1)S(1)}, bf16[512,512]{1,0:T(8,128)(2,1)S(1)}, u32[]{:S(2)}, u32[]{:S(2)}) collective-permute-start(bf16[512,512]{1,0:T(8,128)(2,1)S(1)} %copy-done.19), channel_id=1, source_target_pairs={{0,4},{4,0},{8,12},{12,8},{16,20},{20,16},{24,28},{28,24},{1,5},{5... | collective-permute-start | bytes 1572872 | tf_op jit(solution)/shard_map/ppermute | solution.py:705
  587.2 25.1 %collective-permute-start.56 = (bf16[512,512]{1,0:T(8,128)(2,1)}, bf16[512,512]{1,0:T(8,128)(2,1)S(1)}, u32[]{:S(2)}, u32[]{:S(2)}) collective-permute-start(bf16[512,512]{1,0:T(8,128)(2,1)} %collective-permute-done.43.refs_4_.refs_7_), channel_id=1, source_target_pairs={{0,4},{4,0},{8,12},{12,8},{16,20},{20,16},{24,28},{28,24},{1,5},{5... | collective-permute-start | bytes 1572872 | tf_op jit(solution)/shard_map/ppermute | solution.py:705
  587.3 29.5 %collective-permute-start.57 = (bf16[512,512]{1,0:T(8,128)(2,1)S(1)}, bf16[512,512]{1,0:T(8,128)(2,1)S(1)}, u32[]{:S(2)}, u32[]{:S(2)}) collective-permute-start(bf16[512,512]{1,0:T(8,128)(2,1)S(1)} %copy-done.23), channel_id=1, source_target_pairs={{0,4},{4,0},{8,12},{12,8},{16,20},{20,16},{24,28},{28,24},{1,5},{5... | collective-permute-start | bytes 1572872 | tf_op jit(solution)/shard_map/ppermute | solution.py:705
  587.8 29.0 %collective-permute-start.58 = (bf16[512,512]{1,0:T(8,128)(2,1)S(1)}, bf16[512,512]{1,0:T(8,128)(2,1)S(1)}, u32[]{:S(2)}, u32[]{:S(2)}) collective-permute-start(bf16[512,512]{1,0:T(8,128)(2,1)S(1)} %collective-permute-done.48.refs_8_.refs_3_), channel_id=1, source_target_pairs={{0,4},{4,0},{8,12},{12,8},{16,20},{20,16},{24,28},{28,24},{1,5},{5... | collective-permute-start | bytes 1572872 | tf_op jit(solution)/shard_map/ppermute | solution.py:705
  595.1 21.8 %collective-permute-start.59 = (bf16[512,512]{1,0:T(8,128)(2,1)}, bf16[512,512]{1,0:T(8,128)(2,1)S(1)}, u32[]{:S(2)}, u32[]{:S(2)}) collective-permute-start(bf16[512,512]{1,0:T(8,128)(2,1)} %collective-permute-done.49.refs_9_.refs_5_), channel_id=1, source_target_pairs={{0,4},{4,0},{8,12},{12,8},{16,20},{20,16},{24,28},{28,24},{1,5},{5... | collective-permute-start | bytes 1572872 | tf_op jit(solution)/shard_map/ppermute | solution.py:705
  622.8 155.7 %reduce-scatter.6.cloned.1.call-start = ((), (), s32[]{:S(2)}) async-start(), calls=%async_computation.6 | async-start | bytes 7077888 | tf_op jit(solution)/shard_map/reduce_scatter | solution.py:920
  644.0 270.1 %reduce-scatter.8.cloned.1.call-start = ((), (), s32[]{:S(2)}) async-start(), calls=%async_computation.7 | async-start | bytes 5308416 | tf_op jit(solution)/shard_map/reduce_scatter | solution.py:920
  710.1 23.5 %collective-permute-start.67 = (bf16[256,1536]{1,0:T(8,128)(2,1)}, bf16[256,1536]{1,0:T(8,128)(2,1)S(1)}, u32[]{:S(2)}, u32[]{:S(2)}) collective-permute-start(bf16[256,1536]{1,0:T(8,128)(2,1)} %get-tuple-element.315.refs_2_), channel_id=1, source_target_pairs={{0,1},{3,2},{1,0},{2,3},{4,5},{7,6},{5,4},{6,7},{8,9},{11,10},{9,8... | collective-permute-start | bytes 2359304 | tf_op jit(solution)/shard_map/ppermute | solution.py:858
  712.5 21.1 %collective-permute-start.68 = (bf16[256,1536]{1,0:T(8,128)(2,1)}, bf16[256,1536]{1,0:T(8,128)(2,1)S(1)}, u32[]{:S(2)}, u32[]{:S(2)}) collective-permute-start(bf16[256,1536]{1,0:T(8,128)(2,1)} %get-tuple-element.316.refs_4_), channel_id=1, source_target_pairs={{1,2},{2,1},{5,6},{6,5},{9,10},{10,9},{13,14},{14,13},{17,18},{18,... | collective-permute-start | bytes 2359304 | tf_op jit(solution)/shard_map/ppermute | solution.py:858
  781.0 30.6 %collective-permute-start.69 = (bf16[256,1536]{1,0:T(8,128)(2,1)}, bf16[256,1536]{1,0:T(8,128)(2,1)}, u32[]{:S(2)}, u32[]{:S(2)}) collective-permute-start(bf16[256,1536]{1,0:T(8,128)(2,1)} %get-tuple-element.322.refs_2_), channel_id=1, source_target_pairs={{0,1},{3,2},{1,0},{2,3},{4,5},{7,6},{5,4},{6,7},{8,9},{11,10},{9,8... | collective-permute-start | bytes 2359304 | tf_op jit(solution)/shard_map/ppermute | solution.py:858
  782.6 29.1 %collective-permute-start.70 = (bf16[256,1536]{1,0:T(8,128)(2,1)}, bf16[256,1536]{1,0:T(8,128)(2,1)}, u32[]{:S(2)}, u32[]{:S(2)}) collective-permute-start(bf16[256,1536]{1,0:T(8,128)(2,1)} %get-tuple-element.323.refs_4_), channel_id=1, source_target_pairs={{1,2},{2,1},{5,6},{6,5},{9,10},{10,9},{13,14},{14,13},{17,18},{18,... | collective-permute-start | bytes 2359304 | tf_op jit(solution)/shard_map/ppermute | solution.py:858
  855.1 20.1 %collective-permute-start.71 = (bf16[256,1536]{1,0:T(8,128)(2,1)}, bf16[256,1536]{1,0:T(8,128)(2,1)S(1)}, u32[]{:S(2)}, u32[]{:S(2)}) collective-permute-start(bf16[256,1536]{1,0:T(8,128)(2,1)} %get-tuple-element.336.refs_2_), channel_id=1, source_target_pairs={{0,1},{3,2},{1,0},{2,3},{4,5},{7,6},{5,4},{6,7},{8,9},{11,10},{9,8... | collective-permute-start | bytes 2359304 | tf_op jit(solution)/shard_map/ppermute | solution.py:858
  855.2 20.0 %collective-permute-start.72 = (bf16[256,1536]{1,0:T(8,128)(2,1)}, bf16[256,1536]{1,0:T(8,128)(2,1)S(1)}, u32[]{:S(2)}, u32[]{:S(2)}) collective-permute-start(bf16[256,1536]{1,0:T(8,128)(2,1)} %get-tuple-element.337.refs_4_), channel_id=1, source_target_pairs={{1,2},{2,1},{5,6},{6,5},{9,10},{10,9},{13,14},{14,13},{17,18},{18,... | collective-permute-start | bytes 2359304 | tf_op jit(solution)/shard_map/ppermute | solution.py:858
  879.8 34.2 %collective-permute-start.73 = (bf16[256,1536]{1,0:T(8,128)(2,1)}, bf16[256,1536]{1,0:T(8,128)(2,1)S(1)}, u32[]{:S(2)}, u32[]{:S(2)}) collective-permute-start(bf16[256,1536]{1,0:T(8,128)(2,1)} %get-tuple-element.351.refs_2_), channel_id=1, source_target_pairs={{0,1},{3,2},{1,0},{2,3},{4,5},{7,6},{5,4},{6,7},{8,9},{11,10},{9,8... | collective-permute-start | bytes 2359304 | tf_op jit(solution)/shard_map/ppermute | solution.py:858
  (146 other events, 1201.2 us)
Sparse Core Ops, SparseCore 0:
  98.2 39.2 all-gather.2
  293.9 80.6 all-gather.4
  623.0 90.5 reduce-scatter.3
  716.8 61.7 reduce-scatter.5
  782.2 69.2 reduce-scatter.7

commit v8 on v7

--- a/solution.py
+++ b/solution.py
@@ -764,11 +764,6 @@
     pieces = Gather.pieces
 
 
-def shift(x, by):
-    size = lax.axis_size("wide")
-    return lax.ppermute(x, "wide", [(i, i + by) for i in range(size) if 0 <= i + by < size])
-
-
 def pick(order, sc, pieces, count):
     if not isinstance(pieces[0], list):
         one = lambda x, j: lax.dynamic_index_in_dim(x, sc[1 + SPAN + j], 0, False)
@@ -787,38 +782,68 @@
     )
 
 
+def tree(parts):
+    while len(parts) > 1:
+        parts = [a + b for a, b in zip(parts[::2], parts[1::2])]
+    return parts[0]
+
+
+def pack_kernel(count, place, *refs):
+    c1, hs = refs[:count], refs[count : 2 * count]
+    hc_ref, gs_ref, tg_ref, c2_ref, c3_ref, c4_ref, o_ref = refs[2 * count :]
+    n = hc_ref.shape[1]
+    o_ref[...] = jnp.zeros_like(o_ref)
+    o_ref[0:1, :] = sum(x[...] for x in c1)
+    o_ref[1:2, :] = c2_ref[...]
+    o_ref[2:3, :] = c3_ref[...]
+    o_ref[3:4, :] = c4_ref[...]
+    qk = sum(x[...] for x in hs)
+    o_ref[4:5, :n] = qk[0:1]
+    o_ref[4:5, n : 2 * n] = qk[1:2]
+    o_ref[4:5, 2 * n : 3 * n] = hc_ref[...]
+    gate = gs_ref[...] * (1.0 - tg_ref[...] * tg_ref[...])
+    for z in range(o_ref.shape[1] // n):
+        o_ref[5:6, z * n : (z + 1) * n] = jnp.where(place[0] == z, gate, 0.0)
+
+
+def pack_call(order, c1, hs, hc, gs, tg, c2, c3, c4, place):
+    d = c2.shape[1]
+    ins = (*c1, *hs, hc, gs, tg, c2, c3, c4)
+    spec = lambda x: pl.BlockSpec(x.shape, lambda i, s: (0, 0))
+
+    def kernel(place, *refs):
+        pack_kernel(len(c1), place, *refs)
+
+    return order.run(
+        "note",
+        kernel,
+        (1,),
+        ins,
+        [spec(x) for x in ins],
+        [pl.BlockSpec((8, d), lambda i, s: (0, 0))],
+        [sds((8, d), f32)],
+        scalar=place.astype(jnp.int32).reshape(1),
+    )[0]
+
+
+def fold_kernel(*refs):
+    parts, o_ref = refs[:-1], refs[-1]
+    total = tree([x[...] for x in parts])
+    row_at = lax.broadcasted_iota(jnp.int32, total.shape, 0)
+    o_ref[...] = jnp.where((row_at >= 1) & (row_at < 4), parts[0][...], total)
+
+
+def fold_call(order, parts):
+    spec = pl.BlockSpec(parts[0].shape, lambda i: (0, 0))
+    return order.run("note", fold_kernel, (1,), parts, [spec] * len(parts), [spec], [sds(parts[0].shape, f32)])
+
+
 def pin_kernel(o_ref):
     pass
 
 
 def pin(order, x, after=()):
     return order.run("pin", pin_kernel, (1,), (), [], loose(1), [sds(x.shape, x.dtype)], held=(x,), after=after)[0]
-
-
-def note_kernel(x_ref, o_ref):
-    o_ref[...] = x_ref[...]
-
-
-def note(order, x):
-    n = x.shape[0]
-    size = -(-n // 1024) * 8
-    x = jnp.pad(x, (0, size * 128 - n)).reshape(size, 128)
-    spec = pl.BlockSpec(x.shape, lambda i: (0, 0))
-    return order.run("note", note_kernel, (1,), (x,), [spec], [spec], [sds(x.shape, f32)])[0].reshape(-1)[:n]
-
-
-def gather_small(x, axis):
-    n = x.shape[0]
-    wide = -(-n // 1024) * 1024
-    x = jnp.pad(x, (0, wide - n)).reshape(wide // 128, 128)
-    size = lax.axis_size(axis)
-    if size > 8:
-        return lax.all_gather(x, axis).reshape(size, wide)[:, :n]
-    got = jnp.stack([x] + [swap(x, axis, size, m) for m in range(1, size)])
-    order = jnp.arange(size, dtype=jnp.int32)
-    mine = (order[:, None] ^ lax.axis_index(axis)) == order[None, :]
-    out = jnp.sum(jnp.where(mine[:, :, None, None], got[None], 0.0), 1)
-    return out.reshape(size, wide)[:, :n]
 
 
 def gather_now(x, axis):
@@ -1001,12 +1026,6 @@
     tg = jnp.repeat(tg_heads, HD)[None, :]
 
     order = Order()
-    chunks = range(t // BR)
-    pairs_of = range(t // (2 * BR))
-    sums = Sums(order, deep, mz)
-    a1, k_raw, k, v = key_call(order, patches, vec, w_qkv, tabs, hg, ())
-    kv = Gather(k, v)
-
     cap_raw = jnp.einsum("kd,jde->jke", captions, w_caption, preferred_element_type=f32)
     whole_cap = pl.BlockSpec((text, n), lambda i: (0, 0))
     both_cap = pl.BlockSpec((text, 2 * n), lambda i: (0, 0))
@@ -1019,9 +1038,15 @@
         [both_cap],
         [sds((text, 2 * n), bf16)],
     )
-    offset = me - first
+    cap = lax.all_gather(cap, "wide", axis=0, tiled=True)
+
+    chunks = range(t // BR)
+    pairs_of = range(t // (2 * BR))
+    sums = Sums(order, deep, mz)
+    a1, k_raw, k, v = key_call(order, patches, vec, w_qkv, tabs, hg, ())
+    kv = Gather(k, v)
+
     q_raw, q = query_call(order, a1, w_qkv, tabs, hg, ())
-    cap = lax.all_gather(pin(order, cap, kv.first), "wide", axis=0, tiled=True)
 
     q_all = lax.all_gather(q, "wide", axis=0, tiled=True)
     k_all, v_all = pick(order, sc, kv.pieces(), SPAN)
@@ -1079,10 +1104,9 @@
         dck, dcv, gate_sum = dck + pk, dcv + pv, gate_sum + pg
     d_attn = whole_out[0]
     cap_sum = jnp.concatenate([dck, dcv], 1)
-    cap_low = cap_sum.astype(bf16)
-    for by in range(1, SPAN):
-        cap_sum = cap_sum + jnp.where(by < length, shift(cap_low, -by).astype(f32), 0.0)
-    cap_sum = jnp.where(offset == 0, cap_sum, 0.0)
+    cap_got = lax.all_gather(cap_sum.astype(bf16), "wide")
+    kept = (firsts == me)[:, None, None]
+    cap_sum = jnp.sum(jnp.where(kept, cap_got.astype(f32), 0.0), 0)
     last_half = pairs_of[-1]
 
     def make_dq(h, after):
@@ -1112,59 +1136,55 @@
     ds = [x for h in pairs_of for x in pick(order, sc, d_got[h].pieces(), SPAN)]
     g_mlp = scatter_rows(pin(order, mlp_part[0]))
     whole_out = ()
-    c1 = hs_qk = 0.0
+    c1_parts, hs_parts = [], []
     mixed = jnp.concatenate([heads_out[c][0] for c in chunks[:half]] + [later[0]])
     pairs = n // 128
 
     def project(c, dkv, after=()):
-        nonlocal whole_out, c1, hs_qk
+        nonlocal whole_out
         da1_part, p_hs, p1, *whole_out = dqkv_call(order, c, dqs[c // 2], dkv, q_raw, k_raw, tabs, hg, w_qkv, patches, whole_out)
-        hs_qk, c1 = hs_qk + p_hs, c1 + p1
+        hs_parts.append(p_hs)
+        c1_parts.append(p1)
         return da1_part
 
     dkv = [dkv_call(order, sc, k, v, q_all, ds, 0, 0, pairs)]
     for p in range(2, pieces):
         sums.add(("text", p), text_parts[p])
     g_cap = scatter_rows(pin(order, cap_part))
-    sums.add(("da1", 0), project(0, dkv))
-    da1_part = project(1, dkv)
-    dkv = [dkv_call(order, sc, k, v, q_all, ds, 1, 0, 1)]
+    first_part = project(0, dkv)
+    parts_of = lambda p: dkv_call(order, sc, k, v, q_all, ds, 1, p, 1)
+    first_dkv, dkv = dkv, [parts_of(0)]
+    sums.add(("da1", 0), first_part)
+    da1_part = project(1, first_dkv)
+    dkv.append(parts_of(1))
     sums.add(("da1", 1), da1_part)
-    dkv.append(dkv_call(order, sc, k, v, q_all, ds, 1, 1, pairs - 1))
+    dkv += [parts_of(p) for p in range(2, pairs)]
     for c in chunks[2:]:
         da1_part = project(c, dkv)
         if c == chunks[-1]:
-            (d_qkv,) = whole_out
+            d_qkv = whole_out[0]
+            packed = pack_call(order, c1_parts, hs_parts, hs_c, gate_sum, tg, c2, c3, c4, mz)
+            from_narrow = [packed] + [swap(packed, "narrow", deep, m) for m in range(1, deep)]
             attn_part = pair_grad_call(order, a1, d_qkv, d_attn, mixed)[0]
-        sums.add(("da1", c), da1_part, (g_mlp,) if c == chunks[-1] else ())
+            (folded,) = fold_call(order, from_narrow)
+            got = lax.all_gather(folded, "wide")
+        sums.add(("da1", c), da1_part, (g_mlp, got) if c == chunks[-1] else ())
     g_attn = scatter_rows(pin(order, attn_part))
 
-    head_part = jnp.concatenate([hs_qk, hs_c]).reshape(3, heads, HD).sum(1)
-    gate_part = gate_sum[0, ::HD] * (1.0 - tg_heads * tg_heads)
-    got_narrow = gather_now(note(order, jnp.concatenate([c1[0], head_part.reshape(-1), gate_part])), "narrow")
-    whole_out = last_call(order, 0, sums.get(("da1", 0)), patches, d_mids[0], vec, ())
-    da1 = sums.get(("da1", 1), (g_cap, got_narrow))
-    summed = jnp.sum(got_narrow[:, : d + 3 * HD], 0)
-    sent = note(order, jnp.concatenate([summed, got_narrow[:, d + 3 * HD :].reshape(-1), c2[0], c3[0], c4[0]]))
-    got_wide = gather_now(sent, "wide")
-    whole_out = last_call(order, 1, da1, patches, d_mids[1], vec, whole_out)
-    da1 = sums.get(("da1", 2), (got_wide,))
-    for c in chunks[2:]:
-        whole_out = last_call(order, c, da1 if c == 2 else sums.get(("da1", c), (g_attn,)), patches, d_mids[c], vec, whole_out)
+    whole_out = ()
+    for c in chunks:
+        whole_out = last_call(order, c, sums.get(("da1", c), (g_cap,) if c < 3 else (g_attn,)), patches, d_mids[c], vec, whole_out)
     (grad_patches,) = whole_out
     grad_captions = jnp.concatenate([sums.get(("text", p)) for p in range(pieces)], 1)[:, : d_text.shape[1]]
 
-    got = got_wide
-    one, rest = got[:, :d], got[:, d:]
-    grad_head_gains = jnp.sum(rest[:, : 3 * HD], 0).reshape(3, HD)
-    grad_cross_gate = jnp.sum(rest[:, 3 * HD : 3 * HD + deep * heads], 0)
-    two, three, four = (rest[:, 3 * HD + deep * heads + k * d :][:, :d] for k in range(3))
-    cols = jnp.stack([one, two, three, four], 1)
+    cols = got[:, :4]
+    grad_head_gains = jnp.sum(got[:, 4, : 3 * n], 0).reshape(3, heads, HD).sum(1)
+    grad_cross_gate = jnp.sum(got[:, 5], 0)[::HD]
     gain_factor = jnp.stack([scales[:, 0], gates[:, 1], scales[:, 2], gates[:, 3]], 1)
     gain_grads = jnp.sum(gain_factor * cols, 0)
     wide_cols = d // count
     grad_norm_gains = lax.dynamic_slice_in_dim(gain_grads, me * wide_cols, wide_cols, 1)
-    ones = jnp.ones_like(one)
+    ones = jnp.ones_like(gates[:, 0])
     slope = jnp.stack([ones, 1.0 - gates[:, 1] ** 2, ones, 1.0 - gates[:, 3] ** 2], 1)
     d_mod = lax.dynamic_slice_in_dim(slope * norm_gains[None] * cols, mz * ada, ada, 2)
     at_slot = (firsts[None, :] == blocks[:, None]).astype(f32)
@@ -1174,7 +1194,8 @@
     grad_ada = jnp.sum(silu_mine[:, :, None, None] * d_slots[:, None], 0)
     d_mine = lax.dynamic_index_in_dim(d_slots, me, 0, False)
     cond_part = jnp.sum(d_mine[None] * w_ada.astype(f32), (1, 2))
-    cond_total = jnp.sum(gather_now(cond_part, "narrow"), 0)
+    cond_part = cond_part.reshape(-1, 128)
+    cond_total = tree([cond_part] + [swap(cond_part, "narrow", deep, m) for m in range(1, deep)]).reshape(-1)
     pull_silu = jax.vjp(jax.nn.silu, cond)[1]
     grad_conditioning = pull_silu(cond_total)[0].reshape(1, -1)
 

time: 936 us -> 880 us (0.940)
  Pallas kernels: 375 us -> 472 us
  blocking collectives: 103 us -> 35.6 us
  waiting for transfers between devices: 165 us -> 118 us
  starting transfers between devices: 156 us -> 119 us
    pallas_call x69, Pallas kernels: 375 us -> 472 us  [run(): pl.pallas_call(body, grid_spec=pltpu.PrefetchScalarGridSpec(num_scalar_pr...]
    all_gather x5 -> x2, blocking collectives: 103 us -> 25.2 us  [gather_now(): lax.all_gather(padded, axis, axis=0, tiled=True).reshape(-1, wide)[:, :n]]
    reduce_scatter x3, waiting for transfers between devices: 35.2 us -> 0.02 us  [scatter_rows(): lax.psum_scatter(x.astype(bf16), 'wide', scatter_dimension=0, tiled=True)]
    ppermute x13, starting transfers between devices: 52.6 us -> 27.2 us  [__init__(): send = lambda x, pairs: lax.ppermute(x, 'wide', pairs)]
    ppermute x13, waiting for transfers between devices: 55.5 us -> 42.9 us  [__init__(): send = lambda x, pairs: lax.ppermute(x, 'wide', pairs)]
    all_gather x0 -> x1, blocking collectives: none -> 10.4 us  [local(): got = lax.all_gather(folded, 'wide')]
    unnamed x237 -> x223, local copies, waits for them, and re-layouts: 35.5 us -> 35.1 us
  transfers between devices with their start and end apart: 79 -> 83, of which waited for: 21 -> 17; matrix products, arithmetic and copies ran while one was open for 6% -> 7% of each run, Pallas kernels for 36% -> 45%
where the time goes in v8:
time: 880 us; the launch traced here: 871 us
  Pallas kernels  472 us (54%)
  starting transfers between devices  119 us (14%)
  waiting for transfers between devices  118 us (13%)
  local copies, waits for them, and re-layouts  46.9 us (5%)
  blocking collectives  35.6 us (4%)
  other arithmetic  34.5 us (4%)
  matrix products  24.4 us (3%)
  between operations  21.5 us (2%)
    pallas_call x69, Pallas kernels, run(): pl.pallas_call(body, grid_spec=pltpu.PrefetchScalarGridSpec(num_scalar_pr...  472 us
    ppermute x42, starting transfers between devices, step(): go = lambda x, perm: lax.ppermute(x, 'narrow', perm)  77.7 us
    ppermute x42, waiting for transfers between devices, step(): go = lambda x, perm: lax.ppermute(x, 'narrow', perm)  69.8 us
    ppermute x13, waiting for transfers between devices, __init__(): send = lambda x, pairs: lax.ppermute(x, 'wide', pairs)  42.9 us
    unnamed x223, local copies, waits for them, and re-layouts  35.1 us
    ppermute x13, starting transfers between devices, __init__(): send = lambda x, pairs: lax.ppermute(x, 'wide', pairs)  27.2 us
    all_gather x2, blocking collectives, gather_now(): lax.all_gather(padded, axis, axis=0, tiled=True).reshape(-1, wide)[:, :n]  25.2 us
  transfers between devices with their start and end apart: 83, of which 17 were waited for; matrix products, arithmetic and copies ran while one was open for 7% of the time, Pallas kernels for 45%

profile of v8, /device:TPU:0, one launch (start us, length us, event | category | flops | bytes accessed | tf_op | source)
XLA Modules:
  0.0 871.3 jit_solution(15869886257855781886)
XLA Ops:
  26.2 14.9 %all_gather.22 = f32[4,8,256]{2,1,0:T(8,128)S(1)} all-gather(f32[1,8,256]{2,1,0:T(8,128)S(1)} %reshape.309), channel_id=1, replica_groups=mesh['wide'=8,'narrow'=4] {'narrow'}, dimensions={0}, use_global_device_ids=true | all-gather | bytes 40960 | tf_op jit(solution)/shard_map/all_gather | solution.py:853
  41.1 10.3 %all_gather.23 = f32[8,8,896]{2,1,0:T(8,128)S(1)} all-gather(f32[1,8,896]{2,1,0:T(8,128)S(1)} %reshape.311), channel_id=1, replica_groups=mesh['wide'=8,'narrow'=4] {'wide'}, dimensions={0}, use_global_device_ids=true | all-gather | bytes 258048 | tf_op jit(solution)/shard_map/all_gather | solution.py:853
  57.8 9.0 %key.1 = (bf16[1024,1536]{1,0:T(8,128)(2,1)}, f32[1024,384]{1,0:T(8,128)}, bf16[1024,384]{1,0:T(8,128)(2,1)}, bf16[1024,384]{1,0:T(8,128)(2,1)}) custom-call(bf16[1024,1536]{1,0:T(8,128)(2,1)} %refs_1_.9, f32[4,1536]{1,0:T(4,128)} %maximum_multiply_fusion.1.refs_1_.refs_2_.refs_4_.refs_3_, bf16[3,1536,384]{2,1,0:T(8,128)(2,1)} %refs_13_.3, ...), custom_call_target="tpu_custom_call" | custom-call | flops 2000000000 | bytes 6000000 | tf_op jit(solution)/shard_map/key/pallas_call | solution.py:51
  70.3 17.3 %collective-permute-done.8.refs_11_ = bf16[1024,384]{1,0:T(8,128)(2,1)} collective-permute-done((bf16[1024,384]{1,0:T(8,128)(2,1)}, bf16[1024,384]{1,0:T(8,128)(2,1)}, u32[]{:S(2)}, u32[]{:S(2)}) %collective-permute-start.8) | collective-permute-done | bytes 786464 | tf_op jit(solution)/shard_map/ppermute | solution.py:734
  93.8 10.1 %collective-permute-done.1.refs_3_ = bf16[1024,384]{1,0:T(8,128)(2,1)} collective-permute-done((bf16[1024,384]{1,0:T(8,128)(2,1)}, bf16[1024,384]{1,0:T(8,128)(2,1)}, u32[]{:S(2)}, u32[]{:S(2)}) %collective-permute-start.1) | collective-permute-done | bytes 786464 | tf_op jit(solution)/shard_map/ppermute | solution.py:734
  103.9 5.3 collective-permute-done.12
  109.2 5.3 collective-permute-start.5
  115.9 10.2 %collective-permute-done.5.refs_7_ = bf16[1024,384]{1,0:T(8,128)(2,1)} collective-permute-done((bf16[1024,384]{1,0:T(8,128)(2,1)}, bf16[1024,384]{1,0:T(8,128)(2,1)}, u32[]{:S(2)}, u32[]{:S(2)}) %collective-permute-start.5) | collective-permute-done | bytes 786464 | tf_op jit(solution)/shard_map/ppermute | solution.py:734
  130.9 7.0 query.1
  137.9 6.1 pick.3
  144.1 18.1 %attend.3 = (bf16[256,384]{1,0:T(8,128)(2,1)}, bf16[256,384]{1,0:T(8,128)(2,1)}, f32[256,384]{1,0:T(8,128)}) custom-call(s32[9]{0:T(128)} %pad_add_fusion.refs_0_, bf16[1024,384]{1,0:T(8,128)(2,1)} %get-tuple-element.186.refs_1_, bf16[4096,384]{1,0:T(8,128)(2,1)} %get-tuple-element.190.refs_2_.refs_7_.refs_4_, ...), custom_call_target="tpu_custom_call" | custom-call | flops 4499999744 | bytes 13500000 | tf_op jit(solution)/shard_map/attend/pallas_call | solution.py:51
  166.2 18.0 %attend.4 = (bf16[256,384]{1,0:T(8,128)(2,1)}, bf16[256,384]{1,0:T(8,128)(2,1)}, f32[256,384]{1,0:T(8,128)}) custom-call(s32[9]{0:T(128)} %pad_add_fusion.refs_0_, bf16[1024,384]{1,0:T(8,128)(2,1)} %get-tuple-element.186.refs_1_, bf16[4096,384]{1,0:T(8,128)(2,1)} %get-tuple-element.190.refs_2_.refs_7_.refs_4_, ...), custom_call_target="tpu_custom_call" | custom-call | flops 4499999744 | bytes 13500000 | tf_op jit(solution)/shard_map/attend/pallas_call | solution.py:51
  190.3 22.3 %attend.5 = (bf16[512,384]{1,0:T(8,128)(2,1)}, bf16[512,384]{1,0:T(8,128)(2,1)}, f32[512,384]{1,0:T(8,128)}) custom-call(s32[9]{0:T(128)} %pad_add_fusion.refs_0_, bf16[1024,384]{1,0:T(8,128)(2,1)} %get-tuple-element.186.refs_1_, bf16[4096,384]{1,0:T(8,128)(2,1)} %get-tuple-element.190.refs_2_.refs_7_.refs_4_, ...), custom_call_target="tpu_custom_call" | custom-call | flops 4499999744 | bytes 13500000 | tf_op jit(solution)/shard_map/attend/pallas_call | solution.py:51
  225.7 15.7 %collective-permute-done.18.refs_1_ = bf16[256,1536]{1,0:T(8,128)(2,1)S(1)} collective-permute-done((bf16[256,1536]{1,0:T(8,128)(2,1)}, bf16[256,1536]{1,0:T(8,128)(2,1)S(1)}, u32[]{:S(2)}, u32[]{:S(2)}) %collective-permute-start.18) | collective-permute-done | bytes 786464 | tf_op jit(solution)/shard_map/ppermute | solution.py:883
  250.3 8.5 ffn.4
  258.8 7.6 collective-permute-done.20.refs_1_
  275.1 8.5 ffn.5
  283.6 6.9 collective-permute-done.22.refs_1_
  299.3 8.5 ffn.6
  307.8 6.0 collective-permute-done.24.refs_1_
  322.5 8.5 ffn.7
  345.3 9.5 %ffn_back.4 = (bf16[256,1536]{1,0:T(8,128)(2,1)}, f32[1,1536]{1,0:T(1,128)}, bf16[1024,1536]{1,0:T(8,128)(2,1)}, bf16[1024,1536]{1,0:T(8,128)(2,1)}, bf16[1024,2048]{1,0:T(8,128)(2,1)}) custom-call(bf16[256,1536]{1,0:T(8,128)(2,1)} %get-tuple-element.227.refs_0_.refs_7_, f32[256,1536]{1,0:T(8,128)} %get-tuple-element.203.refs_7_.refs_1_, ...), custom_call_target="tpu_custom_call" | custom-call | flops 2500000000 | bytes 7500000 | tf_op jit(solution)/shard_map/ffn_back/pallas_call | solution.py:51
  366.2 9.6 %ffn_back.5 = (bf16[256,1536]{1,0:T(8,128)(2,1)}, f32[1,1536]{1,0:T(1,128)}, bf16[1024,1536]{1,0:T(8,128)(2,1)}, bf16[1024,1536]{1,0:T(8,128)(2,1)}, bf16[1024,2048]{1,0:T(8,128)(2,1)}) custom-call(bf16[256,1536]{1,0:T(8,128)(2,1)} %get-tuple-element.232.refs_0_.refs_7_, ...), custom_call_target="tpu_custom_call", output_to_operand_aliasing={{2}: (8, {}), {3}: (9, {}), {4}: (10, {})} | custom-call | flops 2500000000 | bytes 7500000 | tf_op jit(solution)/shard_map/ffn_back/pallas_call | solution.py:51
  386.8 9.6 %ffn_back.6 = (bf16[256,1536]{1,0:T(8,128)(2,1)}, f32[1,1536]{1,0:T(1,128)}, bf16[1024,1536]{1,0:T(8,128)(2,1)}, bf16[1024,1536]{1,0:T(8,128)(2,1)}, bf16[1024,2048]{1,0:T(8,128)(2,1)}) custom-call(bf16[256,1536]{1,0:T(8,128)(2,1)} %get-tuple-element.240.refs_0_.refs_7_, ...), custom_call_target="tpu_custom_call", output_to_operand_aliasing={{2}: (8, {}), {3}: (9, {}), {4}: (10, {})} | custom-call | flops 2500000000 | bytes 7500000 | tf_op jit(solution)/shard_map/ffn_back/pallas_call | solution.py:51
  406.5 9.6 %ffn_back.7 = (bf16[256,1536]{1,0:T(8,128)(2,1)}, f32[1,1536]{1,0:T(1,128)}, bf16[1024,1536]{1,0:T(8,128)(2,1)}, bf16[1024,1536]{1,0:T(8,128)(2,1)}, bf16[1024,2048]{1,0:T(8,128)(2,1)}) custom-call(bf16[256,1536]{1,0:T(8,128)(2,1)} %get-tuple-element.246.refs_0_.refs_7_, ...), custom_call_target="tpu_custom_call", output_to_operand_aliasing={{2}: (8, {}), {3}: (9, {}), {4}: (10, {})} | custom-call | flops 2500000000 | bytes 7500000 | tf_op jit(solution)/shard_map/ffn_back/pallas_call | solution.py:51
  424.9 5.6 out_back.4
  430.6 9.9 %pair_grad.3.refs_6_.refs_7_ = bf16[1536,3072]{1,0:T(8,128)(2,1)} custom-call(bf16[1024,1536]{1,0:T(8,128)(2,1)} %get-tuple-element.261.refs_0_, bf16[1024,2048]{1,0:T(8,128)(2,1)} %get-tuple-element.262.refs_1_, bf16[1024,1536]{1,0:T(8,128)(2,1)} %get-tuple-element.263.refs_2_, bf16[1024,1024]{1,0:T(8,128)(2,1)} %get-tuple-element.264.refs_3_, ...), custom_call_target="tpu_custom_call" | custom-call | flops 2500000000 | bytes 7500000 | tf_op jit(solution)/shard_map/pair_grad/pallas_call | solution.py:51
  447.7 5.7 out_back.5
  454.3 6.3 caption_back.2
  473.7 5.7 out_back.6
  480.2 9.9 %pair_grad.4.refs_3_.refs_1_ = bf16[1536,3072]{1,0:T(8,128)(2,1)} custom-call(bf16[1024,1536]{1,0:T(8,128)(2,1)} %get-tuple-element.261.refs_0_, bf16[1024,2048]{1,0:T(8,128)(2,1)} %get-tuple-element.262.refs_1_, bf16[1024,1536]{1,0:T(8,128)(2,1)} %get-tuple-element.263.refs_2_, ...), custom_call_target="tpu_custom_call", output_to_operand_aliasing={{}: (7, {})} | custom-call | flops 2500000000 | bytes 7500000 | tf_op jit(solution)/shard_map/pair_grad/pallas_call | solution.py:51
  493.9 5.7 out_back.7
  499.7 6.4 caption_back.3
  512.1 26.8 %dq.2.refs_4_.refs_0_ = f32[512,384]{1,0:T(8,128)} custom-call(s32[9]{0:T(128)} %pad_add_fusion.refs_0_, bf16[1024,384]{1,0:T(8,128)(2,1)} %get-tuple-element.186.refs_1_, bf16[512,512]{1,0:T(8,128)(2,1)} %get-tuple-element.284.refs_2_.refs_3_.refs_1_, bf16[512,512]{1,0:T(8,128)(2,1)} %get-tuple-element.284.refs_2_.refs_3_.refs_1_, ...), custom_call_target="tpu_custom_call" | custom-call | flops 6750000128 | bytes 20250000 | tf_op jit(solution)/shard_map/dq/pallas_call | solution.py:51
  562.9 26.9 %dq.3.refs_4_.refs_0_ = f32[512,384]{1,0:T(8,128)} custom-call(s32[9]{0:T(128)} %pad_add_fusion.refs_0_, bf16[1024,384]{1,0:T(8,128)(2,1)} %get-tuple-element.186.refs_1_, bf16[512,512]{1,0:T(8,128)(2,1)} %get-tuple-element.294.refs_2_.refs_3_.refs_1_, bf16[512,512]{1,0:T(8,128)(2,1)} %get-tuple-element.294.refs_2_.refs_3_.refs_1_, ...), custom_call_target="tpu_custom_call" | custom-call | flops 6750000128 | bytes 20250000 | tf_op jit(solution)/shard_map/dq/pallas_call | solution.py:51
  609.0 32.9 %dkv.4 = (f32[512,384]{1,0:T(8,128)}, f32[512,384]{1,0:T(8,128)}) custom-call(s32[9]{0:T(128)} %pad_add_fusion.refs_0_, bf16[1024,384]{1,0:T(8,128)(2,1)} %get-tuple-element.187.refs_1_, bf16[1024,384]{1,0:T(8,128)(2,1)} %get-tuple-element.188.refs_9_.refs_2_, bf16[8192,384]{1,0:T(8,128)(2,1)} %all-gather.9.cloned.1.call-done.refs_3_, ...), custom_call_target="tpu_custom_call" | custom-call | flops 6000000000 | bytes 18000000 | tf_op jit(solution)/shard_map/dkv/pallas_call | solution.py:51
  654.6 6.6 dqkv.4
  661.2 12.6 %dkv.5 = (f32[512,128]{1,0:T(8,128)}, f32[512,128]{1,0:T(8,128)}) custom-call(s32[9]{0:T(128)} %pad_add_fusion.refs_0_, bf16[1024,384]{1,0:T(8,128)(2,1)} %get-tuple-element.187.refs_1_, bf16[1024,384]{1,0:T(8,128)(2,1)} %get-tuple-element.188.refs_9_.refs_2_, bf16[8192,384]{1,0:T(8,128)(2,1)} %all-gather.9.cloned.1.call-done.refs_3_, ...), custom_call_target="tpu_custom_call" | custom-call | flops 6000000000 | bytes 18000000 | tf_op jit(solution)/shard_map/dkv/pallas_call | solution.py:51
  680.1 6.6 dqkv.5
  686.7 12.5 %dkv.6 = (f32[512,128]{1,0:T(8,128)}, f32[512,128]{1,0:T(8,128)}) custom-call(s32[9]{0:T(128)} %pad_add_fusion.refs_0_, bf16[1024,384]{1,0:T(8,128)(2,1)} %get-tuple-element.187.refs_1_, bf16[1024,384]{1,0:T(8,128)(2,1)} %get-tuple-element.188.refs_9_.refs_2_, bf16[8192,384]{1,0:T(8,128)(2,1)} %all-gather.9.cloned.1.call-done.refs_3_, ...), custom_call_target="tpu_custom_call" | custom-call | flops 6000000000 | bytes 18000000 | tf_op jit(solution)/shard_map/dkv/pallas_call | solution.py:51
  710.7 12.6 %dkv.7 = (f32[512,128]{1,0:T(8,128)}, f32[512,128]{1,0:T(8,128)}) custom-call(s32[9]{0:T(128)} %pad_add_fusion.refs_0_, bf16[1024,384]{1,0:T(8,128)(2,1)} %get-tuple-element.187.refs_1_, bf16[1024,384]{1,0:T(8,128)(2,1)} %get-tuple-element.188.refs_9_.refs_2_, bf16[8192,384]{1,0:T(8,128)(2,1)} %all-gather.9.cloned.1.call-done.refs_3_, ...), custom_call_target="tpu_custom_call" | custom-call | flops 6000000000 | bytes 18000000 | tf_op jit(solution)/shard_map/dkv/pallas_call | solution.py:51
  723.3 6.7 dqkv.6
  737.9 6.6 dqkv.7
  751.4 10.9 %pair_grad.5.refs_4_.refs_1_ = bf16[1536,1536]{1,0:T(8,128)(2,1)} custom-call(bf16[1024,1536]{1,0:T(8,128)(2,1)} %get-tuple-element.185.refs_0_.refs_6_, bf16[1024,1152]{1,0:T(8,128)(2,1)} %get-tuple-element.347.refs_1_, bf16[1024,1536]{1,0:T(8,128)(2,1)} %get-tuple-element.348.refs_2_, bf16[1024,384]{1,0:T(8,128)(2,1)} %pad_maximum_fusion.2.refs_3_, ...), custom_call_target="tpu_custom_call" | custom-call | flops 2500000000 | bytes 7500000 | tf_op jit(solution)/shard_map/pair_grad/pallas_call | solution.py:51
  765.0 10.4 %all-gather = f32[64,1536]{1,0:T(8,128)} all-gather(f32[8,1536]{1,0:T(8,128)} %note.3.refs_7_), channel_id=2, replica_groups=mesh['wide'=8,'narrow'=4] {'wide'}, dimensions={0}, use_global_device_ids=true | all-gather | bytes 442368 | tf_op jit(solution)/shard_map/all_gather | solution.py:1170
  799.4 5.7 collective-permute-done.69.refs_1_
  823.1 6.3 collective-permute-done.71.refs_1_
  841.9 10.3 %collective-permute-done.73.refs_1_ = bf16[256,1536]{1,0:T(8,128)(2,1)S(1)} collective-permute-done((bf16[256,1536]{1,0:T(8,128)(2,1)}, bf16[256,1536]{1,0:T(8,128)(2,1)S(1)}, u32[]{:S(2)}, u32[]{:S(2)}) %collective-permute-start.73) | collective-permute-done | bytes 786464 | tf_op jit(solution)/shard_map/ppermute | solution.py:883
  (508 shorter events, 337.8 us)
Async XLA Ops:
  7.2 136.9 %all-gather.5.cloned.1.call-start = ((), (), s32[]{:S(2)}) async-start(), calls=%async_computation.3 | async-start | bytes 3538944 | tf_op jit(solution)/shard_map/all_gather | solution.py:1041
  16.6 526.3 %all-gather.7.cloned.1.call-start = ((), (), s32[]{:S(2)}) async-start(), calls=%async_computation.4 | async-start | bytes 3538944 | tf_op jit(solution)/shard_map/all_gather | solution.py:1107
  66.8 20.8 %collective-permute-start.8 = (bf16[1024,384]{1,0:T(8,128)(2,1)}, bf16[1024,384]{1,0:T(8,128)(2,1)}, u32[]{:S(2)}, u32[]{:S(2)}) collective-permute-start(bf16[1024,384]{1,0:T(8,128)(2,1)} %get-tuple-element.188.refs_9_.refs_2_), channel_id=1, source_target_pairs={{0,8},{4,12},{8,0},{12,4},{16,24},{20,28},{24,16},{28,20},{1,9},{5... | collective-permute-start | bytes 2359304 | tf_op jit(solution)/shard_map/ppermute | solution.py:734
  68.1 22.9 %collective-permute-start.10 = (bf16[1024,384]{1,0:T(8,128)(2,1)}, bf16[1024,384]{1,0:T(8,128)(2,1)S(1)}, u32[]{:S(2)}, u32[]{:S(2)}) collective-permute-start(bf16[1024,384]{1,0:T(8,128)(2,1)} %get-tuple-element.188.refs_9_.refs_2_), channel_id=1, source_target_pairs={{4,20},{16,0},{12,28},{24,8},{5,21},{17,1},{13,29},{25,9},{6,22},{... | collective-permute-start | bytes 2359304 | tf_op jit(solution)/shard_map/ppermute | solution.py:734
  69.4 34.5 %collective-permute-start.1 = (bf16[1024,384]{1,0:T(8,128)(2,1)}, bf16[1024,384]{1,0:T(8,128)(2,1)}, u32[]{:S(2)}, u32[]{:S(2)}) collective-permute-start(bf16[1024,384]{1,0:T(8,128)(2,1)} %get-tuple-element.187.refs_1_), channel_id=1, source_target_pairs={{0,8},{4,12},{8,0},{12,4},{16,24},{20,28},{24,16},{28,20},{1,9},{5... | collective-permute-start | bytes 2359304 | tf_op jit(solution)/shard_map/ppermute | solution.py:734
  87.6 21.6 %collective-permute-start.12 = (bf16[1024,384]{1,0:T(8,128)(2,1)}, bf16[1024,384]{1,0:T(8,128)(2,1)S(1)}, u32[]{:S(2)}, u32[]{:S(2)}) collective-permute-start(bf16[1024,384]{1,0:T(8,128)(2,1)} %collective-permute-done.8.refs_11_), channel_id=1, source_target_pairs={{0,16},{28,12},{1,17},{29,13},{2,18},{30,14},{3,19},{31,15}} | collective-permute-start | bytes 2359304 | tf_op jit(solution)/shard_map/ppermute | solution.py:734
  91.0 23.4 %collective-permute-start.13 = (bf16[1024,384]{1,0:T(8,128)(2,1)S(1)}, bf16[1024,384]{1,0:T(8,128)(2,1)S(1)}, u32[]{:S(2)}, u32[]{:S(2)}) collective-permute-start(bf16[1024,384]{1,0:T(8,128)(2,1)S(1)} %collective-permute-done.10.refs_13_), channel_id=1, source_target_pairs={{28,20},{0,8},{29,21},{1,9},{30,22},{2,10},{31,23},{3,11}} | collective-permute-start | bytes 2359304 | tf_op jit(solution)/shard_map/ppermute | solution.py:734
  92.4 22.4 %collective-permute-start.3 = (bf16[1024,384]{1,0:T(8,128)(2,1)}, bf16[1024,384]{1,0:T(8,128)(2,1)}, u32[]{:S(2)}, u32[]{:S(2)}) collective-permute-start(bf16[1024,384]{1,0:T(8,128)(2,1)} %get-tuple-element.187.refs_1_), channel_id=1, source_target_pairs={{4,20},{16,0},{12,28},{24,8},{5,21},{17,1},{13,29},{25,9},{6,22},{... | collective-permute-start | bytes 2359304 | tf_op jit(solution)/shard_map/ppermute | solution.py:734
  93.7 21.7 %collective-permute-start = (bf16[1024,384]{1,0:T(8,128)(2,1)}, bf16[1024,384]{1,0:T(8,128)(2,1)S(1)}, u32[]{:S(2)}, u32[]{:S(2)}) collective-permute-start(bf16[1024,384]{1,0:T(8,128)(2,1)} %get-tuple-element.187.refs_1_), channel_id=1, source_target_pairs={{0,4},{4,0},{8,12},{12,8},{16,20},{20,16},{24,28},{28,24},{1,5},{5... | collective-permute-start | bytes 2359304 | tf_op jit(solution)/shard_map/ppermute | solution.py:705
  114.8 23.1 %collective-permute-start.2 = (bf16[1024,384]{1,0:T(8,128)(2,1)}, bf16[1024,384]{1,0:T(8,128)(2,1)}, u32[]{:S(2)}, u32[]{:S(2)}) collective-permute-start(bf16[1024,384]{1,0:T(8,128)(2,1)} %collective-permute-done.1.refs_3_), channel_id=1, source_target_pairs={{0,4},{4,0},{8,12},{12,8},{16,20},{20,16},{24,28},{28,24},{1,5},{5... | collective-permute-start | bytes 2359304 | tf_op jit(solution)/shard_map/ppermute | solution.py:705
  115.4 22.6 %collective-permute-start.9 = (bf16[1024,384]{1,0:T(8,128)(2,1)}, bf16[1024,384]{1,0:T(8,128)(2,1)}, u32[]{:S(2)}, u32[]{:S(2)}) collective-permute-start(bf16[1024,384]{1,0:T(8,128)(2,1)} %collective-permute-done.8.refs_11_), channel_id=1, source_target_pairs={{0,4},{4,0},{8,12},{12,8},{16,20},{20,16},{24,28},{28,24},{1,5},{5... | collective-permute-start | bytes 2359304 | tf_op jit(solution)/shard_map/ppermute | solution.py:705
  115.5 22.4 %collective-permute-start.4 = (bf16[1024,384]{1,0:T(8,128)(2,1)}, bf16[1024,384]{1,0:T(8,128)(2,1)}, u32[]{:S(2)}, u32[]{:S(2)}) collective-permute-start(bf16[1024,384]{1,0:T(8,128)(2,1)} %collective-permute-done.3.refs_5_), channel_id=1, source_target_pairs={{0,4},{4,0},{8,12},{12,8},{16,20},{20,16},{24,28},{28,24},{1,5},{5... | collective-permute-start | bytes 2359304 | tf_op jit(solution)/shard_map/ppermute | solution.py:705
  164.7 21.9 %collective-permute-start.15 = (bf16[256,1536]{1,0:T(8,128)(2,1)}, bf16[256,1536]{1,0:T(8,128)(2,1)}, u32[]{:S(2)}, u32[]{:S(2)}) collective-permute-start(bf16[256,1536]{1,0:T(8,128)(2,1)} %convolution_convert_fusion.4.refs_2_), channel_id=1, source_target_pairs={{0,1},{3,2},{1,0},{2,3},{4,5},{7,6},{5,4},{6,7},{8,9},{11,10},{9,8... | collective-permute-start | bytes 2359304 | tf_op jit(solution)/shard_map/ppermute | solution.py:883
  189.1 25.9 %collective-permute-start.16 = (bf16[256,1536]{1,0:T(8,128)(2,1)}, bf16[256,1536]{1,0:T(8,128)(2,1)S(1)}, u32[]{:S(2)}, u32[]{:S(2)}) collective-permute-start(bf16[256,1536]{1,0:T(8,128)(2,1)} %get-tuple-element.194), channel_id=1, source_target_pairs={{0,1},{3,2},{1,0},{2,3},{4,5},{7,6},{5,4},{6,7},{8,9},{11,10},{9,8... | collective-permute-start | bytes 2359304 | tf_op jit(solution)/shard_map/ppermute | solution.py:883
  189.6 25.4 %collective-permute-start.17 = (bf16[256,1536]{1,0:T(8,128)(2,1)}, bf16[256,1536]{1,0:T(8,128)(2,1)S(1)}, u32[]{:S(2)}, u32[]{:S(2)}) collective-permute-start(bf16[256,1536]{1,0:T(8,128)(2,1)} %get-tuple-element.195.refs_7_.refs_3_), channel_id=1, source_target_pairs={{1,2},{2,1},{5,6},{6,5},{9,10},{10,9},{13,14},{14,13},{17,18},{18,... | collective-permute-start | bytes 2359304 | tf_op jit(solution)/shard_map/ppermute | solution.py:883
  219.8 21.5 %collective-permute-start.18 = (bf16[256,1536]{1,0:T(8,128)(2,1)}, bf16[256,1536]{1,0:T(8,128)(2,1)S(1)}, u32[]{:S(2)}, u32[]{:S(2)}) collective-permute-start(bf16[256,1536]{1,0:T(8,128)(2,1)} %get-tuple-element.197.refs_2_), channel_id=1, source_target_pairs={{0,1},{3,2},{1,0},{2,3},{4,5},{7,6},{5,4},{6,7},{8,9},{11,10},{9,8... | collective-permute-start | bytes 2359304 | tf_op jit(solution)/shard_map/ppermute | solution.py:883
  246.6 19.8 %collective-permute-start.20 = (bf16[256,1536]{1,0:T(8,128)(2,1)}, bf16[256,1536]{1,0:T(8,128)(2,1)S(1)}, u32[]{:S(2)}, u32[]{:S(2)}) collective-permute-start(bf16[256,1536]{1,0:T(8,128)(2,1)} %get-tuple-element.199.refs_2_), channel_id=1, source_target_pairs={{0,1},{3,2},{1,0},{2,3},{4,5},{7,6},{5,4},{6,7},{8,9},{11,10},{9,8... | collective-permute-start | bytes 2359304 | tf_op jit(solution)/shard_map/ppermute | solution.py:883
  271.0 19.5 %collective-permute-start.22 = (bf16[256,1536]{1,0:T(8,128)(2,1)}, bf16[256,1536]{1,0:T(8,128)(2,1)S(1)}, u32[]{:S(2)}, u32[]{:S(2)}) collective-permute-start(bf16[256,1536]{1,0:T(8,128)(2,1)} %get-tuple-element.204.refs_2_), channel_id=1, source_target_pairs={{0,1},{3,2},{1,0},{2,3},{4,5},{7,6},{5,4},{6,7},{8,9},{11,10},{9,8... | collective-permute-start | bytes 2359304 | tf_op jit(solution)/shard_map/ppermute | solution.py:883
  420.8 19.6 %collective-permute-start.36 = (bf16[256,1536]{1,0:T(8,128)(2,1)}, bf16[256,1536]{1,0:T(8,128)(2,1)S(1)}, u32[]{:S(2)}, u32[]{:S(2)}) collective-permute-start(bf16[256,1536]{1,0:T(8,128)(2,1)} %get-tuple-element.259.refs_2_), channel_id=1, source_target_pairs={{0,1},{3,2},{1,0},{2,3},{4,5},{7,6},{5,4},{6,7},{8,9},{11,10},{9,8... | collective-permute-start | bytes 2359304 | tf_op jit(solution)/shard_map/ppermute | solution.py:883
  464.6 25.5 %collective-permute-start.40 = (bf16[256,1536]{1,0:T(8,128)(2,1)}, bf16[256,1536]{1,0:T(8,128)(2,1)S(1)}, u32[]{:S(2)}, u32[]{:S(2)}) collective-permute-start(bf16[256,1536]{1,0:T(8,128)(2,1)} %get-tuple-element.282.refs_2_), channel_id=1, source_target_pairs={{0,1},{3,2},{1,0},{2,3},{4,5},{7,6},{5,4},{6,7},{8,9},{11,10},{9,8... | collective-permute-start | bytes 2359304 | tf_op jit(solution)/shard_map/ppermute | solution.py:883
  468.9 21.2 %collective-permute-start.43 = (bf16[512,512]{1,0:T(8,128)(2,1)S(1)}, bf16[512,512]{1,0:T(8,128)(2,1)S(1)}, u32[]{:S(2)}, u32[]{:S(2)}) collective-permute-start(bf16[512,512]{1,0:T(8,128)(2,1)S(1)} %collective-permute-done.41.refs_5_.refs_3_), channel_id=1, source_target_pairs={{0,16},{4,20},{24,8},{28,12},{1,17},{5,21},{25,9},{29,13},{2,18},{... | collective-permute-start | bytes 1572872 | tf_op jit(solution)/shard_map/ppermute | solution.py:757
  509.1 99.9 %all-gather.9.cloned.1.call-start = ((), (), s32[]{:S(2)}) async-start(), calls=%async_computation.5 | async-start | bytes 7077888 | tf_op jit(solution)/shard_map/all_gather | solution.py:1051
  509.8 265.7 %reduce-scatter.4.cloned.1.call-start = ((), (), s32[]{:S(2)}) async-start(), calls=%async_computation.6 | async-start | bytes 10616832 | tf_op jit(solution)/shard_map/reduce_scatter | solution.py:945
  509.9 49.0 %collective-permute-start.50 = (bf16[512,512]{1,0:T(8,128)(2,1)S(1)}, bf16[512,512]{1,0:T(8,128)(2,1)}, u32[]{:S(2)}, u32[]{:S(2)}) collective-permute-start(bf16[512,512]{1,0:T(8,128)(2,1)S(1)} %copy-done.26), channel_id=1, source_target_pairs={{0,4},{4,0},{8,12},{12,8},{16,20},{20,16},{24,28},{28,24},{1,5},{5... | collective-permute-start | bytes 1572872 | tf_op jit(solution)/shard_map/ppermute | solution.py:705
  510.0 49.4 %collective-permute-start.45 = (bf16[512,512]{1,0:T(8,128)(2,1)S(1)}, bf16[512,512]{1,0:T(8,128)(2,1)}, u32[]{:S(2)}, u32[]{:S(2)}) collective-permute-start(bf16[512,512]{1,0:T(8,128)(2,1)S(1)} %copy-done.23), channel_id=1, source_target_pairs={{0,8},{4,12},{8,0},{12,4},{16,24},{20,28},{24,16},{28,20},{1,9},{5... | collective-permute-start | bytes 1572872 | tf_op jit(solution)/shard_map/ppermute | solution.py:757
  510.4 49.1 %collective-permute-start.46 = (bf16[512,512]{1,0:T(8,128)(2,1)S(1)}, bf16[512,512]{1,0:T(8,128)(2,1)}, u32[]{:S(2)}, u32[]{:S(2)}) collective-permute-start(bf16[512,512]{1,0:T(8,128)(2,1)S(1)} %copy-done.23), channel_id=1, source_target_pairs={{4,20},{16,0},{12,28},{24,8},{5,21},{17,1},{13,29},{25,9},{6,22},{... | collective-permute-start | bytes 1572872 | tf_op jit(solution)/shard_map/ppermute | solution.py:757
  557.4 33.1 %collective-permute-start.44 = (bf16[256,1536]{1,0:T(8,128)(2,1)S(1)}, bf16[256,1536]{1,0:T(8,128)(2,1)S(1)}, u32[]{:S(2)}, u32[]{:S(2)}) collective-permute-start(bf16[256,1536]{1,0:T(8,128)(2,1)S(1)} %get-tuple-element.416.refs_10_.refs_2_), channel_id=1, source_target_pairs={{0,1},{3,2},{1,0},{2,3},{4,5},{7,6},{5,4},{6,7},{8,9},{11,10},{9,8... | collective-permute-start | bytes 2359304 | tf_op jit(solution)/shard_map/ppermute | solution.py:883
  558.9 30.8 %collective-permute-start.51 = (bf16[512,512]{1,0:T(8,128)(2,1)S(1)}, bf16[512,512]{1,0:T(8,128)(2,1)}, u32[]{:S(2)}, u32[]{:S(2)}) collective-permute-start(bf16[512,512]{1,0:T(8,128)(2,1)S(1)} %copy-done.17), channel_id=1, source_target_pairs={{0,4},{4,0},{8,12},{12,8},{16,20},{20,16},{24,28},{28,24},{1,5},{5... | collective-permute-start | bytes 1572872 | tf_op jit(solution)/shard_map/ppermute | solution.py:705
  558.9 31.1 %collective-permute-start.52 = (bf16[512,512]{1,0:T(8,128)(2,1)S(1)}, bf16[512,512]{1,0:T(8,128)(2,1)S(1)}, u32[]{:S(2)}, u32[]{:S(2)}) collective-permute-start(bf16[512,512]{1,0:T(8,128)(2,1)S(1)} %copy-done.19), channel_id=1, source_target_pairs={{0,4},{4,0},{8,12},{12,8},{16,20},{20,16},{24,28},{28,24},{1,5},{5... | collective-permute-start | bytes 1572872 | tf_op jit(solution)/shard_map/ppermute | solution.py:705
  559.4 38.5 %collective-permute-start.53 = (bf16[512,512]{1,0:T(8,128)(2,1)S(1)}, bf16[512,512]{1,0:T(8,128)(2,1)}, u32[]{:S(2)}, u32[]{:S(2)}) collective-permute-start(bf16[512,512]{1,0:T(8,128)(2,1)S(1)} %copy-done.21), channel_id=1, source_target_pairs={{0,4},{4,0},{8,12},{12,8},{16,20},{20,16},{24,28},{28,24},{1,5},{5... | collective-permute-start | bytes 1572872 | tf_op jit(solution)/shard_map/ppermute | solution.py:705
  559.5 30.8 %collective-permute-start.47 = (bf16[512,512]{1,0:T(8,128)(2,1)}, bf16[512,512]{1,0:T(8,128)(2,1)S(1)}, u32[]{:S(2)}, u32[]{:S(2)}) collective-permute-start(bf16[512,512]{1,0:T(8,128)(2,1)} %collective-permute-done.45.refs_8_.refs_3_), channel_id=1, source_target_pairs={{0,16},{4,20},{24,8},{28,12},{1,17},{5,21},{25,9},{29,13},{2,18},{... | collective-permute-start | bytes 1572872 | tf_op jit(solution)/shard_map/ppermute | solution.py:757
  607.0 192.4 %reduce-scatter.6.cloned.1.call-start = ((), (), s32[]{:S(2)}) async-start(), calls=%async_computation.7 | async-start | bytes 7077888 | tf_op jit(solution)/shard_map/reduce_scatter | solution.py:945
  607.1 34.8 %collective-permute-start.48 = (bf16[256,1536]{1,0:T(8,128)(2,1)}, bf16[256,1536]{1,0:T(8,128)(2,1)S(1)}, u32[]{:S(2)}, u32[]{:S(2)}) collective-permute-start(bf16[256,1536]{1,0:T(8,128)(2,1)} %get-tuple-element.295), channel_id=1, source_target_pairs={{0,1},{3,2},{1,0},{2,3},{4,5},{7,6},{5,4},{6,7},{8,9},{11,10},{9,8... | collective-permute-start | bytes 2359304 | tf_op jit(solution)/shard_map/ppermute | solution.py:883
  608.1 33.8 %collective-permute-start.49 = (bf16[256,1536]{1,0:T(8,128)(2,1)S(1)}, bf16[256,1536]{1,0:T(8,128)(2,1)S(1)}, u32[]{:S(2)}, u32[]{:S(2)}) collective-permute-start(bf16[256,1536]{1,0:T(8,128)(2,1)S(1)} %copy-done.10), channel_id=1, source_target_pairs={{1,2},{2,1},{5,6},{6,5},{9,10},{10,9},{13,14},{14,13},{17,18},{18,... | collective-permute-start | bytes 2359304 | tf_op jit(solution)/shard_map/ppermute | solution.py:883
  646.5 205.8 %reduce-scatter.8.cloned.1.call-start = ((), (), s32[]{:S(2)}) async-start(), calls=%async_computation.8 | async-start | bytes 5308416 | tf_op jit(solution)/shard_map/reduce_scatter | solution.py:945
  647.6 26.2 %collective-permute-start.59 = (bf16[256,1536]{1,0:T(8,128)(2,1)S(1)}, bf16[256,1536]{1,0:T(8,128)(2,1)S(1)}, u32[]{:S(2)}, u32[]{:S(2)}) collective-permute-start(bf16[256,1536]{1,0:T(8,128)(2,1)S(1)} %copy-done.11), channel_id=1, source_target_pairs={{1,2},{2,1},{5,6},{6,5},{9,10},{10,9},{13,14},{14,13},{17,18},{18,... | collective-permute-start | bytes 2359304 | tf_op jit(solution)/shard_map/ppermute | solution.py:883
  648.3 25.5 %collective-permute-start.58 = (bf16[256,1536]{1,0:T(8,128)(2,1)S(1)}, bf16[256,1536]{1,0:T(8,128)(2,1)S(1)}, u32[]{:S(2)}, u32[]{:S(2)}) collective-permute-start(bf16[256,1536]{1,0:T(8,128)(2,1)S(1)} %copy-done.40), channel_id=1, source_target_pairs={{0,1},{3,2},{1,0},{2,3},{4,5},{7,6},{5,4},{6,7},{8,9},{11,10},{9,8... | collective-permute-start | bytes 2359304 | tf_op jit(solution)/shard_map/ppermute | solution.py:883
  678.5 20.8 %collective-permute-start.60 = (bf16[256,1536]{1,0:T(8,128)(2,1)}, bf16[256,1536]{1,0:T(8,128)(2,1)S(1)}, u32[]{:S(2)}, u32[]{:S(2)}) collective-permute-start(bf16[256,1536]{1,0:T(8,128)(2,1)} %get-tuple-element.304.refs_2_), channel_id=1, source_target_pairs={{0,1},{3,2},{1,0},{2,3},{4,5},{7,6},{5,4},{6,7},{8,9},{11,10},{9,8... | collective-permute-start | bytes 2359304 | tf_op jit(solution)/shard_map/ppermute | solution.py:883
  678.5 20.8 %collective-permute-start.61 = (bf16[256,1536]{1,0:T(8,128)(2,1)}, bf16[256,1536]{1,0:T(8,128)(2,1)S(1)}, u32[]{:S(2)}, u32[]{:S(2)}) collective-permute-start(bf16[256,1536]{1,0:T(8,128)(2,1)} %get-tuple-element.305.refs_4_), channel_id=1, source_target_pairs={{1,2},{2,1},{5,6},{6,5},{9,10},{10,9},{13,14},{14,13},{17,18},{18,... | collective-permute-start | bytes 2359304 | tf_op jit(solution)/shard_map/ppermute | solution.py:883
  704.0 26.1 %collective-permute-start.62 = (bf16[256,1536]{1,0:T(8,128)(2,1)}, bf16[256,1536]{1,0:T(8,128)(2,1)S(1)}, u32[]{:S(2)}, u32[]{:S(2)}) collective-permute-start(bf16[256,1536]{1,0:T(8,128)(2,1)} %get-tuple-element.310.refs_2_), channel_id=1, source_target_pairs={{0,1},{3,2},{1,0},{2,3},{4,5},{7,6},{5,4},{6,7},{8,9},{11,10},{9,8... | collective-permute-start | bytes 2359304 | tf_op jit(solution)/shard_map/ppermute | solution.py:883
  708.8 21.3 %collective-permute-start.63 = (bf16[256,1536]{1,0:T(8,128)(2,1)}, bf16[256,1536]{1,0:T(8,128)(2,1)S(1)}, u32[]{:S(2)}, u32[]{:S(2)}) collective-permute-start(bf16[256,1536]{1,0:T(8,128)(2,1)} %get-tuple-element.311.refs_4_), channel_id=1, source_target_pairs={{1,2},{2,1},{5,6},{6,5},{9,10},{10,9},{13,14},{14,13},{17,18},{18,... | collective-permute-start | bytes 2359304 | tf_op jit(solution)/shard_map/ppermute | solution.py:883
  734.8 40.7 %collective-permute-start.64 = (bf16[256,1536]{1,0:T(8,128)(2,1)}, bf16[256,1536]{1,0:T(8,128)(2,1)S(1)}, u32[]{:S(2)}, u32[]{:S(2)}) collective-permute-start(bf16[256,1536]{1,0:T(8,128)(2,1)} %get-tuple-element.319.refs_2_), channel_id=1, source_target_pairs={{0,1},{3,2},{1,0},{2,3},{4,5},{7,6},{5,4},{6,7},{8,9},{11,10},{9,8... | collective-permute-start | bytes 2359304 | tf_op jit(solution)/shard_map/ppermute | solution.py:883
  736.3 39.2 %collective-permute-start.65 = (bf16[256,1536]{1,0:T(8,128)(2,1)}, bf16[256,1536]{1,0:T(8,128)(2,1)S(1)}, u32[]{:S(2)}, u32[]{:S(2)}) collective-permute-start(bf16[256,1536]{1,0:T(8,128)(2,1)} %get-tuple-element.320.refs_4_), channel_id=1, source_target_pairs={{1,2},{2,1},{5,6},{6,5},{9,10},{10,9},{13,14},{14,13},{17,18},{18,... | collective-permute-start | bytes 2359304 | tf_op jit(solution)/shard_map/ppermute | solution.py:883
  785.0 20.1 %collective-permute-start.69 = (bf16[256,1536]{1,0:T(8,128)(2,1)}, bf16[256,1536]{1,0:T(8,128)(2,1)S(1)}, u32[]{:S(2)}, u32[]{:S(2)}) collective-permute-start(bf16[256,1536]{1,0:T(8,128)(2,1)} %get-tuple-element.349.refs_2_), channel_id=1, source_target_pairs={{0,1},{3,2},{1,0},{2,3},{4,5},{7,6},{5,4},{6,7},{8,9},{11,10},{9,8... | collective-permute-start | bytes 2359304 | tf_op jit(solution)/shard_map/ppermute | solution.py:883
  790.9 26.8 %collective-permute-start.74 = (f32[8,128]{1,0:T(8,128)S(1)}, f32[8,128]{1,0:T(8,128)S(1)}, u32[]{:S(2)}, u32[]{:S(2)}) collective-permute-start(f32[8,128]{1,0:T(8,128)S(1)} %bitcast.94), channel_id=1, source_target_pairs={{0,1},{1,0},{2,3},{3,2},{4,5},{5,4},{6,7},{7,6},{8,9},{9,8},{10,11... | collective-permute-start | bytes 12296 | tf_op jit(solution)/shard_map/ppermute | solution.py:705
  793.0 24.7 %collective-permute-start.75 = (f32[8,128]{1,0:T(8,128)S(1)}, f32[8,128]{1,0:T(8,128)S(1)}, u32[]{:S(2)}, u32[]{:S(2)}) collective-permute-start(f32[8,128]{1,0:T(8,128)S(1)} %bitcast.95), channel_id=1, source_target_pairs={{0,2},{1,3},{2,0},{3,1},{4,6},{5,7},{6,4},{7,5},{8,10},{9,11},{10,... | collective-permute-start | bytes 12296 | tf_op jit(solution)/shard_map/ppermute | solution.py:705
  793.7 23.9 %collective-permute-start.76 = (f32[8,128]{1,0:T(8,128)S(1)}, f32[8,128]{1,0:T(8,128)S(1)}, u32[]{:S(2)}, u32[]{:S(2)}) collective-permute-start(f32[8,128]{1,0:T(8,128)S(1)} %bitcast.96), channel_id=1, source_target_pairs={{0,3},{1,2},{2,1},{3,0},{4,7},{5,6},{6,5},{7,4},{8,11},{9,10},{10,... | collective-permute-start | bytes 12296 | tf_op jit(solution)/shard_map/ppermute | solution.py:705
  809.2 20.3 %collective-permute-start.71 = (bf16[256,1536]{1,0:T(8,128)(2,1)}, bf16[256,1536]{1,0:T(8,128)(2,1)S(1)}, u32[]{:S(2)}, u32[]{:S(2)}) collective-permute-start(bf16[256,1536]{1,0:T(8,128)(2,1)} %get-tuple-element.352.refs_2_), channel_id=1, source_target_pairs={{0,1},{3,2},{1,0},{2,3},{4,5},{7,6},{5,4},{6,7},{8,9},{11,10},{9,8... | collective-permute-start | bytes 2359304 | tf_op jit(solution)/shard_map/ppermute | solution.py:883
  (144 other events, 1147.9 us)
Sparse Core Ops, SparseCore 0:
  16.7 35.8 all-gather.4
  509.2 33.6 all-gather.6
  545.4 47.5 all-gather.8
  607.1 74.6 reduce-scatter.3
  685.1 61.7 reduce-scatter.5
  780.3 52.2 reduce-scatter.7

commit v9 on v8

--- a/solution.py
+++ b/solution.py
@@ -31,7 +31,7 @@
 
 COST = {
     "key": 8, "query": 9, "caption_norm": 2, "pick": 5, "attend": 18, "hop": 3, "ffn": 9, "ffn_back": 10, "out_back": 6,
-    "pair_grad": 10, "caption_back": 6, "dq": 27, "dkv": 24, "dqkv": 7, "caption_grad": 3, "last": 3, "note": 1, "pin": 1,
+    "pair_grad": 10, "caption_back": 6, "dq": 45, "dkv": 20, "dqkv": 7, "caption_grad": 3, "last": 3, "note": 1, "pin": 1,
 }
 
 
@@ -216,31 +216,33 @@
     masks = halves(128)
     keys = 512
 
+    def block_sums(h):
+        q = q_ref[...]
+        total = 0.0
+        for c in range(k_ref.shape[0] // keys):
+            at = slice(c * keys, (c + 1) * keys)
+            total = total + soft_sums(q, k_ref[at, :], v_ref[at, :], masks[h])
+        return total
+
     @pl.when(j == 0)
     def _():
-        acc[...] = jnp.zeros_like(acc)
-
-    @pl.when(j < sc[0])
+        for h in range(2):
+            acc[2 + h] = soft_sums(q_ref[...], ck_ref[...], cv_ref[...], masks[h])
+            acc[h] = block_sums(h)
+
+    @pl.when((j > 0) & (j < sc[0]))
     def _():
-        q = q_ref[...]
         for h in range(2):
-            total = acc[h]
-            for c in range(k_ref.shape[0] // keys):
-                at = slice(c * keys, (c + 1) * keys)
-                total = total + soft_sums(q, k_ref[at, :], v_ref[at, :], masks[h])
-            acc[h] = total
+            acc[h] += block_sums(h)
 
     @pl.when(j == SPAN - 1)
     def _():
-        q = q_ref[...]
-
         def finish(a0, a1):
             inverse = 1.0 / jnp.where(masks[0], pltpu.roll(a0, HD, 1), pltpu.roll(a1, HD, 1))
             return jnp.where(masks[0], a0, a1) * inverse, inverse
 
         o, li = finish(acc[0], acc[1])
-        c0, c1 = (soft_sums(q, ck_ref[...], cv_ref[...], m) for m in masks)
-        mix_ref[...] = (o + tg_ref[...] * finish(c0, c1)[0]).astype(bf16)
+        mix_ref[...] = (o + tg_ref[...] * finish(acc[2], acc[3])[0]).astype(bf16)
         o_ref[...] = o.astype(bf16)
         li_ref[...] = li
 
@@ -266,7 +268,7 @@
         ],
         [pl.BlockSpec((bq, 128), mine)] * 3,
         [sds((bq, n), bf16), sds((bq, n), bf16), sds((bq, n), f32)],
-        [pltpu.VMEM((2, bq, 128), f32)],
+        [pltpu.VMEM((4, bq, 128), f32)],
         sc,
     )
 
@@ -330,11 +332,14 @@
     return jnp.where((lane >= 3 * head) & (lane < 3 * head + 3), -1.0, 0.0).astype(bf16)
 
 
-def dq_kernel(sc, q_ref, d_ref, x_ref, k_ref, v_ref, c_ref, dq_ref, acc):
+def dq_kernel(parts, sc, q_ref, k_ref, v_ref, *refs):
+    d_refs, x_refs, c_refs = (refs[k * parts : (k + 1) * parts] for k in range(3))
+    dq_ref, acc = refs[3 * parts :]
     pair = pl.program_id(0)
     j = pl.program_id(1)
     masks = halves(128)
     keys = 512
+    rows = d_refs[0].shape[0]
 
     @pl.when(j == 0)
     def _():
@@ -342,48 +347,48 @@
 
     @pl.when(j < sc[0])
     def _():
-        q = q_ref[...]
-        dx = jnp.concatenate([d_ref[...], x_ref[...]], 1)
-        total = acc[...]
-        for h in range(2):
-            off = minus_delta(keys, 2 * pair + h)
-            for c in range(k_ref.shape[0] // keys):
-                at = slice(c * keys, (c + 1) * keys)
-                k = keep(k_ref[at, :], masks[h])
-                e = jnp.exp2(mm_nt(q, k))
-                dp = mm_nt(dx, jnp.concatenate([keep(v_ref[at, :], masks[h]), off], 1))
-                total = total + mm((e * dp).astype(bf16), k)
-        acc[...] = total
+        for r in range(parts):
+            mine = slice(r * rows, (r + 1) * rows)
+            q = q_ref[mine, :]
+            dx = jnp.concatenate([d_refs[r][...], x_refs[r][...]], 1)
+            total = acc[mine, :]
+            for h in range(2):
+                off = minus_delta(keys, 2 * pair + h)
+                for c in range(k_ref.shape[0] // keys):
+                    at = slice(c * keys, (c + 1) * keys)
+                    k = keep(k_ref[at, :], masks[h])
+                    e = jnp.exp2(mm_nt(q, k))
+                    dp = mm_nt(dx, jnp.concatenate([keep(v_ref[at, :], masks[h]), off], 1))
+                    total = total + mm((e * dp).astype(bf16), k)
+            acc[mine, :] = total
 
     @pl.when(j == SPAN - 1)
     def _():
-        dq_ref[...] = acc[...] * 0.125 + c_ref[...]
-
-
-def dq_call(order, sc, q, d, k, v, cap_dq, h, after=()):
-    n = q.shape[1]
+        for r in range(parts):
+            mine = slice(r * rows, (r + 1) * rows)
+            dq_ref[mine, :] = acc[mine, :] * 0.125 + c_refs[r][...]
+
+
+def dq_call(order, sc, q, ds, k, v, cap_dqs, after=()):
+    t, n = q.shape
     pairs = n // 128
+    parts = len(ds)
     block = k.shape[0] // SPAN
-    bq = 2 * BR
+    rows = t // parts
     mine = lambda p, j, s: (0, p)
-    extra = lambda p, j, s: (0, pairs)
-    other = lambda p, j, s: (item_block(j, s), p)
+    other = pl.BlockSpec((block, 128), lambda p, j, s: (item_block(j, s), p))
     return order.run(
         "dq",
-        dq_kernel,
+        functools.partial(dq_kernel, parts),
         (pairs, SPAN),
-        (q, d, d, k, v, cap_dq),
-        [
-            pl.BlockSpec((bq, 128), lambda p, j, s: (h, p)),
-            pl.BlockSpec((bq, 128), mine),
-            pl.BlockSpec((bq, 128), extra),
-            pl.BlockSpec((block, 128), other),
-            pl.BlockSpec((block, 128), other),
-            pl.BlockSpec((bq, 128), mine),
-        ],
-        [pl.BlockSpec((bq, 128), mine)],
-        [sds((bq, n), f32)],
-        [pltpu.VMEM((bq, 128), f32)],
+        (q, k, v, *ds, *ds, *cap_dqs),
+        [pl.BlockSpec((t, 128), mine), other, other]
+        + [pl.BlockSpec((rows, 128), mine)] * parts
+        + [pl.BlockSpec((rows, 128), lambda p, j, s: (0, pairs))] * parts
+        + [pl.BlockSpec((rows, 128), mine)] * parts,
+        [pl.BlockSpec((t, 128), mine)],
+        [sds((t, n), f32)],
+        [pltpu.VMEM((t, 128), f32)],
         sc,
         after=after,
     )[0]
@@ -404,26 +409,29 @@
 
     @pl.when(j < sc[0])
     def _():
-        dk, dv = dk_ref[...], dv_ref[...]
-        for h in range(2):
-            vx = jnp.concatenate([keep(v_ref[...], masks[h]), minus_delta(v_ref.shape[0], 2 * pair + h)], 1)
-            for r in range(parts):
-                q = keep(q_ref[r * queries : (r + 1) * queries, :], masks[h])
-                d, x = d_refs[r][...], x_refs[r][...]
-                e = jnp.exp2(mm_nt(k_ref[...], q))
-                dp = mm_nt(vx, jnp.concatenate([d, x], 1))
-                dv = dv + mm(e.astype(bf16), keep(d, masks[h]))
-                dk = dk + mm((e * dp).astype(bf16), q)
-        dk_ref[...] = dk
-        dv_ref[...] = dv
-
-
-def dkv_call(order, sc, k, v, q_all, ds, half, base, n_pairs):
+        keys = 512
+        for c in range(k_ref.shape[0] // keys):
+            at = slice(c * keys, (c + 1) * keys)
+            dk, dv = dk_ref[at, :], dv_ref[at, :]
+            for h in range(2):
+                vx = jnp.concatenate([keep(v_ref[at, :], masks[h]), minus_delta(keys, 2 * pair + h)], 1)
+                for r in range(parts):
+                    q = keep(q_ref[r * queries : (r + 1) * queries, :], masks[h])
+                    d, x = d_refs[r][...], x_refs[r][...]
+                    e = jnp.exp2(mm_nt(k_ref[at, :], q))
+                    dp = mm_nt(vx, jnp.concatenate([d, x], 1))
+                    dv = dv + mm(e.astype(bf16), keep(d, masks[h]))
+                    dk = dk + mm((e * dp).astype(bf16), q)
+            dk_ref[at, :] = dk
+            dv_ref[at, :] = dv
+
+
+def dkv_call(order, sc, k, v, q_all, ds, base, n_pairs):
     t, n = k.shape
     pairs = n // 128
-    rows = 2 * BR
-    mine = pl.BlockSpec((rows, 128), lambda p, j, s: (half, base + p))
-    out = pl.BlockSpec((rows, 128), lambda p, j, s: (0, p))
+    rows = t // len(ds)
+    mine = pl.BlockSpec((t, 128), lambda p, j, s: (0, base + p))
+    out = pl.BlockSpec((t, 128), lambda p, j, s: (0, p))
     other = pl.BlockSpec((rows, 128), lambda p, j, s: (item_block(j, s), base + p))
     extra = pl.BlockSpec((rows, 128), lambda p, j, s: (item_block(j, s), pairs))
     return order.run(
@@ -433,7 +441,7 @@
         (k, v, q_all, *(x for d in ds for x in (d, d))),
         [mine, mine, pl.BlockSpec((t, 128), lambda p, j, s: (s[1 + SPAN + j], base + p))] + [other, extra] * len(ds),
         [out, out],
-        [sds((rows, n_pairs * 128), f32)] * 2,
+        [sds((t, n_pairs * 128), f32)] * 2,
         scalar=sc,
     )
 
@@ -648,7 +656,7 @@
         "dqkv",
         c,
         (dq, *(x for two in dkv for x in two), qr, kr, *tabs, hg, w, patches),
-        [part(c % 2, n)] + [part(c % 2, x.shape[1]) for two in dkv for x in two] + [part(c, n)] * 2 + [part(c, 128)] * 3 + [whole(hg.shape), whole(w.shape), part(c, d)],
+        [part(c, n)] + [part(c, x.shape[1]) for two in dkv for x in two] + [part(c, n)] * 2 + [part(c, 128)] * 3 + [whole(hg.shape), whole(w.shape), part(c, d)],
         [(BR, d, bf16)],
         [(2, n, f32), (1, d, f32)],
         [(t, 3 * n, bf16)],
@@ -725,20 +733,21 @@
 
 
 class Gather:
-    def __init__(self, a, b):
+    def __init__(self, order, a, b, between=None):
         self.all = None
         if lax.axis_size("wide") != 8:
-            self.first = self.second = ()
             self.all = [lax.all_gather(x, "wide") for x in (a, b)]
+            between(None)
             return
         send = lambda x, pairs: lax.ppermute(x, "wide", pairs)
         over_x = [(i, i ^ 2) for i in range(8)]
         over_y = [(1, 5), (4, 0), (3, 7), (6, 2)]
         a2, a4, b4, b2 = send(a, over_x), send(a, over_y), send(b, over_y), send(b, over_x)
         a6 = send(a2, [(0, 4), (1, 5), (6, 2), (7, 3)])
+        if between is not None:
+            between(a2)
+            b2 = pin(order, b2)
         b6x, b6y = send(b2, [(0, 4), (7, 3)]), send(b4, [(7, 5), (0, 2)])
-        self.first = (a2, a4, b4, b2)
-        self.second = (a6, b6x, b6y)
         self.kept = ((a, a2, a4, a6), (b, b2, b4, b6x + b6y))
 
     def pieces(self):
@@ -749,17 +758,23 @@
 
 class GatherOne:
     def __init__(self, a):
-        self.all = None
+        self.all, self.first, self.second = None, (), ()
         if lax.axis_size("wide") != 8:
-            self.first = self.second = ()
             self.all = [lax.all_gather(a, "wide")]
             return
-        send = lambda x, pairs: lax.ppermute(x, "wide", pairs)
-        a2 = send(a, [(i, i ^ 2) for i in range(8)])
-        a4 = send(a, [(1, 5), (4, 0), (3, 7), (6, 2)])
-        a6 = send(a2, [(0, 4), (1, 5), (6, 2), (7, 3)])
-        self.first, self.second = (a2, a4), (a6,)
-        self.kept = ((a, a2, a4, a6),)
+        a2 = lax.ppermute(a, "wide", [(i, i ^ 2) for i in range(8)])
+        a4 = lax.ppermute(a, "wide", [(1, 5), (4, 0), (3, 7), (6, 2)])
+        self.first, self.own = (a2, a4), a
+
+    def across(self, order=None):
+        if self.all is not None:
+            return
+        a2, a4 = self.first
+        if order is not None:
+            a2 = pin(order, a2)
+        a6 = lax.ppermute(a2, "wide", [(0, 4), (1, 5), (6, 2), (7, 3)])
+        self.second = (a6,)
+        self.kept = ((self.own, a2, a4, a6),)
 
     pieces = Gather.pieces
 
@@ -1044,9 +1059,13 @@
     pairs_of = range(t // (2 * BR))
     sums = Sums(order, deep, mz)
     a1, k_raw, k, v = key_call(order, patches, vec, w_qkv, tabs, hg, ())
-    kv = Gather(k, v)
-
-    q_raw, q = query_call(order, a1, w_qkv, tabs, hg, ())
+    made = []
+
+    def queries(done):
+        made.extend(query_call(order, a1, w_qkv, tabs, hg, () if done is None else (done,)))
+
+    kv = Gather(order, k, v, queries)
+    q_raw, q = made
 
     q_all = lax.all_gather(q, "wide", axis=0, tiled=True)
     k_all, v_all = pick(order, sc, kv.pieces(), SPAN)
@@ -1100,6 +1119,8 @@
                 early = d_got[h - 1].first if h > 0 else ()
                 mlp_part = pair_grad_call(order, a3, d_gu, d_ffn, hidden, h, len(pairs_of), mlp_part, early)
         d_got[h] = GatherOne(d_scaled[h])
+        if h < pairs_of[-1]:
+            d_got[h].across()
         dq_caps[h], pk, pv, pg = caption_back_call(order, sc, q, d_mixed[2 * h], d_mixed[2 * h + 1], cap, text, tg, h)
         dck, dcv, gate_sum = dck + pk, dcv + pv, gate_sum + pg
     d_attn = whole_out[0]
@@ -1107,13 +1128,9 @@
     cap_got = lax.all_gather(cap_sum.astype(bf16), "wide")
     kept = (firsts == me)[:, None, None]
     cap_sum = jnp.sum(jnp.where(kept, cap_got.astype(f32), 0.0), 0)
-    last_half = pairs_of[-1]
-
-    def make_dq(h, after):
-        return dq_call(order, sc, q, d_scaled[h], k_all, v_all, dq_caps[h], h, after)
-
-    for h in pairs_of[:-1]:
-        dqs[h] = make_dq(h, ())
+    halves_of = lambda table: [table[h] for h in pairs_of]
+    dq = dq_call(order, sc, q, halves_of(d_scaled), k_all, v_all, halves_of(dq_caps))
+    d_got[pairs_of[-1]].across(order)
 
     d_cap, hs_c = order.run(
         "caption_grad",
@@ -1131,8 +1148,6 @@
     text_parts = [padded[:, p * d : (p + 1) * d] for p in range(pieces)]
 
     sums.add(("text", 0), text_parts[0])
-    dqs[last_half] = make_dq(last_half, (*d_got[last_half].first, *text_parts))
-    sums.add(("text", 1), text_parts[1], (cap_part, *d_got[last_half].second))
     ds = [x for h in pairs_of for x in pick(order, sc, d_got[h].pieces(), SPAN)]
     g_mlp = scatter_rows(pin(order, mlp_part[0]))
     whole_out = ()
@@ -1142,24 +1157,21 @@
 
     def project(c, dkv, after=()):
         nonlocal whole_out
-        da1_part, p_hs, p1, *whole_out = dqkv_call(order, c, dqs[c // 2], dkv, q_raw, k_raw, tabs, hg, w_qkv, patches, whole_out)
+        da1_part, p_hs, p1, *whole_out = dqkv_call(order, c, dq, dkv, q_raw, k_raw, tabs, hg, w_qkv, patches, whole_out)
         hs_parts.append(p_hs)
         c1_parts.append(p1)
         return da1_part
 
-    dkv = [dkv_call(order, sc, k, v, q_all, ds, 0, 0, pairs)]
-    for p in range(2, pieces):
+    dkv = []
+    for p in range(pairs):
+        dkv.append(dkv_call(order, sc, k, v, q_all, ds, p, 1))
+        if p + 1 < pieces and p + 1 < pairs:
+            sums.add(("text", p + 1), text_parts[p + 1])
+        if p == 0:
+            g_cap = scatter_rows(pin(order, cap_part))
+    for p in range(pairs, pieces):
         sums.add(("text", p), text_parts[p])
-    g_cap = scatter_rows(pin(order, cap_part))
-    first_part = project(0, dkv)
-    parts_of = lambda p: dkv_call(order, sc, k, v, q_all, ds, 1, p, 1)
-    first_dkv, dkv = dkv, [parts_of(0)]
-    sums.add(("da1", 0), first_part)
-    da1_part = project(1, first_dkv)
-    dkv.append(parts_of(1))
-    sums.add(("da1", 1), da1_part)
-    dkv += [parts_of(p) for p in range(2, pairs)]
-    for c in chunks[2:]:
+    for c in chunks:
         da1_part = project(c, dkv)
         if c == chunks[-1]:
             d_qkv = whole_out[0]

time: 880 us -> 904 us (1.027)
  Pallas kernels: 472 us -> 398 us
  waiting for transfers between devices: 118 us -> 154 us
  starting transfers between devices: 119 us -> 152 us
  blocking collectives: 35.6 us -> 61.7 us
    pallas_call x69, Pallas kernels: 472 us -> 398 us  [run(): pl.pallas_call(body, grid_spec=pltpu.PrefetchScalarGridSpec(num_scalar_pr...]
    ppermute x0 -> x6, starting transfers between devices: none -> 43.7 us  [the longest x2 32.8 us: across(): a6 = lax.ppermute(a2, 'wide', [(0, 4), (1, 5), (6, 2), (7, 3)])]
    all_gather x1, blocking collectives: 10.4 us -> 36.7 us  [local(): got = lax.all_gather(folded, 'wide')]
    ppermute x42, waiting for transfers between devices: 69.8 us -> 85.1 us  [step(): go = lambda x, perm: lax.ppermute(x, 'narrow', perm)]
    ppermute x0 -> x6, waiting for transfers between devices: none -> 13.5 us  [the longest x2 13.5 us: across(): a6 = lax.ppermute(a2, 'wide', [(0, 4), (1, 5), (6, 2), (7, 3)])]
    ppermute x13 -> x7, starting transfers between devices: 27.2 us -> 14.7 us  [__init__(): send = lambda x, pairs: lax.ppermute(x, 'wide', pairs)]
    ppermute x13 -> x7, waiting for transfers between devices: 42.9 us -> 54.6 us  [__init__(): send = lambda x, pairs: lax.ppermute(x, 'wide', pairs)]
    unnamed x223 -> x205, local copies, waits for them, and re-layouts: 35.1 us -> 34.6 us
  transfers between devices with their start and end apart: 83 -> 83, of which waited for: 17 -> 21; matrix products, arithmetic and copies ran while one was open for 7% -> 7% of each run, Pallas kernels for 45% -> 36%
where the time goes in v9:
time: 904 us; the launch traced here: 896 us
  Pallas kernels  398 us (44%)
  waiting for transfers between devices  154 us (17%)
  starting transfers between devices  152 us (17%)
  blocking collectives  61.7 us (7%)
  local copies, waits for them, and re-layouts  46.4 us (5%)
  other arithmetic  38.1 us (4%)
  matrix products  25 us (3%)
  between operations  21.2 us (2%)
    pallas_call x69, Pallas kernels, run(): pl.pallas_call(body, grid_spec=pltpu.PrefetchScalarGridSpec(num_scalar_pr...  398 us
    ppermute x42, waiting for transfers between devices, step(): go = lambda x, perm: lax.ppermute(x, 'narrow', perm)  85.1 us
    ppermute x42, starting transfers between devices, step(): go = lambda x, perm: lax.ppermute(x, 'narrow', perm)  80.5 us
    ppermute x7, waiting for transfers between devices, __init__(): send = lambda x, pairs: lax.ppermute(x, 'wide', pairs)  54.6 us
    all_gather x1, blocking collectives, local(): got = lax.all_gather(folded, 'wide')  36.7 us
    unnamed x205, local copies, waits for them, and re-layouts  34.6 us
    ppermute x2, starting transfers between devices, across(): a6 = lax.ppermute(a2, 'wide', [(0, 4), (1, 5), (6, 2), (7, 3)])  32.8 us
    all_gather x2, blocking collectives, gather_now(): lax.all_gather(padded, axis, axis=0, tiled=True).reshape(-1, wide)[:, :n]  25 us
  transfers between devices with their start and end apart: 83, of which 21 were waited for; matrix products, arithmetic and copies ran while one was open for 7% of the time, Pallas kernels for 36%

profile of v9, /device:TPU:0, one launch (start us, length us, event | category | flops | bytes accessed | tf_op | source)
XLA Modules:
  0.0 896.0 jit_solution(2785333303801462710)
XLA Ops:
  26.7 14.9 %all_gather.22 = f32[4,8,256]{2,1,0:T(8,128)S(1)} all-gather(f32[1,8,256]{2,1,0:T(8,128)S(1)} %reshape.309), channel_id=1, replica_groups=mesh['wide'=8,'narrow'=4] {'narrow'}, dimensions={0}, use_global_device_ids=true | all-gather | bytes 40960 | tf_op jit(solution)/shard_map/all_gather | solution.py:868
  41.6 10.2 %all_gather.23 = f32[8,8,896]{2,1,0:T(8,128)S(1)} all-gather(f32[1,8,896]{2,1,0:T(8,128)S(1)} %reshape.311), channel_id=1, replica_groups=mesh['wide'=8,'narrow'=4] {'wide'}, dimensions={0}, use_global_device_ids=true | all-gather | bytes 258048 | tf_op jit(solution)/shard_map/all_gather | solution.py:868
  58.2 9.0 %key.1 = (bf16[1024,1536]{1,0:T(8,128)(2,1)}, f32[1024,384]{1,0:T(8,128)}, bf16[1024,384]{1,0:T(8,128)(2,1)}, bf16[1024,384]{1,0:T(8,128)(2,1)}) custom-call(bf16[1024,1536]{1,0:T(8,128)(2,1)} %refs_1_.9, f32[4,1536]{1,0:T(4,128)} %maximum_multiply_fusion.1.refs_1_.refs_2_.refs_4_.refs_3_, bf16[3,1536,384]{2,1,0:T(8,128)(2,1)} %refs_13_.7, ...), custom_call_target="tpu_custom_call" | custom-call | flops 2000000000 | bytes 6000000 | tf_op jit(solution)/shard_map/key/pallas_call | solution.py:51
  70.6 17.3 %collective-permute-done.refs_7_.refs_3_ = bf16[1024,384]{1,0:T(8,128)(2,1)S(1)} collective-permute-done((bf16[1024,384]{1,0:T(8,128)(2,1)}, bf16[1024,384]{1,0:T(8,128)(2,1)S(1)}, u32[]{:S(2)}, u32[]{:S(2)}) %collective-permute-start) | collective-permute-done | bytes 786464 | tf_op jit(solution)/shard_map/ppermute | solution.py:742
  88.8 7.0 query.1
  95.8 8.4 collective-permute-done.8.refs_1_
  111.7 14.6 %collective-permute-done.12 = bf16[1024,384]{1,0:T(8,128)(2,1)S(1)} collective-permute-done((bf16[1024,384]{1,0:T(8,128)(2,1)}, bf16[1024,384]{1,0:T(8,128)(2,1)S(1)}, u32[]{:S(2)}, u32[]{:S(2)}) %collective-permute-start.12) | collective-permute-done | bytes 786464 | tf_op jit(solution)/shard_map/ppermute | solution.py:742
  133.8 14.3 %collective-permute-done.5.refs_7_ = bf16[1024,384]{1,0:T(8,128)(2,1)} collective-permute-done((bf16[1024,384]{1,0:T(8,128)(2,1)S(1)}, bf16[1024,384]{1,0:T(8,128)(2,1)}, u32[]{:S(2)}, u32[]{:S(2)}) %collective-permute-start.5) | collective-permute-done | bytes 786464 | tf_op jit(solution)/shard_map/ppermute | solution.py:742
  152.0 6.5 pick.3
  158.6 12.4 %attend.3 = (bf16[256,384]{1,0:T(8,128)(2,1)}, bf16[256,384]{1,0:T(8,128)(2,1)}, f32[256,384]{1,0:T(8,128)}) custom-call(s32[9]{0:T(128)} %pad_add_fusion.refs_0_, bf16[1024,384]{1,0:T(8,128)(2,1)} %get-tuple-element.185.refs_1_, bf16[4096,384]{1,0:T(8,128)(2,1)} %get-tuple-element.188.refs_2_.refs_7_, bf16[4096,384]{1,0:T(8,128)(2,1)} %get-tuple-element.189.refs_3_, ...), custom_call_target="tpu_custom_call" | custom-call | flops 4499999744 | bytes 13500000 | tf_op jit(solution)/shard_map/attend/pallas_call | solution.py:51
  174.8 12.2 %attend.4 = (bf16[256,384]{1,0:T(8,128)(2,1)}, bf16[256,384]{1,0:T(8,128)(2,1)}, f32[256,384]{1,0:T(8,128)}) custom-call(s32[9]{0:T(128)} %pad_add_fusion.refs_0_, bf16[1024,384]{1,0:T(8,128)(2,1)} %get-tuple-element.185.refs_1_, bf16[4096,384]{1,0:T(8,128)(2,1)} %get-tuple-element.188.refs_2_.refs_7_, bf16[4096,384]{1,0:T(8,128)(2,1)} %get-tuple-element.189.refs_3_, ...), custom_call_target="tpu_custom_call" | custom-call | flops 4499999744 | bytes 13500000 | tf_op jit(solution)/shard_map/attend/pallas_call | solution.py:51
  198.3 15.8 %attend.5 = (bf16[512,384]{1,0:T(8,128)(2,1)}, bf16[512,384]{1,0:T(8,128)(2,1)}, f32[512,384]{1,0:T(8,128)}) custom-call(s32[9]{0:T(128)} %pad_add_fusion.refs_0_, bf16[1024,384]{1,0:T(8,128)(2,1)} %get-tuple-element.185.refs_1_, bf16[4096,384]{1,0:T(8,128)(2,1)} %get-tuple-element.188.refs_2_.refs_7_, bf16[4096,384]{1,0:T(8,128)(2,1)} %get-tuple-element.189.refs_3_, ...), custom_call_target="tpu_custom_call" | custom-call | flops 4499999744 | bytes 13500000 | tf_op jit(solution)/shard_map/attend/pallas_call | solution.py:51
  227.8 14.9 %collective-permute-done.18.refs_1_ = bf16[256,1536]{1,0:T(8,128)(2,1)S(1)} collective-permute-done((bf16[256,1536]{1,0:T(8,128)(2,1)}, bf16[256,1536]{1,0:T(8,128)(2,1)S(1)}, u32[]{:S(2)}, u32[]{:S(2)}) %collective-permute-start.18) | collective-permute-done | bytes 786464 | tf_op jit(solution)/shard_map/ppermute | solution.py:898
  251.6 8.5 ffn.4
  260.0 6.7 collective-permute-done.20.refs_1_
  275.5 8.5 ffn.5
  284.0 6.0 collective-permute-done.22.refs_1_
  298.7 8.5 ffn.6
  321.0 8.5 ffn.7
  342.8 9.6 %ffn_back.4 = (bf16[256,1536]{1,0:T(8,128)(2,1)}, f32[1,1536]{1,0:T(1,128)}, bf16[1024,1536]{1,0:T(8,128)(2,1)}, bf16[1024,1536]{1,0:T(8,128)(2,1)}, bf16[1024,2048]{1,0:T(8,128)(2,1)}) custom-call(bf16[256,1536]{1,0:T(8,128)(2,1)} %get-tuple-element.225.refs_0_.refs_7_, f32[256,1536]{1,0:T(8,128)} %get-tuple-element.201.refs_7_.refs_1_, ...), custom_call_target="tpu_custom_call" | custom-call | flops 2500000000 | bytes 7500000 | tf_op jit(solution)/shard_map/ffn_back/pallas_call | solution.py:51
  362.9 9.6 %ffn_back.5 = (bf16[256,1536]{1,0:T(8,128)(2,1)}, f32[1,1536]{1,0:T(1,128)}, bf16[1024,1536]{1,0:T(8,128)(2,1)}, bf16[1024,1536]{1,0:T(8,128)(2,1)}, bf16[1024,2048]{1,0:T(8,128)(2,1)}) custom-call(bf16[256,1536]{1,0:T(8,128)(2,1)} %get-tuple-element.230.refs_0_.refs_7_, ...), custom_call_target="tpu_custom_call", output_to_operand_aliasing={{2}: (8, {}), {3}: (9, {}), {4}: (10, {})} | custom-call | flops 2500000000 | bytes 7500000 | tf_op jit(solution)/shard_map/ffn_back/pallas_call | solution.py:51
  382.7 9.6 %ffn_back.6 = (bf16[256,1536]{1,0:T(8,128)(2,1)}, f32[1,1536]{1,0:T(1,128)}, bf16[1024,1536]{1,0:T(8,128)(2,1)}, bf16[1024,1536]{1,0:T(8,128)(2,1)}, bf16[1024,2048]{1,0:T(8,128)(2,1)}) custom-call(bf16[256,1536]{1,0:T(8,128)(2,1)} %get-tuple-element.238.refs_0_.refs_7_, ...), custom_call_target="tpu_custom_call", output_to_operand_aliasing={{2}: (8, {}), {3}: (9, {}), {4}: (10, {})} | custom-call | flops 2500000000 | bytes 7500000 | tf_op jit(solution)/shard_map/ffn_back/pallas_call | solution.py:51
  401.8 9.6 %ffn_back.7 = (bf16[256,1536]{1,0:T(8,128)(2,1)}, f32[1,1536]{1,0:T(1,128)}, bf16[1024,1536]{1,0:T(8,128)(2,1)}, bf16[1024,1536]{1,0:T(8,128)(2,1)}, bf16[1024,2048]{1,0:T(8,128)(2,1)}) custom-call(bf16[256,1536]{1,0:T(8,128)(2,1)} %get-tuple-element.244.refs_0_.refs_7_, ...), custom_call_target="tpu_custom_call", output_to_operand_aliasing={{2}: (8, {}), {3}: (9, {}), {4}: (10, {})} | custom-call | flops 2500000000 | bytes 7500000 | tf_op jit(solution)/shard_map/ffn_back/pallas_call | solution.py:51
  420.1 5.6 out_back.4
  425.7 9.9 %pair_grad.3.refs_6_.refs_7_ = bf16[1536,3072]{1,0:T(8,128)(2,1)} custom-call(bf16[1024,1536]{1,0:T(8,128)(2,1)} %get-tuple-element.259.refs_0_, bf16[1024,2048]{1,0:T(8,128)(2,1)} %get-tuple-element.260.refs_1_, bf16[1024,1536]{1,0:T(8,128)(2,1)} %get-tuple-element.261.refs_2_, bf16[1024,1024]{1,0:T(8,128)(2,1)} %get-tuple-element.262.refs_3_, ...), custom_call_target="tpu_custom_call" | custom-call | flops 2500000000 | bytes 7500000 | tf_op jit(solution)/shard_map/pair_grad/pallas_call | solution.py:51
  444.3 5.6 out_back.5
  449.9 7.7 collective-permute-start.41
  457.6 6.2 caption_back.2
  471.1 7.9 collective-permute-start.43
  479.0 5.6 out_back.6
  485.4 9.9 %pair_grad.4.refs_3_.refs_1_ = bf16[1536,3072]{1,0:T(8,128)(2,1)} custom-call(bf16[1024,1536]{1,0:T(8,128)(2,1)} %get-tuple-element.259.refs_0_, bf16[1024,2048]{1,0:T(8,128)(2,1)} %get-tuple-element.260.refs_1_, bf16[1024,1536]{1,0:T(8,128)(2,1)} %get-tuple-element.261.refs_2_, ...), custom_call_target="tpu_custom_call", output_to_operand_aliasing={{}: (7, {})} | custom-call | flops 2500000000 | bytes 7500000 | tf_op jit(solution)/shard_map/pair_grad/pallas_call | solution.py:51
  498.3 5.7 out_back.7
  504.0 6.4 caption_back.3
  516.8 28.9 %dq.1.refs_0_ = f32[1024,384]{1,0:T(8,128)} custom-call(s32[9]{0:T(128)} %pad_add_fusion.refs_0_, bf16[1024,384]{1,0:T(8,128)(2,1)} %get-tuple-element.185.refs_1_, bf16[4096,384]{1,0:T(8,128)(2,1)} %get-tuple-element.188.refs_2_.refs_7_, bf16[4096,384]{1,0:T(8,128)(2,1)} %get-tuple-element.189.refs_3_, ...), custom_call_target="tpu_custom_call" | custom-call | flops 11249999872 | bytes 33750000 | tf_op jit(solution)/shard_map/dq/pallas_call | solution.py:51
  546.4 24.9 %collective-permute-start.54 = (bf16[512,512]{1,0:T(8,128)(2,1)}, bf16[512,512]{1,0:T(8,128)(2,1)}, u32[]{:S(2)}, u32[]{:S(2)}) collective-permute-start(bf16[512,512]{1,0:T(8,128)(2,1)} %pin.6.refs_4_.refs_3_), channel_id=1, source_target_pairs={{0,16},{4,20},{24,8},{28,12},{1,17},{5,21},{25,9},{29,13},{2,18},{... | collective-permute-start | bytes 1572872 | tf_op jit(solution)/shard_map/ppermute | solution.py:775
  573.0 13.5 %collective-permute-done.54.refs_7_ = bf16[512,512]{1,0:T(8,128)(2,1)} collective-permute-done((bf16[512,512]{1,0:T(8,128)(2,1)}, bf16[512,512]{1,0:T(8,128)(2,1)}, u32[]{:S(2)}, u32[]{:S(2)}) %collective-permute-start.54) | collective-permute-done | bytes 524320 | tf_op jit(solution)/shard_map/ppermute | solution.py:775
  615.4 12.8 %dkv.3 = (f32[1024,128]{1,0:T(8,128)}, f32[1024,128]{1,0:T(8,128)}) custom-call(s32[9]{0:T(128)} %pad_add_fusion.refs_0_, bf16[1024,384]{1,0:T(8,128)(2,1)} %get-tuple-element.184.refs_1_, bf16[1024,384]{1,0:T(8,128)(2,1)} %get-tuple-element.186.refs_9_.refs_2_, bf16[8192,384]{1,0:T(8,128)(2,1)} %all-gather.9.cloned.1.call-done.refs_3_, ...), custom_call_target="tpu_custom_call" | custom-call | flops 5000000000 | bytes 15000000 | tf_op jit(solution)/shard_map/dkv/pallas_call | solution.py:51
  634.6 12.7 %dkv.4 = (f32[1024,128]{1,0:T(8,128)}, f32[1024,128]{1,0:T(8,128)}) custom-call(s32[9]{0:T(128)} %pad_add_fusion.refs_0_, bf16[1024,384]{1,0:T(8,128)(2,1)} %get-tuple-element.184.refs_1_, bf16[1024,384]{1,0:T(8,128)(2,1)} %get-tuple-element.186.refs_9_.refs_2_, bf16[8192,384]{1,0:T(8,128)(2,1)} %all-gather.9.cloned.1.call-done.refs_3_, ...), custom_call_target="tpu_custom_call" | custom-call | flops 5000000000 | bytes 15000000 | tf_op jit(solution)/shard_map/dkv/pallas_call | solution.py:51
  660.3 12.6 %dkv.5 = (f32[1024,128]{1,0:T(8,128)}, f32[1024,128]{1,0:T(8,128)}) custom-call(s32[9]{0:T(128)} %pad_add_fusion.refs_0_, bf16[1024,384]{1,0:T(8,128)(2,1)} %get-tuple-element.184.refs_1_, bf16[1024,384]{1,0:T(8,128)(2,1)} %get-tuple-element.186.refs_9_.refs_2_, bf16[8192,384]{1,0:T(8,128)(2,1)} %all-gather.9.cloned.1.call-done.refs_3_, ...), custom_call_target="tpu_custom_call" | custom-call | flops 5000000000 | bytes 15000000 | tf_op jit(solution)/shard_map/dkv/pallas_call | solution.py:51
  672.9 6.6 dqkv.4
  688.5 7.5 dqkv.5
  696.0 6.7 collective-permute-done.60.refs_1_
  714.3 6.6 dqkv.6
  736.2 6.7 dqkv.7
  748.8 10.9 %pair_grad.5.refs_4_.refs_1_ = bf16[1536,1536]{1,0:T(8,128)(2,1)} custom-call(bf16[1024,1536]{1,0:T(8,128)(2,1)} %get-tuple-element.183.refs_0_.refs_6_, bf16[1024,1152]{1,0:T(8,128)(2,1)} %get-tuple-element.343.refs_1_, bf16[1024,1536]{1,0:T(8,128)(2,1)} %get-tuple-element.344.refs_2_, bf16[1024,384]{1,0:T(8,128)(2,1)} %pad_maximum_fusion.2.refs_3_, ...), custom_call_target="tpu_custom_call" | custom-call | flops 2500000000 | bytes 7500000 | tf_op jit(solution)/shard_map/pair_grad/pallas_call | solution.py:51
  762.5 36.7 %all-gather = f32[64,1536]{1,0:T(8,128)} all-gather(f32[8,1536]{1,0:T(8,128)} %note.3.refs_7_), channel_id=2, replica_groups=mesh['wide'=8,'narrow'=4] {'wide'}, dimensions={0}, use_global_device_ids=true | all-gather | bytes 442368 | tf_op jit(solution)/shard_map/all_gather | solution.py:1182
  848.0 6.5 collective-permute-done.71.refs_1_
  866.8 10.3 %collective-permute-done.73.refs_1_ = bf16[256,1536]{1,0:T(8,128)(2,1)S(1)} collective-permute-done((bf16[256,1536]{1,0:T(8,128)(2,1)}, bf16[256,1536]{1,0:T(8,128)(2,1)S(1)}, u32[]{:S(2)}, u32[]{:S(2)}) %collective-permute-start.73) | collective-permute-done | bytes 786464 | tf_op jit(solution)/shard_map/ppermute | solution.py:898
  (490 shorter events, 358.0 us)
Async XLA Ops:
  7.2 151.3 %all-gather.5.cloned.1.call-start = ((), (), s32[]{:S(2)}) async-start(), calls=%async_computation.3 | async-start | bytes 3538944 | tf_op jit(solution)/shard_map/all_gather | solution.py:1056
  16.6 569.9 %all-gather.7.cloned.1.call-start = ((), (), s32[]{:S(2)}) async-start(), calls=%async_computation.4 | async-start | bytes 3538944 | tf_op jit(solution)/shard_map/all_gather | solution.py:1128
  67.2 20.6 %collective-permute-start = (bf16[1024,384]{1,0:T(8,128)(2,1)}, bf16[1024,384]{1,0:T(8,128)(2,1)S(1)}, u32[]{:S(2)}, u32[]{:S(2)}) collective-permute-start(bf16[1024,384]{1,0:T(8,128)(2,1)} %get-tuple-element.184.refs_1_), channel_id=1, source_target_pairs={{0,8},{4,12},{8,0},{12,4},{16,24},{20,28},{24,16},{28,20},{1,9},{5... | collective-permute-start | bytes 2359304 | tf_op jit(solution)/shard_map/ppermute | solution.py:742
  68.6 35.6 %collective-permute-start.8 = (bf16[1024,384]{1,0:T(8,128)(2,1)}, bf16[1024,384]{1,0:T(8,128)(2,1)S(1)}, u32[]{:S(2)}, u32[]{:S(2)}) collective-permute-start(bf16[1024,384]{1,0:T(8,128)(2,1)} %get-tuple-element.186.refs_9_.refs_2_), channel_id=1, source_target_pairs={{0,8},{4,12},{8,0},{12,4},{16,24},{20,28},{24,16},{28,20},{1,9},{5... | collective-permute-start | bytes 2359304 | tf_op jit(solution)/shard_map/ppermute | solution.py:742
  69.3 39.1 %collective-permute-start.10 = (bf16[1024,384]{1,0:T(8,128)(2,1)}, bf16[1024,384]{1,0:T(8,128)(2,1)}, u32[]{:S(2)}, u32[]{:S(2)}) collective-permute-start(bf16[1024,384]{1,0:T(8,128)(2,1)} %get-tuple-element.186.refs_9_.refs_2_), channel_id=1, source_target_pairs={{4,20},{16,0},{12,28},{24,8},{5,21},{17,1},{13,29},{25,9},{6,22},{... | collective-permute-start | bytes 2359304 | tf_op jit(solution)/shard_map/ppermute | solution.py:742
  105.0 21.3 %collective-permute-start.12 = (bf16[1024,384]{1,0:T(8,128)(2,1)}, bf16[1024,384]{1,0:T(8,128)(2,1)S(1)}, u32[]{:S(2)}, u32[]{:S(2)}) collective-permute-start(bf16[1024,384]{1,0:T(8,128)(2,1)} %pin.5.refs_11_.refs_17_), channel_id=1, source_target_pairs={{0,16},{28,12},{1,17},{29,13},{2,18},{30,14},{3,19},{31,15}} | collective-permute-start | bytes 2359304 | tf_op jit(solution)/shard_map/ppermute | solution.py:742
  109.8 22.9 %collective-permute-start.3 = (bf16[1024,384]{1,0:T(8,128)(2,1)S(1)}, bf16[1024,384]{1,0:T(8,128)(2,1)}, u32[]{:S(2)}, u32[]{:S(2)}) collective-permute-start(bf16[1024,384]{1,0:T(8,128)(2,1)S(1)} %copy-done.3), channel_id=1, source_target_pairs={{4,20},{16,0},{12,28},{24,8},{5,21},{17,1},{13,29},{25,9},{6,22},{... | collective-permute-start | bytes 2359304 | tf_op jit(solution)/shard_map/ppermute | solution.py:742
  111.1 21.9 %collective-permute-start.1 = (bf16[1024,384]{1,0:T(8,128)(2,1)S(1)}, bf16[1024,384]{1,0:T(8,128)(2,1)S(1)}, u32[]{:S(2)}, u32[]{:S(2)}) collective-permute-start(bf16[1024,384]{1,0:T(8,128)(2,1)S(1)} %copy-done.3), channel_id=1, source_target_pairs={{0,4},{4,0},{8,12},{12,8},{16,20},{20,16},{24,28},{28,24},{1,5},{5... | collective-permute-start | bytes 2359304 | tf_op jit(solution)/shard_map/ppermute | solution.py:713
  111.2 22.1 %collective-permute-start.7 = (bf16[1024,384]{1,0:T(8,128)(2,1)S(1)}, bf16[1024,384]{1,0:T(8,128)(2,1)S(1)}, u32[]{:S(2)}, u32[]{:S(2)}) collective-permute-start(bf16[1024,384]{1,0:T(8,128)(2,1)S(1)} %copy-done.4), channel_id=1, source_target_pairs={{0,4},{4,0},{8,12},{12,8},{16,20},{20,16},{24,28},{28,24},{1,5},{5... | collective-permute-start | bytes 2359304 | tf_op jit(solution)/shard_map/ppermute | solution.py:713
  126.4 21.7 %collective-permute-start.5 = (bf16[1024,384]{1,0:T(8,128)(2,1)S(1)}, bf16[1024,384]{1,0:T(8,128)(2,1)}, u32[]{:S(2)}, u32[]{:S(2)}) collective-permute-start(bf16[1024,384]{1,0:T(8,128)(2,1)S(1)} %copy-done.16), channel_id=1, source_target_pairs={{0,16},{4,20},{24,8},{28,12},{1,17},{5,21},{25,9},{29,13},{2,18},{... | collective-permute-start | bytes 2359304 | tf_op jit(solution)/shard_map/ppermute | solution.py:742
  132.8 19.2 %collective-permute-start.11 = (bf16[1024,384]{1,0:T(8,128)(2,1)}, bf16[1024,384]{1,0:T(8,128)(2,1)}, u32[]{:S(2)}, u32[]{:S(2)}) collective-permute-start(bf16[1024,384]{1,0:T(8,128)(2,1)} %collective-permute-done.10.refs_13_), channel_id=1, source_target_pairs={{0,4},{4,0},{8,12},{12,8},{16,20},{20,16},{24,28},{28,24},{1,5},{5... | collective-permute-start | bytes 2359304 | tf_op jit(solution)/shard_map/ppermute | solution.py:713
  133.0 19.0 %collective-permute-start.2 = (bf16[1024,384]{1,0:T(8,128)(2,1)S(1)}, bf16[1024,384]{1,0:T(8,128)(2,1)}, u32[]{:S(2)}, u32[]{:S(2)}) collective-permute-start(bf16[1024,384]{1,0:T(8,128)(2,1)S(1)} %copy-done.16), channel_id=1, source_target_pairs={{0,4},{4,0},{8,12},{12,8},{16,20},{20,16},{24,28},{28,24},{1,5},{5... | collective-permute-start | bytes 2359304 | tf_op jit(solution)/shard_map/ppermute | solution.py:713
  173.3 20.3 %collective-permute-start.15 = (bf16[256,1536]{1,0:T(8,128)(2,1)}, bf16[256,1536]{1,0:T(8,128)(2,1)}, u32[]{:S(2)}, u32[]{:S(2)}) collective-permute-start(bf16[256,1536]{1,0:T(8,128)(2,1)} %convolution_convert_fusion.4.refs_2_), channel_id=1, source_target_pairs={{0,1},{3,2},{1,0},{2,3},{4,5},{7,6},{5,4},{6,7},{8,9},{11,10},{9,8... | collective-permute-start | bytes 2359304 | tf_op jit(solution)/shard_map/ppermute | solution.py:898
  196.1 20.5 %collective-permute-start.16 = (bf16[256,1536]{1,0:T(8,128)(2,1)}, bf16[256,1536]{1,0:T(8,128)(2,1)S(1)}, u32[]{:S(2)}, u32[]{:S(2)}) collective-permute-start(bf16[256,1536]{1,0:T(8,128)(2,1)} %get-tuple-element.192), channel_id=1, source_target_pairs={{0,1},{3,2},{1,0},{2,3},{4,5},{7,6},{5,4},{6,7},{8,9},{11,10},{9,8... | collective-permute-start | bytes 2359304 | tf_op jit(solution)/shard_map/ppermute | solution.py:898
  221.4 21.2 %collective-permute-start.18 = (bf16[256,1536]{1,0:T(8,128)(2,1)}, bf16[256,1536]{1,0:T(8,128)(2,1)S(1)}, u32[]{:S(2)}, u32[]{:S(2)}) collective-permute-start(bf16[256,1536]{1,0:T(8,128)(2,1)} %get-tuple-element.195.refs_2_), channel_id=1, source_target_pairs={{0,1},{3,2},{1,0},{2,3},{4,5},{7,6},{5,4},{6,7},{8,9},{11,10},{9,8... | collective-permute-start | bytes 2359304 | tf_op jit(solution)/shard_map/ppermute | solution.py:898
  416.0 19.6 %collective-permute-start.36 = (bf16[256,1536]{1,0:T(8,128)(2,1)}, bf16[256,1536]{1,0:T(8,128)(2,1)S(1)}, u32[]{:S(2)}, u32[]{:S(2)}) collective-permute-start(bf16[256,1536]{1,0:T(8,128)(2,1)} %get-tuple-element.257.refs_2_), channel_id=1, source_target_pairs={{0,1},{3,2},{1,0},{2,3},{4,5},{7,6},{5,4},{6,7},{8,9},{11,10},{9,8... | collective-permute-start | bytes 2359304 | tf_op jit(solution)/shard_map/ppermute | solution.py:898
  440.6 23.2 %collective-permute-start.38 = (bf16[256,1536]{1,0:T(8,128)(2,1)}, bf16[256,1536]{1,0:T(8,128)(2,1)S(1)}, u32[]{:S(2)}, u32[]{:S(2)}) collective-permute-start(bf16[256,1536]{1,0:T(8,128)(2,1)} %get-tuple-element.272.refs_2_), channel_id=1, source_target_pairs={{0,1},{3,2},{1,0},{2,3},{4,5},{7,6},{5,4},{6,7},{8,9},{11,10},{9,8... | collective-permute-start | bytes 2359304 | tf_op jit(solution)/shard_map/ppermute | solution.py:898
  443.6 20.3 %collective-permute-start.39 = (bf16[256,1536]{1,0:T(8,128)(2,1)}, bf16[256,1536]{1,0:T(8,128)(2,1)S(1)}, u32[]{:S(2)}, u32[]{:S(2)}) collective-permute-start(bf16[256,1536]{1,0:T(8,128)(2,1)} %get-tuple-element.273.refs_4_), channel_id=1, source_target_pairs={{1,2},{2,1},{5,6},{6,5},{9,10},{10,9},{13,14},{14,13},{17,18},{18,... | collective-permute-start | bytes 2359304 | tf_op jit(solution)/shard_map/ppermute | solution.py:898
  449.9 21.1 %collective-permute-start.41 = (bf16[512,512]{1,0:T(8,128)(2,1)}, bf16[512,512]{1,0:T(8,128)(2,1)S(1)}, u32[]{:S(2)}, u32[]{:S(2)}) collective-permute-start(bf16[512,512]{1,0:T(8,128)(2,1)} %get-tuple-element.282.refs_4_.refs_6_.refs_1_), channel_id=1, source_target_pairs={{0,8},{4,12},{8,0},{12,4},{16,24},{20,28},{24,16},{28,20},{1,9},{5... | collective-permute-start | bytes 1572872 | tf_op jit(solution)/shard_map/ppermute | solution.py:765
  467.8 27.5 %collective-permute-start.40 = (bf16[256,1536]{1,0:T(8,128)(2,1)}, bf16[256,1536]{1,0:T(8,128)(2,1)S(1)}, u32[]{:S(2)}, u32[]{:S(2)}) collective-permute-start(bf16[256,1536]{1,0:T(8,128)(2,1)} %get-tuple-element.280.refs_2_), channel_id=1, source_target_pairs={{0,1},{3,2},{1,0},{2,3},{4,5},{7,6},{5,4},{6,7},{8,9},{11,10},{9,8... | collective-permute-start | bytes 2359304 | tf_op jit(solution)/shard_map/ppermute | solution.py:898
  471.1 24.2 %collective-permute-start.43 = (bf16[512,512]{1,0:T(8,128)(2,1)S(1)}, bf16[512,512]{1,0:T(8,128)(2,1)}, u32[]{:S(2)}, u32[]{:S(2)}) collective-permute-start(bf16[512,512]{1,0:T(8,128)(2,1)S(1)} %collective-permute-done.41.refs_5_.refs_3_), channel_id=1, source_target_pairs={{0,16},{4,20},{24,8},{28,12},{1,17},{5,21},{25,9},{29,13},{2,18},{... | collective-permute-start | bytes 1572872 | tf_op jit(solution)/shard_map/ppermute | solution.py:775
  513.4 102.0 %all-gather.9.cloned.1.call-start = ((), (), s32[]{:S(2)}) async-start(), calls=%async_computation.5 | async-start | bytes 7077888 | tf_op jit(solution)/shard_map/all_gather | solution.py:1070
  514.2 285.0 %reduce-scatter.4.cloned.1.call-start = ((), (), s32[]{:S(2)}) async-start(), calls=%async_computation.6 | async-start | bytes 10616832 | tf_op jit(solution)/shard_map/reduce_scatter | solution.py:960
  514.2 57.2 %collective-permute-start.46 = (bf16[512,512]{1,0:T(8,128)(2,1)}, bf16[512,512]{1,0:T(8,128)(2,1)S(1)}, u32[]{:S(2)}, u32[]{:S(2)}) collective-permute-start(bf16[512,512]{1,0:T(8,128)(2,1)} %get-tuple-element.282.refs_4_.refs_6_.refs_1_), channel_id=1, source_target_pairs={{0,4},{4,0},{8,12},{12,8},{16,20},{20,16},{24,28},{28,24},{1,5},{5... | collective-permute-start | bytes 1572872 | tf_op jit(solution)/shard_map/ppermute | solution.py:713
  514.3 57.2 %collective-permute-start.47 = (bf16[512,512]{1,0:T(8,128)(2,1)S(1)}, bf16[512,512]{1,0:T(8,128)(2,1)S(1)}, u32[]{:S(2)}, u32[]{:S(2)}) collective-permute-start(bf16[512,512]{1,0:T(8,128)(2,1)S(1)} %copy-done.20), channel_id=1, source_target_pairs={{0,4},{4,0},{8,12},{12,8},{16,20},{20,16},{24,28},{28,24},{1,5},{5... | collective-permute-start | bytes 1572872 | tf_op jit(solution)/shard_map/ppermute | solution.py:713
  514.8 57.2 %collective-permute-start.48 = (bf16[512,512]{1,0:T(8,128)(2,1)S(1)}, bf16[512,512]{1,0:T(8,128)(2,1)S(1)}, u32[]{:S(2)}, u32[]{:S(2)}) collective-permute-start(bf16[512,512]{1,0:T(8,128)(2,1)S(1)} %copy-done.22), channel_id=1, source_target_pairs={{0,4},{4,0},{8,12},{12,8},{16,20},{20,16},{24,28},{28,24},{1,5},{5... | collective-permute-start | bytes 1572872 | tf_op jit(solution)/shard_map/ppermute | solution.py:713
  514.9 30.8 %collective-permute-start.44 = (bf16[512,512]{1,0:T(8,128)(2,1)}, bf16[512,512]{1,0:T(8,128)(2,1)S(1)}, u32[]{:S(2)}, u32[]{:S(2)}) collective-permute-start(bf16[512,512]{1,0:T(8,128)(2,1)} %get-tuple-element.290.refs_5_.refs_7_.refs_1_), channel_id=1, source_target_pairs={{0,8},{4,12},{8,0},{12,4},{16,24},{20,28},{24,16},{28,20},{1,9},{5... | collective-permute-start | bytes 1572872 | tf_op jit(solution)/shard_map/ppermute | solution.py:765
  515.5 56.9 %collective-permute-start.52 = (bf16[512,512]{1,0:T(8,128)(2,1)}, bf16[512,512]{1,0:T(8,128)(2,1)}, u32[]{:S(2)}, u32[]{:S(2)}) collective-permute-start(bf16[512,512]{1,0:T(8,128)(2,1)} %get-tuple-element.290.refs_5_.refs_7_.refs_1_), channel_id=1, source_target_pairs={{4,20},{16,0},{12,28},{24,8},{5,21},{17,1},{13,29},{25,9},{6,22},{... | collective-permute-start | bytes 1572872 | tf_op jit(solution)/shard_map/ppermute | solution.py:766
  546.4 40.1 %collective-permute-start.54 = (bf16[512,512]{1,0:T(8,128)(2,1)}, bf16[512,512]{1,0:T(8,128)(2,1)}, u32[]{:S(2)}, u32[]{:S(2)}) collective-permute-start(bf16[512,512]{1,0:T(8,128)(2,1)} %pin.6.refs_4_.refs_3_), channel_id=1, source_target_pairs={{0,16},{4,20},{24,8},{28,12},{1,17},{5,21},{25,9},{29,13},{2,18},{... | collective-permute-start | bytes 1572872 | tf_op jit(solution)/shard_map/ppermute | solution.py:775
  571.4 21.5 %collective-permute-start.49 = (bf16[512,512]{1,0:T(8,128)(2,1)}, bf16[512,512]{1,0:T(8,128)(2,1)}, u32[]{:S(2)}, u32[]{:S(2)}) collective-permute-start(bf16[512,512]{1,0:T(8,128)(2,1)} %collective-permute-done.43.refs_4_.refs_7_), channel_id=1, source_target_pairs={{0,4},{4,0},{8,12},{12,8},{16,20},{20,16},{24,28},{28,24},{1,5},{5... | collective-permute-start | bytes 1572872 | tf_op jit(solution)/shard_map/ppermute | solution.py:713
  571.5 25.0 %collective-permute-start.50 = (bf16[512,512]{1,0:T(8,128)(2,1)}, bf16[512,512]{1,0:T(8,128)(2,1)S(1)}, u32[]{:S(2)}, u32[]{:S(2)}) collective-permute-start(bf16[512,512]{1,0:T(8,128)(2,1)} %get-tuple-element.290.refs_5_.refs_7_.refs_1_), channel_id=1, source_target_pairs={{0,4},{4,0},{8,12},{12,8},{16,20},{20,16},{24,28},{28,24},{1,5},{5... | collective-permute-start | bytes 1572872 | tf_op jit(solution)/shard_map/ppermute | solution.py:713
  572.2 24.3 %collective-permute-start.51 = (bf16[512,512]{1,0:T(8,128)(2,1)}, bf16[512,512]{1,0:T(8,128)(2,1)S(1)}, u32[]{:S(2)}, u32[]{:S(2)}) collective-permute-start(bf16[512,512]{1,0:T(8,128)(2,1)} %pin.6.refs_4_.refs_3_), channel_id=1, source_target_pairs={{0,4},{4,0},{8,12},{12,8},{16,20},{20,16},{24,28},{28,24},{1,5},{5... | collective-permute-start | bytes 1572872 | tf_op jit(solution)/shard_map/ppermute | solution.py:713
  573.0 23.6 %collective-permute-start.53 = (bf16[512,512]{1,0:T(8,128)(2,1)}, bf16[512,512]{1,0:T(8,128)(2,1)}, u32[]{:S(2)}, u32[]{:S(2)}) collective-permute-start(bf16[512,512]{1,0:T(8,128)(2,1)} %collective-permute-done.52.refs_5_), channel_id=1, source_target_pairs={{0,4},{4,0},{8,12},{12,8},{16,20},{20,16},{24,28},{28,24},{1,5},{5... | collective-permute-start | bytes 1572872 | tf_op jit(solution)/shard_map/ppermute | solution.py:713
  601.3 223.8 %reduce-scatter.6.cloned.1.call-start = ((), (), s32[]{:S(2)}) async-start(), calls=%async_computation.7 | async-start | bytes 7077888 | tf_op jit(solution)/shard_map/reduce_scatter | solution.py:960
  610.0 19.9 %collective-permute-start.45 = (bf16[256,1536]{1,0:T(8,128)(2,1)S(1)}, bf16[256,1536]{1,0:T(8,128)(2,1)}, u32[]{:S(2)}, u32[]{:S(2)}) collective-permute-start(bf16[256,1536]{1,0:T(8,128)(2,1)S(1)} %get-tuple-element.412.refs_2_), channel_id=1, source_target_pairs={{0,1},{3,2},{1,0},{2,3},{4,5},{7,6},{5,4},{6,7},{8,9},{11,10},{9,8... | collective-permute-start | bytes 2359304 | tf_op jit(solution)/shard_map/ppermute | solution.py:898
  632.6 244.5 %reduce-scatter.8.cloned.1.call-start = ((), (), s32[]{:S(2)}) async-start(), calls=%async_computation.8 | async-start | bytes 5308416 | tf_op jit(solution)/shard_map/reduce_scatter | solution.py:960
  632.6 19.3 %collective-permute-start.56 = (bf16[256,1536]{1,0:T(8,128)(2,1)}, bf16[256,1536]{1,0:T(8,128)(2,1)S(1)}, u32[]{:S(2)}, u32[]{:S(2)}) collective-permute-start(bf16[256,1536]{1,0:T(8,128)(2,1)} %get-tuple-element.294), channel_id=1, source_target_pairs={{0,1},{3,2},{1,0},{2,3},{4,5},{7,6},{5,4},{6,7},{8,9},{11,10},{9,8... | collective-permute-start | bytes 2359304 | tf_op jit(solution)/shard_map/ppermute | solution.py:898
  656.2 23.4 %collective-permute-start.58 = (bf16[256,1536]{1,0:T(8,128)(2,1)}, bf16[256,1536]{1,0:T(8,128)(2,1)S(1)}, u32[]{:S(2)}, u32[]{:S(2)}) collective-permute-start(bf16[256,1536]{1,0:T(8,128)(2,1)} %get-tuple-element.297.refs_2_), channel_id=1, source_target_pairs={{0,1},{3,2},{1,0},{2,3},{4,5},{7,6},{5,4},{6,7},{8,9},{11,10},{9,8... | collective-permute-start | bytes 2359304 | tf_op jit(solution)/shard_map/ppermute | solution.py:898
  659.6 20.0 %collective-permute-start.59 = (bf16[256,1536]{1,0:T(8,128)(2,1)}, bf16[256,1536]{1,0:T(8,128)(2,1)S(1)}, u32[]{:S(2)}, u32[]{:S(2)}) collective-permute-start(bf16[256,1536]{1,0:T(8,128)(2,1)} %get-tuple-element.298.refs_8_.refs_4_), channel_id=1, source_target_pairs={{1,2},{2,1},{5,6},{6,5},{9,10},{10,9},{13,14},{14,13},{17,18},{18,... | collective-permute-start | bytes 2359304 | tf_op jit(solution)/shard_map/ppermute | solution.py:898
  730.7 68.5 %collective-permute-start.64 = (bf16[256,1536]{1,0:T(8,128)(2,1)}, bf16[256,1536]{1,0:T(8,128)(2,1)S(1)}, u32[]{:S(2)}, u32[]{:S(2)}) collective-permute-start(bf16[256,1536]{1,0:T(8,128)(2,1)} %get-tuple-element.315.refs_2_), channel_id=1, source_target_pairs={{0,1},{3,2},{1,0},{2,3},{4,5},{7,6},{5,4},{6,7},{8,9},{11,10},{9,8... | collective-permute-start | bytes 2359304 | tf_op jit(solution)/shard_map/ppermute | solution.py:898
  734.0 65.1 %collective-permute-start.65 = (bf16[256,1536]{1,0:T(8,128)(2,1)}, bf16[256,1536]{1,0:T(8,128)(2,1)}, u32[]{:S(2)}, u32[]{:S(2)}) collective-permute-start(bf16[256,1536]{1,0:T(8,128)(2,1)} %get-tuple-element.316.refs_4_), channel_id=1, source_target_pairs={{1,2},{2,1},{5,6},{6,5},{9,10},{10,9},{13,14},{14,13},{17,18},{18,... | collective-permute-start | bytes 2359304 | tf_op jit(solution)/shard_map/ppermute | solution.py:898
  810.1 20.3 %collective-permute-start.69 = (bf16[256,1536]{1,0:T(8,128)(2,1)}, bf16[256,1536]{1,0:T(8,128)(2,1)}, u32[]{:S(2)}, u32[]{:S(2)}) collective-permute-start(bf16[256,1536]{1,0:T(8,128)(2,1)} %get-tuple-element.345.refs_2_), channel_id=1, source_target_pairs={{0,1},{3,2},{1,0},{2,3},{4,5},{7,6},{5,4},{6,7},{8,9},{11,10},{9,8... | collective-permute-start | bytes 2359304 | tf_op jit(solution)/shard_map/ppermute | solution.py:898
  810.1 20.2 %collective-permute-start.70 = (bf16[256,1536]{1,0:T(8,128)(2,1)}, bf16[256,1536]{1,0:T(8,128)(2,1)}, u32[]{:S(2)}, u32[]{:S(2)}) collective-permute-start(bf16[256,1536]{1,0:T(8,128)(2,1)} %get-tuple-element.346.refs_4_), channel_id=1, source_target_pairs={{1,2},{2,1},{5,6},{6,5},{9,10},{10,9},{13,14},{14,13},{17,18},{18,... | collective-permute-start | bytes 2359304 | tf_op jit(solution)/shard_map/ppermute | solution.py:898
  814.8 27.5 %collective-permute-start.74 = (f32[8,128]{1,0:T(8,128)S(1)}, f32[8,128]{1,0:T(8,128)S(1)}, u32[]{:S(2)}, u32[]{:S(2)}) collective-permute-start(f32[8,128]{1,0:T(8,128)S(1)} %bitcast.94), channel_id=1, source_target_pairs={{0,1},{1,0},{2,3},{3,2},{4,5},{5,4},{6,7},{7,6},{8,9},{9,8},{10,11... | collective-permute-start | bytes 12296 | tf_op jit(solution)/shard_map/ppermute | solution.py:713
  817.4 24.9 %collective-permute-start.75 = (f32[8,128]{1,0:T(8,128)S(1)}, f32[8,128]{1,0:T(8,128)S(1)}, u32[]{:S(2)}, u32[]{:S(2)}) collective-permute-start(f32[8,128]{1,0:T(8,128)S(1)} %bitcast.95), channel_id=1, source_target_pairs={{0,2},{1,3},{2,0},{3,1},{4,6},{5,7},{6,4},{7,5},{8,10},{9,11},{10,... | collective-permute-start | bytes 12296 | tf_op jit(solution)/shard_map/ppermute | solution.py:713
  818.8 23.6 %collective-permute-start.76 = (f32[8,128]{1,0:T(8,128)S(1)}, f32[8,128]{1,0:T(8,128)S(1)}, u32[]{:S(2)}, u32[]{:S(2)}) collective-permute-start(f32[8,128]{1,0:T(8,128)S(1)} %bitcast.96), channel_id=1, source_target_pairs={{0,3},{1,2},{2,1},{3,0},{4,7},{5,6},{6,5},{7,4},{8,11},{9,10},{10,... | collective-permute-start | bytes 12296 | tf_op jit(solution)/shard_map/ppermute | solution.py:713
  833.6 20.8 %collective-permute-start.71 = (bf16[256,1536]{1,0:T(8,128)(2,1)}, bf16[256,1536]{1,0:T(8,128)(2,1)}, u32[]{:S(2)}, u32[]{:S(2)}) collective-permute-start(bf16[256,1536]{1,0:T(8,128)(2,1)} %get-tuple-element.348.refs_2_), channel_id=1, source_target_pairs={{0,1},{3,2},{1,0},{2,3},{4,5},{7,6},{5,4},{6,7},{8,9},{11,10},{9,8... | collective-permute-start | bytes 2359304 | tf_op jit(solution)/shard_map/ppermute | solution.py:898
  857.4 19.7 %collective-permute-start.73 = (bf16[256,1536]{1,0:T(8,128)(2,1)}, bf16[256,1536]{1,0:T(8,128)(2,1)S(1)}, u32[]{:S(2)}, u32[]{:S(2)}) collective-permute-start(bf16[256,1536]{1,0:T(8,128)(2,1)} %get-tuple-element.351.refs_2_), channel_id=1, source_target_pairs={{0,1},{3,2},{1,0},{2,3},{4,5},{7,6},{5,4},{6,7},{8,9},{11,10},{9,8... | collective-permute-start | bytes 2359304 | tf_op jit(solution)/shard_map/ppermute | solution.py:898
  (135 other events, 1271.0 us)
Sparse Core Ops, SparseCore 0:
  16.7 35.8 all-gather.4
  513.5 34.6 all-gather.6
  550.1 45.9 all-gather.8
  601.4 77.6 reduce-scatter.3
  682.4 61.7 reduce-scatter.5
  803.6 51.9 reduce-scatter.7

commit v10 on v8

--- a/solution.py
+++ b/solution.py
@@ -30,7 +30,7 @@
 
 
 COST = {
-    "key": 8, "query": 9, "caption_norm": 2, "pick": 5, "attend": 18, "hop": 3, "ffn": 9, "ffn_back": 10, "out_back": 6,
+    "key": 8, "query": 9, "caption_norm": 2, "pick": 5, "attend": 15, "hop": 3, "ffn": 9, "ffn_back": 10, "out_back": 6,
     "pair_grad": 10, "caption_back": 6, "dq": 27, "dkv": 24, "dqkv": 7, "caption_grad": 3, "last": 3, "note": 1, "pin": 1,
 }
 
@@ -145,7 +145,7 @@
     return jnp.concatenate([t] * (n // t.shape[1]), 1)
 
 
-def key_kernel(p_ref, v_ref, w_ref, wv_ref, c_ref, s1_ref, s2_ref, hg_ref, a_ref, kr_ref, k_ref, vv_ref):
+def key_kernel(p_ref, v_ref, w_ref, wv_ref, wq_ref, c_ref, s1_ref, s2_ref, hg_ref, a_ref, kr_ref, k_ref, vv_ref, qr_ref, q_ref):
     x = p_ref[...].astype(f32)
     a = (x * inv_rms(x) * row(v_ref, 0)).astype(bf16)
     a_ref[...] = a
@@ -153,6 +153,9 @@
     kr_ref[...] = k
     k_ref[...] = turned(k, row(hg_ref, 1), (c_ref, s1_ref, s2_ref)).astype(bf16)
     vv_ref[...] = mm(a, wv_ref[0]).astype(bf16)
+    q = mm(a, wq_ref[0])
+    qr_ref[...] = q
+    q_ref[...] = (turned(q, row(hg_ref, 0), (c_ref, s1_ref, s2_ref)) * (0.125 * LOG2E)).astype(bf16)
 
 
 def turned(y, gain, tabs):
@@ -160,12 +163,6 @@
     cos, s1, s2 = (tile3(t[...], n) for t in tabs)
     z = y * lax.rsqrt(head_sum(y * y, head_ones(n)) * (1.0 / HD) + EPS) * gain
     return z * cos + pltpu.roll(z, n - 16, 1) * s1 + pltpu.roll(z, 16, 1) * s2
-
-
-def query_kernel(a_ref, wq_ref, c_ref, s1_ref, s2_ref, hg_ref, qr_ref, q_ref):
-    q = mm(a_ref[...], wq_ref[0])
-    qr_ref[...] = q
-    q_ref[...] = (turned(q, row(hg_ref, 0), (c_ref, s1_ref, s2_ref)) * (0.125 * LOG2E)).astype(bf16)
 
 
 def one_weight(w, k):
@@ -179,25 +176,10 @@
         "key",
         key_kernel,
         (t // br,),
-        (patches, vec, w, w, *tabs, hg),
-        [rows_of(br, d), whole(vec.shape), one_weight(w, 1), one_weight(w, 2)] + [rows_of(br, 128)] * 3 + [whole(hg.shape)],
-        [rows_of(br, d)] + [rows_of(br, n)] * 3,
-        [sds((t, d), bf16), sds((t, n), f32), sds((t, n), bf16), sds((t, n), bf16)],
-        after=after,
-    )
-
-
-def query_call(order, a, w, tabs, hg, after, br=256):
-    t, d = a.shape
-    n = w.shape[2]
-    return order.run(
-        "query",
-        query_kernel,
-        (t // br,),
-        (a, w, *tabs, hg),
-        [rows_of(br, d), one_weight(w, 0)] + [rows_of(br, 128)] * 3 + [whole(hg.shape)],
-        [rows_of(br, n)] * 2,
-        [sds((t, n), f32), sds((t, n), bf16)],
+        (patches, vec, w, w, w, *tabs, hg),
+        [rows_of(br, d), whole(vec.shape), one_weight(w, 1), one_weight(w, 2), one_weight(w, 0)] + [rows_of(br, 128)] * 3 + [whole(hg.shape)],
+        [rows_of(br, d)] + [rows_of(br, n)] * 5,
+        [sds((t, d), bf16), sds((t, n), f32), sds((t, n), bf16), sds((t, n), bf16), sds((t, n), f32), sds((t, n), bf16)],
         after=after,
     )
 
@@ -214,33 +196,35 @@
 def attend_kernel(sc, q_ref, k_ref, v_ref, ck_ref, cv_ref, tg_ref, mix_ref, o_ref, li_ref, acc):
     j = pl.program_id(1)
     masks = halves(128)
-    keys = 512
+    keys = k_ref.shape[0] if q_ref.shape[0] <= BR else 512
+
+    def block_sums(h):
+        q = q_ref[...]
+        total = 0.0
+        for c in range(k_ref.shape[0] // keys):
+            at = slice(c * keys, (c + 1) * keys)
+            total = total + soft_sums(q, k_ref[at, :], v_ref[at, :], masks[h])
+        return total
 
     @pl.when(j == 0)
     def _():
-        acc[...] = jnp.zeros_like(acc)
-
-    @pl.when(j < sc[0])
+        for h in range(2):
+            acc[2 + h] = soft_sums(q_ref[...], ck_ref[...], cv_ref[...], masks[h])
+            acc[h] = block_sums(h)
+
+    @pl.when((j > 0) & (j < sc[0]))
     def _():
-        q = q_ref[...]
         for h in range(2):
-            total = acc[h]
-            for c in range(k_ref.shape[0] // keys):
-                at = slice(c * keys, (c + 1) * keys)
-                total = total + soft_sums(q, k_ref[at, :], v_ref[at, :], masks[h])
-            acc[h] = total
+            acc[h] += block_sums(h)
 
     @pl.when(j == SPAN - 1)
     def _():
-        q = q_ref[...]
-
         def finish(a0, a1):
             inverse = 1.0 / jnp.where(masks[0], pltpu.roll(a0, HD, 1), pltpu.roll(a1, HD, 1))
             return jnp.where(masks[0], a0, a1) * inverse, inverse
 
         o, li = finish(acc[0], acc[1])
-        c0, c1 = (soft_sums(q, ck_ref[...], cv_ref[...], m) for m in masks)
-        mix_ref[...] = (o + tg_ref[...] * finish(c0, c1)[0]).astype(bf16)
+        mix_ref[...] = (o + tg_ref[...] * finish(acc[2], acc[3])[0]).astype(bf16)
         o_ref[...] = o.astype(bf16)
         li_ref[...] = li
 
@@ -266,7 +250,7 @@
         ],
         [pl.BlockSpec((bq, 128), mine)] * 3,
         [sds((bq, n), bf16), sds((bq, n), bf16), sds((bq, n), f32)],
-        [pltpu.VMEM((2, bq, 128), f32)],
+        [pltpu.VMEM((4, bq, 128), f32)],
         sc,
     )
 
@@ -1043,23 +1027,16 @@
     chunks = range(t // BR)
     pairs_of = range(t // (2 * BR))
     sums = Sums(order, deep, mz)
-    a1, k_raw, k, v = key_call(order, patches, vec, w_qkv, tabs, hg, ())
+    a1, k_raw, k, v, q_raw, q = key_call(order, patches, vec, w_qkv, tabs, hg, ())
     kv = Gather(k, v)
 
-    q_raw, q = query_call(order, a1, w_qkv, tabs, hg, ())
 
     q_all = lax.all_gather(q, "wide", axis=0, tiled=True)
     k_all, v_all = pick(order, sc, kv.pieces(), SPAN)
     heads_out = {}
-    for c in chunks[: len(chunks) // 2]:
+    for c in chunks:
         heads_out[c] = (*attend_call(order, sc, q, k_all, v_all, cap, text, tg, c, BR), 0)
         sums.add(("attn", c), mm(heads_out[c][0], w_out).astype(bf16))
-    half = (len(chunks) + 1) // 2
-    later = attend_call(order, sc, q, k_all, v_all, cap, text, tg, 1, half * BR)
-    for c in chunks[half:]:
-        heads_out[c] = (*later, c - half)
-        at = (c - half) * BR
-        sums.add(("attn", c), mm(later[0][at : at + BR], w_out).astype(bf16))
 
     mids, gus = {}, {}
     whole_out = ()
@@ -1112,8 +1089,8 @@
     def make_dq(h, after):
         return dq_call(order, sc, q, d_scaled[h], k_all, v_all, dq_caps[h], h, after)
 
-    for h in pairs_of[:-1]:
-        dqs[h] = make_dq(h, ())
+    for h in pairs_of:
+        dqs[h] = make_dq(h, () if h == 0 else d_got[last_half].first)
 
     d_cap, hs_c = order.run(
         "caption_grad",
@@ -1131,13 +1108,12 @@
     text_parts = [padded[:, p * d : (p + 1) * d] for p in range(pieces)]
 
     sums.add(("text", 0), text_parts[0])
-    dqs[last_half] = make_dq(last_half, (*d_got[last_half].first, *text_parts))
-    sums.add(("text", 1), text_parts[1], (cap_part, *d_got[last_half].second))
     ds = [x for h in pairs_of for x in pick(order, sc, d_got[h].pieces(), SPAN)]
+    sums.add(("text", 1), text_parts[1], (cap_part,))
     g_mlp = scatter_rows(pin(order, mlp_part[0]))
     whole_out = ()
     c1_parts, hs_parts = [], []
-    mixed = jnp.concatenate([heads_out[c][0] for c in chunks[:half]] + [later[0]])
+    mixed = jnp.concatenate([heads_out[c][0] for c in chunks])
     pairs = n // 128
 
     def project(c, dkv, after=()):
@@ -1166,14 +1142,17 @@
             packed = pack_call(order, c1_parts, hs_parts, hs_c, gate_sum, tg, c2, c3, c4, mz)
             from_narrow = [packed] + [swap(packed, "narrow", deep, m) for m in range(1, deep)]
             attn_part = pair_grad_call(order, a1, d_qkv, d_attn, mixed)[0]
-            (folded,) = fold_call(order, from_narrow)
-            got = lax.all_gather(folded, "wide")
-        sums.add(("da1", c), da1_part, (g_mlp, got) if c == chunks[-1] else ())
+        sums.add(("da1", c), da1_part, (g_mlp, *from_narrow) if c == chunks[-1] else ())
     g_attn = scatter_rows(pin(order, attn_part))
 
-    whole_out = ()
-    for c in chunks:
-        whole_out = last_call(order, c, sums.get(("da1", c), (g_cap,) if c < 3 else (g_attn,)), patches, d_mids[c], vec, whole_out)
+    (folded,) = fold_call(order, from_narrow)
+    got = lax.all_gather(folded, "wide")
+    whole_out = last_call(order, 0, sums.get(("da1", 0)), patches, d_mids[0], vec, ())
+    for c in chunks[1:]:
+        da1 = sums.get(("da1", c), (g_cap, got) if c == 1 else (g_attn,) if c == chunks[-1] else ())
+        if c == 1:
+            got = pin(order, got)
+        whole_out = last_call(order, c, da1, patches, d_mids[c], vec, whole_out)
     (grad_patches,) = whole_out
     grad_captions = jnp.concatenate([sums.get(("text", p)) for p in range(pieces)], 1)[:, : d_text.shape[1]]
 

time: 880 us -> 871 us (0.990)
  waiting for transfers between devices: 118 us -> 93.8 us
  starting transfers between devices: 119 us -> 136 us
    ppermute x42, waiting for transfers between devices: 69.8 us -> 50 us  [step(): go = lambda x, perm: lax.ppermute(x, 'narrow', perm)]
    ppermute x13, starting transfers between devices: 27.2 us -> 46 us  [__init__(): send = lambda x, pairs: lax.ppermute(x, 'wide', pairs)]
    pallas_call x69 -> x70, Pallas kernels: 472 us -> 470 us  [run(): pl.pallas_call(body, grid_spec=pltpu.PrefetchScalarGridSpec(num_scalar_pr...]
    unnamed x223 -> x207, local copies, waits for them, and re-layouts: 35.1 us -> 34.4 us
  transfers between devices with their start and end apart: 83 -> 83, of which waited for: 17 -> 15; matrix products, arithmetic and copies ran while one was open for 7% -> 7% of each run, Pallas kernels for 45% -> 45%
where the time goes in v10:
time: 871 us
  Pallas kernels  470 us (54%)
  starting transfers between devices  136 us (16%)
  waiting for transfers between devices  93.8 us (11%)
  local copies, waits for them, and re-layouts  46.3 us (5%)
  other arithmetic  42.1 us (5%)
  blocking collectives  36.7 us (4%)
  matrix products  25.2 us (3%)
  between operations  21.4 us (2%)
    pallas_call x70, Pallas kernels, run(): pl.pallas_call(body, grid_spec=pltpu.PrefetchScalarGridSpec(num_scalar_pr...  470 us
    ppermute x42, starting transfers between devices, step(): go = lambda x, perm: lax.ppermute(x, 'narrow', perm)  76.3 us
    ppermute x42, waiting for transfers between devices, step(): go = lambda x, perm: lax.ppermute(x, 'narrow', perm)  50 us
    ppermute x13, starting transfers between devices, __init__(): send = lambda x, pairs: lax.ppermute(x, 'wide', pairs)  46 us
    ppermute x13, waiting for transfers between devices, __init__(): send = lambda x, pairs: lax.ppermute(x, 'wide', pairs)  42.9 us
    unnamed x207, local copies, waits for them, and re-layouts  34.4 us
    all_gather x2, blocking collectives, gather_now(): lax.all_gather(padded, axis, axis=0, tiled=True).reshape(-1, wide)[:, :n]  25.2 us
  transfers between devices with their start and end apart: 83, of which 15 were waited for; matrix products, arithmetic and copies ran while one was open for 7% of the time, Pallas kernels for 45%

profile of v10, /device:TPU:0, one launch (start us, length us, event | category | flops | bytes accessed | tf_op | source)
XLA Modules:
  0.0 870.7 jit_solution(7672256122178016649)
XLA Ops:
  26.2 14.9 %all_gather.22 = f32[4,8,256]{2,1,0:T(8,128)S(1)} all-gather(f32[1,8,256]{2,1,0:T(8,128)S(1)} %reshape.309), channel_id=1, replica_groups=mesh['wide'=8,'narrow'=4] {'narrow'}, dimensions={0}, use_global_device_ids=true | all-gather | bytes 40960 | tf_op jit(solution)/shard_map/all_gather | solution.py:837
  41.1 10.3 %all_gather.23 = f32[8,8,896]{2,1,0:T(8,128)S(1)} all-gather(f32[1,8,896]{2,1,0:T(8,128)S(1)} %reshape.311), channel_id=1, replica_groups=mesh['wide'=8,'narrow'=4] {'wide'}, dimensions={0}, use_global_device_ids=true | all-gather | bytes 258048 | tf_op jit(solution)/shard_map/all_gather | solution.py:837
  57.8 13.4 %key.1 = (bf16[1024,1536]{1,0:T(8,128)(2,1)}, f32[1024,384]{1,0:T(8,128)}, bf16[1024,384]{1,0:T(8,128)(2,1)}, bf16[1024,384]{1,0:T(8,128)(2,1)}, f32[1024,384]{1,0:T(8,128)}, /*index=5*/bf16[1024,384]{1,0:T(8,128)(2,1)}) custom-call(bf16[1024,1536]{1,0:T(8,128)(2,1)} %refs_1_.7, f32[4,1536]{1,0:T(4,128)} %maximum_multiply_fusion.1.refs_1_.refs_2_.refs_4_.refs_3_, ...), custom_call_target="tpu_custom_call" | custom-call | flops 2000000000 | bytes 6000000 | tf_op jit(solution)/shard_map/key/pallas_call | solution.py:51
  74.7 17.3 %collective-permute-done.8.refs_11_ = bf16[1024,384]{1,0:T(8,128)(2,1)} collective-permute-done((bf16[1024,384]{1,0:T(8,128)(2,1)}, bf16[1024,384]{1,0:T(8,128)(2,1)}, u32[]{:S(2)}, u32[]{:S(2)}) %collective-permute-start.8) | collective-permute-done | bytes 786464 | tf_op jit(solution)/shard_map/ppermute | solution.py:718
  98.2 10.1 %collective-permute-done.1.refs_3_ = bf16[1024,384]{1,0:T(8,128)(2,1)} collective-permute-done((bf16[1024,384]{1,0:T(8,128)(2,1)}, bf16[1024,384]{1,0:T(8,128)(2,1)}, u32[]{:S(2)}, u32[]{:S(2)}) %collective-permute-start.1) | collective-permute-done | bytes 786464 | tf_op jit(solution)/shard_map/ppermute | solution.py:718
  108.3 5.3 collective-permute-done.12
  113.6 5.3 collective-permute-start.5
  120.3 10.2 %collective-permute-done.5.refs_7_ = bf16[1024,384]{1,0:T(8,128)(2,1)} collective-permute-done((bf16[1024,384]{1,0:T(8,128)(2,1)}, bf16[1024,384]{1,0:T(8,128)(2,1)}, u32[]{:S(2)}, u32[]{:S(2)}) %collective-permute-start.5) | collective-permute-done | bytes 786464 | tf_op jit(solution)/shard_map/ppermute | solution.py:718
  135.3 6.2 pick.3
  141.6 14.9 %attend.4 = (bf16[256,384]{1,0:T(8,128)(2,1)}, bf16[256,384]{1,0:T(8,128)(2,1)}, f32[256,384]{1,0:T(8,128)}) custom-call(s32[9]{0:T(128)} %pad_add_fusion.refs_0_, bf16[1024,384]{1,0:T(8,128)(2,1)} %get-tuple-element.188.refs_1_, bf16[4096,384]{1,0:T(8,128)(2,1)} %get-tuple-element.192.refs_2_.refs_7_.refs_4_, ...), custom_call_target="tpu_custom_call" | custom-call | flops 3750000128 | bytes 11250000 | tf_op jit(solution)/shard_map/attend/pallas_call | solution.py:51
  160.4 14.8 %attend.5 = (bf16[256,384]{1,0:T(8,128)(2,1)}, bf16[256,384]{1,0:T(8,128)(2,1)}, f32[256,384]{1,0:T(8,128)}) custom-call(s32[9]{0:T(128)} %pad_add_fusion.refs_0_, bf16[1024,384]{1,0:T(8,128)(2,1)} %get-tuple-element.188.refs_1_, bf16[4096,384]{1,0:T(8,128)(2,1)} %get-tuple-element.192.refs_2_.refs_7_.refs_4_, ...), custom_call_target="tpu_custom_call" | custom-call | flops 3750000128 | bytes 11250000 | tf_op jit(solution)/shard_map/attend/pallas_call | solution.py:51
  184.0 14.8 %attend.6 = (bf16[256,384]{1,0:T(8,128)(2,1)}, bf16[256,384]{1,0:T(8,128)(2,1)}, f32[256,384]{1,0:T(8,128)}) custom-call(s32[9]{0:T(128)} %pad_add_fusion.refs_0_, bf16[1024,384]{1,0:T(8,128)(2,1)} %get-tuple-element.188.refs_1_, bf16[4096,384]{1,0:T(8,128)(2,1)} %get-tuple-element.192.refs_2_.refs_7_.refs_4_, ...), custom_call_target="tpu_custom_call" | custom-call | flops 3750000128 | bytes 11250000 | tf_op jit(solution)/shard_map/attend/pallas_call | solution.py:51
  210.8 14.8 %attend.7 = (bf16[256,384]{1,0:T(8,128)(2,1)}, bf16[256,384]{1,0:T(8,128)(2,1)}, f32[256,384]{1,0:T(8,128)}) custom-call(s32[9]{0:T(128)} %pad_add_fusion.refs_0_, bf16[1024,384]{1,0:T(8,128)(2,1)} %get-tuple-element.188.refs_1_, bf16[4096,384]{1,0:T(8,128)(2,1)} %get-tuple-element.192.refs_2_.refs_7_.refs_4_, ...), custom_call_target="tpu_custom_call" | custom-call | flops 3750000128 | bytes 11250000 | tf_op jit(solution)/shard_map/attend/pallas_call | solution.py:51
  236.3 8.5 ffn.4
  244.8 6.9 collective-permute-done.20.refs_1_
  260.4 8.5 ffn.5
  268.9 6.2 collective-permute-done.22.refs_1_
  284.1 8.5 ffn.6
  292.5 5.5 collective-permute-done.24.refs_1_
  307.0 8.5 ffn.7
  329.5 9.6 %ffn_back.4 = (bf16[256,1536]{1,0:T(8,128)(2,1)}, f32[1,1536]{1,0:T(1,128)}, bf16[1024,1536]{1,0:T(8,128)(2,1)}, bf16[1024,1536]{1,0:T(8,128)(2,1)}, bf16[1024,2048]{1,0:T(8,128)(2,1)}) custom-call(bf16[256,1536]{1,0:T(8,128)(2,1)} %get-tuple-element.230.refs_0_.refs_7_, f32[256,1536]{1,0:T(8,128)} %get-tuple-element.206.refs_7_.refs_1_, ...), custom_call_target="tpu_custom_call" | custom-call | flops 2500000000 | bytes 7500000 | tf_op jit(solution)/shard_map/ffn_back/pallas_call | solution.py:51
  350.2 9.5 %ffn_back.5 = (bf16[256,1536]{1,0:T(8,128)(2,1)}, f32[1,1536]{1,0:T(1,128)}, bf16[1024,1536]{1,0:T(8,128)(2,1)}, bf16[1024,1536]{1,0:T(8,128)(2,1)}, bf16[1024,2048]{1,0:T(8,128)(2,1)}) custom-call(bf16[256,1536]{1,0:T(8,128)(2,1)} %get-tuple-element.235.refs_0_.refs_7_, ...), custom_call_target="tpu_custom_call", output_to_operand_aliasing={{2}: (8, {}), {3}: (9, {}), {4}: (10, {})} | custom-call | flops 2500000000 | bytes 7500000 | tf_op jit(solution)/shard_map/ffn_back/pallas_call | solution.py:51
  370.5 9.6 %ffn_back.6 = (bf16[256,1536]{1,0:T(8,128)(2,1)}, f32[1,1536]{1,0:T(1,128)}, bf16[1024,1536]{1,0:T(8,128)(2,1)}, bf16[1024,1536]{1,0:T(8,128)(2,1)}, bf16[1024,2048]{1,0:T(8,128)(2,1)}) custom-call(bf16[256,1536]{1,0:T(8,128)(2,1)} %get-tuple-element.243.refs_0_.refs_7_, ...), custom_call_target="tpu_custom_call", output_to_operand_aliasing={{2}: (8, {}), {3}: (9, {}), {4}: (10, {})} | custom-call | flops 2500000000 | bytes 7500000 | tf_op jit(solution)/shard_map/ffn_back/pallas_call | solution.py:51
  390.0 9.6 %ffn_back.7 = (bf16[256,1536]{1,0:T(8,128)(2,1)}, f32[1,1536]{1,0:T(1,128)}, bf16[1024,1536]{1,0:T(8,128)(2,1)}, bf16[1024,1536]{1,0:T(8,128)(2,1)}, bf16[1024,2048]{1,0:T(8,128)(2,1)}) custom-call(bf16[256,1536]{1,0:T(8,128)(2,1)} %get-tuple-element.249.refs_0_.refs_7_, ...), custom_call_target="tpu_custom_call", output_to_operand_aliasing={{2}: (8, {}), {3}: (9, {}), {4}: (10, {})} | custom-call | flops 2500000000 | bytes 7500000 | tf_op jit(solution)/shard_map/ffn_back/pallas_call | solution.py:51
  408.2 5.6 out_back.4
  413.9 9.9 %pair_grad.3.refs_6_.refs_7_ = bf16[1536,3072]{1,0:T(8,128)(2,1)} custom-call(bf16[1024,1536]{1,0:T(8,128)(2,1)} %get-tuple-element.264.refs_0_, bf16[1024,2048]{1,0:T(8,128)(2,1)} %get-tuple-element.265.refs_1_, bf16[1024,1536]{1,0:T(8,128)(2,1)} %get-tuple-element.266.refs_2_, bf16[1024,1024]{1,0:T(8,128)(2,1)} %get-tuple-element.267.refs_3_, ...), custom_call_target="tpu_custom_call" | custom-call | flops 2500000000 | bytes 7500000 | tf_op jit(solution)/shard_map/pair_grad/pallas_call | solution.py:51
  432.4 5.6 out_back.5
  439.3 6.2 caption_back.2
  452.8 22.2 %collective-permute-start.43 = (bf16[512,512]{1,0:T(8,128)(2,1)S(1)}, bf16[512,512]{1,0:T(8,128)(2,1)}, u32[]{:S(2)}, u32[]{:S(2)}) collective-permute-start(bf16[512,512]{1,0:T(8,128)(2,1)S(1)} %collective-permute-done.41.refs_5_.refs_3_), channel_id=1, source_target_pairs={{0,16},{4,20},{24,8},{28,12},{1,17},{5,21},{25,9},{29,13},{2,18},{... | collective-permute-start | bytes 1572872 | tf_op jit(solution)/shard_map/ppermute | solution.py:741
  475.0 5.6 out_back.6
  481.5 9.9 %pair_grad.4.refs_3_.refs_1_ = bf16[1536,3072]{1,0:T(8,128)(2,1)} custom-call(bf16[1024,1536]{1,0:T(8,128)(2,1)} %get-tuple-element.264.refs_0_, bf16[1024,2048]{1,0:T(8,128)(2,1)} %get-tuple-element.265.refs_1_, bf16[1024,1536]{1,0:T(8,128)(2,1)} %get-tuple-element.266.refs_2_, ...), custom_call_target="tpu_custom_call", output_to_operand_aliasing={{}: (7, {})} | custom-call | flops 2500000000 | bytes 7500000 | tf_op jit(solution)/shard_map/pair_grad/pallas_call | solution.py:51
  494.4 5.6 out_back.7
  500.0 6.4 caption_back.3
  514.8 26.8 %dq.2.refs_7_.refs_0_ = f32[512,384]{1,0:T(8,128)} custom-call(s32[9]{0:T(128)} %pad_add_fusion.refs_0_, bf16[1024,384]{1,0:T(8,128)(2,1)} %get-tuple-element.188.refs_1_, bf16[512,512]{1,0:T(8,128)(2,1)} %get-tuple-element.287.refs_2_.refs_3_.refs_1_, bf16[512,512]{1,0:T(8,128)(2,1)} %get-tuple-element.287.refs_2_.refs_3_.refs_1_, ...), custom_call_target="tpu_custom_call" | custom-call | flops 6750000128 | bytes 20250000 | tf_op jit(solution)/shard_map/dq/pallas_call | solution.py:51
  544.3 26.8 %dq.3.refs_4_.refs_0_ = f32[512,384]{1,0:T(8,128)} custom-call(s32[9]{0:T(128)} %pad_add_fusion.refs_0_, bf16[1024,384]{1,0:T(8,128)(2,1)} %get-tuple-element.188.refs_1_, bf16[512,512]{1,0:T(8,128)(2,1)} %get-tuple-element.297.refs_2_.refs_3_.refs_1_, bf16[512,512]{1,0:T(8,128)(2,1)} %get-tuple-element.297.refs_2_.refs_3_.refs_1_, ...), custom_call_target="tpu_custom_call" | custom-call | flops 6750000128 | bytes 20250000 | tf_op jit(solution)/shard_map/dq/pallas_call | solution.py:51
  600.7 6.2 collective-permute-done.46.refs_1_
  613.0 32.5 %dkv.4 = (f32[512,384]{1,0:T(8,128)}, f32[512,384]{1,0:T(8,128)}) custom-call(s32[9]{0:T(128)} %pad_add_fusion.refs_0_, bf16[1024,384]{1,0:T(8,128)(2,1)} %get-tuple-element.189.refs_1_, bf16[1024,384]{1,0:T(8,128)(2,1)} %get-tuple-element.190.refs_9_.refs_2_, bf16[8192,384]{1,0:T(8,128)(2,1)} %all-gather.9.cloned.1.call-done.refs_3_, ...), custom_call_target="tpu_custom_call" | custom-call | flops 6000000000 | bytes 18000000 | tf_op jit(solution)/shard_map/dkv/pallas_call | solution.py:51
  657.7 6.6 dqkv.4
  664.3 12.6 %dkv.5 = (f32[512,128]{1,0:T(8,128)}, f32[512,128]{1,0:T(8,128)}) custom-call(s32[9]{0:T(128)} %pad_add_fusion.refs_0_, bf16[1024,384]{1,0:T(8,128)(2,1)} %get-tuple-element.189.refs_1_, bf16[1024,384]{1,0:T(8,128)(2,1)} %get-tuple-element.190.refs_9_.refs_2_, bf16[8192,384]{1,0:T(8,128)(2,1)} %all-gather.9.cloned.1.call-done.refs_3_, ...), custom_call_target="tpu_custom_call" | custom-call | flops 6000000000 | bytes 18000000 | tf_op jit(solution)/shard_map/dkv/pallas_call | solution.py:51
  682.9 6.6 dqkv.5
  689.6 12.5 %dkv.6 = (f32[512,128]{1,0:T(8,128)}, f32[512,128]{1,0:T(8,128)}) custom-call(s32[9]{0:T(128)} %pad_add_fusion.refs_0_, bf16[1024,384]{1,0:T(8,128)(2,1)} %get-tuple-element.189.refs_1_, bf16[1024,384]{1,0:T(8,128)(2,1)} %get-tuple-element.190.refs_9_.refs_2_, bf16[8192,384]{1,0:T(8,128)(2,1)} %all-gather.9.cloned.1.call-done.refs_3_, ...), custom_call_target="tpu_custom_call" | custom-call | flops 6000000000 | bytes 18000000 | tf_op jit(solution)/shard_map/dkv/pallas_call | solution.py:51
  712.8 12.6 %dkv.7 = (f32[512,128]{1,0:T(8,128)}, f32[512,128]{1,0:T(8,128)}) custom-call(s32[9]{0:T(128)} %pad_add_fusion.refs_0_, bf16[1024,384]{1,0:T(8,128)(2,1)} %get-tuple-element.189.refs_1_, bf16[1024,384]{1,0:T(8,128)(2,1)} %get-tuple-element.190.refs_9_.refs_2_, bf16[8192,384]{1,0:T(8,128)(2,1)} %all-gather.9.cloned.1.call-done.refs_3_, ...), custom_call_target="tpu_custom_call" | custom-call | flops 6000000000 | bytes 18000000 | tf_op jit(solution)/shard_map/dkv/pallas_call | solution.py:51
  725.4 6.7 dqkv.6
  741.6 6.7 dqkv.7
  754.2 10.9 %pair_grad.5.refs_7_.refs_1_ = bf16[1536,1536]{1,0:T(8,128)(2,1)} custom-call(bf16[1024,1536]{1,0:T(8,128)(2,1)} %get-tuple-element.191.refs_17_.refs_0_, bf16[1024,1152]{1,0:T(8,128)(2,1)} %get-tuple-element.330.refs_1_, bf16[1024,1536]{1,0:T(8,128)(2,1)} %get-tuple-element.331.refs_2_, bf16[1024,384]{1,0:T(8,128)(2,1)} %pad_maximum_fusion.2.refs_3_, ...), custom_call_target="tpu_custom_call" | custom-call | flops 2500000000 | bytes 7500000 | tf_op jit(solution)/shard_map/pair_grad/pallas_call | solution.py:51
  785.6 11.5 %all-gather = f32[64,1536]{1,0:T(8,128)} all-gather(f32[8,1536]{1,0:T(8,128)S(1)} %copy-done.74), channel_id=2, replica_groups=mesh['wide'=8,'narrow'=4] {'wide'}, dimensions={0}, use_global_device_ids=true | all-gather | bytes 442368 | tf_op jit(solution)/shard_map/all_gather | solution.py:1149
  821.4 5.4 collective-permute-done.71.refs_1_
  843.8 7.9 collective-permute-done.73.refs_1_
  (493 shorter events, 336.9 us)
Async XLA Ops:
  7.2 134.4 %all-gather.5.cloned.1.call-start = ((), (), s32[]{:S(2)}) async-start(), calls=%async_computation.3 | async-start | bytes 3538944 | tf_op jit(solution)/shard_map/all_gather | solution.py:1025
  16.6 554.4 %all-gather.7.cloned.1.call-start = ((), (), s32[]{:S(2)}) async-start(), calls=%async_computation.4 | async-start | bytes 3538944 | tf_op jit(solution)/shard_map/all_gather | solution.py:1084
  71.3 20.7 %collective-permute-start.8 = (bf16[1024,384]{1,0:T(8,128)(2,1)}, bf16[1024,384]{1,0:T(8,128)(2,1)}, u32[]{:S(2)}, u32[]{:S(2)}) collective-permute-start(bf16[1024,384]{1,0:T(8,128)(2,1)} %get-tuple-element.190.refs_9_.refs_2_), channel_id=1, source_target_pairs={{0,8},{4,12},{8,0},{12,4},{16,24},{20,28},{24,16},{28,20},{1,9},{5... | collective-permute-start | bytes 2359304 | tf_op jit(solution)/shard_map/ppermute | solution.py:718
  72.6 22.9 %collective-permute-start.10 = (bf16[1024,384]{1,0:T(8,128)(2,1)}, bf16[1024,384]{1,0:T(8,128)(2,1)S(1)}, u32[]{:S(2)}, u32[]{:S(2)}) collective-permute-start(bf16[1024,384]{1,0:T(8,128)(2,1)} %get-tuple-element.190.refs_9_.refs_2_), channel_id=1, source_target_pairs={{4,20},{16,0},{12,28},{24,8},{5,21},{17,1},{13,29},{25,9},{6,22},{... | collective-permute-start | bytes 2359304 | tf_op jit(solution)/shard_map/ppermute | solution.py:718
  73.9 34.4 %collective-permute-start.1 = (bf16[1024,384]{1,0:T(8,128)(2,1)}, bf16[1024,384]{1,0:T(8,128)(2,1)}, u32[]{:S(2)}, u32[]{:S(2)}) collective-permute-start(bf16[1024,384]{1,0:T(8,128)(2,1)} %get-tuple-element.189.refs_1_), channel_id=1, source_target_pairs={{0,8},{4,12},{8,0},{12,4},{16,24},{20,28},{24,16},{28,20},{1,9},{5... | collective-permute-start | bytes 2359304 | tf_op jit(solution)/shard_map/ppermute | solution.py:718
  92.0 21.6 %collective-permute-start.12 = (bf16[1024,384]{1,0:T(8,128)(2,1)}, bf16[1024,384]{1,0:T(8,128)(2,1)S(1)}, u32[]{:S(2)}, u32[]{:S(2)}) collective-permute-start(bf16[1024,384]{1,0:T(8,128)(2,1)} %collective-permute-done.8.refs_11_), channel_id=1, source_target_pairs={{0,16},{28,12},{1,17},{29,13},{2,18},{30,14},{3,19},{31,15}} | collective-permute-start | bytes 2359304 | tf_op jit(solution)/shard_map/ppermute | solution.py:718
  95.5 23.4 %collective-permute-start.13 = (bf16[1024,384]{1,0:T(8,128)(2,1)S(1)}, bf16[1024,384]{1,0:T(8,128)(2,1)S(1)}, u32[]{:S(2)}, u32[]{:S(2)}) collective-permute-start(bf16[1024,384]{1,0:T(8,128)(2,1)S(1)} %collective-permute-done.10.refs_13_), channel_id=1, source_target_pairs={{28,20},{0,8},{29,21},{1,9},{30,22},{2,10},{31,23},{3,11}} | collective-permute-start | bytes 2359304 | tf_op jit(solution)/shard_map/ppermute | solution.py:718
  96.8 22.4 %collective-permute-start.3 = (bf16[1024,384]{1,0:T(8,128)(2,1)}, bf16[1024,384]{1,0:T(8,128)(2,1)}, u32[]{:S(2)}, u32[]{:S(2)}) collective-permute-start(bf16[1024,384]{1,0:T(8,128)(2,1)} %get-tuple-element.189.refs_1_), channel_id=1, source_target_pairs={{4,20},{16,0},{12,28},{24,8},{5,21},{17,1},{13,29},{25,9},{6,22},{... | collective-permute-start | bytes 2359304 | tf_op jit(solution)/shard_map/ppermute | solution.py:718
  98.1 21.7 %collective-permute-start = (bf16[1024,384]{1,0:T(8,128)(2,1)}, bf16[1024,384]{1,0:T(8,128)(2,1)S(1)}, u32[]{:S(2)}, u32[]{:S(2)}) collective-permute-start(bf16[1024,384]{1,0:T(8,128)(2,1)} %get-tuple-element.189.refs_1_), channel_id=1, source_target_pairs={{0,4},{4,0},{8,12},{12,8},{16,20},{20,16},{24,28},{28,24},{1,5},{5... | collective-permute-start | bytes 2359304 | tf_op jit(solution)/shard_map/ppermute | solution.py:689
  158.9 20.3 %collective-permute-start.15 = (bf16[256,1536]{1,0:T(8,128)(2,1)}, bf16[256,1536]{1,0:T(8,128)(2,1)}, u32[]{:S(2)}, u32[]{:S(2)}) collective-permute-start(bf16[256,1536]{1,0:T(8,128)(2,1)} %convolution_convert_fusion.4.refs_2_), channel_id=1, source_target_pairs={{0,1},{3,2},{1,0},{2,3},{4,5},{7,6},{5,4},{6,7},{8,9},{11,10},{9,8... | collective-permute-start | bytes 2359304 | tf_op jit(solution)/shard_map/ppermute | solution.py:867
  181.7 19.4 %collective-permute-start.16 = (bf16[256,1536]{1,0:T(8,128)(2,1)}, bf16[256,1536]{1,0:T(8,128)(2,1)S(1)}, u32[]{:S(2)}, u32[]{:S(2)}) collective-permute-start(bf16[256,1536]{1,0:T(8,128)(2,1)} %get-tuple-element.196), channel_id=1, source_target_pairs={{0,1},{3,2},{1,0},{2,3},{4,5},{7,6},{5,4},{6,7},{8,9},{11,10},{9,8... | collective-permute-start | bytes 2359304 | tf_op jit(solution)/shard_map/ppermute | solution.py:867
  205.9 22.0 %collective-permute-start.18 = (bf16[256,1536]{1,0:T(8,128)(2,1)}, bf16[256,1536]{1,0:T(8,128)(2,1)S(1)}, u32[]{:S(2)}, u32[]{:S(2)}) collective-permute-start(bf16[256,1536]{1,0:T(8,128)(2,1)} %get-tuple-element.199.refs_2_), channel_id=1, source_target_pairs={{0,1},{3,2},{1,0},{2,3},{4,5},{7,6},{5,4},{6,7},{8,9},{11,10},{9,8... | collective-permute-start | bytes 2359304 | tf_op jit(solution)/shard_map/ppermute | solution.py:867
  233.2 18.5 %collective-permute-start.20 = (bf16[256,1536]{1,0:T(8,128)(2,1)}, bf16[256,1536]{1,0:T(8,128)(2,1)S(1)}, u32[]{:S(2)}, u32[]{:S(2)}) collective-permute-start(bf16[256,1536]{1,0:T(8,128)(2,1)} %get-tuple-element.202.refs_2_), channel_id=1, source_target_pairs={{0,1},{3,2},{1,0},{2,3},{4,5},{7,6},{5,4},{6,7},{8,9},{11,10},{9,8... | collective-permute-start | bytes 2359304 | tf_op jit(solution)/shard_map/ppermute | solution.py:867
  256.4 18.7 %collective-permute-start.22 = (bf16[256,1536]{1,0:T(8,128)(2,1)}, bf16[256,1536]{1,0:T(8,128)(2,1)S(1)}, u32[]{:S(2)}, u32[]{:S(2)}) collective-permute-start(bf16[256,1536]{1,0:T(8,128)(2,1)} %get-tuple-element.207.refs_2_), channel_id=1, source_target_pairs={{0,1},{3,2},{1,0},{2,3},{4,5},{7,6},{5,4},{6,7},{8,9},{11,10},{9,8... | collective-permute-start | bytes 2359304 | tf_op jit(solution)/shard_map/ppermute | solution.py:867
  404.2 19.5 %collective-permute-start.36 = (bf16[256,1536]{1,0:T(8,128)(2,1)}, bf16[256,1536]{1,0:T(8,128)(2,1)S(1)}, u32[]{:S(2)}, u32[]{:S(2)}) collective-permute-start(bf16[256,1536]{1,0:T(8,128)(2,1)} %get-tuple-element.262.refs_2_), channel_id=1, source_target_pairs={{0,1},{3,2},{1,0},{2,3},{4,5},{7,6},{5,4},{6,7},{8,9},{11,10},{9,8... | collective-permute-start | bytes 2359304 | tf_op jit(solution)/shard_map/ppermute | solution.py:867
  449.5 41.9 %collective-permute-start.40 = (bf16[256,1536]{1,0:T(8,128)(2,1)}, bf16[256,1536]{1,0:T(8,128)(2,1)S(1)}, u32[]{:S(2)}, u32[]{:S(2)}) collective-permute-start(bf16[256,1536]{1,0:T(8,128)(2,1)} %get-tuple-element.285.refs_2_), channel_id=1, source_target_pairs={{0,1},{3,2},{1,0},{2,3},{4,5},{7,6},{5,4},{6,7},{8,9},{11,10},{9,8... | collective-permute-start | bytes 2359304 | tf_op jit(solution)/shard_map/ppermute | solution.py:867
  451.5 29.2 %collective-permute-start.42 = (bf16[512,512]{1,0:T(8,128)(2,1)S(1)}, bf16[512,512]{1,0:T(8,128)(2,1)S(1)}, u32[]{:S(2)}, u32[]{:S(2)}) collective-permute-start(bf16[512,512]{1,0:T(8,128)(2,1)S(1)} %copy-done.17), channel_id=1, source_target_pairs={{4,20},{16,0},{12,28},{24,8},{5,21},{17,1},{13,29},{25,9},{6,22},{... | collective-permute-start | bytes 1572872 | tf_op jit(solution)/shard_map/ppermute | solution.py:741
  452.8 38.5 %collective-permute-start.43 = (bf16[512,512]{1,0:T(8,128)(2,1)S(1)}, bf16[512,512]{1,0:T(8,128)(2,1)}, u32[]{:S(2)}, u32[]{:S(2)}) collective-permute-start(bf16[512,512]{1,0:T(8,128)(2,1)S(1)} %collective-permute-done.41.refs_5_.refs_3_), channel_id=1, source_target_pairs={{0,16},{4,20},{24,8},{28,12},{1,17},{5,21},{25,9},{29,13},{2,18},{... | collective-permute-start | bytes 1572872 | tf_op jit(solution)/shard_map/ppermute | solution.py:741
  509.4 103.7 %all-gather.9.cloned.1.call-start = ((), (), s32[]{:S(2)}) async-start(), calls=%async_computation.5 | async-start | bytes 7077888 | tf_op jit(solution)/shard_map/all_gather | solution.py:1034
  510.1 255.1 %reduce-scatter.4.cloned.1.call-start = ((), (), s32[]{:S(2)}) async-start(), calls=%async_computation.6 | async-start | bytes 10616832 | tf_op jit(solution)/shard_map/reduce_scatter | solution.py:929
  510.2 74.4 %collective-permute-start.52 = (bf16[512,512]{1,0:T(8,128)(2,1)}, bf16[512,512]{1,0:T(8,128)(2,1)}, u32[]{:S(2)}, u32[]{:S(2)}) collective-permute-start(bf16[512,512]{1,0:T(8,128)(2,1)} %get-tuple-element.287.refs_2_.refs_3_.refs_1_), channel_id=1, source_target_pairs={{0,4},{4,0},{8,12},{12,8},{16,20},{20,16},{24,28},{28,24},{1,5},{5... | collective-permute-start | bytes 1572872 | tf_op jit(solution)/shard_map/ppermute | solution.py:689
  510.3 74.8 %collective-permute-start.53 = (bf16[512,512]{1,0:T(8,128)(2,1)S(1)}, bf16[512,512]{1,0:T(8,128)(2,1)}, u32[]{:S(2)}, u32[]{:S(2)}) collective-permute-start(bf16[512,512]{1,0:T(8,128)(2,1)S(1)} %copy-done.13), channel_id=1, source_target_pairs={{0,4},{4,0},{8,12},{12,8},{16,20},{20,16},{24,28},{28,24},{1,5},{5... | collective-permute-start | bytes 1572872 | tf_op jit(solution)/shard_map/ppermute | solution.py:689
  510.7 74.4 %collective-permute-start.54 = (bf16[512,512]{1,0:T(8,128)(2,1)S(1)}, bf16[512,512]{1,0:T(8,128)(2,1)}, u32[]{:S(2)}, u32[]{:S(2)}) collective-permute-start(bf16[512,512]{1,0:T(8,128)(2,1)S(1)} %copy-done.15), channel_id=1, source_target_pairs={{0,4},{4,0},{8,12},{12,8},{16,20},{20,16},{24,28},{28,24},{1,5},{5... | collective-permute-start | bytes 1572872 | tf_op jit(solution)/shard_map/ppermute | solution.py:689
  510.8 30.7 %collective-permute-start.44 = (bf16[512,512]{1,0:T(8,128)(2,1)}, bf16[512,512]{1,0:T(8,128)(2,1)}, u32[]{:S(2)}, u32[]{:S(2)}) collective-permute-start(bf16[512,512]{1,0:T(8,128)(2,1)} %get-tuple-element.297.refs_2_.refs_3_.refs_1_), channel_id=1, source_target_pairs={{0,8},{4,12},{8,0},{12,4},{16,24},{20,28},{24,16},{28,20},{1,9},{5... | collective-permute-start | bytes 1572872 | tf_op jit(solution)/shard_map/ppermute | solution.py:741
  513.5 28.3 %collective-permute-start.45 = (bf16[512,512]{1,0:T(8,128)(2,1)}, bf16[512,512]{1,0:T(8,128)(2,1)S(1)}, u32[]{:S(2)}, u32[]{:S(2)}) collective-permute-start(bf16[512,512]{1,0:T(8,128)(2,1)} %get-tuple-element.297.refs_2_.refs_3_.refs_1_), channel_id=1, source_target_pairs={{4,20},{16,0},{12,28},{24,8},{5,21},{17,1},{13,29},{25,9},{6,22},{... | collective-permute-start | bytes 1572872 | tf_op jit(solution)/shard_map/ppermute | solution.py:741
  541.6 45.5 %collective-permute-start.55 = (bf16[512,512]{1,0:T(8,128)(2,1)}, bf16[512,512]{1,0:T(8,128)(2,1)}, u32[]{:S(2)}, u32[]{:S(2)}) collective-permute-start(bf16[512,512]{1,0:T(8,128)(2,1)} %collective-permute-done.43.refs_4_.refs_7_), channel_id=1, source_target_pairs={{0,4},{4,0},{8,12},{12,8},{16,20},{20,16},{24,28},{28,24},{1,5},{5... | collective-permute-start | bytes 1572872 | tf_op jit(solution)/shard_map/ppermute | solution.py:689
  541.8 43.8 %collective-permute-start.50 = (bf16[512,512]{1,0:T(8,128)(2,1)}, bf16[512,512]{1,0:T(8,128)(2,1)}, u32[]{:S(2)}, u32[]{:S(2)}) collective-permute-start(bf16[512,512]{1,0:T(8,128)(2,1)} %collective-permute-done.44.refs_8_.refs_3_), channel_id=1, source_target_pairs={{0,16},{4,20},{24,8},{28,12},{1,17},{5,21},{25,9},{29,13},{2,18},{... | collective-permute-start | bytes 1572872 | tf_op jit(solution)/shard_map/ppermute | solution.py:741
  587.0 19.8 %collective-permute-start.46 = (bf16[256,1536]{1,0:T(8,128)(2,1)S(1)}, bf16[256,1536]{1,0:T(8,128)(2,1)S(1)}, u32[]{:S(2)}, u32[]{:S(2)}) collective-permute-start(bf16[256,1536]{1,0:T(8,128)(2,1)S(1)} %get-tuple-element.422.refs_2_), channel_id=1, source_target_pairs={{0,1},{3,2},{1,0},{2,3},{4,5},{7,6},{5,4},{6,7},{8,9},{11,10},{9,8... | collective-permute-start | bytes 2359304 | tf_op jit(solution)/shard_map/ppermute | solution.py:867
  610.4 165.1 %reduce-scatter.6.cloned.1.call-start = ((), (), s32[]{:S(2)}) async-start(), calls=%async_computation.7 | async-start | bytes 7077888 | tf_op jit(solution)/shard_map/reduce_scatter | solution.py:929
  610.4 35.1 %collective-permute-start.56 = (bf16[256,1536]{1,0:T(8,128)(2,1)}, bf16[256,1536]{1,0:T(8,128)(2,1)}, u32[]{:S(2)}, u32[]{:S(2)}) collective-permute-start(bf16[256,1536]{1,0:T(8,128)(2,1)} %get-tuple-element.300), channel_id=1, source_target_pairs={{0,1},{3,2},{1,0},{2,3},{4,5},{7,6},{5,4},{6,7},{8,9},{11,10},{9,8... | collective-permute-start | bytes 2359304 | tf_op jit(solution)/shard_map/ppermute | solution.py:867
  611.5 34.0 %collective-permute-start.57 = (bf16[256,1536]{1,0:T(8,128)(2,1)S(1)}, bf16[256,1536]{1,0:T(8,128)(2,1)}, u32[]{:S(2)}, u32[]{:S(2)}) collective-permute-start(bf16[256,1536]{1,0:T(8,128)(2,1)S(1)} %copy-done.6), channel_id=1, source_target_pairs={{1,2},{2,1},{5,6},{6,5},{9,10},{10,9},{13,14},{14,13},{17,18},{18,... | collective-permute-start | bytes 2359304 | tf_op jit(solution)/shard_map/ppermute | solution.py:867
  648.9 202.9 %reduce-scatter.8.cloned.1.call-start = ((), (), s32[]{:S(2)}) async-start(), calls=%async_computation.8 | async-start | bytes 5308416 | tf_op jit(solution)/shard_map/reduce_scatter | solution.py:929
  650.1 26.8 %collective-permute-start.59 = (bf16[256,1536]{1,0:T(8,128)(2,1)S(1)}, bf16[256,1536]{1,0:T(8,128)(2,1)S(1)}, u32[]{:S(2)}, u32[]{:S(2)}) collective-permute-start(bf16[256,1536]{1,0:T(8,128)(2,1)S(1)} %copy-done.9), channel_id=1, source_target_pairs={{1,2},{2,1},{5,6},{6,5},{9,10},{10,9},{13,14},{14,13},{17,18},{18,... | collective-permute-start | bytes 2359304 | tf_op jit(solution)/shard_map/ppermute | solution.py:867
  650.9 25.9 %collective-permute-start.58 = (bf16[256,1536]{1,0:T(8,128)(2,1)}, bf16[256,1536]{1,0:T(8,128)(2,1)S(1)}, u32[]{:S(2)}, u32[]{:S(2)}) collective-permute-start(bf16[256,1536]{1,0:T(8,128)(2,1)} %get-tuple-element.303.refs_2_), channel_id=1, source_target_pairs={{0,1},{3,2},{1,0},{2,3},{4,5},{7,6},{5,4},{6,7},{8,9},{11,10},{9,8... | collective-permute-start | bytes 2359304 | tf_op jit(solution)/shard_map/ppermute | solution.py:867
  681.6 20.6 %collective-permute-start.60 = (bf16[256,1536]{1,0:T(8,128)(2,1)}, bf16[256,1536]{1,0:T(8,128)(2,1)S(1)}, u32[]{:S(2)}, u32[]{:S(2)}) collective-permute-start(bf16[256,1536]{1,0:T(8,128)(2,1)} %get-tuple-element.310.refs_2_), channel_id=1, source_target_pairs={{0,1},{3,2},{1,0},{2,3},{4,5},{7,6},{5,4},{6,7},{8,9},{11,10},{9,8... | collective-permute-start | bytes 2359304 | tf_op jit(solution)/shard_map/ppermute | solution.py:867
  681.6 20.6 %collective-permute-start.61 = (bf16[256,1536]{1,0:T(8,128)(2,1)}, bf16[256,1536]{1,0:T(8,128)(2,1)S(1)}, u32[]{:S(2)}, u32[]{:S(2)}) collective-permute-start(bf16[256,1536]{1,0:T(8,128)(2,1)} %get-tuple-element.311.refs_4_), channel_id=1, source_target_pairs={{1,2},{2,1},{5,6},{6,5},{9,10},{10,9},{13,14},{14,13},{17,18},{18,... | collective-permute-start | bytes 2359304 | tf_op jit(solution)/shard_map/ppermute | solution.py:867
  706.8 25.3 %collective-permute-start.62 = (bf16[256,1536]{1,0:T(8,128)(2,1)}, bf16[256,1536]{1,0:T(8,128)(2,1)S(1)}, u32[]{:S(2)}, u32[]{:S(2)}) collective-permute-start(bf16[256,1536]{1,0:T(8,128)(2,1)} %get-tuple-element.316.refs_2_), channel_id=1, source_target_pairs={{0,1},{3,2},{1,0},{2,3},{4,5},{7,6},{5,4},{6,7},{8,9},{11,10},{9,8... | collective-permute-start | bytes 2359304 | tf_op jit(solution)/shard_map/ppermute | solution.py:867
  710.6 21.5 %collective-permute-start.63 = (bf16[256,1536]{1,0:T(8,128)(2,1)}, bf16[256,1536]{1,0:T(8,128)(2,1)S(1)}, u32[]{:S(2)}, u32[]{:S(2)}) collective-permute-start(bf16[256,1536]{1,0:T(8,128)(2,1)} %get-tuple-element.317.refs_4_), channel_id=1, source_target_pairs={{1,2},{2,1},{5,6},{6,5},{9,10},{10,9},{13,14},{14,13},{17,18},{18,... | collective-permute-start | bytes 2359304 | tf_op jit(solution)/shard_map/ppermute | solution.py:867
  736.7 28.4 %collective-permute-start.64 = (bf16[256,1536]{1,0:T(8,128)(2,1)}, bf16[256,1536]{1,0:T(8,128)(2,1)S(1)}, u32[]{:S(2)}, u32[]{:S(2)}) collective-permute-start(bf16[256,1536]{1,0:T(8,128)(2,1)} %get-tuple-element.325.refs_2_), channel_id=1, source_target_pairs={{0,1},{3,2},{1,0},{2,3},{4,5},{7,6},{5,4},{6,7},{8,9},{11,10},{9,8... | collective-permute-start | bytes 2359304 | tf_op jit(solution)/shard_map/ppermute | solution.py:867
  739.4 25.7 %collective-permute-start.65 = (bf16[256,1536]{1,0:T(8,128)(2,1)}, bf16[256,1536]{1,0:T(8,128)(2,1)}, u32[]{:S(2)}, u32[]{:S(2)}) collective-permute-start(bf16[256,1536]{1,0:T(8,128)(2,1)} %get-tuple-element.326.refs_4_), channel_id=1, source_target_pairs={{1,2},{2,1},{5,6},{6,5},{9,10},{10,9},{13,14},{14,13},{17,18},{18,... | collective-permute-start | bytes 2359304 | tf_op jit(solution)/shard_map/ppermute | solution.py:867
  778.2 19.8 %collective-permute-start.69 = (bf16[256,1536]{1,0:T(8,128)(2,1)S(1)}, bf16[256,1536]{1,0:T(8,128)(2,1)S(1)}, u32[]{:S(2)}, u32[]{:S(2)}) collective-permute-start(bf16[256,1536]{1,0:T(8,128)(2,1)S(1)} %copy-done.28), channel_id=1, source_target_pairs={{0,1},{3,2},{1,0},{2,3},{4,5},{7,6},{5,4},{6,7},{8,9},{11,10},{9,8... | collective-permute-start | bytes 2359304 | tf_op jit(solution)/shard_map/ppermute | solution.py:867
  778.4 19.6 %collective-permute-start.70 = (bf16[256,1536]{1,0:T(8,128)(2,1)S(1)}, bf16[256,1536]{1,0:T(8,128)(2,1)S(1)}, u32[]{:S(2)}, u32[]{:S(2)}) collective-permute-start(bf16[256,1536]{1,0:T(8,128)(2,1)S(1)} %copy-done.27), channel_id=1, source_target_pairs={{1,2},{2,1},{5,6},{6,5},{9,10},{10,9},{13,14},{14,13},{17,18},{18,... | collective-permute-start | bytes 2359304 | tf_op jit(solution)/shard_map/ppermute | solution.py:867
  804.9 21.8 %collective-permute-start.71 = (bf16[256,1536]{1,0:T(8,128)(2,1)}, bf16[256,1536]{1,0:T(8,128)(2,1)S(1)}, u32[]{:S(2)}, u32[]{:S(2)}) collective-permute-start(bf16[256,1536]{1,0:T(8,128)(2,1)} %get-tuple-element.358.refs_2_), channel_id=1, source_target_pairs={{0,1},{3,2},{1,0},{2,3},{4,5},{7,6},{5,4},{6,7},{8,9},{11,10},{9,8... | collective-permute-start | bytes 2359304 | tf_op jit(solution)/shard_map/ppermute | solution.py:867
  808.3 18.4 %collective-permute-start.72 = (bf16[256,1536]{1,0:T(8,128)(2,1)}, bf16[256,1536]{1,0:T(8,128)(2,1)S(1)}, u32[]{:S(2)}, u32[]{:S(2)}) collective-permute-start(bf16[256,1536]{1,0:T(8,128)(2,1)} %get-tuple-element.359.refs_4_), channel_id=1, source_target_pairs={{1,2},{2,1},{5,6},{6,5},{9,10},{10,9},{13,14},{14,13},{17,18},{18,... | collective-permute-start | bytes 2359304 | tf_op jit(solution)/shard_map/ppermute | solution.py:867
  812.1 27.6 %collective-permute-start.74 = (f32[8,128]{1,0:T(8,128)S(1)}, f32[8,128]{1,0:T(8,128)S(1)}, u32[]{:S(2)}, u32[]{:S(2)}) collective-permute-start(f32[8,128]{1,0:T(8,128)S(1)} %bitcast.94), channel_id=1, source_target_pairs={{0,1},{1,0},{2,3},{3,2},{4,5},{5,4},{6,7},{7,6},{8,9},{9,8},{10,11... | collective-permute-start | bytes 12296 | tf_op jit(solution)/shard_map/ppermute | solution.py:689
  814.9 24.8 %collective-permute-start.75 = (f32[8,128]{1,0:T(8,128)S(1)}, f32[8,128]{1,0:T(8,128)S(1)}, u32[]{:S(2)}, u32[]{:S(2)}) collective-permute-start(f32[8,128]{1,0:T(8,128)S(1)} %bitcast.95), channel_id=1, source_target_pairs={{0,2},{1,3},{2,0},{3,1},{4,6},{5,7},{6,4},{7,5},{8,10},{9,11},{10,... | collective-permute-start | bytes 12296 | tf_op jit(solution)/shard_map/ppermute | solution.py:689
  815.1 24.6 %collective-permute-start.76 = (f32[8,128]{1,0:T(8,128)S(1)}, f32[8,128]{1,0:T(8,128)S(1)}, u32[]{:S(2)}, u32[]{:S(2)}) collective-permute-start(f32[8,128]{1,0:T(8,128)S(1)} %bitcast.96), channel_id=1, source_target_pairs={{0,3},{1,2},{2,1},{3,0},{4,7},{5,6},{6,5},{7,4},{8,11},{9,10},{10,... | collective-permute-start | bytes 12296 | tf_op jit(solution)/shard_map/ppermute | solution.py:689
  831.3 20.5 %collective-permute-start.73 = (bf16[256,1536]{1,0:T(8,128)(2,1)}, bf16[256,1536]{1,0:T(8,128)(2,1)S(1)}, u32[]{:S(2)}, u32[]{:S(2)}) collective-permute-start(bf16[256,1536]{1,0:T(8,128)(2,1)} %get-tuple-element.361.refs_2_), channel_id=1, source_target_pairs={{0,1},{3,2},{1,0},{2,3},{4,5},{7,6},{5,4},{6,7},{8,9},{11,10},{9,8... | collective-permute-start | bytes 2359304 | tf_op jit(solution)/shard_map/ppermute | solution.py:867
  (136 other events, 1018.0 us)
Sparse Core Ops, SparseCore 0:
  16.7 35.8 all-gather.4
  509.5 35.6 all-gather.6
  547.6 45.5 all-gather.8
  610.5 73.4 reduce-scatter.3
  687.2 61.7 reduce-scatter.5
  769.6 51.5 reduce-scatter.7

commit v11 on v10

--- a/solution.py
+++ b/solution.py
@@ -1031,12 +1031,13 @@
     kv = Gather(k, v)
 
 
-    q_all = lax.all_gather(q, "wide", axis=0, tiled=True)
     k_all, v_all = pick(order, sc, kv.pieces(), SPAN)
     heads_out = {}
     for c in chunks:
         heads_out[c] = (*attend_call(order, sc, q, k_all, v_all, cap, text, tg, c, BR), 0)
         sums.add(("attn", c), mm(heads_out[c][0], w_out).astype(bf16))
+        if c == 1:
+            q_all = lax.all_gather(pin(order, q), "wide", axis=0, tiled=True)
 
     mids, gus = {}, {}
     whole_out = ()
@@ -1044,7 +1045,7 @@
         mids[c], gus[c], ffn_part, *whole_out = ffn_call(
             order, c, patches, sums.get(("attn", c)), vec, w_gate_up, w_down, whole_out
         )
-        sums.add(("ffn", c), ffn_part)
+        sums.add(("ffn", c), ffn_part, (q_all,) if c == 1 else ())
     a3, hidden = whole_out
     whole_out = ()
     c4 = 0.0
@@ -1091,6 +1092,8 @@
 
     for h in pairs_of:
         dqs[h] = make_dq(h, () if h == 0 else d_got[last_half].first)
+        if h == 0:
+            g_mlp = scatter_rows(pin(order, mlp_part[0], d_got[last_half].first))
 
     d_cap, hs_c = order.run(
         "caption_grad",
@@ -1103,14 +1106,9 @@
     )
     d_text = (mm_nt(d_cap[:, :n], w_caption[0]) + mm_nt(d_cap[:, n:], w_caption[1])).astype(bf16)
     cap_part = mm_tn(captions, d_cap).astype(bf16)
-    pieces = -(-d_text.shape[1] // d)
-    padded = jnp.pad(d_text, ((0, 0), (0, pieces * d - d_text.shape[1])))
-    text_parts = [padded[:, p * d : (p + 1) * d] for p in range(pieces)]
-
-    sums.add(("text", 0), text_parts[0])
+    grad_captions = lax.psum(d_text, "narrow")
+
     ds = [x for h in pairs_of for x in pick(order, sc, d_got[h].pieces(), SPAN)]
-    sums.add(("text", 1), text_parts[1], (cap_part,))
-    g_mlp = scatter_rows(pin(order, mlp_part[0]))
     whole_out = ()
     c1_parts, hs_parts = [], []
     mixed = jnp.concatenate([heads_out[c][0] for c in chunks])
@@ -1123,17 +1121,14 @@
         c1_parts.append(p1)
         return da1_part
 
-    dkv = [dkv_call(order, sc, k, v, q_all, ds, 0, 0, pairs)]
-    for p in range(2, pieces):
-        sums.add(("text", p), text_parts[p])
+    first_dkv = [dkv_call(order, sc, k, v, q_all, ds, 0, 0, pairs)]
+    parts_of = lambda p: dkv_call(order, sc, k, v, q_all, ds, 1, p, 1)
+    sums.add(("da1", 0), project(0, first_dkv))
+    da1_part = project(1, first_dkv)
+    dkv = [parts_of(0)]
+    sums.add(("da1", 1), da1_part, (g_mlp,))
     g_cap = scatter_rows(pin(order, cap_part))
-    first_part = project(0, dkv)
-    parts_of = lambda p: dkv_call(order, sc, k, v, q_all, ds, 1, p, 1)
-    first_dkv, dkv = dkv, [parts_of(0)]
-    sums.add(("da1", 0), first_part)
-    da1_part = project(1, first_dkv)
     dkv.append(parts_of(1))
-    sums.add(("da1", 1), da1_part)
     dkv += [parts_of(p) for p in range(2, pairs)]
     for c in chunks[2:]:
         da1_part = project(c, dkv)
@@ -1142,19 +1137,18 @@
             packed = pack_call(order, c1_parts, hs_parts, hs_c, gate_sum, tg, c2, c3, c4, mz)
             from_narrow = [packed] + [swap(packed, "narrow", deep, m) for m in range(1, deep)]
             attn_part = pair_grad_call(order, a1, d_qkv, d_attn, mixed)[0]
-        sums.add(("da1", c), da1_part, (g_mlp, *from_narrow) if c == chunks[-1] else ())
+        sums.add(("da1", c), da1_part, (*from_narrow, grad_captions) if c == chunks[-1] else ())
     g_attn = scatter_rows(pin(order, attn_part))
 
     (folded,) = fold_call(order, from_narrow)
     got = lax.all_gather(folded, "wide")
     whole_out = last_call(order, 0, sums.get(("da1", 0)), patches, d_mids[0], vec, ())
     for c in chunks[1:]:
-        da1 = sums.get(("da1", c), (g_cap, got) if c == 1 else (g_attn,) if c == chunks[-1] else ())
+        da1 = sums.get(("da1", c), (got,) if c == 1 else (g_cap,) if c == 2 else ())
         if c == 1:
             got = pin(order, got)
         whole_out = last_call(order, c, da1, patches, d_mids[c], vec, whole_out)
     (grad_patches,) = whole_out
-    grad_captions = jnp.concatenate([sums.get(("text", p)) for p in range(pieces)], 1)[:, : d_text.shape[1]]
 
     cols = got[:, :4]
     grad_head_gains = jnp.sum(got[:, 4, : 3 * n], 0).reshape(3, heads, HD).sum(1)

time: 871 us -> 895 us (1.028)
  waiting for transfers between devices: 93.8 us -> 142 us
  Pallas kernels: 470 us -> 459 us
  starting transfers between devices: 136 us -> 125 us
    reduce_scatter x3, waiting for transfers between devices: 0.02 us -> 24.9 us  [scatter_rows(): lax.psum_scatter(x.astype(bf16), 'wide', scatter_dimension=0, tiled=True)]
    ppermute x42 -> x36, waiting for transfers between devices: 50 us -> 73.8 us  [step(): go = lambda x, perm: lax.ppermute(x, 'narrow', perm)]
    ppermute x42 -> x36, starting transfers between devices: 76.3 us -> 64.3 us  [step(): go = lambda x, perm: lax.ppermute(x, 'narrow', perm)]
    pallas_call x70 -> x68, Pallas kernels: 470 us -> 459 us  [run(): pl.pallas_call(body, grid_spec=pltpu.PrefetchScalarGridSpec(num_scalar_pr...]
    unnamed x207 -> x179, local copies, waits for them, and re-layouts: 34.4 us -> 32.6 us
  transfers between devices with their start and end apart: 83 -> 78, of which waited for: 15 -> 16; matrix products, arithmetic and copies ran while one was open for 7% -> 8% of each run, Pallas kernels for 45% -> 44%
where the time goes in v11:
time: 895 us; the launch traced here: 891 us
  Pallas kernels  459 us (51%)
  waiting for transfers between devices  142 us (16%)
  starting transfers between devices  125 us (14%)
  local copies, waits for them, and re-layouts  43.1 us (5%)
  other arithmetic  38.9 us (4%)
  blocking collectives  35.5 us (4%)
  matrix products  26.7 us (3%)
  between operations  21 us (2%)
    pallas_call x68, Pallas kernels, run(): pl.pallas_call(body, grid_spec=pltpu.PrefetchScalarGridSpec(num_scalar_pr...  459 us
    ppermute x36, waiting for transfers between devices, step(): go = lambda x, perm: lax.ppermute(x, 'narrow', perm)  73.8 us
    ppermute x36, starting transfers between devices, step(): go = lambda x, perm: lax.ppermute(x, 'narrow', perm)  64.3 us
    ppermute x13, starting transfers between devices, __init__(): send = lambda x, pairs: lax.ppermute(x, 'wide', pairs)  45.1 us
    ppermute x13, waiting for transfers between devices, __init__(): send = lambda x, pairs: lax.ppermute(x, 'wide', pairs)  42.8 us
    unnamed x179, local copies, waits for them, and re-layouts  32.6 us
    all_gather x2, blocking collectives, gather_now(): lax.all_gather(padded, axis, axis=0, tiled=True).reshape(-1, wide)[:, :n]  25 us
    reduce_scatter x3, waiting for transfers between devices, scatter_rows(): lax.psum_scatter(x.astype(bf16), 'wide', scatter_dimension=0, tiled=True)  24.9 us
  transfers between devices with their start and end apart: 78, of which 16 were waited for; matrix products, arithmetic and copies ran while one was open for 8% of the time, Pallas kernels for 44%

profile of v11, /device:TPU:0, one launch (start us, length us, event | category | flops | bytes accessed | tf_op | source)
XLA Modules:
  0.0 890.9 jit_solution(16573147149937143829)
XLA Ops:
  26.7 14.9 %all_gather.22 = f32[4,8,256]{2,1,0:T(8,128)S(1)} all-gather(f32[1,8,256]{2,1,0:T(8,128)S(1)} %reshape.309), channel_id=1, replica_groups=mesh['wide'=8,'narrow'=4] {'narrow'}, dimensions={0}, use_global_device_ids=true | all-gather | bytes 40960 | tf_op jit(solution)/shard_map/all_gather | solution.py:837
  41.7 10.2 %all_gather.23 = f32[8,8,896]{2,1,0:T(8,128)S(1)} all-gather(f32[1,8,896]{2,1,0:T(8,128)S(1)} %reshape.311), channel_id=1, replica_groups=mesh['wide'=8,'narrow'=4] {'wide'}, dimensions={0}, use_global_device_ids=true | all-gather | bytes 258048 | tf_op jit(solution)/shard_map/all_gather | solution.py:837
  58.2 13.4 %key.1 = (bf16[1024,1536]{1,0:T(8,128)(2,1)}, f32[1024,384]{1,0:T(8,128)}, bf16[1024,384]{1,0:T(8,128)(2,1)}, bf16[1024,384]{1,0:T(8,128)(2,1)}, f32[1024,384]{1,0:T(8,128)}, /*index=5*/bf16[1024,384]{1,0:T(8,128)(2,1)}) custom-call(bf16[1024,1536]{1,0:T(8,128)(2,1)} %refs_1_.7, f32[4,1536]{1,0:T(4,128)} %maximum_multiply_fusion.1.refs_1_.refs_2_.refs_4_.refs_3_, ...), custom_call_target="tpu_custom_call" | custom-call | flops 2000000000 | bytes 6000000 | tf_op jit(solution)/shard_map/key/pallas_call | solution.py:51
  75.1 17.3 %collective-permute-done.8.refs_11_ = bf16[1024,384]{1,0:T(8,128)(2,1)} collective-permute-done((bf16[1024,384]{1,0:T(8,128)(2,1)}, bf16[1024,384]{1,0:T(8,128)(2,1)}, u32[]{:S(2)}, u32[]{:S(2)}) %collective-permute-start.8) | collective-permute-done | bytes 786464 | tf_op jit(solution)/shard_map/ppermute | solution.py:718
  98.6 10.1 %collective-permute-done.1.refs_3_ = bf16[1024,384]{1,0:T(8,128)(2,1)} collective-permute-done((bf16[1024,384]{1,0:T(8,128)(2,1)}, bf16[1024,384]{1,0:T(8,128)(2,1)}, u32[]{:S(2)}, u32[]{:S(2)}) %collective-permute-start.1) | collective-permute-done | bytes 786464 | tf_op jit(solution)/shard_map/ppermute | solution.py:718
  108.7 5.3 collective-permute-done.12
  114.0 5.4 collective-permute-start.5
  120.7 10.1 %collective-permute-done.5.refs_7_ = bf16[1024,384]{1,0:T(8,128)(2,1)} collective-permute-done((bf16[1024,384]{1,0:T(8,128)(2,1)}, bf16[1024,384]{1,0:T(8,128)(2,1)}, u32[]{:S(2)}, u32[]{:S(2)}) %collective-permute-start.5) | collective-permute-done | bytes 786464 | tf_op jit(solution)/shard_map/ppermute | solution.py:718
  135.7 6.2 pick.3
  141.9 14.9 %attend.4 = (bf16[256,384]{1,0:T(8,128)(2,1)}, bf16[256,384]{1,0:T(8,128)(2,1)}, f32[256,384]{1,0:T(8,128)}) custom-call(s32[9]{0:T(128)} %pad_add_fusion.refs_0_, bf16[1024,384]{1,0:T(8,128)(2,1)} %get-tuple-element.179.refs_1_, bf16[4096,384]{1,0:T(8,128)(2,1)} %get-tuple-element.183.refs_2_.refs_7_.refs_4_, ...), custom_call_target="tpu_custom_call" | custom-call | flops 3750000128 | bytes 11250000 | tf_op jit(solution)/shard_map/attend/pallas_call | solution.py:51
  162.9 14.7 %attend.5 = (bf16[256,384]{1,0:T(8,128)(2,1)}, bf16[256,384]{1,0:T(8,128)(2,1)}, f32[256,384]{1,0:T(8,128)}) custom-call(s32[9]{0:T(128)} %pad_add_fusion.refs_0_, bf16[1024,384]{1,0:T(8,128)(2,1)} %get-tuple-element.179.refs_1_, bf16[4096,384]{1,0:T(8,128)(2,1)} %get-tuple-element.183.refs_2_.refs_7_.refs_4_, ...), custom_call_target="tpu_custom_call" | custom-call | flops 3750000128 | bytes 11250000 | tf_op jit(solution)/shard_map/attend/pallas_call | solution.py:51
  184.4 14.9 %attend.6 = (bf16[256,384]{1,0:T(8,128)(2,1)}, bf16[256,384]{1,0:T(8,128)(2,1)}, f32[256,384]{1,0:T(8,128)}) custom-call(s32[9]{0:T(128)} %pad_add_fusion.refs_0_, bf16[1024,384]{1,0:T(8,128)(2,1)} %get-tuple-element.179.refs_1_, bf16[4096,384]{1,0:T(8,128)(2,1)} %get-tuple-element.183.refs_2_.refs_7_.refs_4_, ...), custom_call_target="tpu_custom_call" | custom-call | flops 3750000128 | bytes 11250000 | tf_op jit(solution)/shard_map/attend/pallas_call | solution.py:51
  212.0 14.8 %attend.7 = (bf16[256,384]{1,0:T(8,128)(2,1)}, bf16[256,384]{1,0:T(8,128)(2,1)}, f32[256,384]{1,0:T(8,128)}) custom-call(s32[9]{0:T(128)} %pad_add_fusion.refs_0_, bf16[1024,384]{1,0:T(8,128)(2,1)} %get-tuple-element.179.refs_1_, bf16[4096,384]{1,0:T(8,128)(2,1)} %get-tuple-element.183.refs_2_.refs_7_.refs_4_, ...), custom_call_target="tpu_custom_call" | custom-call | flops 3750000128 | bytes 11250000 | tf_op jit(solution)/shard_map/attend/pallas_call | solution.py:51
  237.1 8.5 ffn.4
  245.6 6.8 collective-permute-done.20.refs_1_
  262.0 8.5 ffn.5
  270.5 5.0 collective-permute-done.22.refs_1_
  283.5 8.5 ffn.6
  305.6 8.5 ffn.7
  327.3 9.6 %ffn_back.4 = (bf16[256,1536]{1,0:T(8,128)(2,1)}, f32[1,1536]{1,0:T(1,128)}, bf16[1024,1536]{1,0:T(8,128)(2,1)}, bf16[1024,1536]{1,0:T(8,128)(2,1)}, bf16[1024,2048]{1,0:T(8,128)(2,1)}) custom-call(bf16[256,1536]{1,0:T(8,128)(2,1)} %get-tuple-element.221.refs_0_.refs_7_, f32[256,1536]{1,0:T(8,128)} %get-tuple-element.197.refs_7_.refs_1_, ...), custom_call_target="tpu_custom_call" | custom-call | flops 2500000000 | bytes 7500000 | tf_op jit(solution)/shard_map/ffn_back/pallas_call | solution.py:51
  347.6 9.6 %ffn_back.5 = (bf16[256,1536]{1,0:T(8,128)(2,1)}, f32[1,1536]{1,0:T(1,128)}, bf16[1024,1536]{1,0:T(8,128)(2,1)}, bf16[1024,1536]{1,0:T(8,128)(2,1)}, bf16[1024,2048]{1,0:T(8,128)(2,1)}) custom-call(bf16[256,1536]{1,0:T(8,128)(2,1)} %get-tuple-element.226.refs_0_.refs_7_, ...), custom_call_target="tpu_custom_call", output_to_operand_aliasing={{2}: (8, {}), {3}: (9, {}), {4}: (10, {})} | custom-call | flops 2500000000 | bytes 7500000 | tf_op jit(solution)/shard_map/ffn_back/pallas_call | solution.py:51
  367.2 9.6 %ffn_back.6 = (bf16[256,1536]{1,0:T(8,128)(2,1)}, f32[1,1536]{1,0:T(1,128)}, bf16[1024,1536]{1,0:T(8,128)(2,1)}, bf16[1024,1536]{1,0:T(8,128)(2,1)}, bf16[1024,2048]{1,0:T(8,128)(2,1)}) custom-call(bf16[256,1536]{1,0:T(8,128)(2,1)} %get-tuple-element.234.refs_0_.refs_7_, ...), custom_call_target="tpu_custom_call", output_to_operand_aliasing={{2}: (8, {}), {3}: (9, {}), {4}: (10, {})} | custom-call | flops 2500000000 | bytes 7500000 | tf_op jit(solution)/shard_map/ffn_back/pallas_call | solution.py:51
  386.2 9.6 %ffn_back.7 = (bf16[256,1536]{1,0:T(8,128)(2,1)}, f32[1,1536]{1,0:T(1,128)}, bf16[1024,1536]{1,0:T(8,128)(2,1)}, bf16[1024,1536]{1,0:T(8,128)(2,1)}, bf16[1024,2048]{1,0:T(8,128)(2,1)}) custom-call(bf16[256,1536]{1,0:T(8,128)(2,1)} %get-tuple-element.240.refs_0_.refs_7_, ...), custom_call_target="tpu_custom_call", output_to_operand_aliasing={{2}: (8, {}), {3}: (9, {}), {4}: (10, {})} | custom-call | flops 2500000000 | bytes 7500000 | tf_op jit(solution)/shard_map/ffn_back/pallas_call | solution.py:51
  404.3 5.6 out_back.4
  409.9 9.9 %pair_grad.3.refs_6_.refs_7_ = bf16[1536,3072]{1,0:T(8,128)(2,1)} custom-call(bf16[1024,1536]{1,0:T(8,128)(2,1)} %get-tuple-element.251.refs_0_, bf16[1024,2048]{1,0:T(8,128)(2,1)} %get-tuple-element.252.refs_1_, bf16[1024,1536]{1,0:T(8,128)(2,1)} %get-tuple-element.253.refs_2_, bf16[1024,1024]{1,0:T(8,128)(2,1)} %get-tuple-element.254.refs_3_, ...), custom_call_target="tpu_custom_call" | custom-call | flops 2500000000 | bytes 7500000 | tf_op jit(solution)/shard_map/pair_grad/pallas_call | solution.py:51
  428.5 5.6 out_back.5
  437.0 6.3 caption_back.2
  450.6 21.7 %collective-permute-start.43 = (bf16[512,512]{1,0:T(8,128)(2,1)S(1)}, bf16[512,512]{1,0:T(8,128)(2,1)S(1)}, u32[]{:S(2)}, u32[]{:S(2)}) collective-permute-start(bf16[512,512]{1,0:T(8,128)(2,1)S(1)} %collective-permute-done.41.refs_5_.refs_3_), channel_id=1, source_target_pairs={{0,16},{4,20},{24,8},{28,12},{1,17},{5,21},{25,9},{29,13},{2,18},{... | collective-permute-start | bytes 1572872 | tf_op jit(solution)/shard_map/ppermute | solution.py:741
  472.4 5.6 out_back.6
  478.8 9.9 %pair_grad.4.refs_3_ = bf16[1536,3072]{1,0:T(8,128)(2,1)} custom-call(bf16[1024,1536]{1,0:T(8,128)(2,1)} %get-tuple-element.251.refs_0_, bf16[1024,2048]{1,0:T(8,128)(2,1)} %get-tuple-element.252.refs_1_, bf16[1024,1536]{1,0:T(8,128)(2,1)} %get-tuple-element.253.refs_2_, ...), custom_call_target="tpu_custom_call", output_to_operand_aliasing={{}: (7, {})} | custom-call | flops 2500000000 | bytes 7500000 | tf_op jit(solution)/shard_map/pair_grad/pallas_call | solution.py:51
  492.5 5.6 out_back.7
  498.1 6.4 caption_back.3
  508.8 26.8 %dq.2.refs_0_ = f32[512,384]{1,0:T(8,128)} custom-call(s32[9]{0:T(128)} %pad_add_fusion.refs_0_, bf16[1024,384]{1,0:T(8,128)(2,1)} %get-tuple-element.179.refs_1_, bf16[512,512]{1,0:T(8,128)(2,1)} %get-tuple-element.264.refs_2_.refs_3_.refs_1_, bf16[512,512]{1,0:T(8,128)(2,1)} %get-tuple-element.264.refs_2_.refs_3_.refs_1_, ...), custom_call_target="tpu_custom_call" | custom-call | flops 6750000128 | bytes 20250000 | tf_op jit(solution)/shard_map/dq/pallas_call | solution.py:51
  540.3 26.7 %dq.3.refs_4_.refs_0_ = f32[512,384]{1,0:T(8,128)} custom-call(s32[9]{0:T(128)} %pad_add_fusion.refs_0_, bf16[1024,384]{1,0:T(8,128)(2,1)} %get-tuple-element.179.refs_1_, bf16[512,512]{1,0:T(8,128)(2,1)} %get-tuple-element.289.refs_2_.refs_3_.refs_1_, bf16[512,512]{1,0:T(8,128)(2,1)} %get-tuple-element.289.refs_2_.refs_3_.refs_1_, ...), custom_call_target="tpu_custom_call" | custom-call | flops 6750000128 | bytes 20250000 | tf_op jit(solution)/shard_map/dq/pallas_call | solution.py:51
  591.0 32.5 %dkv.4 = (f32[512,384]{1,0:T(8,128)}, f32[512,384]{1,0:T(8,128)}) custom-call(s32[9]{0:T(128)} %pad_add_fusion.refs_0_, bf16[1024,384]{1,0:T(8,128)(2,1)} %get-tuple-element.180.refs_1_, bf16[1024,384]{1,0:T(8,128)(2,1)} %get-tuple-element.181.refs_9_.refs_2_, bf16[8192,384]{1,0:T(8,128)(2,1)} %all-gather.7.cloned.1.call-done.refs_8_.refs_3_, ...), custom_call_target="tpu_custom_call" | custom-call | flops 6000000000 | bytes 18000000 | tf_op jit(solution)/shard_map/dkv/pallas_call | solution.py:51
  623.5 6.6 dqkv.4
  634.5 6.6 dqkv.5
  641.1 12.5 %dkv.5 = (f32[512,128]{1,0:T(8,128)}, f32[512,128]{1,0:T(8,128)}) custom-call(s32[9]{0:T(128)} %pad_add_fusion.refs_0_, bf16[1024,384]{1,0:T(8,128)(2,1)} %get-tuple-element.180.refs_1_, bf16[1024,384]{1,0:T(8,128)(2,1)} %get-tuple-element.181.refs_9_.refs_2_, bf16[8192,384]{1,0:T(8,128)(2,1)} %all-gather.7.cloned.1.call-done.refs_8_.refs_3_, ...), custom_call_target="tpu_custom_call" | custom-call | flops 6000000000 | bytes 18000000 | tf_op jit(solution)/shard_map/dkv/pallas_call | solution.py:51
  653.6 26.1 %collective-permute-done.55.refs_1_ = bf16[256,1536]{1,0:T(8,128)(2,1)S(1)} collective-permute-done((bf16[256,1536]{1,0:T(8,128)(2,1)}, bf16[256,1536]{1,0:T(8,128)(2,1)S(1)}, u32[]{:S(2)}, u32[]{:S(2)}) %collective-permute-start.55) | collective-permute-done | bytes 786464 | tf_op jit(solution)/shard_map/ppermute | solution.py:867
  691.5 12.6 %dkv.6 = (f32[512,128]{1,0:T(8,128)}, f32[512,128]{1,0:T(8,128)}) custom-call(s32[9]{0:T(128)} %pad_add_fusion.refs_0_, bf16[1024,384]{1,0:T(8,128)(2,1)} %get-tuple-element.180.refs_1_, bf16[1024,384]{1,0:T(8,128)(2,1)} %get-tuple-element.181.refs_9_.refs_2_, bf16[8192,384]{1,0:T(8,128)(2,1)} %all-gather.7.cloned.1.call-done.refs_8_.refs_3_, ...), custom_call_target="tpu_custom_call" | custom-call | flops 6000000000 | bytes 18000000 | tf_op jit(solution)/shard_map/dkv/pallas_call | solution.py:51
  704.1 12.6 %dkv.7 = (f32[512,128]{1,0:T(8,128)}, f32[512,128]{1,0:T(8,128)}) custom-call(s32[9]{0:T(128)} %pad_add_fusion.refs_0_, bf16[1024,384]{1,0:T(8,128)(2,1)} %get-tuple-element.180.refs_1_, bf16[1024,384]{1,0:T(8,128)(2,1)} %get-tuple-element.181.refs_9_.refs_2_, bf16[8192,384]{1,0:T(8,128)(2,1)} %all-gather.7.cloned.1.call-done.refs_8_.refs_3_, ...), custom_call_target="tpu_custom_call" | custom-call | flops 6000000000 | bytes 18000000 | tf_op jit(solution)/shard_map/dkv/pallas_call | solution.py:51
  716.7 6.7 dqkv.6
  723.4 15.9 %collective-permute-done.56.refs_1_ = bf16[256,1536]{1,0:T(8,128)(2,1)S(1)} collective-permute-done((bf16[256,1536]{1,0:T(8,128)(2,1)}, bf16[256,1536]{1,0:T(8,128)(2,1)S(1)}, u32[]{:S(2)}, u32[]{:S(2)}) %collective-permute-start.56) | collective-permute-done | bytes 786464 | tf_op jit(solution)/shard_map/ppermute | solution.py:867
  747.3 6.6 dqkv.7
  760.4 11.1 %pair_grad.5.refs_7_.refs_1_ = bf16[1536,1536]{1,0:T(8,128)(2,1)} custom-call(bf16[1024,1536]{1,0:T(8,128)(2,1)} %get-tuple-element.182.refs_17_.refs_0_, bf16[1024,1152]{1,0:T(8,128)(2,1)} %get-tuple-element.312.refs_1_, bf16[1024,1536]{1,0:T(8,128)(2,1)} %get-tuple-element.313.refs_2_, bf16[1024,384]{1,0:T(8,128)(2,1)} %pad_maximum_fusion.refs_3_, ...), custom_call_target="tpu_custom_call" | custom-call | flops 2500000000 | bytes 7500000 | tf_op jit(solution)/shard_map/pair_grad/pallas_call | solution.py:51
  787.8 10.5 %all-gather = f32[64,1536]{1,0:T(8,128)} all-gather(f32[8,1536]{1,0:T(8,128)S(1)} %copy-done.58), channel_id=2, replica_groups=mesh['wide'=8,'narrow'=4] {'wide'}, dimensions={0}, use_global_device_ids=true | all-gather | bytes 442368 | tf_op jit(solution)/shard_map/all_gather | solution.py:1144
  827.3 6.4 collective-permute-done.65.refs_1_
  839.8 24.9 %reduce-scatter.8.cloned.1.call-done = bf16[192,1536]{1,0:T(8,128)(2,1)} async-done(((bf16[1536,1536]{1,0:T(8,128)(2,1)}), bf16[192,1536]{1,0:T(8,128)(2,1)}) %reduce-scatter.8.cloned.1.call-update) | async-done | bytes 589840 | tf_op jit(solution)/shard_map/reduce_scatter | solution.py:929
  (452 shorter events, 312.0 us)
Async XLA Ops:
  7.2 134.7 %all-gather.5.cloned.1.call-start = ((), (), s32[]{:S(2)}) async-start(), calls=%async_computation.3 | async-start | bytes 3538944 | tf_op jit(solution)/shard_map/all_gather | solution.py:1025
  16.6 258.9 %all-gather.7.cloned.1.call-start = ((), (), s32[]{:S(2)}) async-start(), calls=%async_computation.4 | async-start | bytes 7077888 | tf_op jit(solution)/shard_map/all_gather | solution.py:1040
  71.7 20.7 %collective-permute-start.8 = (bf16[1024,384]{1,0:T(8,128)(2,1)}, bf16[1024,384]{1,0:T(8,128)(2,1)}, u32[]{:S(2)}, u32[]{:S(2)}) collective-permute-start(bf16[1024,384]{1,0:T(8,128)(2,1)} %get-tuple-element.181.refs_9_.refs_2_), channel_id=1, source_target_pairs={{0,8},{4,12},{8,0},{12,4},{16,24},{20,28},{24,16},{28,20},{1,9},{5... | collective-permute-start | bytes 2359304 | tf_op jit(solution)/shard_map/ppermute | solution.py:718
  73.0 22.8 %collective-permute-start.10 = (bf16[1024,384]{1,0:T(8,128)(2,1)}, bf16[1024,384]{1,0:T(8,128)(2,1)S(1)}, u32[]{:S(2)}, u32[]{:S(2)}) collective-permute-start(bf16[1024,384]{1,0:T(8,128)(2,1)} %get-tuple-element.181.refs_9_.refs_2_), channel_id=1, source_target_pairs={{4,20},{16,0},{12,28},{24,8},{5,21},{17,1},{13,29},{25,9},{6,22},{... | collective-permute-start | bytes 2359304 | tf_op jit(solution)/shard_map/ppermute | solution.py:718
  74.3 34.4 %collective-permute-start.1 = (bf16[1024,384]{1,0:T(8,128)(2,1)}, bf16[1024,384]{1,0:T(8,128)(2,1)}, u32[]{:S(2)}, u32[]{:S(2)}) collective-permute-start(bf16[1024,384]{1,0:T(8,128)(2,1)} %get-tuple-element.180.refs_1_), channel_id=1, source_target_pairs={{0,8},{4,12},{8,0},{12,4},{16,24},{20,28},{24,16},{28,20},{1,9},{5... | collective-permute-start | bytes 2359304 | tf_op jit(solution)/shard_map/ppermute | solution.py:718
  92.4 21.6 %collective-permute-start.12 = (bf16[1024,384]{1,0:T(8,128)(2,1)}, bf16[1024,384]{1,0:T(8,128)(2,1)S(1)}, u32[]{:S(2)}, u32[]{:S(2)}) collective-permute-start(bf16[1024,384]{1,0:T(8,128)(2,1)} %collective-permute-done.8.refs_11_), channel_id=1, source_target_pairs={{0,16},{28,12},{1,17},{29,13},{2,18},{30,14},{3,19},{31,15}} | collective-permute-start | bytes 2359304 | tf_op jit(solution)/shard_map/ppermute | solution.py:718
  95.8 23.5 %collective-permute-start.13 = (bf16[1024,384]{1,0:T(8,128)(2,1)S(1)}, bf16[1024,384]{1,0:T(8,128)(2,1)S(1)}, u32[]{:S(2)}, u32[]{:S(2)}) collective-permute-start(bf16[1024,384]{1,0:T(8,128)(2,1)S(1)} %collective-permute-done.10.refs_13_), channel_id=1, source_target_pairs={{28,20},{0,8},{29,21},{1,9},{30,22},{2,10},{31,23},{3,11}} | collective-permute-start | bytes 2359304 | tf_op jit(solution)/shard_map/ppermute | solution.py:718
  97.2 22.4 %collective-permute-start.3 = (bf16[1024,384]{1,0:T(8,128)(2,1)}, bf16[1024,384]{1,0:T(8,128)(2,1)}, u32[]{:S(2)}, u32[]{:S(2)}) collective-permute-start(bf16[1024,384]{1,0:T(8,128)(2,1)} %get-tuple-element.180.refs_1_), channel_id=1, source_target_pairs={{4,20},{16,0},{12,28},{24,8},{5,21},{17,1},{13,29},{25,9},{6,22},{... | collective-permute-start | bytes 2359304 | tf_op jit(solution)/shard_map/ppermute | solution.py:718
  98.5 21.7 %collective-permute-start = (bf16[1024,384]{1,0:T(8,128)(2,1)}, bf16[1024,384]{1,0:T(8,128)(2,1)S(1)}, u32[]{:S(2)}, u32[]{:S(2)}) collective-permute-start(bf16[1024,384]{1,0:T(8,128)(2,1)} %get-tuple-element.180.refs_1_), channel_id=1, source_target_pairs={{0,4},{4,0},{8,12},{12,8},{16,20},{20,16},{24,28},{28,24},{1,5},{5... | collective-permute-start | bytes 2359304 | tf_op jit(solution)/shard_map/ppermute | solution.py:689
  114.0 16.9 %collective-permute-start.5 = (bf16[1024,384]{1,0:T(8,128)(2,1)}, bf16[1024,384]{1,0:T(8,128)(2,1)}, u32[]{:S(2)}, u32[]{:S(2)}) collective-permute-start(bf16[1024,384]{1,0:T(8,128)(2,1)} %collective-permute-done.1.refs_3_), channel_id=1, source_target_pairs={{0,16},{4,20},{24,8},{28,12},{1,17},{5,21},{25,9},{29,13},{2,18},{... | collective-permute-start | bytes 2359304 | tf_op jit(solution)/shard_map/ppermute | solution.py:718
  159.2 20.8 %collective-permute-start.15 = (bf16[256,1536]{1,0:T(8,128)(2,1)}, bf16[256,1536]{1,0:T(8,128)(2,1)}, u32[]{:S(2)}, u32[]{:S(2)}) collective-permute-start(bf16[256,1536]{1,0:T(8,128)(2,1)} %convolution_convert_fusion.4.refs_2_), channel_id=1, source_target_pairs={{0,1},{3,2},{1,0},{2,3},{4,5},{7,6},{5,4},{6,7},{8,9},{11,10},{9,8... | collective-permute-start | bytes 2359304 | tf_op jit(solution)/shard_map/ppermute | solution.py:867
  182.6 384.4 %all-gather.9.cloned.1.call-start = ((), (), s32[]{:S(2)}) async-start(), calls=%async_computation.5 | async-start | bytes 3538944 | tf_op jit(solution)/shard_map/all_gather | solution.py:1085
  182.6 19.9 %collective-permute-start.16 = (bf16[256,1536]{1,0:T(8,128)(2,1)}, bf16[256,1536]{1,0:T(8,128)(2,1)S(1)}, u32[]{:S(2)}, u32[]{:S(2)}) collective-permute-start(bf16[256,1536]{1,0:T(8,128)(2,1)} %get-tuple-element.187), channel_id=1, source_target_pairs={{0,1},{3,2},{1,0},{2,3},{4,5},{7,6},{5,4},{6,7},{8,9},{11,10},{9,8... | collective-permute-start | bytes 2359304 | tf_op jit(solution)/shard_map/ppermute | solution.py:867
  183.7 18.9 %collective-permute-start.17 = (bf16[256,1536]{1,0:T(8,128)(2,1)}, bf16[256,1536]{1,0:T(8,128)(2,1)S(1)}, u32[]{:S(2)}, u32[]{:S(2)}) collective-permute-start(bf16[256,1536]{1,0:T(8,128)(2,1)} %get-tuple-element.188.refs_0_.refs_3_), channel_id=1, source_target_pairs={{1,2},{2,1},{5,6},{6,5},{9,10},{10,9},{13,14},{14,13},{17,18},{18,... | collective-permute-start | bytes 2359304 | tf_op jit(solution)/shard_map/ppermute | solution.py:867
  207.4 21.8 %collective-permute-start.18 = (bf16[256,1536]{1,0:T(8,128)(2,1)}, bf16[256,1536]{1,0:T(8,128)(2,1)S(1)}, u32[]{:S(2)}, u32[]{:S(2)}) collective-permute-start(bf16[256,1536]{1,0:T(8,128)(2,1)} %get-tuple-element.190.refs_2_), channel_id=1, source_target_pairs={{0,1},{3,2},{1,0},{2,3},{4,5},{7,6},{5,4},{6,7},{8,9},{11,10},{9,8... | collective-permute-start | bytes 2359304 | tf_op jit(solution)/shard_map/ppermute | solution.py:867
  211.3 17.9 %collective-permute-start.19 = (bf16[256,1536]{1,0:T(8,128)(2,1)}, bf16[256,1536]{1,0:T(8,128)(2,1)S(1)}, u32[]{:S(2)}, u32[]{:S(2)}) collective-permute-start(bf16[256,1536]{1,0:T(8,128)(2,1)} %get-tuple-element.191.refs_7_.refs_4_), channel_id=1, source_target_pairs={{1,2},{2,1},{5,6},{6,5},{9,10},{10,9},{13,14},{14,13},{17,18},{18,... | collective-permute-start | bytes 2359304 | tf_op jit(solution)/shard_map/ppermute | solution.py:867
  234.5 18.0 %collective-permute-start.20 = (bf16[256,1536]{1,0:T(8,128)(2,1)}, bf16[256,1536]{1,0:T(8,128)(2,1)S(1)}, u32[]{:S(2)}, u32[]{:S(2)}) collective-permute-start(bf16[256,1536]{1,0:T(8,128)(2,1)} %get-tuple-element.193.refs_2_), channel_id=1, source_target_pairs={{0,1},{3,2},{1,0},{2,3},{4,5},{7,6},{5,4},{6,7},{8,9},{11,10},{9,8... | collective-permute-start | bytes 2359304 | tf_op jit(solution)/shard_map/ppermute | solution.py:867
  257.1 18.4 %collective-permute-start.22 = (bf16[256,1536]{1,0:T(8,128)(2,1)}, bf16[256,1536]{1,0:T(8,128)(2,1)S(1)}, u32[]{:S(2)}, u32[]{:S(2)}) collective-permute-start(bf16[256,1536]{1,0:T(8,128)(2,1)} %get-tuple-element.198.refs_2_), channel_id=1, source_target_pairs={{0,1},{3,2},{1,0},{2,3},{4,5},{7,6},{5,4},{6,7},{8,9},{11,10},{9,8... | collective-permute-start | bytes 2359304 | tf_op jit(solution)/shard_map/ppermute | solution.py:867
  279.9 17.0 %collective-permute-start.24 = (bf16[256,1536]{1,0:T(8,128)(2,1)}, bf16[256,1536]{1,0:T(8,128)(2,1)S(1)}, u32[]{:S(2)}, u32[]{:S(2)}) collective-permute-start(bf16[256,1536]{1,0:T(8,128)(2,1)} %get-tuple-element.205.refs_2_), channel_id=1, source_target_pairs={{0,1},{3,2},{1,0},{2,3},{4,5},{7,6},{5,4},{6,7},{8,9},{11,10},{9,8... | collective-permute-start | bytes 2359304 | tf_op jit(solution)/shard_map/ppermute | solution.py:867
  301.5 16.7 %collective-permute-start.26 = (bf16[256,1536]{1,0:T(8,128)(2,1)}, bf16[256,1536]{1,0:T(8,128)(2,1)S(1)}, u32[]{:S(2)}, u32[]{:S(2)}) collective-permute-start(bf16[256,1536]{1,0:T(8,128)(2,1)} %get-tuple-element.212.refs_2_), channel_id=1, source_target_pairs={{0,1},{3,2},{1,0},{2,3},{4,5},{7,6},{5,4},{6,7},{8,9},{11,10},{9,8... | collective-permute-start | bytes 2359304 | tf_op jit(solution)/shard_map/ppermute | solution.py:867
  400.5 19.4 %collective-permute-start.36 = (bf16[256,1536]{1,0:T(8,128)(2,1)}, bf16[256,1536]{1,0:T(8,128)(2,1)S(1)}, u32[]{:S(2)}, u32[]{:S(2)}) collective-permute-start(bf16[256,1536]{1,0:T(8,128)(2,1)} %get-tuple-element.249.refs_2_), channel_id=1, source_target_pairs={{0,1},{3,2},{1,0},{2,3},{4,5},{7,6},{5,4},{6,7},{8,9},{11,10},{9,8... | collective-permute-start | bytes 2359304 | tf_op jit(solution)/shard_map/ppermute | solution.py:867
  424.9 18.5 %collective-permute-start.38 = (bf16[256,1536]{1,0:T(8,128)(2,1)}, bf16[256,1536]{1,0:T(8,128)(2,1)S(1)}, u32[]{:S(2)}, u32[]{:S(2)}) collective-permute-start(bf16[256,1536]{1,0:T(8,128)(2,1)} %get-tuple-element.269.refs_2_), channel_id=1, source_target_pairs={{0,1},{3,2},{1,0},{2,3},{4,5},{7,6},{5,4},{6,7},{8,9},{11,10},{9,8... | collective-permute-start | bytes 2359304 | tf_op jit(solution)/shard_map/ppermute | solution.py:867
  434.1 16.5 %collective-permute-start.41 = (bf16[512,512]{1,0:T(8,128)(2,1)}, bf16[512,512]{1,0:T(8,128)(2,1)S(1)}, u32[]{:S(2)}, u32[]{:S(2)}) collective-permute-start(bf16[512,512]{1,0:T(8,128)(2,1)} %get-tuple-element.264.refs_2_.refs_3_.refs_1_), channel_id=1, source_target_pairs={{0,8},{4,12},{8,0},{12,4},{16,24},{20,28},{24,16},{28,20},{1,9},{5... | collective-permute-start | bytes 1572872 | tf_op jit(solution)/shard_map/ppermute | solution.py:741
  447.3 41.4 %collective-permute-start.40 = (bf16[256,1536]{1,0:T(8,128)(2,1)}, bf16[256,1536]{1,0:T(8,128)(2,1)S(1)}, u32[]{:S(2)}, u32[]{:S(2)}) collective-permute-start(bf16[256,1536]{1,0:T(8,128)(2,1)} %get-tuple-element.276.refs_2_), channel_id=1, source_target_pairs={{0,1},{3,2},{1,0},{2,3},{4,5},{7,6},{5,4},{6,7},{8,9},{11,10},{9,8... | collective-permute-start | bytes 2359304 | tf_op jit(solution)/shard_map/ppermute | solution.py:867
  449.3 28.7 %collective-permute-start.42 = (bf16[512,512]{1,0:T(8,128)(2,1)S(1)}, bf16[512,512]{1,0:T(8,128)(2,1)S(1)}, u32[]{:S(2)}, u32[]{:S(2)}) collective-permute-start(bf16[512,512]{1,0:T(8,128)(2,1)S(1)} %copy-done.14), channel_id=1, source_target_pairs={{4,20},{16,0},{12,28},{24,8},{5,21},{17,1},{13,29},{25,9},{6,22},{... | collective-permute-start | bytes 1572872 | tf_op jit(solution)/shard_map/ppermute | solution.py:741
  450.6 38.1 %collective-permute-start.43 = (bf16[512,512]{1,0:T(8,128)(2,1)S(1)}, bf16[512,512]{1,0:T(8,128)(2,1)S(1)}, u32[]{:S(2)}, u32[]{:S(2)}) collective-permute-start(bf16[512,512]{1,0:T(8,128)(2,1)S(1)} %collective-permute-done.41.refs_5_.refs_3_), channel_id=1, source_target_pairs={{0,16},{4,20},{24,8},{28,12},{1,17},{5,21},{25,9},{29,13},{2,18},{... | collective-permute-start | bytes 1572872 | tf_op jit(solution)/shard_map/ppermute | solution.py:741
  507.4 172.4 %reduce-scatter.4.cloned.1.call-start = ((), (), s32[]{:S(2)}) async-start(), calls=%async_computation.6 | async-start | bytes 10616832 | tf_op jit(solution)/shard_map/reduce_scatter | solution.py:929
  507.4 28.1 %collective-permute-start.48 = (bf16[512,512]{1,0:T(8,128)(2,1)}, bf16[512,512]{1,0:T(8,128)(2,1)}, u32[]{:S(2)}, u32[]{:S(2)}) collective-permute-start(bf16[512,512]{1,0:T(8,128)(2,1)} %get-tuple-element.289.refs_2_.refs_3_.refs_1_), channel_id=1, source_target_pairs={{0,8},{4,12},{8,0},{12,4},{16,24},{20,28},{24,16},{28,20},{1,9},{5... | collective-permute-start | bytes 1572872 | tf_op jit(solution)/shard_map/ppermute | solution.py:741
  507.5 28.1 %collective-permute-start.49 = (bf16[512,512]{1,0:T(8,128)(2,1)}, bf16[512,512]{1,0:T(8,128)(2,1)}, u32[]{:S(2)}, u32[]{:S(2)}) collective-permute-start(bf16[512,512]{1,0:T(8,128)(2,1)} %get-tuple-element.289.refs_2_.refs_3_.refs_1_), channel_id=1, source_target_pairs={{4,20},{16,0},{12,28},{24,8},{5,21},{17,1},{13,29},{25,9},{6,22},{... | collective-permute-start | bytes 1572872 | tf_op jit(solution)/shard_map/ppermute | solution.py:741
  535.6 235.9 %all-reduce.3.cloned.1.call-start = ((), (), s32[]{:S(2)}) async-start(), calls=%async_computation.7 | async-start | bytes 4194304 | tf_op jit(solution)/shard_map/psum | solution.py:1109
  536.2 40.5 %collective-permute-start.44 = (bf16[512,512]{1,0:T(8,128)(2,1)}, bf16[512,512]{1,0:T(8,128)(2,1)}, u32[]{:S(2)}, u32[]{:S(2)}) collective-permute-start(bf16[512,512]{1,0:T(8,128)(2,1)} %get-tuple-element.264.refs_2_.refs_3_.refs_1_), channel_id=1, source_target_pairs={{0,4},{4,0},{8,12},{12,8},{16,20},{20,16},{24,28},{28,24},{1,5},{5... | collective-permute-start | bytes 1572872 | tf_op jit(solution)/shard_map/ppermute | solution.py:689
  536.6 40.2 %collective-permute-start.45 = (bf16[512,512]{1,0:T(8,128)(2,1)S(1)}, bf16[512,512]{1,0:T(8,128)(2,1)}, u32[]{:S(2)}, u32[]{:S(2)}) collective-permute-start(bf16[512,512]{1,0:T(8,128)(2,1)S(1)} %copy-done.10), channel_id=1, source_target_pairs={{0,4},{4,0},{8,12},{12,8},{16,20},{20,16},{24,28},{28,24},{1,5},{5... | collective-permute-start | bytes 1572872 | tf_op jit(solution)/shard_map/ppermute | solution.py:689
  536.8 40.4 %collective-permute-start.46 = (bf16[512,512]{1,0:T(8,128)(2,1)S(1)}, bf16[512,512]{1,0:T(8,128)(2,1)}, u32[]{:S(2)}, u32[]{:S(2)}) collective-permute-start(bf16[512,512]{1,0:T(8,128)(2,1)S(1)} %copy-done.12), channel_id=1, source_target_pairs={{0,4},{4,0},{8,12},{12,8},{16,20},{20,16},{24,28},{28,24},{1,5},{5... | collective-permute-start | bytes 1572872 | tf_op jit(solution)/shard_map/ppermute | solution.py:689
  537.2 45.7 %collective-permute-start.47 = (bf16[512,512]{1,0:T(8,128)(2,1)}, bf16[512,512]{1,0:T(8,128)(2,1)}, u32[]{:S(2)}, u32[]{:S(2)}) collective-permute-start(bf16[512,512]{1,0:T(8,128)(2,1)} %copy-done.13), channel_id=1, source_target_pairs={{0,4},{4,0},{8,12},{12,8},{16,20},{20,16},{24,28},{28,24},{1,5},{5... | collective-permute-start | bytes 1572872 | tf_op jit(solution)/shard_map/ppermute | solution.py:689
  537.3 40.0 %collective-permute-start.53 = (bf16[512,512]{1,0:T(8,128)(2,1)}, bf16[512,512]{1,0:T(8,128)(2,1)}, u32[]{:S(2)}, u32[]{:S(2)}) collective-permute-start(bf16[512,512]{1,0:T(8,128)(2,1)} %collective-permute-done.48.refs_1_.refs_8_.refs_3_), channel_id=1, source_target_pairs={{0,16},{4,20},{24,8},{28,12},{1,17},{5,21},{25,9},{29,13},{2,18},{... | collective-permute-start | bytes 1572872 | tf_op jit(solution)/shard_map/ppermute | solution.py:741
  582.6 251.1 %reduce-scatter.6.cloned.1.call-start = ((), (), s32[]{:S(2)}) async-start(), calls=%async_computation.8 | async-start | bytes 7077888 | tf_op jit(solution)/shard_map/reduce_scatter | solution.py:929
  630.1 49.7 %collective-permute-start.55 = (bf16[256,1536]{1,0:T(8,128)(2,1)}, bf16[256,1536]{1,0:T(8,128)(2,1)S(1)}, u32[]{:S(2)}, u32[]{:S(2)}) collective-permute-start(bf16[256,1536]{1,0:T(8,128)(2,1)} %get-tuple-element.295.refs_11_.refs_2_), channel_id=1, source_target_pairs={{0,1},{3,2},{1,0},{2,3},{4,5},{7,6},{5,4},{6,7},{8,9},{11,10},{9,8... | collective-permute-start | bytes 2359304 | tf_op jit(solution)/shard_map/ppermute | solution.py:867
  683.4 181.3 %reduce-scatter.8.cloned.1.call-start = ((), (), s32[]{:S(2)}) async-start(), calls=%async_computation.9 | async-start | bytes 5308416 | tf_op jit(solution)/shard_map/reduce_scatter | solution.py:929
  688.0 51.3 %collective-permute-start.57 = (bf16[256,1536]{1,0:T(8,128)(2,1)S(1)}, bf16[256,1536]{1,0:T(8,128)(2,1)S(1)}, u32[]{:S(2)}, u32[]{:S(2)}) collective-permute-start(bf16[256,1536]{1,0:T(8,128)(2,1)S(1)} %copy-done.8), channel_id=1, source_target_pairs={{1,2},{2,1},{5,6},{6,5},{9,10},{10,9},{13,14},{14,13},{17,18},{18,... | collective-permute-start | bytes 2359304 | tf_op jit(solution)/shard_map/ppermute | solution.py:867
  689.1 50.2 %collective-permute-start.56 = (bf16[256,1536]{1,0:T(8,128)(2,1)}, bf16[256,1536]{1,0:T(8,128)(2,1)S(1)}, u32[]{:S(2)}, u32[]{:S(2)}) collective-permute-start(bf16[256,1536]{1,0:T(8,128)(2,1)} %get-tuple-element.299), channel_id=1, source_target_pairs={{0,1},{3,2},{1,0},{2,3},{4,5},{7,6},{5,4},{6,7},{8,9},{11,10},{9,8... | collective-permute-start | bytes 2359304 | tf_op jit(solution)/shard_map/ppermute | solution.py:867
  743.5 28.1 %collective-permute-start.58 = (bf16[256,1536]{1,0:T(8,128)(2,1)}, bf16[256,1536]{1,0:T(8,128)(2,1)S(1)}, u32[]{:S(2)}, u32[]{:S(2)}) collective-permute-start(bf16[256,1536]{1,0:T(8,128)(2,1)} %get-tuple-element.308.refs_2_), channel_id=1, source_target_pairs={{0,1},{3,2},{1,0},{2,3},{4,5},{7,6},{5,4},{6,7},{8,9},{11,10},{9,8... | collective-permute-start | bytes 2359304 | tf_op jit(solution)/shard_map/ppermute | solution.py:867
  744.9 26.7 %collective-permute-start.59 = (bf16[256,1536]{1,0:T(8,128)(2,1)}, bf16[256,1536]{1,0:T(8,128)(2,1)}, u32[]{:S(2)}, u32[]{:S(2)}) collective-permute-start(bf16[256,1536]{1,0:T(8,128)(2,1)} %get-tuple-element.309.refs_15_.refs_4_), channel_id=1, source_target_pairs={{1,2},{2,1},{5,6},{6,5},{9,10},{10,9},{13,14},{14,13},{17,18},{18,... | collective-permute-start | bytes 2359304 | tf_op jit(solution)/shard_map/ppermute | solution.py:867
  778.5 19.8 %collective-permute-start.63 = (bf16[256,1536]{1,0:T(8,128)(2,1)}, bf16[256,1536]{1,0:T(8,128)(2,1)S(1)}, u32[]{:S(2)}, u32[]{:S(2)}) collective-permute-start(bf16[256,1536]{1,0:T(8,128)(2,1)} %get-tuple-element.337.refs_2_), channel_id=1, source_target_pairs={{0,1},{3,2},{1,0},{2,3},{4,5},{7,6},{5,4},{6,7},{8,9},{11,10},{9,8... | collective-permute-start | bytes 2359304 | tf_op jit(solution)/shard_map/ppermute | solution.py:867
  779.7 18.6 %collective-permute-start.64 = (bf16[256,1536]{1,0:T(8,128)(2,1)}, bf16[256,1536]{1,0:T(8,128)(2,1)S(1)}, u32[]{:S(2)}, u32[]{:S(2)}) collective-permute-start(bf16[256,1536]{1,0:T(8,128)(2,1)} %get-tuple-element.338.refs_4_), channel_id=1, source_target_pairs={{1,2},{2,1},{5,6},{6,5},{9,10},{10,9},{13,14},{14,13},{17,18},{18,... | collective-permute-start | bytes 2359304 | tf_op jit(solution)/shard_map/ppermute | solution.py:867
  807.7 18.9 %collective-permute-start.68 = (f32[8,128]{1,0:T(8,128)S(1)}, f32[8,128]{1,0:T(8,128)S(1)}, u32[]{:S(2)}, u32[]{:S(2)}) collective-permute-start(f32[8,128]{1,0:T(8,128)S(1)} %bitcast.94), channel_id=1, source_target_pairs={{0,1},{1,0},{2,3},{3,2},{4,5},{5,4},{6,7},{7,6},{8,9},{9,8},{10,11... | collective-permute-start | bytes 12296 | tf_op jit(solution)/shard_map/ppermute | solution.py:689
  813.9 19.7 %collective-permute-start.65 = (bf16[256,1536]{1,0:T(8,128)(2,1)}, bf16[256,1536]{1,0:T(8,128)(2,1)}, u32[]{:S(2)}, u32[]{:S(2)}) collective-permute-start(bf16[256,1536]{1,0:T(8,128)(2,1)} %get-tuple-element.340.refs_2_), channel_id=1, source_target_pairs={{0,1},{3,2},{1,0},{2,3},{4,5},{7,6},{5,4},{6,7},{8,9},{11,10},{9,8... | collective-permute-start | bytes 2359304 | tf_op jit(solution)/shard_map/ppermute | solution.py:867
  815.0 18.7 %collective-permute-start.66 = (bf16[256,1536]{1,0:T(8,128)(2,1)S(1)}, bf16[256,1536]{1,0:T(8,128)(2,1)}, u32[]{:S(2)}, u32[]{:S(2)}) collective-permute-start(bf16[256,1536]{1,0:T(8,128)(2,1)S(1)} %copy-done.24), channel_id=1, source_target_pairs={{1,2},{2,1},{5,6},{6,5},{9,10},{10,9},{13,14},{14,13},{17,18},{18,... | collective-permute-start | bytes 2359304 | tf_op jit(solution)/shard_map/ppermute | solution.py:867
  836.5 40.2 %collective-permute-start.67 = (bf16[256,1536]{1,0:T(8,128)(2,1)}, bf16[256,1536]{1,0:T(8,128)(2,1)}, u32[]{:S(2)}, u32[]{:S(2)}) collective-permute-start(bf16[256,1536]{1,0:T(8,128)(2,1)} %get-tuple-element.343.refs_2_), channel_id=1, source_target_pairs={{0,1},{3,2},{1,0},{2,3},{4,5},{7,6},{5,4},{6,7},{8,9},{11,10},{9,8... | collective-permute-start | bytes 2359304 | tf_op jit(solution)/shard_map/ppermute | solution.py:867
  (116 other events, 895.6 us)
Sparse Core Ops, SparseCore 0:
  16.7 35.8 all-gather.4
  182.7 45.2 all-gather.6
  507.5 32.6 all-gather.8
  543.6 75.9 reduce-scatter.3
  621.8 118.9 all-reduce.2
  744.4 62.8 reduce-scatter.5
  810.8 53.8 reduce-scatter.7

commit v12 on v10

--- a/solution.py
+++ b/solution.py
@@ -31,7 +31,7 @@
 
 COST = {
     "key": 8, "query": 9, "caption_norm": 2, "pick": 5, "attend": 15, "hop": 3, "ffn": 9, "ffn_back": 10, "out_back": 6,
-    "pair_grad": 10, "caption_back": 6, "dq": 27, "dkv": 24, "dqkv": 7, "caption_grad": 3, "last": 3, "note": 1, "pin": 1,
+    "pair_grad": 10, "caption_back": 6, "dq": 45, "dkv": 24, "dqkv": 7, "caption_grad": 3, "last": 3, "note": 1, "pin": 1,
 }
 
 
@@ -314,11 +314,14 @@
     return jnp.where((lane >= 3 * head) & (lane < 3 * head + 3), -1.0, 0.0).astype(bf16)
 
 
-def dq_kernel(sc, q_ref, d_ref, x_ref, k_ref, v_ref, c_ref, dq_ref, acc):
+def dq_kernel(parts, sc, q_ref, k_ref, v_ref, *refs):
+    d_refs, x_refs, c_refs = (refs[k * parts : (k + 1) * parts] for k in range(3))
+    dq_ref, acc = refs[3 * parts :]
     pair = pl.program_id(0)
     j = pl.program_id(1)
     masks = halves(128)
     keys = 512
+    rows = d_refs[0].shape[0]
 
     @pl.when(j == 0)
     def _():
@@ -326,48 +329,48 @@
 
     @pl.when(j < sc[0])
     def _():
-        q = q_ref[...]
-        dx = jnp.concatenate([d_ref[...], x_ref[...]], 1)
-        total = acc[...]
-        for h in range(2):
-            off = minus_delta(keys, 2 * pair + h)
-            for c in range(k_ref.shape[0] // keys):
-                at = slice(c * keys, (c + 1) * keys)
-                k = keep(k_ref[at, :], masks[h])
-                e = jnp.exp2(mm_nt(q, k))
-                dp = mm_nt(dx, jnp.concatenate([keep(v_ref[at, :], masks[h]), off], 1))
-                total = total + mm((e * dp).astype(bf16), k)
-        acc[...] = total
+        for r in range(parts):
+            mine = slice(r * rows, (r + 1) * rows)
+            q = q_ref[mine, :]
+            dx = jnp.concatenate([d_refs[r][...], x_refs[r][...]], 1)
+            total = acc[mine, :]
+            for h in range(2):
+                off = minus_delta(keys, 2 * pair + h)
+                for c in range(k_ref.shape[0] // keys):
+                    at = slice(c * keys, (c + 1) * keys)
+                    k = keep(k_ref[at, :], masks[h])
+                    e = jnp.exp2(mm_nt(q, k))
+                    dp = mm_nt(dx, jnp.concatenate([keep(v_ref[at, :], masks[h]), off], 1))
+                    total = total + mm((e * dp).astype(bf16), k)
+            acc[mine, :] = total
 
     @pl.when(j == SPAN - 1)
     def _():
-        dq_ref[...] = acc[...] * 0.125 + c_ref[...]
-
-
-def dq_call(order, sc, q, d, k, v, cap_dq, h, after=()):
-    n = q.shape[1]
+        for r in range(parts):
+            mine = slice(r * rows, (r + 1) * rows)
+            dq_ref[mine, :] = acc[mine, :] * 0.125 + c_refs[r][...]
+
+
+def dq_call(order, sc, q, ds, k, v, cap_dqs, after=()):
+    t, n = q.shape
     pairs = n // 128
+    parts = len(ds)
     block = k.shape[0] // SPAN
-    bq = 2 * BR
+    rows = t // parts
     mine = lambda p, j, s: (0, p)
-    extra = lambda p, j, s: (0, pairs)
-    other = lambda p, j, s: (item_block(j, s), p)
+    other = pl.BlockSpec((block, 128), lambda p, j, s: (item_block(j, s), p))
     return order.run(
         "dq",
-        dq_kernel,
+        functools.partial(dq_kernel, parts),
         (pairs, SPAN),
-        (q, d, d, k, v, cap_dq),
-        [
-            pl.BlockSpec((bq, 128), lambda p, j, s: (h, p)),
-            pl.BlockSpec((bq, 128), mine),
-            pl.BlockSpec((bq, 128), extra),
-            pl.BlockSpec((block, 128), other),
-            pl.BlockSpec((block, 128), other),
-            pl.BlockSpec((bq, 128), mine),
-        ],
-        [pl.BlockSpec((bq, 128), mine)],
-        [sds((bq, n), f32)],
-        [pltpu.VMEM((bq, 128), f32)],
+        (q, k, v, *ds, *ds, *cap_dqs),
+        [pl.BlockSpec((t, 128), mine), other, other]
+        + [pl.BlockSpec((rows, 128), mine)] * parts
+        + [pl.BlockSpec((rows, 128), lambda p, j, s: (0, pairs))] * parts
+        + [pl.BlockSpec((rows, 128), mine)] * parts,
+        [pl.BlockSpec((t, 128), mine)],
+        [sds((t, n), f32)],
+        [pltpu.VMEM((t, 128), f32)],
         sc,
         after=after,
     )[0]
@@ -632,7 +635,7 @@
         "dqkv",
         c,
         (dq, *(x for two in dkv for x in two), qr, kr, *tabs, hg, w, patches),
-        [part(c % 2, n)] + [part(c % 2, x.shape[1]) for two in dkv for x in two] + [part(c, n)] * 2 + [part(c, 128)] * 3 + [whole(hg.shape), whole(w.shape), part(c, d)],
+        [part(c, n)] + [part(c % 2, x.shape[1]) for two in dkv for x in two] + [part(c, n)] * 2 + [part(c, 128)] * 3 + [whole(hg.shape), whole(w.shape), part(c, d)],
         [(BR, d, bf16)],
         [(2, n, f32), (1, d, f32)],
         [(t, 3 * n, bf16)],
@@ -733,17 +736,23 @@
 
 class GatherOne:
     def __init__(self, a):
-        self.all = None
+        self.all, self.first, self.second = None, (), ()
         if lax.axis_size("wide") != 8:
-            self.first = self.second = ()
             self.all = [lax.all_gather(a, "wide")]
             return
-        send = lambda x, pairs: lax.ppermute(x, "wide", pairs)
-        a2 = send(a, [(i, i ^ 2) for i in range(8)])
-        a4 = send(a, [(1, 5), (4, 0), (3, 7), (6, 2)])
-        a6 = send(a2, [(0, 4), (1, 5), (6, 2), (7, 3)])
-        self.first, self.second = (a2, a4), (a6,)
-        self.kept = ((a, a2, a4, a6),)
+        a2 = lax.ppermute(a, "wide", [(i, i ^ 2) for i in range(8)])
+        a4 = lax.ppermute(a, "wide", [(1, 5), (4, 0), (3, 7), (6, 2)])
+        self.first, self.own = (a2, a4), a
+
+    def across(self, order=None):
+        if self.all is not None:
+            return
+        a2, a4 = self.first
+        if order is not None:
+            a2 = pin(order, a2)
+        a6 = lax.ppermute(a2, "wide", [(0, 4), (1, 5), (6, 2), (7, 3)])
+        self.second = (a6,)
+        self.kept = ((self.own, a2, a4, a6),)
 
     pieces = Gather.pieces
 
@@ -1077,6 +1086,8 @@
                 early = d_got[h - 1].first if h > 0 else ()
                 mlp_part = pair_grad_call(order, a3, d_gu, d_ffn, hidden, h, len(pairs_of), mlp_part, early)
         d_got[h] = GatherOne(d_scaled[h])
+        if h < pairs_of[-1]:
+            d_got[h].across()
         dq_caps[h], pk, pv, pg = caption_back_call(order, sc, q, d_mixed[2 * h], d_mixed[2 * h + 1], cap, text, tg, h)
         dck, dcv, gate_sum = dck + pk, dcv + pv, gate_sum + pg
     d_attn = whole_out[0]
@@ -1086,11 +1097,8 @@
     cap_sum = jnp.sum(jnp.where(kept, cap_got.astype(f32), 0.0), 0)
     last_half = pairs_of[-1]
 
-    def make_dq(h, after):
-        return dq_call(order, sc, q, d_scaled[h], k_all, v_all, dq_caps[h], h, after)
-
-    for h in pairs_of:
-        dqs[h] = make_dq(h, () if h == 0 else d_got[last_half].first)
+    halves_of = lambda table: [table[h] for h in pairs_of]
+    dq = dq_call(order, sc, q, halves_of(d_scaled), k_all, v_all, halves_of(dq_caps))
 
     d_cap, hs_c = order.run(
         "caption_grad",
@@ -1101,6 +1109,7 @@
         [both_cap, pl.BlockSpec((1, n), lambda i: (0, 0))],
         [sds((text, 2 * n), bf16), sds((1, n), f32)],
     )
+    d_got[last_half].across(order)
     d_text = (mm_nt(d_cap[:, :n], w_caption[0]) + mm_nt(d_cap[:, n:], w_caption[1])).astype(bf16)
     cap_part = mm_tn(captions, d_cap).astype(bf16)
     pieces = -(-d_text.shape[1] // d)
@@ -1118,7 +1127,7 @@
 
     def project(c, dkv, after=()):
         nonlocal whole_out
-        da1_part, p_hs, p1, *whole_out = dqkv_call(order, c, dqs[c // 2], dkv, q_raw, k_raw, tabs, hg, w_qkv, patches, whole_out)
+        da1_part, p_hs, p1, *whole_out = dqkv_call(order, c, dq, dkv, q_raw, k_raw, tabs, hg, w_qkv, patches, whole_out)
         hs_parts.append(p_hs)
         c1_parts.append(p1)
         return da1_part

time: 871 us -> 882 us (1.013); the launches traced: 871 us -> 867 us
  Pallas kernels: 470 us -> 407 us
  blocking collectives: 36.7 us -> 59.3 us
  waiting for transfers between devices: 93.8 us -> 115 us
  starting transfers between devices: 136 us -> 153 us
    pallas_call x70, Pallas kernels: 470 us -> 407 us  [run(): pl.pallas_call(body, grid_spec=pltpu.PrefetchScalarGridSpec(num_scalar_pr...]
    ppermute x0 -> x6, starting transfers between devices: none -> 39.2 us  [the longest x2 23.9 us: across(): a6 = lax.ppermute(a2, 'wide', [(0, 4), (1, 5), (6, 2), (7, 3)])]
    ppermute x13 -> x7, starting transfers between devices: 46 us -> 14.9 us  [__init__(): send = lambda x, pairs: lax.ppermute(x, 'wide', pairs)]
    all_gather x1, blocking collectives: 11.5 us -> 34.1 us  [local(): got = lax.all_gather(folded, 'wide')]
    ppermute x0 -> x6, waiting for transfers between devices: none -> 16.8 us  [the longest x2 9.74 us: across(): a6 = lax.ppermute(a2, 'wide', [(0, 4), (1, 5), (6, 2), (7, 3)])]
    ppermute x22, starting transfers between devices: 13.3 us -> 22.9 us  [swap(): return lax.ppermute(x, axis, [(i, i ^ m) for i in range(size)])]
    unnamed x207 -> x213, local copies, waits for them, and re-layouts: 34.4 us -> 35.4 us
    ppermute x13 -> x7, waiting for transfers between devices: 42.9 us -> 42.8 us  [__init__(): send = lambda x, pairs: lax.ppermute(x, 'wide', pairs)]
  transfers between devices with their start and end apart: 83 -> 83, of which waited for: 15 -> 21; matrix products, arithmetic and copies ran while one was open for 7% -> 7% of each run, Pallas kernels for 45% -> 38%
where the time goes in v12:
time: 882 us; the launch traced here: 867 us
  Pallas kernels  407 us (46%)
  starting transfers between devices  153 us (17%)
  waiting for transfers between devices  115 us (13%)
  blocking collectives  59.3 us (7%)
  local copies, waits for them, and re-layouts  47.3 us (5%)
  other arithmetic  38.5 us (4%)
  matrix products  25.2 us (3%)
  between operations  21.2 us (2%)
    pallas_call x70, Pallas kernels, run(): pl.pallas_call(body, grid_spec=pltpu.PrefetchScalarGridSpec(num_scalar_pr...  407 us
    ppermute x42, starting transfers between devices, step(): go = lambda x, perm: lax.ppermute(x, 'narrow', perm)  76.1 us
    ppermute x42, waiting for transfers between devices, step(): go = lambda x, perm: lax.ppermute(x, 'narrow', perm)  48.4 us
    ppermute x7, waiting for transfers between devices, __init__(): send = lambda x, pairs: lax.ppermute(x, 'wide', pairs)  42.8 us
    unnamed x213, local copies, waits for them, and re-layouts  35.4 us
    all_gather x1, blocking collectives, local(): got = lax.all_gather(folded, 'wide')  34.1 us
    all_gather x2, blocking collectives, gather_now(): lax.all_gather(padded, axis, axis=0, tiled=True).reshape(-1, wide)[:, :n]  25.2 us
    ppermute x2, starting transfers between devices, across(): a6 = lax.ppermute(a2, 'wide', [(0, 4), (1, 5), (6, 2), (7, 3)])  23.9 us
  transfers between devices with their start and end apart: 83, of which 21 were waited for; matrix products, arithmetic and copies ran while one was open for 7% of the time, Pallas kernels for 38%

profile of v12, /device:TPU:0, one launch (start us, length us, event | category | flops | bytes accessed | tf_op | source)
XLA Modules:
  0.0 867.1 jit_solution(10237609586093214312)
XLA Ops:
  26.2 14.9 %all_gather.22 = f32[4,8,256]{2,1,0:T(8,128)S(1)} all-gather(f32[1,8,256]{2,1,0:T(8,128)S(1)} %reshape.309), channel_id=1, replica_groups=mesh['wide'=8,'narrow'=4] {'narrow'}, dimensions={0}, use_global_device_ids=true | all-gather | bytes 40960 | tf_op jit(solution)/shard_map/all_gather | solution.py:846
  41.1 10.3 %all_gather.23 = f32[8,8,896]{2,1,0:T(8,128)S(1)} all-gather(f32[1,8,896]{2,1,0:T(8,128)S(1)} %reshape.311), channel_id=1, replica_groups=mesh['wide'=8,'narrow'=4] {'wide'}, dimensions={0}, use_global_device_ids=true | all-gather | bytes 258048 | tf_op jit(solution)/shard_map/all_gather | solution.py:846
  57.8 13.4 %key.1 = (bf16[1024,1536]{1,0:T(8,128)(2,1)}, f32[1024,384]{1,0:T(8,128)}, bf16[1024,384]{1,0:T(8,128)(2,1)}, bf16[1024,384]{1,0:T(8,128)(2,1)}, f32[1024,384]{1,0:T(8,128)}, /*index=5*/bf16[1024,384]{1,0:T(8,128)(2,1)}) custom-call(bf16[1024,1536]{1,0:T(8,128)(2,1)} %refs_1_.7, f32[4,1536]{1,0:T(4,128)} %maximum_multiply_fusion.1.refs_1_.refs_2_.refs_4_.refs_3_, ...), custom_call_target="tpu_custom_call" | custom-call | flops 2000000000 | bytes 6000000 | tf_op jit(solution)/shard_map/key/pallas_call | solution.py:51
  74.7 17.3 %collective-permute-done.8.refs_11_ = bf16[1024,384]{1,0:T(8,128)(2,1)} collective-permute-done((bf16[1024,384]{1,0:T(8,128)(2,1)}, bf16[1024,384]{1,0:T(8,128)(2,1)}, u32[]{:S(2)}, u32[]{:S(2)}) %collective-permute-start.8) | collective-permute-done | bytes 786464 | tf_op jit(solution)/shard_map/ppermute | solution.py:721
  98.2 10.1 %collective-permute-done.1.refs_3_ = bf16[1024,384]{1,0:T(8,128)(2,1)} collective-permute-done((bf16[1024,384]{1,0:T(8,128)(2,1)}, bf16[1024,384]{1,0:T(8,128)(2,1)}, u32[]{:S(2)}, u32[]{:S(2)}) %collective-permute-start.1) | collective-permute-done | bytes 786464 | tf_op jit(solution)/shard_map/ppermute | solution.py:721
  113.6 5.4 collective-permute-start.5
  120.3 10.1 %collective-permute-done.5.refs_7_ = bf16[1024,384]{1,0:T(8,128)(2,1)} collective-permute-done((bf16[1024,384]{1,0:T(8,128)(2,1)}, bf16[1024,384]{1,0:T(8,128)(2,1)}, u32[]{:S(2)}, u32[]{:S(2)}) %collective-permute-start.5) | collective-permute-done | bytes 786464 | tf_op jit(solution)/shard_map/ppermute | solution.py:721
  135.4 6.5 pick.3
  141.9 11.5 %attend.4 = (bf16[256,384]{1,0:T(8,128)(2,1)}, bf16[256,384]{1,0:T(8,128)(2,1)}, f32[256,384]{1,0:T(8,128)}) custom-call(s32[9]{0:T(128)} %pad_add_fusion.refs_0_, bf16[1024,384]{1,0:T(8,128)(2,1)} %get-tuple-element.188.refs_1_, bf16[4096,384]{1,0:T(8,128)(2,1)} %get-tuple-element.192.refs_2_.refs_7_, bf16[4096,384]{1,0:T(8,128)(2,1)} %get-tuple-element.193.refs_3_, ...), custom_call_target="tpu_custom_call" | custom-call | flops 3750000128 | bytes 11250000 | tf_op jit(solution)/shard_map/attend/pallas_call | solution.py:51
  157.3 11.4 %attend.5 = (bf16[256,384]{1,0:T(8,128)(2,1)}, bf16[256,384]{1,0:T(8,128)(2,1)}, f32[256,384]{1,0:T(8,128)}) custom-call(s32[9]{0:T(128)} %pad_add_fusion.refs_0_, bf16[1024,384]{1,0:T(8,128)(2,1)} %get-tuple-element.188.refs_1_, bf16[4096,384]{1,0:T(8,128)(2,1)} %get-tuple-element.192.refs_2_.refs_7_, bf16[4096,384]{1,0:T(8,128)(2,1)} %get-tuple-element.193.refs_3_, ...), custom_call_target="tpu_custom_call" | custom-call | flops 3750000128 | bytes 11250000 | tf_op jit(solution)/shard_map/attend/pallas_call | solution.py:51
  180.8 11.4 %attend.6 = (bf16[256,384]{1,0:T(8,128)(2,1)}, bf16[256,384]{1,0:T(8,128)(2,1)}, f32[256,384]{1,0:T(8,128)}) custom-call(s32[9]{0:T(128)} %pad_add_fusion.refs_0_, bf16[1024,384]{1,0:T(8,128)(2,1)} %get-tuple-element.188.refs_1_, bf16[4096,384]{1,0:T(8,128)(2,1)} %get-tuple-element.192.refs_2_.refs_7_, bf16[4096,384]{1,0:T(8,128)(2,1)} %get-tuple-element.193.refs_3_, ...), custom_call_target="tpu_custom_call" | custom-call | flops 3750000128 | bytes 11250000 | tf_op jit(solution)/shard_map/attend/pallas_call | solution.py:51
  207.0 11.4 %attend.7 = (bf16[256,384]{1,0:T(8,128)(2,1)}, bf16[256,384]{1,0:T(8,128)(2,1)}, f32[256,384]{1,0:T(8,128)}) custom-call(s32[9]{0:T(128)} %pad_add_fusion.refs_0_, bf16[1024,384]{1,0:T(8,128)(2,1)} %get-tuple-element.188.refs_1_, bf16[4096,384]{1,0:T(8,128)(2,1)} %get-tuple-element.192.refs_2_.refs_7_, bf16[4096,384]{1,0:T(8,128)(2,1)} %get-tuple-element.193.refs_3_, ...), custom_call_target="tpu_custom_call" | custom-call | flops 3750000128 | bytes 11250000 | tf_op jit(solution)/shard_map/attend/pallas_call | solution.py:51
  232.1 8.5 ffn.4
  240.6 6.3 collective-permute-done.20.refs_1_
  255.6 8.5 ffn.5
  264.1 5.7 collective-permute-done.22.refs_1_
  278.5 8.5 ffn.6
  300.6 8.5 ffn.7
  321.9 9.6 %ffn_back.4 = (bf16[256,1536]{1,0:T(8,128)(2,1)}, f32[1,1536]{1,0:T(1,128)}, bf16[1024,1536]{1,0:T(8,128)(2,1)}, bf16[1024,1536]{1,0:T(8,128)(2,1)}, bf16[1024,2048]{1,0:T(8,128)(2,1)}) custom-call(bf16[256,1536]{1,0:T(8,128)(2,1)} %get-tuple-element.230.refs_0_.refs_7_, f32[256,1536]{1,0:T(8,128)} %get-tuple-element.206.refs_7_.refs_1_, ...), custom_call_target="tpu_custom_call" | custom-call | flops 2500000000 | bytes 7500000 | tf_op jit(solution)/shard_map/ffn_back/pallas_call | solution.py:51
  341.9 9.6 %ffn_back.5 = (bf16[256,1536]{1,0:T(8,128)(2,1)}, f32[1,1536]{1,0:T(1,128)}, bf16[1024,1536]{1,0:T(8,128)(2,1)}, bf16[1024,1536]{1,0:T(8,128)(2,1)}, bf16[1024,2048]{1,0:T(8,128)(2,1)}) custom-call(bf16[256,1536]{1,0:T(8,128)(2,1)} %get-tuple-element.235.refs_0_.refs_7_, ...), custom_call_target="tpu_custom_call", output_to_operand_aliasing={{2}: (8, {}), {3}: (9, {}), {4}: (10, {})} | custom-call | flops 2500000000 | bytes 7500000 | tf_op jit(solution)/shard_map/ffn_back/pallas_call | solution.py:51
  361.2 9.6 %ffn_back.6 = (bf16[256,1536]{1,0:T(8,128)(2,1)}, f32[1,1536]{1,0:T(1,128)}, bf16[1024,1536]{1,0:T(8,128)(2,1)}, bf16[1024,1536]{1,0:T(8,128)(2,1)}, bf16[1024,2048]{1,0:T(8,128)(2,1)}) custom-call(bf16[256,1536]{1,0:T(8,128)(2,1)} %get-tuple-element.243.refs_0_.refs_7_, ...), custom_call_target="tpu_custom_call", output_to_operand_aliasing={{2}: (8, {}), {3}: (9, {}), {4}: (10, {})} | custom-call | flops 2500000000 | bytes 7500000 | tf_op jit(solution)/shard_map/ffn_back/pallas_call | solution.py:51
  380.0 9.6 %ffn_back.7 = (bf16[256,1536]{1,0:T(8,128)(2,1)}, f32[1,1536]{1,0:T(1,128)}, bf16[1024,1536]{1,0:T(8,128)(2,1)}, bf16[1024,1536]{1,0:T(8,128)(2,1)}, bf16[1024,2048]{1,0:T(8,128)(2,1)}) custom-call(bf16[256,1536]{1,0:T(8,128)(2,1)} %get-tuple-element.249.refs_0_.refs_7_, ...), custom_call_target="tpu_custom_call", output_to_operand_aliasing={{2}: (8, {}), {3}: (9, {}), {4}: (10, {})} | custom-call | flops 2500000000 | bytes 7500000 | tf_op jit(solution)/shard_map/ffn_back/pallas_call | solution.py:51
  398.4 5.6 out_back.4
  404.0 9.9 %pair_grad.3.refs_6_.refs_7_ = bf16[1536,3072]{1,0:T(8,128)(2,1)} custom-call(bf16[1024,1536]{1,0:T(8,128)(2,1)} %get-tuple-element.264.refs_0_, bf16[1024,2048]{1,0:T(8,128)(2,1)} %get-tuple-element.265.refs_1_, bf16[1024,1536]{1,0:T(8,128)(2,1)} %get-tuple-element.266.refs_2_, bf16[1024,1024]{1,0:T(8,128)(2,1)} %get-tuple-element.267.refs_3_, ...), custom_call_target="tpu_custom_call" | custom-call | flops 2500000000 | bytes 7500000 | tf_op jit(solution)/shard_map/pair_grad/pallas_call | solution.py:51
  420.9 5.6 out_back.5
  426.5 12.7 %collective-permute-start.41 = (bf16[512,512]{1,0:T(8,128)(2,1)}, bf16[512,512]{1,0:T(8,128)(2,1)S(1)}, u32[]{:S(2)}, u32[]{:S(2)}) collective-permute-start(bf16[512,512]{1,0:T(8,128)(2,1)} %get-tuple-element.287.refs_4_.refs_6_.refs_1_), channel_id=1, source_target_pairs={{0,8},{4,12},{8,0},{12,4},{16,24},{20,28},{24,16},{28,20},{1,9},{5... | collective-permute-start | bytes 1572872 | tf_op jit(solution)/shard_map/ppermute | solution.py:743
  439.2 6.2 caption_back.2
  452.7 6.5 collective-permute-start.43
  459.2 5.6 out_back.6
  464.9 9.9 %pair_grad.4.refs_3_.refs_1_ = bf16[1536,3072]{1,0:T(8,128)(2,1)} custom-call(bf16[1024,1536]{1,0:T(8,128)(2,1)} %get-tuple-element.264.refs_0_, bf16[1024,2048]{1,0:T(8,128)(2,1)} %get-tuple-element.265.refs_1_, bf16[1024,1536]{1,0:T(8,128)(2,1)} %get-tuple-element.266.refs_2_, ...), custom_call_target="tpu_custom_call", output_to_operand_aliasing={{}: (7, {})} | custom-call | flops 2500000000 | bytes 7500000 | tf_op jit(solution)/shard_map/pair_grad/pallas_call | solution.py:51
  477.8 5.6 out_back.7
  483.4 6.4 caption_back.3
  494.9 28.5 %dq.1.refs_4_.refs_0_ = f32[1024,384]{1,0:T(8,128)} custom-call(s32[9]{0:T(128)} %pad_add_fusion.refs_0_, bf16[1024,384]{1,0:T(8,128)(2,1)} %get-tuple-element.188.refs_1_, bf16[4096,384]{1,0:T(8,128)(2,1)} %get-tuple-element.192.refs_2_.refs_7_, bf16[4096,384]{1,0:T(8,128)(2,1)} %get-tuple-element.193.refs_3_, ...), custom_call_target="tpu_custom_call" | custom-call | flops 11249999872 | bytes 33750000 | tf_op jit(solution)/shard_map/dq/pallas_call | solution.py:51
  541.4 17.4 %collective-permute-start.50 = (bf16[512,512]{1,0:T(8,128)(2,1)S(1)}, bf16[512,512]{1,0:T(8,128)(2,1)S(1)}, u32[]{:S(2)}, u32[]{:S(2)}) collective-permute-start(bf16[512,512]{1,0:T(8,128)(2,1)S(1)} %copy-done.6), channel_id=1, source_target_pairs={{0,16},{4,20},{24,8},{28,12},{1,17},{5,21},{25,9},{29,13},{2,18},{... | collective-permute-start | bytes 1572872 | tf_op jit(solution)/shard_map/ppermute | solution.py:753
  560.7 7.0 collective-permute-done.48.refs_5_
  572.5 9.7 %collective-permute-done.50.refs_7_ = bf16[512,512]{1,0:T(8,128)(2,1)S(1)} collective-permute-done((bf16[512,512]{1,0:T(8,128)(2,1)S(1)}, bf16[512,512]{1,0:T(8,128)(2,1)S(1)}, u32[]{:S(2)}, u32[]{:S(2)}) %collective-permute-start.50) | collective-permute-done | bytes 524320 | tf_op jit(solution)/shard_map/ppermute | solution.py:753
  606.6 21.2 %dkv.4 = (f32[512,384]{1,0:T(8,128)}, f32[512,384]{1,0:T(8,128)}) custom-call(s32[9]{0:T(128)} %pad_add_fusion.refs_0_, bf16[1024,384]{1,0:T(8,128)(2,1)} %get-tuple-element.189.refs_1_, bf16[1024,384]{1,0:T(8,128)(2,1)} %get-tuple-element.190.refs_9_.refs_2_, bf16[8192,384]{1,0:T(8,128)(2,1)} %all-gather.9.cloned.1.call-done.refs_3_, ...), custom_call_target="tpu_custom_call" | custom-call | flops 6000000000 | bytes 18000000 | tf_op jit(solution)/shard_map/dkv/pallas_call | solution.py:51
  634.0 5.9 collective-permute-start.58
  640.9 6.7 dqkv.4
  647.5 7.9 dkv.5
  665.1 7.0 dqkv.5
  672.2 7.9 dkv.6
  689.9 7.9 dkv.7
  697.8 7.6 dqkv.6
  713.8 6.6 dqkv.7
  726.5 11.1 %pair_grad.5.refs_7_.refs_1_ = bf16[1536,1536]{1,0:T(8,128)(2,1)} custom-call(bf16[1024,1536]{1,0:T(8,128)(2,1)} %get-tuple-element.191.refs_17_.refs_0_, bf16[1024,1152]{1,0:T(8,128)(2,1)} %get-tuple-element.330.refs_1_, bf16[1024,1536]{1,0:T(8,128)(2,1)} %get-tuple-element.331.refs_2_, bf16[1024,384]{1,0:T(8,128)(2,1)} %pad_maximum_fusion.2.refs_3_, ...), custom_call_target="tpu_custom_call" | custom-call | flops 2500000000 | bytes 7500000 | tf_op jit(solution)/shard_map/pair_grad/pallas_call | solution.py:51
  760.2 34.1 %all-gather = f32[64,1536]{1,0:T(8,128)} all-gather(f32[8,1536]{1,0:T(8,128)S(1)} %copy-done.78), channel_id=2, replica_groups=mesh['wide'=8,'narrow'=4] {'wide'}, dimensions={0}, use_global_device_ids=true | all-gather | bytes 442368 | tf_op jit(solution)/shard_map/all_gather | solution.py:1158
  840.6 7.7 collective-permute-done.73.refs_1_
  (499 shorter events, 359.7 us)
Async XLA Ops:
  7.2 134.7 %all-gather.5.cloned.1.call-start = ((), (), s32[]{:S(2)}) async-start(), calls=%async_computation.3 | async-start | bytes 3538944 | tf_op jit(solution)/shard_map/all_gather | solution.py:1034
  16.6 510.4 %all-gather.7.cloned.1.call-start = ((), (), s32[]{:S(2)}) async-start(), calls=%async_computation.4 | async-start | bytes 3538944 | tf_op jit(solution)/shard_map/all_gather | solution.py:1095
  71.2 20.8 %collective-permute-start.8 = (bf16[1024,384]{1,0:T(8,128)(2,1)}, bf16[1024,384]{1,0:T(8,128)(2,1)}, u32[]{:S(2)}, u32[]{:S(2)}) collective-permute-start(bf16[1024,384]{1,0:T(8,128)(2,1)} %get-tuple-element.190.refs_9_.refs_2_), channel_id=1, source_target_pairs={{0,8},{4,12},{8,0},{12,4},{16,24},{20,28},{24,16},{28,20},{1,9},{5... | collective-permute-start | bytes 2359304 | tf_op jit(solution)/shard_map/ppermute | solution.py:721
  72.6 22.9 %collective-permute-start.10 = (bf16[1024,384]{1,0:T(8,128)(2,1)}, bf16[1024,384]{1,0:T(8,128)(2,1)S(1)}, u32[]{:S(2)}, u32[]{:S(2)}) collective-permute-start(bf16[1024,384]{1,0:T(8,128)(2,1)} %get-tuple-element.190.refs_9_.refs_2_), channel_id=1, source_target_pairs={{4,20},{16,0},{12,28},{24,8},{5,21},{17,1},{13,29},{25,9},{6,22},{... | collective-permute-start | bytes 2359304 | tf_op jit(solution)/shard_map/ppermute | solution.py:721
  73.8 34.4 %collective-permute-start.1 = (bf16[1024,384]{1,0:T(8,128)(2,1)}, bf16[1024,384]{1,0:T(8,128)(2,1)}, u32[]{:S(2)}, u32[]{:S(2)}) collective-permute-start(bf16[1024,384]{1,0:T(8,128)(2,1)} %get-tuple-element.189.refs_1_), channel_id=1, source_target_pairs={{0,8},{4,12},{8,0},{12,4},{16,24},{20,28},{24,16},{28,20},{1,9},{5... | collective-permute-start | bytes 2359304 | tf_op jit(solution)/shard_map/ppermute | solution.py:721
  92.0 21.6 %collective-permute-start.12 = (bf16[1024,384]{1,0:T(8,128)(2,1)}, bf16[1024,384]{1,0:T(8,128)(2,1)S(1)}, u32[]{:S(2)}, u32[]{:S(2)}) collective-permute-start(bf16[1024,384]{1,0:T(8,128)(2,1)} %collective-permute-done.8.refs_11_), channel_id=1, source_target_pairs={{0,16},{28,12},{1,17},{29,13},{2,18},{30,14},{3,19},{31,15}} | collective-permute-start | bytes 2359304 | tf_op jit(solution)/shard_map/ppermute | solution.py:721
  95.5 23.5 %collective-permute-start.13 = (bf16[1024,384]{1,0:T(8,128)(2,1)S(1)}, bf16[1024,384]{1,0:T(8,128)(2,1)S(1)}, u32[]{:S(2)}, u32[]{:S(2)}) collective-permute-start(bf16[1024,384]{1,0:T(8,128)(2,1)S(1)} %collective-permute-done.10.refs_13_), channel_id=1, source_target_pairs={{28,20},{0,8},{29,21},{1,9},{30,22},{2,10},{31,23},{3,11}} | collective-permute-start | bytes 2359304 | tf_op jit(solution)/shard_map/ppermute | solution.py:721
  96.8 22.4 %collective-permute-start.3 = (bf16[1024,384]{1,0:T(8,128)(2,1)}, bf16[1024,384]{1,0:T(8,128)(2,1)}, u32[]{:S(2)}, u32[]{:S(2)}) collective-permute-start(bf16[1024,384]{1,0:T(8,128)(2,1)} %get-tuple-element.189.refs_1_), channel_id=1, source_target_pairs={{4,20},{16,0},{12,28},{24,8},{5,21},{17,1},{13,29},{25,9},{6,22},{... | collective-permute-start | bytes 2359304 | tf_op jit(solution)/shard_map/ppermute | solution.py:721
  98.1 21.7 %collective-permute-start = (bf16[1024,384]{1,0:T(8,128)(2,1)}, bf16[1024,384]{1,0:T(8,128)(2,1)S(1)}, u32[]{:S(2)}, u32[]{:S(2)}) collective-permute-start(bf16[1024,384]{1,0:T(8,128)(2,1)} %get-tuple-element.189.refs_1_), channel_id=1, source_target_pairs={{0,4},{4,0},{8,12},{12,8},{16,20},{20,16},{24,28},{28,24},{1,5},{5... | collective-permute-start | bytes 2359304 | tf_op jit(solution)/shard_map/ppermute | solution.py:692
  155.8 20.3 %collective-permute-start.15 = (bf16[256,1536]{1,0:T(8,128)(2,1)}, bf16[256,1536]{1,0:T(8,128)(2,1)}, u32[]{:S(2)}, u32[]{:S(2)}) collective-permute-start(bf16[256,1536]{1,0:T(8,128)(2,1)} %convolution_convert_fusion.4.refs_2_), channel_id=1, source_target_pairs={{0,1},{3,2},{1,0},{2,3},{4,5},{7,6},{5,4},{6,7},{8,9},{11,10},{9,8... | collective-permute-start | bytes 2359304 | tf_op jit(solution)/shard_map/ppermute | solution.py:876
  178.6 19.4 %collective-permute-start.16 = (bf16[256,1536]{1,0:T(8,128)(2,1)}, bf16[256,1536]{1,0:T(8,128)(2,1)S(1)}, u32[]{:S(2)}, u32[]{:S(2)}) collective-permute-start(bf16[256,1536]{1,0:T(8,128)(2,1)} %get-tuple-element.196), channel_id=1, source_target_pairs={{0,1},{3,2},{1,0},{2,3},{4,5},{7,6},{5,4},{6,7},{8,9},{11,10},{9,8... | collective-permute-start | bytes 2359304 | tf_op jit(solution)/shard_map/ppermute | solution.py:876
  202.8 20.2 %collective-permute-start.18 = (bf16[256,1536]{1,0:T(8,128)(2,1)}, bf16[256,1536]{1,0:T(8,128)(2,1)S(1)}, u32[]{:S(2)}, u32[]{:S(2)}) collective-permute-start(bf16[256,1536]{1,0:T(8,128)(2,1)} %get-tuple-element.199.refs_2_), channel_id=1, source_target_pairs={{0,1},{3,2},{1,0},{2,3},{4,5},{7,6},{5,4},{6,7},{8,9},{11,10},{9,8... | collective-permute-start | bytes 2359304 | tf_op jit(solution)/shard_map/ppermute | solution.py:876
  228.3 18.6 %collective-permute-start.20 = (bf16[256,1536]{1,0:T(8,128)(2,1)}, bf16[256,1536]{1,0:T(8,128)(2,1)S(1)}, u32[]{:S(2)}, u32[]{:S(2)}) collective-permute-start(bf16[256,1536]{1,0:T(8,128)(2,1)} %get-tuple-element.202.refs_2_), channel_id=1, source_target_pairs={{0,1},{3,2},{1,0},{2,3},{4,5},{7,6},{5,4},{6,7},{8,9},{11,10},{9,8... | collective-permute-start | bytes 2359304 | tf_op jit(solution)/shard_map/ppermute | solution.py:876
  394.2 19.7 %collective-permute-start.36 = (bf16[256,1536]{1,0:T(8,128)(2,1)}, bf16[256,1536]{1,0:T(8,128)(2,1)S(1)}, u32[]{:S(2)}, u32[]{:S(2)}) collective-permute-start(bf16[256,1536]{1,0:T(8,128)(2,1)} %get-tuple-element.262.refs_2_), channel_id=1, source_target_pairs={{0,1},{3,2},{1,0},{2,3},{4,5},{7,6},{5,4},{6,7},{8,9},{11,10},{9,8... | collective-permute-start | bytes 2359304 | tf_op jit(solution)/shard_map/ppermute | solution.py:876
  418.9 26.6 %collective-permute-start.38 = (bf16[256,1536]{1,0:T(8,128)(2,1)}, bf16[256,1536]{1,0:T(8,128)(2,1)S(1)}, u32[]{:S(2)}, u32[]{:S(2)}) collective-permute-start(bf16[256,1536]{1,0:T(8,128)(2,1)} %get-tuple-element.277.refs_2_), channel_id=1, source_target_pairs={{0,1},{3,2},{1,0},{2,3},{4,5},{7,6},{5,4},{6,7},{8,9},{11,10},{9,8... | collective-permute-start | bytes 2359304 | tf_op jit(solution)/shard_map/ppermute | solution.py:876
  420.2 25.3 %collective-permute-start.39 = (bf16[256,1536]{1,0:T(8,128)(2,1)}, bf16[256,1536]{1,0:T(8,128)(2,1)S(1)}, u32[]{:S(2)}, u32[]{:S(2)}) collective-permute-start(bf16[256,1536]{1,0:T(8,128)(2,1)} %get-tuple-element.278.refs_4_), channel_id=1, source_target_pairs={{1,2},{2,1},{5,6},{6,5},{9,10},{10,9},{13,14},{14,13},{17,18},{18,... | collective-permute-start | bytes 2359304 | tf_op jit(solution)/shard_map/ppermute | solution.py:876
  426.5 26.2 %collective-permute-start.41 = (bf16[512,512]{1,0:T(8,128)(2,1)}, bf16[512,512]{1,0:T(8,128)(2,1)S(1)}, u32[]{:S(2)}, u32[]{:S(2)}) collective-permute-start(bf16[512,512]{1,0:T(8,128)(2,1)} %get-tuple-element.287.refs_4_.refs_6_.refs_1_), channel_id=1, source_target_pairs={{0,8},{4,12},{8,0},{12,4},{16,24},{20,28},{24,16},{28,20},{1,9},{5... | collective-permute-start | bytes 1572872 | tf_op jit(solution)/shard_map/ppermute | solution.py:743
  449.4 25.4 %collective-permute-start.40 = (bf16[256,1536]{1,0:T(8,128)(2,1)}, bf16[256,1536]{1,0:T(8,128)(2,1)S(1)}, u32[]{:S(2)}, u32[]{:S(2)}) collective-permute-start(bf16[256,1536]{1,0:T(8,128)(2,1)} %get-tuple-element.285.refs_2_), channel_id=1, source_target_pairs={{0,1},{3,2},{1,0},{2,3},{4,5},{7,6},{5,4},{6,7},{8,9},{11,10},{9,8... | collective-permute-start | bytes 2359304 | tf_op jit(solution)/shard_map/ppermute | solution.py:876
  452.7 22.1 %collective-permute-start.43 = (bf16[512,512]{1,0:T(8,128)(2,1)S(1)}, bf16[512,512]{1,0:T(8,128)(2,1)}, u32[]{:S(2)}, u32[]{:S(2)}) collective-permute-start(bf16[512,512]{1,0:T(8,128)(2,1)S(1)} %collective-permute-done.41.refs_5_.refs_3_), channel_id=1, source_target_pairs={{0,16},{4,20},{24,8},{28,12},{1,17},{5,21},{25,9},{29,13},{2,18},{... | collective-permute-start | bytes 1572872 | tf_op jit(solution)/shard_map/ppermute | solution.py:753
  492.8 113.8 %all-gather.9.cloned.1.call-start = ((), (), s32[]{:S(2)}) async-start(), calls=%async_computation.5 | async-start | bytes 7077888 | tf_op jit(solution)/shard_map/all_gather | solution.py:1043
  493.5 244.1 %reduce-scatter.4.cloned.1.call-start = ((), (), s32[]{:S(2)}) async-start(), calls=%async_computation.6 | async-start | bytes 10616832 | tf_op jit(solution)/shard_map/reduce_scatter | solution.py:938
  493.8 47.6 %collective-permute-start.52 = (bf16[512,512]{1,0:T(8,128)(2,1)}, bf16[512,512]{1,0:T(8,128)(2,1)}, u32[]{:S(2)}, u32[]{:S(2)}) collective-permute-start(bf16[512,512]{1,0:T(8,128)(2,1)} %get-tuple-element.287.refs_4_.refs_6_.refs_1_), channel_id=1, source_target_pairs={{0,4},{4,0},{8,12},{12,8},{16,20},{20,16},{24,28},{28,24},{1,5},{5... | collective-permute-start | bytes 1572872 | tf_op jit(solution)/shard_map/ppermute | solution.py:692
  493.9 66.4 %collective-permute-start.53 = (bf16[512,512]{1,0:T(8,128)(2,1)S(1)}, bf16[512,512]{1,0:T(8,128)(2,1)}, u32[]{:S(2)}, u32[]{:S(2)}) collective-permute-start(bf16[512,512]{1,0:T(8,128)(2,1)S(1)} %copy-done.16), channel_id=1, source_target_pairs={{0,4},{4,0},{8,12},{12,8},{16,20},{20,16},{24,28},{28,24},{1,5},{5... | collective-permute-start | bytes 1572872 | tf_op jit(solution)/shard_map/ppermute | solution.py:692
  494.3 65.9 %collective-permute-start.54 = (bf16[512,512]{1,0:T(8,128)(2,1)}, bf16[512,512]{1,0:T(8,128)(2,1)}, u32[]{:S(2)}, u32[]{:S(2)}) collective-permute-start(bf16[512,512]{1,0:T(8,128)(2,1)} %collective-permute-done.42.refs_6_.refs_5_), channel_id=1, source_target_pairs={{0,4},{4,0},{8,12},{12,8},{16,20},{20,16},{24,28},{28,24},{1,5},{5... | collective-permute-start | bytes 1572872 | tf_op jit(solution)/shard_map/ppermute | solution.py:692
  494.4 78.1 %collective-permute-start.55 = (bf16[512,512]{1,0:T(8,128)(2,1)}, bf16[512,512]{1,0:T(8,128)(2,1)}, u32[]{:S(2)}, u32[]{:S(2)}) collective-permute-start(bf16[512,512]{1,0:T(8,128)(2,1)} %collective-permute-done.43.refs_4_.refs_7_), channel_id=1, source_target_pairs={{0,4},{4,0},{8,12},{12,8},{16,20},{20,16},{24,28},{28,24},{1,5},{5... | collective-permute-start | bytes 1572872 | tf_op jit(solution)/shard_map/ppermute | solution.py:692
  494.9 41.9 %collective-permute-start.46 = (bf16[512,512]{1,0:T(8,128)(2,1)}, bf16[512,512]{1,0:T(8,128)(2,1)S(1)}, u32[]{:S(2)}, u32[]{:S(2)}) collective-permute-start(bf16[512,512]{1,0:T(8,128)(2,1)} %get-tuple-element.297.refs_5_.refs_7_.refs_1_), channel_id=1, source_target_pairs={{0,8},{4,12},{8,0},{12,4},{16,24},{20,28},{24,16},{28,20},{1,9},{5... | collective-permute-start | bytes 1572872 | tf_op jit(solution)/shard_map/ppermute | solution.py:743
  536.8 31.0 %collective-permute-start.48 = (bf16[512,512]{1,0:T(8,128)(2,1)}, bf16[512,512]{1,0:T(8,128)(2,1)}, u32[]{:S(2)}, u32[]{:S(2)}) collective-permute-start(bf16[512,512]{1,0:T(8,128)(2,1)} %get-tuple-element.297.refs_5_.refs_7_.refs_1_), channel_id=1, source_target_pairs={{4,20},{16,0},{12,28},{24,8},{5,21},{17,1},{13,29},{25,9},{6,22},{... | collective-permute-start | bytes 1572872 | tf_op jit(solution)/shard_map/ppermute | solution.py:744
  541.4 40.8 %collective-permute-start.50 = (bf16[512,512]{1,0:T(8,128)(2,1)S(1)}, bf16[512,512]{1,0:T(8,128)(2,1)S(1)}, u32[]{:S(2)}, u32[]{:S(2)}) collective-permute-start(bf16[512,512]{1,0:T(8,128)(2,1)S(1)} %copy-done.6), channel_id=1, source_target_pairs={{0,16},{4,20},{24,8},{28,12},{1,17},{5,21},{25,9},{29,13},{2,18},{... | collective-permute-start | bytes 1572872 | tf_op jit(solution)/shard_map/ppermute | solution.py:753
  560.2 40.8 %collective-permute-start.44 = (bf16[256,1536]{1,0:T(8,128)(2,1)S(1)}, bf16[256,1536]{1,0:T(8,128)(2,1)S(1)}, u32[]{:S(2)}, u32[]{:S(2)}) collective-permute-start(bf16[256,1536]{1,0:T(8,128)(2,1)S(1)} %get-tuple-element.422.refs_2_), channel_id=1, source_target_pairs={{0,1},{3,2},{1,0},{2,3},{4,5},{7,6},{5,4},{6,7},{8,9},{11,10},{9,8... | collective-permute-start | bytes 2359304 | tf_op jit(solution)/shard_map/ppermute | solution.py:876
  560.2 35.3 %collective-permute-start.45 = (bf16[512,512]{1,0:T(8,128)(2,1)}, bf16[512,512]{1,0:T(8,128)(2,1)S(1)}, u32[]{:S(2)}, u32[]{:S(2)}) collective-permute-start(bf16[512,512]{1,0:T(8,128)(2,1)} %get-tuple-element.297.refs_5_.refs_7_.refs_1_), channel_id=1, source_target_pairs={{0,4},{4,0},{8,12},{12,8},{16,20},{20,16},{24,28},{28,24},{1,5},{5... | collective-permute-start | bytes 1572872 | tf_op jit(solution)/shard_map/ppermute | solution.py:692
  567.7 27.8 %collective-permute-start.49 = (bf16[512,512]{1,0:T(8,128)(2,1)}, bf16[512,512]{1,0:T(8,128)(2,1)S(1)}, u32[]{:S(2)}, u32[]{:S(2)}) collective-permute-start(bf16[512,512]{1,0:T(8,128)(2,1)} %collective-permute-done.48.refs_5_), channel_id=1, source_target_pairs={{0,4},{4,0},{8,12},{12,8},{16,20},{20,16},{24,28},{28,24},{1,5},{5... | collective-permute-start | bytes 1572872 | tf_op jit(solution)/shard_map/ppermute | solution.py:692
  572.5 23.0 %collective-permute-start.47 = (bf16[512,512]{1,0:T(8,128)(2,1)S(1)}, bf16[512,512]{1,0:T(8,128)(2,1)S(1)}, u32[]{:S(2)}, u32[]{:S(2)}) collective-permute-start(bf16[512,512]{1,0:T(8,128)(2,1)S(1)} %copy-done.6), channel_id=1, source_target_pairs={{0,4},{4,0},{8,12},{12,8},{16,20},{20,16},{24,28},{28,24},{1,5},{5... | collective-permute-start | bytes 1572872 | tf_op jit(solution)/shard_map/ppermute | solution.py:692
  604.5 144.4 %reduce-scatter.6.cloned.1.call-start = ((), (), s32[]{:S(2)}) async-start(), calls=%async_computation.7 | async-start | bytes 7077888 | tf_op jit(solution)/shard_map/reduce_scatter | solution.py:938
  604.6 23.2 %collective-permute-start.56 = (bf16[256,1536]{1,0:T(8,128)(2,1)}, bf16[256,1536]{1,0:T(8,128)(2,1)S(1)}, u32[]{:S(2)}, u32[]{:S(2)}) collective-permute-start(bf16[256,1536]{1,0:T(8,128)(2,1)} %get-tuple-element.300), channel_id=1, source_target_pairs={{0,1},{3,2},{1,0},{2,3},{4,5},{7,6},{5,4},{6,7},{8,9},{11,10},{9,8... | collective-permute-start | bytes 2359304 | tf_op jit(solution)/shard_map/ppermute | solution.py:876
  605.6 22.2 %collective-permute-start.57 = (bf16[256,1536]{1,0:T(8,128)(2,1)S(1)}, bf16[256,1536]{1,0:T(8,128)(2,1)S(1)}, u32[]{:S(2)}, u32[]{:S(2)}) collective-permute-start(bf16[256,1536]{1,0:T(8,128)(2,1)S(1)} %copy-done.8), channel_id=1, source_target_pairs={{1,2},{2,1},{5,6},{6,5},{9,10},{10,9},{13,14},{14,13},{17,18},{18,... | collective-permute-start | bytes 2359304 | tf_op jit(solution)/shard_map/ppermute | solution.py:876
  632.2 216.2 %reduce-scatter.8.cloned.1.call-start = ((), (), s32[]{:S(2)}) async-start(), calls=%async_computation.8 | async-start | bytes 5308416 | tf_op jit(solution)/shard_map/reduce_scatter | solution.py:938
  633.2 23.6 %collective-permute-start.59 = (bf16[256,1536]{1,0:T(8,128)(2,1)S(1)}, bf16[256,1536]{1,0:T(8,128)(2,1)S(1)}, u32[]{:S(2)}, u32[]{:S(2)}) collective-permute-start(bf16[256,1536]{1,0:T(8,128)(2,1)S(1)} %copy-done.12), channel_id=1, source_target_pairs={{1,2},{2,1},{5,6},{6,5},{9,10},{10,9},{13,14},{14,13},{17,18},{18,... | collective-permute-start | bytes 2359304 | tf_op jit(solution)/shard_map/ppermute | solution.py:876
  634.0 22.9 %collective-permute-start.58 = (bf16[256,1536]{1,0:T(8,128)(2,1)S(1)}, bf16[256,1536]{1,0:T(8,128)(2,1)S(1)}, u32[]{:S(2)}, u32[]{:S(2)}) collective-permute-start(bf16[256,1536]{1,0:T(8,128)(2,1)S(1)} %copy-done.28), channel_id=1, source_target_pairs={{0,1},{3,2},{1,0},{2,3},{4,5},{7,6},{5,4},{6,7},{8,9},{11,10},{9,8... | collective-permute-start | bytes 2359304 | tf_op jit(solution)/shard_map/ppermute | solution.py:876
  684.7 20.7 %collective-permute-start.62 = (bf16[256,1536]{1,0:T(8,128)(2,1)}, bf16[256,1536]{1,0:T(8,128)(2,1)S(1)}, u32[]{:S(2)}, u32[]{:S(2)}) collective-permute-start(bf16[256,1536]{1,0:T(8,128)(2,1)} %get-tuple-element.316.refs_2_), channel_id=1, source_target_pairs={{0,1},{3,2},{1,0},{2,3},{4,5},{7,6},{5,4},{6,7},{8,9},{11,10},{9,8... | collective-permute-start | bytes 2359304 | tf_op jit(solution)/shard_map/ppermute | solution.py:876
  710.0 27.5 %collective-permute-start.64 = (bf16[256,1536]{1,0:T(8,128)(2,1)}, bf16[256,1536]{1,0:T(8,128)(2,1)S(1)}, u32[]{:S(2)}, u32[]{:S(2)}) collective-permute-start(bf16[256,1536]{1,0:T(8,128)(2,1)} %get-tuple-element.325.refs_2_), channel_id=1, source_target_pairs={{0,1},{3,2},{1,0},{2,3},{4,5},{7,6},{5,4},{6,7},{8,9},{11,10},{9,8... | collective-permute-start | bytes 2359304 | tf_op jit(solution)/shard_map/ppermute | solution.py:876
  712.3 25.3 %collective-permute-start.65 = (bf16[256,1536]{1,0:T(8,128)(2,1)}, bf16[256,1536]{1,0:T(8,128)(2,1)S(1)}, u32[]{:S(2)}, u32[]{:S(2)}) collective-permute-start(bf16[256,1536]{1,0:T(8,128)(2,1)} %get-tuple-element.326.refs_4_), channel_id=1, source_target_pairs={{1,2},{2,1},{5,6},{6,5},{9,10},{10,9},{13,14},{14,13},{17,18},{18,... | collective-permute-start | bytes 2359304 | tf_op jit(solution)/shard_map/ppermute | solution.py:876
  751.6 43.8 %collective-permute-start.69 = (bf16[256,1536]{1,0:T(8,128)(2,1)S(1)}, bf16[256,1536]{1,0:T(8,128)(2,1)S(1)}, u32[]{:S(2)}, u32[]{:S(2)}) collective-permute-start(bf16[256,1536]{1,0:T(8,128)(2,1)S(1)} %copy-done.27), channel_id=1, source_target_pairs={{0,1},{3,2},{1,0},{2,3},{4,5},{7,6},{5,4},{6,7},{8,9},{11,10},{9,8... | collective-permute-start | bytes 2359304 | tf_op jit(solution)/shard_map/ppermute | solution.py:876
  753.1 42.3 %collective-permute-start.70 = (bf16[256,1536]{1,0:T(8,128)(2,1)S(1)}, bf16[256,1536]{1,0:T(8,128)(2,1)S(1)}, u32[]{:S(2)}, u32[]{:S(2)}) collective-permute-start(bf16[256,1536]{1,0:T(8,128)(2,1)S(1)} %copy-done.26), channel_id=1, source_target_pairs={{1,2},{2,1},{5,6},{6,5},{9,10},{10,9},{13,14},{14,13},{17,18},{18,... | collective-permute-start | bytes 2359304 | tf_op jit(solution)/shard_map/ppermute | solution.py:876
  802.1 21.4 %collective-permute-start.71 = (bf16[256,1536]{1,0:T(8,128)(2,1)}, bf16[256,1536]{1,0:T(8,128)(2,1)S(1)}, u32[]{:S(2)}, u32[]{:S(2)}) collective-permute-start(bf16[256,1536]{1,0:T(8,128)(2,1)} %get-tuple-element.358.refs_2_), channel_id=1, source_target_pairs={{0,1},{3,2},{1,0},{2,3},{4,5},{7,6},{5,4},{6,7},{8,9},{11,10},{9,8... | collective-permute-start | bytes 2359304 | tf_op jit(solution)/shard_map/ppermute | solution.py:876
  809.3 27.2 %collective-permute-start.74 = (f32[8,128]{1,0:T(8,128)S(1)}, f32[8,128]{1,0:T(8,128)S(1)}, u32[]{:S(2)}, u32[]{:S(2)}) collective-permute-start(f32[8,128]{1,0:T(8,128)S(1)} %bitcast.94), channel_id=1, source_target_pairs={{0,1},{1,0},{2,3},{3,2},{4,5},{5,4},{6,7},{7,6},{8,9},{9,8},{10,11... | collective-permute-start | bytes 12296 | tf_op jit(solution)/shard_map/ppermute | solution.py:692
  812.0 24.5 %collective-permute-start.75 = (f32[8,128]{1,0:T(8,128)S(1)}, f32[8,128]{1,0:T(8,128)S(1)}, u32[]{:S(2)}, u32[]{:S(2)}) collective-permute-start(f32[8,128]{1,0:T(8,128)S(1)} %bitcast.95), channel_id=1, source_target_pairs={{0,2},{1,3},{2,0},{3,1},{4,6},{5,7},{6,4},{7,5},{8,10},{9,11},{10,... | collective-permute-start | bytes 12296 | tf_op jit(solution)/shard_map/ppermute | solution.py:692
  812.2 24.3 %collective-permute-start.76 = (f32[8,128]{1,0:T(8,128)S(1)}, f32[8,128]{1,0:T(8,128)S(1)}, u32[]{:S(2)}, u32[]{:S(2)}) collective-permute-start(f32[8,128]{1,0:T(8,128)S(1)} %bitcast.96), channel_id=1, source_target_pairs={{0,3},{1,2},{2,1},{3,0},{4,7},{5,6},{6,5},{7,4},{8,11},{9,10},{10,... | collective-permute-start | bytes 12296 | tf_op jit(solution)/shard_map/ppermute | solution.py:692
  828.1 20.3 %collective-permute-start.73 = (bf16[256,1536]{1,0:T(8,128)(2,1)}, bf16[256,1536]{1,0:T(8,128)(2,1)S(1)}, u32[]{:S(2)}, u32[]{:S(2)}) collective-permute-start(bf16[256,1536]{1,0:T(8,128)(2,1)} %get-tuple-element.361.refs_2_), channel_id=1, source_target_pairs={{0,1},{3,2},{1,0},{2,3},{4,5},{7,6},{5,4},{6,7},{8,9},{11,10},{9,8... | collective-permute-start | bytes 2359304 | tf_op jit(solution)/shard_map/ppermute | solution.py:876
  (139 other events, 1084.5 us)
Sparse Core Ops, SparseCore 0:
  16.8 35.8 all-gather.4
  492.9 34.1 all-gather.6
  529.6 55.5 all-gather.8
  604.6 79.2 reduce-scatter.3
  687.2 61.7 reduce-scatter.5
  752.6 67.6 reduce-scatter.7
